TPU v7x, 32 devices: a whole 2x2x4 slice. The times are simulated.
32 devices in a mesh: replica: 2 (over x), serve: 16 (over z, y, core).
Axes of the slice: x: 2, y: 2, z: 4, core: 2. Of those that a mesh axis runs over, the one named last changes fastest.
Arguments:
- residual_first: bfloat16 [64, 8192], P(('replica', 'serve')), parts along dimension 0, may hold values from -6 to 6
- residual_second: bfloat16 [64, 8192], P(('replica', 'serve')), parts along dimension 0, may hold values from -6 to 6
- attention_norm_gain: bfloat16 [8192], replicated, may hold values from 0.5 to 1.5
- query_matrix: bfloat16 [8192, 8192], P(None, 'serve'), may hold values from -0.0625 to 0.0625
- key_matrix: bfloat16 [8192, 1024], P(None, 'serve'), may hold values from -0.0625 to 0.0625
- value_matrix: bfloat16 [8192, 1024], P(None, 'serve'), may hold values from -0.0625 to 0.0625
- output_matrix: bfloat16 [8192, 8192], P('serve'), may hold values from -0.0625 to 0.0625
- query_down_weights: bfloat16 [32, 8192, 16], P('serve'), may hold values from -0.0625 to 0.0625
- value_down_weights: bfloat16 [32, 8192, 16], P('serve'), may hold values from -0.0625 to 0.0625
- query_up_weights: bfloat16 [32, 16, 8192], P(None, None, 'serve'), may hold values from -1.5 to 1.5
- value_up_weights: bfloat16 [32, 16, 1024], P(None, None, 'serve'), may hold values from -1.5 to 1.5
- rotated_key_cache: bfloat16 [64, 384, 1024], P(('replica', 'serve')), parts along dimension 0, may hold values from -256 to 256
- stored_value_cache: bfloat16 [64, 384, 1024], P(('replica', 'serve')), parts along dimension 0, may hold values from -6 to 6
- lengths: int32 [64], P('replica'), parts along dimension 0, may hold values from 1 to 384, as said below
- request_adapter: int32 [64], P('replica'), parts along dimension 0, may hold values from 0 to 31
- adapter_slot: int32 [32], replicated, may hold values from 0 to 31, each once
Outputs:
- out_one: bfloat16 [64, 8192], P(('replica', 'serve')), parts along dimension 0
- out_two: bfloat16 [64, 8192], P(('replica', 'serve')), parts along dimension 0
- new_keys: bfloat16 [64, 2, 1024], P(('replica', 'serve')), parts along dimension 0
- new_values: bfloat16 [64, 2, 1024], P(('replica', 'serve')), parts along dimension 0
There are 2 independent parts, one for each index of `replica`. A program takes and returns all parts, laid end to end along the dimension named above; an argument that names none is the same for every part. Nothing has to cross between parts.
Inputs may be any that keep to these rules, and one draw needn't show every extreme that they name: `lengths`: at least one request has exactly 384 cached tokens. `adapter_slot`: each slot appears once; slot s lies on index s // 2 of serve.
All inputs are finite; a program needn't handle non-finite values.
Results may differ from a plain program's by a relative error of at most 0.007.
The roundings to bfloat16 on the way count: a program that leaves them out, or rounds other values in their place, can miss the bound.
Values may be sent and summed in bfloat16 or wider, within the bound.
No kernel may reach another device: no remote copies, remote signals or barrier semaphores. Data moves between devices by JAX's collectives and lax.ppermute only.
A program may use at most 128 MiB of HBM per device.

v0:
```python
import math

import jax
import jax.numpy as jnp
from jax import lax
from jax.sharding import PartitionSpec as P

HEADS = 64
KV_HEADS = 8
HEAD = 128


def rms_normed(hidden, attention_norm_gain):
    values = hidden.astype(jnp.float32)
    factor = lax.rsqrt(jnp.mean(values * values, axis=-1, keepdims=True) + 1e-05)
    return (values * factor * attention_norm_gain.astype(jnp.float32)).astype(jnp.bfloat16)


def scaled_frequency(pair_index):
    base = jnp.exp(pair_index.astype(jnp.float32) * (-2.0 * math.log(500000.0) / HEAD))
    wavelength = 2.0 * math.pi / base
    smooth = jnp.clip((8192.0 / wavelength - 1.0) / 3.0, 0.0, 1.0)
    return (1.0 - smooth) * base / 8.0 + smooth * base


def rotate(values, offset, positions):
    width = values.shape[-1]
    pair_index = (offset + 2 * jnp.arange(width // 2)) % HEAD // 2
    inverse = scaled_frequency(pair_index)
    angle = positions[..., None] * inverse
    cosine = jnp.cos(angle)
    sine = jnp.sin(angle)
    pairs = values.reshape(values.shape[:-1] + (width // 2, 2))
    even = pairs[..., 0]
    odd = pairs[..., 1]
    turned = jnp.stack((even * cosine - odd * sine, even * sine + odd * cosine), axis=-1)
    return turned.reshape(values.shape)


def shards(
    residual_first,
    residual_second,
    attention_norm_gain,
    query_matrix,
    key_matrix,
    value_matrix,
    output_matrix,
    query_down_weights,
    value_down_weights,
    query_up_weights,
    value_up_weights,
    rotated_key_cache,
    stored_value_cache,
    lengths,
    request_adapter,
    adapter_slot,
):
    index = lax.axis_index("serve")
    own = residual_first.shape[0]
    adapters_present = query_down_weights.shape[0]
    query_cols = query_matrix.shape[1]
    key_cols = key_matrix.shape[1]
    rank_width = query_down_weights.shape[2]
    group = HEADS // KV_HEADS
    span = rotated_key_cache.shape[1]
    table = jnp.arange(adapter_slot.shape[0])
    storage_slots = jnp.sum(
        jnp.where(request_adapter[:, None] == table[None, :], adapter_slot[None, :], 0), axis=1
    )
    stored = index * adapters_present + jnp.arange(adapters_present)
    owned = (storage_slots[:, None] == stored[None, :]).astype(jnp.float32)
    down_maps_pair = jnp.concatenate((query_down_weights, value_down_weights), axis=2)
    query_up_map = query_up_weights[storage_slots]
    value_up_map = value_up_weights[storage_slots]
    own_lengths = lax.dynamic_slice_in_dim(lengths, index * own, own)

    def project(normed, first):
        steps_here = normed.shape[0]
        piece = lax.all_gather(normed, "serve", axis=1, tiled=True)
        base_q = jnp.einsum("srd,dc->src", piece, query_matrix, preferred_element_type=jnp.float32)
        base_k = jnp.einsum("srd,dc->src", piece, key_matrix, preferred_element_type=jnp.float32)
        base_v = jnp.einsum("srd,dc->src", piece, value_matrix, preferred_element_type=jnp.float32)
        low_all = jnp.einsum(
            "srd,adk->srak", piece, down_maps_pair, preferred_element_type=jnp.float32
        )
        low = jnp.einsum("srak,ra->srk", low_all, owned)
        projected = jnp.concatenate((base_q, base_k, base_v, low), axis=2)
        low = lax.psum(projected[..., query_cols + 2 * key_cols :], "serve").astype(jnp.bfloat16)
        base_q = projected[..., :query_cols]
        base_k = projected[..., query_cols : query_cols + key_cols]
        base_v = projected[..., query_cols + key_cols : query_cols + 2 * key_cols]
        query = base_q + jnp.einsum(
            "sbk,bkc->sbc", low[..., :rank_width], query_up_map, preferred_element_type=jnp.float32
        )
        value = (
            base_v
            + jnp.einsum(
                "sbk,bkc->sbc",
                low[..., rank_width:],
                value_up_map,
                preferred_element_type=jnp.float32,
            )
        ).astype(jnp.bfloat16)
        positions = (lengths[None, :] + first + jnp.arange(steps_here)[:, None]).astype(jnp.float32)
        query = rotate(query, index * query_cols, positions).astype(jnp.bfloat16)
        key = rotate(base_k, index * key_cols, positions).astype(jnp.bfloat16)
        return (
            lax.all_to_all(query, "serve", split_axis=1, concat_axis=2, tiled=True),
            lax.all_to_all(key, "serve", split_axis=1, concat_axis=2, tiled=True),
            lax.all_to_all(value, "serve", split_axis=1, concat_axis=2, tiled=True),
        )

    def attend(query, fresh_keys, fresh_values):
        queries = query.reshape(own, KV_HEADS, group, HEAD)
        cached_keys = rotated_key_cache.reshape(own, span, KV_HEADS, HEAD)
        cached_values = stored_value_cache.reshape(own, span, KV_HEADS, HEAD)
        newest_keys = fresh_keys.reshape(own, -1, KV_HEADS, HEAD)
        newest_values = fresh_values.reshape(own, -1, KV_HEADS, HEAD)
        cached = jnp.einsum(
            "rgqe,rtge->rgqt", queries, cached_keys, preferred_element_type=jnp.float32
        ) * HEAD ** (-0.5)
        visible = jnp.arange(span)[None, :] < own_lengths[:, None]
        cached = jnp.where(visible[:, None, None, :], cached, -1e30)
        fresh = jnp.einsum(
            "rgqe,rnge->rgqn", queries, newest_keys, preferred_element_type=jnp.float32
        ) * HEAD ** (-0.5)
        scores = jnp.concatenate((cached, fresh), axis=-1)
        top = jnp.max(scores, axis=-1, keepdims=True)
        weights = jnp.exp(scores - top)
        probs = (weights / jnp.sum(weights, axis=-1, keepdims=True)).astype(jnp.bfloat16)
        context = jnp.einsum(
            "rgqt,rtge->rgqe", probs[..., :span], cached_values, preferred_element_type=jnp.float32
        )
        context = context + jnp.einsum(
            "rgqn,rnge->rgqe", probs[..., span:], newest_values, preferred_element_type=jnp.float32
        )
        return context.reshape(own, -1).astype(jnp.bfloat16)

    def finish(context, hidden):
        heads_rows = lax.all_to_all(context, "serve", split_axis=2, concat_axis=0, tiled=True)
        summed = lax.psum_scatter(
            jnp.einsum(
                "bsc,cd->bsd", heads_rows, output_matrix, preferred_element_type=jnp.float32
            ),
            "serve",
            scatter_dimension=0,
            tiled=True,
        )
        return (hidden.astype(jnp.float32) + summed).astype(jnp.bfloat16)

    normed_one = rms_normed(residual_first, attention_norm_gain)
    normed_two = rms_normed(residual_second, attention_norm_gain)
    query_one, key_one, value_one = project(normed_one[None], 0)
    keys_one = jnp.transpose(key_one, (1, 0, 2))
    values_one = jnp.transpose(value_one, (1, 0, 2))
    out_one = finish(attend(query_one[0], keys_one, values_one)[:, None], residual_first[:, None])[
        :, 0
    ]
    query_two, key_two, value_two = project(normed_two[None], 1)
    fresh_keys = jnp.concatenate((keys_one, jnp.transpose(key_two, (1, 0, 2))), axis=1)
    fresh_values = jnp.concatenate((values_one, jnp.transpose(value_two, (1, 0, 2))), axis=1)
    out_two = finish(
        attend(query_two[0], fresh_keys, fresh_values)[:, None], residual_second[:, None]
    )[:, 0]
    return (out_one, out_two, fresh_keys, fresh_values)


def solution(mesh):
    return jax.shard_map(
        shards,
        mesh=mesh,
        in_specs=(
            P(("replica", "serve"), None),
            P(("replica", "serve"), None),
            P(),
            P(None, "serve"),
            P(None, "serve"),
            P(None, "serve"),
            P("serve", None),
            P("serve", None, None),
            P("serve", None, None),
            P(None, None, "serve"),
            P(None, None, "serve"),
            P(("replica", "serve"), None, None),
            P(("replica", "serve"), None, None),
            P("replica"),
            P("replica"),
            P(),
        ),
        out_specs=(
            P(("replica", "serve"), None),
            P(("replica", "serve"), None),
            P(("replica", "serve"), None, None),
            P(("replica", "serve"), None, None),
        ),
        check_vma=False,
    )
```

profile of v0, /device:TPU:0, one launch (start us, length us, event | category | flops | bytes accessed | tf_op | source)
XLA Modules:
  0.0 487.1 jit_solution(9551486561752521545)
XLA Ops:
  11.6 24.6 %all-gather.3 = bf16[16,2,8192]{2,1,0:T(2,128)(2,1)S(1)} all-gather(bf16[1,2,8192]{2,1,0:T(2,128)(2,1)S(1)} %get-tuple-element.48), channel_id=3, replica_groups=mesh['replica'=2,'serve'=16] {'serve'}, dimensions={0}, use_global_device_ids=true | all-gather | bytes 557056 | tf_op jit(solution)/shard_map/all_gather | solution.py:79
  36.4 18.9 %all-gather.2 = bf16[16,2,8192]{2,1,0:T(2,128)(2,1)S(1)} all-gather(bf16[1,2,8192]{2,1,0:T(2,128)(2,1)S(1)} %get-tuple-element.49), channel_id=2, replica_groups=mesh['replica'=2,'serve'=16] {'serve'}, dimensions={0}, use_global_device_ids=true | all-gather | bytes 557056 | tf_op jit(solution)/shard_map/all_gather | solution.py:79
  56.3 2.5 dot_general.94
  63.0 3.5 all-to-all-start.5
  74.3 61.9 %all-reduce.2 = (bf16[1,32,32]{2,1,0:T(8,128)(2,1)S(1)}, bf16[1,32,32]{2,1,0:T(8,128)(2,1)S(1)}) all-reduce(f32[1,32,32]{2,1,0:T(8,128)S(1)} %bitcast.256, f32[1,32,32]{2,1,0:T(8,128)S(1)} %bitcast.257), channel_id=1, replica_groups=mesh['replica'=2,'serve'=16] {'serve'}, use_global_device_ids=true, to_apply=%region_2.3 | all-reduce | flops 2048 | bytes 12288 | tf_op jit(solution)/shard_map/psum | solution.py:88
  137.0 4.9 %convolution_add_fusion.1 = f32[32,512]{1,0:T(8,128)S(1)} fusion(bf16[32,8192]{1,0:T(8,128)(2,1)S(1)} %reshape.915, bf16[8192,512]{1,0:T(8,128)(2,1)} %param.19, f32[32,1,512]{2,1,0:T(1,128)S(1)} %fusion.108), kind=kOutput, calls=%fused_computation.24 | convolution fusion | flops 268451840 | bytes 9043968 | tf_op jit(solution)/shard_map/srd,dc->src/dot_general | solution.py:80
  142.5 4.9 %convolution_add_fusion = f32[32,512]{1,0:T(8,128)S(1)} fusion(bf16[32,8192]{1,0:T(8,128)(2,1)S(1)} %reshape.917, bf16[8192,512]{1,0:T(8,128)(2,1)} %param.19, f32[32,1,512]{2,1,0:T(1,128)S(1)} %fusion.104), kind=kOutput, calls=%fused_computation.23 | convolution fusion | flops 268451840 | bytes 9043968 | tf_op jit(solution)/shard_map/srd,dc->src/dot_general | solution.py:80
  150.7 3.5 all-to-all-start.1
  156.4 4.2 all-to-all-done.1
  160.6 3.5 all-to-all-start.2
  164.7 5.8 %all-to-all-done.2 = bf16[1,32,64]{2,0,1:T(2,128)(2,1)S(1)} async-done(((bf16[1,32,64]{2,0,1:T(2,128)(2,1)}), bf16[1,32,64]{2,0,1:T(2,128)(2,1)S(1)}, u32[]{:S(2)}, u32[]{:S(2)}) %all-to-all-start.2) | async-done | bytes 4128 | tf_op jit(solution)/shard_map/all_to_all | solution.py:110
  170.6 3.5 all-to-all-start.6
  178.1 2.4 all-to-all-done.6
  180.5 3.5 all-to-all-start
  186.5 4.2 all-to-all-done
  190.7 3.7 all-to-all-start.4
  194.7 6.1 %all-to-all-done.4 = bf16[16,2,512]{2,1,0:T(2,128)(2,1)S(1)} async-done(((bf16[16,2,512]{2,1,0:T(2,128)(2,1)}), bf16[16,2,512]{2,1,0:T(2,128)(2,1)S(1)}, u32[]{:S(2)}, u32[]{:S(2)}) %all-to-all-start.4) | async-done | bytes 32800 | tf_op jit(solution)/shard_map/all_to_all | solution.py:108
  206.3 6.8 %copy.296 = bf16[2,1,8192]{0,1,2:T(2,128)(2,1)} copy(bf16[2,1,8192]{2,0,1:T(2,128)(2,1)S(1)} %convert_element_type.167) | data formatting | bytes 65536 | tf_op jit(solution)/shard_map/convert_element_type | solution.py:137
  213.1 46.5 %reduce.11 = bf16[8192,2]{1,0:T(8,128)(2,1)} reduce(bf16[8192,1,2]{2,1,0:T(2,128)(2,1)} %bitcast.232, bf16[]{:T(256)} %broadcast.761), dimensions={1}, to_apply=%bitcast.176.reduce_sub_computation | reduce | bytes 65538
  259.6 4.8 reshape.948
  264.4 3.7 all-to-all-start.3
  268.8 6.8 %copy.320 = bf16[2,1,8192]{0,1,2:T(2,128)(2,1)} copy(bf16[2,1,8192]{2,0,1:T(2,128)(2,1)S(1)} %convert_element_type.180) | data formatting | bytes 65536 | tf_op jit(solution)/shard_map/convert_element_type | solution.py:137
  275.5 46.5 %reduce.13 = bf16[8192,2]{1,0:T(8,128)(2,1)} reduce(bf16[8192,1,2]{2,1,0:T(2,128)(2,1)} %bitcast.231, bf16[]{:T(256)} %broadcast.761), dimensions={1}, to_apply=%bitcast.180.reduce_sub_computation | reduce | bytes 65538
  322.1 4.8 reshape.952
  326.9 5.7 %all-to-all-start.7 = ((bf16[16,2,512]{2,1,0:T(2,128)(2,1)}), bf16[16,2,512]{2,1,0:T(2,128)(2,1)S(1)}, u32[]{:S(2)}, u32[]{:S(2)}) async-start(bf16[16,2,512]{2,1,0:T(2,128)(2,1)} %reshape.952), calls=%async_computation.7 | async-start | bytes 65536 | tf_op jit(solution)/shard_map/all_to_all | solution.py:140
  332.7 8.3 %reshape.949 = bf16[8192,1,2]{2,1,0:T(2,128)(2,1)} reshape(bf16[16,2,512]{2,1,0:T(2,128)(2,1)S(1)} %all-to-all-done.3) | data formatting | bytes 65536
  341.0 8.1 %copy.297 = bf16[2,1,8192]{2,0,1:T(2,128)(2,1)S(1)} copy(bf16[2,1,8192]{0,1,2:T(2,128)(2,1)} %bitcast.233) | data formatting | bytes 65536 | tf_op jit(solution)/shard_map/all_to_all | solution.py:140
  349.1 8.3 %reshape.953 = bf16[8192,1,2]{2,1,0:T(2,128)(2,1)} reshape(bf16[16,2,512]{2,1,0:T(2,128)(2,1)S(1)} %all-to-all-done.7) | data formatting | bytes 65536
  357.4 8.1 %copy.321 = bf16[2,1,8192]{2,0,1:T(2,128)(2,1)S(1)} copy(bf16[2,1,8192]{0,1,2:T(2,128)(2,1)} %bitcast.234) | data formatting | bytes 65536 | tf_op jit(solution)/shard_map/all_to_all | solution.py:140
  365.6 5.9 %convolution_bitcast_fusion.1 = f32[32,1,8192]{2,0,1:T(8,128)} fusion(bf16[32,512]{1,0:T(8,128)(2,1)S(1)} %reshape.886, bf16[512,8192]{1,0:T(8,128)(2,1)} %param.22), kind=kOutput, calls=%fused_computation.3 | convolution fusion | flops 268435456 | bytes 9469952 | tf_op jit(solution)/shard_map/bsc,cd->bsd/dot_general | solution.py:142
  371.5 5.9 %convolution_bitcast_fusion = f32[32,1,8192]{2,0,1:T(8,128)} fusion(bf16[32,512]{1,0:T(8,128)(2,1)S(1)} %reshape.891, bf16[512,8192]{1,0:T(8,128)(2,1)} %param.22), kind=kOutput, calls=%fused_computation.2 | convolution fusion | flops 268435456 | bytes 9469952 | tf_op jit(solution)/shard_map/bsc,cd->bsd/dot_general | solution.py:142
  381.0 96.0 %all-reduce.6.cloned.1.call-done = (f32[32,1,8192]{2,0,1:T(8,128)}, f32[32,1,8192]{2,0,1:T(8,128)}) async-done(((f32[32,1,8192]{2,0,1:T(8,128)}, f32[32,1,8192]{2,0,1:T(8,128)}), (f32[32,1,8192]{2,0,1:T(8,128)}, f32[32,1,8192]{2,0,1:T(8,128)})) %all-reduce.6.cloned.1.call-update) | async-done | bytes 2097168
  (173 shorter events, 43.7 us)
Async XLA Ops:
  7.2 194.1 %copy-start = (bf16[2,384,1024]{2,1,0:T(8,128)(2,1)S(1)}, bf16[2,384,1024]{2,1,0:T(8,128)(2,1)}, u32[]{:S(2)}) copy-start(bf16[2,384,1024]{2,1,0:T(8,128)(2,1)} %param.27) | copy-start | bytes 4718596
  36.4 22.4 %copy-start.1 = (bf16[32,8192,1]{1,0,2:T(8,128)(2,1)}, bf16[32,8192,1]{1,0,2:T(8,128)(2,1)S(1)}, u32[]{:S(2)}) copy-start(bf16[32,8192,1]{1,0,2:T(8,128)(2,1)S(1)} %reshape.927) | copy-start | bytes 1572868
  58.8 2.3 copy-start.3
  58.8 2.3 copy-start.6
  63.0 87.6 %all-to-all-start.5 = ((bf16[1,32,64]{2,0,1:T(2,128)(2,1)}), bf16[1,32,64]{2,0,1:T(2,128)(2,1)S(1)}, u32[]{:S(2)}, u32[]{:S(2)}) async-start(bf16[1,32,64]{2,0,1:T(2,128)(2,1)} %copy.309), calls=%async_computation.5 | async-start | bytes 32768 | tf_op jit(solution)/shard_map/all_to_all | solution.py:109
  67.0 2.3 copy-start.2
  68.1 2.2 copy-start.4
  69.3 2.0 copy-start.18
  69.3 2.0 copy-start.19
  69.3 2.0 copy-start.20
  69.3 2.4 copy-start.9
  150.7 10.0 %all-to-all-start.1 = ((bf16[1,32,64]{2,0,1:T(2,128)(2,1)}), bf16[1,32,64]{2,0,1:T(2,128)(2,1)S(1)}, u32[]{:S(2)}, u32[]{:S(2)}) async-start(bf16[1,32,64]{2,0,1:T(2,128)(2,1)} %copy.290), calls=%async_computation.1 | async-start | bytes 32768 | tf_op jit(solution)/shard_map/all_to_all | solution.py:109
  160.6 10.0 %all-to-all-start.2 = ((bf16[1,32,64]{2,0,1:T(2,128)(2,1)}), bf16[1,32,64]{2,0,1:T(2,128)(2,1)S(1)}, u32[]{:S(2)}, u32[]{:S(2)}) async-start(bf16[1,32,64]{2,0,1:T(2,128)(2,1)} %copy.294), calls=%async_computation.2 | async-start | bytes 32768 | tf_op jit(solution)/shard_map/all_to_all | solution.py:110
  170.6 9.9 %all-to-all-start.6 = ((bf16[1,32,64]{2,0,1:T(2,128)(2,1)}), bf16[1,32,64]{2,0,1:T(2,128)(2,1)S(1)}, u32[]{:S(2)}, u32[]{:S(2)}) async-start(bf16[1,32,64]{2,0,1:T(2,128)(2,1)} %copy.315), calls=%async_computation.6 | async-start | bytes 32768 | tf_op jit(solution)/shard_map/all_to_all | solution.py:110
  180.5 10.2 %all-to-all-start = ((bf16[16,2,512]{2,1,0:T(2,128)(2,1)}), bf16[16,2,512]{2,1,0:T(2,128)(2,1)S(1)}, u32[]{:S(2)}, u32[]{:S(2)}) async-start(bf16[16,2,512]{2,1,0:T(2,128)(2,1)} %reshape.946), calls=%async_computation | async-start | bytes 65536 | tf_op jit(solution)/shard_map/all_to_all | solution.py:108
  184.1 1.7 copy-start.14
  184.3 6.4 %copy-start.10 = (bf16[1,2,16,64]{3,2,1,0:T(8,128)(2,1)}, bf16[1,2,16,64]{3,2,1,0:T(8,128)(2,1)S(1)}, u32[]{:S(2)}) copy-start(bf16[1,2,16,64]{3,2,1,0:T(8,128)(2,1)S(1)} %copy.310) | copy-start | bytes 12292
  185.8 4.9 %copy-start.12 = (bf16[1,2,16,64]{3,2,1,0:T(8,128)(2,1)}, bf16[1,2,16,64]{3,2,1,0:T(8,128)(2,1)S(1)}, u32[]{:S(2)}) copy-start(bf16[1,2,16,64]{3,2,1,0:T(8,128)(2,1)S(1)} %copy.316) | copy-start | bytes 12292
  190.7 10.1 %all-to-all-start.4 = ((bf16[16,2,512]{2,1,0:T(2,128)(2,1)}), bf16[16,2,512]{2,1,0:T(2,128)(2,1)S(1)}, u32[]{:S(2)}, u32[]{:S(2)}) async-start(bf16[16,2,512]{2,1,0:T(2,128)(2,1)} %reshape.950), calls=%async_computation.4 | async-start | bytes 65536 | tf_op jit(solution)/shard_map/all_to_all | solution.py:108
  202.0 3.2 copy-start.5
  259.6 8.5 %copy-start.16 = (bf16[2,1,8,128]{3,1,2,0:T(2,128)(2,1)S(1)}, bf16[2,1,8,128]{3,1,2,0:T(2,128)(2,1)}, u32[]{:S(2)}) copy-start(bf16[2,1,8,128]{3,1,2,0:T(2,128)(2,1)} %concatenate.42) | copy-start | bytes 12292
  259.6 8.5 %copy-start.17 = (bf16[2,1,8,128]{3,1,2,0:T(2,128)(2,1)S(1)}, bf16[2,1,8,128]{3,1,2,0:T(2,128)(2,1)}, u32[]{:S(2)}) copy-start(bf16[2,1,8,128]{3,1,2,0:T(2,128)(2,1)} %concatenate.43) | copy-start | bytes 12292
  264.4 62.4 %all-to-all-start.3 = ((bf16[16,2,512]{2,1,0:T(2,128)(2,1)}), bf16[16,2,512]{2,1,0:T(2,128)(2,1)S(1)}, u32[]{:S(2)}, u32[]{:S(2)}) async-start(bf16[16,2,512]{2,1,0:T(2,128)(2,1)} %reshape.948), calls=%async_computation.3 | async-start | bytes 65536 | tf_op jit(solution)/shard_map/all_to_all | solution.py:140
  326.9 22.3 %all-to-all-start.7 = ((bf16[16,2,512]{2,1,0:T(2,128)(2,1)}), bf16[16,2,512]{2,1,0:T(2,128)(2,1)S(1)}, u32[]{:S(2)}, u32[]{:S(2)}) async-start(bf16[16,2,512]{2,1,0:T(2,128)(2,1)} %reshape.952), calls=%async_computation.7 | async-start | bytes 65536 | tf_op jit(solution)/shard_map/all_to_all | solution.py:140
  332.6 144.4 %all-reduce.6.cloned.1.call-start = ((), (), s32[]{:S(2)}) async-start(), calls=%async_computation.8 | async-start | bytes 4194304
  377.4 0.7 copy-start.21
  377.5 1.9 copy-start.11
  377.5 2.1 copy-start.15
  377.5 2.2 copy-start.13
  377.5 99.5 %copy-start.7 = (bf16[2,8192]{1,0:T(2,128)(2,1)S(1)}, bf16[2,8192]{1,0:T(2,128)(2,1)}, u32[]{:S(2)}) copy-start(bf16[2,8192]{1,0:T(2,128)(2,1)} %param.16) | copy-start | bytes 98308
  377.5 101.1 %copy-start.8 = (bf16[2,8192]{1,0:T(2,128)(2,1)S(1)}, bf16[2,8192]{1,0:T(2,128)(2,1)}, u32[]{:S(2)}) copy-start(bf16[2,8192]{1,0:T(2,128)(2,1)} %param.17) | copy-start | bytes 98308
Sparse Core Ops, SparseCore 0:
  377.6 99.3 all-reduce.5
where the time goes:
time: 489 us; the launch traced here: 487 us
  waiting for transfers between devices  119 us (24%)
  other arithmetic  105 us (21%)
  blocking collectives  105 us (21%)
  local copies, waits for them, and re-layouts  77.6 us (16%)
  matrix products  34.5 us (7%)
  starting transfers between devices  30.7 us (6%)
  between operations  15.4 us (3%)
    unnamed x2, waiting for transfers between devices  96.1 us
    unnamed x5, other arithmetic  95.6 us
    psum x1, blocking collectives, project(): lax.psum(projected[..., query_cols + 2 * key_cols:], 'serve')  61.9 us
    all_gather x2, blocking collectives, project(): piece = lax.all_gather(normed, 'serve', axis=1, tiled=True)  43.5 us
    unnamed x71, local copies, waits for them, and re-layouts  33.6 us
    all_to_all x4, local copies, waits for them, and re-layouts, finish(): lax.all_to_all(context, 'serve', split_axis=2, concat_axis=0, tiled=True)  16.2 us
    convert_element_type x4, local copies, waits for them, and re-layouts, attend(): return context.reshape(own, -1).astype(jnp.bfloat16)  13.6 us
    dot_general x2, matrix products, finish(): jnp.einsum('bsc,cd->bsd', heads_rows, output_matrix, preferred_element_ty...  11.8 us
  transfers between devices with their start and end apart: 9, of which 6 were waited for; matrix products, arithmetic and copies ran while one was open for 22% of the time, Pallas kernels for 0%

commit v1 on v0

v1 whole, which is shorter than its diff:
```python
import functools
import math

import jax
import jax.numpy as jnp
from jax import lax
from jax.experimental import pallas as pl
from jax.experimental.pallas import tpu as pltpu
from jax.sharding import PartitionSpec as P

HEADS = 64
KV_HEADS = 8
HEAD = 128
STEPS = 2
LIMIT = 48 * 1024 * 1024
NT = (((1,), (1,)), ((), ()))
F32 = jnp.float32
BF16 = jnp.bfloat16


def dot(a, b):
    return jnp.dot(a, b, preferred_element_type=F32)


def dot_nt(a, b):
    return lax.dot_general(a, b, NT, preferred_element_type=F32)


def whole_call(body, out_shape, args, smem=0, scratch=()):
    specs = [pl.BlockSpec(memory_space=pltpu.SMEM)] * smem
    specs += [pl.BlockSpec(memory_space=pltpu.VMEM)] * (len(args) - smem)
    many = isinstance(out_shape, (tuple, list))
    vmem = pl.BlockSpec(memory_space=pltpu.VMEM)
    return pl.pallas_call(
        body,
        out_shape=out_shape,
        in_specs=specs,
        out_specs=tuple(vmem for _ in out_shape) if many else vmem,
        scratch_shapes=list(scratch),
        compiler_params=pltpu.CompilerParams(vmem_limit_bytes=LIMIT),
    )(*args)


def scaled_frequency(pair_index):
    base = jnp.exp(pair_index.astype(F32) * (-2.0 * math.log(500000.0) / HEAD))
    wavelength = 2.0 * math.pi / base
    smooth = jnp.clip((8192.0 / wavelength - 1.0) / 3.0, 0.0, 1.0)
    return (1.0 - smooth) * base / 8.0 + smooth * base


def turn_tables(positions, offset, width):
    lane = offset + jnp.arange(width)
    angle = positions[:, None] * scaled_frequency(lane % HEAD // 2)[None, :]
    sign = jnp.where(lane % 2 == 0, -1.0, 1.0)
    return jnp.cos(angle), jnp.sin(angle) * sign[None, :]


def norm_body(first_ref, second_ref, gain_ref, out_ref):
    gain = gain_ref[...].astype(F32)
    rows = []
    for ref in (first_ref, second_ref):
        values = ref[...].astype(F32)
        factor = lax.rsqrt(jnp.mean(values * values, axis=-1, keepdims=True) + 1e-05)
        rows.append(values * factor * gain)
    out_ref[...] = jnp.concatenate(rows, axis=0).astype(BF16)


def low_body(rank, x_ref, qd_ref, vd_ref, local_ref, place_ref, out_ref):
    adapters = qd_ref.shape[0] // rank
    maps = jnp.concatenate((qd_ref[...], vd_ref[...]), axis=0)
    low = dot_nt(x_ref[...], maps)
    lane = lax.broadcasted_iota(jnp.int32, low.shape, 1)
    low = jnp.where(lane // rank % adapters == local_ref[...], low, 0.0)
    total = 0.0
    for a in range(adapters):
        q = low[:, a * rank : (a + 1) * rank]
        v = low[:, (adapters + a) * rank : (adapters + a + 1) * rank]
        total = total + jnp.concatenate((q, v), axis=1)
    rows = dot(place_ref[...], total.astype(BF16))
    pack = HEAD // (2 * rank)
    step = rows.shape[0] // pack
    packed = jnp.concatenate([rows[i * step : (i + 1) * step] for i in range(pack)], axis=1)
    packed = packed.astype(BF16)
    for i in range(out_ref.shape[0]):
        out_ref[i] = packed


def base_body(x_ref, q_ref, k_ref, v_ref, oq_ref, okv_ref):
    @pl.when(pl.program_id(0) == 0)
    def _():
        oq_ref[...] = jnp.zeros_like(oq_ref)
        okv_ref[...] = jnp.zeros_like(okv_ref)

    x = x_ref[...]
    oq_ref[...] += dot(x, q_ref[...])
    okv_ref[...] += dot_nt(x, jnp.concatenate((k_ref[...], v_ref[...]), axis=0))


def turned(values, cosine, sine):
    lane = lax.broadcasted_iota(jnp.int32, values.shape, 1)
    width = values.shape[1]
    ahead = pltpu.roll(values, width - 1, 1)
    behind = pltpu.roll(values, 1, 1)
    return values * cosine + jnp.where(lane % 2 == 0, ahead, behind) * sine


def ready_body(
    rank, oq_ref, okv_ref, low_ref, unplace_ref, slot_ref, uq_ref, uv_ref, cos_ref, sin_ref,
    kcos_ref, ksin_ref, send_ref, out_ref,
):
    packed = jnp.sum(low_ref[...].astype(F32), axis=0)
    pack = HEAD // (2 * rank)
    low = jnp.concatenate(
        [packed[:, i * 2 * rank : (i + 1) * 2 * rank] for i in range(pack)], axis=0
    )
    low = dot(unplace_ref[...], low.astype(BF16)).astype(BF16)
    wide = uq_ref.shape[0]
    lane = lax.broadcasted_iota(jnp.int32, (low.shape[0], wide), 1)
    here = lane // rank == slot_ref[...]
    row = lax.broadcasted_iota(jnp.int32, (2 * rank, wide), 0)
    column = lax.broadcasted_iota(jnp.int32, (2 * rank, wide), 1)
    spread_q = jnp.where(column % rank == row, 1.0, 0.0).astype(BF16)
    spread_v = jnp.where(column % rank + rank == row, 1.0, 0.0).astype(BF16)
    wide_q = jnp.where(here, dot(low, spread_q), 0.0).astype(BF16)
    wide_v = jnp.where(here, dot(low, spread_v), 0.0).astype(BF16)
    query = oq_ref[...] + dot(wide_q, uq_ref[...])
    columns = okv_ref.shape[1] // 2
    key = okv_ref[:, :columns]
    value = okv_ref[:, columns:] + dot(wide_v, uv_ref[...])
    cosine, sine = cos_ref[...], sin_ref[...]
    parts = []
    for h in range(query.shape[1] // HEAD):
        parts.append(turned(query[:, h * HEAD : (h + 1) * HEAD], cosine, sine))
    fresh = [turned_narrow(key, kcos_ref[...], ksin_ref[...]), value]
    if 2 * columns < HEAD:
        fresh.append(jnp.zeros((key.shape[0], HEAD - 2 * columns), F32))
    parts.append(jnp.concatenate(fresh, axis=1))
    stacked = jnp.concatenate(parts, axis=0).astype(BF16)
    out_ref[...] = dot(send_ref[...], stacked).astype(BF16).reshape(out_ref.shape)


def turned_narrow(values, cosine, sine):
    width = values.shape[1]
    lane = lax.broadcasted_iota(jnp.int32, values.shape, 1)
    ahead = jnp.concatenate((values[:, 1:], values[:, :1]), axis=1)
    behind = jnp.concatenate((values[:, width - 1 :], values[:, : width - 1]), axis=1)
    return values * cosine + jnp.where(lane % 2 == 0, ahead, behind) * sine


def attend_body(own, columns, len_ref, x_ref, order_ref, k_ref, v_ref, ctx_ref, nk_ref, nv_ref, s_ref):
    n, span = x_ref.shape[0], k_ref.shape[1]
    group = HEADS // KV_HEADS
    local = HEADS // n
    rows = own * STEPS
    mine = group * STEPS
    x = x_ref[...]
    queries = dot(order_ref[...], x.reshape(n * x.shape[1], HEAD)).astype(BF16)
    wide = x.astype(F32)
    first = rows * local
    fresh = [wide[i, first : first + rows] for i in range(n)]
    each = n // KV_HEADS
    keys, values = [], []
    for g in range(KV_HEADS):
        pieces = fresh[g * each : (g + 1) * each]
        keys.append(jnp.concatenate([p[:, :columns] for p in pieces], axis=1))
        values.append(jnp.concatenate([p[:, columns : 2 * columns] for p in pieces], axis=1))
    nk_ref[...] = jnp.concatenate(keys, axis=1).astype(BF16)
    nv_ref[...] = jnp.concatenate(values, axis=1).astype(BF16)
    pad = jnp.zeros((16 - rows, HEAD), F32)
    keys = [jnp.concatenate((k, pad), axis=0).astype(BF16) for k in keys]
    values = [jnp.concatenate((v, pad), axis=0).astype(BF16) for v in values]
    scale = HEAD ** (-0.5)
    contexts = []
    for b in range(own):
        q = queries[b * KV_HEADS * mine : (b + 1) * KV_HEADS * mine]
        cached, newer = [], []
        for g in range(KV_HEADS):
            qg = q[g * mine : (g + 1) * mine]
            cached.append(dot_nt(qg, k_ref[b, :, g * HEAD : (g + 1) * HEAD]))
            newer.append(dot_nt(qg, keys[g]))
        cached = jnp.concatenate(cached, axis=0) * scale
        newer = jnp.concatenate(newer, axis=0) * scale
        place = lax.broadcasted_iota(jnp.int32, cached.shape, 1)
        cached = jnp.where(place < len_ref[b], cached, -1e30)
        step = lax.broadcasted_iota(jnp.int32, newer.shape, 0) % STEPS
        at = lax.broadcasted_iota(jnp.int32, newer.shape, 1) - b * STEPS
        newer = jnp.where((at >= 0) & (at <= step), newer, -1e30)
        top = jnp.maximum(
            jnp.max(cached, axis=1, keepdims=True), jnp.max(newer, axis=1, keepdims=True)
        )
        cached = jnp.exp(cached - top)
        newer = jnp.exp(newer - top)
        total = jnp.sum(cached, axis=1, keepdims=True) + jnp.sum(newer, axis=1, keepdims=True)
        cached = (cached / total).astype(BF16)
        newer = (newer / total).astype(BF16)
        for g in range(KV_HEADS):
            at_rows = slice(g * mine, (g + 1) * mine)
            part = dot(cached[at_rows], v_ref[b, :, g * HEAD : (g + 1) * HEAD])
            s_ref[(b * KV_HEADS + g) * mine : (b * KV_HEADS + g + 1) * mine] = part + dot(
                newer[at_rows], values[g]
            )
    step = local * STEPS
    half = KV_HEADS * mine
    for i in range(n):
        block = [s_ref[b * half + i * step : b * half + (i + 1) * step] for b in range(own)]
        ctx_ref[i] = jnp.concatenate(block, axis=0).astype(BF16)


def out_body(ctx_ref, take_ref, w_ref, mine_ref, other_ref, a_ref):
    @pl.when(pl.program_id(0) == 0)
    def _():
        rows = a_ref.shape[0]
        n = ctx_ref.shape[0]
        x = ctx_ref[...].reshape(n * ctx_ref.shape[1], HEAD)
        taken = dot(take_ref[...], x).astype(BF16)
        for h in range(a_ref.shape[1] // HEAD):
            a_ref[:, h * HEAD : (h + 1) * HEAD] = taken[h * rows : (h + 1) * rows]

    half = mine_ref.shape[0]
    product = dot(a_ref[...], w_ref[...])
    mine_ref[...] = product[:half]
    other_ref[...] = product[half:]


def shards(
    sizes,
    residual_first,
    residual_second,
    attention_norm_gain,
    query_matrix,
    key_matrix,
    value_matrix,
    output_matrix,
    query_down_weights,
    value_down_weights,
    query_up_weights,
    value_up_weights,
    rotated_key_cache,
    stored_value_cache,
    lengths,
    request_adapter,
    adapter_slot,
):
    far, near, cores = sizes
    n = far * near * cores
    index = lax.axis_index("serve")
    own, width = residual_first.shape
    adapters, _, rank = query_down_weights.shape
    query_cols = query_matrix.shape[1]
    key_cols = key_matrix.shape[1]
    local = query_cols // HEAD
    rows = own * STEPS
    all_rows = n * rows
    stored = query_up_weights.shape[0]

    def partner(f, m, c):
        pairs = []
        for z in range(far):
            for y in range(near):
                for k in range(cores):
                    to = (((z + f) % far) * near + (y + m) % near) * cores + (k + c) % cores
                    pairs.append(((z * near + y) * cores + k, to))
        return pairs

    def shift(value, f, m, c):
        return lax.ppermute(value, "serve", partner(f, m, c))

    core_at = index % cores
    near_at = index // cores % near
    far_at = index // (cores * near)
    block = jnp.arange(n)
    block_c, block_m, block_f = block // (far * near), block // far % near, block % far

    def device_of(sign):
        return (
            ((far_at + sign * block_f) % far) * near + (near_at + sign * block_m) % near
        ) * cores + (core_at + sign * block_c) % cores

    source = device_of(-1)
    target = device_of(1)

    row_device = jnp.repeat(source, rows)
    row_step = jnp.tile(jnp.repeat(jnp.arange(STEPS), own), n)
    row_own = jnp.tile(jnp.arange(own), n * STEPS)
    request = row_device * own + row_own
    hot = request[:, None] == jnp.arange(lengths.shape[0])[None, :]
    row_length = jnp.sum(jnp.where(hot, lengths[None, :], 0), axis=1)
    row_adapter = jnp.sum(jnp.where(hot, request_adapter[None, :], 0), axis=1)
    table = jnp.arange(adapter_slot.shape[0])
    slot = jnp.sum(
        jnp.where(row_adapter[:, None] == table[None, :], adapter_slot[None, :], 0), axis=1
    )[:, None]
    positions = (row_length + row_step).astype(F32)
    cosine, sine = turn_tables(positions, 0, HEAD)
    key_cosine, key_sine = turn_tables(positions, index * key_cols, key_cols)
    absolute = (row_device * STEPS + row_step) * own + row_own
    place = (jnp.arange(all_rows)[:, None] == absolute[None, :]).astype(BF16)
    unplace = (absolute[:, None] == jnp.arange(all_rows)[None, :]).astype(BF16)

    sent = -(-(rows * local + rows) // 16) * 16
    wanted = [
        row_device * sent + (row_own * local + h) * STEPS + row_step for h in range(local)
    ]
    wanted.append(row_device * sent + rows * local + row_own * STEPS + row_step)
    wanted = jnp.concatenate(wanted)
    send = (jnp.arange(n * sent)[:, None] == wanted[None, :]).astype(BF16)

    a = jnp.arange(own * HEADS * STEPS)
    a_own, a_head, a_step = a // (HEADS * STEPS), a // STEPS % HEADS, a % STEPS
    held = (a_head // local) * sent + (a_own * local + a_head % local) * STEPS + a_step
    order = (held[:, None] == jnp.arange(n * sent)[None, :]).astype(BF16)

    out_device = jnp.repeat(target, rows)
    came = [
        out_device * rows * local + (row_own * local + h) * STEPS + row_step for h in range(local)
    ]
    came = jnp.concatenate(came)
    take = (came[:, None] == jnp.arange(n * rows * local)[None, :]).astype(BF16)

    normed = whole_call(
        norm_body,
        jax.ShapeDtypeStruct((rows, width), BF16),
        (residual_first, residual_second, attention_norm_gain[None, :]),
    )
    gathered = normed[None]
    gathered = jnp.concatenate([gathered] + [shift(gathered, f, 0, 0) for f in range(1, far)])
    gathered = jnp.concatenate([gathered] + [shift(gathered, 0, m, 0) for m in range(1, near)])
    gathered = jnp.concatenate([gathered] + [shift(gathered, 0, 0, c) for c in range(1, cores)])
    x = gathered.reshape(all_rows, width)

    query_down = jnp.swapaxes(query_down_weights, 1, 2).reshape(adapters * rank, width)
    value_down = jnp.swapaxes(value_down_weights, 1, 2).reshape(adapters * rank, width)
    packed_rows = all_rows * 2 * rank // HEAD
    low = whole_call(
        functools.partial(low_body, rank),
        jax.ShapeDtypeStruct((n, packed_rows, HEAD), BF16),
        (x, query_down, value_down, slot - index * adapters, place),
    )
    low = lax.all_to_all(low, "serve", split_axis=0, concat_axis=0, tiled=True)

    depth = 1024
    base_q, base_kv = pl.pallas_call(
        base_body,
        grid=(width // depth,),
        in_specs=[
            pl.BlockSpec((all_rows, depth), lambda i: (0, i)),
            pl.BlockSpec((depth, query_cols), lambda i: (i, 0)),
            pl.BlockSpec((key_cols, depth), lambda i: (0, i)),
            pl.BlockSpec((key_cols, depth), lambda i: (0, i)),
        ],
        out_specs=(
            pl.BlockSpec((all_rows, query_cols), lambda i: (0, 0)),
            pl.BlockSpec((all_rows, 2 * key_cols), lambda i: (0, 0)),
        ),
        out_shape=(
            jax.ShapeDtypeStruct((all_rows, query_cols), F32),
            jax.ShapeDtypeStruct((all_rows, 2 * key_cols), F32),
        ),
        compiler_params=pltpu.CompilerParams(vmem_limit_bytes=LIMIT),
        cost_estimate=pl.CostEstimate(
            flops=2 * all_rows * width * (query_cols + 2 * key_cols),
            bytes_accessed=2 * width * (query_cols + 2 * key_cols + all_rows),
            transcendentals=0,
        ),
    )(x, query_matrix, key_matrix.T, value_matrix.T)

    ready = whole_call(
        functools.partial(ready_body, rank),
        jax.ShapeDtypeStruct((n, sent, HEAD), BF16),
        (
            base_q,
            base_kv,
            low,
            unplace,
            slot,
            query_up_weights.reshape(stored * rank, query_cols),
            value_up_weights.reshape(stored * rank, key_cols),
            cosine,
            sine,
            key_cosine,
            key_sine,
            send,
        ),
    )
    arrived = lax.all_to_all(ready, "serve", split_axis=0, concat_axis=0, tiled=True)

    own_lengths = lax.dynamic_slice_in_dim(lengths, index * own, own)
    context, new_keys, new_values = whole_call(
        functools.partial(attend_body, own, key_cols),
        (
            jax.ShapeDtypeStruct((n, rows * local, HEAD), BF16),
            jax.ShapeDtypeStruct((rows, KV_HEADS * HEAD), BF16),
            jax.ShapeDtypeStruct((rows, KV_HEADS * HEAD), BF16),
        ),
        (own_lengths, arrived, order, rotated_key_cache, stored_value_cache),
        smem=1,
        scratch=[pltpu.VMEM((own * HEADS * STEPS, HEAD), F32)],
    )
    context = lax.all_to_all(context, "serve", split_axis=0, concat_axis=0, tiled=True)

    tile = 1024
    kept = all_rows // cores
    kinds = jax.ShapeDtypeStruct((kept, width), F32)
    mine, other = pl.pallas_call(
        out_body,
        grid=(width // tile,),
        in_specs=[
            pl.BlockSpec(context.shape, lambda i: (0, 0, 0)),
            pl.BlockSpec(take.shape, lambda i: (0, 0)),
            pl.BlockSpec((query_cols, tile), lambda i: (0, i)),
        ],
        out_specs=(
            pl.BlockSpec((kept, tile), lambda i: (0, i)),
            pl.BlockSpec((kept, tile), lambda i: (0, i)),
        ),
        out_shape=(kinds, kinds),
        scratch_shapes=[pltpu.VMEM((all_rows, query_cols), BF16)],
        compiler_params=pltpu.CompilerParams(vmem_limit_bytes=LIMIT),
        cost_estimate=pl.CostEstimate(
            flops=2 * all_rows * width * query_cols,
            bytes_accessed=2 * width * query_cols + 4 * width * all_rows,
            transcendentals=0,
        ),
    )(context, take, output_matrix)

    total = (mine + shift(other, 0, 0, 1)).reshape(near, far, rows, width)
    nearer = total[0]
    for m in range(1, near):
        nearer = nearer + shift(total[m].astype(BF16), 0, m, 0).astype(F32)
    last = nearer[0]
    for f in range(1, far):
        last = last + shift(nearer[f].astype(BF16), f, 0, 0).astype(F32)
    out_one = (residual_first.astype(F32) + last[:own]).astype(BF16)
    out_two = (residual_second.astype(F32) + last[own:]).astype(BF16)
    shape = (own, STEPS, KV_HEADS * HEAD)
    return (out_one, out_two, new_keys.reshape(shape), new_values.reshape(shape))


def solution(mesh):
    n = mesh.shape["serve"]
    sizes = (n // 4, 2, 2)
    return jax.shard_map(
        functools.partial(shards, sizes),
        mesh=mesh,
        in_specs=(
            P(("replica", "serve"), None),
            P(("replica", "serve"), None),
            P(),
            P(None, "serve"),
            P(None, "serve"),
            P(None, "serve"),
            P("serve", None),
            P("serve", None, None),
            P("serve", None, None),
            P(None, None, "serve"),
            P(None, None, "serve"),
            P(("replica", "serve"), None, None),
            P(("replica", "serve"), None, None),
            P("replica"),
            P("replica"),
            P(),
        ),
        out_specs=(
            P(("replica", "serve"), None),
            P(("replica", "serve"), None),
            P(("replica", "serve"), None, None),
            P(("replica", "serve"), None, None),
        ),
        check_vma=False,
    )
```

time: 489 us -> 112 us (0.23)
  blocking collectives: 105 us -> 0 us
  other arithmetic: 105 us -> 8.7 us
  waiting for transfers between devices: 119 us -> 34 us
  local copies, waits for them, and re-layouts: 77.6 us -> 22.2 us
  matrix products: 34.5 us -> 0 us
  Pallas kernels: 0 us -> 20 us
  between operations: 15.4 us -> 0.99 us
  starting transfers between devices: 30.7 us -> 24.7 us
    unnamed x2 -> x0, waiting for transfers between devices: 96.1 us -> none
    unnamed x5 -> x0, other arithmetic: 95.6 us -> none
    psum x1 -> x0, blocking collectives: 61.9 us -> none  [project(): lax.psum(projected[..., query_cols + 2 * key_cols:], 'serve')]
    all_gather x2 -> x0, blocking collectives: 43.5 us -> none  [project(): piece = lax.all_gather(normed, 'serve', axis=1, tiled=True)]
    dot_general x23 -> x0, matrix products: 34.5 us -> none  [the longest x2 11.8 us: finish(): jnp.einsum('bsc,cd->bsd', heads_rows, output_matrix, preferred_element_ty...]
    ppermute x0 -> x10, waiting for transfers between devices: none -> 21.6 us  [shift(): return lax.ppermute(value, 'serve', partner(f, m, c))]
    pallas_call x0 -> x6, Pallas kernels: none -> 20 us  [the longest x1 7.21 us: shards(): pl.pallas_call(base_body, grid=(width // depth,), in_specs=[pl.BlockSpec(...]
    all_to_all x8 -> x3, starting transfers between devices: 30.6 us -> 13.5 us  [the longest x1 5.91 us: shards(): lax.all_to_all(ready, 'serve', split_axis=0, concat_axis=0, tiled=True)]
  transfers between devices with their start and end apart: 9 -> 13, of which waited for: 6 -> 8; matrix products, arithmetic and copies ran while one was open for 22% -> 10% of each run, Pallas kernels for 0% -> 7%
where the time goes in v1:
time: 112 us; the launch traced here: 111 us
  waiting for transfers between devices  34 us (30%)
  starting transfers between devices  24.7 us (22%)
  local copies, waits for them, and re-layouts  22.2 us (20%)
  Pallas kernels  20 us (18%)
  other arithmetic  8.7 us (8%)
    ppermute x10, waiting for transfers between devices, shift(): return lax.ppermute(value, 'serve', partner(f, m, c))  21.6 us
    unnamed x54, local copies, waits for them, and re-layouts  17.5 us
    ppermute x10, starting transfers between devices, shift(): return lax.ppermute(value, 'serve', partner(f, m, c))  11.2 us
    pallas_call x1, Pallas kernels, shards(): pl.pallas_call(base_body, grid=(width // depth,), in_specs=[pl.BlockSpec(...  7.21 us
    pallas_call x1, Pallas kernels, shards(): pl.pallas_call(out_body, grid=(width // tile,), in_specs=[pl.BlockSpec(co...  6.93 us
    all_to_all x1, waiting for transfers between devices, shards(): lax.all_to_all(context, 'serve', split_axis=0, concat_axis=0, tiled=True)  6.73 us
    all_to_all x1, starting transfers between devices, shards(): lax.all_to_all(ready, 'serve', split_axis=0, concat_axis=0, tiled=True)  5.91 us
    pallas_call x4, Pallas kernels, whole_call(): pl.pallas_call(body, out_shape=out_shape, in_specs=specs, out_specs=tuple...  5.88 us
  transfers between devices with their start and end apart: 13, of which 8 were waited for; matrix products, arithmetic and copies ran while one was open for 10% of the time, Pallas kernels for 7%

profile of v1, /device:TPU:0, one launch (start us, length us, event | category | flops | bytes accessed | tf_op | source)
XLA Modules:
  0.0 110.7 jit_solution(7706135230297979549)
XLA Ops:
  3.1 3.1 %collective-permute-start = (bf16[1,4,8192]{2,1,0:T(4,128)(2,1)S(1)}, bf16[1,4,8192]{2,1,0:T(4,128)(2,1)S(1)}, u32[]{:S(2)}, u32[]{:S(2)}) collective-permute-start(bf16[1,4,8192]{2,1,0:T(4,128)(2,1)S(1)} %bitcast.30), channel_id=1, source_target_pairs={{0,4},{1,5},{2,6},{3,7},{4,8},{5,9},{6,10},{7,11},{8,12},{9,13},{1... | collective-permute-start | bytes 196616 | tf_op jit(solution)/shard_map/ppermute | solution.py:266
  6.2 2.6 %collective-permute-start.1 = (bf16[1,4,8192]{2,1,0:T(4,128)(2,1)S(1)}, bf16[1,4,8192]{2,1,0:T(4,128)(2,1)S(1)}, u32[]{:S(2)}, u32[]{:S(2)}) collective-permute-start(bf16[1,4,8192]{2,1,0:T(4,128)(2,1)S(1)} %bitcast.31), channel_id=1, source_target_pairs={{0,8},{1,9},{2,10},{3,11},{4,12},{5,13},{6,14},{7,15},{8,0},{9,1},... | collective-permute-start | bytes 196616 | tf_op jit(solution)/shard_map/ppermute | solution.py:266
  8.8 1.3 %collective-permute-start.2 = (bf16[1,4,8192]{2,1,0:T(4,128)(2,1)S(1)}, bf16[1,4,8192]{2,1,0:T(4,128)(2,1)S(1)}, u32[]{:S(2)}, u32[]{:S(2)}) collective-permute-start(bf16[1,4,8192]{2,1,0:T(4,128)(2,1)S(1)} %bitcast.32), channel_id=1, source_target_pairs={{0,12},{1,13},{2,14},{3,15},{4,0},{5,1},{6,2},{7,3},{8,4},{9,5},{1... | collective-permute-start | bytes 196616 | tf_op jit(solution)/shard_map/ppermute | solution.py:266
  11.7 0.8 select_reduce_fusion
  13.9 0.8 fusion.8
  15.7 1.6 %collective-permute-start.3 = (bf16[4,4,8192]{2,1,0:T(4,128)(2,1)S(1)}, bf16[4,4,8192]{2,1,0:T(4,128)(2,1)S(1)}, u32[]{:S(2)}, u32[]{:S(2)}) collective-permute-start(bf16[4,4,8192]{2,1,0:T(4,128)(2,1)S(1)} %pad_maximum_fusion), channel_id=1, source_target_pairs={{0,2},{1,3},{2,0},{3,1},{4,6},{5,7},{6,4},{7,5},{8,10},{9,11},{10,... | collective-permute-start | bytes 786440 | tf_op jit(solution)/shard_map/ppermute | solution.py:266
  17.5 5.5 %collective-permute-done.3 = bf16[4,4,8192]{2,1,0:T(4,128)(2,1)S(1)} collective-permute-done((bf16[4,4,8192]{2,1,0:T(4,128)(2,1)S(1)}, bf16[4,4,8192]{2,1,0:T(4,128)(2,1)S(1)}, u32[]{:S(2)}, u32[]{:S(2)}) %collective-permute-start.3) | collective-permute-done | bytes 262176 | tf_op jit(solution)/shard_map/ppermute | solution.py:266
  23.3 0.8 fusion.9
  24.2 0.9 collective-permute-done.4
  25.7 1.1 %copy-done.5 = bf16[2,8192,16]{1,2,0:T(8,128)(2,1)S(1)} copy-done((bf16[2,8192,16]{1,2,0:T(8,128)(2,1)S(1)}, bf16[2,8192,16]{1,2,0:T(8,128)(2,1)}, u32[]{:S(2)}) %copy-start.5) | copy-done | bytes 524312
  26.8 1.0 copy-done.6
  30.7 4.1 %all-to-all-start = ((bf16[16,16,128]{2,1,0:T(8,128)(2,1)}), bf16[16,16,128]{2,1,0:T(8,128)(2,1)}, u32[]{:S(2)}, u32[]{:S(2)}) async-start(bf16[16,16,128]{2,1,0:T(8,128)(2,1)} %copy-done.9), calls=%async_computation | async-start | bytes 131072 | tf_op jit(solution)/shard_map/all_to_all | solution.py:339
  35.4 1.2 %copy-done.2 = bf16[8192,64]{0,1:T(8,128)(2,1)S(1)} copy-done((bf16[8192,64]{0,1:T(8,128)(2,1)S(1)}, bf16[8192,64]{0,1:T(8,128)(2,1)}, u32[]{:S(2)}) %copy-start.2) | copy-done | bytes 1048600
  36.6 1.2 %copy-done.3 = bf16[8192,64]{0,1:T(8,128)(2,1)S(1)} copy-done((bf16[8192,64]{0,1:T(8,128)(2,1)S(1)}, bf16[8192,64]{0,1:T(8,128)(2,1)}, u32[]{:S(2)}) %copy-start.3) | copy-done | bytes 1048600
  37.8 7.2 %shard_map.184 = (f32[64,512]{1,0:T(8,128)S(1)}, f32[64,128]{1,0:T(8,128)S(1)}) custom-call(bf16[64,8192]{1,0:T(8,128)(2,1)S(1)} %reshape.286.x_ref, bf16[8192,512]{1,0:T(8,128)(2,1)} %q_ref.1, bf16[64,8192]{1,0:T(8,128)(2,1)S(1)} %bitcast.28, bf16[64,8192]{1,0:T(8,128)(2,1)S(1)} %bitcast.29), custom_call_target="tpu_custom_call" | custom-call | flops 671088640 | bytes 11534336 | tf_op jit(solution)/shard_map/pallas_call | solution.py:342
  46.3 0.8 copy-done.8
  47.1 0.9 copy-done.11
  48.0 0.9 copy-done.13
  52.7 2.4 %shard_map.186 = bf16[16,32,128]{2,1,0:T(8,128)(2,1)} custom-call(f32[64,512]{1,0:T(8,128)S(1)} %copy-done.13, f32[64,128]{1,0:T(8,128)S(1)} %copy-done.24, bf16[16,16,128]{2,1,0:T(8,128)(2,1)} %all-to-all-done.low_ref, bf16[64,64]{1,0:T(8,128)(2,1)S(1)} %get-tuple-element.57.unplace_ref, s32[64,1]{1,0:T(8,128)S(1)} %copy-done.8, ...), custom_call_target="tpu_custom_call" | custom-call | tf_op jit(solution)/shard_map/pallas_call | solution.py:34
  55.1 5.9 %all-to-all-start.1 = ((bf16[16,32,128]{2,1,0:T(8,128)(2,1)}), bf16[16,32,128]{2,1,0:T(8,128)(2,1)S(1)}, u32[]{:S(2)}, u32[]{:S(2)}) async-start(bf16[16,32,128]{2,1,0:T(8,128)(2,1)} %shard_map.186), calls=%async_computation.1 | async-start | bytes 262144 | tf_op jit(solution)/shard_map/all_to_all | solution.py:385
  62.5 0.8 fusion.1.order_ref
  63.3 5.7 %all-to-all-done.1.x_ref = bf16[16,32,128]{2,1,0:T(8,128)(2,1)S(1)} async-done(((bf16[16,32,128]{2,1,0:T(8,128)(2,1)}), bf16[16,32,128]{2,1,0:T(8,128)(2,1)S(1)}, u32[]{:S(2)}, u32[]{:S(2)}) %all-to-all-start.1) | async-done | bytes 131104 | tf_op jit(solution)/shard_map/all_to_all | solution.py:385
  68.9 1.4 %copy-done.1 = bf16[2,384,1024]{2,1,0:T(8,128)(2,1)S(1)} copy-done((bf16[2,384,1024]{2,1,0:T(8,128)(2,1)S(1)}, bf16[2,384,1024]{2,1,0:T(8,128)(2,1)}, u32[]{:S(2)}) %copy-start.1) | copy-done | bytes 1572888
  70.3 2.6 %shard_map.187 = (bf16[16,16,128]{2,1,0:T(8,128)(2,1)}, bf16[4,1024]{1,0:T(4,128)(2,1)S(1)}, bf16[4,1024]{1,0:T(4,128)(2,1)S(1)}) custom-call(s32[2]{0:T(128)S(1)} %dynamic_slice.3.len_ref, bf16[16,32,128]{2,1,0:T(8,128)(2,1)S(1)} %all-to-all-done.1.x_ref, bf16[256,512]{1,0:T(8,128)(2,1)S(1)} %fusion.1.order_ref, bf16[2,384,1024]{2,1,0:T(8,128)(2,1)S(1)} %copy-done, ...), custom_call_target="tpu_custom_call" | custom-call | tf_op jit(solution)/shard_map/pallas_call | solution.py:34
  72.9 3.5 %all-to-all-start.2 = ((bf16[16,16,128]{2,1,0:T(8,128)(2,1)}), bf16[16,16,128]{2,1,0:T(8,128)(2,1)S(1)}, u32[]{:S(2)}, u32[]{:S(2)}) async-start(bf16[16,16,128]{2,1,0:T(8,128)(2,1)} %get-tuple-element.13), calls=%async_computation.2 | async-start | bytes 131072 | tf_op jit(solution)/shard_map/all_to_all | solution.py:399
  76.6 6.7 %all-to-all-done.2.ctx_ref = bf16[16,16,128]{2,1,0:T(8,128)(2,1)S(1)} async-done(((bf16[16,16,128]{2,1,0:T(8,128)(2,1)}), bf16[16,16,128]{2,1,0:T(8,128)(2,1)S(1)}, u32[]{:S(2)}, u32[]{:S(2)}) %all-to-all-start.2) | async-done | bytes 65568 | tf_op jit(solution)/shard_map/all_to_all | solution.py:399
  83.3 6.9 %shard_map.188 = (f32[32,8192]{1,0:T(8,128)S(1)}, f32[32,8192]{1,0:T(8,128)S(1)}) custom-call(bf16[16,16,128]{2,1,0:T(8,128)(2,1)S(1)} %all-to-all-done.2.ctx_ref, bf16[256,256]{1,0:T(8,128)(2,1)S(1)} %fusion.2.take_ref, bf16[512,8192]{1,0:T(8,128)(2,1)} %w_ref.1), custom_call_target="tpu_custom_call" | custom-call | flops 536870912 | bytes 10485760 | tf_op jit(solution)/shard_map/pallas_call | solution.py:404
  90.3 2.6 %collective-permute-done.5 = f32[32,8192]{1,0:T(8,128)S(1)} collective-permute-done((f32[32,8192]{1,0:T(8,128)S(1)}, f32[32,8192]{1,0:T(8,128)S(1)}, u32[]{:S(2)}, u32[]{:S(2)}) %collective-permute-start.5) | collective-permute-done | bytes 1048608 | tf_op jit(solution)/shard_map/ppermute | solution.py:266
  93.6 8.0 %collective-permute-done.6 = bf16[4,4,8192]{2,1,0:T(4,128)(2,1)S(1)} collective-permute-done((bf16[4,4,8192]{2,1,0:T(4,128)(2,1)S(1)}, bf16[4,4,8192]{2,1,0:T(4,128)(2,1)S(1)}, u32[]{:S(2)}, u32[]{:S(2)}) %collective-permute-start.6) | collective-permute-done | bytes 262176 | tf_op jit(solution)/shard_map/ppermute | solution.py:266
  102.4 1.1 collective-permute-start.8
  105.4 1.1 collective-permute-done.9
  106.5 3.4 %collective-permute-done.8 = bf16[4,8192]{1,0:T(4,128)(2,1)S(1)} collective-permute-done((bf16[4,8192]{1,0:T(4,128)(2,1)S(1)}, bf16[4,8192]{1,0:T(4,128)(2,1)S(1)}, u32[]{:S(2)}, u32[]{:S(2)}) %collective-permute-start.8) | collective-permute-done | bytes 65568 | tf_op jit(solution)/shard_map/ppermute | solution.py:266
  (102 shorter events, 21.5 us)
Async XLA Ops:
  1.4 0.8 copy-start.18
  2.1 0.8 copy-start.20
  3.1 12.3 %collective-permute-start = (bf16[1,4,8192]{2,1,0:T(4,128)(2,1)S(1)}, bf16[1,4,8192]{2,1,0:T(4,128)(2,1)S(1)}, u32[]{:S(2)}, u32[]{:S(2)}) collective-permute-start(bf16[1,4,8192]{2,1,0:T(4,128)(2,1)S(1)} %bitcast.30), channel_id=1, source_target_pairs={{0,4},{1,5},{2,6},{3,7},{4,8},{5,9},{6,10},{7,11},{8,12},{9,13},{1... | collective-permute-start | bytes 196616 | tf_op jit(solution)/shard_map/ppermute | solution.py:266
  6.2 9.3 %collective-permute-start.1 = (bf16[1,4,8192]{2,1,0:T(4,128)(2,1)S(1)}, bf16[1,4,8192]{2,1,0:T(4,128)(2,1)S(1)}, u32[]{:S(2)}, u32[]{:S(2)}) collective-permute-start(bf16[1,4,8192]{2,1,0:T(4,128)(2,1)S(1)} %bitcast.31), channel_id=1, source_target_pairs={{0,8},{1,9},{2,10},{3,11},{4,12},{5,13},{6,14},{7,15},{8,0},{9,1},... | collective-permute-start | bytes 196616 | tf_op jit(solution)/shard_map/ppermute | solution.py:266
  8.8 6.7 %collective-permute-start.2 = (bf16[1,4,8192]{2,1,0:T(4,128)(2,1)S(1)}, bf16[1,4,8192]{2,1,0:T(4,128)(2,1)S(1)}, u32[]{:S(2)}, u32[]{:S(2)}) collective-permute-start(bf16[1,4,8192]{2,1,0:T(4,128)(2,1)S(1)} %bitcast.32), channel_id=1, source_target_pairs={{0,12},{1,13},{2,14},{3,15},{4,0},{5,1},{6,2},{7,3},{8,4},{9,5},{1... | collective-permute-start | bytes 196616 | tf_op jit(solution)/shard_map/ppermute | solution.py:266
  13.3 11.9 %copy-start.7 = (s32[64,1]{1,0:T(8,128)}, s32[64,1]{1,0:T(8,128)S(1)}, u32[]{:S(2)}) copy-start(s32[64,1]{1,0:T(8,128)S(1)} %copy.26.slot_ref) | copy-start | bytes 772
  15.7 7.3 %collective-permute-start.3 = (bf16[4,4,8192]{2,1,0:T(4,128)(2,1)S(1)}, bf16[4,4,8192]{2,1,0:T(4,128)(2,1)S(1)}, u32[]{:S(2)}, u32[]{:S(2)}) collective-permute-start(bf16[4,4,8192]{2,1,0:T(4,128)(2,1)S(1)} %pad_maximum_fusion), channel_id=1, source_target_pairs={{0,2},{1,3},{2,0},{3,1},{4,6},{5,7},{6,4},{7,5},{8,10},{9,11},{10,... | collective-permute-start | bytes 786440 | tf_op jit(solution)/shard_map/ppermute | solution.py:266
  23.2 2.0 %collective-permute-start.4 = (bf16[8,4,8192]{2,1,0:T(4,128)(2,1)S(1)}, bf16[8,4,8192]{2,1,0:T(4,128)(2,1)S(1)}, u32[]{:S(2)}, u32[]{:S(2)}) collective-permute-start(bf16[8,4,8192]{2,1,0:T(4,128)(2,1)S(1)} %get-tuple-element.25), channel_id=1, source_target_pairs={{0,1},{1,0},{2,3},{3,2},{4,5},{5,4},{6,7},{7,6},{8,9},{9,8},{10,11... | collective-permute-start | bytes 1572872 | tf_op jit(solution)/shard_map/ppermute | solution.py:266
  25.1 21.2 %copy-start.4 = (bf16[32,16,512]{2,1,0:T(8,128)(2,1)S(1)}, bf16[32,16,512]{2,1,0:T(8,128)(2,1)}, u32[]{:S(2)}) copy-start(bf16[32,16,512]{2,1,0:T(8,128)(2,1)} %param.25) | copy-start | bytes 1572868
  25.7 43.3 %copy-start = (bf16[2,384,1024]{2,1,0:T(8,128)(2,1)S(1)}, bf16[2,384,1024]{2,1,0:T(8,128)(2,1)}, u32[]{:S(2)}) copy-start(bf16[2,384,1024]{2,1,0:T(8,128)(2,1)} %k_ref.1) | copy-start | bytes 4718596
  25.7 1.2 %copy-start.5 = (bf16[2,8192,16]{1,2,0:T(8,128)(2,1)S(1)}, bf16[2,8192,16]{1,2,0:T(8,128)(2,1)}, u32[]{:S(2)}) copy-start(bf16[2,8192,16]{1,2,0:T(8,128)(2,1)} %param.23) | copy-start | bytes 1572868
  26.8 1.0 copy-start.6
  27.9 0.8 copy-start.10
  30.7 15.7 %all-to-all-start = ((bf16[16,16,128]{2,1,0:T(8,128)(2,1)}), bf16[16,16,128]{2,1,0:T(8,128)(2,1)}, u32[]{:S(2)}, u32[]{:S(2)}) async-start(bf16[16,16,128]{2,1,0:T(8,128)(2,1)} %copy-done.9), calls=%async_computation | async-start | bytes 131072 | tf_op jit(solution)/shard_map/all_to_all | solution.py:339
  35.4 1.2 %copy-start.2 = (bf16[8192,64]{0,1:T(8,128)(2,1)S(1)}, bf16[8192,64]{0,1:T(8,128)(2,1)}, u32[]{:S(2)}) copy-start(bf16[8192,64]{0,1:T(8,128)(2,1)} %param.20) | copy-start | bytes 3145732
  36.6 1.2 %copy-start.3 = (bf16[8192,64]{0,1:T(8,128)(2,1)S(1)}, bf16[8192,64]{0,1:T(8,128)(2,1)}, u32[]{:S(2)}) copy-start(bf16[8192,64]{0,1:T(8,128)(2,1)} %param.21) | copy-start | bytes 3145732
  46.3 0.8 copy-start.8
  47.1 0.9 copy-start.11
  48.0 0.9 copy-start.13
  48.9 0.8 copy-start.14
  49.7 0.8 copy-start.15
  50.4 0.8 copy-start.16
  55.1 13.9 %all-to-all-start.1 = ((bf16[16,32,128]{2,1,0:T(8,128)(2,1)}), bf16[16,32,128]{2,1,0:T(8,128)(2,1)S(1)}, u32[]{:S(2)}, u32[]{:S(2)}) async-start(bf16[16,32,128]{2,1,0:T(8,128)(2,1)} %shard_map.186), calls=%async_computation.1 | async-start | bytes 262144 | tf_op jit(solution)/shard_map/all_to_all | solution.py:385
  68.9 1.4 %copy-start.1 = (bf16[2,384,1024]{2,1,0:T(8,128)(2,1)S(1)}, bf16[2,384,1024]{2,1,0:T(8,128)(2,1)}, u32[]{:S(2)}) copy-start(bf16[2,384,1024]{2,1,0:T(8,128)(2,1)} %v_ref.1) | copy-start | bytes 4718596
  72.9 10.4 %all-to-all-start.2 = ((bf16[16,16,128]{2,1,0:T(8,128)(2,1)}), bf16[16,16,128]{2,1,0:T(8,128)(2,1)S(1)}, u32[]{:S(2)}, u32[]{:S(2)}) async-start(bf16[16,16,128]{2,1,0:T(8,128)(2,1)} %get-tuple-element.13), calls=%async_computation.2 | async-start | bytes 131072 | tf_op jit(solution)/shard_map/all_to_all | solution.py:399
  76.5 33.4 %copy-start.19 = (bf16[2,8192]{1,0:T(2,128)(2,1)S(1)}, bf16[2,8192]{1,0:T(2,128)(2,1)}, u32[]{:S(2)}) copy-start(bf16[2,8192]{1,0:T(2,128)(2,1)} %first_ref.1) | copy-start | bytes 98308
  76.5 33.4 %copy-start.21 = (bf16[2,8192]{1,0:T(2,128)(2,1)S(1)}, bf16[2,8192]{1,0:T(2,128)(2,1)}, u32[]{:S(2)}) copy-start(bf16[2,8192]{1,0:T(2,128)(2,1)} %second_ref.1) | copy-start | bytes 98308
  90.2 2.7 %collective-permute-start.5 = (f32[32,8192]{1,0:T(8,128)S(1)}, f32[32,8192]{1,0:T(8,128)S(1)}, u32[]{:S(2)}, u32[]{:S(2)}) collective-permute-start(f32[32,8192]{1,0:T(8,128)S(1)} %get-tuple-element.15), channel_id=1, source_target_pairs={{0,1},{1,0},{2,3},{3,2},{4,5},{5,4},{6,7},{7,6},{8,9},{9,8},{10,11... | collective-permute-start | bytes 3145736 | tf_op jit(solution)/shard_map/ppermute | solution.py:266
  93.2 8.4 %collective-permute-start.6 = (bf16[4,4,8192]{2,1,0:T(4,128)(2,1)S(1)}, bf16[4,4,8192]{2,1,0:T(4,128)(2,1)S(1)}, u32[]{:S(2)}, u32[]{:S(2)}) collective-permute-start(bf16[4,4,8192]{2,1,0:T(4,128)(2,1)S(1)} %convert_element_type.85), channel_id=1, source_target_pairs={{0,2},{1,3},{2,0},{3,1},{4,6},{5,7},{6,4},{7,5},{8,10},{9,11},{10,... | collective-permute-start | bytes 786440 | tf_op jit(solution)/shard_map/ppermute | solution.py:266
  101.9 4.6 %collective-permute-start.9 = (bf16[4,8192]{1,0:T(4,128)(2,1)S(1)}, bf16[4,8192]{1,0:T(4,128)(2,1)S(1)}, u32[]{:S(2)}, u32[]{:S(2)}) collective-permute-start(bf16[4,8192]{1,0:T(4,128)(2,1)S(1)} %get-tuple-element.23), channel_id=1, source_target_pairs={{0,12},{1,13},{2,14},{3,15},{4,0},{5,1},{6,2},{7,3},{8,4},{9,5},{1... | collective-permute-start | bytes 196616 | tf_op jit(solution)/shard_map/ppermute | solution.py:266
  102.4 7.4 %collective-permute-start.8 = (bf16[4,8192]{1,0:T(4,128)(2,1)S(1)}, bf16[4,8192]{1,0:T(4,128)(2,1)S(1)}, u32[]{:S(2)}, u32[]{:S(2)}) collective-permute-start(bf16[4,8192]{1,0:T(4,128)(2,1)S(1)} %get-tuple-element.24), channel_id=1, source_target_pairs={{0,8},{1,9},{2,10},{3,11},{4,12},{5,13},{6,14},{7,15},{8,0},{9,1},... | collective-permute-start | bytes 196616 | tf_op jit(solution)/shard_map/ppermute | solution.py:266
  103.5 6.4 %collective-permute-start.7 = (bf16[4,8192]{1,0:T(4,128)(2,1)S(1)}, bf16[4,8192]{1,0:T(4,128)(2,1)S(1)}, u32[]{:S(2)}, u32[]{:S(2)}) collective-permute-start(bf16[4,8192]{1,0:T(4,128)(2,1)S(1)} %get-tuple-element.22), channel_id=1, source_target_pairs={{0,4},{1,5},{2,6},{3,7},{4,8},{5,9},{6,10},{7,11},{8,12},{9,13},{1... | collective-permute-start | bytes 196616 | tf_op jit(solution)/shard_map/ppermute | solution.py:266
  (6 other events, 4.1 us)

commit v2 on v1

--- a/solution.py
+++ b/solution.py
@@ -12,7 +12,7 @@
 KV_HEADS = 8
 HEAD = 128
 STEPS = 2
-LIMIT = 48 * 1024 * 1024
+LIMIT = 8 * 1024 * 1024
 NT = (((1,), (1,)), ((), ()))
 F32 = jnp.float32
 BF16 = jnp.bfloat16
@@ -48,21 +48,99 @@
     return (1.0 - smooth) * base / 8.0 + smooth * base
 
 
-def turn_tables(positions, offset, width):
-    lane = offset + jnp.arange(width)
-    angle = positions[:, None] * scaled_frequency(lane % HEAD // 2)[None, :]
-    sign = jnp.where(lane % 2 == 0, -1.0, 1.0)
-    return jnp.cos(angle), jnp.sin(angle) * sign[None, :]
-
-
 def norm_body(first_ref, second_ref, gain_ref, out_ref):
     gain = gain_ref[...].astype(F32)
-    rows = []
+    factors = []
     for ref in (first_ref, second_ref):
         values = ref[...].astype(F32)
-        factor = lax.rsqrt(jnp.mean(values * values, axis=-1, keepdims=True) + 1e-05)
-        rows.append(values * factor * gain)
-    out_ref[...] = jnp.concatenate(rows, axis=0).astype(BF16)
+        factors.append(lax.rsqrt(jnp.mean(values * values, axis=-1, keepdims=True) + 1e-05))
+    factor = jnp.concatenate(factors, axis=0)
+    for i in range(gain.shape[0]):
+        at = slice(i * HEAD, (i + 1) * HEAD)
+        values = jnp.concatenate((first_ref[:, at].astype(F32), second_ref[:, at].astype(F32)))
+        out_ref[:, at] = (values * factor * gain[i : i + 1]).astype(BF16)
+
+
+def prep_body(
+    sizes, rank, own, key_cols, adapters,
+    index_ref, length_ref, adapter_ref, slot_ref,
+    held_ref, local_ref, cos_ref, sin_ref, kcos_ref, ksin_ref, place_ref, unplace_ref, send_ref,
+    order_ref, take_ref,
+):
+    far, near, cores = sizes
+    n = far * near * cores
+    rows = own * STEPS
+    all_rows = n * rows
+    heads = HEADS // n
+    sent = send_ref.shape[0] // n
+    index = index_ref[0]
+    core_at = index % cores
+    near_at = index // cores % near
+    far_at = index // (cores * near)
+
+    def device_of(block, sign):
+        c, m, f = block // (far * near), block // far % near, block % far
+        f = (far_at + sign * f + far) % far
+        m = (near_at + sign * m + near) % near
+        c = (core_at + sign * c + cores) % cores
+        return (f * near + m) * cores + c
+
+    def iota(shape, axis):
+        return lax.broadcasted_iota(jnp.int32, shape, axis)
+
+    def split(row):
+        return row // rows, row % rows // own, row % own
+
+    block, step, mine = split(iota((all_rows, 1), 0))
+    device = device_of(block, -1)
+    request = device * own + mine
+    length = jnp.zeros_like(request)
+    adapter = jnp.zeros_like(request)
+    for j in range(length_ref.shape[0]):
+        length = jnp.where(request == j, length_ref[j], length)
+        adapter = jnp.where(request == j, adapter_ref[j], adapter)
+    slot = jnp.zeros_like(request)
+    for j in range(slot_ref.shape[0]):
+        slot = jnp.where(adapter == j, slot_ref[j], slot)
+    held_ref[...] = slot
+    local_ref[...] = slot - index * adapters
+    position = (length + step).astype(F32)
+    lane = iota((1, HEAD), 1)
+    odd = jnp.where(lane % 2 == 0, -1.0, 1.0)
+    angle = position * scaled_frequency(lane // 2)
+    cos_ref[...] = jnp.cos(angle)
+    sin_ref[...] = jnp.sin(angle) * odd
+    angle = position * scaled_frequency((index * key_cols + lane) % HEAD // 2)
+    kcos_ref[...] = jnp.where(lane < key_cols, jnp.cos(angle), 1.0)
+    ksin_ref[...] = jnp.where(lane < key_cols, jnp.sin(angle) * odd, 0.0)
+
+    def hot(ref, row, column):
+        ref[...] = jnp.where(row == column, 1.0, 0.0).astype(BF16)
+
+    absolute = (device * STEPS + step) * own + mine
+    hot(unplace_ref, absolute, iota((1, all_rows), 1))
+    block, step, mine = split(iota((1, all_rows), 1))
+    absolute = (device_of(block, -1) * STEPS + step) * own + mine
+    hot(place_ref, iota((all_rows, 1), 0), absolute)
+
+    column = iota((1, send_ref.shape[1]), 1)
+    h = column // all_rows
+    block, step, mine = split(column % all_rows)
+    wanted = device_of(block, -1) * sent + jnp.where(
+        h < heads, (mine * heads + h) * STEPS + step, rows * heads + mine * STEPS + step
+    )
+    hot(send_ref, iota((n * sent, 1), 0), wanted)
+
+    row = iota((order_ref.shape[0], 1), 0)
+    mine, head, step = row // (HEADS * STEPS), row // STEPS % HEADS, row % STEPS
+    wanted = (head // heads) * sent + (mine * heads + head % heads) * STEPS + step
+    hot(order_ref, wanted, iota((1, n * sent), 1))
+
+    row = iota((take_ref.shape[0], 1), 0)
+    h = row // all_rows
+    block, step, mine = split(row % all_rows)
+    wanted = device_of(block, 1) * rows * heads + (mine * heads + h) * STEPS + step
+    hot(take_ref, wanted, iota((1, take_ref.shape[1]), 1))
 
 
 def low_body(rank, x_ref, qd_ref, vd_ref, local_ref, place_ref, out_ref):
@@ -85,15 +163,21 @@
         out_ref[i] = packed
 
 
-def base_body(x_ref, q_ref, k_ref, v_ref, oq_ref, okv_ref):
-    @pl.when(pl.program_id(0) == 0)
-    def _():
-        oq_ref[...] = jnp.zeros_like(oq_ref)
-        okv_ref[...] = jnp.zeros_like(okv_ref)
-
-    x = x_ref[...]
-    oq_ref[...] += dot(x, q_ref[...])
-    okv_ref[...] += dot_nt(x, jnp.concatenate((k_ref[...], v_ref[...]), axis=0))
+def base_body(depth, x_ref, q_ref, k_ref, v_ref, oq_ref, okv_ref):
+    oq_ref[...] = jnp.zeros_like(oq_ref)
+    okv_ref[...] = jnp.zeros_like(okv_ref)
+    columns = k_ref.shape[0]
+    narrow = jnp.zeros((HEAD - 2 * columns, depth), BF16)
+
+    @pl.loop(0, x_ref.shape[1] // depth)
+    def _(i):
+        at = pl.ds(pl.multiple_of(i * depth, depth), depth)
+        x = x_ref[:, at]
+        oq_ref[...] += dot(x, q_ref[at, :])
+        both = (k_ref[:, at], v_ref[:, at])
+        if 2 * columns < HEAD:
+            both += (narrow,)
+        okv_ref[...] += dot_nt(x, jnp.concatenate(both, axis=0))
 
 
 def turned(values, cosine, sine):
@@ -124,30 +208,23 @@
     wide_q = jnp.where(here, dot(low, spread_q), 0.0).astype(BF16)
     wide_v = jnp.where(here, dot(low, spread_v), 0.0).astype(BF16)
     query = oq_ref[...] + dot(wide_q, uq_ref[...])
-    columns = okv_ref.shape[1] // 2
-    key = okv_ref[:, :columns]
-    value = okv_ref[:, columns:] + dot(wide_v, uv_ref[...])
+    fresh = turned(okv_ref[...], kcos_ref[...], ksin_ref[...])
+    columns = uv_ref.shape[1]
+    value = dot(wide_v, uv_ref[...])
+    pieces = [jnp.zeros((value.shape[0], columns), F32), value]
+    if 2 * columns < HEAD:
+        pieces.append(jnp.zeros((value.shape[0], HEAD - 2 * columns), F32))
+    fresh = fresh + jnp.concatenate(pieces, axis=1)
     cosine, sine = cos_ref[...], sin_ref[...]
     parts = []
     for h in range(query.shape[1] // HEAD):
         parts.append(turned(query[:, h * HEAD : (h + 1) * HEAD], cosine, sine))
-    fresh = [turned_narrow(key, kcos_ref[...], ksin_ref[...]), value]
-    if 2 * columns < HEAD:
-        fresh.append(jnp.zeros((key.shape[0], HEAD - 2 * columns), F32))
-    parts.append(jnp.concatenate(fresh, axis=1))
+    parts.append(fresh)
     stacked = jnp.concatenate(parts, axis=0).astype(BF16)
     out_ref[...] = dot(send_ref[...], stacked).astype(BF16).reshape(out_ref.shape)
 
 
-def turned_narrow(values, cosine, sine):
-    width = values.shape[1]
-    lane = lax.broadcasted_iota(jnp.int32, values.shape, 1)
-    ahead = jnp.concatenate((values[:, 1:], values[:, :1]), axis=1)
-    behind = jnp.concatenate((values[:, width - 1 :], values[:, : width - 1]), axis=1)
-    return values * cosine + jnp.where(lane % 2 == 0, ahead, behind) * sine
-
-
-def attend_body(own, columns, len_ref, x_ref, order_ref, k_ref, v_ref, ctx_ref, nk_ref, nv_ref, s_ref):
+def attend_body(own, columns, index_ref, len_ref, x_ref, order_ref, k_ref, v_ref, ctx_ref, nk_ref, nv_ref, s_ref):
     n, span = x_ref.shape[0], k_ref.shape[1]
     group = HEADS // KV_HEADS
     local = HEADS // n
@@ -181,7 +258,7 @@
         cached = jnp.concatenate(cached, axis=0) * scale
         newer = jnp.concatenate(newer, axis=0) * scale
         place = lax.broadcasted_iota(jnp.int32, cached.shape, 1)
-        cached = jnp.where(place < len_ref[b], cached, -1e30)
+        cached = jnp.where(place < len_ref[index_ref[0] * own + b], cached, -1e30)
         step = lax.broadcasted_iota(jnp.int32, newer.shape, 0) % STEPS
         at = lax.broadcasted_iota(jnp.int32, newer.shape, 1) - b * STEPS
         newer = jnp.where((at >= 0) & (at <= step), newer, -1e30)
@@ -206,20 +283,21 @@
         ctx_ref[i] = jnp.concatenate(block, axis=0).astype(BF16)
 
 
-def out_body(ctx_ref, take_ref, w_ref, mine_ref, other_ref, a_ref):
-    @pl.when(pl.program_id(0) == 0)
-    def _():
-        rows = a_ref.shape[0]
-        n = ctx_ref.shape[0]
-        x = ctx_ref[...].reshape(n * ctx_ref.shape[1], HEAD)
-        taken = dot(take_ref[...], x).astype(BF16)
-        for h in range(a_ref.shape[1] // HEAD):
-            a_ref[:, h * HEAD : (h + 1) * HEAD] = taken[h * rows : (h + 1) * rows]
-
+def out_body(tile, ctx_ref, take_ref, w_ref, mine_ref, other_ref, a_ref):
+    rows = a_ref.shape[0]
+    n = ctx_ref.shape[0]
+    x = ctx_ref[...].reshape(n * ctx_ref.shape[1], HEAD)
+    taken = dot(take_ref[...], x).astype(BF16)
+    for h in range(a_ref.shape[1] // HEAD):
+        a_ref[:, h * HEAD : (h + 1) * HEAD] = taken[h * rows : (h + 1) * rows]
     half = mine_ref.shape[0]
-    product = dot(a_ref[...], w_ref[...])
-    mine_ref[...] = product[:half]
-    other_ref[...] = product[half:]
+
+    @pl.loop(0, w_ref.shape[1] // tile)
+    def _(i):
+        at = pl.ds(pl.multiple_of(i * tile, tile), tile)
+        product = dot(a_ref[...], w_ref[:, at])
+        mine_ref[:, at] = product[:half]
+        other_ref[:, at] = product[half:]
 
 
 def shards(
@@ -265,62 +343,32 @@
     def shift(value, f, m, c):
         return lax.ppermute(value, "serve", partner(f, m, c))
 
-    core_at = index % cores
-    near_at = index // cores % near
-    far_at = index // (cores * near)
-    block = jnp.arange(n)
-    block_c, block_m, block_f = block // (far * near), block // far % near, block % far
-
-    def device_of(sign):
-        return (
-            ((far_at + sign * block_f) % far) * near + (near_at + sign * block_m) % near
-        ) * cores + (core_at + sign * block_c) % cores
-
-    source = device_of(-1)
-    target = device_of(1)
-
-    row_device = jnp.repeat(source, rows)
-    row_step = jnp.tile(jnp.repeat(jnp.arange(STEPS), own), n)
-    row_own = jnp.tile(jnp.arange(own), n * STEPS)
-    request = row_device * own + row_own
-    hot = request[:, None] == jnp.arange(lengths.shape[0])[None, :]
-    row_length = jnp.sum(jnp.where(hot, lengths[None, :], 0), axis=1)
-    row_adapter = jnp.sum(jnp.where(hot, request_adapter[None, :], 0), axis=1)
-    table = jnp.arange(adapter_slot.shape[0])
-    slot = jnp.sum(
-        jnp.where(row_adapter[:, None] == table[None, :], adapter_slot[None, :], 0), axis=1
-    )[:, None]
-    positions = (row_length + row_step).astype(F32)
-    cosine, sine = turn_tables(positions, 0, HEAD)
-    key_cosine, key_sine = turn_tables(positions, index * key_cols, key_cols)
-    absolute = (row_device * STEPS + row_step) * own + row_own
-    place = (jnp.arange(all_rows)[:, None] == absolute[None, :]).astype(BF16)
-    unplace = (absolute[:, None] == jnp.arange(all_rows)[None, :]).astype(BF16)
-
-    sent = -(-(rows * local + rows) // 16) * 16
-    wanted = [
-        row_device * sent + (row_own * local + h) * STEPS + row_step for h in range(local)
-    ]
-    wanted.append(row_device * sent + rows * local + row_own * STEPS + row_step)
-    wanted = jnp.concatenate(wanted)
-    send = (jnp.arange(n * sent)[:, None] == wanted[None, :]).astype(BF16)
-
-    a = jnp.arange(own * HEADS * STEPS)
-    a_own, a_head, a_step = a // (HEADS * STEPS), a // STEPS % HEADS, a % STEPS
-    held = (a_head // local) * sent + (a_own * local + a_head % local) * STEPS + a_step
-    order = (held[:, None] == jnp.arange(n * sent)[None, :]).astype(BF16)
-
-    out_device = jnp.repeat(target, rows)
-    came = [
-        out_device * rows * local + (row_own * local + h) * STEPS + row_step for h in range(local)
-    ]
-    came = jnp.concatenate(came)
-    take = (came[:, None] == jnp.arange(n * rows * local)[None, :]).astype(BF16)
-
-    normed = whole_call(
+    normed = pl.pallas_call(
         norm_body,
-        jax.ShapeDtypeStruct((rows, width), BF16),
-        (residual_first, residual_second, attention_norm_gain[None, :]),
+        out_shape=jax.ShapeDtypeStruct((rows, width), BF16),
+        compiler_params=pltpu.CompilerParams(vmem_limit_bytes=LIMIT),
+    )(residual_first, residual_second, attention_norm_gain.reshape(width // HEAD, HEAD))
+    sent = -(-(rows * local + rows) // 8) * 8
+    narrow = jax.ShapeDtypeStruct((all_rows, 1), jnp.int32)
+    table = jax.ShapeDtypeStruct((all_rows, HEAD), F32)
+    square = jax.ShapeDtypeStruct((all_rows, all_rows), BF16)
+    slot, near_slot, cosine, sine, key_cosine, key_sine, place, unplace, send, order, take = whole_call(
+        functools.partial(prep_body, sizes, rank, own, key_cols, adapters),
+        (
+            narrow,
+            narrow,
+            table,
+            table,
+            table,
+            table,
+            square,
+            square,
+            jax.ShapeDtypeStruct((n * sent, all_rows * (local + 1)), BF16),
+            jax.ShapeDtypeStruct((own * HEADS * STEPS, n * sent), BF16),
+            jax.ShapeDtypeStruct((all_rows * local, n * rows * local), BF16),
+        ),
+        (index[None], lengths, request_adapter, adapter_slot),
+        smem=4,
     )
     gathered = normed[None]
     gathered = jnp.concatenate([gathered] + [shift(gathered, f, 0, 0) for f in range(1, far)])
@@ -334,35 +382,18 @@
     low = whole_call(
         functools.partial(low_body, rank),
         jax.ShapeDtypeStruct((n, packed_rows, HEAD), BF16),
-        (x, query_down, value_down, slot - index * adapters, place),
+        (x, query_down, value_down, near_slot, place),
     )
     low = lax.all_to_all(low, "serve", split_axis=0, concat_axis=0, tiled=True)
 
-    depth = 1024
-    base_q, base_kv = pl.pallas_call(
-        base_body,
-        grid=(width // depth,),
-        in_specs=[
-            pl.BlockSpec((all_rows, depth), lambda i: (0, i)),
-            pl.BlockSpec((depth, query_cols), lambda i: (i, 0)),
-            pl.BlockSpec((key_cols, depth), lambda i: (0, i)),
-            pl.BlockSpec((key_cols, depth), lambda i: (0, i)),
-        ],
-        out_specs=(
-            pl.BlockSpec((all_rows, query_cols), lambda i: (0, 0)),
-            pl.BlockSpec((all_rows, 2 * key_cols), lambda i: (0, 0)),
-        ),
-        out_shape=(
+    base_q, base_kv = whole_call(
+        functools.partial(base_body, 2048),
+        (
             jax.ShapeDtypeStruct((all_rows, query_cols), F32),
-            jax.ShapeDtypeStruct((all_rows, 2 * key_cols), F32),
-        ),
-        compiler_params=pltpu.CompilerParams(vmem_limit_bytes=LIMIT),
-        cost_estimate=pl.CostEstimate(
-            flops=2 * all_rows * width * (query_cols + 2 * key_cols),
-            bytes_accessed=2 * width * (query_cols + 2 * key_cols + all_rows),
-            transcendentals=0,
-        ),
-    )(x, query_matrix, key_matrix.T, value_matrix.T)
+            jax.ShapeDtypeStruct((all_rows, HEAD), F32),
+        ),
+        (x, query_matrix, key_matrix.T, value_matrix.T),
+    )
 
     ready = whole_call(
         functools.partial(ready_body, rank),
@@ -384,7 +415,6 @@
     )
     arrived = lax.all_to_all(ready, "serve", split_axis=0, concat_axis=0, tiled=True)
 
-    own_lengths = lax.dynamic_slice_in_dim(lengths, index * own, own)
     context, new_keys, new_values = whole_call(
         functools.partial(attend_body, own, key_cols),
         (
@@ -392,36 +422,19 @@
             jax.ShapeDtypeStruct((rows, KV_HEADS * HEAD), BF16),
             jax.ShapeDtypeStruct((rows, KV_HEADS * HEAD), BF16),
         ),
-        (own_lengths, arrived, order, rotated_key_cache, stored_value_cache),
-        smem=1,
+        (index[None], lengths, arrived, order, rotated_key_cache, stored_value_cache),
+        smem=2,
         scratch=[pltpu.VMEM((own * HEADS * STEPS, HEAD), F32)],
     )
     context = lax.all_to_all(context, "serve", split_axis=0, concat_axis=0, tiled=True)
 
-    tile = 1024
-    kept = all_rows // cores
-    kinds = jax.ShapeDtypeStruct((kept, width), F32)
-    mine, other = pl.pallas_call(
-        out_body,
-        grid=(width // tile,),
-        in_specs=[
-            pl.BlockSpec(context.shape, lambda i: (0, 0, 0)),
-            pl.BlockSpec(take.shape, lambda i: (0, 0)),
-            pl.BlockSpec((query_cols, tile), lambda i: (0, i)),
-        ],
-        out_specs=(
-            pl.BlockSpec((kept, tile), lambda i: (0, i)),
-            pl.BlockSpec((kept, tile), lambda i: (0, i)),
-        ),
-        out_shape=(kinds, kinds),
-        scratch_shapes=[pltpu.VMEM((all_rows, query_cols), BF16)],
-        compiler_params=pltpu.CompilerParams(vmem_limit_bytes=LIMIT),
-        cost_estimate=pl.CostEstimate(
-            flops=2 * all_rows * width * query_cols,
-            bytes_accessed=2 * width * query_cols + 4 * width * all_rows,
-            transcendentals=0,
-        ),
-    )(context, take, output_matrix)
+    kinds = jax.ShapeDtypeStruct((all_rows // cores, width), F32)
+    mine, other = whole_call(
+        functools.partial(out_body, 1024),
+        (kinds, kinds),
+        (context, take, output_matrix),
+        scratch=[pltpu.VMEM((all_rows, query_cols), BF16)],
+    )
 
     total = (mine + shift(other, 0, 0, 1)).reshape(near, far, rows, width)
     nearer = total[0]

time: 112 us -> 114 us (1.018)
  blocking collectives: 0 us -> 22.7 us
  local copies, waits for them, and re-layouts: 22.2 us -> 39.5 us
  waiting for transfers between devices: 34 us -> 20.4 us
  Pallas kernels: 20 us -> 10.8 us
  starting transfers between devices: 24.7 us -> 16.9 us
  other arithmetic: 8.7 us -> 1.28 us
    all_to_all x0 -> x2, blocking collectives: none -> 22.7 us  [the longest x1 13.2 us: shards(): lax.all_to_all(ready, 'serve', split_axis=0, concat_axis=0, tiled=True)]
    unnamed x54 -> x80, local copies, waits for them, and re-layouts: 17.5 us -> 34.6 us
    pallas_call x2 -> x1, Pallas kernels: 14.1 us -> 0.29 us  [shards(): pl.pallas_call(norm_body, out_shape=jax.ShapeDtypeStruct((rows, width), B...]
    all_to_all x2 -> x0, waiting for transfers between devices: 12.4 us -> none  [the longest x1 6.73 us: shards(): lax.all_to_all(context, 'serve', split_axis=0, concat_axis=0, tiled=True)]
    all_to_all x2 -> x0, starting transfers between devices: 9.4 us -> none  [the longest x1 5.91 us: shards(): lax.all_to_all(ready, 'serve', split_axis=0, concat_axis=0, tiled=True)]
    pallas_call x4 -> x6, Pallas kernels: 5.88 us -> 10.5 us  [whole_call(): pl.pallas_call(body, out_shape=out_shape, in_specs=specs, out_specs=tuple...]
    mul x4 -> x0, other arithmetic: 1.7 us -> none  [the longest x2 1.66 us: turn_tables(): return (jnp.cos(angle), jnp.sin(angle) * sign[None, :])]
    convert_element_type x5 -> x0, other arithmetic: 1.6 us -> none  [the longest x1 0.79 us: shards(): order = (held[:, None] == jnp.arange(n * sent)[None, :]).astype(BF16)]
  transfers between devices with their start and end apart: 13 -> 11, of which waited for: 8 -> 7; matrix products, arithmetic and copies ran while one was open for 10% -> 4% of each run, Pallas kernels for 7% -> 4%
where the time goes in v2:
time: 114 us; the launch traced here: 113 us
  local copies, waits for them, and re-layouts  39.5 us (35%)
  blocking collectives  22.7 us (20%)
  waiting for transfers between devices  20.4 us (18%)
  starting transfers between devices  16.9 us (15%)
  Pallas kernels  10.8 us (9%)
  other arithmetic  1.28 us (1%)
    unnamed x80, local copies, waits for them, and re-layouts  34.6 us
    ppermute x10, waiting for transfers between devices, shift(): return lax.ppermute(value, 'serve', partner(f, m, c))  20.4 us
    all_to_all x1, blocking collectives, shards(): lax.all_to_all(ready, 'serve', split_axis=0, concat_axis=0, tiled=True)  13.2 us
    ppermute x10, starting transfers between devices, shift(): return lax.ppermute(value, 'serve', partner(f, m, c))  12.8 us
    pallas_call x6, Pallas kernels, whole_call(): pl.pallas_call(body, out_shape=out_shape, in_specs=specs, out_specs=tuple...  10.5 us
    all_to_all x1, blocking collectives, shards(): lax.all_to_all(context, 'serve', split_axis=0, concat_axis=0, tiled=True)  9.48 us
    all_to_all x1, starting transfers between devices, shards(): low = lax.all_to_all(low, 'serve', split_axis=0, concat_axis=0, tiled=True)  4.14 us
  transfers between devices with their start and end apart: 11, of which 7 were waited for; matrix products, arithmetic and copies ran while one was open for 4% of the time, Pallas kernels for 4%

profile of v2, /device:TPU:0, one launch (start us, length us, event | category | flops | bytes accessed | tf_op | source)
XLA Modules:
  0.0 112.5 jit_solution(13531917671868905874)
XLA Ops:
  3.2 3.1 %collective-permute-start = (bf16[1,4,8192]{2,1,0:T(4,128)(2,1)S(1)}, bf16[1,4,8192]{2,1,0:T(4,128)(2,1)S(1)}, u32[]{:S(2)}, u32[]{:S(2)}) collective-permute-start(bf16[1,4,8192]{2,1,0:T(4,128)(2,1)S(1)} %bitcast.31), channel_id=1, source_target_pairs={{0,4},{1,5},{2,6},{3,7},{4,8},{5,9},{6,10},{7,11},{8,12},{9,13},{1... | collective-permute-start | bytes 196616 | tf_op jit(solution)/shard_map/ppermute | solution.py:344
  6.2 2.6 %collective-permute-start.1 = (bf16[1,4,8192]{2,1,0:T(4,128)(2,1)S(1)}, bf16[1,4,8192]{2,1,0:T(4,128)(2,1)S(1)}, u32[]{:S(2)}, u32[]{:S(2)}) collective-permute-start(bf16[1,4,8192]{2,1,0:T(4,128)(2,1)S(1)} %bitcast.32), channel_id=1, source_target_pairs={{0,8},{1,9},{2,10},{3,11},{4,12},{5,13},{6,14},{7,15},{8,0},{9,1},... | collective-permute-start | bytes 196616 | tf_op jit(solution)/shard_map/ppermute | solution.py:344
  8.8 1.3 %collective-permute-start.2 = (bf16[1,4,8192]{2,1,0:T(4,128)(2,1)S(1)}, bf16[1,4,8192]{2,1,0:T(4,128)(2,1)S(1)}, u32[]{:S(2)}, u32[]{:S(2)}) collective-permute-start(bf16[1,4,8192]{2,1,0:T(4,128)(2,1)S(1)} %bitcast.33), channel_id=1, source_target_pairs={{0,12},{1,13},{2,14},{3,15},{4,0},{5,1},{6,2},{7,3},{8,4},{9,5},{1... | collective-permute-start | bytes 196616 | tf_op jit(solution)/shard_map/ppermute | solution.py:344
  10.8 2.5 %collective-permute-done.1 = bf16[1,4,8192]{2,1,0:T(4,128)(2,1)S(1)} collective-permute-done((bf16[1,4,8192]{2,1,0:T(4,128)(2,1)S(1)}, bf16[1,4,8192]{2,1,0:T(4,128)(2,1)S(1)}, u32[]{:S(2)}, u32[]{:S(2)}) %collective-permute-start.1) | collective-permute-done | bytes 65568 | tf_op jit(solution)/shard_map/ppermute | solution.py:344
  13.8 1.6 %collective-permute-start.3 = (bf16[4,4,8192]{2,1,0:T(4,128)(2,1)S(1)}, bf16[4,4,8192]{2,1,0:T(4,128)(2,1)S(1)}, u32[]{:S(2)}, u32[]{:S(2)}) collective-permute-start(bf16[4,4,8192]{2,1,0:T(4,128)(2,1)S(1)} %pad_maximum_fusion), channel_id=1, source_target_pairs={{0,2},{1,3},{2,0},{3,1},{4,6},{5,7},{6,4},{7,5},{8,10},{9,11},{10,... | collective-permute-start | bytes 786440 | tf_op jit(solution)/shard_map/ppermute | solution.py:344
  17.4 4.2 %collective-permute-done.3 = bf16[4,4,8192]{2,1,0:T(4,128)(2,1)S(1)} collective-permute-done((bf16[4,4,8192]{2,1,0:T(4,128)(2,1)S(1)}, bf16[4,4,8192]{2,1,0:T(4,128)(2,1)S(1)}, u32[]{:S(2)}, u32[]{:S(2)}) %collective-permute-start.3) | collective-permute-done | bytes 262176 | tf_op jit(solution)/shard_map/ppermute | solution.py:344
  24.5 1.8 %shard_map.185 = (s32[64,1]{1,0:T(8,128)S(1)}, s32[64,1]{1,0:T(8,128)S(1)}, f32[64,128]{1,0:T(8,128)S(1)}, f32[64,128]{1,0:T(8,128)S(1)}, f32[64,128]{1,0:T(8,12...) custom-call(s32[1]{0:T(128)} %bitcast.index_ref, ...), custom_call_target="tpu_custom_call" | custom-call | tf_op jit(solution)/shard_map/pallas_call | solution.py:34
  31.3 1.0 constant_dynamic-update-slice_fusion.5
  32.3 1.5 %reshape.42.x_ref = bf16[64,8192]{1,0:T(8,128)(2,1)S(1)} reshape(bf16[16,4,8192]{2,1,0:T(4,128)(2,1)} %constant_dynamic-update-slice_fusion.5) | data formatting | bytes 2097152 | tf_op jit(solution)/shard_map/reshape | solution.py:377
  33.8 1.0 copy-done.6
  34.8 1.0 copy-done.7
  37.9 4.1 %all-to-all-start = ((bf16[16,16,128]{2,1,0:T(8,128)(2,1)}), bf16[16,16,128]{2,1,0:T(8,128)(2,1)S(1)}, u32[]{:S(2)}, u32[]{:S(2)}) async-start(bf16[16,16,128]{2,1,0:T(8,128)(2,1)} %copy-done.9), calls=%async_computation | async-start | bytes 131072 | tf_op jit(solution)/shard_map/all_to_all | solution.py:387
  42.0 3.4 %copy-done = bf16[8192,512]{1,0:T(8,128)(2,1)S(1)} copy-done((bf16[8192,512]{1,0:T(8,128)(2,1)S(1)}, bf16[8192,512]{1,0:T(8,128)(2,1)}, u32[]{:S(2)}) %copy-start) | copy-done | bytes 8388632
  45.4 1.2 %copy-done.4 = bf16[8192,64]{0,1:T(8,128)(2,1)S(1)} copy-done((bf16[8192,64]{0,1:T(8,128)(2,1)S(1)}, bf16[8192,64]{0,1:T(8,128)(2,1)}, u32[]{:S(2)}) %copy-start.4) | copy-done | bytes 1048600
  46.6 1.2 %copy-done.5 = bf16[8192,64]{0,1:T(8,128)(2,1)S(1)} copy-done((bf16[8192,64]{0,1:T(8,128)(2,1)S(1)}, bf16[8192,64]{0,1:T(8,128)(2,1)}, u32[]{:S(2)}) %copy-start.5) | copy-done | bytes 1048600
  47.8 2.7 %shard_map.184 = (f32[64,512]{1,0:T(8,128)S(1)}, f32[64,128]{1,0:T(8,128)S(1)}) custom-call(bf16[64,8192]{1,0:T(8,128)(2,1)S(1)} %reshape.42.x_ref, bf16[8192,512]{1,0:T(8,128)(2,1)S(1)} %copy-done, bf16[64,8192]{1,0:T(8,128)(2,1)S(1)} %bitcast.29, bf16[64,8192]{1,0:T(8,128)(2,1)S(1)} %bitcast.30), custom_call_target="tpu_custom_call" | custom-call | tf_op jit(solution)/shard_map/pallas_call | solution.py:34
  51.2 0.9 copy-done.14
  52.1 0.9 copy-done.16
  57.6 13.2 %all_to_all.15.x_ref = bf16[16,24,128]{2,1,0:T(8,128)(2,1)S(1)} all-to-all(bf16[16,24,128]{2,1,0:T(8,128)(2,1)S(1)} %shard_map.187), channel_id=1, replica_groups=mesh['replica'=2,'serve'=16] {'serve'}, dimensions={0} | all-to-all | bytes 196608 | tf_op jit(solution)/shard_map/all_to_all | solution.py:416
  70.9 1.4 %copy-done.3 = bf16[2,384,1024]{2,1,0:T(8,128)(2,1)S(1)} copy-done((bf16[2,384,1024]{2,1,0:T(8,128)(2,1)S(1)}, bf16[2,384,1024]{2,1,0:T(8,128)(2,1)}, u32[]{:S(2)}) %copy-start.3) | copy-done | bytes 1572888
  72.3 0.9 copy-done.11
  73.9 2.0 %shard_map.188 = (bf16[16,16,128]{2,1,0:T(8,128)(2,1)S(1)}, bf16[4,1024]{1,0:T(4,128)(2,1)S(1)}, bf16[4,1024]{1,0:T(4,128)(2,1)S(1)}) custom-call(s32[1]{0:T(128)} %bitcast.index_ref, s32[32]{0:T(128)S(1)} %copy-done.35, bf16[16,24,128]{2,1,0:T(8,128)(2,1)S(1)} %all_to_all.15.x_ref, bf16[256,384]{1,0:T(8,128)(2,1)S(1)} %copy-done.11, ...), custom_call_target="tpu_custom_call" | custom-call | tf_op jit(solution)/shard_map/pallas_call | solution.py:34
  75.8 9.5 %all_to_all.16.ctx_ref = bf16[16,16,128]{2,1,0:T(8,128)(2,1)S(1)} all-to-all(bf16[16,16,128]{2,1,0:T(8,128)(2,1)S(1)} %get-tuple-element.34), channel_id=1, replica_groups=mesh['replica'=2,'serve'=16] {'serve'}, dimensions={0} | all-to-all | bytes 131072 | tf_op jit(solution)/shard_map/all_to_all | solution.py:429
  85.3 3.4 %copy-done.1 = bf16[512,8192]{1,0:T(8,128)(2,1)S(1)} copy-done((bf16[512,8192]{1,0:T(8,128)(2,1)S(1)}, bf16[512,8192]{1,0:T(8,128)(2,1)}, u32[]{:S(2)}) %copy-start.1) | copy-done | bytes 8388632
  88.7 0.9 copy-done.13
  89.6 2.6 %shard_map.189 = (f32[32,8192]{1,0:T(8,128)S(1)}, f32[32,8192]{1,0:T(8,128)S(1)}) custom-call(bf16[16,16,128]{2,1,0:T(8,128)(2,1)S(1)} %all_to_all.16.ctx_ref, bf16[256,256]{1,0:T(8,128)(2,1)S(1)} %copy-done.13, bf16[512,8192]{1,0:T(8,128)(2,1)S(1)} %copy-done.1), custom_call_target="tpu_custom_call" | custom-call | tf_op jit(solution)/shard_map/pallas_call | solution.py:34
  92.3 2.6 %collective-permute-done.5 = f32[32,8192]{1,0:T(8,128)S(1)} collective-permute-done((f32[32,8192]{1,0:T(8,128)S(1)}, f32[32,8192]{1,0:T(8,128)S(1)}, u32[]{:S(2)}, u32[]{:S(2)}) %collective-permute-start.5) | collective-permute-done | bytes 1048608 | tf_op jit(solution)/shard_map/ppermute | solution.py:344
  95.5 8.0 %collective-permute-done.6 = bf16[4,4,8192]{2,1,0:T(4,128)(2,1)S(1)} collective-permute-done((bf16[4,4,8192]{2,1,0:T(4,128)(2,1)S(1)}, bf16[4,4,8192]{2,1,0:T(4,128)(2,1)S(1)}, u32[]{:S(2)}, u32[]{:S(2)}) %collective-permute-start.6) | collective-permute-done | bytes 262176 | tf_op jit(solution)/shard_map/ppermute | solution.py:344
  104.0 0.9 collective-permute-start.8
  105.0 2.8 %collective-permute-start.9 = (bf16[4,8192]{1,0:T(4,128)(2,1)S(1)}, bf16[4,8192]{1,0:T(4,128)(2,1)S(1)}, u32[]{:S(2)}, u32[]{:S(2)}) collective-permute-start(bf16[4,8192]{1,0:T(4,128)(2,1)S(1)} %get-tuple-element.43), channel_id=1, source_target_pairs={{0,12},{1,13},{2,14},{3,15},{4,0},{5,1},{6,2},{7,3},{8,4},{9,5},{1... | collective-permute-start | bytes 196616 | tf_op jit(solution)/shard_map/ppermute | solution.py:344
  108.9 1.5 %collective-permute-done.7 = bf16[4,8192]{1,0:T(4,128)(2,1)S(1)} collective-permute-done((bf16[4,8192]{1,0:T(4,128)(2,1)S(1)}, bf16[4,8192]{1,0:T(4,128)(2,1)S(1)}, u32[]{:S(2)}, u32[]{:S(2)}) %collective-permute-start.7) | collective-permute-done | bytes 65568 | tf_op jit(solution)/shard_map/ppermute | solution.py:344
  110.4 1.3 %collective-permute-done.8 = bf16[4,8192]{1,0:T(4,128)(2,1)S(1)} collective-permute-done((bf16[4,8192]{1,0:T(4,128)(2,1)S(1)}, bf16[4,8192]{1,0:T(4,128)(2,1)S(1)}, u32[]{:S(2)}, u32[]{:S(2)}) %collective-permute-start.8) | collective-permute-done | bytes 65568 | tf_op jit(solution)/shard_map/ppermute | solution.py:344
  (94 shorter events, 24.6 us)
Async XLA Ops:
  0.6 0.8 copy-start.17
  3.2 7.7 %collective-permute-start = (bf16[1,4,8192]{2,1,0:T(4,128)(2,1)S(1)}, bf16[1,4,8192]{2,1,0:T(4,128)(2,1)S(1)}, u32[]{:S(2)}, u32[]{:S(2)}) collective-permute-start(bf16[1,4,8192]{2,1,0:T(4,128)(2,1)S(1)} %bitcast.31), channel_id=1, source_target_pairs={{0,4},{1,5},{2,6},{3,7},{4,8},{5,9},{6,10},{7,11},{8,12},{9,13},{1... | collective-permute-start | bytes 196616 | tf_op jit(solution)/shard_map/ppermute | solution.py:344
  6.2 7.1 %collective-permute-start.1 = (bf16[1,4,8192]{2,1,0:T(4,128)(2,1)S(1)}, bf16[1,4,8192]{2,1,0:T(4,128)(2,1)S(1)}, u32[]{:S(2)}, u32[]{:S(2)}) collective-permute-start(bf16[1,4,8192]{2,1,0:T(4,128)(2,1)S(1)} %bitcast.32), channel_id=1, source_target_pairs={{0,8},{1,9},{2,10},{3,11},{4,12},{5,13},{6,14},{7,15},{8,0},{9,1},... | collective-permute-start | bytes 196616 | tf_op jit(solution)/shard_map/ppermute | solution.py:344
  8.8 4.7 %collective-permute-start.2 = (bf16[1,4,8192]{2,1,0:T(4,128)(2,1)S(1)}, bf16[1,4,8192]{2,1,0:T(4,128)(2,1)S(1)}, u32[]{:S(2)}, u32[]{:S(2)}) collective-permute-start(bf16[1,4,8192]{2,1,0:T(4,128)(2,1)S(1)} %bitcast.33), channel_id=1, source_target_pairs={{0,12},{1,13},{2,14},{3,15},{4,0},{5,1},{6,2},{7,3},{8,4},{9,5},{1... | collective-permute-start | bytes 196616 | tf_op jit(solution)/shard_map/ppermute | solution.py:344
  13.8 7.9 %collective-permute-start.3 = (bf16[4,4,8192]{2,1,0:T(4,128)(2,1)S(1)}, bf16[4,4,8192]{2,1,0:T(4,128)(2,1)S(1)}, u32[]{:S(2)}, u32[]{:S(2)}) collective-permute-start(bf16[4,4,8192]{2,1,0:T(4,128)(2,1)S(1)} %pad_maximum_fusion), channel_id=1, source_target_pairs={{0,2},{1,3},{2,0},{3,1},{4,6},{5,7},{6,4},{7,5},{8,10},{9,11},{10,... | collective-permute-start | bytes 786440 | tf_op jit(solution)/shard_map/ppermute | solution.py:344
  22.5 8.7 %collective-permute-start.4 = (bf16[8,4,8192]{2,1,0:T(4,128)(2,1)S(1)}, bf16[8,4,8192]{2,1,0:T(4,128)(2,1)S(1)}, u32[]{:S(2)}, u32[]{:S(2)}) collective-permute-start(bf16[8,4,8192]{2,1,0:T(4,128)(2,1)S(1)} %get-tuple-element.45), channel_id=1, source_target_pairs={{0,1},{1,0},{2,3},{3,2},{4,5},{5,4},{6,7},{7,6},{8,9},{9,8},{10,11... | collective-permute-start | bytes 1572872 | tf_op jit(solution)/shard_map/ppermute | solution.py:344
  31.3 19.9 %copy-start.8 = (bf16[32,16,512]{2,1,0:T(8,128)(2,1)S(1)}, bf16[32,16,512]{2,1,0:T(8,128)(2,1)}, u32[]{:S(2)}) copy-start(bf16[32,16,512]{2,1,0:T(8,128)(2,1)} %param.25) | copy-start | bytes 1572868
  32.3 38.6 %copy-start.2 = (bf16[2,384,1024]{2,1,0:T(8,128)(2,1)S(1)}, bf16[2,384,1024]{2,1,0:T(8,128)(2,1)}, u32[]{:S(2)}) copy-start(bf16[2,384,1024]{2,1,0:T(8,128)(2,1)} %k_ref.1) | copy-start | bytes 4718596
  33.7 1.0 copy-start.6
  34.8 1.0 copy-start.7
  37.9 13.3 %all-to-all-start = ((bf16[16,16,128]{2,1,0:T(8,128)(2,1)}), bf16[16,16,128]{2,1,0:T(8,128)(2,1)S(1)}, u32[]{:S(2)}, u32[]{:S(2)}) async-start(bf16[16,16,128]{2,1,0:T(8,128)(2,1)} %copy-done.9), calls=%async_computation | async-start | bytes 131072 | tf_op jit(solution)/shard_map/all_to_all | solution.py:387
  42.0 3.4 %copy-start = (bf16[8192,512]{1,0:T(8,128)(2,1)S(1)}, bf16[8192,512]{1,0:T(8,128)(2,1)}, u32[]{:S(2)}) copy-start(bf16[8192,512]{1,0:T(8,128)(2,1)} %q_ref.1) | copy-start | bytes 25165828
  45.4 1.2 %copy-start.4 = (bf16[8192,64]{0,1:T(8,128)(2,1)S(1)}, bf16[8192,64]{0,1:T(8,128)(2,1)}, u32[]{:S(2)}) copy-start(bf16[8192,64]{0,1:T(8,128)(2,1)} %param.20) | copy-start | bytes 3145732
  46.6 1.2 %copy-start.5 = (bf16[8192,64]{0,1:T(8,128)(2,1)S(1)}, bf16[8192,64]{0,1:T(8,128)(2,1)}, u32[]{:S(2)}) copy-start(bf16[8192,64]{0,1:T(8,128)(2,1)} %param.21) | copy-start | bytes 3145732
  51.2 0.9 copy-start.14
  52.1 0.9 copy-start.16
  53.0 0.8 copy-start.22
  53.8 0.8 copy-start.24
  54.5 0.8 copy-start.26
  55.3 0.8 copy-start.28
  56.0 0.8 copy-start.30
  70.9 1.4 %copy-start.3 = (bf16[2,384,1024]{2,1,0:T(8,128)(2,1)S(1)}, bf16[2,384,1024]{2,1,0:T(8,128)(2,1)}, u32[]{:S(2)}) copy-start(bf16[2,384,1024]{2,1,0:T(8,128)(2,1)} %v_ref.1) | copy-start | bytes 4718596
  72.3 0.9 copy-start.11
  85.3 3.4 %copy-start.1 = (bf16[512,8192]{1,0:T(8,128)(2,1)S(1)}, bf16[512,8192]{1,0:T(8,128)(2,1)}, u32[]{:S(2)}) copy-start(bf16[512,8192]{1,0:T(8,128)(2,1)} %w_ref.1) | copy-start | bytes 25165828
  88.7 0.9 copy-start.13
  89.6 22.2 %copy-start.18 = (bf16[2,8192]{1,0:T(2,128)(2,1)S(1)}, bf16[2,8192]{1,0:T(2,128)(2,1)}, u32[]{:S(2)}) copy-start(bf16[2,8192]{1,0:T(2,128)(2,1)} %first_ref.1) | copy-start | bytes 98308
  89.6 22.2 %copy-start.20 = (bf16[2,8192]{1,0:T(2,128)(2,1)S(1)}, bf16[2,8192]{1,0:T(2,128)(2,1)}, u32[]{:S(2)}) copy-start(bf16[2,8192]{1,0:T(2,128)(2,1)} %second_ref.1) | copy-start | bytes 98308
  92.2 2.7 %collective-permute-start.5 = (f32[32,8192]{1,0:T(8,128)S(1)}, f32[32,8192]{1,0:T(8,128)S(1)}, u32[]{:S(2)}, u32[]{:S(2)}) collective-permute-start(f32[32,8192]{1,0:T(8,128)S(1)} %get-tuple-element.37), channel_id=1, source_target_pairs={{0,1},{1,0},{2,3},{3,2},{4,5},{5,4},{6,7},{7,6},{8,9},{9,8},{10,11... | collective-permute-start | bytes 3145736 | tf_op jit(solution)/shard_map/ppermute | solution.py:344
  95.2 8.4 %collective-permute-start.6 = (bf16[4,4,8192]{2,1,0:T(4,128)(2,1)S(1)}, bf16[4,4,8192]{2,1,0:T(4,128)(2,1)S(1)}, u32[]{:S(2)}, u32[]{:S(2)}) collective-permute-start(bf16[4,4,8192]{2,1,0:T(4,128)(2,1)S(1)} %convert_element_type.41), channel_id=1, source_target_pairs={{0,2},{1,3},{2,0},{3,1},{4,6},{5,7},{6,4},{7,5},{8,10},{9,11},{10,... | collective-permute-start | bytes 786440 | tf_op jit(solution)/shard_map/ppermute | solution.py:344
  103.8 6.6 %collective-permute-start.7 = (bf16[4,8192]{1,0:T(4,128)(2,1)S(1)}, bf16[4,8192]{1,0:T(4,128)(2,1)S(1)}, u32[]{:S(2)}, u32[]{:S(2)}) collective-permute-start(bf16[4,8192]{1,0:T(4,128)(2,1)S(1)} %get-tuple-element.42), channel_id=1, source_target_pairs={{0,4},{1,5},{2,6},{3,7},{4,8},{5,9},{6,10},{7,11},{8,12},{9,13},{1... | collective-permute-start | bytes 196616 | tf_op jit(solution)/shard_map/ppermute | solution.py:344
  104.0 7.7 %collective-permute-start.8 = (bf16[4,8192]{1,0:T(4,128)(2,1)S(1)}, bf16[4,8192]{1,0:T(4,128)(2,1)S(1)}, u32[]{:S(2)}, u32[]{:S(2)}) collective-permute-start(bf16[4,8192]{1,0:T(4,128)(2,1)S(1)} %get-tuple-element.44), channel_id=1, source_target_pairs={{0,8},{1,9},{2,10},{3,11},{4,12},{5,13},{6,14},{7,15},{8,0},{9,1},... | collective-permute-start | bytes 196616 | tf_op jit(solution)/shard_map/ppermute | solution.py:344
  105.0 6.8 %collective-permute-start.9 = (bf16[4,8192]{1,0:T(4,128)(2,1)S(1)}, bf16[4,8192]{1,0:T(4,128)(2,1)S(1)}, u32[]{:S(2)}, u32[]{:S(2)}) collective-permute-start(bf16[4,8192]{1,0:T(4,128)(2,1)S(1)} %get-tuple-element.43), channel_id=1, source_target_pairs={{0,12},{1,13},{2,14},{3,15},{4,0},{5,1},{6,2},{7,3},{8,4},{9,5},{1... | collective-permute-start | bytes 196616 | tf_op jit(solution)/shard_map/ppermute | solution.py:344
  (17 other events, 11.1 us)

commit v3 on v2

--- a/solution.py
+++ b/solution.py
@@ -26,9 +26,10 @@
     return lax.dot_general(a, b, NT, preferred_element_type=F32)
 
 
-def whole_call(body, out_shape, args, smem=0, scratch=()):
+def whole_call(body, out_shape, args, smem=0, hbm=0, scratch=()):
     specs = [pl.BlockSpec(memory_space=pltpu.SMEM)] * smem
-    specs += [pl.BlockSpec(memory_space=pltpu.VMEM)] * (len(args) - smem)
+    specs += [pl.BlockSpec(memory_space=pltpu.HBM)] * hbm
+    specs += [pl.BlockSpec(memory_space=pltpu.VMEM)] * (len(args) - smem - hbm)
     many = isinstance(out_shape, (tuple, list))
     vmem = pl.BlockSpec(memory_space=pltpu.VMEM)
     return pl.pallas_call(
@@ -48,7 +49,19 @@
     return (1.0 - smooth) * base / 8.0 + smooth * base
 
 
-def norm_body(first_ref, second_ref, gain_ref, out_ref):
+def fetch(pairs, sems):
+    copies = [
+        pltpu.make_async_copy(source, target, sems.at[i])
+        for i, (source, target) in enumerate(pairs)
+    ]
+    for copy in copies:
+        copy.start()
+    for copy in copies:
+        copy.wait()
+
+
+def norm_body(first_hbm, second_hbm, gain_hbm, out_ref, first_ref, second_ref, gain_ref, sems):
+    fetch(((first_hbm, first_ref), (second_hbm, second_ref), (gain_hbm, gain_ref)), sems)
     gain = gain_ref[...].astype(F32)
     factors = []
     for ref in (first_ref, second_ref):
@@ -63,10 +76,11 @@
 
 def prep_body(
     sizes, rank, own, key_cols, adapters,
-    index_ref, length_ref, adapter_ref, slot_ref,
+    index_ref, length_hbm, adapter_hbm, slot_hbm,
     held_ref, local_ref, cos_ref, sin_ref, kcos_ref, ksin_ref, place_ref, unplace_ref, send_ref,
-    order_ref, take_ref,
+    order_ref, take_ref, length_ref, adapter_ref, slot_ref, sems,
 ):
+    fetch(((length_hbm, length_ref), (adapter_hbm, adapter_ref), (slot_hbm, slot_ref)), sems)
     far, near, cores = sizes
     n = far * near * cores
     rows = own * STEPS
@@ -143,7 +157,17 @@
     hot(take_ref, wanted, iota((1, take_ref.shape[1]), 1))
 
 
-def low_body(rank, x_ref, qd_ref, vd_ref, local_ref, place_ref, out_ref):
+def low_body(rank, groups, *refs):
+    parts, (qd_ref, vd_ref, local_ref, place_ref, x_ref, out_ref) = refs[:groups], refs[groups:]
+    rows = parts[0].shape[1]
+    sets = max(1, 16 // rows)
+    for p, part in enumerate(parts):
+        for i in range(0, part.shape[0], sets):
+            at = (p * part.shape[0] + i) * rows
+            for lane in range(0, x_ref.shape[1], 1024):
+                lanes = slice(lane, lane + 1024)
+                block = [part[i + j, :, lanes].astype(F32) for j in range(sets)]
+                x_ref[at : at + sets * rows, lanes] = jnp.concatenate(block, axis=0).astype(BF16)
     adapters = qd_ref.shape[0] // rank
     maps = jnp.concatenate((qd_ref[...], vd_ref[...]), axis=0)
     low = dot_nt(x_ref[...], maps)
@@ -158,9 +182,14 @@
     pack = HEAD // (2 * rank)
     step = rows.shape[0] // pack
     packed = jnp.concatenate([rows[i * step : (i + 1) * step] for i in range(pack)], axis=1)
-    packed = packed.astype(BF16)
-    for i in range(out_ref.shape[0]):
-        out_ref[i] = packed
+    out_ref[...] = packed.astype(BF16)
+
+
+def join_body(*refs):
+    total = refs[0][...].astype(F32)
+    for ref in refs[1:-1]:
+        total = total + ref[...].astype(F32)
+    refs[-1][...] = total.astype(BF16)
 
 
 def base_body(depth, x_ref, q_ref, k_ref, v_ref, oq_ref, okv_ref):
@@ -189,10 +218,15 @@
 
 
 def ready_body(
-    rank, oq_ref, okv_ref, low_ref, unplace_ref, slot_ref, uq_ref, uv_ref, cos_ref, sin_ref,
-    kcos_ref, ksin_ref, send_ref, out_ref,
+    rank, lows, oq_ref, okv_ref, *refs
 ):
-    packed = jnp.sum(low_ref[...].astype(F32), axis=0)
+    low_refs = refs[:lows]
+    (
+        unplace_ref, slot_ref, uq_ref, uv_ref, cos_ref, sin_ref, kcos_ref, ksin_ref, send_ref, out_ref,
+    ) = refs[lows:]
+    packed = low_refs[0][...].astype(F32)
+    for ref in low_refs[1:]:
+        packed = packed + ref[...].astype(F32)
     pack = HEAD // (2 * rank)
     low = jnp.concatenate(
         [packed[:, i * 2 * rank : (i + 1) * 2 * rank] for i in range(pack)], axis=0
@@ -241,8 +275,12 @@
         pieces = fresh[g * each : (g + 1) * each]
         keys.append(jnp.concatenate([p[:, :columns] for p in pieces], axis=1))
         values.append(jnp.concatenate([p[:, columns : 2 * columns] for p in pieces], axis=1))
-    nk_ref[...] = jnp.concatenate(keys, axis=1).astype(BF16)
-    nv_ref[...] = jnp.concatenate(values, axis=1).astype(BF16)
+    new_keys = jnp.concatenate(keys, axis=1)
+    new_values = jnp.concatenate(values, axis=1)
+    for b in range(own):
+        at = slice(b * STEPS, (b + 1) * STEPS)
+        nk_ref[b] = new_keys[at].astype(BF16)
+        nv_ref[b] = new_values[at].astype(BF16)
     pad = jnp.zeros((16 - rows, HEAD), F32)
     keys = [jnp.concatenate((k, pad), axis=0).astype(BF16) for k in keys]
     values = [jnp.concatenate((v, pad), axis=0).astype(BF16) for v in values]
@@ -300,6 +338,36 @@
         other_ref[:, at] = product[half:]
 
 
+def near_body(mine_ref, came_ref, *refs):
+    rows = refs[0].shape[0]
+    total = mine_ref[...] + came_ref[...]
+    refs[0][...] = total[:rows]
+    for m, ref in enumerate(refs[1:], 1):
+        ref[...] = total[m * rows : (m + 1) * rows].astype(BF16)
+
+
+def far_body(came, *refs):
+    total = refs[0][...]
+    for ref in refs[1 : 1 + came]:
+        total = total + ref[...].astype(F32)
+    refs = refs[1 + came :]
+    rows = refs[0].shape[0]
+    refs[0][...] = total[:rows]
+    for f, ref in enumerate(refs[1:], 1):
+        ref[...] = total[f * rows : (f + 1) * rows].astype(BF16)
+
+
+def last_body(came, first_hbm, second_hbm, keep_ref, *refs):
+    one_ref, two_ref, first_ref, second_ref, sems = refs[came:]
+    fetch(((first_hbm, first_ref), (second_hbm, second_ref)), sems)
+    total = keep_ref[...]
+    for ref in refs[:came]:
+        total = total + ref[...].astype(F32)
+    own = one_ref.shape[0]
+    one_ref[...] = (first_ref[...].astype(F32) + total[:own]).astype(BF16)
+    two_ref[...] = (second_ref[...].astype(F32) + total[own:]).astype(BF16)
+
+
 def shards(
     sizes,
     residual_first,
@@ -343,11 +411,19 @@
     def shift(value, f, m, c):
         return lax.ppermute(value, "serve", partner(f, m, c))
 
-    normed = pl.pallas_call(
+    gain = attention_norm_gain.reshape(width // HEAD, HEAD)
+    normed = whole_call(
         norm_body,
-        out_shape=jax.ShapeDtypeStruct((rows, width), BF16),
-        compiler_params=pltpu.CompilerParams(vmem_limit_bytes=LIMIT),
-    )(residual_first, residual_second, attention_norm_gain.reshape(width // HEAD, HEAD))
+        jax.ShapeDtypeStruct((rows, width), BF16),
+        (residual_first, residual_second, gain),
+        hbm=3,
+        scratch=[
+            pltpu.VMEM((own, width), BF16),
+            pltpu.VMEM((own, width), BF16),
+            pltpu.VMEM(gain.shape, BF16),
+            pltpu.SemaphoreType.DMA((3,)),
+        ],
+    )
     sent = -(-(rows * local + rows) // 8) * 8
     narrow = jax.ShapeDtypeStruct((all_rows, 1), jnp.int32)
     table = jax.ShapeDtypeStruct((all_rows, HEAD), F32)
@@ -368,23 +444,34 @@
             jax.ShapeDtypeStruct((all_rows * local, n * rows * local), BF16),
         ),
         (index[None], lengths, request_adapter, adapter_slot),
-        smem=4,
-    )
-    gathered = normed[None]
-    gathered = jnp.concatenate([gathered] + [shift(gathered, f, 0, 0) for f in range(1, far)])
-    gathered = jnp.concatenate([gathered] + [shift(gathered, 0, m, 0) for m in range(1, near)])
-    gathered = jnp.concatenate([gathered] + [shift(gathered, 0, 0, c) for c in range(1, cores)])
-    x = gathered.reshape(all_rows, width)
+        smem=1,
+        hbm=3,
+        scratch=[
+            pltpu.SMEM(lengths.shape, jnp.int32),
+            pltpu.SMEM(request_adapter.shape, jnp.int32),
+            pltpu.SMEM(adapter_slot.shape, jnp.int32),
+            pltpu.SemaphoreType.DMA((3,)),
+        ],
+    )
+    normed = normed[None]
+    groups = [jnp.concatenate([normed] + [shift(normed, f, 0, 0) for f in range(1, far)])]
+    groups += [shift(groups[0], 0, m, 0) for m in range(1, near)]
+    groups += [shift(group, 0, 0, c) for c in range(1, cores) for group in groups[:near]]
 
     query_down = jnp.swapaxes(query_down_weights, 1, 2).reshape(adapters * rank, width)
     value_down = jnp.swapaxes(value_down_weights, 1, 2).reshape(adapters * rank, width)
     packed_rows = all_rows * 2 * rank // HEAD
-    low = whole_call(
-        functools.partial(low_body, rank),
-        jax.ShapeDtypeStruct((n, packed_rows, HEAD), BF16),
-        (x, query_down, value_down, near_slot, place),
-    )
-    low = lax.all_to_all(low, "serve", split_axis=0, concat_axis=0, tiled=True)
+    x, low = whole_call(
+        functools.partial(low_body, rank, len(groups)),
+        (
+            jax.ShapeDtypeStruct((all_rows, width), BF16),
+            jax.ShapeDtypeStruct((packed_rows, HEAD), BF16),
+        ),
+        (*groups, query_down, value_down, near_slot, place),
+    )
+    lows = [shift(low, 0, m, c) for m in range(near) for c in range(cores) if m + c]
+    low = whole_call(join_body, jax.ShapeDtypeStruct(low.shape, BF16), (low, *lows))
+    lows = [low] + [shift(low, f, 0, 0) for f in range(1, far)]
 
     base_q, base_kv = whole_call(
         functools.partial(base_body, 2048),
@@ -396,12 +483,12 @@
     )
 
     ready = whole_call(
-        functools.partial(ready_body, rank),
+        functools.partial(ready_body, rank, len(lows)),
         jax.ShapeDtypeStruct((n, sent, HEAD), BF16),
         (
             base_q,
             base_kv,
-            low,
+            *lows,
             unplace,
             slot,
             query_up_weights.reshape(stored * rank, query_cols),
@@ -419,8 +506,8 @@
         functools.partial(attend_body, own, key_cols),
         (
             jax.ShapeDtypeStruct((n, rows * local, HEAD), BF16),
-            jax.ShapeDtypeStruct((rows, KV_HEADS * HEAD), BF16),
-            jax.ShapeDtypeStruct((rows, KV_HEADS * HEAD), BF16),
+            jax.ShapeDtypeStruct((own, STEPS, KV_HEADS * HEAD), BF16),
+            jax.ShapeDtypeStruct((own, STEPS, KV_HEADS * HEAD), BF16),
         ),
         (index[None], lengths, arrived, order, rotated_key_cache, stored_value_cache),
         smem=2,
@@ -436,17 +523,34 @@
         scratch=[pltpu.VMEM((all_rows, query_cols), BF16)],
     )
 
-    total = (mine + shift(other, 0, 0, 1)).reshape(near, far, rows, width)
-    nearer = total[0]
-    for m in range(1, near):
-        nearer = nearer + shift(total[m].astype(BF16), 0, m, 0).astype(F32)
-    last = nearer[0]
-    for f in range(1, far):
-        last = last + shift(nearer[f].astype(BF16), f, 0, 0).astype(F32)
-    out_one = (residual_first.astype(F32) + last[:own]).astype(BF16)
-    out_two = (residual_second.astype(F32) + last[own:]).astype(BF16)
-    shape = (own, STEPS, KV_HEADS * HEAD)
-    return (out_one, out_two, new_keys.reshape(shape), new_values.reshape(shape))
+    def kind(count, dtype):
+        return jax.ShapeDtypeStruct((count * rows, width), dtype)
+
+    keep, *others = whole_call(
+        near_body,
+        (kind(far, F32),) + (kind(far, BF16),) * (near - 1),
+        (mine, shift(other, 0, 0, 1)),
+    )
+    others = [shift(other, 0, m, 0) for m, other in enumerate(others, 1)]
+    keep, *others = whole_call(
+        functools.partial(far_body, len(others)),
+        (kind(1, F32),) + (kind(1, BF16),) * (far - 1),
+        (keep, *others),
+    )
+    others = [shift(other, f, 0, 0) for f, other in enumerate(others, 1)]
+    result = jax.ShapeDtypeStruct((own, width), BF16)
+    out_one, out_two = whole_call(
+        functools.partial(last_body, len(others)),
+        (result, result),
+        (residual_first, residual_second, keep, *others),
+        hbm=2,
+        scratch=[
+            pltpu.VMEM((own, width), BF16),
+            pltpu.VMEM((own, width), BF16),
+            pltpu.SemaphoreType.DMA((2,)),
+        ],
+    )
+    return (out_one, out_two, new_keys, new_values)
 
 
 def solution(mesh):

time: 114 us -> 93.2 us (0.82)
  local copies, waits for them, and re-layouts: 39.5 us -> 12.2 us
  waiting for transfers between devices: 20.4 us -> 30 us
  blocking collectives: 22.7 us -> 20 us
  Pallas kernels: 10.8 us -> 12 us
    unnamed x80 -> x36, local copies, waits for them, and re-layouts: 34.6 us -> 12.2 us
    ppermute x10 -> x17, waiting for transfers between devices: 20.4 us -> 30 us  [shift(): return lax.ppermute(value, 'serve', partner(f, m, c))]
    ppermute x10 -> x17, starting transfers between devices: 12.8 us -> 17.5 us  [shift(): return lax.ppermute(value, 'serve', partner(f, m, c))]
    all_to_all x1 -> x0, starting transfers between devices: 4.14 us -> none  [shards(): low = lax.all_to_all(low, 'serve', split_axis=0, concat_axis=0, tiled=True)]
    all_to_all x1, blocking collectives: 13.2 us -> 10.5 us  [shards(): lax.all_to_all(ready, 'serve', split_axis=0, concat_axis=0, tiled=True)]
    reshape x3 -> x0, local copies, waits for them, and re-layouts: 2.67 us -> none  [the longest x1 1.45 us: shards(): x = gathered.reshape(all_rows, width)]
    concatenate x2 -> x0, local copies, waits for them, and re-layouts: 1.9 us -> none  [the longest x1 1.01 us: shards(): jnp.concatenate([gathered] + [shift(gathered, 0, 0, c) for c in range(1,...]
    pallas_call x6 -> x11, Pallas kernels: 10.5 us -> 12 us  [whole_call(): pl.pallas_call(body, out_shape=out_shape, in_specs=specs, out_specs=tuple...]
  transfers between devices with their start and end apart: 11 -> 17, of which waited for: 7 -> 9; matrix products, arithmetic and copies ran while one was open for 4% -> 0% of each run, Pallas kernels for 4% -> 5%
where the time goes in v3:
time: 93.2 us; the launch traced here: 92.7 us
  waiting for transfers between devices  30 us (32%)
  blocking collectives  20 us (21%)
  starting transfers between devices  17.5 us (19%)
  local copies, waits for them, and re-layouts  12.2 us (13%)
  Pallas kernels  12 us (13%)
    ppermute x17, waiting for transfers between devices, shift(): return lax.ppermute(value, 'serve', partner(f, m, c))  30 us
    ppermute x17, starting transfers between devices, shift(): return lax.ppermute(value, 'serve', partner(f, m, c))  17.5 us
    unnamed x36, local copies, waits for them, and re-layouts  12.2 us
    pallas_call x11, Pallas kernels, whole_call(): pl.pallas_call(body, out_shape=out_shape, in_specs=specs, out_specs=tuple...  12 us
    all_to_all x1, blocking collectives, shards(): lax.all_to_all(ready, 'serve', split_axis=0, concat_axis=0, tiled=True)  10.5 us
    all_to_all x1, blocking collectives, shards(): lax.all_to_all(context, 'serve', split_axis=0, concat_axis=0, tiled=True)  9.48 us
  transfers between devices with their start and end apart: 17, of which 9 were waited for; matrix products, arithmetic and copies ran while one was open for 0% of the time, Pallas kernels for 5%

profile of v3, /device:TPU:0, one launch (start us, length us, event | category | flops | bytes accessed | tf_op | source)
XLA Modules:
  0.0 92.7 jit_solution(524506599181026169)
XLA Ops:
  0.7 0.9 copy-done.9
  1.5 0.8 copy-done.11
  3.4 5.1 %collective-permute-start.2 = (bf16[1,4,8192]{2,1,0:T(4,128)(2,1)S(1)}, bf16[1,4,8192]{2,1,0:T(4,128)(2,1)S(1)}, u32[]{:S(2)}, u32[]{:S(2)}) collective-permute-start(bf16[1,4,8192]{2,1,0:T(4,128)(2,1)S(1)} %bitcast.18), channel_id=1, source_target_pairs={{0,12},{1,13},{2,14},{3,15},{4,0},{5,1},{6,2},{7,3},{8,4},{9,5},{1... | collective-permute-start | bytes 196616 | tf_op jit(solution)/shard_map/ppermute | solution.py:412
  8.5 1.0 %collective-permute-start = (bf16[1,4,8192]{2,1,0:T(4,128)(2,1)S(1)}, bf16[1,4,8192]{2,1,0:T(4,128)(2,1)S(1)}, u32[]{:S(2)}, u32[]{:S(2)}) collective-permute-start(bf16[1,4,8192]{2,1,0:T(4,128)(2,1)S(1)} %bitcast.20), channel_id=1, source_target_pairs={{0,4},{1,5},{2,6},{3,7},{4,8},{5,9},{6,10},{7,11},{8,12},{9,13},{1... | collective-permute-start | bytes 196616 | tf_op jit(solution)/shard_map/ppermute | solution.py:412
  9.5 1.5 %collective-permute-done.2 = bf16[1,4,8192]{2,1,0:T(4,128)(2,1)S(1)} collective-permute-done((bf16[1,4,8192]{2,1,0:T(4,128)(2,1)S(1)}, bf16[1,4,8192]{2,1,0:T(4,128)(2,1)S(1)}, u32[]{:S(2)}, u32[]{:S(2)}) %collective-permute-start.2) | collective-permute-done | bytes 65568 | tf_op jit(solution)/shard_map/ppermute | solution.py:412
  11.0 4.0 %collective-permute-done.1 = bf16[1,4,8192]{2,1,0:T(4,128)(2,1)S(1)} collective-permute-done((bf16[1,4,8192]{2,1,0:T(4,128)(2,1)S(1)}, bf16[1,4,8192]{2,1,0:T(4,128)(2,1)S(1)}, u32[]{:S(2)}, u32[]{:S(2)}) %collective-permute-start.1) | collective-permute-done | bytes 65568 | tf_op jit(solution)/shard_map/ppermute | solution.py:412
  15.2 1.6 %collective-permute-start.3 = (bf16[4,4,8192]{2,1,0:T(4,128)(2,1)S(1)}, bf16[4,4,8192]{2,1,0:T(4,128)(2,1)S(1)}, u32[]{:S(2)}, u32[]{:S(2)}) collective-permute-start(bf16[4,4,8192]{2,1,0:T(4,128)(2,1)S(1)} %pad_maximum_fusion.refs_0_), channel_id=1, source_target_pairs={{0,2},{1,3},{2,0},{3,1},{4,6},{5,7},{6,4},{7,5},{8,10},{9,11},{10,... | collective-permute-start | bytes 786440 | tf_op jit(solution)/shard_map/ppermute | solution.py:412
  16.8 6.5 %collective-permute-done.3.refs_1_ = bf16[4,4,8192]{2,1,0:T(4,128)(2,1)S(1)} collective-permute-done((bf16[4,4,8192]{2,1,0:T(4,128)(2,1)S(1)}, bf16[4,4,8192]{2,1,0:T(4,128)(2,1)S(1)}, u32[]{:S(2)}, u32[]{:S(2)}) %collective-permute-start.3) | collective-permute-done | bytes 262176 | tf_op jit(solution)/shard_map/ppermute | solution.py:412
  25.3 1.8 %shard_map.184 = (s32[64,1]{1,0:T(8,128)S(1)}, s32[64,1]{1,0:T(8,128)S(1)}, f32[64,128]{1,0:T(8,128)S(1)}, f32[64,128]{1,0:T(8,128)S(1)}, f32[64,128]{1,0:T(8,12...) custom-call(s32[1]{0:T(128)} %bitcast.index_ref, ...), custom_call_target="tpu_custom_call" | custom-call | tf_op jit(solution)/shard_map/pallas_call | solution.py:35
  27.1 1.0 %copy-done.6 = bf16[2,8192,16]{1,2,0:T(8,128)(2,1)S(1)} copy-done((bf16[2,8192,16]{1,2,0:T(8,128)(2,1)S(1)}, bf16[2,8192,16]{1,2,0:T(8,128)(2,1)}, u32[]{:S(2)}) %copy-start.6) | copy-done | bytes 524312
  28.2 1.0 %copy-done.7 = bf16[2,8192,16]{1,2,0:T(8,128)(2,1)S(1)} copy-done((bf16[2,8192,16]{1,2,0:T(8,128)(2,1)S(1)}, bf16[2,8192,16]{1,2,0:T(8,128)(2,1)}, u32[]{:S(2)}) %copy-start.7) | copy-done | bytes 524312
  29.9 1.6 %collective-permute-start.8 = (bf16[16,128]{1,0:T(8,128)(2,1)S(1)}, bf16[16,128]{1,0:T(8,128)(2,1)S(1)}, u32[]{:S(2)}, u32[]{:S(2)}) collective-permute-start(bf16[16,128]{1,0:T(8,128)(2,1)S(1)} %get-tuple-element.37.refs_0_), channel_id=1, source_target_pairs={{0,3},{1,2},{2,1},{3,0},{4,7},{5,6},{6,5},{7,4},{8,11},{9,10},{10,... | collective-permute-start | bytes 12296 | tf_op jit(solution)/shard_map/ppermute | solution.py:412
  32.1 0.9 collective-permute-done.8.refs_3_
  33.0 2.2 %collective-permute-done.7.refs_2_ = bf16[16,128]{1,0:T(8,128)(2,1)S(1)} collective-permute-done((bf16[16,128]{1,0:T(8,128)(2,1)S(1)}, bf16[16,128]{1,0:T(8,128)(2,1)S(1)}, u32[]{:S(2)}, u32[]{:S(2)}) %collective-permute-start.7) | collective-permute-done | bytes 4128 | tf_op jit(solution)/shard_map/ppermute | solution.py:412
  35.5 1.3 %collective-permute-start.10 = (bf16[16,128]{1,0:T(8,128)(2,1)S(1)}, bf16[16,128]{1,0:T(8,128)(2,1)S(1)}, u32[]{:S(2)}, u32[]{:S(2)}) collective-permute-start(bf16[16,128]{1,0:T(8,128)(2,1)S(1)} %shard_map.187.refs_0_), channel_id=1, source_target_pairs={{0,8},{1,9},{2,10},{3,11},{4,12},{5,13},{6,14},{7,15},{8,0},{9,1},... | collective-permute-start | bytes 12296 | tf_op jit(solution)/shard_map/ppermute | solution.py:412
  36.8 1.9 %collective-permute-start.9 = (bf16[16,128]{1,0:T(8,128)(2,1)S(1)}, bf16[16,128]{1,0:T(8,128)(2,1)S(1)}, u32[]{:S(2)}, u32[]{:S(2)}) collective-permute-start(bf16[16,128]{1,0:T(8,128)(2,1)S(1)} %shard_map.187.refs_0_), channel_id=1, source_target_pairs={{0,4},{1,5},{2,6},{3,7},{4,8},{5,9},{6,10},{7,11},{8,12},{9,13},{1... | collective-permute-start | bytes 12296 | tf_op jit(solution)/shard_map/ppermute | solution.py:412
  38.7 3.4 %copy-done = bf16[8192,512]{1,0:T(8,128)(2,1)S(1)} copy-done((bf16[8192,512]{1,0:T(8,128)(2,1)S(1)}, bf16[8192,512]{1,0:T(8,128)(2,1)}, u32[]{:S(2)}) %copy-start) | copy-done | bytes 8388632
  42.1 1.2 %copy-done.4 = bf16[8192,64]{0,1:T(8,128)(2,1)S(1)} copy-done((bf16[8192,64]{0,1:T(8,128)(2,1)S(1)}, bf16[8192,64]{0,1:T(8,128)(2,1)}, u32[]{:S(2)}) %copy-start.4) | copy-done | bytes 1048600
  43.3 1.2 %copy-done.5 = bf16[8192,64]{0,1:T(8,128)(2,1)S(1)} copy-done((bf16[8192,64]{0,1:T(8,128)(2,1)S(1)}, bf16[8192,64]{0,1:T(8,128)(2,1)}, u32[]{:S(2)}) %copy-start.5) | copy-done | bytes 1048600
  44.5 2.7 %shard_map.186 = (f32[64,512]{1,0:T(8,128)S(1)}, f32[64,128]{1,0:T(8,128)S(1)}) custom-call(bf16[64,8192]{1,0:T(8,128)(2,1)S(1)} %get-tuple-element.34.x_ref, bf16[8192,512]{1,0:T(8,128)(2,1)S(1)} %copy-done, bf16[64,8192]{1,0:T(8,128)(2,1)S(1)} %bitcast.13, bf16[64,8192]{1,0:T(8,128)(2,1)S(1)} %bitcast.14), custom_call_target="tpu_custom_call" | custom-call | tf_op jit(solution)/shard_map/pallas_call | solution.py:35
  47.3 0.8 shard_map.188
  48.1 10.5 %all_to_all.10.x_ref = bf16[16,24,128]{2,1,0:T(8,128)(2,1)S(1)} all-to-all(bf16[16,24,128]{2,1,0:T(8,128)(2,1)S(1)} %shard_map.188), channel_id=1, replica_groups=mesh['replica'=2,'serve'=16] {'serve'}, dimensions={0} | all-to-all | bytes 196608 | tf_op jit(solution)/shard_map/all_to_all | solution.py:503
  58.6 2.0 %shard_map.189 = (bf16[16,16,128]{2,1,0:T(8,128)(2,1)S(1)}, bf16[2,2,1024]{2,1,0:T(2,128)(2,1)}, bf16[2,2,1024]{2,1,0:T(2,128)(2,1)}) custom-call(s32[1]{0:T(128)} %bitcast.index_ref, s32[32]{0:T(128)S(1)} %copy-done.15, bf16[16,24,128]{2,1,0:T(8,128)(2,1)S(1)} %all_to_all.10.x_ref, bf16[256,384]{1,0:T(8,128)(2,1)S(1)} %get-tuple-element.45.order_ref, ...), custom_call_target="tpu_custom_call" | custom-call | tf_op jit(solution)/shard_map/pallas_call | solution.py:35
  60.6 9.5 %all_to_all.11.ctx_ref = bf16[16,16,128]{2,1,0:T(8,128)(2,1)S(1)} all-to-all(bf16[16,16,128]{2,1,0:T(8,128)(2,1)S(1)} %get-tuple-element.46), channel_id=1, replica_groups=mesh['replica'=2,'serve'=16] {'serve'}, dimensions={0} | all-to-all | bytes 131072 | tf_op jit(solution)/shard_map/all_to_all | solution.py:516
  70.1 2.6 %shard_map.190 = (f32[32,8192]{1,0:T(8,128)S(1)}, f32[32,8192]{1,0:T(8,128)S(1)}) custom-call(bf16[16,16,128]{2,1,0:T(8,128)(2,1)S(1)} %all_to_all.11.ctx_ref, bf16[256,256]{1,0:T(8,128)(2,1)S(1)} %get-tuple-element.47.take_ref, bf16[512,8192]{1,0:T(8,128)(2,1)S(1)} %copy-done.1), custom_call_target="tpu_custom_call" | custom-call | tf_op jit(solution)/shard_map/pallas_call | solution.py:35
  72.7 2.6 %collective-permute-done.12.came_ref = f32[32,8192]{1,0:T(8,128)S(1)} collective-permute-done((f32[32,8192]{1,0:T(8,128)S(1)}, f32[32,8192]{1,0:T(8,128)S(1)}, u32[]{:S(2)}, u32[]{:S(2)}) %collective-permute-start.12) | collective-permute-done | bytes 1048608 | tf_op jit(solution)/shard_map/ppermute | solution.py:412
  75.7 8.2 %collective-permute-done.13.refs_1_ = bf16[16,8192]{1,0:T(8,128)(2,1)S(1)} collective-permute-done((bf16[16,8192]{1,0:T(8,128)(2,1)S(1)}, bf16[16,8192]{1,0:T(8,128)(2,1)S(1)}, u32[]{:S(2)}, u32[]{:S(2)}) %collective-permute-start.13) | collective-permute-done | bytes 262176 | tf_op jit(solution)/shard_map/ppermute | solution.py:412
  84.1 0.9 %collective-permute-start.15 = (bf16[4,8192]{1,0:T(4,128)(2,1)S(1)}, bf16[4,8192]{1,0:T(4,128)(2,1)S(1)}, u32[]{:S(2)}, u32[]{:S(2)}) collective-permute-start(bf16[4,8192]{1,0:T(4,128)(2,1)S(1)} %get-tuple-element.54), channel_id=1, source_target_pairs={{0,8},{1,9},{2,10},{3,11},{4,12},{5,13},{6,14},{7,15},{8,0},{9,1},... | collective-permute-start | bytes 196616 | tf_op jit(solution)/shard_map/ppermute | solution.py:412
  85.1 2.8 %collective-permute-start.16 = (bf16[4,8192]{1,0:T(4,128)(2,1)S(1)}, bf16[4,8192]{1,0:T(4,128)(2,1)S(1)}, u32[]{:S(2)}, u32[]{:S(2)}) collective-permute-start(bf16[4,8192]{1,0:T(4,128)(2,1)S(1)} %get-tuple-element.55), channel_id=1, source_target_pairs={{0,12},{1,13},{2,14},{3,15},{4,0},{5,1},{6,2},{7,3},{8,4},{9,5},{1... | collective-permute-start | bytes 196616 | tf_op jit(solution)/shard_map/ppermute | solution.py:412
  87.8 2.7 %collective-permute-done.14.refs_0_ = bf16[4,8192]{1,0:T(4,128)(2,1)S(1)} collective-permute-done((bf16[4,8192]{1,0:T(4,128)(2,1)S(1)}, bf16[4,8192]{1,0:T(4,128)(2,1)S(1)}, u32[]{:S(2)}, u32[]{:S(2)}) %collective-permute-start.14) | collective-permute-done | bytes 65568 | tf_op jit(solution)/shard_map/ppermute | solution.py:412
  90.6 1.3 %collective-permute-done.15.refs_1_ = bf16[4,8192]{1,0:T(4,128)(2,1)S(1)} collective-permute-done((bf16[4,8192]{1,0:T(4,128)(2,1)S(1)}, bf16[4,8192]{1,0:T(4,128)(2,1)S(1)}, u32[]{:S(2)}, u32[]{:S(2)}) %collective-permute-start.15) | collective-permute-done | bytes 65568 | tf_op jit(solution)/shard_map/ppermute | solution.py:412
  91.9 0.8 shard_map.193
  (52 shorter events, 5.5 us)
Async XLA Ops:
  0.6 58.0 %copy-start.2 = (bf16[2,384,1024]{2,1,0:T(8,128)(2,1)S(1)}, bf16[2,384,1024]{2,1,0:T(8,128)(2,1)}, u32[]{:S(2)}) copy-start(bf16[2,384,1024]{2,1,0:T(8,128)(2,1)} %k_ref.1) | copy-start | bytes 4718596
  0.6 0.9 copy-start.9
  1.5 0.8 copy-start.11
  2.3 0.7 copy-start.14
  3.4 7.6 %collective-permute-start.2 = (bf16[1,4,8192]{2,1,0:T(4,128)(2,1)S(1)}, bf16[1,4,8192]{2,1,0:T(4,128)(2,1)S(1)}, u32[]{:S(2)}, u32[]{:S(2)}) collective-permute-start(bf16[1,4,8192]{2,1,0:T(4,128)(2,1)S(1)} %bitcast.18), channel_id=1, source_target_pairs={{0,12},{1,13},{2,14},{3,15},{4,0},{5,1},{6,2},{7,3},{8,4},{9,5},{1... | collective-permute-start | bytes 196616 | tf_op jit(solution)/shard_map/ppermute | solution.py:412
  8.5 6.5 %collective-permute-start.1 = (bf16[1,4,8192]{2,1,0:T(4,128)(2,1)S(1)}, bf16[1,4,8192]{2,1,0:T(4,128)(2,1)S(1)}, u32[]{:S(2)}, u32[]{:S(2)}) collective-permute-start(bf16[1,4,8192]{2,1,0:T(4,128)(2,1)S(1)} %bitcast.19), channel_id=1, source_target_pairs={{0,8},{1,9},{2,10},{3,11},{4,12},{5,13},{6,14},{7,15},{8,0},{9,1},... | collective-permute-start | bytes 196616 | tf_op jit(solution)/shard_map/ppermute | solution.py:412
  8.5 6.5 %collective-permute-start = (bf16[1,4,8192]{2,1,0:T(4,128)(2,1)S(1)}, bf16[1,4,8192]{2,1,0:T(4,128)(2,1)S(1)}, u32[]{:S(2)}, u32[]{:S(2)}) collective-permute-start(bf16[1,4,8192]{2,1,0:T(4,128)(2,1)S(1)} %bitcast.20), channel_id=1, source_target_pairs={{0,4},{1,5},{2,6},{3,7},{4,8},{5,9},{6,10},{7,11},{8,12},{9,13},{1... | collective-permute-start | bytes 196616 | tf_op jit(solution)/shard_map/ppermute | solution.py:412
  15.2 8.1 %collective-permute-start.3 = (bf16[4,4,8192]{2,1,0:T(4,128)(2,1)S(1)}, bf16[4,4,8192]{2,1,0:T(4,128)(2,1)S(1)}, u32[]{:S(2)}, u32[]{:S(2)}) collective-permute-start(bf16[4,4,8192]{2,1,0:T(4,128)(2,1)S(1)} %pad_maximum_fusion.refs_0_), channel_id=1, source_target_pairs={{0,2},{1,3},{2,0},{3,1},{4,6},{5,7},{6,4},{7,5},{8,10},{9,11},{10,... | collective-permute-start | bytes 786440 | tf_op jit(solution)/shard_map/ppermute | solution.py:412
  16.8 10.3 %collective-permute-start.4 = (bf16[4,4,8192]{2,1,0:T(4,128)(2,1)S(1)}, bf16[4,4,8192]{2,1,0:T(4,128)(2,1)S(1)}, u32[]{:S(2)}, u32[]{:S(2)}) collective-permute-start(bf16[4,4,8192]{2,1,0:T(4,128)(2,1)S(1)} %pad_maximum_fusion.refs_0_), channel_id=1, source_target_pairs={{0,1},{1,0},{2,3},{3,2},{4,5},{5,4},{6,7},{7,6},{8,9},{9,8},{10,11... | collective-permute-start | bytes 786440 | tf_op jit(solution)/shard_map/ppermute | solution.py:412
  23.3 3.8 %collective-permute-start.5 = (bf16[4,4,8192]{2,1,0:T(4,128)(2,1)S(1)}, bf16[4,4,8192]{2,1,0:T(4,128)(2,1)S(1)}, u32[]{:S(2)}, u32[]{:S(2)}) collective-permute-start(bf16[4,4,8192]{2,1,0:T(4,128)(2,1)S(1)} %collective-permute-done.3.refs_1_), channel_id=1, source_target_pairs={{0,1},{1,0},{2,3},{3,2},{4,5},{5,4},{6,7},{7,6},{8,9},{9,8},{10,11... | collective-permute-start | bytes 786440 | tf_op jit(solution)/shard_map/ppermute | solution.py:412
  27.1 1.0 %copy-start.6 = (bf16[2,8192,16]{1,2,0:T(8,128)(2,1)S(1)}, bf16[2,8192,16]{1,2,0:T(8,128)(2,1)}, u32[]{:S(2)}) copy-start(bf16[2,8192,16]{1,2,0:T(8,128)(2,1)} %param.23) | copy-start | bytes 1572868
  28.2 1.0 %copy-start.7 = (bf16[2,8192,16]{1,2,0:T(8,128)(2,1)S(1)}, bf16[2,8192,16]{1,2,0:T(8,128)(2,1)}, u32[]{:S(2)}) copy-start(bf16[2,8192,16]{1,2,0:T(8,128)(2,1)} %param.24) | copy-start | bytes 1572868
  29.2 18.1 %copy-start.8 = (bf16[32,16,512]{2,1,0:T(8,128)(2,1)S(1)}, bf16[32,16,512]{2,1,0:T(8,128)(2,1)}, u32[]{:S(2)}) copy-start(bf16[32,16,512]{2,1,0:T(8,128)(2,1)} %param.25) | copy-start | bytes 1572868
  29.2 18.1 %copy-start.13 = (bf16[32,16,64]{2,1,0:T(8,128)(2,1)S(1)}, bf16[32,16,64]{2,1,0:T(8,128)(2,1)}, u32[]{:S(2)}) copy-start(bf16[32,16,64]{2,1,0:T(8,128)(2,1)} %param.26) | copy-start | bytes 196612
  29.9 3.0 %collective-permute-start.8 = (bf16[16,128]{1,0:T(8,128)(2,1)S(1)}, bf16[16,128]{1,0:T(8,128)(2,1)S(1)}, u32[]{:S(2)}, u32[]{:S(2)}) collective-permute-start(bf16[16,128]{1,0:T(8,128)(2,1)S(1)} %get-tuple-element.37.refs_0_), channel_id=1, source_target_pairs={{0,3},{1,2},{2,1},{3,0},{4,7},{5,6},{6,5},{7,4},{8,11},{9,10},{10,... | collective-permute-start | bytes 12296 | tf_op jit(solution)/shard_map/ppermute | solution.py:412
  31.6 3.6 %collective-permute-start.7 = (bf16[16,128]{1,0:T(8,128)(2,1)S(1)}, bf16[16,128]{1,0:T(8,128)(2,1)S(1)}, u32[]{:S(2)}, u32[]{:S(2)}) collective-permute-start(bf16[16,128]{1,0:T(8,128)(2,1)S(1)} %get-tuple-element.37.refs_0_), channel_id=1, source_target_pairs={{0,2},{1,3},{2,0},{3,1},{4,6},{5,7},{6,4},{7,5},{8,10},{9,11},{10,... | collective-permute-start | bytes 12296 | tf_op jit(solution)/shard_map/ppermute | solution.py:412
  32.1 3.1 %collective-permute-start.6 = (bf16[16,128]{1,0:T(8,128)(2,1)S(1)}, bf16[16,128]{1,0:T(8,128)(2,1)S(1)}, u32[]{:S(2)}, u32[]{:S(2)}) collective-permute-start(bf16[16,128]{1,0:T(8,128)(2,1)S(1)} %get-tuple-element.37.refs_0_), channel_id=1, source_target_pairs={{0,1},{1,0},{2,3},{3,2},{4,5},{5,4},{6,7},{7,6},{8,9},{9,8},{10,11... | collective-permute-start | bytes 12296 | tf_op jit(solution)/shard_map/ppermute | solution.py:412
  35.2 12.0 %collective-permute-start.11 = (bf16[16,128]{1,0:T(8,128)(2,1)S(1)}, bf16[16,128]{1,0:T(8,128)(2,1)S(1)}, u32[]{:S(2)}, u32[]{:S(2)}) collective-permute-start(bf16[16,128]{1,0:T(8,128)(2,1)S(1)} %shard_map.187.refs_0_), channel_id=1, source_target_pairs={{0,12},{1,13},{2,14},{3,15},{4,0},{5,1},{6,2},{7,3},{8,4},{9,5},{1... | collective-permute-start | bytes 12296 | tf_op jit(solution)/shard_map/ppermute | solution.py:412
  35.5 11.8 %collective-permute-start.10 = (bf16[16,128]{1,0:T(8,128)(2,1)S(1)}, bf16[16,128]{1,0:T(8,128)(2,1)S(1)}, u32[]{:S(2)}, u32[]{:S(2)}) collective-permute-start(bf16[16,128]{1,0:T(8,128)(2,1)S(1)} %shard_map.187.refs_0_), channel_id=1, source_target_pairs={{0,8},{1,9},{2,10},{3,11},{4,12},{5,13},{6,14},{7,15},{8,0},{9,1},... | collective-permute-start | bytes 12296 | tf_op jit(solution)/shard_map/ppermute | solution.py:412
  36.8 10.5 %collective-permute-start.9 = (bf16[16,128]{1,0:T(8,128)(2,1)S(1)}, bf16[16,128]{1,0:T(8,128)(2,1)S(1)}, u32[]{:S(2)}, u32[]{:S(2)}) collective-permute-start(bf16[16,128]{1,0:T(8,128)(2,1)S(1)} %shard_map.187.refs_0_), channel_id=1, source_target_pairs={{0,4},{1,5},{2,6},{3,7},{4,8},{5,9},{6,10},{7,11},{8,12},{9,13},{1... | collective-permute-start | bytes 12296 | tf_op jit(solution)/shard_map/ppermute | solution.py:412
  38.7 3.4 %copy-start = (bf16[8192,512]{1,0:T(8,128)(2,1)S(1)}, bf16[8192,512]{1,0:T(8,128)(2,1)}, u32[]{:S(2)}) copy-start(bf16[8192,512]{1,0:T(8,128)(2,1)} %q_ref.1) | copy-start | bytes 25165828
  42.1 1.2 %copy-start.4 = (bf16[8192,64]{0,1:T(8,128)(2,1)S(1)}, bf16[8192,64]{0,1:T(8,128)(2,1)}, u32[]{:S(2)}) copy-start(bf16[8192,64]{0,1:T(8,128)(2,1)} %param.20) | copy-start | bytes 3145732
  43.3 1.2 %copy-start.5 = (bf16[8192,64]{0,1:T(8,128)(2,1)S(1)}, bf16[8192,64]{0,1:T(8,128)(2,1)}, u32[]{:S(2)}) copy-start(bf16[8192,64]{0,1:T(8,128)(2,1)} %param.21) | copy-start | bytes 3145732
  44.5 14.1 %copy-start.3 = (bf16[2,384,1024]{2,1,0:T(8,128)(2,1)S(1)}, bf16[2,384,1024]{2,1,0:T(8,128)(2,1)}, u32[]{:S(2)}) copy-start(bf16[2,384,1024]{2,1,0:T(8,128)(2,1)} %v_ref.1) | copy-start | bytes 4718596
  44.5 25.5 %copy-start.1 = (bf16[512,8192]{1,0:T(8,128)(2,1)S(1)}, bf16[512,8192]{1,0:T(8,128)(2,1)}, u32[]{:S(2)}) copy-start(bf16[512,8192]{1,0:T(8,128)(2,1)} %w_ref.1) | copy-start | bytes 25165828
  47.2 44.7 %copy-start.10 = (bf16[2,8192]{1,0:T(2,128)(2,1)S(1)}, bf16[2,8192]{1,0:T(2,128)(2,1)}, u32[]{:S(2)}) copy-start(bf16[2,8192]{1,0:T(2,128)(2,1)} %first_hbm.3) | copy-start | bytes 98308
  47.2 44.7 %copy-start.12 = (bf16[2,8192]{1,0:T(2,128)(2,1)S(1)}, bf16[2,8192]{1,0:T(2,128)(2,1)}, u32[]{:S(2)}) copy-start(bf16[2,8192]{1,0:T(2,128)(2,1)} %second_hbm.3) | copy-start | bytes 98308
  72.7 2.7 %collective-permute-start.12 = (f32[32,8192]{1,0:T(8,128)S(1)}, f32[32,8192]{1,0:T(8,128)S(1)}, u32[]{:S(2)}, u32[]{:S(2)}) collective-permute-start(f32[32,8192]{1,0:T(8,128)S(1)} %get-tuple-element.49), channel_id=1, source_target_pairs={{0,1},{1,0},{2,3},{3,2},{4,5},{5,4},{6,7},{7,6},{8,9},{9,8},{10,11... | collective-permute-start | bytes 3145736 | tf_op jit(solution)/shard_map/ppermute | solution.py:412
  75.5 8.4 %collective-permute-start.13 = (bf16[16,8192]{1,0:T(8,128)(2,1)S(1)}, bf16[16,8192]{1,0:T(8,128)(2,1)S(1)}, u32[]{:S(2)}, u32[]{:S(2)}) collective-permute-start(bf16[16,8192]{1,0:T(8,128)(2,1)S(1)} %get-tuple-element.51), channel_id=1, source_target_pairs={{0,2},{1,3},{2,0},{3,1},{4,6},{5,7},{6,4},{7,5},{8,10},{9,11},{10,... | collective-permute-start | bytes 786440 | tf_op jit(solution)/shard_map/ppermute | solution.py:412
  84.0 6.6 %collective-permute-start.14 = (bf16[4,8192]{1,0:T(4,128)(2,1)S(1)}, bf16[4,8192]{1,0:T(4,128)(2,1)S(1)}, u32[]{:S(2)}, u32[]{:S(2)}) collective-permute-start(bf16[4,8192]{1,0:T(4,128)(2,1)S(1)} %get-tuple-element.53), channel_id=1, source_target_pairs={{0,4},{1,5},{2,6},{3,7},{4,8},{5,9},{6,10},{7,11},{8,12},{9,13},{1... | collective-permute-start | bytes 196616 | tf_op jit(solution)/shard_map/ppermute | solution.py:412
  84.1 7.7 %collective-permute-start.15 = (bf16[4,8192]{1,0:T(4,128)(2,1)S(1)}, bf16[4,8192]{1,0:T(4,128)(2,1)S(1)}, u32[]{:S(2)}, u32[]{:S(2)}) collective-permute-start(bf16[4,8192]{1,0:T(4,128)(2,1)S(1)} %get-tuple-element.54), channel_id=1, source_target_pairs={{0,8},{1,9},{2,10},{3,11},{4,12},{5,13},{6,14},{7,15},{8,0},{9,1},... | collective-permute-start | bytes 196616 | tf_op jit(solution)/shard_map/ppermute | solution.py:412
  85.1 6.8 %collective-permute-start.16 = (bf16[4,8192]{1,0:T(4,128)(2,1)S(1)}, bf16[4,8192]{1,0:T(4,128)(2,1)S(1)}, u32[]{:S(2)}, u32[]{:S(2)}) collective-permute-start(bf16[4,8192]{1,0:T(4,128)(2,1)S(1)} %get-tuple-element.55), channel_id=1, source_target_pairs={{0,12},{1,13},{2,14},{3,15},{4,0},{5,1},{6,2},{7,3},{8,4},{9,5},{1... | collective-permute-start | bytes 196616 | tf_op jit(solution)/shard_map/ppermute | solution.py:412
  (3 other events, 2.0 us)

commit v4 on v3

--- a/solution.py
+++ b/solution.py
@@ -13,6 +13,7 @@
 HEAD = 128
 STEPS = 2
 LIMIT = 8 * 1024 * 1024
+PEAK = 1.15e9
 NT = (((1,), (1,)), ((), ()))
 F32 = jnp.float32
 BF16 = jnp.bfloat16
@@ -26,7 +27,7 @@
     return lax.dot_general(a, b, NT, preferred_element_type=F32)
 
 
-def whole_call(body, out_shape, args, smem=0, hbm=0, scratch=()):
+def whole_call(body, out_shape, args, cost, smem=0, hbm=0, scratch=()):
     specs = [pl.BlockSpec(memory_space=pltpu.SMEM)] * smem
     specs += [pl.BlockSpec(memory_space=pltpu.HBM)] * hbm
     specs += [pl.BlockSpec(memory_space=pltpu.VMEM)] * (len(args) - smem - hbm)
@@ -39,6 +40,9 @@
         out_specs=tuple(vmem for _ in out_shape) if many else vmem,
         scratch_shapes=list(scratch),
         compiler_params=pltpu.CompilerParams(vmem_limit_bytes=LIMIT),
+        cost_estimate=pl.CostEstimate(
+            flops=int(cost * PEAK), bytes_accessed=0, transcendentals=0
+        ),
     )(*args)
 
 
@@ -357,9 +361,8 @@
         ref[...] = total[f * rows : (f + 1) * rows].astype(BF16)
 
 
-def last_body(came, first_hbm, second_hbm, keep_ref, *refs):
-    one_ref, two_ref, first_ref, second_ref, sems = refs[came:]
-    fetch(((first_hbm, first_ref), (second_hbm, second_ref)), sems)
+def last_body(came, first_ref, second_ref, keep_ref, *refs):
+    one_ref, two_ref = refs[came:]
     total = keep_ref[...]
     for ref in refs[:came]:
         total = total + ref[...].astype(F32)
@@ -423,7 +426,13 @@
             pltpu.VMEM(gain.shape, BF16),
             pltpu.SemaphoreType.DMA((3,)),
         ],
-    )
+        cost=1.0,
+    )
+    normed = normed[None]
+    groups = [jnp.concatenate([normed] + [shift(normed, f, 0, 0) for f in range(1, far)])]
+    groups += [shift(groups[0], 0, m, 0) for m in range(1, near)]
+
+    groups[0], at = lax.optimization_barrier((groups[0], index[None]))
     sent = -(-(rows * local + rows) // 8) * 8
     narrow = jax.ShapeDtypeStruct((all_rows, 1), jnp.int32)
     table = jax.ShapeDtypeStruct((all_rows, HEAD), F32)
@@ -443,7 +452,7 @@
             jax.ShapeDtypeStruct((own * HEADS * STEPS, n * sent), BF16),
             jax.ShapeDtypeStruct((all_rows * local, n * rows * local), BF16),
         ),
-        (index[None], lengths, request_adapter, adapter_slot),
+        (at, lengths, request_adapter, adapter_slot),
         smem=1,
         hbm=3,
         scratch=[
@@ -452,10 +461,10 @@
             pltpu.SMEM(adapter_slot.shape, jnp.int32),
             pltpu.SemaphoreType.DMA((3,)),
         ],
-    )
-    normed = normed[None]
-    groups = [jnp.concatenate([normed] + [shift(normed, f, 0, 0) for f in range(1, far)])]
-    groups += [shift(groups[0], 0, m, 0) for m in range(1, near)]
+        cost=4.0,
+    )
+    slot, groups[1] = lax.optimization_barrier((slot, groups[1]))
+
     groups += [shift(group, 0, 0, c) for c in range(1, cores) for group in groups[:near]]
 
     query_down = jnp.swapaxes(query_down_weights, 1, 2).reshape(adapters * rank, width)
@@ -468,9 +477,12 @@
             jax.ShapeDtypeStruct((packed_rows, HEAD), BF16),
         ),
         (*groups, query_down, value_down, near_slot, place),
+        cost=0.3,
     )
     lows = [shift(low, 0, m, c) for m in range(near) for c in range(cores) if m + c]
-    low = whole_call(join_body, jax.ShapeDtypeStruct(low.shape, BF16), (low, *lows))
+    low = whole_call(
+        join_body, jax.ShapeDtypeStruct(low.shape, BF16), (low, *lows), cost=0.1
+    )
     lows = [low] + [shift(low, f, 0, 0) for f in range(1, far)]
 
     base_q, base_kv = whole_call(
@@ -480,6 +492,7 @@
             jax.ShapeDtypeStruct((all_rows, HEAD), F32),
         ),
         (x, query_matrix, key_matrix.T, value_matrix.T),
+        cost=0.6,
     )
 
     ready = whole_call(
@@ -499,6 +512,7 @@
             key_sine,
             send,
         ),
+        cost=0.9,
     )
     arrived = lax.all_to_all(ready, "serve", split_axis=0, concat_axis=0, tiled=True)
 
@@ -512,6 +526,7 @@
         (index[None], lengths, arrived, order, rotated_key_cache, stored_value_cache),
         smem=2,
         scratch=[pltpu.VMEM((own * HEADS * STEPS, HEAD), F32)],
+        cost=1.0,
     )
     context = lax.all_to_all(context, "serve", split_axis=0, concat_axis=0, tiled=True)
 
@@ -521,6 +536,7 @@
         (kinds, kinds),
         (context, take, output_matrix),
         scratch=[pltpu.VMEM((all_rows, query_cols), BF16)],
+        cost=0.5,
     )
 
     def kind(count, dtype):
@@ -530,12 +546,14 @@
         near_body,
         (kind(far, F32),) + (kind(far, BF16),) * (near - 1),
         (mine, shift(other, 0, 0, 1)),
+        cost=0.1,
     )
     others = [shift(other, 0, m, 0) for m, other in enumerate(others, 1)]
     keep, *others = whole_call(
         functools.partial(far_body, len(others)),
         (kind(1, F32),) + (kind(1, BF16),) * (far - 1),
         (keep, *others),
+        cost=0.1,
     )
     others = [shift(other, f, 0, 0) for f, other in enumerate(others, 1)]
     result = jax.ShapeDtypeStruct((own, width), BF16)
@@ -543,12 +561,7 @@
         functools.partial(last_body, len(others)),
         (result, result),
         (residual_first, residual_second, keep, *others),
-        hbm=2,
-        scratch=[
-            pltpu.VMEM((own, width), BF16),
-            pltpu.VMEM((own, width), BF16),
-            pltpu.SemaphoreType.DMA((2,)),
-        ],
+        cost=0.1,
     )
     return (out_one, out_two, new_keys, new_values)
 

time: 93.2 us -> 82.7 us (0.89)
  local copies, waits for them, and re-layouts: 12.2 us -> 5.64 us
  waiting for transfers between devices: 30 us -> 26.8 us
    unnamed x36 -> x42, local copies, waits for them, and re-layouts: 12.2 us -> 5.64 us
    ppermute x17, waiting for transfers between devices: 30 us -> 26.8 us  [shift(): return lax.ppermute(value, 'serve', partner(f, m, c))]
  transfers between devices with their start and end apart: 17 -> 17, of which waited for: 9 -> 11; matrix products, arithmetic and copies ran while one was open for 0% -> 0% of each run, Pallas kernels for 5% -> 5%
where the time goes in v4:
time: 82.7 us; the launch traced here: 82.3 us
  waiting for transfers between devices  26.8 us (32%)
  blocking collectives  19.5 us (24%)
  starting transfers between devices  17.3 us (21%)
  Pallas kernels  11.9 us (14%)
  local copies, waits for them, and re-layouts  5.64 us (7%)
  between operations  0.85 us (1%)
    ppermute x17, waiting for transfers between devices, shift(): return lax.ppermute(value, 'serve', partner(f, m, c))  26.8 us
    ppermute x17, starting transfers between devices, shift(): return lax.ppermute(value, 'serve', partner(f, m, c))  17.3 us
    pallas_call x11, Pallas kernels, whole_call(): pl.pallas_call(body, out_shape=out_shape, in_specs=specs, out_specs=tuple...  11.9 us
    all_to_all x1, blocking collectives, shards(): lax.all_to_all(ready, 'serve', split_axis=0, concat_axis=0, tiled=True)  9.99 us
    all_to_all x1, blocking collectives, shards(): lax.all_to_all(context, 'serve', split_axis=0, concat_axis=0, tiled=True)  9.48 us
    unnamed x42, local copies, waits for them, and re-layouts  5.64 us
  transfers between devices with their start and end apart: 17, of which 11 were waited for; matrix products, arithmetic and copies ran while one was open for 0% of the time, Pallas kernels for 5%

profile of v4, /device:TPU:0, one launch (start us, length us, event | category | flops | bytes accessed | tf_op | source)
XLA Modules:
  0.0 82.3 jit_solution(4241695703335541370)
XLA Ops:
  0.6 0.7 copy-done.8
  1.4 0.8 copy-done.10
  2.2 0.7 copy-done.12
  3.3 5.1 %collective-permute-start.2 = (bf16[1,4,8192]{2,1,0:T(4,128)(2,1)S(1)}, bf16[1,4,8192]{2,1,0:T(4,128)(2,1)S(1)}, u32[]{:S(2)}, u32[]{:S(2)}) collective-permute-start(bf16[1,4,8192]{2,1,0:T(4,128)(2,1)S(1)} %bitcast.21), channel_id=1, source_target_pairs={{0,12},{1,13},{2,14},{3,15},{4,0},{5,1},{6,2},{7,3},{8,4},{9,5},{1... | collective-permute-start | bytes 196616 | tf_op jit(solution)/shard_map/ppermute | solution.py:415
  8.4 1.0 %collective-permute-start = (bf16[1,4,8192]{2,1,0:T(4,128)(2,1)S(1)}, bf16[1,4,8192]{2,1,0:T(4,128)(2,1)S(1)}, u32[]{:S(2)}, u32[]{:S(2)}) collective-permute-start(bf16[1,4,8192]{2,1,0:T(4,128)(2,1)S(1)} %bitcast.23), channel_id=1, source_target_pairs={{0,4},{1,5},{2,6},{3,7},{4,8},{5,9},{6,10},{7,11},{8,12},{9,13},{1... | collective-permute-start | bytes 196616 | tf_op jit(solution)/shard_map/ppermute | solution.py:415
  9.4 1.5 %collective-permute-done.2 = bf16[1,4,8192]{2,1,0:T(4,128)(2,1)S(1)} collective-permute-done((bf16[1,4,8192]{2,1,0:T(4,128)(2,1)S(1)}, bf16[1,4,8192]{2,1,0:T(4,128)(2,1)S(1)}, u32[]{:S(2)}, u32[]{:S(2)}) %collective-permute-start.2) | collective-permute-done | bytes 65568 | tf_op jit(solution)/shard_map/ppermute | solution.py:415
  10.9 4.0 %collective-permute-done.1 = bf16[1,4,8192]{2,1,0:T(4,128)(2,1)S(1)} collective-permute-done((bf16[1,4,8192]{2,1,0:T(4,128)(2,1)S(1)}, bf16[1,4,8192]{2,1,0:T(4,128)(2,1)S(1)}, u32[]{:S(2)}, u32[]{:S(2)}) %collective-permute-start.1) | collective-permute-done | bytes 65568 | tf_op jit(solution)/shard_map/ppermute | solution.py:415
  15.1 1.6 %collective-permute-start.3 = (bf16[4,4,8192]{2,1,0:T(4,128)(2,1)S(1)}, bf16[4,4,8192]{2,1,0:T(4,128)(2,1)S(1)}, u32[]{:S(2)}, u32[]{:S(2)}) collective-permute-start(bf16[4,4,8192]{2,1,0:T(4,128)(2,1)S(1)} %pad_maximum_fusion.refs_0_), channel_id=1, source_target_pairs={{0,2},{1,3},{2,0},{3,1},{4,6},{5,7},{6,4},{7,5},{8,10},{9,11},{10,... | collective-permute-start | bytes 786440 | tf_op jit(solution)/shard_map/ppermute | solution.py:415
  16.8 0.8 copy-done.13
  17.6 1.1 %copy-done.14 = s32[32]{0:T(128)S(1)} copy-done((s32[32]{0:T(128)S(1)}, s32[32]{0:T(128)}, u32[]{:S(2)}) %copy-start.14) | copy-done | bytes 152
  18.7 1.4 %copy-done.15 = s32[32]{0:T(128)S(1)} copy-done((s32[32]{0:T(128)S(1)}, s32[32]{0:T(128)}, u32[]{:S(2)}) %copy-start.15) | copy-done | bytes 152
  20.1 1.8 %shard_map.184 = (s32[64,1]{1,0:T(8,128)S(1)}, s32[64,1]{1,0:T(8,128)S(1)}, f32[64,128]{1,0:T(8,128)S(1)}, f32[64,128]{1,0:T(8,128)S(1)}, f32[64,128]{1,0:T(8,12...) custom-call(s32[1]{0:T(128)} %bitcast.index_ref, ...), custom_call_target="tpu_custom_call" | custom-call | flops 4600000000 | tf_op jit(solution)/shard_map/pallas_call | solution.py:36
  22.0 1.2 %collective-permute-done.3.refs_1_ = bf16[4,4,8192]{2,1,0:T(4,128)(2,1)S(1)} collective-permute-done((bf16[4,4,8192]{2,1,0:T(4,128)(2,1)S(1)}, bf16[4,4,8192]{2,1,0:T(4,128)(2,1)S(1)}, u32[]{:S(2)}, u32[]{:S(2)}) %collective-permute-start.3) | collective-permute-done | bytes 262176 | tf_op jit(solution)/shard_map/ppermute | solution.py:415
  23.2 1.5 %collective-permute-done.5.refs_3_ = bf16[4,4,8192]{2,1,0:T(4,128)(2,1)S(1)} collective-permute-done((bf16[4,4,8192]{2,1,0:T(4,128)(2,1)S(1)}, bf16[4,4,8192]{2,1,0:T(4,128)(2,1)S(1)}, u32[]{:S(2)}, u32[]{:S(2)}) %collective-permute-start.5) | collective-permute-done | bytes 262176 | tf_op jit(solution)/shard_map/ppermute | solution.py:415
  24.7 0.7 shard_map.185
  25.5 1.3 %collective-permute-start.8 = (bf16[16,128]{1,0:T(8,128)(2,1)S(1)}, bf16[16,128]{1,0:T(8,128)(2,1)S(1)}, u32[]{:S(2)}, u32[]{:S(2)}) collective-permute-start(bf16[16,128]{1,0:T(8,128)(2,1)S(1)} %get-tuple-element.45.refs_0_), channel_id=1, source_target_pairs={{0,3},{1,2},{2,1},{3,0},{4,7},{5,6},{6,5},{7,4},{8,11},{9,10},{10,... | collective-permute-start | bytes 12296 | tf_op jit(solution)/shard_map/ppermute | solution.py:415
  27.4 1.2 %collective-permute-done.8.refs_3_ = bf16[16,128]{1,0:T(8,128)(2,1)S(1)} collective-permute-done((bf16[16,128]{1,0:T(8,128)(2,1)S(1)}, bf16[16,128]{1,0:T(8,128)(2,1)S(1)}, u32[]{:S(2)}, u32[]{:S(2)}) %collective-permute-start.8) | collective-permute-done | bytes 4128 | tf_op jit(solution)/shard_map/ppermute | solution.py:415
  28.6 1.9 %collective-permute-done.7.refs_2_ = bf16[16,128]{1,0:T(8,128)(2,1)S(1)} collective-permute-done((bf16[16,128]{1,0:T(8,128)(2,1)S(1)}, bf16[16,128]{1,0:T(8,128)(2,1)S(1)}, u32[]{:S(2)}, u32[]{:S(2)}) %collective-permute-start.7) | collective-permute-done | bytes 4128 | tf_op jit(solution)/shard_map/ppermute | solution.py:415
  30.7 1.3 %collective-permute-start.10 = (bf16[16,128]{1,0:T(8,128)(2,1)S(1)}, bf16[16,128]{1,0:T(8,128)(2,1)S(1)}, u32[]{:S(2)}, u32[]{:S(2)}) collective-permute-start(bf16[16,128]{1,0:T(8,128)(2,1)S(1)} %shard_map.187.refs_0_), channel_id=1, source_target_pairs={{0,8},{1,9},{2,10},{3,11},{4,12},{5,13},{6,14},{7,15},{8,0},{9,1},... | collective-permute-start | bytes 12296 | tf_op jit(solution)/shard_map/ppermute | solution.py:415
  32.0 1.9 %collective-permute-start.9 = (bf16[16,128]{1,0:T(8,128)(2,1)S(1)}, bf16[16,128]{1,0:T(8,128)(2,1)S(1)}, u32[]{:S(2)}, u32[]{:S(2)}) collective-permute-start(bf16[16,128]{1,0:T(8,128)(2,1)S(1)} %shard_map.187.refs_0_), channel_id=1, source_target_pairs={{0,4},{1,5},{2,6},{3,7},{4,8},{5,9},{6,10},{7,11},{8,12},{9,13},{1... | collective-permute-start | bytes 12296 | tf_op jit(solution)/shard_map/ppermute | solution.py:415
  34.0 2.7 %shard_map.186 = (f32[64,512]{1,0:T(8,128)S(1)}, f32[64,128]{1,0:T(8,128)S(1)}) custom-call(bf16[64,8192]{1,0:T(8,128)(2,1)S(1)} %get-tuple-element.42.x_ref, bf16[8192,512]{1,0:T(8,128)(2,1)S(1)} %bitcast.14, bf16[64,8192]{1,0:T(8,128)(2,1)S(1)} %bitcast.17, bf16[64,8192]{1,0:T(8,128)(2,1)S(1)} %bitcast.18), custom_call_target="tpu_custom_call" | custom-call | flops 690000000 | tf_op jit(solution)/shard_map/pallas_call | solution.py:36
  37.4 0.8 %shard_map.188 = bf16[16,24,128]{2,1,0:T(8,128)(2,1)S(1)} custom-call(f32[64,512]{1,0:T(8,128)S(1)} %get-tuple-element.43.oq_ref, f32[64,128]{1,0:T(8,128)S(1)} %get-tuple-element.44.okv_ref, bf16[16,128]{1,0:T(8,128)(2,1)S(1)} %shard_map.187.refs_0_, bf16[16,128]{1,0:T(8,128)(2,1)S(1)} %collective-permute-done.9.refs_1_, ...), custom_call_target="tpu_custom_call" | custom-call | flops 1035000000 | tf_op jit(solution)/shard_map/pallas_call | solution.py:36
  38.3 10.0 %all_to_all.10.x_ref = bf16[16,24,128]{2,1,0:T(8,128)(2,1)S(1)} all-to-all(bf16[16,24,128]{2,1,0:T(8,128)(2,1)S(1)} %shard_map.188), channel_id=1, replica_groups=mesh['replica'=2,'serve'=16] {'serve'}, dimensions={0} | all-to-all | bytes 196608 | tf_op jit(solution)/shard_map/all_to_all | solution.py:517
  48.3 2.0 %shard_map.189 = (bf16[16,16,128]{2,1,0:T(8,128)(2,1)S(1)}, bf16[2,2,1024]{2,1,0:T(2,128)(2,1)}, bf16[2,2,1024]{2,1,0:T(2,128)(2,1)}) custom-call(s32[1]{0:T(128)} %bitcast.index_ref, s32[32]{0:T(128)S(1)} %copy-done.16, bf16[16,24,128]{2,1,0:T(8,128)(2,1)S(1)} %all_to_all.10.x_ref, bf16[256,384]{1,0:T(8,128)(2,1)S(1)} %get-tuple-element.53.order_ref, ...), custom_call_target="tpu_custom_call" | custom-call | flops 1150000000 | tf_op jit(solution)/shard_map/pallas_call | solution.py:36
  50.3 9.5 %all_to_all.11.ctx_ref = bf16[16,16,128]{2,1,0:T(8,128)(2,1)S(1)} all-to-all(bf16[16,16,128]{2,1,0:T(8,128)(2,1)S(1)} %get-tuple-element.54), channel_id=1, replica_groups=mesh['replica'=2,'serve'=16] {'serve'}, dimensions={0} | all-to-all | bytes 131072 | tf_op jit(solution)/shard_map/all_to_all | solution.py:531
  59.8 2.6 %shard_map.190 = (f32[32,8192]{1,0:T(8,128)S(1)}, f32[32,8192]{1,0:T(8,128)S(1)}) custom-call(bf16[16,16,128]{2,1,0:T(8,128)(2,1)S(1)} %all_to_all.11.ctx_ref, bf16[256,256]{1,0:T(8,128)(2,1)S(1)} %get-tuple-element.55.take_ref, bf16[512,8192]{1,0:T(8,128)(2,1)S(1)} %bitcast.16), custom_call_target="tpu_custom_call" | custom-call | flops 575000000 | tf_op jit(solution)/shard_map/pallas_call | solution.py:36
  62.4 2.6 %collective-permute-done.12.came_ref = f32[32,8192]{1,0:T(8,128)S(1)} collective-permute-done((f32[32,8192]{1,0:T(8,128)S(1)}, f32[32,8192]{1,0:T(8,128)S(1)}, u32[]{:S(2)}, u32[]{:S(2)}) %collective-permute-start.12) | collective-permute-done | bytes 1048608 | tf_op jit(solution)/shard_map/ppermute | solution.py:415
  65.3 8.2 %collective-permute-done.13.refs_1_ = bf16[16,8192]{1,0:T(8,128)(2,1)S(1)} collective-permute-done((bf16[16,8192]{1,0:T(8,128)(2,1)S(1)}, bf16[16,8192]{1,0:T(8,128)(2,1)S(1)}, u32[]{:S(2)}, u32[]{:S(2)}) %collective-permute-start.13) | collective-permute-done | bytes 262176 | tf_op jit(solution)/shard_map/ppermute | solution.py:415
  73.8 0.9 %collective-permute-start.15 = (bf16[4,8192]{1,0:T(4,128)(2,1)S(1)}, bf16[4,8192]{1,0:T(4,128)(2,1)S(1)}, u32[]{:S(2)}, u32[]{:S(2)}) collective-permute-start(bf16[4,8192]{1,0:T(4,128)(2,1)S(1)} %get-tuple-element.62), channel_id=1, source_target_pairs={{0,8},{1,9},{2,10},{3,11},{4,12},{5,13},{6,14},{7,15},{8,0},{9,1},... | collective-permute-start | bytes 196616 | tf_op jit(solution)/shard_map/ppermute | solution.py:415
  74.8 2.8 %collective-permute-start.16 = (bf16[4,8192]{1,0:T(4,128)(2,1)S(1)}, bf16[4,8192]{1,0:T(4,128)(2,1)S(1)}, u32[]{:S(2)}, u32[]{:S(2)}) collective-permute-start(bf16[4,8192]{1,0:T(4,128)(2,1)S(1)} %get-tuple-element.63), channel_id=1, source_target_pairs={{0,12},{1,13},{2,14},{3,15},{4,0},{5,1},{6,2},{7,3},{8,4},{9,5},{1... | collective-permute-start | bytes 196616 | tf_op jit(solution)/shard_map/ppermute | solution.py:415
  77.5 2.7 %collective-permute-done.14.refs_0_ = bf16[4,8192]{1,0:T(4,128)(2,1)S(1)} collective-permute-done((bf16[4,8192]{1,0:T(4,128)(2,1)S(1)}, bf16[4,8192]{1,0:T(4,128)(2,1)S(1)}, u32[]{:S(2)}, u32[]{:S(2)}) %collective-permute-start.14) | collective-permute-done | bytes 65568 | tf_op jit(solution)/shard_map/ppermute | solution.py:415
  80.3 1.3 %collective-permute-done.15.refs_1_ = bf16[4,8192]{1,0:T(4,128)(2,1)S(1)} collective-permute-done((bf16[4,8192]{1,0:T(4,128)(2,1)S(1)}, bf16[4,8192]{1,0:T(4,128)(2,1)S(1)}, u32[]{:S(2)}, u32[]{:S(2)}) %collective-permute-start.15) | collective-permute-done | bytes 65568 | tf_op jit(solution)/shard_map/ppermute | solution.py:415
  (60 shorter events, 3.7 us)
Async XLA Ops:
  3.3 7.6 %collective-permute-start.2 = (bf16[1,4,8192]{2,1,0:T(4,128)(2,1)S(1)}, bf16[1,4,8192]{2,1,0:T(4,128)(2,1)S(1)}, u32[]{:S(2)}, u32[]{:S(2)}) collective-permute-start(bf16[1,4,8192]{2,1,0:T(4,128)(2,1)S(1)} %bitcast.21), channel_id=1, source_target_pairs={{0,12},{1,13},{2,14},{3,15},{4,0},{5,1},{6,2},{7,3},{8,4},{9,5},{1... | collective-permute-start | bytes 196616 | tf_op jit(solution)/shard_map/ppermute | solution.py:415
  8.4 6.5 %collective-permute-start.1 = (bf16[1,4,8192]{2,1,0:T(4,128)(2,1)S(1)}, bf16[1,4,8192]{2,1,0:T(4,128)(2,1)S(1)}, u32[]{:S(2)}, u32[]{:S(2)}) collective-permute-start(bf16[1,4,8192]{2,1,0:T(4,128)(2,1)S(1)} %bitcast.22), channel_id=1, source_target_pairs={{0,8},{1,9},{2,10},{3,11},{4,12},{5,13},{6,14},{7,15},{8,0},{9,1},... | collective-permute-start | bytes 196616 | tf_op jit(solution)/shard_map/ppermute | solution.py:415
  8.4 6.5 %collective-permute-start = (bf16[1,4,8192]{2,1,0:T(4,128)(2,1)S(1)}, bf16[1,4,8192]{2,1,0:T(4,128)(2,1)S(1)}, u32[]{:S(2)}, u32[]{:S(2)}) collective-permute-start(bf16[1,4,8192]{2,1,0:T(4,128)(2,1)S(1)} %bitcast.23), channel_id=1, source_target_pairs={{0,4},{1,5},{2,6},{3,7},{4,8},{5,9},{6,10},{7,11},{8,12},{9,13},{1... | collective-permute-start | bytes 196616 | tf_op jit(solution)/shard_map/ppermute | solution.py:415
  15.1 8.1 %collective-permute-start.3 = (bf16[4,4,8192]{2,1,0:T(4,128)(2,1)S(1)}, bf16[4,4,8192]{2,1,0:T(4,128)(2,1)S(1)}, u32[]{:S(2)}, u32[]{:S(2)}) collective-permute-start(bf16[4,4,8192]{2,1,0:T(4,128)(2,1)S(1)} %pad_maximum_fusion.refs_0_), channel_id=1, source_target_pairs={{0,2},{1,3},{2,0},{3,1},{4,6},{5,7},{6,4},{7,5},{8,10},{9,11},{10,... | collective-permute-start | bytes 786440 | tf_op jit(solution)/shard_map/ppermute | solution.py:415
  16.7 17.3 %slice-start = ((s8[8388608]{0:T(1024)(128)(4,1)}), s8[4194304]{0:T(1024)(128)(4,1)S(1)}, s32[]{:S(2)}) async-start(s8[8388608]{0:T(1024)(128)(4,1)} %bitcast.13), calls=%async_computation.2 | async-start | bytes 8388608
  16.7 8.1 %copy-start.2 = (bf16[2,8192,16]{1,2,0:T(8,128)(2,1)S(1)}, bf16[2,8192,16]{1,2,0:T(8,128)(2,1)}, u32[]{:S(2)}) copy-start(bf16[2,8192,16]{1,2,0:T(8,128)(2,1)} %param.23) | copy-start | bytes 1572868
  16.7 8.1 %copy-start.3 = (bf16[2,8192,16]{1,2,0:T(8,128)(2,1)S(1)}, bf16[2,8192,16]{1,2,0:T(8,128)(2,1)}, u32[]{:S(2)}) copy-start(bf16[2,8192,16]{1,2,0:T(8,128)(2,1)} %param.24) | copy-start | bytes 1572868
  16.7 17.3 %slice-start.1 = ((s8[8388608]{0:T(1024)(128)(4,1)}), s8[4194304]{0:T(1024)(128)(4,1)S(1)}, s32[]{:S(2)}) async-start(s8[8388608]{0:T(1024)(128)(4,1)} %bitcast.13), calls=%async_computation.3 | async-start | bytes 8388608
  16.7 17.3 %copy-start = (bf16[8192,64]{0,1:T(8,128)(2,1)S(1)}, bf16[8192,64]{0,1:T(8,128)(2,1)}, u32[]{:S(2)}) copy-start(bf16[8192,64]{0,1:T(8,128)(2,1)} %param.20) | copy-start | bytes 3145732
  16.7 17.3 %copy-start.1 = (bf16[8192,64]{0,1:T(8,128)(2,1)S(1)}, bf16[8192,64]{0,1:T(8,128)(2,1)}, u32[]{:S(2)}) copy-start(bf16[8192,64]{0,1:T(8,128)(2,1)} %param.21) | copy-start | bytes 3145732
  16.7 6.5 %collective-permute-start.4 = (bf16[4,4,8192]{2,1,0:T(4,128)(2,1)S(1)}, bf16[4,4,8192]{2,1,0:T(4,128)(2,1)S(1)}, u32[]{:S(2)}, u32[]{:S(2)}) collective-permute-start(bf16[4,4,8192]{2,1,0:T(4,128)(2,1)S(1)} %pad_maximum_fusion.refs_0_), channel_id=1, source_target_pairs={{0,1},{1,0},{2,3},{3,2},{4,5},{5,4},{6,7},{7,6},{8,9},{9,8},{10,11... | collective-permute-start | bytes 786440 | tf_op jit(solution)/shard_map/ppermute | solution.py:415
  21.9 15.5 %copy-start.6 = (bf16[32,16,512]{2,1,0:T(8,128)(2,1)S(1)}, bf16[32,16,512]{2,1,0:T(8,128)(2,1)}, u32[]{:S(2)}) copy-start(bf16[32,16,512]{2,1,0:T(8,128)(2,1)} %param.25) | copy-start | bytes 1572868
  22.0 15.4 %copy-start.7 = (bf16[32,16,64]{2,1,0:T(8,128)(2,1)S(1)}, bf16[32,16,64]{2,1,0:T(8,128)(2,1)}, u32[]{:S(2)}) copy-start(bf16[32,16,64]{2,1,0:T(8,128)(2,1)} %param.26) | copy-start | bytes 196612
  23.2 1.5 %collective-permute-start.5 = (bf16[4,4,8192]{2,1,0:T(4,128)(2,1)S(1)}, bf16[4,4,8192]{2,1,0:T(4,128)(2,1)S(1)}, u32[]{:S(2)}, u32[]{:S(2)}) collective-permute-start(bf16[4,4,8192]{2,1,0:T(4,128)(2,1)S(1)} %collective-permute-done.3.refs_1_), channel_id=1, source_target_pairs={{0,1},{1,0},{2,3},{3,2},{4,5},{5,4},{6,7},{7,6},{8,9},{9,8},{10,11... | collective-permute-start | bytes 786440 | tf_op jit(solution)/shard_map/ppermute | solution.py:415
  25.4 22.8 %copy-start.4 = (bf16[2,384,1024]{2,1,0:T(8,128)(2,1)S(1)}, bf16[2,384,1024]{2,1,0:T(8,128)(2,1)}, u32[]{:S(2)}) copy-start(bf16[2,384,1024]{2,1,0:T(8,128)(2,1)} %k_ref.1) | copy-start | bytes 4718596
  25.5 22.8 %copy-start.5 = (bf16[2,384,1024]{2,1,0:T(8,128)(2,1)S(1)}, bf16[2,384,1024]{2,1,0:T(8,128)(2,1)}, u32[]{:S(2)}) copy-start(bf16[2,384,1024]{2,1,0:T(8,128)(2,1)} %v_ref.1) | copy-start | bytes 4718596
  25.5 22.8 %copy-start.16 = (s32[32]{0:T(128)S(1)}, s32[32]{0:T(128)}, u32[]{:S(2)}) copy-start(s32[32]{0:T(128)} %len_ref.1) | copy-start | bytes 388
  25.5 3.1 %collective-permute-start.8 = (bf16[16,128]{1,0:T(8,128)(2,1)S(1)}, bf16[16,128]{1,0:T(8,128)(2,1)S(1)}, u32[]{:S(2)}, u32[]{:S(2)}) collective-permute-start(bf16[16,128]{1,0:T(8,128)(2,1)S(1)} %get-tuple-element.45.refs_0_), channel_id=1, source_target_pairs={{0,3},{1,2},{2,1},{3,0},{4,7},{5,6},{6,5},{7,4},{8,11},{9,10},{10,... | collective-permute-start | bytes 12296 | tf_op jit(solution)/shard_map/ppermute | solution.py:415
  26.8 3.6 %collective-permute-start.7 = (bf16[16,128]{1,0:T(8,128)(2,1)S(1)}, bf16[16,128]{1,0:T(8,128)(2,1)S(1)}, u32[]{:S(2)}, u32[]{:S(2)}) collective-permute-start(bf16[16,128]{1,0:T(8,128)(2,1)S(1)} %get-tuple-element.45.refs_0_), channel_id=1, source_target_pairs={{0,2},{1,3},{2,0},{3,1},{4,6},{5,7},{6,4},{7,5},{8,10},{9,11},{10,... | collective-permute-start | bytes 12296 | tf_op jit(solution)/shard_map/ppermute | solution.py:415
  27.3 3.1 %collective-permute-start.6 = (bf16[16,128]{1,0:T(8,128)(2,1)S(1)}, bf16[16,128]{1,0:T(8,128)(2,1)S(1)}, u32[]{:S(2)}, u32[]{:S(2)}) collective-permute-start(bf16[16,128]{1,0:T(8,128)(2,1)S(1)} %get-tuple-element.45.refs_0_), channel_id=1, source_target_pairs={{0,1},{1,0},{2,3},{3,2},{4,5},{5,4},{6,7},{7,6},{8,9},{9,8},{10,11... | collective-permute-start | bytes 12296 | tf_op jit(solution)/shard_map/ppermute | solution.py:415
  30.4 6.2 %collective-permute-start.11 = (bf16[16,128]{1,0:T(8,128)(2,1)S(1)}, bf16[16,128]{1,0:T(8,128)(2,1)S(1)}, u32[]{:S(2)}, u32[]{:S(2)}) collective-permute-start(bf16[16,128]{1,0:T(8,128)(2,1)S(1)} %shard_map.187.refs_0_), channel_id=1, source_target_pairs={{0,12},{1,13},{2,14},{3,15},{4,0},{5,1},{6,2},{7,3},{8,4},{9,5},{1... | collective-permute-start | bytes 12296 | tf_op jit(solution)/shard_map/ppermute | solution.py:415
  30.7 6.0 %collective-permute-start.10 = (bf16[16,128]{1,0:T(8,128)(2,1)S(1)}, bf16[16,128]{1,0:T(8,128)(2,1)S(1)}, u32[]{:S(2)}, u32[]{:S(2)}) collective-permute-start(bf16[16,128]{1,0:T(8,128)(2,1)S(1)} %shard_map.187.refs_0_), channel_id=1, source_target_pairs={{0,8},{1,9},{2,10},{3,11},{4,12},{5,13},{6,14},{7,15},{8,0},{9,1},... | collective-permute-start | bytes 12296 | tf_op jit(solution)/shard_map/ppermute | solution.py:415
  32.0 5.4 %collective-permute-start.9 = (bf16[16,128]{1,0:T(8,128)(2,1)S(1)}, bf16[16,128]{1,0:T(8,128)(2,1)S(1)}, u32[]{:S(2)}, u32[]{:S(2)}) collective-permute-start(bf16[16,128]{1,0:T(8,128)(2,1)S(1)} %shard_map.187.refs_0_), channel_id=1, source_target_pairs={{0,4},{1,5},{2,6},{3,7},{4,8},{5,9},{6,10},{7,11},{8,12},{9,13},{1... | collective-permute-start | bytes 12296 | tf_op jit(solution)/shard_map/ppermute | solution.py:415
  33.9 25.8 %slice-start.2 = ((s8[8388608]{0:T(1024)(128)(4,1)}), s8[4194304]{0:T(1024)(128)(4,1)S(1)}, s32[]{:S(2)}) async-start(s8[8388608]{0:T(1024)(128)(4,1)} %bitcast.15), calls=%async_computation.4 | async-start | bytes 8388608
  34.0 25.8 %slice-start.3 = ((s8[8388608]{0:T(1024)(128)(4,1)}), s8[4194304]{0:T(1024)(128)(4,1)S(1)}, s32[]{:S(2)}) async-start(s8[8388608]{0:T(1024)(128)(4,1)} %bitcast.15), calls=%async_computation.5 | async-start | bytes 8388608
  38.2 43.3 %copy-start.9 = (bf16[2,8192]{1,0:T(2,128)(2,1)S(1)}, bf16[2,8192]{1,0:T(2,128)(2,1)}, u32[]{:S(2)}) copy-start(bf16[2,8192]{1,0:T(2,128)(2,1)} %first_ref.1) | copy-start | bytes 98308
  38.3 43.3 %copy-start.11 = (bf16[2,8192]{1,0:T(2,128)(2,1)S(1)}, bf16[2,8192]{1,0:T(2,128)(2,1)}, u32[]{:S(2)}) copy-start(bf16[2,8192]{1,0:T(2,128)(2,1)} %second_ref.1) | copy-start | bytes 98308
  62.3 2.7 %collective-permute-start.12 = (f32[32,8192]{1,0:T(8,128)S(1)}, f32[32,8192]{1,0:T(8,128)S(1)}, u32[]{:S(2)}, u32[]{:S(2)}) collective-permute-start(f32[32,8192]{1,0:T(8,128)S(1)} %get-tuple-element.57), channel_id=1, source_target_pairs={{0,1},{1,0},{2,3},{3,2},{4,5},{5,4},{6,7},{7,6},{8,9},{9,8},{10,11... | collective-permute-start | bytes 3145736 | tf_op jit(solution)/shard_map/ppermute | solution.py:415
  65.2 8.4 %collective-permute-start.13 = (bf16[16,8192]{1,0:T(8,128)(2,1)S(1)}, bf16[16,8192]{1,0:T(8,128)(2,1)S(1)}, u32[]{:S(2)}, u32[]{:S(2)}) collective-permute-start(bf16[16,8192]{1,0:T(8,128)(2,1)S(1)} %get-tuple-element.59), channel_id=1, source_target_pairs={{0,2},{1,3},{2,0},{3,1},{4,6},{5,7},{6,4},{7,5},{8,10},{9,11},{10,... | collective-permute-start | bytes 786440 | tf_op jit(solution)/shard_map/ppermute | solution.py:415
  73.7 6.6 %collective-permute-start.14 = (bf16[4,8192]{1,0:T(4,128)(2,1)S(1)}, bf16[4,8192]{1,0:T(4,128)(2,1)S(1)}, u32[]{:S(2)}, u32[]{:S(2)}) collective-permute-start(bf16[4,8192]{1,0:T(4,128)(2,1)S(1)} %get-tuple-element.61), channel_id=1, source_target_pairs={{0,4},{1,5},{2,6},{3,7},{4,8},{5,9},{6,10},{7,11},{8,12},{9,13},{1... | collective-permute-start | bytes 196616 | tf_op jit(solution)/shard_map/ppermute | solution.py:415
  73.8 7.7 %collective-permute-start.15 = (bf16[4,8192]{1,0:T(4,128)(2,1)S(1)}, bf16[4,8192]{1,0:T(4,128)(2,1)S(1)}, u32[]{:S(2)}, u32[]{:S(2)}) collective-permute-start(bf16[4,8192]{1,0:T(4,128)(2,1)S(1)} %get-tuple-element.62), channel_id=1, source_target_pairs={{0,8},{1,9},{2,10},{3,11},{4,12},{5,13},{6,14},{7,15},{8,0},{9,1},... | collective-permute-start | bytes 196616 | tf_op jit(solution)/shard_map/ppermute | solution.py:415
  74.8 6.8 %collective-permute-start.16 = (bf16[4,8192]{1,0:T(4,128)(2,1)S(1)}, bf16[4,8192]{1,0:T(4,128)(2,1)S(1)}, u32[]{:S(2)}, u32[]{:S(2)}) collective-permute-start(bf16[4,8192]{1,0:T(4,128)(2,1)S(1)} %get-tuple-element.63), channel_id=1, source_target_pairs={{0,12},{1,13},{2,14},{3,15},{4,0},{5,1},{6,2},{7,3},{8,4},{9,5},{1... | collective-permute-start | bytes 196616 | tf_op jit(solution)/shard_map/ppermute | solution.py:415
  (6 other events, 5.6 us)

commit v5 on v4

--- a/solution.py
+++ b/solution.py
@@ -64,7 +64,9 @@
         copy.wait()
 
 
-def norm_body(first_hbm, second_hbm, gain_hbm, out_ref, first_ref, second_ref, gain_ref, sems):
+def norm_body(
+    first_hbm, second_hbm, gain_hbm, long_ref, short_ref, first_ref, second_ref, gain_ref, sems
+):
     fetch(((first_hbm, first_ref), (second_hbm, second_ref), (gain_hbm, gain_ref)), sems)
     gain = gain_ref[...].astype(F32)
     factors = []
@@ -75,7 +77,12 @@
     for i in range(gain.shape[0]):
         at = slice(i * HEAD, (i + 1) * HEAD)
         values = jnp.concatenate((first_ref[:, at].astype(F32), second_ref[:, at].astype(F32)))
-        out_ref[:, at] = (values * factor * gain[i : i + 1]).astype(BF16)
+        values = (values * factor * gain[i : i + 1]).astype(BF16)
+        cut = long_ref.shape[1]
+        if i * HEAD < cut:
+            long_ref[:, at] = values
+        else:
+            short_ref[:, i * HEAD - cut : (i + 1) * HEAD - cut] = values
 
 
 def prep_body(
@@ -157,21 +164,34 @@
     row = iota((take_ref.shape[0], 1), 0)
     h = row // all_rows
     block, step, mine = split(row % all_rows)
-    wanted = device_of(block, 1) * rows * heads + (mine * heads + h) * STEPS + step
+    c, m, f = block // (far * near), block // far % near, block % far
+    c, m, f = (cores - c) % cores, (near - m) % near, (far - f) % far
+    wanted = ((f * near + m) * cores + c) * rows * heads + (mine * heads + h) * STEPS + step
     hot(take_ref, wanted, iota((1, take_ref.shape[1]), 1))
 
 
-def low_body(rank, groups, *refs):
-    parts, (qd_ref, vd_ref, local_ref, place_ref, x_ref, out_ref) = refs[:groups], refs[groups:]
-    rows = parts[0].shape[1]
+def low_body(rank, sizes, *refs):
+    far, near, cores = sizes
+    longs, shorts = refs[: cores * near], refs[cores * near : cores * near + 2 * cores]
+    qd_ref, vd_ref, local_ref, place_ref, x_ref, out_ref = refs[cores * near + 2 * cores :]
+    rows, cut = longs[0].shape[1:]
     sets = max(1, 16 // rows)
-    for p, part in enumerate(parts):
-        for i in range(0, part.shape[0], sets):
-            at = (p * part.shape[0] + i) * rows
-            for lane in range(0, x_ref.shape[1], 1024):
-                lanes = slice(lane, lane + 1024)
-                block = [part[i + j, :, lanes].astype(F32) for j in range(sets)]
-                x_ref[at : at + sets * rows, lanes] = jnp.concatenate(block, axis=0).astype(BF16)
+
+    def fill(at, start, parts):
+        for lane in range(0, parts[0][0].shape[-1], 1024):
+            lanes = slice(lane, lane + 1024)
+            block = [ref[(*where, slice(None), lanes)].astype(F32) for ref, *where in parts]
+            block = jnp.concatenate(block, axis=0).astype(BF16)
+            x_ref[at : at + sets * rows, start + lane : start + lane + 1024] = block
+
+    for c in range(cores):
+        for m in range(near):
+            for f in range(0, far, sets):
+                at = ((c * near + m) * far + f) * rows
+                group = range(f, f + sets)
+                fill(at, 0, [(longs[c * near + m], g) for g in group])
+                here, there = shorts[2 * c : 2 * c + 2]
+                fill(at, cut, [(there, g - 1, m) if g else (here, m) for g in group])
     adapters = qd_ref.shape[0] // rank
     maps = jnp.concatenate((qd_ref[...], vd_ref[...]), axis=0)
     low = dot_nt(x_ref[...], maps)
@@ -262,7 +282,11 @@
     out_ref[...] = dot(send_ref[...], stacked).astype(BF16).reshape(out_ref.shape)
 
 
-def attend_body(own, columns, index_ref, len_ref, x_ref, order_ref, k_ref, v_ref, ctx_ref, nk_ref, nv_ref, s_ref):
+def attend_body(
+    sizes, own, columns, index_ref, len_ref, x_ref, order_ref, k_ref, v_ref, nk_ref, nv_ref, *refs
+):
+    far, near, cores = sizes
+    ctx_refs, s_ref = refs[:-1], refs[-1]
     n, span = x_ref.shape[0], k_ref.shape[1]
     group = HEADS // KV_HEADS
     local = HEADS // n
@@ -320,26 +344,54 @@
             )
     step = local * STEPS
     half = KV_HEADS * mine
-    for i in range(n):
-        block = [s_ref[b * half + i * step : b * half + (i + 1) * step] for b in range(own)]
-        ctx_ref[i] = jnp.concatenate(block, axis=0).astype(BF16)
-
-
-def out_body(tile, ctx_ref, take_ref, w_ref, mine_ref, other_ref, a_ref):
+    index = index_ref[0]
+    core_at = index % cores
+    near_at = index // cores % near
+    far_at = index // (cores * near)
+    for p, ref in enumerate(ctx_refs):
+        m, c = p // cores, p % cores
+        for f in range(far):
+            i = ((far_at + f) % far * near + (near_at + m) % near) * cores + (core_at + c) % cores
+            at = pl.multiple_of(i * step, step)
+            block = [s_ref[pl.ds(b * half + at, step)] for b in range(own)]
+            ref[f] = jnp.concatenate(block, axis=0).astype(BF16)
+
+
+def take_body(came, *refs):
+    ctx_refs, (take_ref, w_ref, a_ref, mine_ref, other_ref) = refs[:came], refs[came:]
     rows = a_ref.shape[0]
-    n = ctx_ref.shape[0]
-    x = ctx_ref[...].reshape(n * ctx_ref.shape[1], HEAD)
+    x = jnp.concatenate([ref[...].reshape(-1, HEAD) for ref in ctx_refs], axis=0)
     taken = dot(take_ref[...], x).astype(BF16)
     for h in range(a_ref.shape[1] // HEAD):
         a_ref[:, h * HEAD : (h + 1) * HEAD] = taken[h * rows : (h + 1) * rows]
+    out_body(0, a_ref, w_ref, mine_ref, other_ref)
+
+
+def out_body(start, a_ref, w_ref, mine_ref, other_ref):
     half = mine_ref.shape[0]
-
-    @pl.loop(0, w_ref.shape[1] // tile)
+    tile = 1024
+
+    @pl.loop(0, mine_ref.shape[1] // tile)
     def _(i):
         at = pl.ds(pl.multiple_of(i * tile, tile), tile)
-        product = dot(a_ref[...], w_ref[:, at])
+        product = dot(a_ref[...], w_ref[:, pl.ds(pl.multiple_of(start + i * tile, tile), tile)])
         mine_ref[:, at] = product[:half]
         other_ref[:, at] = product[half:]
+
+
+def far_first_body(near, mine_ref, came_ref, *refs):
+    total = mine_ref[...] + came_ref[...]
+    rows = refs[0].shape[0] // near
+    for f, ref in enumerate(refs):
+        blocks = [(m * len(refs) + f) * rows for m in range(near)]
+        value = jnp.concatenate([total[at : at + rows] for at in blocks], axis=0)
+        ref[...] = value.astype(ref.dtype)
+
+
+def pack_body(came, *refs):
+    for f, ref in enumerate(refs[came:]):
+        for p in range(came):
+            ref[p] = refs[p][f]
 
 
 def near_body(mine_ref, came_ref, *refs):
@@ -361,11 +413,15 @@
         ref[...] = total[f * rows : (f + 1) * rows].astype(BF16)
 
 
-def last_body(came, first_ref, second_ref, keep_ref, *refs):
-    one_ref, two_ref = refs[came:]
-    total = keep_ref[...]
-    for ref in refs[:came]:
-        total = total + ref[...].astype(F32)
+def last_body(longs, first_ref, second_ref, *refs):
+    one_ref, two_ref = refs[-2:]
+    totals = []
+    for part in (refs[:longs], refs[longs:-2]):
+        total = part[0][...]
+        for ref in part[1:]:
+            total = total + ref[...].astype(F32)
+        totals.append(total)
+    total = jnp.concatenate(totals, axis=1)
     own = one_ref.shape[0]
     one_ref[...] = (first_ref[...].astype(F32) + total[:own]).astype(BF16)
     two_ref[...] = (second_ref[...].astype(F32) + total[own:]).astype(BF16)
@@ -414,10 +470,17 @@
     def shift(value, f, m, c):
         return lax.ppermute(value, "serve", partner(f, m, c))
 
+    def swap(value, bit):
+        return lax.ppermute(value, "serve", [(i, i ^ bit) for i in range(n)])
+
     gain = attention_norm_gain.reshape(width // HEAD, HEAD)
-    normed = whole_call(
+    cut = width * 5 // 8
+    normed, short = whole_call(
         norm_body,
-        jax.ShapeDtypeStruct((rows, width), BF16),
+        (
+            jax.ShapeDtypeStruct((rows, cut), BF16),
+            jax.ShapeDtypeStruct((rows, width - cut), BF16),
+        ),
         (residual_first, residual_second, gain),
         hbm=3,
         scratch=[
@@ -428,11 +491,13 @@
         ],
         cost=1.0,
     )
-    normed = normed[None]
-    groups = [jnp.concatenate([normed] + [shift(normed, f, 0, 0) for f in range(1, far)])]
-    groups += [shift(groups[0], 0, m, 0) for m in range(1, near)]
-
-    groups[0], at = lax.optimization_barrier((groups[0], index[None]))
+    normed, short = normed[None], short[None]
+    shorts = [jnp.concatenate([short] + [shift(short, 0, m, 0) for m in range(1, near)])]
+    longs = [jnp.concatenate([normed] + [shift(normed, f, 0, 0) for f in range(1, far)])]
+    longs += [shift(longs[0], 0, m, 0) for m in range(1, near)]
+    shorts.append(jnp.stack([shift(shorts[0], f, 0, 0) for f in range(1, far)]))
+
+    longs[0], at = lax.optimization_barrier((longs[0], index[None]))
     sent = -(-(rows * local + rows) // 8) * 8
     narrow = jax.ShapeDtypeStruct((all_rows, 1), jnp.int32)
     table = jax.ShapeDtypeStruct((all_rows, HEAD), F32)
@@ -463,27 +528,30 @@
         ],
         cost=4.0,
     )
-    slot, groups[1] = lax.optimization_barrier((slot, groups[1]))
-
-    groups += [shift(group, 0, 0, c) for c in range(1, cores) for group in groups[:near]]
+    slot, longs[1] = lax.optimization_barrier((slot, longs[1]))
+
+    longs += [shift(part, 0, 0, c) for c in range(1, cores) for part in longs[:near]]
+    shorts += [shift(part, 0, 0, c) for c in range(1, cores) for part in shorts[:2]]
 
     query_down = jnp.swapaxes(query_down_weights, 1, 2).reshape(adapters * rank, width)
     value_down = jnp.swapaxes(value_down_weights, 1, 2).reshape(adapters * rank, width)
     packed_rows = all_rows * 2 * rank // HEAD
     x, low = whole_call(
-        functools.partial(low_body, rank, len(groups)),
+        functools.partial(low_body, rank, sizes),
         (
             jax.ShapeDtypeStruct((all_rows, width), BF16),
             jax.ShapeDtypeStruct((packed_rows, HEAD), BF16),
         ),
-        (*groups, query_down, value_down, near_slot, place),
+        (*longs, *shorts, query_down, value_down, near_slot, place),
         cost=0.3,
     )
-    lows = [shift(low, 0, m, c) for m in range(near) for c in range(cores) if m + c]
-    low = whole_call(
-        join_body, jax.ShapeDtypeStruct(low.shape, BF16), (low, *lows), cost=0.1
-    )
-    lows = [low] + [shift(low, f, 0, 0) for f in range(1, far)]
+    bit = 1
+    while 2 * bit < n:
+        low = whole_call(
+            join_body, jax.ShapeDtypeStruct(low.shape, BF16), (low, swap(low, bit)), cost=0.1
+        )
+        bit *= 2
+    lows = [low, swap(low, bit)]
 
     base_q, base_kv = whole_call(
         functools.partial(base_body, 2048),
@@ -516,51 +584,79 @@
     )
     arrived = lax.all_to_all(ready, "serve", split_axis=0, concat_axis=0, tiled=True)
 
-    context, new_keys, new_values = whole_call(
-        functools.partial(attend_body, own, key_cols),
-        (
-            jax.ShapeDtypeStruct((n, rows * local, HEAD), BF16),
-            jax.ShapeDtypeStruct((own, STEPS, KV_HEADS * HEAD), BF16),
-            jax.ShapeDtypeStruct((own, STEPS, KV_HEADS * HEAD), BF16),
-        ),
+    fresh = jax.ShapeDtypeStruct((own, STEPS, KV_HEADS * HEAD), BF16)
+    plane = near * cores
+    new_keys, new_values, *context = whole_call(
+        functools.partial(attend_body, sizes, own, key_cols),
+        (fresh, fresh) + (jax.ShapeDtypeStruct((far, rows * local, HEAD), BF16),) * plane,
         (index[None], lengths, arrived, order, rotated_key_cache, stored_value_cache),
         smem=2,
         scratch=[pltpu.VMEM((own * HEADS * STEPS, HEAD), F32)],
         cost=1.0,
     )
-    context = lax.all_to_all(context, "serve", split_axis=0, concat_axis=0, tiled=True)
-
-    kinds = jax.ShapeDtypeStruct((all_rows // cores, width), F32)
-    mine, other = whole_call(
-        functools.partial(out_body, 1024),
-        (kinds, kinds),
-        (context, take, output_matrix),
-        scratch=[pltpu.VMEM((all_rows, query_cols), BF16)],
-        cost=0.5,
-    )
-
-    def kind(count, dtype):
-        return jax.ShapeDtypeStruct((count * rows, width), dtype)
+    context = context[:1] + [shift(context[p], 0, p // cores, p % cores) for p in range(1, plane)]
+    context = whole_call(
+        functools.partial(pack_body, plane),
+        (jax.ShapeDtypeStruct((plane, rows * local, HEAD), BF16),) * far,
+        tuple(context),
+        cost=0.1,
+    )
+    context = [context[0]] + [shift(context[f], f, 0, 0) for f in range(1, far)]
+
+    half = all_rows // cores
+
+    def kinds(count, columns):
+        return (jax.ShapeDtypeStruct((count, columns), F32),) * 2
+
+    taken, mine_long, other_long = whole_call(
+        functools.partial(take_body, far),
+        (jax.ShapeDtypeStruct((all_rows, query_cols), BF16),) + kinds(half, cut),
+        (*context, take, output_matrix),
+        cost=0.4,
+    )
+    mine_short, other_short = whole_call(
+        functools.partial(out_body, cut),
+        kinds(half, width - cut),
+        (taken, output_matrix),
+        cost=0.3,
+    )
+
+    def kind(count, columns, dtype):
+        return jax.ShapeDtypeStruct((count * rows, columns), dtype)
 
     keep, *others = whole_call(
         near_body,
-        (kind(far, F32),) + (kind(far, BF16),) * (near - 1),
-        (mine, shift(other, 0, 0, 1)),
+        (kind(far, cut, F32),) + (kind(far, cut, BF16),) * (near - 1),
+        (mine_long, shift(other_long, 0, 0, 1)),
         cost=0.1,
     )
     others = [shift(other, 0, m, 0) for m, other in enumerate(others, 1)]
+    short, *sides = whole_call(
+        functools.partial(far_first_body, near),
+        (kind(near, width - cut, F32),) + (kind(near, width - cut, BF16),) * (far - 1),
+        (mine_short, shift(other_short, 0, 0, 1)),
+        cost=0.1,
+    )
+    sides = [shift(side, f, 0, 0) for f, side in enumerate(sides, 1)]
     keep, *others = whole_call(
         functools.partial(far_body, len(others)),
-        (kind(1, F32),) + (kind(1, BF16),) * (far - 1),
+        (kind(1, cut, F32),) + (kind(1, cut, BF16),) * (far - 1),
         (keep, *others),
         cost=0.1,
     )
     others = [shift(other, f, 0, 0) for f, other in enumerate(others, 1)]
+    short, *sides = whole_call(
+        functools.partial(far_body, len(sides)),
+        (kind(1, width - cut, F32),) + (kind(1, width - cut, BF16),) * (near - 1),
+        (short, *sides),
+        cost=0.1,
+    )
+    sides = [shift(side, 0, m, 0) for m, side in enumerate(sides, 1)]
     result = jax.ShapeDtypeStruct((own, width), BF16)
     out_one, out_two = whole_call(
-        functools.partial(last_body, len(others)),
+        functools.partial(last_body, 1 + len(others)),
         (result, result),
-        (residual_first, residual_second, keep, *others),
+        (residual_first, residual_second, keep, *others, short, *sides),
         cost=0.1,
     )
     return (out_one, out_two, new_keys, new_values)

time: 82.7 us -> 83.2 us (level)
  starting transfers between devices: 17.3 us -> 35.9 us
  waiting for transfers between devices: 26.8 us -> 15.5 us
  blocking collectives: 19.5 us -> 12.2 us
    ppermute x17 -> x28, waiting for transfers between devices: 26.8 us -> 9.87 us  [shift(): return lax.ppermute(value, 'serve', partner(f, m, c))]
    ppermute x17 -> x28, starting transfers between devices: 17.3 us -> 31.3 us  [shift(): return lax.ppermute(value, 'serve', partner(f, m, c))]
    all_to_all x1 -> x0, blocking collectives: 9.48 us -> none  [shards(): lax.all_to_all(context, 'serve', split_axis=0, concat_axis=0, tiled=True)]
    ppermute x0 -> x4, waiting for transfers between devices: none -> 5.59 us  [swap(): return lax.ppermute(value, 'serve', [(i, i ^ bit) for i in range(n)])]
    ppermute x0 -> x4, starting transfers between devices: none -> 4.63 us  [swap(): return lax.ppermute(value, 'serve', [(i, i ^ bit) for i in range(n)])]
    all_to_all x1, blocking collectives: 9.99 us -> 12.2 us  [shards(): lax.all_to_all(ready, 'serve', split_axis=0, concat_axis=0, tiled=True)]
    pallas_call x11 -> x17, Pallas kernels: 11.9 us -> 12.4 us  [whole_call(): pl.pallas_call(body, out_shape=out_shape, in_specs=specs, out_specs=tuple...]
  transfers between devices with their start and end apart: 17 -> 32, of which waited for: 11 -> 13; matrix products, arithmetic and copies ran while one was open for 0% -> 0% of each run, Pallas kernels for 5% -> 7%
where the time goes in v5:
time: 83.2 us; the launch traced here: 82.9 us
  starting transfers between devices  35.9 us (43%)
  waiting for transfers between devices  15.5 us (19%)
  Pallas kernels  12.4 us (15%)
  blocking collectives  12.2 us (15%)
  local copies, waits for them, and re-layouts  5.64 us (7%)
  between operations  0.93 us (1%)
    ppermute x28, starting transfers between devices, shift(): return lax.ppermute(value, 'serve', partner(f, m, c))  31.3 us
    pallas_call x17, Pallas kernels, whole_call(): pl.pallas_call(body, out_shape=out_shape, in_specs=specs, out_specs=tuple...  12.4 us
    all_to_all x1, blocking collectives, shards(): lax.all_to_all(ready, 'serve', split_axis=0, concat_axis=0, tiled=True)  12.2 us
    ppermute x28, waiting for transfers between devices, shift(): return lax.ppermute(value, 'serve', partner(f, m, c))  9.87 us
    unnamed x42, local copies, waits for them, and re-layouts  5.64 us
    ppermute x4, waiting for transfers between devices, swap(): return lax.ppermute(value, 'serve', [(i, i ^ bit) for i in range(n)])  5.59 us
    ppermute x4, starting transfers between devices, swap(): return lax.ppermute(value, 'serve', [(i, i ^ bit) for i in range(n)])  4.63 us
  transfers between devices with their start and end apart: 32, of which 13 were waited for; matrix products, arithmetic and copies ran while one was open for 0% of the time, Pallas kernels for 7%

profile of v5, /device:TPU:0, one launch (start us, length us, event | category | flops | bytes accessed | tf_op | source)
XLA Modules:
  0.0 82.9 jit_solution(17998057199741674195)
XLA Ops:
  3.3 3.0 %collective-permute-start.6 = (bf16[1,4,3072]{2,1,0:T(4,128)(2,1)S(1)}, bf16[1,4,3072]{2,1,0:T(4,128)(2,1)S(1)}, u32[]{:S(2)}, u32[]{:S(2)}) collective-permute-start(bf16[1,4,3072]{2,1,0:T(4,128)(2,1)S(1)} %bitcast.29), channel_id=1, source_target_pairs={{0,2},{1,3},{2,0},{3,1},{4,6},{5,7},{6,4},{7,5},{8,10},{9,11},{10,... | collective-permute-start | bytes 73736 | tf_op jit(solution)/shard_map/ppermute | solution.py:471
  6.3 3.6 %collective-permute-start.2 = (bf16[1,4,5120]{2,1,0:T(4,128)(2,1)S(1)}, bf16[1,4,5120]{2,1,0:T(4,128)(2,1)S(1)}, u32[]{:S(2)}, u32[]{:S(2)}) collective-permute-start(bf16[1,4,5120]{2,1,0:T(4,128)(2,1)S(1)} %bitcast.25), channel_id=1, source_target_pairs={{0,12},{1,13},{2,14},{3,15},{4,0},{5,1},{6,2},{7,3},{8,4},{9,5},{1... | collective-permute-start | bytes 122888 | tf_op jit(solution)/shard_map/ppermute | solution.py:471
  9.9 1.0 %collective-permute-start = (bf16[1,4,5120]{2,1,0:T(4,128)(2,1)S(1)}, bf16[1,4,5120]{2,1,0:T(4,128)(2,1)S(1)}, u32[]{:S(2)}, u32[]{:S(2)}) collective-permute-start(bf16[1,4,5120]{2,1,0:T(4,128)(2,1)S(1)} %bitcast.27), channel_id=1, source_target_pairs={{0,4},{1,5},{2,6},{3,7},{4,8},{5,9},{6,10},{7,11},{8,12},{9,13},{1... | collective-permute-start | bytes 122888 | tf_op jit(solution)/shard_map/ppermute | solution.py:471
  11.0 2.9 %collective-permute-start.9 = (bf16[2,4,3072]{2,1,0:T(4,128)(2,1)S(1)}, bf16[2,4,3072]{2,1,0:T(4,128)(2,1)S(1)}, u32[]{:S(2)}, u32[]{:S(2)}) collective-permute-start(bf16[2,4,3072]{2,1,0:T(4,128)(2,1)S(1)} %pad_maximum_fusion.2.refs_4_), channel_id=1, source_target_pairs={{0,12},{1,13},{2,14},{3,15},{4,0},{5,1},{6,2},{7,3},{8,4},{9,5},{1... | collective-permute-start | bytes 147464 | tf_op jit(solution)/shard_map/ppermute | solution.py:471
  13.8 1.1 %collective-permute-start.8 = (bf16[2,4,3072]{2,1,0:T(4,128)(2,1)S(1)}, bf16[2,4,3072]{2,1,0:T(4,128)(2,1)S(1)}, u32[]{:S(2)}, u32[]{:S(2)}) collective-permute-start(bf16[2,4,3072]{2,1,0:T(4,128)(2,1)S(1)} %pad_maximum_fusion.2.refs_4_), channel_id=1, source_target_pairs={{0,8},{1,9},{2,10},{3,11},{4,12},{5,13},{6,14},{7,15},{8,0},{9,1},... | collective-permute-start | bytes 147464 | tf_op jit(solution)/shard_map/ppermute | solution.py:471
  15.2 0.9 %collective-permute-done = bf16[1,4,5120]{2,1,0:T(4,128)(2,1)S(1)} collective-permute-done((bf16[1,4,5120]{2,1,0:T(4,128)(2,1)S(1)}, bf16[1,4,5120]{2,1,0:T(4,128)(2,1)S(1)}, u32[]{:S(2)}, u32[]{:S(2)}) %collective-permute-start) | collective-permute-done | bytes 40992 | tf_op jit(solution)/shard_map/ppermute | solution.py:471
  17.8 1.1 %copy-done.14 = s32[32]{0:T(128)S(1)} copy-done((s32[32]{0:T(128)S(1)}, s32[32]{0:T(128)}, u32[]{:S(2)}) %copy-start.14) | copy-done | bytes 152
  18.9 1.4 %copy-done.15 = s32[32]{0:T(128)S(1)} copy-done((s32[32]{0:T(128)S(1)}, s32[32]{0:T(128)}, u32[]{:S(2)}) %copy-start.15) | copy-done | bytes 152
  20.3 1.8 %shard_map.184 = (s32[64,1]{1,0:T(8,128)S(1)}, s32[64,1]{1,0:T(8,128)S(1)}, f32[64,128]{1,0:T(8,128)S(1)}, f32[64,128]{1,0:T(8,128)S(1)}, f32[64,128]{1,0:T(8,12...) custom-call(s32[1]{0:T(128)} %bitcast.index_ref, ...), custom_call_target="tpu_custom_call" | custom-call | flops 4600000000 | tf_op jit(solution)/shard_map/pallas_call | solution.py:36
  23.0 1.2 %collective-permute-done.10.refs_6_ = bf16[2,4,3072]{2,1,0:T(4,128)(2,1)S(1)} collective-permute-done((bf16[2,4,3072]{2,1,0:T(4,128)(2,1)S(1)}, bf16[2,4,3072]{2,1,0:T(4,128)(2,1)S(1)}, u32[]{:S(2)}, u32[]{:S(2)}) %collective-permute-start.10) | collective-permute-done | bytes 49184 | tf_op jit(solution)/shard_map/ppermute | solution.py:471
  25.2 1.0 %collective-permute-done.12.refs_1_ = bf16[16,128]{1,0:T(8,128)(2,1)S(1)} collective-permute-done((bf16[16,128]{1,0:T(8,128)(2,1)S(1)}, bf16[16,128]{1,0:T(8,128)(2,1)S(1)}, u32[]{:S(2)}, u32[]{:S(2)}) %collective-permute-start.12) | collective-permute-done | bytes 4128 | tf_op jit(solution)/shard_map/ppermute | solution.py:474
  26.2 1.5 %collective-permute-start.13 = (bf16[16,128]{1,0:T(8,128)(2,1)S(1)}, bf16[16,128]{1,0:T(8,128)(2,1)S(1)}, u32[]{:S(2)}, u32[]{:S(2)}) collective-permute-start(bf16[16,128]{1,0:T(8,128)(2,1)S(1)} %shard_map.187.refs_0_), channel_id=1, source_target_pairs={{0,2},{1,3},{2,0},{3,1},{4,6},{5,7},{6,4},{7,5},{8,10},{9,11},{10,... | collective-permute-start | bytes 12296 | tf_op jit(solution)/shard_map/ppermute | solution.py:474
  27.7 2.1 %collective-permute-done.13.refs_1_ = bf16[16,128]{1,0:T(8,128)(2,1)S(1)} collective-permute-done((bf16[16,128]{1,0:T(8,128)(2,1)S(1)}, bf16[16,128]{1,0:T(8,128)(2,1)S(1)}, u32[]{:S(2)}, u32[]{:S(2)}) %collective-permute-start.13) | collective-permute-done | bytes 4128 | tf_op jit(solution)/shard_map/ppermute | solution.py:474
  29.8 1.2 %collective-permute-start.14 = (bf16[16,128]{1,0:T(8,128)(2,1)S(1)}, bf16[16,128]{1,0:T(8,128)(2,1)S(1)}, u32[]{:S(2)}, u32[]{:S(2)}) collective-permute-start(bf16[16,128]{1,0:T(8,128)(2,1)S(1)} %shard_map.188.refs_0_), channel_id=1, source_target_pairs={{0,4},{1,5},{2,6},{3,7},{4,0},{5,1},{6,2},{7,3},{8,12},{9,13},{10,... | collective-permute-start | bytes 12296 | tf_op jit(solution)/shard_map/ppermute | solution.py:474
  31.0 2.4 %collective-permute-done.14.refs_1_ = bf16[16,128]{1,0:T(8,128)(2,1)S(1)} collective-permute-done((bf16[16,128]{1,0:T(8,128)(2,1)S(1)}, bf16[16,128]{1,0:T(8,128)(2,1)S(1)}, u32[]{:S(2)}, u32[]{:S(2)}) %collective-permute-start.14) | collective-permute-done | bytes 4128 | tf_op jit(solution)/shard_map/ppermute | solution.py:474
  33.4 1.7 %collective-permute-start.15 = (bf16[16,128]{1,0:T(8,128)(2,1)S(1)}, bf16[16,128]{1,0:T(8,128)(2,1)S(1)}, u32[]{:S(2)}, u32[]{:S(2)}) collective-permute-start(bf16[16,128]{1,0:T(8,128)(2,1)S(1)} %shard_map.189.refs_0_), channel_id=1, source_target_pairs={{0,8},{1,9},{2,10},{3,11},{4,12},{5,13},{6,14},{7,15},{8,0},{9,1},... | collective-permute-start | bytes 12296 | tf_op jit(solution)/shard_map/ppermute | solution.py:474
  35.1 2.7 %shard_map.186 = (f32[64,512]{1,0:T(8,128)S(1)}, f32[64,128]{1,0:T(8,128)S(1)}) custom-call(bf16[64,8192]{1,0:T(8,128)(2,1)S(1)} %get-tuple-element.62.x_ref, bf16[8192,512]{1,0:T(8,128)(2,1)S(1)} %bitcast.20, bf16[64,8192]{1,0:T(8,128)(2,1)S(1)} %bitcast.21, bf16[64,8192]{1,0:T(8,128)(2,1)S(1)} %bitcast.22), custom_call_target="tpu_custom_call" | custom-call | flops 690000000 | tf_op jit(solution)/shard_map/pallas_call | solution.py:36
  38.8 12.2 %all_to_all.5.x_ref = bf16[16,24,128]{2,1,0:T(8,128)(2,1)S(1)} all-to-all(bf16[16,24,128]{2,1,0:T(8,128)(2,1)S(1)} %shard_map.190), channel_id=1, replica_groups=mesh['replica'=2,'serve'=16] {'serve'}, dimensions={0} | all-to-all | bytes 196608 | tf_op jit(solution)/shard_map/all_to_all | solution.py:585
  51.0 2.5 %shard_map.191 = (bf16[2,2,1024]{2,1,0:T(2,128)(2,1)}, bf16[2,2,1024]{2,1,0:T(2,128)(2,1)}, bf16[4,16,128]{2,1,0:T(8,128)(2,1)S(1)}, bf16[4,16,128]{2,1,0:T(8,12...) custom-call(s32[1]{0:T(128)} %bitcast.index_ref, s32[32]{0:T(128)S(1)} %copy-done.16, ...), custom_call_target="tpu_custom_call" | custom-call | flops 1150000000 | tf_op jit(solution)/shard_map/pallas_call | solution.py:36
  53.6 1.7 %collective-permute-start.18 = (bf16[4,16,128]{2,1,0:T(8,128)(2,1)S(1)}, bf16[4,16,128]{2,1,0:T(8,128)(2,1)S(1)}, u32[]{:S(2)}, u32[]{:S(2)}) collective-permute-start(bf16[4,16,128]{2,1,0:T(8,128)(2,1)S(1)} %get-tuple-element.77), channel_id=1, source_target_pairs={{0,3},{1,2},{2,1},{3,0},{4,7},{5,6},{6,5},{7,4},{8,11},{9,10},{10,... | collective-permute-start | bytes 49160 | tf_op jit(solution)/shard_map/ppermute | solution.py:471
  55.3 1.9 %collective-permute-done.17.refs_2_ = bf16[4,16,128]{2,1,0:T(8,128)(2,1)S(1)} collective-permute-done((bf16[4,16,128]{2,1,0:T(8,128)(2,1)S(1)}, bf16[4,16,128]{2,1,0:T(8,128)(2,1)S(1)}, u32[]{:S(2)}, u32[]{:S(2)}) %collective-permute-start.17) | collective-permute-done | bytes 16416 | tf_op jit(solution)/shard_map/ppermute | solution.py:471
  57.6 1.1 %collective-permute-start.20 = (bf16[4,16,128]{2,1,0:T(8,128)(2,1)S(1)}, bf16[4,16,128]{2,1,0:T(8,128)(2,1)S(1)}, u32[]{:S(2)}, u32[]{:S(2)}) collective-permute-start(bf16[4,16,128]{2,1,0:T(8,128)(2,1)S(1)} %get-tuple-element.80), channel_id=1, source_target_pairs={{0,8},{1,9},{2,10},{3,11},{4,12},{5,13},{6,14},{7,15},{8,0},{9,1},... | collective-permute-start | bytes 49160 | tf_op jit(solution)/shard_map/ppermute | solution.py:471
  58.7 2.4 %collective-permute-start.21 = (bf16[4,16,128]{2,1,0:T(8,128)(2,1)S(1)}, bf16[4,16,128]{2,1,0:T(8,128)(2,1)S(1)}, u32[]{:S(2)}, u32[]{:S(2)}) collective-permute-start(bf16[4,16,128]{2,1,0:T(8,128)(2,1)S(1)} %get-tuple-element.81), channel_id=1, source_target_pairs={{0,12},{1,13},{2,14},{3,15},{4,0},{5,1},{6,2},{7,3},{8,4},{9,5},{1... | collective-permute-start | bytes 49160 | tf_op jit(solution)/shard_map/ppermute | solution.py:471
  61.1 1.7 %collective-permute-done.19.refs_1_ = bf16[4,16,128]{2,1,0:T(8,128)(2,1)S(1)} collective-permute-done((bf16[4,16,128]{2,1,0:T(8,128)(2,1)S(1)}, bf16[4,16,128]{2,1,0:T(8,128)(2,1)S(1)}, u32[]{:S(2)}, u32[]{:S(2)}) %collective-permute-start.19) | collective-permute-done | bytes 16416 | tf_op jit(solution)/shard_map/ppermute | solution.py:471
  63.4 1.7 %shard_map.193 = (bf16[64,512]{1,0:T(8,128)(2,1)S(1)}, f32[32,5120]{1,0:T(8,128)S(1)}, f32[32,5120]{1,0:T(8,128)S(1)}) custom-call(bf16[4,16,128]{2,1,0:T(8,128)(2,1)S(1)} %get-tuple-element.78.refs_0_, bf16[4,16,128]{2,1,0:T(8,128)(2,1)S(1)} %collective-permute-done.19.refs_1_, bf16[4,16,128]{2,1,0:T(8,128)(2,1)S(1)} %collective-permute-done.20.refs_2_, ...), custom_call_target="tpu_custom_call" | custom-call | flops 460000000 | tf_op jit(solution)/shard_map/pallas_call | solution.py:36
  67.3 1.5 %collective-permute-start.23 = (bf16[16,5120]{1,0:T(8,128)(2,1)S(1)}, bf16[16,5120]{1,0:T(8,128)(2,1)S(1)}, u32[]{:S(2)}, u32[]{:S(2)}) collective-permute-start(bf16[16,5120]{1,0:T(8,128)(2,1)S(1)} %get-tuple-element.86), channel_id=1, source_target_pairs={{0,2},{1,3},{2,0},{3,1},{4,6},{5,7},{6,4},{7,5},{8,10},{9,11},{10,... | collective-permute-start | bytes 491528 | tf_op jit(solution)/shard_map/ppermute | solution.py:471
  68.8 2.1 %collective-permute-start.28 = (bf16[8,3072]{1,0:T(8,128)(2,1)S(1)}, bf16[8,3072]{1,0:T(8,128)(2,1)S(1)}, u32[]{:S(2)}, u32[]{:S(2)}) collective-permute-start(bf16[8,3072]{1,0:T(8,128)(2,1)S(1)} %get-tuple-element.95), channel_id=1, source_target_pairs={{0,4},{1,5},{2,6},{3,7},{4,8},{5,9},{6,10},{7,11},{8,12},{9,13},{1... | collective-permute-start | bytes 147464 | tf_op jit(solution)/shard_map/ppermute | solution.py:471
  70.9 1.8 %collective-permute-start.29 = (bf16[8,3072]{1,0:T(8,128)(2,1)S(1)}, bf16[8,3072]{1,0:T(8,128)(2,1)S(1)}, u32[]{:S(2)}, u32[]{:S(2)}) collective-permute-start(bf16[8,3072]{1,0:T(8,128)(2,1)S(1)} %get-tuple-element.96), channel_id=1, source_target_pairs={{0,8},{1,9},{2,10},{3,11},{4,12},{5,13},{6,14},{7,15},{8,0},{9,1},... | collective-permute-start | bytes 147464 | tf_op jit(solution)/shard_map/ppermute | solution.py:471
  73.7 2.1 %collective-permute-start.24 = (bf16[4,5120]{1,0:T(4,128)(2,1)S(1)}, bf16[4,5120]{1,0:T(4,128)(2,1)S(1)}, u32[]{:S(2)}, u32[]{:S(2)}) collective-permute-start(bf16[4,5120]{1,0:T(4,128)(2,1)S(1)} %get-tuple-element.88), channel_id=1, source_target_pairs={{0,4},{1,5},{2,6},{3,7},{4,8},{5,9},{6,10},{7,11},{8,12},{9,13},{1... | collective-permute-start | bytes 122888 | tf_op jit(solution)/shard_map/ppermute | solution.py:471
  75.7 1.8 %collective-permute-start.25 = (bf16[4,5120]{1,0:T(4,128)(2,1)S(1)}, bf16[4,5120]{1,0:T(4,128)(2,1)S(1)}, u32[]{:S(2)}, u32[]{:S(2)}) collective-permute-start(bf16[4,5120]{1,0:T(4,128)(2,1)S(1)} %get-tuple-element.89), channel_id=1, source_target_pairs={{0,8},{1,9},{2,10},{3,11},{4,12},{5,13},{6,14},{7,15},{8,0},{9,1},... | collective-permute-start | bytes 122888 | tf_op jit(solution)/shard_map/ppermute | solution.py:471
  78.2 1.5 %collective-permute-start.31 = (bf16[4,3072]{1,0:T(4,128)(2,1)S(1)}, bf16[4,3072]{1,0:T(4,128)(2,1)S(1)}, u32[]{:S(2)}, u32[]{:S(2)}) collective-permute-start(bf16[4,3072]{1,0:T(4,128)(2,1)S(1)} %get-tuple-element.99), channel_id=1, source_target_pairs={{0,2},{1,3},{2,0},{3,1},{4,6},{5,7},{6,4},{7,5},{8,10},{9,11},{10,... | collective-permute-start | bytes 73736 | tf_op jit(solution)/shard_map/ppermute | solution.py:471
  79.7 2.4 %collective-permute-done.31.refs_5_ = bf16[4,3072]{1,0:T(4,128)(2,1)S(1)} collective-permute-done((bf16[4,3072]{1,0:T(4,128)(2,1)S(1)}, bf16[4,3072]{1,0:T(4,128)(2,1)S(1)}, u32[]{:S(2)}, u32[]{:S(2)}) %collective-permute-start.31) | collective-permute-done | bytes 24608 | tf_op jit(solution)/shard_map/ppermute | solution.py:471
  (97 shorter events, 13.1 us)
Async XLA Ops:
  3.3 7.7 %collective-permute-start.6 = (bf16[1,4,3072]{2,1,0:T(4,128)(2,1)S(1)}, bf16[1,4,3072]{2,1,0:T(4,128)(2,1)S(1)}, u32[]{:S(2)}, u32[]{:S(2)}) collective-permute-start(bf16[1,4,3072]{2,1,0:T(4,128)(2,1)S(1)} %bitcast.29), channel_id=1, source_target_pairs={{0,2},{1,3},{2,0},{3,1},{4,6},{5,7},{6,4},{7,5},{8,10},{9,11},{10,... | collective-permute-start | bytes 73736 | tf_op jit(solution)/shard_map/ppermute | solution.py:471
  6.3 8.7 %collective-permute-start.2 = (bf16[1,4,5120]{2,1,0:T(4,128)(2,1)S(1)}, bf16[1,4,5120]{2,1,0:T(4,128)(2,1)S(1)}, u32[]{:S(2)}, u32[]{:S(2)}) collective-permute-start(bf16[1,4,5120]{2,1,0:T(4,128)(2,1)S(1)} %bitcast.25), channel_id=1, source_target_pairs={{0,12},{1,13},{2,14},{3,15},{4,0},{5,1},{6,2},{7,3},{8,4},{9,5},{1... | collective-permute-start | bytes 122888 | tf_op jit(solution)/shard_map/ppermute | solution.py:471
  9.9 5.3 %collective-permute-start.1 = (bf16[1,4,5120]{2,1,0:T(4,128)(2,1)S(1)}, bf16[1,4,5120]{2,1,0:T(4,128)(2,1)S(1)}, u32[]{:S(2)}, u32[]{:S(2)}) collective-permute-start(bf16[1,4,5120]{2,1,0:T(4,128)(2,1)S(1)} %bitcast.26), channel_id=1, source_target_pairs={{0,8},{1,9},{2,10},{3,11},{4,12},{5,13},{6,14},{7,15},{8,0},{9,1},... | collective-permute-start | bytes 122888 | tf_op jit(solution)/shard_map/ppermute | solution.py:471
  9.9 6.2 %collective-permute-start = (bf16[1,4,5120]{2,1,0:T(4,128)(2,1)S(1)}, bf16[1,4,5120]{2,1,0:T(4,128)(2,1)S(1)}, u32[]{:S(2)}, u32[]{:S(2)}) collective-permute-start(bf16[1,4,5120]{2,1,0:T(4,128)(2,1)S(1)} %bitcast.27), channel_id=1, source_target_pairs={{0,4},{1,5},{2,6},{3,7},{4,8},{5,9},{6,10},{7,11},{8,12},{9,13},{1... | collective-permute-start | bytes 122888 | tf_op jit(solution)/shard_map/ppermute | solution.py:471
  11.0 11.3 %collective-permute-start.9 = (bf16[2,4,3072]{2,1,0:T(4,128)(2,1)S(1)}, bf16[2,4,3072]{2,1,0:T(4,128)(2,1)S(1)}, u32[]{:S(2)}, u32[]{:S(2)}) collective-permute-start(bf16[2,4,3072]{2,1,0:T(4,128)(2,1)S(1)} %pad_maximum_fusion.2.refs_4_), channel_id=1, source_target_pairs={{0,12},{1,13},{2,14},{3,15},{4,0},{5,1},{6,2},{7,3},{8,4},{9,5},{1... | collective-permute-start | bytes 147464 | tf_op jit(solution)/shard_map/ppermute | solution.py:471
  13.8 8.4 %collective-permute-start.8 = (bf16[2,4,3072]{2,1,0:T(4,128)(2,1)S(1)}, bf16[2,4,3072]{2,1,0:T(4,128)(2,1)S(1)}, u32[]{:S(2)}, u32[]{:S(2)}) collective-permute-start(bf16[2,4,3072]{2,1,0:T(4,128)(2,1)S(1)} %pad_maximum_fusion.2.refs_4_), channel_id=1, source_target_pairs={{0,8},{1,9},{2,10},{3,11},{4,12},{5,13},{6,14},{7,15},{8,0},{9,1},... | collective-permute-start | bytes 147464 | tf_op jit(solution)/shard_map/ppermute | solution.py:471
  15.0 7.3 %collective-permute-start.7 = (bf16[2,4,3072]{2,1,0:T(4,128)(2,1)S(1)}, bf16[2,4,3072]{2,1,0:T(4,128)(2,1)S(1)}, u32[]{:S(2)}, u32[]{:S(2)}) collective-permute-start(bf16[2,4,3072]{2,1,0:T(4,128)(2,1)S(1)} %pad_maximum_fusion.2.refs_4_), channel_id=1, source_target_pairs={{0,4},{1,5},{2,6},{3,7},{4,8},{5,9},{6,10},{7,11},{8,12},{9,13},{1... | collective-permute-start | bytes 147464 | tf_op jit(solution)/shard_map/ppermute | solution.py:471
  16.3 5.9 %collective-permute-start.3 = (bf16[4,4,5120]{2,1,0:T(4,128)(2,1)S(1)}, bf16[4,4,5120]{2,1,0:T(4,128)(2,1)S(1)}, u32[]{:S(2)}, u32[]{:S(2)}) collective-permute-start(bf16[4,4,5120]{2,1,0:T(4,128)(2,1)S(1)} %pad_maximum_fusion.refs_0_), channel_id=1, source_target_pairs={{0,2},{1,3},{2,0},{3,1},{4,6},{5,7},{6,4},{7,5},{8,10},{9,11},{10,... | collective-permute-start | bytes 491528 | tf_op jit(solution)/shard_map/ppermute | solution.py:471
  16.9 7.3 %collective-permute-start.4 = (bf16[4,4,5120]{2,1,0:T(4,128)(2,1)S(1)}, bf16[4,4,5120]{2,1,0:T(4,128)(2,1)S(1)}, u32[]{:S(2)}, u32[]{:S(2)}) collective-permute-start(bf16[4,4,5120]{2,1,0:T(4,128)(2,1)S(1)} %pad_maximum_fusion.refs_0_), channel_id=1, source_target_pairs={{0,1},{1,0},{2,3},{3,2},{4,5},{5,4},{6,7},{7,6},{8,9},{9,8},{10,11... | collective-permute-start | bytes 491528 | tf_op jit(solution)/shard_map/ppermute | solution.py:471
  22.2 2.0 %collective-permute-start.5 = (bf16[4,4,5120]{2,1,0:T(4,128)(2,1)S(1)}, bf16[4,4,5120]{2,1,0:T(4,128)(2,1)S(1)}, u32[]{:S(2)}, u32[]{:S(2)}) collective-permute-start(bf16[4,4,5120]{2,1,0:T(4,128)(2,1)S(1)} %collective-permute-done.3.refs_1_), channel_id=1, source_target_pairs={{0,1},{1,0},{2,3},{3,2},{4,5},{5,4},{6,7},{7,6},{8,9},{9,8},{10,11... | collective-permute-start | bytes 491528 | tf_op jit(solution)/shard_map/ppermute | solution.py:471
  22.4 1.8 %collective-permute-start.11 = (bf16[3,2,4,3072]{3,2,1,0:T(4,128)(2,1)S(1)}, bf16[3,2,4,3072]{3,2,1,0:T(4,128)(2,1)S(1)}, u32[]{:S(2)}, u32[]{:S(2)}) collective-permute-start(bf16[3,2,4,3072]{3,2,1,0:T(4,128)(2,1)S(1)} %pad_maximum_fusion.1.refs_5_), channel_id=1, source_target_pairs={{0,1},{1,0},{2,3},{3,2},{4,5},{5,4},{6,7},{7,6},{8,9},{9,8},{10,11... | collective-permute-start | bytes 442376 | tf_op jit(solution)/shard_map/ppermute | solution.py:471
  23.0 1.2 %collective-permute-start.10 = (bf16[2,4,3072]{2,1,0:T(4,128)(2,1)S(1)}, bf16[2,4,3072]{2,1,0:T(4,128)(2,1)S(1)}, u32[]{:S(2)}, u32[]{:S(2)}) collective-permute-start(bf16[2,4,3072]{2,1,0:T(4,128)(2,1)S(1)} %pad_maximum_fusion.2.refs_4_), channel_id=1, source_target_pairs={{0,1},{1,0},{2,3},{3,2},{4,5},{5,4},{6,7},{7,6},{8,9},{9,8},{10,11... | collective-permute-start | bytes 147464 | tf_op jit(solution)/shard_map/ppermute | solution.py:471
  25.0 1.2 %collective-permute-start.12 = (bf16[16,128]{1,0:T(8,128)(2,1)S(1)}, bf16[16,128]{1,0:T(8,128)(2,1)S(1)}, u32[]{:S(2)}, u32[]{:S(2)}) collective-permute-start(bf16[16,128]{1,0:T(8,128)(2,1)S(1)} %get-tuple-element.65.refs_0_), channel_id=1, source_target_pairs={{0,1},{1,0},{2,3},{3,2},{4,5},{5,4},{6,7},{7,6},{8,9},{9,8},{10,11... | collective-permute-start | bytes 12296 | tf_op jit(solution)/shard_map/ppermute | solution.py:474
  26.2 3.6 %collective-permute-start.13 = (bf16[16,128]{1,0:T(8,128)(2,1)S(1)}, bf16[16,128]{1,0:T(8,128)(2,1)S(1)}, u32[]{:S(2)}, u32[]{:S(2)}) collective-permute-start(bf16[16,128]{1,0:T(8,128)(2,1)S(1)} %shard_map.187.refs_0_), channel_id=1, source_target_pairs={{0,2},{1,3},{2,0},{3,1},{4,6},{5,7},{6,4},{7,5},{8,10},{9,11},{10,... | collective-permute-start | bytes 12296 | tf_op jit(solution)/shard_map/ppermute | solution.py:474
  29.8 3.6 %collective-permute-start.14 = (bf16[16,128]{1,0:T(8,128)(2,1)S(1)}, bf16[16,128]{1,0:T(8,128)(2,1)S(1)}, u32[]{:S(2)}, u32[]{:S(2)}) collective-permute-start(bf16[16,128]{1,0:T(8,128)(2,1)S(1)} %shard_map.188.refs_0_), channel_id=1, source_target_pairs={{0,4},{1,5},{2,6},{3,7},{4,0},{5,1},{6,2},{7,3},{8,12},{9,13},{10,... | collective-permute-start | bytes 12296 | tf_op jit(solution)/shard_map/ppermute | solution.py:474
  33.4 4.5 %collective-permute-start.15 = (bf16[16,128]{1,0:T(8,128)(2,1)S(1)}, bf16[16,128]{1,0:T(8,128)(2,1)S(1)}, u32[]{:S(2)}, u32[]{:S(2)}) collective-permute-start(bf16[16,128]{1,0:T(8,128)(2,1)S(1)} %shard_map.189.refs_0_), channel_id=1, source_target_pairs={{0,8},{1,9},{2,10},{3,11},{4,12},{5,13},{6,14},{7,15},{8,0},{9,1},... | collective-permute-start | bytes 12296 | tf_op jit(solution)/shard_map/ppermute | solution.py:474
  53.5 1.9 %collective-permute-start.16 = (bf16[4,16,128]{2,1,0:T(8,128)(2,1)S(1)}, bf16[4,16,128]{2,1,0:T(8,128)(2,1)S(1)}, u32[]{:S(2)}, u32[]{:S(2)}) collective-permute-start(bf16[4,16,128]{2,1,0:T(8,128)(2,1)S(1)} %get-tuple-element.75), channel_id=1, source_target_pairs={{0,1},{1,0},{2,3},{3,2},{4,5},{5,4},{6,7},{7,6},{8,9},{9,8},{10,11... | collective-permute-start | bytes 49160 | tf_op jit(solution)/shard_map/ppermute | solution.py:471
  53.5 3.7 %collective-permute-start.17 = (bf16[4,16,128]{2,1,0:T(8,128)(2,1)S(1)}, bf16[4,16,128]{2,1,0:T(8,128)(2,1)S(1)}, u32[]{:S(2)}, u32[]{:S(2)}) collective-permute-start(bf16[4,16,128]{2,1,0:T(8,128)(2,1)S(1)} %get-tuple-element.76), channel_id=1, source_target_pairs={{0,2},{1,3},{2,0},{3,1},{4,6},{5,7},{6,4},{7,5},{8,10},{9,11},{10,... | collective-permute-start | bytes 49160 | tf_op jit(solution)/shard_map/ppermute | solution.py:471
  53.6 3.6 %collective-permute-start.18 = (bf16[4,16,128]{2,1,0:T(8,128)(2,1)S(1)}, bf16[4,16,128]{2,1,0:T(8,128)(2,1)S(1)}, u32[]{:S(2)}, u32[]{:S(2)}) collective-permute-start(bf16[4,16,128]{2,1,0:T(8,128)(2,1)S(1)} %get-tuple-element.77), channel_id=1, source_target_pairs={{0,3},{1,2},{2,1},{3,0},{4,7},{5,6},{6,5},{7,4},{8,11},{9,10},{10,... | collective-permute-start | bytes 49160 | tf_op jit(solution)/shard_map/ppermute | solution.py:471
  57.2 5.6 %collective-permute-start.19 = (bf16[4,16,128]{2,1,0:T(8,128)(2,1)S(1)}, bf16[4,16,128]{2,1,0:T(8,128)(2,1)S(1)}, u32[]{:S(2)}, u32[]{:S(2)}) collective-permute-start(bf16[4,16,128]{2,1,0:T(8,128)(2,1)S(1)} %get-tuple-element.79), channel_id=1, source_target_pairs={{0,4},{1,5},{2,6},{3,7},{4,8},{5,9},{6,10},{7,11},{8,12},{9,13},{1... | collective-permute-start | bytes 49160 | tf_op jit(solution)/shard_map/ppermute | solution.py:471
  57.6 5.2 %collective-permute-start.20 = (bf16[4,16,128]{2,1,0:T(8,128)(2,1)S(1)}, bf16[4,16,128]{2,1,0:T(8,128)(2,1)S(1)}, u32[]{:S(2)}, u32[]{:S(2)}) collective-permute-start(bf16[4,16,128]{2,1,0:T(8,128)(2,1)S(1)} %get-tuple-element.80), channel_id=1, source_target_pairs={{0,8},{1,9},{2,10},{3,11},{4,12},{5,13},{6,14},{7,15},{8,0},{9,1},... | collective-permute-start | bytes 49160 | tf_op jit(solution)/shard_map/ppermute | solution.py:471
  58.7 4.6 %collective-permute-start.21 = (bf16[4,16,128]{2,1,0:T(8,128)(2,1)S(1)}, bf16[4,16,128]{2,1,0:T(8,128)(2,1)S(1)}, u32[]{:S(2)}, u32[]{:S(2)}) collective-permute-start(bf16[4,16,128]{2,1,0:T(8,128)(2,1)S(1)} %get-tuple-element.81), channel_id=1, source_target_pairs={{0,12},{1,13},{2,14},{3,15},{4,0},{5,1},{6,2},{7,3},{8,4},{9,5},{1... | collective-permute-start | bytes 49160 | tf_op jit(solution)/shard_map/ppermute | solution.py:471
  65.1 2.2 %collective-permute-start.22 = (f32[32,5120]{1,0:T(8,128)S(1)}, f32[32,5120]{1,0:T(8,128)S(1)}, u32[]{:S(2)}, u32[]{:S(2)}) collective-permute-start(f32[32,5120]{1,0:T(8,128)S(1)} %get-tuple-element.84), channel_id=1, source_target_pairs={{0,1},{1,0},{2,3},{3,2},{4,5},{5,4},{6,7},{7,6},{8,9},{9,8},{10,11... | collective-permute-start | bytes 1966088 | tf_op jit(solution)/shard_map/ppermute | solution.py:471
  66.1 2.7 %collective-permute-start.27 = (f32[32,3072]{1,0:T(8,128)S(1)}, f32[32,3072]{1,0:T(8,128)S(1)}, u32[]{:S(2)}, u32[]{:S(2)}) collective-permute-start(f32[32,3072]{1,0:T(8,128)S(1)} %get-tuple-element.93), channel_id=1, source_target_pairs={{0,1},{1,0},{2,3},{3,2},{4,5},{5,4},{6,7},{7,6},{8,9},{9,8},{10,11... | collective-permute-start | bytes 1179656 | tf_op jit(solution)/shard_map/ppermute | solution.py:471
  67.3 6.3 %collective-permute-start.23 = (bf16[16,5120]{1,0:T(8,128)(2,1)S(1)}, bf16[16,5120]{1,0:T(8,128)(2,1)S(1)}, u32[]{:S(2)}, u32[]{:S(2)}) collective-permute-start(bf16[16,5120]{1,0:T(8,128)(2,1)S(1)} %get-tuple-element.86), channel_id=1, source_target_pairs={{0,2},{1,3},{2,0},{3,1},{4,6},{5,7},{6,4},{7,5},{8,10},{9,11},{10,... | collective-permute-start | bytes 491528 | tf_op jit(solution)/shard_map/ppermute | solution.py:471
  68.8 8.7 %collective-permute-start.28 = (bf16[8,3072]{1,0:T(8,128)(2,1)S(1)}, bf16[8,3072]{1,0:T(8,128)(2,1)S(1)}, u32[]{:S(2)}, u32[]{:S(2)}) collective-permute-start(bf16[8,3072]{1,0:T(8,128)(2,1)S(1)} %get-tuple-element.95), channel_id=1, source_target_pairs={{0,4},{1,5},{2,6},{3,7},{4,8},{5,9},{6,10},{7,11},{8,12},{9,13},{1... | collective-permute-start | bytes 147464 | tf_op jit(solution)/shard_map/ppermute | solution.py:471
  70.9 7.3 %collective-permute-start.29 = (bf16[8,3072]{1,0:T(8,128)(2,1)S(1)}, bf16[8,3072]{1,0:T(8,128)(2,1)S(1)}, u32[]{:S(2)}, u32[]{:S(2)}) collective-permute-start(bf16[8,3072]{1,0:T(8,128)(2,1)S(1)} %get-tuple-element.96), channel_id=1, source_target_pairs={{0,8},{1,9},{2,10},{3,11},{4,12},{5,13},{6,14},{7,15},{8,0},{9,1},... | collective-permute-start | bytes 147464 | tf_op jit(solution)/shard_map/ppermute | solution.py:471
  72.7 5.5 %collective-permute-start.30 = (bf16[8,3072]{1,0:T(8,128)(2,1)S(1)}, bf16[8,3072]{1,0:T(8,128)(2,1)S(1)}, u32[]{:S(2)}, u32[]{:S(2)}) collective-permute-start(bf16[8,3072]{1,0:T(8,128)(2,1)S(1)} %get-tuple-element.97), channel_id=1, source_target_pairs={{0,12},{1,13},{2,14},{3,15},{4,0},{5,1},{6,2},{7,3},{8,4},{9,5},{1... | collective-permute-start | bytes 147464 | tf_op jit(solution)/shard_map/ppermute | solution.py:471
  73.7 8.5 %collective-permute-start.24 = (bf16[4,5120]{1,0:T(4,128)(2,1)S(1)}, bf16[4,5120]{1,0:T(4,128)(2,1)S(1)}, u32[]{:S(2)}, u32[]{:S(2)}) collective-permute-start(bf16[4,5120]{1,0:T(4,128)(2,1)S(1)} %get-tuple-element.88), channel_id=1, source_target_pairs={{0,4},{1,5},{2,6},{3,7},{4,8},{5,9},{6,10},{7,11},{8,12},{9,13},{1... | collective-permute-start | bytes 122888 | tf_op jit(solution)/shard_map/ppermute | solution.py:471
  75.7 6.4 %collective-permute-start.25 = (bf16[4,5120]{1,0:T(4,128)(2,1)S(1)}, bf16[4,5120]{1,0:T(4,128)(2,1)S(1)}, u32[]{:S(2)}, u32[]{:S(2)}) collective-permute-start(bf16[4,5120]{1,0:T(4,128)(2,1)S(1)} %get-tuple-element.89), channel_id=1, source_target_pairs={{0,8},{1,9},{2,10},{3,11},{4,12},{5,13},{6,14},{7,15},{8,0},{9,1},... | collective-permute-start | bytes 122888 | tf_op jit(solution)/shard_map/ppermute | solution.py:471
  77.5 4.6 %collective-permute-start.26 = (bf16[4,5120]{1,0:T(4,128)(2,1)S(1)}, bf16[4,5120]{1,0:T(4,128)(2,1)S(1)}, u32[]{:S(2)}, u32[]{:S(2)}) collective-permute-start(bf16[4,5120]{1,0:T(4,128)(2,1)S(1)} %get-tuple-element.90), channel_id=1, source_target_pairs={{0,12},{1,13},{2,14},{3,15},{4,0},{5,1},{6,2},{7,3},{8,4},{9,5},{1... | collective-permute-start | bytes 122888 | tf_op jit(solution)/shard_map/ppermute | solution.py:471
  78.2 3.9 %collective-permute-start.31 = (bf16[4,3072]{1,0:T(4,128)(2,1)S(1)}, bf16[4,3072]{1,0:T(4,128)(2,1)S(1)}, u32[]{:S(2)}, u32[]{:S(2)}) collective-permute-start(bf16[4,3072]{1,0:T(4,128)(2,1)S(1)} %get-tuple-element.99), channel_id=1, source_target_pairs={{0,2},{1,3},{2,0},{3,1},{4,6},{5,7},{6,4},{7,5},{8,10},{9,11},{10,... | collective-permute-start | bytes 73736 | tf_op jit(solution)/shard_map/ppermute | solution.py:471
  (21 other events, 296.8 us)

commit v6 on v4

--- a/solution.py
+++ b/solution.py
@@ -98,7 +98,7 @@
 
     def device_of(block, sign):
         c, m, f = block // (far * near), block // far % near, block % far
-        f = (far_at + sign * f + far) % far
+        f = f if sign < 0 else (far_at + f) % far
         m = (near_at + sign * m + near) % near
         c = (core_at + sign * c + cores) % cores
         return (f * near + m) * cores + c
@@ -189,11 +189,8 @@
     out_ref[...] = packed.astype(BF16)
 
 
-def join_body(*refs):
-    total = refs[0][...].astype(F32)
-    for ref in refs[1:-1]:
-        total = total + ref[...].astype(F32)
-    refs[-1][...] = total.astype(BF16)
+def join_body(came_ref, out_ref):
+    out_ref[...] = jnp.sum(came_ref[...].astype(F32), axis=0).astype(BF16)
 
 
 def base_body(depth, x_ref, q_ref, k_ref, v_ref, oq_ref, okv_ref):
@@ -222,15 +219,10 @@
 
 
 def ready_body(
-    rank, lows, oq_ref, okv_ref, *refs
+    rank, oq_ref, okv_ref, low_ref, unplace_ref, slot_ref, uq_ref, uv_ref, cos_ref, sin_ref,
+    kcos_ref, ksin_ref, send_ref, out_ref,
 ):
-    low_refs = refs[:lows]
-    (
-        unplace_ref, slot_ref, uq_ref, uv_ref, cos_ref, sin_ref, kcos_ref, ksin_ref, send_ref, out_ref,
-    ) = refs[lows:]
-    packed = low_refs[0][...].astype(F32)
-    for ref in low_refs[1:]:
-        packed = packed + ref[...].astype(F32)
+    packed = jnp.sum(low_ref[...].astype(F32), axis=0)
     pack = HEAD // (2 * rank)
     low = jnp.concatenate(
         [packed[:, i * 2 * rank : (i + 1) * 2 * rank] for i in range(pack)], axis=0
@@ -262,7 +254,9 @@
     out_ref[...] = dot(send_ref[...], stacked).astype(BF16).reshape(out_ref.shape)
 
 
-def attend_body(own, columns, index_ref, len_ref, x_ref, order_ref, k_ref, v_ref, ctx_ref, nk_ref, nv_ref, s_ref):
+def attend_body(
+    own, columns, index_ref, len_ref, x_ref, order_ref, k_ref, v_ref, nk_ref, nv_ref, ctx_ref, s_ref
+):
     n, span = x_ref.shape[0], k_ref.shape[1]
     group = HEADS // KV_HEADS
     local = HEADS // n
@@ -325,21 +319,34 @@
         ctx_ref[i] = jnp.concatenate(block, axis=0).astype(BF16)
 
 
-def out_body(tile, ctx_ref, take_ref, w_ref, mine_ref, other_ref, a_ref):
+def take_body(ctx_ref, take_ref, w_ref, a_ref, mine_ref, other_ref):
     rows = a_ref.shape[0]
-    n = ctx_ref.shape[0]
-    x = ctx_ref[...].reshape(n * ctx_ref.shape[1], HEAD)
+    x = ctx_ref[...].reshape(-1, HEAD)
     taken = dot(take_ref[...], x).astype(BF16)
     for h in range(a_ref.shape[1] // HEAD):
         a_ref[:, h * HEAD : (h + 1) * HEAD] = taken[h * rows : (h + 1) * rows]
+    out_body(0, a_ref, w_ref, mine_ref, other_ref)
+
+
+def out_body(start, a_ref, w_ref, mine_ref, other_ref):
     half = mine_ref.shape[0]
-
-    @pl.loop(0, w_ref.shape[1] // tile)
+    tile = 1024
+
+    @pl.loop(0, mine_ref.shape[1] // tile)
     def _(i):
         at = pl.ds(pl.multiple_of(i * tile, tile), tile)
-        product = dot(a_ref[...], w_ref[:, at])
+        product = dot(a_ref[...], w_ref[:, pl.ds(pl.multiple_of(start + i * tile, tile), tile)])
         mine_ref[:, at] = product[:half]
         other_ref[:, at] = product[half:]
+
+
+def far_first_body(near, mine_ref, came_ref, *refs):
+    total = mine_ref[...] + came_ref[...]
+    rows = refs[0].shape[0] // near
+    for f, ref in enumerate(refs):
+        blocks = [(m * len(refs) + f) * rows for m in range(near)]
+        value = jnp.concatenate([total[at : at + rows] for at in blocks], axis=0)
+        ref[...] = value.astype(ref.dtype)
 
 
 def near_body(mine_ref, came_ref, *refs):
@@ -361,11 +368,15 @@
         ref[...] = total[f * rows : (f + 1) * rows].astype(BF16)
 
 
-def last_body(came, first_ref, second_ref, keep_ref, *refs):
-    one_ref, two_ref = refs[came:]
-    total = keep_ref[...]
-    for ref in refs[:came]:
-        total = total + ref[...].astype(F32)
+def last_body(longs, first_ref, second_ref, *refs):
+    one_ref, two_ref = refs[-2:]
+    totals = []
+    for part in (refs[:longs], refs[longs:-2]):
+        total = part[0][...]
+        for ref in part[1:]:
+            total = total + ref[...].astype(F32)
+        totals.append(total)
+    total = jnp.concatenate(totals, axis=1)
     own = one_ref.shape[0]
     one_ref[...] = (first_ref[...].astype(F32) + total[:own]).astype(BF16)
     two_ref[...] = (second_ref[...].astype(F32) + total[own:]).astype(BF16)
@@ -414,6 +425,16 @@
     def shift(value, f, m, c):
         return lax.ppermute(value, "serve", partner(f, m, c))
 
+    plane = near * cores
+
+    def along_far(value):
+        groups = [[f * plane + p for f in range(far)] for p in range(plane)]
+        return lax.all_gather(value, "serve", axis_index_groups=groups)
+
+    def along_plane(value):
+        groups = [[f * plane + p for p in range(plane)] for f in range(far)]
+        return lax.all_gather(value, "serve", axis_index_groups=groups)
+
     gain = attention_norm_gain.reshape(width // HEAD, HEAD)
     normed = whole_call(
         norm_body,
@@ -428,8 +449,7 @@
         ],
         cost=1.0,
     )
-    normed = normed[None]
-    groups = [jnp.concatenate([normed] + [shift(normed, f, 0, 0) for f in range(1, far)])]
+    groups = [along_far(normed)]
     groups += [shift(groups[0], 0, m, 0) for m in range(1, near)]
 
     groups[0], at = lax.optimization_barrier((groups[0], index[None]))
@@ -465,7 +485,7 @@
     )
     slot, groups[1] = lax.optimization_barrier((slot, groups[1]))
 
-    groups += [shift(group, 0, 0, c) for c in range(1, cores) for group in groups[:near]]
+    groups += [shift(part, 0, 0, c) for c in range(1, cores) for part in groups[:near]]
 
     query_down = jnp.swapaxes(query_down_weights, 1, 2).reshape(adapters * rank, width)
     value_down = jnp.swapaxes(value_down_weights, 1, 2).reshape(adapters * rank, width)
@@ -479,11 +499,9 @@
         (*groups, query_down, value_down, near_slot, place),
         cost=0.3,
     )
-    lows = [shift(low, 0, m, c) for m in range(near) for c in range(cores) if m + c]
-    low = whole_call(
-        join_body, jax.ShapeDtypeStruct(low.shape, BF16), (low, *lows), cost=0.1
-    )
-    lows = [low] + [shift(low, f, 0, 0) for f in range(1, far)]
+    lows = along_plane(low)
+    low = whole_call(join_body, jax.ShapeDtypeStruct(low.shape, BF16), (lows,), cost=0.1)
+    lows = along_far(low)
 
     base_q, base_kv = whole_call(
         functools.partial(base_body, 2048),
@@ -496,12 +514,12 @@
     )
 
     ready = whole_call(
-        functools.partial(ready_body, rank, len(lows)),
+        functools.partial(ready_body, rank),
         jax.ShapeDtypeStruct((n, sent, HEAD), BF16),
         (
             base_q,
             base_kv,
-            *lows,
+            lows,
             unplace,
             slot,
             query_up_weights.reshape(stored * rank, query_cols),
@@ -516,13 +534,10 @@
     )
     arrived = lax.all_to_all(ready, "serve", split_axis=0, concat_axis=0, tiled=True)
 
-    context, new_keys, new_values = whole_call(
+    fresh = jax.ShapeDtypeStruct((own, STEPS, KV_HEADS * HEAD), BF16)
+    new_keys, new_values, context = whole_call(
         functools.partial(attend_body, own, key_cols),
-        (
-            jax.ShapeDtypeStruct((n, rows * local, HEAD), BF16),
-            jax.ShapeDtypeStruct((own, STEPS, KV_HEADS * HEAD), BF16),
-            jax.ShapeDtypeStruct((own, STEPS, KV_HEADS * HEAD), BF16),
-        ),
+        (fresh, fresh, jax.ShapeDtypeStruct((n, rows * local, HEAD), BF16)),
         (index[None], lengths, arrived, order, rotated_key_cache, stored_value_cache),
         smem=2,
         scratch=[pltpu.VMEM((own * HEADS * STEPS, HEAD), F32)],
@@ -530,37 +545,61 @@
     )
     context = lax.all_to_all(context, "serve", split_axis=0, concat_axis=0, tiled=True)
 
-    kinds = jax.ShapeDtypeStruct((all_rows // cores, width), F32)
-    mine, other = whole_call(
-        functools.partial(out_body, 1024),
-        (kinds, kinds),
+    half = all_rows // cores
+    cut = width * 5 // 8
+
+    def kinds(count, columns):
+        return (jax.ShapeDtypeStruct((count, columns), F32),) * 2
+
+    taken, mine_long, other_long = whole_call(
+        take_body,
+        (jax.ShapeDtypeStruct((all_rows, query_cols), BF16),) + kinds(half, cut),
         (context, take, output_matrix),
-        scratch=[pltpu.VMEM((all_rows, query_cols), BF16)],
-        cost=0.5,
-    )
-
-    def kind(count, dtype):
-        return jax.ShapeDtypeStruct((count * rows, width), dtype)
+        cost=0.4,
+    )
+    mine_short, other_short = whole_call(
+        functools.partial(out_body, cut),
+        kinds(half, width - cut),
+        (taken, output_matrix),
+        cost=0.3,
+    )
+
+    def kind(count, columns, dtype):
+        return jax.ShapeDtypeStruct((count * rows, columns), dtype)
 
     keep, *others = whole_call(
         near_body,
-        (kind(far, F32),) + (kind(far, BF16),) * (near - 1),
-        (mine, shift(other, 0, 0, 1)),
+        (kind(far, cut, F32),) + (kind(far, cut, BF16),) * (near - 1),
+        (mine_long, shift(other_long, 0, 0, 1)),
         cost=0.1,
     )
     others = [shift(other, 0, m, 0) for m, other in enumerate(others, 1)]
+    short, *sides = whole_call(
+        functools.partial(far_first_body, near),
+        (kind(near, width - cut, F32),) + (kind(near, width - cut, BF16),) * (far - 1),
+        (mine_short, shift(other_short, 0, 0, 1)),
+        cost=0.1,
+    )
+    sides = [shift(side, f, 0, 0) for f, side in enumerate(sides, 1)]
     keep, *others = whole_call(
         functools.partial(far_body, len(others)),
-        (kind(1, F32),) + (kind(1, BF16),) * (far - 1),
+        (kind(1, cut, F32),) + (kind(1, cut, BF16),) * (far - 1),
         (keep, *others),
         cost=0.1,
     )
     others = [shift(other, f, 0, 0) for f, other in enumerate(others, 1)]
+    short, *sides = whole_call(
+        functools.partial(far_body, len(sides)),
+        (kind(1, width - cut, F32),) + (kind(1, width - cut, BF16),) * (near - 1),
+        (short, *sides),
+        cost=0.1,
+    )
+    sides = [shift(side, 0, m, 0) for m, side in enumerate(sides, 1)]
     result = jax.ShapeDtypeStruct((own, width), BF16)
     out_one, out_two = whole_call(
-        functools.partial(last_body, len(others)),
+        functools.partial(last_body, 1 + len(others)),
         (result, result),
-        (residual_first, residual_second, keep, *others),
+        (residual_first, residual_second, keep, *others, short, *sides),
         cost=0.1,
     )
     return (out_one, out_two, new_keys, new_values)

time: 82.7 us -> 93.8 us (1.13)
  blocking collectives: 19.5 us -> 56.5 us
  waiting for transfers between devices: 26.8 us -> 7.32 us
  starting transfers between devices: 17.3 us -> 11.1 us
    all_gather x0 -> x3, blocking collectives: none -> 34.1 us  [the longest x2 28.8 us: along_far(): return lax.all_gather(value, 'serve', axis_index_groups=groups)]
    ppermute x17 -> x13, waiting for transfers between devices: 26.8 us -> 7.32 us  [shift(): return lax.ppermute(value, 'serve', partner(f, m, c))]
    ppermute x17 -> x13, starting transfers between devices: 17.3 us -> 11.1 us  [shift(): return lax.ppermute(value, 'serve', partner(f, m, c))]
    all_to_all x1, blocking collectives: 9.99 us -> 12.9 us  [shards(): lax.all_to_all(ready, 'serve', split_axis=0, concat_axis=0, tiled=True)]
    pallas_call x11 -> x14, Pallas kernels: 11.9 us -> 11.9 us  [whole_call(): pl.pallas_call(body, out_shape=out_shape, in_specs=specs, out_specs=tuple...]
  transfers between devices with their start and end apart: 17 -> 13, of which waited for: 11 -> 5; matrix products, arithmetic and copies ran while one was open for 0% -> 0% of each run, Pallas kernels for 5% -> 3%
where the time goes in v6:
time: 93.8 us; the launch traced here: 93.4 us
  blocking collectives  56.5 us (60%)
  Pallas kernels  11.9 us (13%)
  starting transfers between devices  11.1 us (12%)
  waiting for transfers between devices  7.32 us (8%)
  local copies, waits for them, and re-layouts  5.64 us (6%)
    all_gather x2, blocking collectives, along_far(): return lax.all_gather(value, 'serve', axis_index_groups=groups)  28.8 us
    all_to_all x1, blocking collectives, shards(): lax.all_to_all(ready, 'serve', split_axis=0, concat_axis=0, tiled=True)  12.9 us
    pallas_call x14, Pallas kernels, whole_call(): pl.pallas_call(body, out_shape=out_shape, in_specs=specs, out_specs=tuple...  11.9 us
    ppermute x13, starting transfers between devices, shift(): return lax.ppermute(value, 'serve', partner(f, m, c))  11.1 us
    all_to_all x1, blocking collectives, shards(): lax.all_to_all(context, 'serve', split_axis=0, concat_axis=0, tiled=True)  9.48 us
    ppermute x13, waiting for transfers between devices, shift(): return lax.ppermute(value, 'serve', partner(f, m, c))  7.32 us
    unnamed x42, local copies, waits for them, and re-layouts  5.64 us
    all_gather x1, blocking collectives, along_plane(): return lax.all_gather(value, 'serve', axis_index_groups=groups)  5.32 us
  transfers between devices with their start and end apart: 13, of which 5 were waited for; matrix products, arithmetic and copies ran while one was open for 0% of the time, Pallas kernels for 3%

profile of v6, /device:TPU:0, one launch (start us, length us, event | category | flops | bytes accessed | tf_op | source)
XLA Modules:
  0.0 93.4 jit_solution(9889638485051231757)
XLA Ops:
  0.6 0.7 copy-done.8
  1.4 0.8 copy-done.10
  2.2 0.7 copy-done.12
  2.9 0.4 shard_map.183
  3.3 15.6 %all-gather.3.refs_0_ = bf16[4,4,8192]{2,1,0:T(4,128)(2,1)S(1)} all-gather(bf16[1,4,8192]{2,1,0:T(4,128)(2,1)S(1)} %bitcast.23), channel_id=2, replica_groups={{0,4,8,12},{1,5,9,13},{2,6,10,14},{3,7,11,15},{16,20,24,28},{17,21,25,2..., dimensions={0}, use_global_device_ids=true | all-gather | bytes 327680 | tf_op jit(solution)/shard_map/all_gather | solution.py:432
  18.9 1.5 %collective-permute-start = (bf16[4,4,8192]{2,1,0:T(4,128)(2,1)S(1)}, bf16[4,4,8192]{2,1,0:T(4,128)(2,1)S(1)}, u32[]{:S(2)}, u32[]{:S(2)}) collective-permute-start(bf16[4,4,8192]{2,1,0:T(4,128)(2,1)S(1)} %all-gather.3.refs_0_), channel_id=1, source_target_pairs={{0,2},{1,3},{2,0},{3,1},{4,6},{5,7},{6,4},{7,5},{8,10},{9,11},{10,... | collective-permute-start | bytes 786440 | tf_op jit(solution)/shard_map/ppermute | solution.py:426
  20.5 0.8 copy-done.13
  21.3 1.1 %copy-done.14 = s32[32]{0:T(128)S(1)} copy-done((s32[32]{0:T(128)S(1)}, s32[32]{0:T(128)}, u32[]{:S(2)}) %copy-start.14) | copy-done | bytes 152
  22.5 1.4 %copy-done.15 = s32[32]{0:T(128)S(1)} copy-done((s32[32]{0:T(128)S(1)}, s32[32]{0:T(128)}, u32[]{:S(2)}) %copy-start.15) | copy-done | bytes 152
  23.9 1.8 %shard_map.184 = (s32[64,1]{1,0:T(8,128)S(1)}, s32[64,1]{1,0:T(8,128)S(1)}, f32[64,128]{1,0:T(8,128)S(1)}, f32[64,128]{1,0:T(8,128)S(1)}, f32[64,128]{1,0:T(8,12...) custom-call(s32[1]{0:T(128)} %bitcast.index_ref, ...), custom_call_target="tpu_custom_call" | custom-call | flops 4600000000 | tf_op jit(solution)/shard_map/pallas_call | solution.py:36
  25.8 1.5 %collective-permute-done.2.refs_3_ = bf16[4,4,8192]{2,1,0:T(4,128)(2,1)S(1)} collective-permute-done((bf16[4,4,8192]{2,1,0:T(4,128)(2,1)S(1)}, bf16[4,4,8192]{2,1,0:T(4,128)(2,1)S(1)}, u32[]{:S(2)}, u32[]{:S(2)}) %collective-permute-start.2) | collective-permute-done | bytes 262176 | tf_op jit(solution)/shard_map/ppermute | solution.py:426
  27.3 0.7 shard_map.185
  28.1 5.3 %all-gather.1 = bf16[64,128]{1,0:T(8,128)(2,1)S(1)} all-gather(bf16[16,128]{1,0:T(8,128)(2,1)S(1)} %get-tuple-element.54), channel_id=3, replica_groups={{0,1,2,3},{4,5,6,7},{8,9,10,11},{12,13,14,15},{16,17,18,19},{20,21,22,2..., dimensions={0}, use_global_device_ids=true | all-gather | bytes 20480 | tf_op jit(solution)/shard_map/all_gather | solution.py:436
  33.4 13.2 %all-gather.2 = bf16[64,128]{1,0:T(8,128)(2,1)S(1)} all-gather(bf16[16,128]{1,0:T(8,128)(2,1)S(1)} %shard_map.187), channel_id=4, replica_groups={{0,4,8,12},{1,5,9,13},{2,6,10,14},{3,7,11,15},{16,20,24,28},{17,21,25,2..., dimensions={0}, use_global_device_ids=true | all-gather | bytes 20480 | tf_op jit(solution)/shard_map/all_gather | solution.py:432
  46.6 2.7 %shard_map.186 = (f32[64,512]{1,0:T(8,128)S(1)}, f32[64,128]{1,0:T(8,128)S(1)}) custom-call(bf16[64,8192]{1,0:T(8,128)(2,1)S(1)} %get-tuple-element.51.x_ref, bf16[8192,512]{1,0:T(8,128)(2,1)S(1)} %bitcast.18, bf16[64,8192]{1,0:T(8,128)(2,1)S(1)} %bitcast.19, bf16[64,8192]{1,0:T(8,128)(2,1)S(1)} %bitcast.20), custom_call_target="tpu_custom_call" | custom-call | flops 690000000 | tf_op jit(solution)/shard_map/pallas_call | solution.py:36
  49.3 0.8 shard_map.188
  50.2 12.9 %all_to_all.10.x_ref = bf16[16,24,128]{2,1,0:T(8,128)(2,1)S(1)} all-to-all(bf16[16,24,128]{2,1,0:T(8,128)(2,1)S(1)} %shard_map.188), channel_id=1, replica_groups=mesh['replica'=2,'serve'=16] {'serve'}, dimensions={0} | all-to-all | bytes 196608 | tf_op jit(solution)/shard_map/all_to_all | solution.py:535
  63.0 2.0 %shard_map.189 = (bf16[2,2,1024]{2,1,0:T(2,128)(2,1)}, bf16[2,2,1024]{2,1,0:T(2,128)(2,1)}, bf16[16,16,128]{2,1,0:T(8,128)(2,1)S(1)}) custom-call(s32[1]{0:T(128)} %bitcast.index_ref, s32[32]{0:T(128)S(1)} %copy-done.16, bf16[16,24,128]{2,1,0:T(8,128)(2,1)S(1)} %all_to_all.10.x_ref, bf16[256,384]{1,0:T(8,128)(2,1)S(1)} %get-tuple-element.62.order_ref, ...), custom_call_target="tpu_custom_call" | custom-call | flops 1150000000 | tf_op jit(solution)/shard_map/pallas_call | solution.py:36
  65.0 9.5 %all_to_all.11.ctx_ref = bf16[16,16,128]{2,1,0:T(8,128)(2,1)S(1)} all-to-all(bf16[16,16,128]{2,1,0:T(8,128)(2,1)S(1)} %get-tuple-element.63), channel_id=1, replica_groups=mesh['replica'=2,'serve'=16] {'serve'}, dimensions={0} | all-to-all | bytes 131072 | tf_op jit(solution)/shard_map/all_to_all | solution.py:546
  74.5 1.7 %shard_map.190 = (bf16[64,512]{1,0:T(8,128)(2,1)S(1)}, f32[32,5120]{1,0:T(8,128)S(1)}, f32[32,5120]{1,0:T(8,128)S(1)}) custom-call(bf16[16,16,128]{2,1,0:T(8,128)(2,1)S(1)} %all_to_all.11.ctx_ref, bf16[256,256]{1,0:T(8,128)(2,1)S(1)} %get-tuple-element.64.take_ref, bf16[512,8192]{1,0:T(8,128)(2,1)S(1)} %bitcast.16), custom_call_target="tpu_custom_call" | custom-call | flops 460000000 | tf_op jit(solution)/shard_map/pallas_call | solution.py:36
  76.3 0.9 shard_map.193
  77.2 0.6 collective-permute-start.8
  77.8 0.6 collective-permute-done.3.came_ref
  78.6 0.5 collective-permute-done.8.came_ref
  79.4 1.0 %collective-permute-start.10 = (bf16[8,3072]{1,0:T(8,128)(2,1)S(1)}, bf16[8,3072]{1,0:T(8,128)(2,1)S(1)}, u32[]{:S(2)}, u32[]{:S(2)}) collective-permute-start(bf16[8,3072]{1,0:T(8,128)(2,1)S(1)} %get-tuple-element.78), channel_id=1, source_target_pairs={{0,8},{1,9},{2,10},{3,11},{4,12},{5,13},{6,14},{7,15},{8,0},{9,1},... | collective-permute-start | bytes 147464 | tf_op jit(solution)/shard_map/ppermute | solution.py:426
  80.3 2.7 %collective-permute-start.11 = (bf16[8,3072]{1,0:T(8,128)(2,1)S(1)}, bf16[8,3072]{1,0:T(8,128)(2,1)S(1)}, u32[]{:S(2)}, u32[]{:S(2)}) collective-permute-start(bf16[8,3072]{1,0:T(8,128)(2,1)S(1)} %get-tuple-element.79), channel_id=1, source_target_pairs={{0,12},{1,13},{2,14},{3,15},{4,0},{5,1},{6,2},{7,3},{8,4},{9,5},{1... | collective-permute-start | bytes 147464 | tf_op jit(solution)/shard_map/ppermute | solution.py:426
  83.1 1.7 %collective-permute-done.4.refs_1_ = bf16[16,5120]{1,0:T(8,128)(2,1)S(1)} collective-permute-done((bf16[16,5120]{1,0:T(8,128)(2,1)S(1)}, bf16[16,5120]{1,0:T(8,128)(2,1)S(1)}, u32[]{:S(2)}, u32[]{:S(2)}) %collective-permute-start.4) | collective-permute-done | bytes 163872 | tf_op jit(solution)/shard_map/ppermute | solution.py:426
  85.0 0.9 %collective-permute-start.6 = (bf16[4,5120]{1,0:T(4,128)(2,1)S(1)}, bf16[4,5120]{1,0:T(4,128)(2,1)S(1)}, u32[]{:S(2)}, u32[]{:S(2)}) collective-permute-start(bf16[4,5120]{1,0:T(4,128)(2,1)S(1)} %get-tuple-element.71), channel_id=1, source_target_pairs={{0,8},{1,9},{2,10},{3,11},{4,12},{5,13},{6,14},{7,15},{8,0},{9,1},... | collective-permute-start | bytes 122888 | tf_op jit(solution)/shard_map/ppermute | solution.py:426
  85.9 2.8 %collective-permute-start.7 = (bf16[4,5120]{1,0:T(4,128)(2,1)S(1)}, bf16[4,5120]{1,0:T(4,128)(2,1)S(1)}, u32[]{:S(2)}, u32[]{:S(2)}) collective-permute-start(bf16[4,5120]{1,0:T(4,128)(2,1)S(1)} %get-tuple-element.72), channel_id=1, source_target_pairs={{0,12},{1,13},{2,14},{3,15},{4,0},{5,1},{6,2},{7,3},{8,4},{9,5},{1... | collective-permute-start | bytes 122888 | tf_op jit(solution)/shard_map/ppermute | solution.py:426
  88.7 0.9 collective-permute-start.12
  89.6 3.0 %collective-permute-done.12.refs_5_ = bf16[4,3072]{1,0:T(4,128)(2,1)S(1)} collective-permute-done((bf16[4,3072]{1,0:T(4,128)(2,1)S(1)}, bf16[4,3072]{1,0:T(4,128)(2,1)S(1)}, u32[]{:S(2)}, u32[]{:S(2)}) %collective-permute-start.12) | collective-permute-done | bytes 24608 | tf_op jit(solution)/shard_map/ppermute | solution.py:426
  92.7 0.7 shard_map.196
  (57 shorter events, 1.1 us)
Async XLA Ops:
  0.6 0.8 copy-start.8
  18.9 6.8 %collective-permute-start = (bf16[4,4,8192]{2,1,0:T(4,128)(2,1)S(1)}, bf16[4,4,8192]{2,1,0:T(4,128)(2,1)S(1)}, u32[]{:S(2)}, u32[]{:S(2)}) collective-permute-start(bf16[4,4,8192]{2,1,0:T(4,128)(2,1)S(1)} %all-gather.3.refs_0_), channel_id=1, source_target_pairs={{0,2},{1,3},{2,0},{3,1},{4,6},{5,7},{6,4},{7,5},{8,10},{9,11},{10,... | collective-permute-start | bytes 786440 | tf_op jit(solution)/shard_map/ppermute | solution.py:426
  20.4 26.2 %slice-start.2 = ((s8[8388608]{0:T(1024)(128)(4,1)}), s8[4194304]{0:T(1024)(128)(4,1)S(1)}, s32[]{:S(2)}) async-start(s8[8388608]{0:T(1024)(128)(4,1)} %bitcast.17), calls=%async_computation.4 | async-start | bytes 8388608
  20.4 6.9 %copy-start.2 = (bf16[2,8192,16]{1,2,0:T(8,128)(2,1)S(1)}, bf16[2,8192,16]{1,2,0:T(8,128)(2,1)}, u32[]{:S(2)}) copy-start(bf16[2,8192,16]{1,2,0:T(8,128)(2,1)} %param.23) | copy-start | bytes 1572868
  20.4 6.9 %copy-start.3 = (bf16[2,8192,16]{1,2,0:T(8,128)(2,1)S(1)}, bf16[2,8192,16]{1,2,0:T(8,128)(2,1)}, u32[]{:S(2)}) copy-start(bf16[2,8192,16]{1,2,0:T(8,128)(2,1)} %param.24) | copy-start | bytes 1572868
  20.4 26.2 %slice-start.3 = ((s8[8388608]{0:T(1024)(128)(4,1)}), s8[4194304]{0:T(1024)(128)(4,1)S(1)}, s32[]{:S(2)}) async-start(s8[8388608]{0:T(1024)(128)(4,1)} %bitcast.17), calls=%async_computation.5 | async-start | bytes 8388608
  20.4 26.2 %copy-start = (bf16[8192,64]{0,1:T(8,128)(2,1)S(1)}, bf16[8192,64]{0,1:T(8,128)(2,1)}, u32[]{:S(2)}) copy-start(bf16[8192,64]{0,1:T(8,128)(2,1)} %param.20) | copy-start | bytes 3145732
  20.4 26.2 %copy-start.1 = (bf16[8192,64]{0,1:T(8,128)(2,1)S(1)}, bf16[8192,64]{0,1:T(8,128)(2,1)}, u32[]{:S(2)}) copy-start(bf16[8192,64]{0,1:T(8,128)(2,1)} %param.21) | copy-start | bytes 3145732
  20.5 5.3 %collective-permute-start.1 = (bf16[4,4,8192]{2,1,0:T(4,128)(2,1)S(1)}, bf16[4,4,8192]{2,1,0:T(4,128)(2,1)S(1)}, u32[]{:S(2)}, u32[]{:S(2)}) collective-permute-start(bf16[4,4,8192]{2,1,0:T(4,128)(2,1)S(1)} %all-gather.3.refs_0_), channel_id=1, source_target_pairs={{0,1},{1,0},{2,3},{3,2},{4,5},{5,4},{6,7},{7,6},{8,9},{9,8},{10,11... | collective-permute-start | bytes 786440 | tf_op jit(solution)/shard_map/ppermute | solution.py:426
  20.5 0.8 copy-start.13
  21.3 1.1 %copy-start.14 = (s32[32]{0:T(128)S(1)}, s32[32]{0:T(128)}, u32[]{:S(2)}) copy-start(s32[32]{0:T(128)} %slot_hbm.1) | copy-start | bytes 388
  22.5 1.4 %copy-start.15 = (s32[32]{0:T(128)S(1)}, s32[32]{0:T(128)}, u32[]{:S(2)}) copy-start(s32[32]{0:T(128)} %len_ref.1) | copy-start | bytes 388
  25.7 23.6 %copy-start.6 = (bf16[32,16,512]{2,1,0:T(8,128)(2,1)S(1)}, bf16[32,16,512]{2,1,0:T(8,128)(2,1)}, u32[]{:S(2)}) copy-start(bf16[32,16,512]{2,1,0:T(8,128)(2,1)} %param.25) | copy-start | bytes 1572868
  25.7 23.6 %copy-start.7 = (bf16[32,16,64]{2,1,0:T(8,128)(2,1)S(1)}, bf16[32,16,64]{2,1,0:T(8,128)(2,1)}, u32[]{:S(2)}) copy-start(bf16[32,16,64]{2,1,0:T(8,128)(2,1)} %param.26) | copy-start | bytes 196612
  25.7 1.6 %collective-permute-start.2 = (bf16[4,4,8192]{2,1,0:T(4,128)(2,1)S(1)}, bf16[4,4,8192]{2,1,0:T(4,128)(2,1)S(1)}, u32[]{:S(2)}, u32[]{:S(2)}) collective-permute-start(bf16[4,4,8192]{2,1,0:T(4,128)(2,1)S(1)} %collective-permute-done.refs_1_), channel_id=1, source_target_pairs={{0,1},{1,0},{2,3},{3,2},{4,5},{5,4},{6,7},{7,6},{8,9},{9,8},{10,11... | collective-permute-start | bytes 786440 | tf_op jit(solution)/shard_map/ppermute | solution.py:426
  28.0 35.0 %copy-start.4 = (bf16[2,384,1024]{2,1,0:T(8,128)(2,1)S(1)}, bf16[2,384,1024]{2,1,0:T(8,128)(2,1)}, u32[]{:S(2)}) copy-start(bf16[2,384,1024]{2,1,0:T(8,128)(2,1)} %k_ref.1) | copy-start | bytes 4718596
  28.0 35.0 %copy-start.5 = (bf16[2,384,1024]{2,1,0:T(8,128)(2,1)S(1)}, bf16[2,384,1024]{2,1,0:T(8,128)(2,1)}, u32[]{:S(2)}) copy-start(bf16[2,384,1024]{2,1,0:T(8,128)(2,1)} %v_ref.1) | copy-start | bytes 4718596
  28.0 35.0 %copy-start.16 = (s32[32]{0:T(128)S(1)}, s32[32]{0:T(128)}, u32[]{:S(2)}) copy-start(s32[32]{0:T(128)} %len_ref.1) | copy-start | bytes 388
  46.6 27.9 %slice-start = ((s8[8388608]{0:T(1024)(128)(4,1)}), s8[4194304]{0:T(1024)(128)(4,1)S(1)}, s32[]{:S(2)}) async-start(s8[8388608]{0:T(1024)(128)(4,1)} %bitcast.15), calls=%async_computation.2 | async-start | bytes 8388608
  46.6 27.9 %slice-start.1 = ((s8[8388608]{0:T(1024)(128)(4,1)}), s8[4194304]{0:T(1024)(128)(4,1)S(1)}, s32[]{:S(2)}) async-start(s8[8388608]{0:T(1024)(128)(4,1)} %bitcast.15), calls=%async_computation.3 | async-start | bytes 8388608
  74.5 18.1 %copy-start.9 = (bf16[2,8192]{1,0:T(2,128)(2,1)S(1)}, bf16[2,8192]{1,0:T(2,128)(2,1)}, u32[]{:S(2)}) copy-start(bf16[2,8192]{1,0:T(2,128)(2,1)} %first_ref.1) | copy-start | bytes 98308
  74.5 18.1 %copy-start.11 = (bf16[2,8192]{1,0:T(2,128)(2,1)S(1)}, bf16[2,8192]{1,0:T(2,128)(2,1)}, u32[]{:S(2)}) copy-start(bf16[2,8192]{1,0:T(2,128)(2,1)} %second_ref.1) | copy-start | bytes 98308
  76.2 2.2 %collective-permute-start.3 = (f32[32,5120]{1,0:T(8,128)S(1)}, f32[32,5120]{1,0:T(8,128)S(1)}, u32[]{:S(2)}, u32[]{:S(2)}) collective-permute-start(f32[32,5120]{1,0:T(8,128)S(1)} %get-tuple-element.66), channel_id=1, source_target_pairs={{0,1},{1,0},{2,3},{3,2},{4,5},{5,4},{6,7},{7,6},{8,9},{9,8},{10,11... | collective-permute-start | bytes 1966088 | tf_op jit(solution)/shard_map/ppermute | solution.py:426
  77.2 1.9 %collective-permute-start.8 = (f32[32,3072]{1,0:T(8,128)S(1)}, f32[32,3072]{1,0:T(8,128)S(1)}, u32[]{:S(2)}, u32[]{:S(2)}) collective-permute-start(f32[32,3072]{1,0:T(8,128)S(1)} %get-tuple-element.75), channel_id=1, source_target_pairs={{0,1},{1,0},{2,3},{3,2},{4,5},{5,4},{6,7},{7,6},{8,9},{9,8},{10,11... | collective-permute-start | bytes 1179656 | tf_op jit(solution)/shard_map/ppermute | solution.py:426
  78.4 6.3 %collective-permute-start.4 = (bf16[16,5120]{1,0:T(8,128)(2,1)S(1)}, bf16[16,5120]{1,0:T(8,128)(2,1)S(1)}, u32[]{:S(2)}, u32[]{:S(2)}) collective-permute-start(bf16[16,5120]{1,0:T(8,128)(2,1)S(1)} %get-tuple-element.68), channel_id=1, source_target_pairs={{0,2},{1,3},{2,0},{3,1},{4,6},{5,7},{6,4},{7,5},{8,10},{9,11},{10,... | collective-permute-start | bytes 491528 | tf_op jit(solution)/shard_map/ppermute | solution.py:426
  79.2 6.8 %collective-permute-start.9 = (bf16[8,3072]{1,0:T(8,128)(2,1)S(1)}, bf16[8,3072]{1,0:T(8,128)(2,1)S(1)}, u32[]{:S(2)}, u32[]{:S(2)}) collective-permute-start(bf16[8,3072]{1,0:T(8,128)(2,1)S(1)} %get-tuple-element.77), channel_id=1, source_target_pairs={{0,4},{1,5},{2,6},{3,7},{4,8},{5,9},{6,10},{7,11},{8,12},{9,13},{1... | collective-permute-start | bytes 147464 | tf_op jit(solution)/shard_map/ppermute | solution.py:426
  79.4 9.3 %collective-permute-start.10 = (bf16[8,3072]{1,0:T(8,128)(2,1)S(1)}, bf16[8,3072]{1,0:T(8,128)(2,1)S(1)}, u32[]{:S(2)}, u32[]{:S(2)}) collective-permute-start(bf16[8,3072]{1,0:T(8,128)(2,1)S(1)} %get-tuple-element.78), channel_id=1, source_target_pairs={{0,8},{1,9},{2,10},{3,11},{4,12},{5,13},{6,14},{7,15},{8,0},{9,1},... | collective-permute-start | bytes 147464 | tf_op jit(solution)/shard_map/ppermute | solution.py:426
  80.3 8.4 %collective-permute-start.11 = (bf16[8,3072]{1,0:T(8,128)(2,1)S(1)}, bf16[8,3072]{1,0:T(8,128)(2,1)S(1)}, u32[]{:S(2)}, u32[]{:S(2)}) collective-permute-start(bf16[8,3072]{1,0:T(8,128)(2,1)S(1)} %get-tuple-element.79), channel_id=1, source_target_pairs={{0,12},{1,13},{2,14},{3,15},{4,0},{5,1},{6,2},{7,3},{8,4},{9,5},{1... | collective-permute-start | bytes 147464 | tf_op jit(solution)/shard_map/ppermute | solution.py:426
  84.8 7.8 %collective-permute-start.5 = (bf16[4,5120]{1,0:T(4,128)(2,1)S(1)}, bf16[4,5120]{1,0:T(4,128)(2,1)S(1)}, u32[]{:S(2)}, u32[]{:S(2)}) collective-permute-start(bf16[4,5120]{1,0:T(4,128)(2,1)S(1)} %get-tuple-element.70), channel_id=1, source_target_pairs={{0,4},{1,5},{2,6},{3,7},{4,8},{5,9},{6,10},{7,11},{8,12},{9,13},{1... | collective-permute-start | bytes 122888 | tf_op jit(solution)/shard_map/ppermute | solution.py:426
  85.0 7.6 %collective-permute-start.6 = (bf16[4,5120]{1,0:T(4,128)(2,1)S(1)}, bf16[4,5120]{1,0:T(4,128)(2,1)S(1)}, u32[]{:S(2)}, u32[]{:S(2)}) collective-permute-start(bf16[4,5120]{1,0:T(4,128)(2,1)S(1)} %get-tuple-element.71), channel_id=1, source_target_pairs={{0,8},{1,9},{2,10},{3,11},{4,12},{5,13},{6,14},{7,15},{8,0},{9,1},... | collective-permute-start | bytes 122888 | tf_op jit(solution)/shard_map/ppermute | solution.py:426
  85.9 6.7 %collective-permute-start.7 = (bf16[4,5120]{1,0:T(4,128)(2,1)S(1)}, bf16[4,5120]{1,0:T(4,128)(2,1)S(1)}, u32[]{:S(2)}, u32[]{:S(2)}) collective-permute-start(bf16[4,5120]{1,0:T(4,128)(2,1)S(1)} %get-tuple-element.72), channel_id=1, source_target_pairs={{0,12},{1,13},{2,14},{3,15},{4,0},{5,1},{6,2},{7,3},{8,4},{9,5},{1... | collective-permute-start | bytes 122888 | tf_op jit(solution)/shard_map/ppermute | solution.py:426
  88.7 3.9 %collective-permute-start.12 = (bf16[4,3072]{1,0:T(4,128)(2,1)S(1)}, bf16[4,3072]{1,0:T(4,128)(2,1)S(1)}, u32[]{:S(2)}, u32[]{:S(2)}) collective-permute-start(bf16[4,3072]{1,0:T(4,128)(2,1)S(1)} %get-tuple-element.81), channel_id=1, source_target_pairs={{0,2},{1,3},{2,0},{3,1},{4,6},{5,7},{6,4},{7,5},{8,10},{9,11},{10,... | collective-permute-start | bytes 73736 | tf_op jit(solution)/shard_map/ppermute | solution.py:426
  (2 other events, 1.5 us)

commit v7 on v6

--- a/solution.py
+++ b/solution.py
@@ -78,9 +78,13 @@
         out_ref[:, at] = (values * factor * gain[i : i + 1]).astype(BF16)
 
 
+def frequency_body(out_ref):
+    out_ref[...] = scaled_frequency(lax.broadcasted_iota(jnp.int32, out_ref.shape, 1) // 2)
+
+
 def prep_body(
     sizes, rank, own, key_cols, adapters,
-    index_ref, length_hbm, adapter_hbm, slot_hbm,
+    index_ref, length_hbm, adapter_hbm, slot_hbm, frequency_ref,
     held_ref, local_ref, cos_ref, sin_ref, kcos_ref, ksin_ref, place_ref, unplace_ref, send_ref,
     order_ref, take_ref, length_ref, adapter_ref, slot_ref, sems,
 ):
@@ -98,7 +102,7 @@
 
     def device_of(block, sign):
         c, m, f = block // (far * near), block // far % near, block % far
-        f = f if sign < 0 else (far_at + f) % far
+        f = (far_at + sign * f + far) % far
         m = (near_at + sign * m + near) % near
         c = (core_at + sign * c + cores) % cores
         return (f * near + m) * cores + c
@@ -125,7 +129,7 @@
     position = (length + step).astype(F32)
     lane = iota((1, HEAD), 1)
     odd = jnp.where(lane % 2 == 0, -1.0, 1.0)
-    angle = position * scaled_frequency(lane // 2)
+    angle = position * frequency_ref[...]
     cos_ref[...] = jnp.cos(angle)
     sin_ref[...] = jnp.sin(angle) * odd
     angle = position * scaled_frequency((index * key_cols + lane) % HEAD // 2)
@@ -157,7 +161,8 @@
     row = iota((take_ref.shape[0], 1), 0)
     h = row // all_rows
     block, step, mine = split(row % all_rows)
-    wanted = device_of(block, 1) * rows * heads + (mine * heads + h) * STEPS + step
+    device, c = device_of(block, 1), (cores - block // (far * near)) % cores
+    wanted = (device // cores * cores + c) * rows * heads + (mine * heads + h) * STEPS + step
     hot(take_ref, wanted, iota((1, take_ref.shape[1]), 1))
 
 
@@ -189,25 +194,35 @@
     out_ref[...] = packed.astype(BF16)
 
 
-def join_body(came_ref, out_ref):
-    out_ref[...] = jnp.sum(came_ref[...].astype(F32), axis=0).astype(BF16)
-
-
-def base_body(depth, x_ref, q_ref, k_ref, v_ref, oq_ref, okv_ref):
-    oq_ref[...] = jnp.zeros_like(oq_ref)
-    okv_ref[...] = jnp.zeros_like(okv_ref)
-    columns = k_ref.shape[0]
-    narrow = jnp.zeros((HEAD - 2 * columns, depth), BF16)
+def join_body(*refs):
+    total = refs[0][...].astype(F32)
+    for ref in refs[1:-1]:
+        total = total + ref[...].astype(F32)
+    refs[-1][...] = total.astype(BF16)
+
+
+def half_body(depth, start, x_ref, q_ref, out_ref):
+    out_ref[...] = jnp.zeros_like(out_ref)
+    columns = slice(start, start + out_ref.shape[1])
 
     @pl.loop(0, x_ref.shape[1] // depth)
     def _(i):
         at = pl.ds(pl.multiple_of(i * depth, depth), depth)
-        x = x_ref[:, at]
-        oq_ref[...] += dot(x, q_ref[at, :])
+        out_ref[...] += dot(x_ref[:, at], q_ref[at, columns])
+
+
+def narrow_body(depth, x_ref, k_ref, v_ref, out_ref):
+    out_ref[...] = jnp.zeros_like(out_ref)
+    columns = k_ref.shape[0]
+    narrow = jnp.zeros((HEAD - 2 * columns, depth), BF16)
+
+    @pl.loop(0, x_ref.shape[1] // depth)
+    def _(i):
+        at = pl.ds(pl.multiple_of(i * depth, depth), depth)
         both = (k_ref[:, at], v_ref[:, at])
         if 2 * columns < HEAD:
             both += (narrow,)
-        okv_ref[...] += dot_nt(x, jnp.concatenate(both, axis=0))
+        out_ref[...] += dot_nt(x_ref[:, at], jnp.concatenate(both, axis=0))
 
 
 def turned(values, cosine, sine):
@@ -219,10 +234,16 @@
 
 
 def ready_body(
-    rank, oq_ref, okv_ref, low_ref, unplace_ref, slot_ref, uq_ref, uv_ref, cos_ref, sin_ref,
-    kcos_ref, ksin_ref, send_ref, out_ref,
+    rank, lows, bases, *refs
 ):
-    packed = jnp.sum(low_ref[...].astype(F32), axis=0)
+    low_refs, base_refs = refs[:lows], refs[lows : lows + bases]
+    (
+        okv_ref, unplace_ref, slot_ref, uq_ref, uv_ref, cos_ref, sin_ref, kcos_ref, ksin_ref,
+        send_ref, out_ref,
+    ) = refs[lows + bases :]
+    packed = low_refs[0][...].astype(F32)
+    for ref in low_refs[1:]:
+        packed = packed + ref[...].astype(F32)
     pack = HEAD // (2 * rank)
     low = jnp.concatenate(
         [packed[:, i * 2 * rank : (i + 1) * 2 * rank] for i in range(pack)], axis=0
@@ -237,7 +258,7 @@
     spread_v = jnp.where(column % rank + rank == row, 1.0, 0.0).astype(BF16)
     wide_q = jnp.where(here, dot(low, spread_q), 0.0).astype(BF16)
     wide_v = jnp.where(here, dot(low, spread_v), 0.0).astype(BF16)
-    query = oq_ref[...] + dot(wide_q, uq_ref[...])
+    query = jnp.concatenate([ref[...] for ref in base_refs], axis=1) + dot(wide_q, uq_ref[...])
     fresh = turned(okv_ref[...], kcos_ref[...], ksin_ref[...])
     columns = uv_ref.shape[1]
     value = dot(wide_v, uv_ref[...])
@@ -255,8 +276,9 @@
 
 
 def attend_body(
-    own, columns, index_ref, len_ref, x_ref, order_ref, k_ref, v_ref, nk_ref, nv_ref, ctx_ref, s_ref
+    own, columns, index_ref, len_ref, x_ref, order_ref, k_ref, v_ref, nk_ref, nv_ref, *refs
 ):
+    ctx_refs, s_ref = refs[:-1], refs[-1]
     n, span = x_ref.shape[0], k_ref.shape[1]
     group = HEADS // KV_HEADS
     local = HEADS // n
@@ -314,9 +336,19 @@
             )
     step = local * STEPS
     half = KV_HEADS * mine
-    for i in range(n):
-        block = [s_ref[b * half + i * step : b * half + (i + 1) * step] for b in range(own)]
-        ctx_ref[i] = jnp.concatenate(block, axis=0).astype(BF16)
+    cores = len(ctx_refs)
+    for c, ref in enumerate(ctx_refs):
+        core = (index_ref[0] + c) % cores
+        for i in range(n // cores):
+            at = pl.multiple_of((i * cores + core) * step, step)
+            block = [s_ref[pl.ds(b * half + at, step)] for b in range(own)]
+            ref[i] = jnp.concatenate(block, axis=0).astype(BF16)
+
+
+def pack_body(*refs):
+    rows = refs[0].shape[1]
+    for c, ref in enumerate(refs[:-1]):
+        refs[-1][:, c * rows : (c + 1) * rows] = ref[...]
 
 
 def take_body(ctx_ref, take_ref, w_ref, a_ref, mine_ref, other_ref):
@@ -425,17 +457,9 @@
     def shift(value, f, m, c):
         return lax.ppermute(value, "serve", partner(f, m, c))
 
-    plane = near * cores
-
-    def along_far(value):
-        groups = [[f * plane + p for f in range(far)] for p in range(plane)]
-        return lax.all_gather(value, "serve", axis_index_groups=groups)
-
-    def along_plane(value):
-        groups = [[f * plane + p for p in range(plane)] for f in range(far)]
-        return lax.all_gather(value, "serve", axis_index_groups=groups)
-
+    frequency = whole_call(frequency_body, jax.ShapeDtypeStruct((1, HEAD), F32), (), cost=1.0)
     gain = attention_norm_gain.reshape(width // HEAD, HEAD)
+    gain, frequency = lax.optimization_barrier((gain, frequency))
     normed = whole_call(
         norm_body,
         jax.ShapeDtypeStruct((rows, width), BF16),
@@ -449,7 +473,8 @@
         ],
         cost=1.0,
     )
-    groups = [along_far(normed)]
+    normed = normed[None]
+    groups = [jnp.concatenate([normed] + [shift(normed, f, 0, 0) for f in range(1, far)])]
     groups += [shift(groups[0], 0, m, 0) for m in range(1, near)]
 
     groups[0], at = lax.optimization_barrier((groups[0], index[None]))
@@ -472,7 +497,7 @@
             jax.ShapeDtypeStruct((own * HEADS * STEPS, n * sent), BF16),
             jax.ShapeDtypeStruct((all_rows * local, n * rows * local), BF16),
         ),
-        (at, lengths, request_adapter, adapter_slot),
+        (at, lengths, request_adapter, adapter_slot, frequency),
         smem=1,
         hbm=3,
         scratch=[
@@ -499,27 +524,41 @@
         (*groups, query_down, value_down, near_slot, place),
         cost=0.3,
     )
-    lows = along_plane(low)
-    low = whole_call(join_body, jax.ShapeDtypeStruct(low.shape, BF16), (lows,), cost=0.1)
-    lows = along_far(low)
-
-    base_q, base_kv = whole_call(
-        functools.partial(base_body, 2048),
-        (
-            jax.ShapeDtypeStruct((all_rows, query_cols), F32),
-            jax.ShapeDtypeStruct((all_rows, HEAD), F32),
-        ),
-        (x, query_matrix, key_matrix.T, value_matrix.T),
-        cost=0.6,
+    half_cols = query_cols // 2 if query_cols % 256 == 0 else query_cols
+    lows = [shift(low, 0, m, c) for m in range(near) for c in range(cores) if m + c]
+    base_first = whole_call(
+        functools.partial(half_body, 2048, 0),
+        jax.ShapeDtypeStruct((all_rows, half_cols), F32),
+        (x, query_matrix),
+        cost=0.3,
+    )
+    low = whole_call(join_body, jax.ShapeDtypeStruct(low.shape, BF16), (low, *lows), cost=0.1)
+    low, base_first = lax.optimization_barrier((low, base_first))
+    lows = [low] + [shift(low, f, 0, 0) for f in range(1, far)]
+    bases = [base_first]
+    if half_cols < query_cols:
+        bases.append(
+            whole_call(
+                functools.partial(half_body, 2048, half_cols),
+                jax.ShapeDtypeStruct((all_rows, query_cols - half_cols), F32),
+                (x, query_matrix),
+                cost=0.3,
+            )
+        )
+    base_kv = whole_call(
+        functools.partial(narrow_body, 2048),
+        jax.ShapeDtypeStruct((all_rows, HEAD), F32),
+        (x, key_matrix.T, value_matrix.T),
+        cost=0.1,
     )
 
     ready = whole_call(
-        functools.partial(ready_body, rank),
+        functools.partial(ready_body, rank, len(lows), len(bases)),
         jax.ShapeDtypeStruct((n, sent, HEAD), BF16),
         (
-            base_q,
+            *lows,
+            *bases,
             base_kv,
-            lows,
             unplace,
             slot,
             query_up_weights.reshape(stored * rank, query_cols),
@@ -535,15 +574,26 @@
     arrived = lax.all_to_all(ready, "serve", split_axis=0, concat_axis=0, tiled=True)
 
     fresh = jax.ShapeDtypeStruct((own, STEPS, KV_HEADS * HEAD), BF16)
-    new_keys, new_values, context = whole_call(
+    new_keys, new_values, *context = whole_call(
         functools.partial(attend_body, own, key_cols),
-        (fresh, fresh, jax.ShapeDtypeStruct((n, rows * local, HEAD), BF16)),
+        (fresh, fresh)
+        + (jax.ShapeDtypeStruct((n // cores, rows * local, HEAD), BF16),) * cores,
         (index[None], lengths, arrived, order, rotated_key_cache, stored_value_cache),
         smem=2,
         scratch=[pltpu.VMEM((own * HEADS * STEPS, HEAD), F32)],
         cost=1.0,
     )
-    context = lax.all_to_all(context, "serve", split_axis=0, concat_axis=0, tiled=True)
+    context = context[:1] + [shift(context[c], 0, 0, c) for c in range(1, cores)]
+    context = whole_call(
+        pack_body,
+        jax.ShapeDtypeStruct((n // cores, cores * rows * local, HEAD), BF16),
+        tuple(context),
+        cost=0.1,
+    )
+    same_core = [[i * cores + c for i in range(n // cores)] for c in range(cores)]
+    context = lax.all_to_all(
+        context, "serve", split_axis=0, concat_axis=0, axis_index_groups=same_core, tiled=True
+    )
 
     half = all_rows // cores
     cut = width * 5 // 8
@@ -581,6 +631,13 @@
         cost=0.1,
     )
     sides = [shift(side, f, 0, 0) for f, side in enumerate(sides, 1)]
+    short, *sides = whole_call(
+        functools.partial(far_body, len(sides)),
+        (kind(1, width - cut, F32),) + (kind(1, width - cut, BF16),) * (near - 1),
+        (short, *sides),
+        cost=0.1,
+    )
+    keep, short = lax.optimization_barrier((keep, short))
     keep, *others = whole_call(
         functools.partial(far_body, len(others)),
         (kind(1, cut, F32),) + (kind(1, cut, BF16),) * (far - 1),
@@ -588,12 +645,6 @@
         cost=0.1,
     )
     others = [shift(other, f, 0, 0) for f, other in enumerate(others, 1)]
-    short, *sides = whole_call(
-        functools.partial(far_body, len(sides)),
-        (kind(1, width - cut, F32),) + (kind(1, width - cut, BF16),) * (near - 1),
-        (short, *sides),
-        cost=0.1,
-    )
     sides = [shift(side, 0, m, 0) for m, side in enumerate(sides, 1)]
     result = jax.ShapeDtypeStruct((own, width), BF16)
     out_one, out_two = whole_call(

time: 93.8 us -> 82.5 us (0.88)
  blocking collectives: 56.5 us -> 19.5 us
  waiting for transfers between devices: 7.32 us -> 23.2 us
  starting transfers between devices: 11.1 us -> 22.8 us
  local copies, waits for them, and re-layouts: 5.64 us -> 2.32 us
  Pallas kernels: 11.9 us -> 13.1 us
    all_gather x3 -> x0, blocking collectives: 34.1 us -> none  [the longest x2 28.8 us: along_far(): return lax.all_gather(value, 'serve', axis_index_groups=groups)]
    ppermute x13 -> x23, waiting for transfers between devices: 7.32 us -> 23.2 us  [shift(): return lax.ppermute(value, 'serve', partner(f, m, c))]
    ppermute x13 -> x23, starting transfers between devices: 11.1 us -> 22.8 us  [shift(): return lax.ppermute(value, 'serve', partner(f, m, c))]
    unnamed x42 -> x40, local copies, waits for them, and re-layouts: 5.64 us -> 2.32 us
    all_to_all x1, blocking collectives: 12.9 us -> 10.2 us  [shards(): lax.all_to_all(ready, 'serve', split_axis=0, concat_axis=0, tiled=True)]
    pallas_call x14 -> x18, Pallas kernels: 11.9 us -> 13.1 us  [whole_call(): pl.pallas_call(body, out_shape=out_shape, in_specs=specs, out_specs=tuple...]
  transfers between devices with their start and end apart: 13 -> 23, of which waited for: 5 -> 13; matrix products, arithmetic and copies ran while one was open for 0% -> 0% of each run, Pallas kernels for 3% -> 8%
where the time goes in v7:
time: 82.5 us; the launch traced here: 82.1 us
  waiting for transfers between devices  23.2 us (28%)
  starting transfers between devices  22.8 us (28%)
  blocking collectives  19.5 us (24%)
  Pallas kernels  13.1 us (16%)
  local copies, waits for them, and re-layouts  2.32 us (3%)
  between operations  0.94 us (1%)
    ppermute x23, waiting for transfers between devices, shift(): return lax.ppermute(value, 'serve', partner(f, m, c))  23.2 us
    ppermute x23, starting transfers between devices, shift(): return lax.ppermute(value, 'serve', partner(f, m, c))  22.8 us
    pallas_call x18, Pallas kernels, whole_call(): pl.pallas_call(body, out_shape=out_shape, in_specs=specs, out_specs=tuple...  13.1 us
    all_to_all x1, blocking collectives, shards(): lax.all_to_all(ready, 'serve', split_axis=0, concat_axis=0, tiled=True)  10.2 us
    all_to_all x1, blocking collectives, shards(): lax.all_to_all(context, 'serve', split_axis=0, concat_axis=0, axis_index_...  9.27 us
    unnamed x40, local copies, waits for them, and re-layouts  2.32 us
  transfers between devices with their start and end apart: 23, of which 13 were waited for; matrix products, arithmetic and copies ran while one was open for 0% of the time, Pallas kernels for 8%

profile of v7, /device:TPU:0, one launch (start us, length us, event | category | flops | bytes accessed | tf_op | source)
XLA Modules:
  0.0 82.1 jit_solution(15134208916717733957)
XLA Ops:
  0.7 0.8 copy-done.8
  1.5 0.8 copy-done.10
  3.3 5.1 %collective-permute-start.2 = (bf16[1,4,8192]{2,1,0:T(4,128)(2,1)S(1)}, bf16[1,4,8192]{2,1,0:T(4,128)(2,1)S(1)}, u32[]{:S(2)}, u32[]{:S(2)}) collective-permute-start(bf16[1,4,8192]{2,1,0:T(4,128)(2,1)S(1)} %bitcast.21), channel_id=1, source_target_pairs={{0,12},{1,13},{2,14},{3,15},{4,0},{5,1},{6,2},{7,3},{8,4},{9,5},{1... | collective-permute-start | bytes 196616 | tf_op jit(solution)/shard_map/ppermute | solution.py:458
  8.4 1.0 %collective-permute-start = (bf16[1,4,8192]{2,1,0:T(4,128)(2,1)S(1)}, bf16[1,4,8192]{2,1,0:T(4,128)(2,1)S(1)}, u32[]{:S(2)}, u32[]{:S(2)}) collective-permute-start(bf16[1,4,8192]{2,1,0:T(4,128)(2,1)S(1)} %bitcast.23), channel_id=1, source_target_pairs={{0,4},{1,5},{2,6},{3,7},{4,8},{5,9},{6,10},{7,11},{8,12},{9,13},{1... | collective-permute-start | bytes 196616 | tf_op jit(solution)/shard_map/ppermute | solution.py:458
  9.4 1.5 %collective-permute-done.2 = bf16[1,4,8192]{2,1,0:T(4,128)(2,1)S(1)} collective-permute-done((bf16[1,4,8192]{2,1,0:T(4,128)(2,1)S(1)}, bf16[1,4,8192]{2,1,0:T(4,128)(2,1)S(1)}, u32[]{:S(2)}, u32[]{:S(2)}) %collective-permute-start.2) | collective-permute-done | bytes 65568 | tf_op jit(solution)/shard_map/ppermute | solution.py:458
  10.9 4.0 %collective-permute-done.1 = bf16[1,4,8192]{2,1,0:T(4,128)(2,1)S(1)} collective-permute-done((bf16[1,4,8192]{2,1,0:T(4,128)(2,1)S(1)}, bf16[1,4,8192]{2,1,0:T(4,128)(2,1)S(1)}, u32[]{:S(2)}, u32[]{:S(2)}) %collective-permute-start.1) | collective-permute-done | bytes 65568 | tf_op jit(solution)/shard_map/ppermute | solution.py:458
  15.1 1.6 %collective-permute-start.3 = (bf16[4,4,8192]{2,1,0:T(4,128)(2,1)S(1)}, bf16[4,4,8192]{2,1,0:T(4,128)(2,1)S(1)}, u32[]{:S(2)}, u32[]{:S(2)}) collective-permute-start(bf16[4,4,8192]{2,1,0:T(4,128)(2,1)S(1)} %pad_maximum_fusion.refs_0_), channel_id=1, source_target_pairs={{0,2},{1,3},{2,0},{3,1},{4,6},{5,7},{6,4},{7,5},{8,10},{9,11},{10,... | collective-permute-start | bytes 786440 | tf_op jit(solution)/shard_map/ppermute | solution.py:458
  16.9 1.9 %shard_map.185 = (s32[64,1]{1,0:T(8,128)S(1)}, s32[64,1]{1,0:T(8,128)S(1)}, f32[64,128]{1,0:T(8,128)S(1)}, f32[64,128]{1,0:T(8,128)S(1)}, f32[64,128]{1,0:T(8,12...) custom-call(s32[1]{0:T(128)} %bitcast.index_ref, ...), custom_call_target="tpu_custom_call" | custom-call | flops 4600000000 | tf_op jit(solution)/shard_map/pallas_call | solution.py:36
  18.8 4.5 %collective-permute-done.3.refs_1_ = bf16[4,4,8192]{2,1,0:T(4,128)(2,1)S(1)} collective-permute-done((bf16[4,4,8192]{2,1,0:T(4,128)(2,1)S(1)}, bf16[4,4,8192]{2,1,0:T(4,128)(2,1)S(1)}, u32[]{:S(2)}, u32[]{:S(2)}) %collective-permute-start.3) | collective-permute-done | bytes 262176 | tf_op jit(solution)/shard_map/ppermute | solution.py:458
  23.3 1.5 %collective-permute-done.5.refs_3_ = bf16[4,4,8192]{2,1,0:T(4,128)(2,1)S(1)} collective-permute-done((bf16[4,4,8192]{2,1,0:T(4,128)(2,1)S(1)}, bf16[4,4,8192]{2,1,0:T(4,128)(2,1)S(1)}, u32[]{:S(2)}, u32[]{:S(2)}) %collective-permute-start.5) | collective-permute-done | bytes 262176 | tf_op jit(solution)/shard_map/ppermute | solution.py:458
  25.5 1.3 %collective-permute-start.8 = (bf16[16,128]{1,0:T(8,128)(2,1)S(1)}, bf16[16,128]{1,0:T(8,128)(2,1)S(1)}, u32[]{:S(2)}, u32[]{:S(2)}) collective-permute-start(bf16[16,128]{1,0:T(8,128)(2,1)S(1)} %get-tuple-element.58.refs_0_), channel_id=1, source_target_pairs={{0,3},{1,2},{2,1},{3,0},{4,7},{5,6},{6,5},{7,4},{8,11},{9,10},{10,... | collective-permute-start | bytes 12296 | tf_op jit(solution)/shard_map/ppermute | solution.py:458
  27.4 1.3 %shard_map.189.refs_5_ = f32[64,256]{1,0:T(8,128)S(1)} custom-call(bf16[64,8192]{1,0:T(8,128)(2,1)S(1)} %get-tuple-element.59.x_ref, bf16[8192,512]{1,0:T(8,128)(2,1)S(1)} %bitcast.14), custom_call_target="tpu_custom_call" | custom-call | flops 345000000 | tf_op jit(solution)/shard_map/pallas_call | solution.py:36
  28.7 1.2 %shard_map.188.refs_4_ = f32[64,256]{1,0:T(8,128)S(1)} custom-call(bf16[64,8192]{1,0:T(8,128)(2,1)S(1)} %get-tuple-element.59.x_ref, bf16[8192,512]{1,0:T(8,128)(2,1)S(1)} %bitcast.14), custom_call_target="tpu_custom_call" | custom-call | flops 345000000 | tf_op jit(solution)/shard_map/pallas_call | solution.py:36
  30.7 1.3 %collective-permute-start.10 = (bf16[16,128]{1,0:T(8,128)(2,1)S(1)}, bf16[16,128]{1,0:T(8,128)(2,1)S(1)}, u32[]{:S(2)}, u32[]{:S(2)}) collective-permute-start(bf16[16,128]{1,0:T(8,128)(2,1)S(1)} %shard_map.187.refs_0_), channel_id=1, source_target_pairs={{0,8},{1,9},{2,10},{3,11},{4,12},{5,13},{6,14},{7,15},{8,0},{9,1},... | collective-permute-start | bytes 12296 | tf_op jit(solution)/shard_map/ppermute | solution.py:458
  32.0 1.9 %collective-permute-start.9 = (bf16[16,128]{1,0:T(8,128)(2,1)S(1)}, bf16[16,128]{1,0:T(8,128)(2,1)S(1)}, u32[]{:S(2)}, u32[]{:S(2)}) collective-permute-start(bf16[16,128]{1,0:T(8,128)(2,1)S(1)} %shard_map.187.refs_0_), channel_id=1, source_target_pairs={{0,4},{1,5},{2,6},{3,7},{4,8},{5,9},{6,10},{7,11},{8,12},{9,13},{1... | collective-permute-start | bytes 12296 | tf_op jit(solution)/shard_map/ppermute | solution.py:458
  33.9 1.2 %shard_map.190.refs_6_ = f32[64,128]{1,0:T(8,128)S(1)} custom-call(bf16[64,8192]{1,0:T(8,128)(2,1)S(1)} %get-tuple-element.59.x_ref, bf16[64,8192]{1,0:T(8,128)(2,1)S(1)} %bitcast.17, bf16[64,8192]{1,0:T(8,128)(2,1)S(1)} %bitcast.18), custom_call_target="tpu_custom_call" | custom-call | flops 115000000 | tf_op jit(solution)/shard_map/pallas_call | solution.py:36
  35.2 2.2 %collective-permute-done.9.refs_1_ = bf16[16,128]{1,0:T(8,128)(2,1)S(1)} collective-permute-done((bf16[16,128]{1,0:T(8,128)(2,1)S(1)}, bf16[16,128]{1,0:T(8,128)(2,1)S(1)}, u32[]{:S(2)}, u32[]{:S(2)}) %collective-permute-start.9) | collective-permute-done | bytes 4128 | tf_op jit(solution)/shard_map/ppermute | solution.py:458
  37.4 0.8 %shard_map.191 = bf16[16,24,128]{2,1,0:T(8,128)(2,1)S(1)} custom-call(bf16[16,128]{1,0:T(8,128)(2,1)S(1)} %shard_map.187.refs_0_, bf16[16,128]{1,0:T(8,128)(2,1)S(1)} %collective-permute-done.9.refs_1_, bf16[16,128]{1,0:T(8,128)(2,1)S(1)} %collective-permute-done.10.refs_2_, bf16[16,128]{1,0:T(8,128)(2,1)S(1)} %collective-permute-done.11.refs_3_, ...), custom_call_target="tpu_custom_call" | custom-call | flops 1035000000 | tf_op jit(solution)/shard_map/pallas_call | solution.py:36
  38.2 10.2 %all_to_all.10.x_ref = bf16[16,24,128]{2,1,0:T(8,128)(2,1)S(1)} all-to-all(bf16[16,24,128]{2,1,0:T(8,128)(2,1)S(1)} %shard_map.191), channel_id=1, replica_groups=mesh['replica'=2,'serve'=16] {'serve'}, dimensions={0} | all-to-all | bytes 196608 | tf_op jit(solution)/shard_map/all_to_all | solution.py:574
  48.5 2.0 %shard_map.192 = (bf16[2,2,1024]{2,1,0:T(2,128)(2,1)}, bf16[2,2,1024]{2,1,0:T(2,128)(2,1)}, bf16[8,16,128]{2,1,0:T(8,128)(2,1)S(1)}, bf16[8,16,128]{2,1,0:T(8,128)(2,1)S(1)}) custom-call(s32[1]{0:T(128)} %bitcast.index_ref, s32[32]{0:T(128)S(1)} %copy-done.15, bf16[16,24,128]{2,1,0:T(8,128)(2,1)S(1)} %all_to_all.10.x_ref, ...), custom_call_target="tpu_custom_call" | custom-call | flops 1150000000 | tf_op jit(solution)/shard_map/pallas_call | solution.py:36
  50.6 1.2 %collective-permute-done.12.refs_1_ = bf16[8,16,128]{2,1,0:T(8,128)(2,1)S(1)} collective-permute-done((bf16[8,16,128]{2,1,0:T(8,128)(2,1)S(1)}, bf16[8,16,128]{2,1,0:T(8,128)(2,1)S(1)}, u32[]{:S(2)}, u32[]{:S(2)}) %collective-permute-start.12) | collective-permute-done | bytes 32800 | tf_op jit(solution)/shard_map/ppermute | solution.py:458
  51.8 9.3 %all_to_all.11.ctx_ref = bf16[8,32,128]{2,1,0:T(8,128)(2,1)S(1)} all-to-all(bf16[8,32,128]{2,1,0:T(8,128)(2,1)S(1)} %shard_map.193), channel_id=1, replica_groups={{0,2,4,6,8,10,12,14},{1,3,5,7,9,11,13,15},{16,18,20,22,24,26,28,30},{17..., dimensions={0} | all-to-all | bytes 131072 | tf_op jit(solution)/shard_map/all_to_all | solution.py:594
  61.1 1.7 %shard_map.194 = (bf16[64,512]{1,0:T(8,128)(2,1)S(1)}, f32[32,5120]{1,0:T(8,128)S(1)}, f32[32,5120]{1,0:T(8,128)S(1)}) custom-call(bf16[8,32,128]{2,1,0:T(8,128)(2,1)S(1)} %all_to_all.11.ctx_ref, bf16[256,256]{1,0:T(8,128)(2,1)S(1)} %get-tuple-element.72.take_ref, bf16[512,8192]{1,0:T(8,128)(2,1)S(1)} %bitcast.16), custom_call_target="tpu_custom_call" | custom-call | flops 460000000 | tf_op jit(solution)/shard_map/pallas_call | solution.py:36
  62.8 0.9 %shard_map.196 = (f32[32,3072]{1,0:T(8,128)S(1)}, f32[32,3072]{1,0:T(8,128)S(1)}) custom-call(bf16[64,512]{1,0:T(8,128)(2,1)S(1)} %get-tuple-element.76.a_ref, bf16[512,8192]{1,0:T(8,128)(2,1)S(1)} %bitcast.16), custom_call_target="tpu_custom_call" | custom-call | flops 345000000 | tf_op jit(solution)/shard_map/pallas_call | solution.py:36
  67.1 2.5 %collective-permute-start.17 = (bf16[8,3072]{1,0:T(8,128)(2,1)S(1)}, bf16[8,3072]{1,0:T(8,128)(2,1)S(1)}, u32[]{:S(2)}, u32[]{:S(2)}) collective-permute-start(bf16[8,3072]{1,0:T(8,128)(2,1)S(1)} %get-tuple-element.82), channel_id=1, source_target_pairs={{0,12},{1,13},{2,14},{3,15},{4,0},{5,1},{6,2},{7,3},{8,4},{9,5},{1... | collective-permute-start | bytes 147464 | tf_op jit(solution)/shard_map/ppermute | solution.py:458
  69.6 2.6 %collective-permute-done.15.refs_1_ = bf16[8,3072]{1,0:T(8,128)(2,1)S(1)} collective-permute-done((bf16[8,3072]{1,0:T(8,128)(2,1)S(1)}, bf16[8,3072]{1,0:T(8,128)(2,1)S(1)}, u32[]{:S(2)}, u32[]{:S(2)}) %collective-permute-start.15) | collective-permute-done | bytes 49184 | tf_op jit(solution)/shard_map/ppermute | solution.py:458
  72.2 1.4 %collective-permute-done.16.refs_2_ = bf16[8,3072]{1,0:T(8,128)(2,1)S(1)} collective-permute-done((bf16[8,3072]{1,0:T(8,128)(2,1)S(1)}, bf16[8,3072]{1,0:T(8,128)(2,1)S(1)}, u32[]{:S(2)}, u32[]{:S(2)}) %collective-permute-start.16) | collective-permute-done | bytes 49184 | tf_op jit(solution)/shard_map/ppermute | solution.py:458
  73.7 1.2 %collective-permute-start.19 = (bf16[4,5120]{1,0:T(4,128)(2,1)S(1)}, bf16[4,5120]{1,0:T(4,128)(2,1)S(1)}, u32[]{:S(2)}, u32[]{:S(2)}) collective-permute-start(bf16[4,5120]{1,0:T(4,128)(2,1)S(1)} %get-tuple-element.87), channel_id=1, source_target_pairs={{0,4},{1,5},{2,6},{3,7},{4,8},{5,9},{6,10},{7,11},{8,12},{9,13},{1... | collective-permute-start | bytes 122888 | tf_op jit(solution)/shard_map/ppermute | solution.py:458
  74.9 1.4 %collective-permute-start.20 = (bf16[4,5120]{1,0:T(4,128)(2,1)S(1)}, bf16[4,5120]{1,0:T(4,128)(2,1)S(1)}, u32[]{:S(2)}, u32[]{:S(2)}) collective-permute-start(bf16[4,5120]{1,0:T(4,128)(2,1)S(1)} %get-tuple-element.88), channel_id=1, source_target_pairs={{0,8},{1,9},{2,10},{3,11},{4,12},{5,13},{6,14},{7,15},{8,0},{9,1},... | collective-permute-start | bytes 122888 | tf_op jit(solution)/shard_map/ppermute | solution.py:458
  76.3 1.2 %collective-permute-start.21 = (bf16[4,5120]{1,0:T(4,128)(2,1)S(1)}, bf16[4,5120]{1,0:T(4,128)(2,1)S(1)}, u32[]{:S(2)}, u32[]{:S(2)}) collective-permute-start(bf16[4,5120]{1,0:T(4,128)(2,1)S(1)} %get-tuple-element.89), channel_id=1, source_target_pairs={{0,12},{1,13},{2,14},{3,15},{4,0},{5,1},{6,2},{7,3},{8,4},{9,5},{1... | collective-permute-start | bytes 122888 | tf_op jit(solution)/shard_map/ppermute | solution.py:458
  77.6 0.8 collective-permute-start.22
  78.3 3.1 %collective-permute-done.22.refs_5_ = bf16[4,3072]{1,0:T(4,128)(2,1)S(1)} collective-permute-done((bf16[4,3072]{1,0:T(4,128)(2,1)S(1)}, bf16[4,3072]{1,0:T(4,128)(2,1)S(1)}, u32[]{:S(2)}, u32[]{:S(2)}) %collective-permute-start.22) | collective-permute-done | bytes 24608 | tf_op jit(solution)/shard_map/ppermute | solution.py:458
  (77 shorter events, 7.9 us)
Async XLA Ops:
  0.6 16.2 %copy-start.15 = (s32[32]{0:T(128)S(1)}, s32[32]{0:T(128)}, u32[]{:S(2)}) copy-start(s32[32]{0:T(128)} %len_ref.1) | copy-start | bytes 388
  0.6 16.2 %copy-start.14 = (s32[32]{0:T(128)S(1)}, s32[32]{0:T(128)}, u32[]{:S(2)}) copy-start(s32[32]{0:T(128)} %slot_hbm.1) | copy-start | bytes 388
  0.7 16.2 %copy-start.13 = (s32[32]{0:T(128)S(1)}, s32[32]{0:T(128)}, u32[]{:S(2)}) copy-start(s32[32]{0:T(128)} %adapter_hbm.1) | copy-start | bytes 388
  3.3 7.6 %collective-permute-start.2 = (bf16[1,4,8192]{2,1,0:T(4,128)(2,1)S(1)}, bf16[1,4,8192]{2,1,0:T(4,128)(2,1)S(1)}, u32[]{:S(2)}, u32[]{:S(2)}) collective-permute-start(bf16[1,4,8192]{2,1,0:T(4,128)(2,1)S(1)} %bitcast.21), channel_id=1, source_target_pairs={{0,12},{1,13},{2,14},{3,15},{4,0},{5,1},{6,2},{7,3},{8,4},{9,5},{1... | collective-permute-start | bytes 196616 | tf_op jit(solution)/shard_map/ppermute | solution.py:458
  8.4 6.5 %collective-permute-start.1 = (bf16[1,4,8192]{2,1,0:T(4,128)(2,1)S(1)}, bf16[1,4,8192]{2,1,0:T(4,128)(2,1)S(1)}, u32[]{:S(2)}, u32[]{:S(2)}) collective-permute-start(bf16[1,4,8192]{2,1,0:T(4,128)(2,1)S(1)} %bitcast.22), channel_id=1, source_target_pairs={{0,8},{1,9},{2,10},{3,11},{4,12},{5,13},{6,14},{7,15},{8,0},{9,1},... | collective-permute-start | bytes 196616 | tf_op jit(solution)/shard_map/ppermute | solution.py:458
  8.4 6.5 %collective-permute-start = (bf16[1,4,8192]{2,1,0:T(4,128)(2,1)S(1)}, bf16[1,4,8192]{2,1,0:T(4,128)(2,1)S(1)}, u32[]{:S(2)}, u32[]{:S(2)}) collective-permute-start(bf16[1,4,8192]{2,1,0:T(4,128)(2,1)S(1)} %bitcast.23), channel_id=1, source_target_pairs={{0,4},{1,5},{2,6},{3,7},{4,8},{5,9},{6,10},{7,11},{8,12},{9,13},{1... | collective-permute-start | bytes 196616 | tf_op jit(solution)/shard_map/ppermute | solution.py:458
  15.1 8.1 %collective-permute-start.3 = (bf16[4,4,8192]{2,1,0:T(4,128)(2,1)S(1)}, bf16[4,4,8192]{2,1,0:T(4,128)(2,1)S(1)}, u32[]{:S(2)}, u32[]{:S(2)}) collective-permute-start(bf16[4,4,8192]{2,1,0:T(4,128)(2,1)S(1)} %pad_maximum_fusion.refs_0_), channel_id=1, source_target_pairs={{0,2},{1,3},{2,0},{3,1},{4,6},{5,7},{6,4},{7,5},{8,10},{9,11},{10,... | collective-permute-start | bytes 786440 | tf_op jit(solution)/shard_map/ppermute | solution.py:458
  16.7 6.5 %collective-permute-start.4 = (bf16[4,4,8192]{2,1,0:T(4,128)(2,1)S(1)}, bf16[4,4,8192]{2,1,0:T(4,128)(2,1)S(1)}, u32[]{:S(2)}, u32[]{:S(2)}) collective-permute-start(bf16[4,4,8192]{2,1,0:T(4,128)(2,1)S(1)} %pad_maximum_fusion.refs_0_), channel_id=1, source_target_pairs={{0,1},{1,0},{2,3},{3,2},{4,5},{5,4},{6,7},{7,6},{8,9},{9,8},{10,11... | collective-permute-start | bytes 786440 | tf_op jit(solution)/shard_map/ppermute | solution.py:458
  23.2 1.5 %collective-permute-start.5 = (bf16[4,4,8192]{2,1,0:T(4,128)(2,1)S(1)}, bf16[4,4,8192]{2,1,0:T(4,128)(2,1)S(1)}, u32[]{:S(2)}, u32[]{:S(2)}) collective-permute-start(bf16[4,4,8192]{2,1,0:T(4,128)(2,1)S(1)} %collective-permute-done.3.refs_1_), channel_id=1, source_target_pairs={{0,1},{1,0},{2,3},{3,2},{4,5},{5,4},{6,7},{7,6},{8,9},{9,8},{10,11... | collective-permute-start | bytes 786440 | tf_op jit(solution)/shard_map/ppermute | solution.py:458
  25.5 4.5 %collective-permute-start.8 = (bf16[16,128]{1,0:T(8,128)(2,1)S(1)}, bf16[16,128]{1,0:T(8,128)(2,1)S(1)}, u32[]{:S(2)}, u32[]{:S(2)}) collective-permute-start(bf16[16,128]{1,0:T(8,128)(2,1)S(1)} %get-tuple-element.58.refs_0_), channel_id=1, source_target_pairs={{0,3},{1,2},{2,1},{3,0},{4,7},{5,6},{6,5},{7,4},{8,11},{9,10},{10,... | collective-permute-start | bytes 12296 | tf_op jit(solution)/shard_map/ppermute | solution.py:458
  26.8 3.6 %collective-permute-start.7 = (bf16[16,128]{1,0:T(8,128)(2,1)S(1)}, bf16[16,128]{1,0:T(8,128)(2,1)S(1)}, u32[]{:S(2)}, u32[]{:S(2)}) collective-permute-start(bf16[16,128]{1,0:T(8,128)(2,1)S(1)} %get-tuple-element.58.refs_0_), channel_id=1, source_target_pairs={{0,2},{1,3},{2,0},{3,1},{4,6},{5,7},{6,4},{7,5},{8,10},{9,11},{10,... | collective-permute-start | bytes 12296 | tf_op jit(solution)/shard_map/ppermute | solution.py:458
  27.3 3.1 %collective-permute-start.6 = (bf16[16,128]{1,0:T(8,128)(2,1)S(1)}, bf16[16,128]{1,0:T(8,128)(2,1)S(1)}, u32[]{:S(2)}, u32[]{:S(2)}) collective-permute-start(bf16[16,128]{1,0:T(8,128)(2,1)S(1)} %get-tuple-element.58.refs_0_), channel_id=1, source_target_pairs={{0,1},{1,0},{2,3},{3,2},{4,5},{5,4},{6,7},{7,6},{8,9},{9,8},{10,11... | collective-permute-start | bytes 12296 | tf_op jit(solution)/shard_map/ppermute | solution.py:458
  28.7 19.8 %copy-start.4 = (bf16[2,384,1024]{2,1,0:T(8,128)(2,1)S(1)}, bf16[2,384,1024]{2,1,0:T(8,128)(2,1)}, u32[]{:S(2)}) copy-start(bf16[2,384,1024]{2,1,0:T(8,128)(2,1)} %k_ref.1) | copy-start | bytes 4718596
  28.7 19.8 %copy-start.5 = (bf16[2,384,1024]{2,1,0:T(8,128)(2,1)S(1)}, bf16[2,384,1024]{2,1,0:T(8,128)(2,1)}, u32[]{:S(2)}) copy-start(bf16[2,384,1024]{2,1,0:T(8,128)(2,1)} %v_ref.1) | copy-start | bytes 4718596
  28.7 32.3 %slice-start.2 = ((s8[8388608]{0:T(1024)(128)(4,1)}), s8[4194304]{0:T(1024)(128)(4,1)S(1)}, s32[]{:S(2)}) async-start(s8[8388608]{0:T(1024)(128)(4,1)} %bitcast.15), calls=%async_computation.4 | async-start | bytes 8388608
  30.4 4.7 %collective-permute-start.11 = (bf16[16,128]{1,0:T(8,128)(2,1)S(1)}, bf16[16,128]{1,0:T(8,128)(2,1)S(1)}, u32[]{:S(2)}, u32[]{:S(2)}) collective-permute-start(bf16[16,128]{1,0:T(8,128)(2,1)S(1)} %shard_map.187.refs_0_), channel_id=1, source_target_pairs={{0,12},{1,13},{2,14},{3,15},{4,0},{5,1},{6,2},{7,3},{8,4},{9,5},{1... | collective-permute-start | bytes 12296 | tf_op jit(solution)/shard_map/ppermute | solution.py:458
  30.7 4.5 %collective-permute-start.10 = (bf16[16,128]{1,0:T(8,128)(2,1)S(1)}, bf16[16,128]{1,0:T(8,128)(2,1)S(1)}, u32[]{:S(2)}, u32[]{:S(2)}) collective-permute-start(bf16[16,128]{1,0:T(8,128)(2,1)S(1)} %shard_map.187.refs_0_), channel_id=1, source_target_pairs={{0,8},{1,9},{2,10},{3,11},{4,12},{5,13},{6,14},{7,15},{8,0},{9,1},... | collective-permute-start | bytes 12296 | tf_op jit(solution)/shard_map/ppermute | solution.py:458
  32.0 5.4 %collective-permute-start.9 = (bf16[16,128]{1,0:T(8,128)(2,1)S(1)}, bf16[16,128]{1,0:T(8,128)(2,1)S(1)}, u32[]{:S(2)}, u32[]{:S(2)}) collective-permute-start(bf16[16,128]{1,0:T(8,128)(2,1)S(1)} %shard_map.187.refs_0_), channel_id=1, source_target_pairs={{0,4},{1,5},{2,6},{3,7},{4,8},{5,9},{6,10},{7,11},{8,12},{9,13},{1... | collective-permute-start | bytes 12296 | tf_op jit(solution)/shard_map/ppermute | solution.py:458
  33.9 27.1 %slice-start.3 = ((s8[8388608]{0:T(1024)(128)(4,1)}), s8[4194304]{0:T(1024)(128)(4,1)S(1)}, s32[]{:S(2)}) async-start(s8[8388608]{0:T(1024)(128)(4,1)} %bitcast.15), calls=%async_computation.5 | async-start | bytes 8388608
  50.5 1.3 %collective-permute-start.12 = (bf16[8,16,128]{2,1,0:T(8,128)(2,1)S(1)}, bf16[8,16,128]{2,1,0:T(8,128)(2,1)S(1)}, u32[]{:S(2)}, u32[]{:S(2)}) collective-permute-start(bf16[8,16,128]{2,1,0:T(8,128)(2,1)S(1)} %get-tuple-element.71), channel_id=1, source_target_pairs={{0,1},{1,0},{2,3},{3,2},{4,5},{5,4},{6,7},{7,6},{8,9},{9,8},{10,11... | collective-permute-start | bytes 98312 | tf_op jit(solution)/shard_map/ppermute | solution.py:458
  61.1 20.3 %copy-start.9 = (bf16[2,8192]{1,0:T(2,128)(2,1)S(1)}, bf16[2,8192]{1,0:T(2,128)(2,1)}, u32[]{:S(2)}) copy-start(bf16[2,8192]{1,0:T(2,128)(2,1)} %first_ref.1) | copy-start | bytes 98308
  61.1 20.4 %copy-start.11 = (bf16[2,8192]{1,0:T(2,128)(2,1)S(1)}, bf16[2,8192]{1,0:T(2,128)(2,1)}, u32[]{:S(2)}) copy-start(bf16[2,8192]{1,0:T(2,128)(2,1)} %second_ref.1) | copy-start | bytes 98308
  62.8 2.2 %collective-permute-start.13 = (f32[32,5120]{1,0:T(8,128)S(1)}, f32[32,5120]{1,0:T(8,128)S(1)}, u32[]{:S(2)}, u32[]{:S(2)}) collective-permute-start(f32[32,5120]{1,0:T(8,128)S(1)} %get-tuple-element.74), channel_id=1, source_target_pairs={{0,1},{1,0},{2,3},{3,2},{4,5},{5,4},{6,7},{7,6},{8,9},{9,8},{10,11... | collective-permute-start | bytes 1966088 | tf_op jit(solution)/shard_map/ppermute | solution.py:458
  63.7 1.9 %collective-permute-start.14 = (f32[32,3072]{1,0:T(8,128)S(1)}, f32[32,3072]{1,0:T(8,128)S(1)}, u32[]{:S(2)}, u32[]{:S(2)}) collective-permute-start(f32[32,3072]{1,0:T(8,128)S(1)} %get-tuple-element.78), channel_id=1, source_target_pairs={{0,1},{1,0},{2,3},{3,2},{4,5},{5,4},{6,7},{7,6},{8,9},{9,8},{10,11... | collective-permute-start | bytes 1179656 | tf_op jit(solution)/shard_map/ppermute | solution.py:458
  65.0 8.6 %collective-permute-start.18 = (bf16[16,5120]{1,0:T(8,128)(2,1)S(1)}, bf16[16,5120]{1,0:T(8,128)(2,1)S(1)}, u32[]{:S(2)}, u32[]{:S(2)}) collective-permute-start(bf16[16,5120]{1,0:T(8,128)(2,1)S(1)} %get-tuple-element.85), channel_id=1, source_target_pairs={{0,2},{1,3},{2,0},{3,1},{4,6},{5,7},{6,4},{7,5},{8,10},{9,11},{10,... | collective-permute-start | bytes 491528 | tf_op jit(solution)/shard_map/ppermute | solution.py:458
  65.7 6.5 %collective-permute-start.15 = (bf16[8,3072]{1,0:T(8,128)(2,1)S(1)}, bf16[8,3072]{1,0:T(8,128)(2,1)S(1)}, u32[]{:S(2)}, u32[]{:S(2)}) collective-permute-start(bf16[8,3072]{1,0:T(8,128)(2,1)S(1)} %get-tuple-element.80), channel_id=1, source_target_pairs={{0,4},{1,5},{2,6},{3,7},{4,8},{5,9},{6,10},{7,11},{8,12},{9,13},{1... | collective-permute-start | bytes 147464 | tf_op jit(solution)/shard_map/ppermute | solution.py:458
  66.4 7.2 %collective-permute-start.16 = (bf16[8,3072]{1,0:T(8,128)(2,1)S(1)}, bf16[8,3072]{1,0:T(8,128)(2,1)S(1)}, u32[]{:S(2)}, u32[]{:S(2)}) collective-permute-start(bf16[8,3072]{1,0:T(8,128)(2,1)S(1)} %get-tuple-element.81), channel_id=1, source_target_pairs={{0,8},{1,9},{2,10},{3,11},{4,12},{5,13},{6,14},{7,15},{8,0},{9,1},... | collective-permute-start | bytes 147464 | tf_op jit(solution)/shard_map/ppermute | solution.py:458
  67.1 6.5 %collective-permute-start.17 = (bf16[8,3072]{1,0:T(8,128)(2,1)S(1)}, bf16[8,3072]{1,0:T(8,128)(2,1)S(1)}, u32[]{:S(2)}, u32[]{:S(2)}) collective-permute-start(bf16[8,3072]{1,0:T(8,128)(2,1)S(1)} %get-tuple-element.82), channel_id=1, source_target_pairs={{0,12},{1,13},{2,14},{3,15},{4,0},{5,1},{6,2},{7,3},{8,4},{9,5},{1... | collective-permute-start | bytes 147464 | tf_op jit(solution)/shard_map/ppermute | solution.py:458
  73.7 7.7 %collective-permute-start.19 = (bf16[4,5120]{1,0:T(4,128)(2,1)S(1)}, bf16[4,5120]{1,0:T(4,128)(2,1)S(1)}, u32[]{:S(2)}, u32[]{:S(2)}) collective-permute-start(bf16[4,5120]{1,0:T(4,128)(2,1)S(1)} %get-tuple-element.87), channel_id=1, source_target_pairs={{0,4},{1,5},{2,6},{3,7},{4,8},{5,9},{6,10},{7,11},{8,12},{9,13},{1... | collective-permute-start | bytes 122888 | tf_op jit(solution)/shard_map/ppermute | solution.py:458
  74.9 6.5 %collective-permute-start.20 = (bf16[4,5120]{1,0:T(4,128)(2,1)S(1)}, bf16[4,5120]{1,0:T(4,128)(2,1)S(1)}, u32[]{:S(2)}, u32[]{:S(2)}) collective-permute-start(bf16[4,5120]{1,0:T(4,128)(2,1)S(1)} %get-tuple-element.88), channel_id=1, source_target_pairs={{0,8},{1,9},{2,10},{3,11},{4,12},{5,13},{6,14},{7,15},{8,0},{9,1},... | collective-permute-start | bytes 122888 | tf_op jit(solution)/shard_map/ppermute | solution.py:458
  76.3 5.0 %collective-permute-start.21 = (bf16[4,5120]{1,0:T(4,128)(2,1)S(1)}, bf16[4,5120]{1,0:T(4,128)(2,1)S(1)}, u32[]{:S(2)}, u32[]{:S(2)}) collective-permute-start(bf16[4,5120]{1,0:T(4,128)(2,1)S(1)} %get-tuple-element.89), channel_id=1, source_target_pairs={{0,12},{1,13},{2,14},{3,15},{4,0},{5,1},{6,2},{7,3},{8,4},{9,5},{1... | collective-permute-start | bytes 122888 | tf_op jit(solution)/shard_map/ppermute | solution.py:458
  77.6 3.8 %collective-permute-start.22 = (bf16[4,3072]{1,0:T(4,128)(2,1)S(1)}, bf16[4,3072]{1,0:T(4,128)(2,1)S(1)}, u32[]{:S(2)}, u32[]{:S(2)}) collective-permute-start(bf16[4,3072]{1,0:T(4,128)(2,1)S(1)} %get-tuple-element.91), channel_id=1, source_target_pairs={{0,2},{1,3},{2,0},{3,1},{4,6},{5,7},{6,4},{7,5},{8,10},{9,11},{10,... | collective-permute-start | bytes 73736 | tf_op jit(solution)/shard_map/ppermute | solution.py:458
  (11 other events, 70.2 us)

commit v8 on v6

--- a/solution.py
+++ b/solution.py
@@ -78,9 +78,13 @@
         out_ref[:, at] = (values * factor * gain[i : i + 1]).astype(BF16)
 
 
+def frequency_body(out_ref):
+    out_ref[...] = scaled_frequency(lax.broadcasted_iota(jnp.int32, out_ref.shape, 1) // 2)
+
+
 def prep_body(
     sizes, rank, own, key_cols, adapters,
-    index_ref, length_hbm, adapter_hbm, slot_hbm,
+    index_ref, length_hbm, adapter_hbm, slot_hbm, frequency_ref,
     held_ref, local_ref, cos_ref, sin_ref, kcos_ref, ksin_ref, place_ref, unplace_ref, send_ref,
     order_ref, take_ref, length_ref, adapter_ref, slot_ref, sems,
 ):
@@ -98,7 +102,7 @@
 
     def device_of(block, sign):
         c, m, f = block // (far * near), block // far % near, block % far
-        f = f if sign < 0 else (far_at + f) % far
+        f = (far_at + sign * f + far) % far
         m = (near_at + sign * m + near) % near
         c = (core_at + sign * c + cores) % cores
         return (f * near + m) * cores + c
@@ -125,7 +129,7 @@
     position = (length + step).astype(F32)
     lane = iota((1, HEAD), 1)
     odd = jnp.where(lane % 2 == 0, -1.0, 1.0)
-    angle = position * scaled_frequency(lane // 2)
+    angle = position * frequency_ref[...]
     cos_ref[...] = jnp.cos(angle)
     sin_ref[...] = jnp.sin(angle) * odd
     angle = position * scaled_frequency((index * key_cols + lane) % HEAD // 2)
@@ -165,13 +169,14 @@
     parts, (qd_ref, vd_ref, local_ref, place_ref, x_ref, out_ref) = refs[:groups], refs[groups:]
     rows = parts[0].shape[1]
     sets = max(1, 16 // rows)
-    for p, part in enumerate(parts):
-        for i in range(0, part.shape[0], sets):
-            at = (p * part.shape[0] + i) * rows
-            for lane in range(0, x_ref.shape[1], 1024):
-                lanes = slice(lane, lane + 1024)
-                block = [part[i + j, :, lanes].astype(F32) for j in range(sets)]
-                x_ref[at : at + sets * rows, lanes] = jnp.concatenate(block, axis=0).astype(BF16)
+    blocks = [(part, i) for part in parts for i in range(part.shape[0])]
+    for first in range(0, len(blocks), sets):
+        group = blocks[first : first + sets]
+        for lane in range(0, x_ref.shape[1], 1024):
+            lanes = slice(lane, lane + 1024)
+            block = [part[i, :, lanes].astype(F32) for part, i in group]
+            block = jnp.concatenate(block, axis=0).astype(BF16)
+            x_ref[first * rows : (first + sets) * rows, lanes] = block
     adapters = qd_ref.shape[0] // rank
     maps = jnp.concatenate((qd_ref[...], vd_ref[...]), axis=0)
     low = dot_nt(x_ref[...], maps)
@@ -189,17 +194,20 @@
     out_ref[...] = packed.astype(BF16)
 
 
-def join_body(came_ref, out_ref):
-    out_ref[...] = jnp.sum(came_ref[...].astype(F32), axis=0).astype(BF16)
-
-
-def base_body(depth, x_ref, q_ref, k_ref, v_ref, oq_ref, okv_ref):
+def join_body(*refs):
+    total = refs[0][...].astype(F32)
+    for ref in refs[1:-1]:
+        total = total + ref[...].astype(F32)
+    refs[-1][...] = total.astype(BF16)
+
+
+def base_body(depth, start, stop, x_ref, q_ref, k_ref, v_ref, oq_ref, okv_ref):
     oq_ref[...] = jnp.zeros_like(oq_ref)
     okv_ref[...] = jnp.zeros_like(okv_ref)
     columns = k_ref.shape[0]
     narrow = jnp.zeros((HEAD - 2 * columns, depth), BF16)
 
-    @pl.loop(0, x_ref.shape[1] // depth)
+    @pl.loop(start // depth, stop // depth)
     def _(i):
         at = pl.ds(pl.multiple_of(i * depth, depth), depth)
         x = x_ref[:, at]
@@ -219,10 +227,16 @@
 
 
 def ready_body(
-    rank, oq_ref, okv_ref, low_ref, unplace_ref, slot_ref, uq_ref, uv_ref, cos_ref, sin_ref,
-    kcos_ref, ksin_ref, send_ref, out_ref,
+    rank, lows, *refs
 ):
-    packed = jnp.sum(low_ref[...].astype(F32), axis=0)
+    low_refs = refs[:lows]
+    (
+        oq_ref, okv_ref, oq2_ref, okv2_ref, unplace_ref, slot_ref, uq_ref, uv_ref, cos_ref, sin_ref, kcos_ref, ksin_ref,
+        send_ref, out_ref,
+    ) = refs[lows:]
+    packed = low_refs[0][...].astype(F32)
+    for ref in low_refs[1:]:
+        packed = packed + ref[...].astype(F32)
     pack = HEAD // (2 * rank)
     low = jnp.concatenate(
         [packed[:, i * 2 * rank : (i + 1) * 2 * rank] for i in range(pack)], axis=0
@@ -237,8 +251,8 @@
     spread_v = jnp.where(column % rank + rank == row, 1.0, 0.0).astype(BF16)
     wide_q = jnp.where(here, dot(low, spread_q), 0.0).astype(BF16)
     wide_v = jnp.where(here, dot(low, spread_v), 0.0).astype(BF16)
-    query = oq_ref[...] + dot(wide_q, uq_ref[...])
-    fresh = turned(okv_ref[...], kcos_ref[...], ksin_ref[...])
+    query = oq_ref[...] + oq2_ref[...] + dot(wide_q, uq_ref[...])
+    fresh = turned(okv_ref[...] + okv2_ref[...], kcos_ref[...], ksin_ref[...])
     columns = uv_ref.shape[1]
     value = dot(wide_v, uv_ref[...])
     pieces = [jnp.zeros((value.shape[0], columns), F32), value]
@@ -425,17 +439,9 @@
     def shift(value, f, m, c):
         return lax.ppermute(value, "serve", partner(f, m, c))
 
-    plane = near * cores
-
-    def along_far(value):
-        groups = [[f * plane + p for f in range(far)] for p in range(plane)]
-        return lax.all_gather(value, "serve", axis_index_groups=groups)
-
-    def along_plane(value):
-        groups = [[f * plane + p for p in range(plane)] for f in range(far)]
-        return lax.all_gather(value, "serve", axis_index_groups=groups)
-
+    frequency = whole_call(frequency_body, jax.ShapeDtypeStruct((1, HEAD), F32), (), cost=3.0)
     gain = attention_norm_gain.reshape(width // HEAD, HEAD)
+    gain, frequency = lax.optimization_barrier((gain, frequency))
     normed = whole_call(
         norm_body,
         jax.ShapeDtypeStruct((rows, width), BF16),
@@ -449,10 +455,14 @@
         ],
         cost=1.0,
     )
-    groups = [along_far(normed)]
-    groups += [shift(groups[0], 0, m, 0) for m in range(1, near)]
-
-    groups[0], at = lax.optimization_barrier((groups[0], index[None]))
+    normed = normed[None]
+    fars = [shift(normed, f, 0, 0) for f in range(1, far)]
+    nears = [shift(normed, 0, m, 0) for m in range(1, near)]
+    rest = jnp.concatenate(fars)
+    groups = [jnp.concatenate([normed, *fars, *nears[:1]])]
+    groups += [shift(rest, 0, m, 0) for m in range(1, near)]
+
+    rest, at = lax.optimization_barrier((rest, index[None]))
     sent = -(-(rows * local + rows) // 8) * 8
     narrow = jax.ShapeDtypeStruct((all_rows, 1), jnp.int32)
     table = jax.ShapeDtypeStruct((all_rows, HEAD), F32)
@@ -472,7 +482,7 @@
             jax.ShapeDtypeStruct((own * HEADS * STEPS, n * sent), BF16),
             jax.ShapeDtypeStruct((all_rows * local, n * rows * local), BF16),
         ),
-        (at, lengths, request_adapter, adapter_slot),
+        (at, lengths, request_adapter, adapter_slot, frequency),
         smem=1,
         hbm=3,
         scratch=[
@@ -499,27 +509,30 @@
         (*groups, query_down, value_down, near_slot, place),
         cost=0.3,
     )
-    lows = along_plane(low)
-    low = whole_call(join_body, jax.ShapeDtypeStruct(low.shape, BF16), (lows,), cost=0.1)
-    lows = along_far(low)
-
-    base_q, base_kv = whole_call(
-        functools.partial(base_body, 2048),
-        (
-            jax.ShapeDtypeStruct((all_rows, query_cols), F32),
-            jax.ShapeDtypeStruct((all_rows, HEAD), F32),
-        ),
-        (x, query_matrix, key_matrix.T, value_matrix.T),
-        cost=0.6,
-    )
+    def base(start, stop):
+        return whole_call(
+            functools.partial(base_body, 2048, start, stop),
+            (
+                jax.ShapeDtypeStruct((all_rows, query_cols), F32),
+                jax.ShapeDtypeStruct((all_rows, HEAD), F32),
+            ),
+            (x, query_matrix, key_matrix.T, value_matrix.T),
+            cost=0.3,
+        )
+
+    lows = [shift(low, 0, m, c) for m in range(near) for c in range(cores) if m + c]
+    base_q, base_kv = base(0, width // 2)
+    low = whole_call(join_body, jax.ShapeDtypeStruct(low.shape, BF16), (low, *lows), cost=0.1)
+    low, base_q = lax.optimization_barrier((low, base_q))
+    lows = [low] + [shift(low, f, 0, 0) for f in range(1, far)]
+    bases = (base_q, base_kv, *base(width // 2, width))
 
     ready = whole_call(
-        functools.partial(ready_body, rank),
+        functools.partial(ready_body, rank, len(lows)),
         jax.ShapeDtypeStruct((n, sent, HEAD), BF16),
         (
-            base_q,
-            base_kv,
-            lows,
+            *lows,
+            *bases,
             unplace,
             slot,
             query_up_weights.reshape(stored * rank, query_cols),

time: 93.8 us -> 76.2 us (0.81)
  blocking collectives: 56.5 us -> 19.6 us
  starting transfers between devices: 11.1 us -> 24 us
  waiting for transfers between devices: 7.32 us -> 18.3 us
  local copies, waits for them, and re-layouts: 5.64 us -> 1.02 us
    all_gather x3 -> x0, blocking collectives: 34.1 us -> none  [the longest x2 28.8 us: along_far(): return lax.all_gather(value, 'serve', axis_index_groups=groups)]
    ppermute x13 -> x23, starting transfers between devices: 11.1 us -> 24 us  [shift(): return lax.ppermute(value, 'serve', partner(f, m, c))]
    ppermute x13 -> x23, waiting for transfers between devices: 7.32 us -> 18.3 us  [shift(): return lax.ppermute(value, 'serve', partner(f, m, c))]
    unnamed x42 -> x39, local copies, waits for them, and re-layouts: 5.64 us -> 0.93 us
    all_to_all x1, blocking collectives: 12.9 us -> 10.1 us  [shards(): lax.all_to_all(ready, 'serve', split_axis=0, concat_axis=0, tiled=True)]
    pallas_call x14 -> x16, Pallas kernels: 11.9 us -> 12 us  [whole_call(): pl.pallas_call(body, out_shape=out_shape, in_specs=specs, out_specs=tuple...]
  transfers between devices with their start and end apart: 13 -> 23, of which waited for: 5 -> 10; matrix products, arithmetic and copies ran while one was open for 0% -> 0% of each run, Pallas kernels for 3% -> 7%
where the time goes in v8:
time: 76.2 us; the launch traced here: 75.8 us
  starting transfers between devices  24 us (31%)
  blocking collectives  19.6 us (26%)
  waiting for transfers between devices  18.3 us (24%)
  Pallas kernels  12 us (16%)
  local copies, waits for them, and re-layouts  1.02 us (1%)
  between operations  0.95 us (1%)
    ppermute x23, starting transfers between devices, shift(): return lax.ppermute(value, 'serve', partner(f, m, c))  24 us
    ppermute x23, waiting for transfers between devices, shift(): return lax.ppermute(value, 'serve', partner(f, m, c))  18.3 us
    pallas_call x16, Pallas kernels, whole_call(): pl.pallas_call(body, out_shape=out_shape, in_specs=specs, out_specs=tuple...  12 us
    all_to_all x1, blocking collectives, shards(): lax.all_to_all(ready, 'serve', split_axis=0, concat_axis=0, tiled=True)  10.1 us
    all_to_all x1, blocking collectives, shards(): lax.all_to_all(context, 'serve', split_axis=0, concat_axis=0, tiled=True)  9.48 us
  transfers between devices with their start and end apart: 23, of which 10 were waited for; matrix products, arithmetic and copies ran while one was open for 0% of the time, Pallas kernels for 7%

profile of v8, /device:TPU:0, one launch (start us, length us, event | category | flops | bytes accessed | tf_op | source)
XLA Modules:
  0.0 75.8 jit_solution(12403788027461685181)
XLA Ops:
  0.7 0.6 copy-done.10
  1.8 3.0 %collective-permute-start.3 = (bf16[1,4,8192]{2,1,0:T(4,128)(2,1)S(1)}, bf16[1,4,8192]{2,1,0:T(4,128)(2,1)S(1)}, u32[]{:S(2)}, u32[]{:S(2)}) collective-permute-start(bf16[1,4,8192]{2,1,0:T(4,128)(2,1)S(1)} %bitcast.24), channel_id=1, source_target_pairs={{0,2},{1,3},{2,0},{3,1},{4,6},{5,7},{6,4},{7,5},{8,10},{9,11},{10,... | collective-permute-start | bytes 196616 | tf_op jit(solution)/shard_map/ppermute | solution.py:440
  4.9 3.6 %collective-permute-start.2 = (bf16[1,4,8192]{2,1,0:T(4,128)(2,1)S(1)}, bf16[1,4,8192]{2,1,0:T(4,128)(2,1)S(1)}, u32[]{:S(2)}, u32[]{:S(2)}) collective-permute-start(bf16[1,4,8192]{2,1,0:T(4,128)(2,1)S(1)} %bitcast.25), channel_id=1, source_target_pairs={{0,12},{1,13},{2,14},{3,15},{4,0},{5,1},{6,2},{7,3},{8,4},{9,5},{1... | collective-permute-start | bytes 196616 | tf_op jit(solution)/shard_map/ppermute | solution.py:440
  8.5 1.0 %collective-permute-start = (bf16[1,4,8192]{2,1,0:T(4,128)(2,1)S(1)}, bf16[1,4,8192]{2,1,0:T(4,128)(2,1)S(1)}, u32[]{:S(2)}, u32[]{:S(2)}) collective-permute-start(bf16[1,4,8192]{2,1,0:T(4,128)(2,1)S(1)} %bitcast.27), channel_id=1, source_target_pairs={{0,4},{1,5},{2,6},{3,7},{4,8},{5,9},{6,10},{7,11},{8,12},{9,13},{1... | collective-permute-start | bytes 196616 | tf_op jit(solution)/shard_map/ppermute | solution.py:440
  9.5 5.1 %collective-permute-done = bf16[1,4,8192]{2,1,0:T(4,128)(2,1)S(1)} collective-permute-done((bf16[1,4,8192]{2,1,0:T(4,128)(2,1)S(1)}, bf16[1,4,8192]{2,1,0:T(4,128)(2,1)S(1)}, u32[]{:S(2)}, u32[]{:S(2)}) %collective-permute-start) | collective-permute-done | bytes 65568 | tf_op jit(solution)/shard_map/ppermute | solution.py:440
  15.6 1.8 %shard_map.185 = (s32[64,1]{1,0:T(8,128)S(1)}, s32[64,1]{1,0:T(8,128)S(1)}, f32[64,128]{1,0:T(8,128)S(1)}, f32[64,128]{1,0:T(8,128)S(1)}, f32[64,128]{1,0:T(8,12...) custom-call(s32[1]{0:T(128)} %bitcast.index_ref, ...), custom_call_target="tpu_custom_call" | custom-call | flops 4600000000 | tf_op jit(solution)/shard_map/pallas_call | solution.py:36
  17.4 3.2 %collective-permute-done.4.refs_1_ = bf16[3,4,8192]{2,1,0:T(4,128)(2,1)S(1)} collective-permute-done((bf16[3,4,8192]{2,1,0:T(4,128)(2,1)S(1)}, bf16[3,4,8192]{2,1,0:T(4,128)(2,1)S(1)}, u32[]{:S(2)}, u32[]{:S(2)}) %collective-permute-start.4) | collective-permute-done | bytes 196640 | tf_op jit(solution)/shard_map/ppermute | solution.py:440
  20.6 1.4 %collective-permute-done.6.refs_3_ = bf16[3,4,8192]{2,1,0:T(4,128)(2,1)S(1)} collective-permute-done((bf16[3,4,8192]{2,1,0:T(4,128)(2,1)S(1)}, bf16[3,4,8192]{2,1,0:T(4,128)(2,1)S(1)}, u32[]{:S(2)}, u32[]{:S(2)}) %collective-permute-start.6) | collective-permute-done | bytes 196640 | tf_op jit(solution)/shard_map/ppermute | solution.py:440
  22.1 0.7 shard_map.186
  23.1 1.5 %collective-permute-start.8 = (bf16[16,128]{1,0:T(8,128)(2,1)S(1)}, bf16[16,128]{1,0:T(8,128)(2,1)S(1)}, u32[]{:S(2)}, u32[]{:S(2)}) collective-permute-start(bf16[16,128]{1,0:T(8,128)(2,1)S(1)} %get-tuple-element.57.refs_0_), channel_id=1, source_target_pairs={{0,2},{1,3},{2,0},{3,1},{4,6},{5,7},{6,4},{7,5},{8,10},{9,11},{10,... | collective-permute-start | bytes 12296 | tf_op jit(solution)/shard_map/ppermute | solution.py:440
  24.7 1.3 %shard_map.188 = (f32[64,512]{1,0:T(8,128)S(1)}, f32[64,128]{1,0:T(8,128)S(1)}) custom-call(bf16[64,8192]{1,0:T(8,128)(2,1)S(1)} %get-tuple-element.58.x_ref, bf16[8192,512]{1,0:T(8,128)(2,1)S(1)} %bitcast.15, bf16[64,8192]{1,0:T(8,128)(2,1)S(1)} %bitcast.18, bf16[64,8192]{1,0:T(8,128)(2,1)S(1)} %bitcast.20), custom_call_target="tpu_custom_call" | custom-call | flops 345000000 | tf_op jit(solution)/shard_map/pallas_call | solution.py:36
  26.1 0.6 collective-permute-done.8.refs_2_
  26.7 1.8 %collective-permute-start.12 = (bf16[16,128]{1,0:T(8,128)(2,1)S(1)}, bf16[16,128]{1,0:T(8,128)(2,1)S(1)}, u32[]{:S(2)}, u32[]{:S(2)}) collective-permute-start(bf16[16,128]{1,0:T(8,128)(2,1)S(1)} %shard_map.187.refs_0_), channel_id=1, source_target_pairs={{0,12},{1,13},{2,14},{3,15},{4,0},{5,1},{6,2},{7,3},{8,4},{9,5},{1... | collective-permute-start | bytes 12296 | tf_op jit(solution)/shard_map/ppermute | solution.py:440
  28.6 0.6 collective-permute-start.11
  29.2 1.9 %collective-permute-start.10 = (bf16[16,128]{1,0:T(8,128)(2,1)S(1)}, bf16[16,128]{1,0:T(8,128)(2,1)S(1)}, u32[]{:S(2)}, u32[]{:S(2)}) collective-permute-start(bf16[16,128]{1,0:T(8,128)(2,1)S(1)} %shard_map.187.refs_0_), channel_id=1, source_target_pairs={{0,4},{1,5},{2,6},{3,7},{4,8},{5,9},{6,10},{7,11},{8,12},{9,13},{1... | collective-permute-start | bytes 12296 | tf_op jit(solution)/shard_map/ppermute | solution.py:440
  31.1 1.3 %shard_map.189 = (f32[64,512]{1,0:T(8,128)S(1)}, f32[64,128]{1,0:T(8,128)S(1)}) custom-call(bf16[64,8192]{1,0:T(8,128)(2,1)S(1)} %get-tuple-element.58.x_ref, bf16[8192,512]{1,0:T(8,128)(2,1)S(1)} %bitcast.15, bf16[64,8192]{1,0:T(8,128)(2,1)S(1)} %bitcast.19, bf16[64,8192]{1,0:T(8,128)(2,1)S(1)} %bitcast.21), custom_call_target="tpu_custom_call" | custom-call | flops 345000000 | tf_op jit(solution)/shard_map/pallas_call | solution.py:36
  33.1 1.5 %collective-permute-done.10.refs_1_ = bf16[16,128]{1,0:T(8,128)(2,1)S(1)} collective-permute-done((bf16[16,128]{1,0:T(8,128)(2,1)S(1)}, bf16[16,128]{1,0:T(8,128)(2,1)S(1)}, u32[]{:S(2)}, u32[]{:S(2)}) %collective-permute-start.10) | collective-permute-done | bytes 4128 | tf_op jit(solution)/shard_map/ppermute | solution.py:440
  34.6 0.8 %shard_map.190 = bf16[16,24,128]{2,1,0:T(8,128)(2,1)S(1)} custom-call(bf16[16,128]{1,0:T(8,128)(2,1)S(1)} %shard_map.187.refs_0_, bf16[16,128]{1,0:T(8,128)(2,1)S(1)} %collective-permute-done.10.refs_1_, bf16[16,128]{1,0:T(8,128)(2,1)S(1)} %collective-permute-done.11.refs_2_, bf16[16,128]{1,0:T(8,128)(2,1)S(1)} %collective-permute-done.12.refs_3_, ...), custom_call_target="tpu_custom_call" | custom-call | flops 1035000000 | tf_op jit(solution)/shard_map/pallas_call | solution.py:36
  35.4 10.1 %all_to_all.10.x_ref = bf16[16,24,128]{2,1,0:T(8,128)(2,1)S(1)} all-to-all(bf16[16,24,128]{2,1,0:T(8,128)(2,1)S(1)} %shard_map.190), channel_id=1, replica_groups=mesh['replica'=2,'serve'=16] {'serve'}, dimensions={0} | all-to-all | bytes 196608 | tf_op jit(solution)/shard_map/all_to_all | solution.py:548
  45.6 2.0 %shard_map.191 = (bf16[2,2,1024]{2,1,0:T(2,128)(2,1)}, bf16[2,2,1024]{2,1,0:T(2,128)(2,1)}, bf16[16,16,128]{2,1,0:T(8,128)(2,1)S(1)}) custom-call(s32[1]{0:T(128)} %bitcast.index_ref, s32[32]{0:T(128)S(1)} %copy-done.13, bf16[16,24,128]{2,1,0:T(8,128)(2,1)S(1)} %all_to_all.10.x_ref, bf16[256,384]{1,0:T(8,128)(2,1)S(1)} %get-tuple-element.72.order_ref, ...), custom_call_target="tpu_custom_call" | custom-call | flops 1150000000 | tf_op jit(solution)/shard_map/pallas_call | solution.py:36
  47.5 9.5 %all_to_all.11.ctx_ref = bf16[16,16,128]{2,1,0:T(8,128)(2,1)S(1)} all-to-all(bf16[16,16,128]{2,1,0:T(8,128)(2,1)S(1)} %get-tuple-element.73), channel_id=1, replica_groups=mesh['replica'=2,'serve'=16] {'serve'}, dimensions={0} | all-to-all | bytes 131072 | tf_op jit(solution)/shard_map/all_to_all | solution.py:559
  57.0 1.7 %shard_map.192 = (bf16[64,512]{1,0:T(8,128)(2,1)S(1)}, f32[32,5120]{1,0:T(8,128)S(1)}, f32[32,5120]{1,0:T(8,128)S(1)}) custom-call(bf16[16,16,128]{2,1,0:T(8,128)(2,1)S(1)} %all_to_all.11.ctx_ref, bf16[256,256]{1,0:T(8,128)(2,1)S(1)} %get-tuple-element.74.take_ref, bf16[512,8192]{1,0:T(8,128)(2,1)S(1)} %bitcast.17), custom_call_target="tpu_custom_call" | custom-call | flops 460000000 | tf_op jit(solution)/shard_map/pallas_call | solution.py:36
  58.8 0.9 %shard_map.195 = (f32[32,3072]{1,0:T(8,128)S(1)}, f32[32,3072]{1,0:T(8,128)S(1)}) custom-call(bf16[64,512]{1,0:T(8,128)(2,1)S(1)} %get-tuple-element.83.a_ref, bf16[512,8192]{1,0:T(8,128)(2,1)S(1)} %bitcast.17), custom_call_target="tpu_custom_call" | custom-call | flops 345000000 | tf_op jit(solution)/shard_map/pallas_call | solution.py:36
  60.3 0.6 collective-permute-done.13.came_ref
  61.9 1.0 %collective-permute-start.20 = (bf16[8,3072]{1,0:T(8,128)(2,1)S(1)}, bf16[8,3072]{1,0:T(8,128)(2,1)S(1)}, u32[]{:S(2)}, u32[]{:S(2)}) collective-permute-start(bf16[8,3072]{1,0:T(8,128)(2,1)S(1)} %get-tuple-element.88), channel_id=1, source_target_pairs={{0,8},{1,9},{2,10},{3,11},{4,12},{5,13},{6,14},{7,15},{8,0},{9,1},... | collective-permute-start | bytes 147464 | tf_op jit(solution)/shard_map/ppermute | solution.py:440
  62.8 2.7 %collective-permute-start.21 = (bf16[8,3072]{1,0:T(8,128)(2,1)S(1)}, bf16[8,3072]{1,0:T(8,128)(2,1)S(1)}, u32[]{:S(2)}, u32[]{:S(2)}) collective-permute-start(bf16[8,3072]{1,0:T(8,128)(2,1)S(1)} %get-tuple-element.89), channel_id=1, source_target_pairs={{0,12},{1,13},{2,14},{3,15},{4,0},{5,1},{6,2},{7,3},{8,4},{9,5},{1... | collective-permute-start | bytes 147464 | tf_op jit(solution)/shard_map/ppermute | solution.py:440
  65.5 1.7 %collective-permute-done.14.refs_1_ = bf16[16,5120]{1,0:T(8,128)(2,1)S(1)} collective-permute-done((bf16[16,5120]{1,0:T(8,128)(2,1)S(1)}, bf16[16,5120]{1,0:T(8,128)(2,1)S(1)}, u32[]{:S(2)}, u32[]{:S(2)}) %collective-permute-start.14) | collective-permute-done | bytes 163872 | tf_op jit(solution)/shard_map/ppermute | solution.py:440
  67.5 0.9 %collective-permute-start.16 = (bf16[4,5120]{1,0:T(4,128)(2,1)S(1)}, bf16[4,5120]{1,0:T(4,128)(2,1)S(1)}, u32[]{:S(2)}, u32[]{:S(2)}) collective-permute-start(bf16[4,5120]{1,0:T(4,128)(2,1)S(1)} %get-tuple-element.81), channel_id=1, source_target_pairs={{0,8},{1,9},{2,10},{3,11},{4,12},{5,13},{6,14},{7,15},{8,0},{9,1},... | collective-permute-start | bytes 122888 | tf_op jit(solution)/shard_map/ppermute | solution.py:440
  68.4 2.8 %collective-permute-start.17 = (bf16[4,5120]{1,0:T(4,128)(2,1)S(1)}, bf16[4,5120]{1,0:T(4,128)(2,1)S(1)}, u32[]{:S(2)}, u32[]{:S(2)}) collective-permute-start(bf16[4,5120]{1,0:T(4,128)(2,1)S(1)} %get-tuple-element.82), channel_id=1, source_target_pairs={{0,12},{1,13},{2,14},{3,15},{4,0},{5,1},{6,2},{7,3},{8,4},{9,5},{1... | collective-permute-start | bytes 122888 | tf_op jit(solution)/shard_map/ppermute | solution.py:440
  71.2 0.9 %collective-permute-start.22 = (bf16[4,3072]{1,0:T(4,128)(2,1)S(1)}, bf16[4,3072]{1,0:T(4,128)(2,1)S(1)}, u32[]{:S(2)}, u32[]{:S(2)}) collective-permute-start(bf16[4,3072]{1,0:T(4,128)(2,1)S(1)} %get-tuple-element.91), channel_id=1, source_target_pairs={{0,2},{1,3},{2,0},{3,1},{4,6},{5,7},{6,4},{7,5},{8,10},{9,11},{10,... | collective-permute-start | bytes 73736 | tf_op jit(solution)/shard_map/ppermute | solution.py:440
  72.1 3.0 %collective-permute-done.22.refs_5_ = bf16[4,3072]{1,0:T(4,128)(2,1)S(1)} collective-permute-done((bf16[4,3072]{1,0:T(4,128)(2,1)S(1)}, bf16[4,3072]{1,0:T(4,128)(2,1)S(1)}, u32[]{:S(2)}, u32[]{:S(2)}) %collective-permute-start.22) | collective-permute-done | bytes 24608 | tf_op jit(solution)/shard_map/ppermute | solution.py:440
  75.1 0.7 shard_map.198
  (75 shorter events, 4.3 us)
Async XLA Ops:
  0.7 14.9 %copy-start.13 = (s32[32]{0:T(128)S(1)}, s32[32]{0:T(128)}, u32[]{:S(2)}) copy-start(s32[32]{0:T(128)} %len_ref.1) | copy-start | bytes 388
  0.7 14.9 %copy-start.12 = (s32[32]{0:T(128)S(1)}, s32[32]{0:T(128)}, u32[]{:S(2)}) copy-start(s32[32]{0:T(128)} %slot_hbm.1) | copy-start | bytes 388
  0.7 14.9 %copy-start.11 = (s32[32]{0:T(128)S(1)}, s32[32]{0:T(128)}, u32[]{:S(2)}) copy-start(s32[32]{0:T(128)} %adapter_hbm.1) | copy-start | bytes 388
  1.8 13.6 %collective-permute-start.3 = (bf16[1,4,8192]{2,1,0:T(4,128)(2,1)S(1)}, bf16[1,4,8192]{2,1,0:T(4,128)(2,1)S(1)}, u32[]{:S(2)}, u32[]{:S(2)}) collective-permute-start(bf16[1,4,8192]{2,1,0:T(4,128)(2,1)S(1)} %bitcast.24), channel_id=1, source_target_pairs={{0,2},{1,3},{2,0},{3,1},{4,6},{5,7},{6,4},{7,5},{8,10},{9,11},{10,... | collective-permute-start | bytes 196616 | tf_op jit(solution)/shard_map/ppermute | solution.py:440
  4.9 9.9 %collective-permute-start.2 = (bf16[1,4,8192]{2,1,0:T(4,128)(2,1)S(1)}, bf16[1,4,8192]{2,1,0:T(4,128)(2,1)S(1)}, u32[]{:S(2)}, u32[]{:S(2)}) collective-permute-start(bf16[1,4,8192]{2,1,0:T(4,128)(2,1)S(1)} %bitcast.25), channel_id=1, source_target_pairs={{0,12},{1,13},{2,14},{3,15},{4,0},{5,1},{6,2},{7,3},{8,4},{9,5},{1... | collective-permute-start | bytes 196616 | tf_op jit(solution)/shard_map/ppermute | solution.py:440
  8.5 6.2 %collective-permute-start.1 = (bf16[1,4,8192]{2,1,0:T(4,128)(2,1)S(1)}, bf16[1,4,8192]{2,1,0:T(4,128)(2,1)S(1)}, u32[]{:S(2)}, u32[]{:S(2)}) collective-permute-start(bf16[1,4,8192]{2,1,0:T(4,128)(2,1)S(1)} %bitcast.26), channel_id=1, source_target_pairs={{0,8},{1,9},{2,10},{3,11},{4,12},{5,13},{6,14},{7,15},{8,0},{9,1},... | collective-permute-start | bytes 196616 | tf_op jit(solution)/shard_map/ppermute | solution.py:440
  8.5 6.2 %collective-permute-start = (bf16[1,4,8192]{2,1,0:T(4,128)(2,1)S(1)}, bf16[1,4,8192]{2,1,0:T(4,128)(2,1)S(1)}, u32[]{:S(2)}, u32[]{:S(2)}) collective-permute-start(bf16[1,4,8192]{2,1,0:T(4,128)(2,1)S(1)} %bitcast.27), channel_id=1, source_target_pairs={{0,4},{1,5},{2,6},{3,7},{4,8},{5,9},{6,10},{7,11},{8,12},{9,13},{1... | collective-permute-start | bytes 196616 | tf_op jit(solution)/shard_map/ppermute | solution.py:440
  14.8 5.8 %collective-permute-start.4 = (bf16[3,4,8192]{2,1,0:T(4,128)(2,1)S(1)}, bf16[3,4,8192]{2,1,0:T(4,128)(2,1)S(1)}, u32[]{:S(2)}, u32[]{:S(2)}) collective-permute-start(bf16[3,4,8192]{2,1,0:T(4,128)(2,1)S(1)} %get-tuple-element.96), channel_id=1, source_target_pairs={{0,2},{1,3},{2,0},{3,1},{4,6},{5,7},{6,4},{7,5},{8,10},{9,11},{10,... | collective-permute-start | bytes 589832 | tf_op jit(solution)/shard_map/ppermute | solution.py:440
  15.4 9.3 %slice-start = ((s8[8388608]{0:T(1024)(128)(4,1)}), s8[4194304]{0:T(1024)(128)(4,1)S(1)}, s32[]{:S(2)}) async-start(s8[8388608]{0:T(1024)(128)(4,1)} %bitcast.14), calls=%async_computation.2 | async-start | bytes 8388608
  15.4 9.2 %slice-start.1 = ((s8[8388608]{0:T(1024)(128)(4,1)}), s8[4194304]{0:T(1024)(128)(4,1)S(1)}, s32[]{:S(2)}) async-start(s8[8388608]{0:T(1024)(128)(4,1)} %bitcast.14), calls=%async_computation.3 | async-start | bytes 8388608
  15.5 5.1 %collective-permute-start.5 = (bf16[5,4,8192]{2,1,0:T(4,128)(2,1)S(1)}, bf16[5,4,8192]{2,1,0:T(4,128)(2,1)S(1)}, u32[]{:S(2)}, u32[]{:S(2)}) collective-permute-start(bf16[5,4,8192]{2,1,0:T(4,128)(2,1)S(1)} %constant_dynamic-update-slice_fusion.refs_0_), channel_id=1, source_target_pairs={{0,1},{1,0},{2,3},{3,2},{4,5},{5,4},{6,7},{7,6},{8,9},{9,8},{10,11... | collective-permute-start | bytes 983048 | tf_op jit(solution)/shard_map/ppermute | solution.py:440
  20.6 1.4 %collective-permute-start.6 = (bf16[3,4,8192]{2,1,0:T(4,128)(2,1)S(1)}, bf16[3,4,8192]{2,1,0:T(4,128)(2,1)S(1)}, u32[]{:S(2)}, u32[]{:S(2)}) collective-permute-start(bf16[3,4,8192]{2,1,0:T(4,128)(2,1)S(1)} %collective-permute-done.4.refs_1_), channel_id=1, source_target_pairs={{0,1},{1,0},{2,3},{3,2},{4,5},{5,4},{6,7},{7,6},{8,9},{9,8},{10,11... | collective-permute-start | bytes 589832 | tf_op jit(solution)/shard_map/ppermute | solution.py:440
  22.8 3.3 %collective-permute-start.9 = (bf16[16,128]{1,0:T(8,128)(2,1)S(1)}, bf16[16,128]{1,0:T(8,128)(2,1)S(1)}, u32[]{:S(2)}, u32[]{:S(2)}) collective-permute-start(bf16[16,128]{1,0:T(8,128)(2,1)S(1)} %get-tuple-element.57.refs_0_), channel_id=1, source_target_pairs={{0,3},{1,2},{2,1},{3,0},{4,7},{5,6},{6,5},{7,4},{8,11},{9,10},{10,... | collective-permute-start | bytes 12296 | tf_op jit(solution)/shard_map/ppermute | solution.py:440
  23.1 3.6 %collective-permute-start.8 = (bf16[16,128]{1,0:T(8,128)(2,1)S(1)}, bf16[16,128]{1,0:T(8,128)(2,1)S(1)}, u32[]{:S(2)}, u32[]{:S(2)}) collective-permute-start(bf16[16,128]{1,0:T(8,128)(2,1)S(1)} %get-tuple-element.57.refs_0_), channel_id=1, source_target_pairs={{0,2},{1,3},{2,0},{3,1},{4,6},{5,7},{6,4},{7,5},{8,10},{9,11},{10,... | collective-permute-start | bytes 12296 | tf_op jit(solution)/shard_map/ppermute | solution.py:440
  24.6 2.1 %collective-permute-start.7 = (bf16[16,128]{1,0:T(8,128)(2,1)S(1)}, bf16[16,128]{1,0:T(8,128)(2,1)S(1)}, u32[]{:S(2)}, u32[]{:S(2)}) collective-permute-start(bf16[16,128]{1,0:T(8,128)(2,1)S(1)} %get-tuple-element.57.refs_0_), channel_id=1, source_target_pairs={{0,1},{1,0},{2,3},{3,2},{4,5},{5,4},{6,7},{7,6},{8,9},{9,8},{10,11... | collective-permute-start | bytes 12296 | tf_op jit(solution)/shard_map/ppermute | solution.py:440
  26.1 19.5 %copy-start.4 = (bf16[2,384,1024]{2,1,0:T(8,128)(2,1)S(1)}, bf16[2,384,1024]{2,1,0:T(8,128)(2,1)}, u32[]{:S(2)}) copy-start(bf16[2,384,1024]{2,1,0:T(8,128)(2,1)} %k_ref.1) | copy-start | bytes 4718596
  26.1 19.5 %copy-start.5 = (bf16[2,384,1024]{2,1,0:T(8,128)(2,1)S(1)}, bf16[2,384,1024]{2,1,0:T(8,128)(2,1)}, u32[]{:S(2)}) copy-start(bf16[2,384,1024]{2,1,0:T(8,128)(2,1)} %v_ref.1) | copy-start | bytes 4718596
  26.7 30.3 %slice-start.2 = ((s8[8388608]{0:T(1024)(128)(4,1)}), s8[4194304]{0:T(1024)(128)(4,1)S(1)}, s32[]{:S(2)}) async-start(s8[8388608]{0:T(1024)(128)(4,1)} %bitcast.16), calls=%async_computation.4 | async-start | bytes 8388608
  26.7 30.3 %slice-start.3 = ((s8[8388608]{0:T(1024)(128)(4,1)}), s8[4194304]{0:T(1024)(128)(4,1)S(1)}, s32[]{:S(2)}) async-start(s8[8388608]{0:T(1024)(128)(4,1)} %bitcast.16), calls=%async_computation.5 | async-start | bytes 8388608
  26.7 5.7 %collective-permute-start.12 = (bf16[16,128]{1,0:T(8,128)(2,1)S(1)}, bf16[16,128]{1,0:T(8,128)(2,1)S(1)}, u32[]{:S(2)}, u32[]{:S(2)}) collective-permute-start(bf16[16,128]{1,0:T(8,128)(2,1)S(1)} %shard_map.187.refs_0_), channel_id=1, source_target_pairs={{0,12},{1,13},{2,14},{3,15},{4,0},{5,1},{6,2},{7,3},{8,4},{9,5},{1... | collective-permute-start | bytes 12296 | tf_op jit(solution)/shard_map/ppermute | solution.py:440
  28.6 4.5 %collective-permute-start.11 = (bf16[16,128]{1,0:T(8,128)(2,1)S(1)}, bf16[16,128]{1,0:T(8,128)(2,1)S(1)}, u32[]{:S(2)}, u32[]{:S(2)}) collective-permute-start(bf16[16,128]{1,0:T(8,128)(2,1)S(1)} %shard_map.187.refs_0_), channel_id=1, source_target_pairs={{0,8},{1,9},{2,10},{3,11},{4,12},{5,13},{6,14},{7,15},{8,0},{9,1},... | collective-permute-start | bytes 12296 | tf_op jit(solution)/shard_map/ppermute | solution.py:440
  29.2 5.4 %collective-permute-start.10 = (bf16[16,128]{1,0:T(8,128)(2,1)S(1)}, bf16[16,128]{1,0:T(8,128)(2,1)S(1)}, u32[]{:S(2)}, u32[]{:S(2)}) collective-permute-start(bf16[16,128]{1,0:T(8,128)(2,1)S(1)} %shard_map.187.refs_0_), channel_id=1, source_target_pairs={{0,4},{1,5},{2,6},{3,7},{4,8},{5,9},{6,10},{7,11},{8,12},{9,13},{1... | collective-permute-start | bytes 12296 | tf_op jit(solution)/shard_map/ppermute | solution.py:440
  58.7 2.2 %collective-permute-start.13 = (f32[32,5120]{1,0:T(8,128)S(1)}, f32[32,5120]{1,0:T(8,128)S(1)}, u32[]{:S(2)}, u32[]{:S(2)}) collective-permute-start(f32[32,5120]{1,0:T(8,128)S(1)} %get-tuple-element.76), channel_id=1, source_target_pairs={{0,1},{1,0},{2,3},{3,2},{4,5},{5,4},{6,7},{7,6},{8,9},{9,8},{10,11... | collective-permute-start | bytes 1966088 | tf_op jit(solution)/shard_map/ppermute | solution.py:440
  59.7 1.9 %collective-permute-start.18 = (f32[32,3072]{1,0:T(8,128)S(1)}, f32[32,3072]{1,0:T(8,128)S(1)}, u32[]{:S(2)}, u32[]{:S(2)}) collective-permute-start(f32[32,3072]{1,0:T(8,128)S(1)} %get-tuple-element.85), channel_id=1, source_target_pairs={{0,1},{1,0},{2,3},{3,2},{4,5},{5,4},{6,7},{7,6},{8,9},{9,8},{10,11... | collective-permute-start | bytes 1179656 | tf_op jit(solution)/shard_map/ppermute | solution.py:440
  60.9 6.3 %collective-permute-start.14 = (bf16[16,5120]{1,0:T(8,128)(2,1)S(1)}, bf16[16,5120]{1,0:T(8,128)(2,1)S(1)}, u32[]{:S(2)}, u32[]{:S(2)}) collective-permute-start(bf16[16,5120]{1,0:T(8,128)(2,1)S(1)} %get-tuple-element.78), channel_id=1, source_target_pairs={{0,2},{1,3},{2,0},{3,1},{4,6},{5,7},{6,4},{7,5},{8,10},{9,11},{10,... | collective-permute-start | bytes 491528 | tf_op jit(solution)/shard_map/ppermute | solution.py:440
  61.7 6.8 %collective-permute-start.19 = (bf16[8,3072]{1,0:T(8,128)(2,1)S(1)}, bf16[8,3072]{1,0:T(8,128)(2,1)S(1)}, u32[]{:S(2)}, u32[]{:S(2)}) collective-permute-start(bf16[8,3072]{1,0:T(8,128)(2,1)S(1)} %get-tuple-element.87), channel_id=1, source_target_pairs={{0,4},{1,5},{2,6},{3,7},{4,8},{5,9},{6,10},{7,11},{8,12},{9,13},{1... | collective-permute-start | bytes 147464 | tf_op jit(solution)/shard_map/ppermute | solution.py:440
  61.9 9.3 %collective-permute-start.20 = (bf16[8,3072]{1,0:T(8,128)(2,1)S(1)}, bf16[8,3072]{1,0:T(8,128)(2,1)S(1)}, u32[]{:S(2)}, u32[]{:S(2)}) collective-permute-start(bf16[8,3072]{1,0:T(8,128)(2,1)S(1)} %get-tuple-element.88), channel_id=1, source_target_pairs={{0,8},{1,9},{2,10},{3,11},{4,12},{5,13},{6,14},{7,15},{8,0},{9,1},... | collective-permute-start | bytes 147464 | tf_op jit(solution)/shard_map/ppermute | solution.py:440
  62.8 8.3 %collective-permute-start.21 = (bf16[8,3072]{1,0:T(8,128)(2,1)S(1)}, bf16[8,3072]{1,0:T(8,128)(2,1)S(1)}, u32[]{:S(2)}, u32[]{:S(2)}) collective-permute-start(bf16[8,3072]{1,0:T(8,128)(2,1)S(1)} %get-tuple-element.89), channel_id=1, source_target_pairs={{0,12},{1,13},{2,14},{3,15},{4,0},{5,1},{6,2},{7,3},{8,4},{9,5},{1... | collective-permute-start | bytes 147464 | tf_op jit(solution)/shard_map/ppermute | solution.py:440
  67.3 7.8 %collective-permute-start.15 = (bf16[4,5120]{1,0:T(4,128)(2,1)S(1)}, bf16[4,5120]{1,0:T(4,128)(2,1)S(1)}, u32[]{:S(2)}, u32[]{:S(2)}) collective-permute-start(bf16[4,5120]{1,0:T(4,128)(2,1)S(1)} %get-tuple-element.80), channel_id=1, source_target_pairs={{0,4},{1,5},{2,6},{3,7},{4,8},{5,9},{6,10},{7,11},{8,12},{9,13},{1... | collective-permute-start | bytes 122888 | tf_op jit(solution)/shard_map/ppermute | solution.py:440
  67.5 7.6 %collective-permute-start.16 = (bf16[4,5120]{1,0:T(4,128)(2,1)S(1)}, bf16[4,5120]{1,0:T(4,128)(2,1)S(1)}, u32[]{:S(2)}, u32[]{:S(2)}) collective-permute-start(bf16[4,5120]{1,0:T(4,128)(2,1)S(1)} %get-tuple-element.81), channel_id=1, source_target_pairs={{0,8},{1,9},{2,10},{3,11},{4,12},{5,13},{6,14},{7,15},{8,0},{9,1},... | collective-permute-start | bytes 122888 | tf_op jit(solution)/shard_map/ppermute | solution.py:440
  68.4 6.7 %collective-permute-start.17 = (bf16[4,5120]{1,0:T(4,128)(2,1)S(1)}, bf16[4,5120]{1,0:T(4,128)(2,1)S(1)}, u32[]{:S(2)}, u32[]{:S(2)}) collective-permute-start(bf16[4,5120]{1,0:T(4,128)(2,1)S(1)} %get-tuple-element.82), channel_id=1, source_target_pairs={{0,12},{1,13},{2,14},{3,15},{4,0},{5,1},{6,2},{7,3},{8,4},{9,5},{1... | collective-permute-start | bytes 122888 | tf_op jit(solution)/shard_map/ppermute | solution.py:440
  71.2 3.9 %collective-permute-start.22 = (bf16[4,3072]{1,0:T(4,128)(2,1)S(1)}, bf16[4,3072]{1,0:T(4,128)(2,1)S(1)}, u32[]{:S(2)}, u32[]{:S(2)}) collective-permute-start(bf16[4,3072]{1,0:T(4,128)(2,1)S(1)} %get-tuple-element.91), channel_id=1, source_target_pairs={{0,2},{1,3},{2,0},{3,1},{4,6},{5,7},{6,4},{7,5},{8,10},{9,11},{10,... | collective-permute-start | bytes 73736 | tf_op jit(solution)/shard_map/ppermute | solution.py:440
  (9 other events, 51.0 us)

commit v9 on v8

--- a/solution.py
+++ b/solution.py
@@ -82,6 +82,12 @@
     out_ref[...] = scaled_frequency(lax.broadcasted_iota(jnp.int32, out_ref.shape, 1) // 2)
 
 
+def moved(at, distance, size):
+    if size & (size - 1) == 0:
+        return at ^ distance
+    return (at + distance) % size
+
+
 def prep_body(
     sizes, rank, own, key_cols, adapters,
     index_ref, length_hbm, adapter_hbm, slot_hbm, frequency_ref,
@@ -102,9 +108,9 @@
 
     def device_of(block, sign):
         c, m, f = block // (far * near), block // far % near, block % far
-        f = (far_at + sign * f + far) % far
-        m = (near_at + sign * m + near) % near
-        c = (core_at + sign * c + cores) % cores
+        f = moved(far_at, f if sign > 0 or far & (far - 1) == 0 else far - f, far)
+        m = moved(near_at, m, near)
+        c = moved(core_at, c, cores)
         return (f * near + m) * cores + c
 
     def iota(shape, axis):
@@ -379,7 +385,7 @@
     rows = refs[0].shape[0]
     refs[0][...] = total[:rows]
     for f, ref in enumerate(refs[1:], 1):
-        ref[...] = total[f * rows : (f + 1) * rows].astype(BF16)
+        ref[...] = total[f * rows : (f + 1) * rows].astype(ref.dtype)
 
 
 def last_body(longs, first_ref, second_ref, *refs):
@@ -432,7 +438,8 @@
         for z in range(far):
             for y in range(near):
                 for k in range(cores):
-                    to = (((z + f) % far) * near + (y + m) % near) * cores + (k + c) % cores
+                    to = moved(z, f, far) * near + moved(y, m, near)
+                    to = to * cores + moved(k, c, cores)
                     pairs.append(((z * near + y) * cores + k, to))
         return pairs
 
@@ -603,7 +610,7 @@
     others = [shift(other, f, 0, 0) for f, other in enumerate(others, 1)]
     short, *sides = whole_call(
         functools.partial(far_body, len(sides)),
-        (kind(1, width - cut, F32),) + (kind(1, width - cut, BF16),) * (near - 1),
+        (kind(1, width - cut, F32),) * near,
         (short, *sides),
         cost=0.1,
     )

time: 76.2 us -> 80.9 us (1.062)
  waiting for transfers between devices: 18.3 us -> 20.8 us
  blocking collectives: 19.6 us -> 21.1 us
  starting transfers between devices: 24 us -> 25 us
    ppermute x23, waiting for transfers between devices: 18.3 us -> 20.8 us  [shift(): return lax.ppermute(value, 'serve', partner(f, m, c))]
    all_to_all x1, blocking collectives: 10.1 us -> 11.6 us  [shards(): lax.all_to_all(ready, 'serve', split_axis=0, concat_axis=0, tiled=True)]
    ppermute x23, starting transfers between devices: 24 us -> 25 us  [shift(): return lax.ppermute(value, 'serve', partner(f, m, c))]
  transfers between devices with their start and end apart: 23 -> 23, of which waited for: 10 -> 11; matrix products, arithmetic and copies ran while one was open for 0% -> 0% of each run, Pallas kernels for 7% -> 7%
where the time goes in v9:
time: 80.9 us; the launch traced here: 80.6 us
  starting transfers between devices  25 us (31%)
  blocking collectives  21.1 us (26%)
  waiting for transfers between devices  20.8 us (26%)
  Pallas kernels  11.7 us (14%)
  local copies, waits for them, and re-layouts  1.02 us (1%)
  between operations  0.95 us (1%)
    ppermute x23, starting transfers between devices, shift(): return lax.ppermute(value, 'serve', partner(f, m, c))  25 us
    ppermute x23, waiting for transfers between devices, shift(): return lax.ppermute(value, 'serve', partner(f, m, c))  20.8 us
    pallas_call x16, Pallas kernels, whole_call(): pl.pallas_call(body, out_shape=out_shape, in_specs=specs, out_specs=tuple...  11.7 us
    all_to_all x1, blocking collectives, shards(): lax.all_to_all(ready, 'serve', split_axis=0, concat_axis=0, tiled=True)  11.6 us
    all_to_all x1, blocking collectives, shards(): lax.all_to_all(context, 'serve', split_axis=0, concat_axis=0, tiled=True)  9.48 us
  transfers between devices with their start and end apart: 23, of which 11 were waited for; matrix products, arithmetic and copies ran while one was open for 0% of the time, Pallas kernels for 7%

profile of v9, /device:TPU:0, one launch (start us, length us, event | category | flops | bytes accessed | tf_op | source)
XLA Modules:
  0.0 80.6 jit_solution(11728110959496179879)
XLA Ops:
  0.7 0.6 copy-done.10
  1.8 3.0 %collective-permute-start.3 = (bf16[1,4,8192]{2,1,0:T(4,128)(2,1)S(1)}, bf16[1,4,8192]{2,1,0:T(4,128)(2,1)S(1)}, u32[]{:S(2)}, u32[]{:S(2)}) collective-permute-start(bf16[1,4,8192]{2,1,0:T(4,128)(2,1)S(1)} %bitcast.24), channel_id=1, source_target_pairs={{0,2},{1,3},{2,0},{3,1},{4,6},{5,7},{6,4},{7,5},{8,10},{9,11},{10,... | collective-permute-start | bytes 196616 | tf_op jit(solution)/shard_map/ppermute | solution.py:447
  4.9 3.6 %collective-permute-start.2 = (bf16[1,4,8192]{2,1,0:T(4,128)(2,1)S(1)}, bf16[1,4,8192]{2,1,0:T(4,128)(2,1)S(1)}, u32[]{:S(2)}, u32[]{:S(2)}) collective-permute-start(bf16[1,4,8192]{2,1,0:T(4,128)(2,1)S(1)} %bitcast.25), channel_id=1, source_target_pairs={{0,12},{1,13},{2,14},{3,15},{4,8},{5,9},{6,10},{7,11},{8,4},{9,5},... | collective-permute-start | bytes 196616 | tf_op jit(solution)/shard_map/ppermute | solution.py:447
  8.5 0.8 collective-permute-start
  9.3 4.6 %collective-permute-done = bf16[1,4,8192]{2,1,0:T(4,128)(2,1)S(1)} collective-permute-done((bf16[1,4,8192]{2,1,0:T(4,128)(2,1)S(1)}, bf16[1,4,8192]{2,1,0:T(4,128)(2,1)S(1)}, u32[]{:S(2)}, u32[]{:S(2)}) %collective-permute-start) | collective-permute-done | bytes 65568 | tf_op jit(solution)/shard_map/ppermute | solution.py:447
  14.7 1.6 %shard_map.185 = (s32[64,1]{1,0:T(8,128)S(1)}, s32[64,1]{1,0:T(8,128)S(1)}, f32[64,128]{1,0:T(8,128)S(1)}, f32[64,128]{1,0:T(8,128)S(1)}, f32[64,128]{1,0:T(8,12...) custom-call(s32[1]{0:T(128)} %bitcast.index_ref, ...), custom_call_target="tpu_custom_call" | custom-call | flops 4600000000 | tf_op jit(solution)/shard_map/pallas_call | solution.py:36
  16.3 4.0 %collective-permute-done.4.refs_1_ = bf16[3,4,8192]{2,1,0:T(4,128)(2,1)S(1)} collective-permute-done((bf16[3,4,8192]{2,1,0:T(4,128)(2,1)S(1)}, bf16[3,4,8192]{2,1,0:T(4,128)(2,1)S(1)}, u32[]{:S(2)}, u32[]{:S(2)}) %collective-permute-start.4) | collective-permute-done | bytes 196640 | tf_op jit(solution)/shard_map/ppermute | solution.py:447
  20.3 1.4 %collective-permute-done.6.refs_3_ = bf16[3,4,8192]{2,1,0:T(4,128)(2,1)S(1)} collective-permute-done((bf16[3,4,8192]{2,1,0:T(4,128)(2,1)S(1)}, bf16[3,4,8192]{2,1,0:T(4,128)(2,1)S(1)}, u32[]{:S(2)}, u32[]{:S(2)}) %collective-permute-start.6) | collective-permute-done | bytes 196640 | tf_op jit(solution)/shard_map/ppermute | solution.py:447
  21.7 0.7 shard_map.186
  22.7 1.5 %collective-permute-start.8 = (bf16[16,128]{1,0:T(8,128)(2,1)S(1)}, bf16[16,128]{1,0:T(8,128)(2,1)S(1)}, u32[]{:S(2)}, u32[]{:S(2)}) collective-permute-start(bf16[16,128]{1,0:T(8,128)(2,1)S(1)} %get-tuple-element.57.refs_0_), channel_id=1, source_target_pairs={{0,2},{1,3},{2,0},{3,1},{4,6},{5,7},{6,4},{7,5},{8,10},{9,11},{10,... | collective-permute-start | bytes 12296 | tf_op jit(solution)/shard_map/ppermute | solution.py:447
  24.3 1.3 %shard_map.188 = (f32[64,512]{1,0:T(8,128)S(1)}, f32[64,128]{1,0:T(8,128)S(1)}) custom-call(bf16[64,8192]{1,0:T(8,128)(2,1)S(1)} %get-tuple-element.58.x_ref, bf16[8192,512]{1,0:T(8,128)(2,1)S(1)} %bitcast.15, bf16[64,8192]{1,0:T(8,128)(2,1)S(1)} %bitcast.18, bf16[64,8192]{1,0:T(8,128)(2,1)S(1)} %bitcast.20), custom_call_target="tpu_custom_call" | custom-call | flops 345000000 | tf_op jit(solution)/shard_map/pallas_call | solution.py:36
  26.4 2.1 %collective-permute-start.12 = (bf16[16,128]{1,0:T(8,128)(2,1)S(1)}, bf16[16,128]{1,0:T(8,128)(2,1)S(1)}, u32[]{:S(2)}, u32[]{:S(2)}) collective-permute-start(bf16[16,128]{1,0:T(8,128)(2,1)S(1)} %shard_map.187.refs_0_), channel_id=1, source_target_pairs={{0,12},{1,13},{2,14},{3,15},{4,8},{5,9},{6,10},{7,11},{8,4},{9,5},... | collective-permute-start | bytes 12296 | tf_op jit(solution)/shard_map/ppermute | solution.py:447
  28.4 2.4 %collective-permute-start.10 = (bf16[16,128]{1,0:T(8,128)(2,1)S(1)}, bf16[16,128]{1,0:T(8,128)(2,1)S(1)}, u32[]{:S(2)}, u32[]{:S(2)}) collective-permute-start(bf16[16,128]{1,0:T(8,128)(2,1)S(1)} %shard_map.187.refs_0_), channel_id=1, source_target_pairs={{0,4},{1,5},{2,6},{3,7},{4,0},{5,1},{6,2},{7,3},{8,12},{9,13},{10,... | collective-permute-start | bytes 12296 | tf_op jit(solution)/shard_map/ppermute | solution.py:447
  30.8 1.3 %shard_map.189 = (f32[64,512]{1,0:T(8,128)S(1)}, f32[64,128]{1,0:T(8,128)S(1)}) custom-call(bf16[64,8192]{1,0:T(8,128)(2,1)S(1)} %get-tuple-element.58.x_ref, bf16[8192,512]{1,0:T(8,128)(2,1)S(1)} %bitcast.15, bf16[64,8192]{1,0:T(8,128)(2,1)S(1)} %bitcast.19, bf16[64,8192]{1,0:T(8,128)(2,1)S(1)} %bitcast.21), custom_call_target="tpu_custom_call" | custom-call | flops 345000000 | tf_op jit(solution)/shard_map/pallas_call | solution.py:36
  32.2 0.8 collective-permute-done.11.refs_2_
  33.0 0.8 %shard_map.190 = bf16[16,24,128]{2,1,0:T(8,128)(2,1)S(1)} custom-call(bf16[16,128]{1,0:T(8,128)(2,1)S(1)} %shard_map.187.refs_0_, bf16[16,128]{1,0:T(8,128)(2,1)S(1)} %collective-permute-done.10.refs_1_, bf16[16,128]{1,0:T(8,128)(2,1)S(1)} %collective-permute-done.11.refs_2_, bf16[16,128]{1,0:T(8,128)(2,1)S(1)} %collective-permute-done.12.refs_3_, ...), custom_call_target="tpu_custom_call" | custom-call | flops 1035000000 | tf_op jit(solution)/shard_map/pallas_call | solution.py:36
  33.8 11.6 %all_to_all.10.x_ref = bf16[16,24,128]{2,1,0:T(8,128)(2,1)S(1)} all-to-all(bf16[16,24,128]{2,1,0:T(8,128)(2,1)S(1)} %shard_map.190), channel_id=1, replica_groups=mesh['replica'=2,'serve'=16] {'serve'}, dimensions={0} | all-to-all | bytes 196608 | tf_op jit(solution)/shard_map/all_to_all | solution.py:555
  45.4 2.0 %shard_map.191 = (bf16[2,2,1024]{2,1,0:T(2,128)(2,1)}, bf16[2,2,1024]{2,1,0:T(2,128)(2,1)}, bf16[16,16,128]{2,1,0:T(8,128)(2,1)S(1)}) custom-call(s32[1]{0:T(128)} %bitcast.index_ref, s32[32]{0:T(128)S(1)} %copy-done.13, bf16[16,24,128]{2,1,0:T(8,128)(2,1)S(1)} %all_to_all.10.x_ref, bf16[256,384]{1,0:T(8,128)(2,1)S(1)} %get-tuple-element.72.order_ref, ...), custom_call_target="tpu_custom_call" | custom-call | flops 1150000000 | tf_op jit(solution)/shard_map/pallas_call | solution.py:36
  47.4 9.5 %all_to_all.11.ctx_ref = bf16[16,16,128]{2,1,0:T(8,128)(2,1)S(1)} all-to-all(bf16[16,16,128]{2,1,0:T(8,128)(2,1)S(1)} %get-tuple-element.73), channel_id=1, replica_groups=mesh['replica'=2,'serve'=16] {'serve'}, dimensions={0} | all-to-all | bytes 131072 | tf_op jit(solution)/shard_map/all_to_all | solution.py:566
  56.9 1.7 %shard_map.192 = (bf16[64,512]{1,0:T(8,128)(2,1)S(1)}, f32[32,5120]{1,0:T(8,128)S(1)}, f32[32,5120]{1,0:T(8,128)S(1)}) custom-call(bf16[16,16,128]{2,1,0:T(8,128)(2,1)S(1)} %all_to_all.11.ctx_ref, bf16[256,256]{1,0:T(8,128)(2,1)S(1)} %get-tuple-element.74.take_ref, bf16[512,8192]{1,0:T(8,128)(2,1)S(1)} %bitcast.17), custom_call_target="tpu_custom_call" | custom-call | flops 460000000 | tf_op jit(solution)/shard_map/pallas_call | solution.py:36
  58.6 0.9 %shard_map.195 = (f32[32,3072]{1,0:T(8,128)S(1)}, f32[32,3072]{1,0:T(8,128)S(1)}) custom-call(bf16[64,512]{1,0:T(8,128)(2,1)S(1)} %get-tuple-element.83.a_ref, bf16[512,8192]{1,0:T(8,128)(2,1)S(1)} %bitcast.17), custom_call_target="tpu_custom_call" | custom-call | flops 345000000 | tf_op jit(solution)/shard_map/pallas_call | solution.py:36
  60.1 0.6 collective-permute-done.13.came_ref
  61.7 1.0 %collective-permute-start.20 = (bf16[8,3072]{1,0:T(8,128)(2,1)S(1)}, bf16[8,3072]{1,0:T(8,128)(2,1)S(1)}, u32[]{:S(2)}, u32[]{:S(2)}) collective-permute-start(bf16[8,3072]{1,0:T(8,128)(2,1)S(1)} %get-tuple-element.88), channel_id=1, source_target_pairs={{0,8},{1,9},{2,10},{3,11},{4,12},{5,13},{6,14},{7,15},{8,0},{9,1},... | collective-permute-start | bytes 147464 | tf_op jit(solution)/shard_map/ppermute | solution.py:447
  62.7 3.3 %collective-permute-start.21 = (bf16[8,3072]{1,0:T(8,128)(2,1)S(1)}, bf16[8,3072]{1,0:T(8,128)(2,1)S(1)}, u32[]{:S(2)}, u32[]{:S(2)}) collective-permute-start(bf16[8,3072]{1,0:T(8,128)(2,1)S(1)} %get-tuple-element.89), channel_id=1, source_target_pairs={{0,12},{1,13},{2,14},{3,15},{4,8},{5,9},{6,10},{7,11},{8,4},{9,5},... | collective-permute-start | bytes 147464 | tf_op jit(solution)/shard_map/ppermute | solution.py:447
  66.2 3.0 %collective-permute-done.20.refs_2_ = bf16[8,3072]{1,0:T(8,128)(2,1)S(1)} collective-permute-done((bf16[8,3072]{1,0:T(8,128)(2,1)S(1)}, bf16[8,3072]{1,0:T(8,128)(2,1)S(1)}, u32[]{:S(2)}, u32[]{:S(2)}) %collective-permute-start.20) | collective-permute-done | bytes 49184 | tf_op jit(solution)/shard_map/ppermute | solution.py:447
  69.2 1.0 %collective-permute-start.22 = (f32[4,3072]{1,0:T(4,128)S(1)}, f32[4,3072]{1,0:T(4,128)S(1)}, u32[]{:S(2)}, u32[]{:S(2)}) collective-permute-start(f32[4,3072]{1,0:T(4,128)S(1)} %get-tuple-element.91), channel_id=1, source_target_pairs={{0,2},{1,3},{2,0},{3,1},{4,6},{5,7},{6,4},{7,5},{8,10},{9,11},{10,... | collective-permute-start | bytes 147464 | tf_op jit(solution)/shard_map/ppermute | solution.py:447
  70.3 1.2 %collective-permute-start.15 = (bf16[4,5120]{1,0:T(4,128)(2,1)S(1)}, bf16[4,5120]{1,0:T(4,128)(2,1)S(1)}, u32[]{:S(2)}, u32[]{:S(2)}) collective-permute-start(bf16[4,5120]{1,0:T(4,128)(2,1)S(1)} %get-tuple-element.80), channel_id=1, source_target_pairs={{0,4},{1,5},{2,6},{3,7},{4,0},{5,1},{6,2},{7,3},{8,12},{9,13},{10,... | collective-permute-start | bytes 122888 | tf_op jit(solution)/shard_map/ppermute | solution.py:447
  71.5 2.6 %collective-permute-start.16 = (bf16[4,5120]{1,0:T(4,128)(2,1)S(1)}, bf16[4,5120]{1,0:T(4,128)(2,1)S(1)}, u32[]{:S(2)}, u32[]{:S(2)}) collective-permute-start(bf16[4,5120]{1,0:T(4,128)(2,1)S(1)} %get-tuple-element.81), channel_id=1, source_target_pairs={{0,8},{1,9},{2,10},{3,11},{4,12},{5,13},{6,14},{7,15},{8,0},{9,1},... | collective-permute-start | bytes 122888 | tf_op jit(solution)/shard_map/ppermute | solution.py:447
  74.0 0.7 collective-permute-start.17
  74.8 2.4 %collective-permute-done.16.refs_2_ = bf16[4,5120]{1,0:T(4,128)(2,1)S(1)} collective-permute-done((bf16[4,5120]{1,0:T(4,128)(2,1)S(1)}, bf16[4,5120]{1,0:T(4,128)(2,1)S(1)}, u32[]{:S(2)}, u32[]{:S(2)}) %collective-permute-start.16) | collective-permute-done | bytes 40992 | tf_op jit(solution)/shard_map/ppermute | solution.py:447
  77.2 2.7 %collective-permute-done.17.refs_3_ = bf16[4,5120]{1,0:T(4,128)(2,1)S(1)} collective-permute-done((bf16[4,5120]{1,0:T(4,128)(2,1)S(1)}, bf16[4,5120]{1,0:T(4,128)(2,1)S(1)}, u32[]{:S(2)}, u32[]{:S(2)}) %collective-permute-start.17) | collective-permute-done | bytes 40992 | tf_op jit(solution)/shard_map/ppermute | solution.py:447
  79.8 0.7 shard_map.198
  (75 shorter events, 4.2 us)
Async XLA Ops:
  0.7 14.0 %copy-start.13 = (s32[32]{0:T(128)S(1)}, s32[32]{0:T(128)}, u32[]{:S(2)}) copy-start(s32[32]{0:T(128)} %len_ref.1) | copy-start | bytes 388
  0.7 14.0 %copy-start.12 = (s32[32]{0:T(128)S(1)}, s32[32]{0:T(128)}, u32[]{:S(2)}) copy-start(s32[32]{0:T(128)} %slot_hbm.1) | copy-start | bytes 388
  0.7 14.0 %copy-start.11 = (s32[32]{0:T(128)S(1)}, s32[32]{0:T(128)}, u32[]{:S(2)}) copy-start(s32[32]{0:T(128)} %adapter_hbm.1) | copy-start | bytes 388
  1.8 12.7 %collective-permute-start.3 = (bf16[1,4,8192]{2,1,0:T(4,128)(2,1)S(1)}, bf16[1,4,8192]{2,1,0:T(4,128)(2,1)S(1)}, u32[]{:S(2)}, u32[]{:S(2)}) collective-permute-start(bf16[1,4,8192]{2,1,0:T(4,128)(2,1)S(1)} %bitcast.24), channel_id=1, source_target_pairs={{0,2},{1,3},{2,0},{3,1},{4,6},{5,7},{6,4},{7,5},{8,10},{9,11},{10,... | collective-permute-start | bytes 196616 | tf_op jit(solution)/shard_map/ppermute | solution.py:447
  4.9 9.2 %collective-permute-start.2 = (bf16[1,4,8192]{2,1,0:T(4,128)(2,1)S(1)}, bf16[1,4,8192]{2,1,0:T(4,128)(2,1)S(1)}, u32[]{:S(2)}, u32[]{:S(2)}) collective-permute-start(bf16[1,4,8192]{2,1,0:T(4,128)(2,1)S(1)} %bitcast.25), channel_id=1, source_target_pairs={{0,12},{1,13},{2,14},{3,15},{4,8},{5,9},{6,10},{7,11},{8,4},{9,5},... | collective-permute-start | bytes 196616 | tf_op jit(solution)/shard_map/ppermute | solution.py:447
  8.5 5.5 %collective-permute-start.1 = (bf16[1,4,8192]{2,1,0:T(4,128)(2,1)S(1)}, bf16[1,4,8192]{2,1,0:T(4,128)(2,1)S(1)}, u32[]{:S(2)}, u32[]{:S(2)}) collective-permute-start(bf16[1,4,8192]{2,1,0:T(4,128)(2,1)S(1)} %bitcast.26), channel_id=1, source_target_pairs={{0,8},{1,9},{2,10},{3,11},{4,12},{5,13},{6,14},{7,15},{8,0},{9,1},... | collective-permute-start | bytes 196616 | tf_op jit(solution)/shard_map/ppermute | solution.py:447
  8.5 5.4 %collective-permute-start = (bf16[1,4,8192]{2,1,0:T(4,128)(2,1)S(1)}, bf16[1,4,8192]{2,1,0:T(4,128)(2,1)S(1)}, u32[]{:S(2)}, u32[]{:S(2)}) collective-permute-start(bf16[1,4,8192]{2,1,0:T(4,128)(2,1)S(1)} %bitcast.27), channel_id=1, source_target_pairs={{0,4},{1,5},{2,6},{3,7},{4,0},{5,1},{6,2},{7,3},{8,12},{9,13},{10,... | collective-permute-start | bytes 196616 | tf_op jit(solution)/shard_map/ppermute | solution.py:447
  14.1 6.2 %collective-permute-start.4 = (bf16[3,4,8192]{2,1,0:T(4,128)(2,1)S(1)}, bf16[3,4,8192]{2,1,0:T(4,128)(2,1)S(1)}, u32[]{:S(2)}, u32[]{:S(2)}) collective-permute-start(bf16[3,4,8192]{2,1,0:T(4,128)(2,1)S(1)} %get-tuple-element.96), channel_id=1, source_target_pairs={{0,2},{1,3},{2,0},{3,1},{4,6},{5,7},{6,4},{7,5},{8,10},{9,11},{10,... | collective-permute-start | bytes 589832 | tf_op jit(solution)/shard_map/ppermute | solution.py:447
  14.5 9.8 %slice-start = ((s8[8388608]{0:T(1024)(128)(4,1)}), s8[4194304]{0:T(1024)(128)(4,1)S(1)}, s32[]{:S(2)}) async-start(s8[8388608]{0:T(1024)(128)(4,1)} %bitcast.14), calls=%async_computation.2 | async-start | bytes 8388608
  14.6 9.8 %slice-start.1 = ((s8[8388608]{0:T(1024)(128)(4,1)}), s8[4194304]{0:T(1024)(128)(4,1)S(1)}, s32[]{:S(2)}) async-start(s8[8388608]{0:T(1024)(128)(4,1)} %bitcast.14), calls=%async_computation.3 | async-start | bytes 8388608
  14.6 5.7 %collective-permute-start.5 = (bf16[5,4,8192]{2,1,0:T(4,128)(2,1)S(1)}, bf16[5,4,8192]{2,1,0:T(4,128)(2,1)S(1)}, u32[]{:S(2)}, u32[]{:S(2)}) collective-permute-start(bf16[5,4,8192]{2,1,0:T(4,128)(2,1)S(1)} %constant_dynamic-update-slice_fusion.refs_0_), channel_id=1, source_target_pairs={{0,1},{1,0},{2,3},{3,2},{4,5},{5,4},{6,7},{7,6},{8,9},{9,8},{10,11... | collective-permute-start | bytes 983048 | tf_op jit(solution)/shard_map/ppermute | solution.py:447
  20.3 1.4 %collective-permute-start.6 = (bf16[3,4,8192]{2,1,0:T(4,128)(2,1)S(1)}, bf16[3,4,8192]{2,1,0:T(4,128)(2,1)S(1)}, u32[]{:S(2)}, u32[]{:S(2)}) collective-permute-start(bf16[3,4,8192]{2,1,0:T(4,128)(2,1)S(1)} %collective-permute-done.4.refs_1_), channel_id=1, source_target_pairs={{0,1},{1,0},{2,3},{3,2},{4,5},{5,4},{6,7},{7,6},{8,9},{9,8},{10,11... | collective-permute-start | bytes 589832 | tf_op jit(solution)/shard_map/ppermute | solution.py:447
  22.4 3.3 %collective-permute-start.9 = (bf16[16,128]{1,0:T(8,128)(2,1)S(1)}, bf16[16,128]{1,0:T(8,128)(2,1)S(1)}, u32[]{:S(2)}, u32[]{:S(2)}) collective-permute-start(bf16[16,128]{1,0:T(8,128)(2,1)S(1)} %get-tuple-element.57.refs_0_), channel_id=1, source_target_pairs={{0,3},{1,2},{2,1},{3,0},{4,7},{5,6},{6,5},{7,4},{8,11},{9,10},{10,... | collective-permute-start | bytes 12296 | tf_op jit(solution)/shard_map/ppermute | solution.py:447
  22.7 3.6 %collective-permute-start.8 = (bf16[16,128]{1,0:T(8,128)(2,1)S(1)}, bf16[16,128]{1,0:T(8,128)(2,1)S(1)}, u32[]{:S(2)}, u32[]{:S(2)}) collective-permute-start(bf16[16,128]{1,0:T(8,128)(2,1)S(1)} %get-tuple-element.57.refs_0_), channel_id=1, source_target_pairs={{0,2},{1,3},{2,0},{3,1},{4,6},{5,7},{6,4},{7,5},{8,10},{9,11},{10,... | collective-permute-start | bytes 12296 | tf_op jit(solution)/shard_map/ppermute | solution.py:447
  24.2 2.1 %collective-permute-start.7 = (bf16[16,128]{1,0:T(8,128)(2,1)S(1)}, bf16[16,128]{1,0:T(8,128)(2,1)S(1)}, u32[]{:S(2)}, u32[]{:S(2)}) collective-permute-start(bf16[16,128]{1,0:T(8,128)(2,1)S(1)} %get-tuple-element.57.refs_0_), channel_id=1, source_target_pairs={{0,1},{1,0},{2,3},{3,2},{4,5},{5,4},{6,7},{7,6},{8,9},{9,8},{10,11... | collective-permute-start | bytes 12296 | tf_op jit(solution)/shard_map/ppermute | solution.py:447
  25.7 19.7 %copy-start.4 = (bf16[2,384,1024]{2,1,0:T(8,128)(2,1)S(1)}, bf16[2,384,1024]{2,1,0:T(8,128)(2,1)}, u32[]{:S(2)}) copy-start(bf16[2,384,1024]{2,1,0:T(8,128)(2,1)} %k_ref.1) | copy-start | bytes 4718596
  25.7 19.7 %copy-start.5 = (bf16[2,384,1024]{2,1,0:T(8,128)(2,1)S(1)}, bf16[2,384,1024]{2,1,0:T(8,128)(2,1)}, u32[]{:S(2)}) copy-start(bf16[2,384,1024]{2,1,0:T(8,128)(2,1)} %v_ref.1) | copy-start | bytes 4718596
  26.4 30.5 %slice-start.2 = ((s8[8388608]{0:T(1024)(128)(4,1)}), s8[4194304]{0:T(1024)(128)(4,1)S(1)}, s32[]{:S(2)}) async-start(s8[8388608]{0:T(1024)(128)(4,1)} %bitcast.16), calls=%async_computation.4 | async-start | bytes 8388608
  26.4 30.5 %slice-start.3 = ((s8[8388608]{0:T(1024)(128)(4,1)}), s8[4194304]{0:T(1024)(128)(4,1)S(1)}, s32[]{:S(2)}) async-start(s8[8388608]{0:T(1024)(128)(4,1)} %bitcast.16), calls=%async_computation.5 | async-start | bytes 8388608
  26.4 5.8 %collective-permute-start.12 = (bf16[16,128]{1,0:T(8,128)(2,1)S(1)}, bf16[16,128]{1,0:T(8,128)(2,1)S(1)}, u32[]{:S(2)}, u32[]{:S(2)}) collective-permute-start(bf16[16,128]{1,0:T(8,128)(2,1)S(1)} %shard_map.187.refs_0_), channel_id=1, source_target_pairs={{0,12},{1,13},{2,14},{3,15},{4,8},{5,9},{6,10},{7,11},{8,4},{9,5},... | collective-permute-start | bytes 12296 | tf_op jit(solution)/shard_map/ppermute | solution.py:447
  28.4 4.5 %collective-permute-start.11 = (bf16[16,128]{1,0:T(8,128)(2,1)S(1)}, bf16[16,128]{1,0:T(8,128)(2,1)S(1)}, u32[]{:S(2)}, u32[]{:S(2)}) collective-permute-start(bf16[16,128]{1,0:T(8,128)(2,1)S(1)} %shard_map.187.refs_0_), channel_id=1, source_target_pairs={{0,8},{1,9},{2,10},{3,11},{4,12},{5,13},{6,14},{7,15},{8,0},{9,1},... | collective-permute-start | bytes 12296 | tf_op jit(solution)/shard_map/ppermute | solution.py:447
  28.4 4.5 %collective-permute-start.10 = (bf16[16,128]{1,0:T(8,128)(2,1)S(1)}, bf16[16,128]{1,0:T(8,128)(2,1)S(1)}, u32[]{:S(2)}, u32[]{:S(2)}) collective-permute-start(bf16[16,128]{1,0:T(8,128)(2,1)S(1)} %shard_map.187.refs_0_), channel_id=1, source_target_pairs={{0,4},{1,5},{2,6},{3,7},{4,0},{5,1},{6,2},{7,3},{8,12},{9,13},{10,... | collective-permute-start | bytes 12296 | tf_op jit(solution)/shard_map/ppermute | solution.py:447
  58.5 2.2 %collective-permute-start.13 = (f32[32,5120]{1,0:T(8,128)S(1)}, f32[32,5120]{1,0:T(8,128)S(1)}, u32[]{:S(2)}, u32[]{:S(2)}) collective-permute-start(f32[32,5120]{1,0:T(8,128)S(1)} %get-tuple-element.76), channel_id=1, source_target_pairs={{0,1},{1,0},{2,3},{3,2},{4,5},{5,4},{6,7},{7,6},{8,9},{9,8},{10,11... | collective-permute-start | bytes 1966088 | tf_op jit(solution)/shard_map/ppermute | solution.py:447
  59.5 1.9 %collective-permute-start.18 = (f32[32,3072]{1,0:T(8,128)S(1)}, f32[32,3072]{1,0:T(8,128)S(1)}, u32[]{:S(2)}, u32[]{:S(2)}) collective-permute-start(f32[32,3072]{1,0:T(8,128)S(1)} %get-tuple-element.85), channel_id=1, source_target_pairs={{0,1},{1,0},{2,3},{3,2},{4,5},{5,4},{6,7},{7,6},{8,9},{9,8},{10,11... | collective-permute-start | bytes 1179656 | tf_op jit(solution)/shard_map/ppermute | solution.py:447
  60.8 9.5 %collective-permute-start.14 = (bf16[16,5120]{1,0:T(8,128)(2,1)S(1)}, bf16[16,5120]{1,0:T(8,128)(2,1)S(1)}, u32[]{:S(2)}, u32[]{:S(2)}) collective-permute-start(bf16[16,5120]{1,0:T(8,128)(2,1)S(1)} %get-tuple-element.78), channel_id=1, source_target_pairs={{0,2},{1,3},{2,0},{3,1},{4,6},{5,7},{6,4},{7,5},{8,10},{9,11},{10,... | collective-permute-start | bytes 491528 | tf_op jit(solution)/shard_map/ppermute | solution.py:447
  61.5 4.7 %collective-permute-start.19 = (bf16[8,3072]{1,0:T(8,128)(2,1)S(1)}, bf16[8,3072]{1,0:T(8,128)(2,1)S(1)}, u32[]{:S(2)}, u32[]{:S(2)}) collective-permute-start(bf16[8,3072]{1,0:T(8,128)(2,1)S(1)} %get-tuple-element.87), channel_id=1, source_target_pairs={{0,4},{1,5},{2,6},{3,7},{4,0},{5,1},{6,2},{7,3},{8,12},{9,13},{10,... | collective-permute-start | bytes 147464 | tf_op jit(solution)/shard_map/ppermute | solution.py:447
  61.7 7.5 %collective-permute-start.20 = (bf16[8,3072]{1,0:T(8,128)(2,1)S(1)}, bf16[8,3072]{1,0:T(8,128)(2,1)S(1)}, u32[]{:S(2)}, u32[]{:S(2)}) collective-permute-start(bf16[8,3072]{1,0:T(8,128)(2,1)S(1)} %get-tuple-element.88), channel_id=1, source_target_pairs={{0,8},{1,9},{2,10},{3,11},{4,12},{5,13},{6,14},{7,15},{8,0},{9,1},... | collective-permute-start | bytes 147464 | tf_op jit(solution)/shard_map/ppermute | solution.py:447
  62.7 6.5 %collective-permute-start.21 = (bf16[8,3072]{1,0:T(8,128)(2,1)S(1)}, bf16[8,3072]{1,0:T(8,128)(2,1)S(1)}, u32[]{:S(2)}, u32[]{:S(2)}) collective-permute-start(bf16[8,3072]{1,0:T(8,128)(2,1)S(1)} %get-tuple-element.89), channel_id=1, source_target_pairs={{0,12},{1,13},{2,14},{3,15},{4,8},{5,9},{6,10},{7,11},{8,4},{9,5},... | collective-permute-start | bytes 147464 | tf_op jit(solution)/shard_map/ppermute | solution.py:447
  69.2 5.5 %collective-permute-start.22 = (f32[4,3072]{1,0:T(4,128)S(1)}, f32[4,3072]{1,0:T(4,128)S(1)}, u32[]{:S(2)}, u32[]{:S(2)}) collective-permute-start(f32[4,3072]{1,0:T(4,128)S(1)} %get-tuple-element.91), channel_id=1, source_target_pairs={{0,2},{1,3},{2,0},{3,1},{4,6},{5,7},{6,4},{7,5},{8,10},{9,11},{10,... | collective-permute-start | bytes 147464 | tf_op jit(solution)/shard_map/ppermute | solution.py:447
  70.3 4.5 %collective-permute-start.15 = (bf16[4,5120]{1,0:T(4,128)(2,1)S(1)}, bf16[4,5120]{1,0:T(4,128)(2,1)S(1)}, u32[]{:S(2)}, u32[]{:S(2)}) collective-permute-start(bf16[4,5120]{1,0:T(4,128)(2,1)S(1)} %get-tuple-element.80), channel_id=1, source_target_pairs={{0,4},{1,5},{2,6},{3,7},{4,0},{5,1},{6,2},{7,3},{8,12},{9,13},{10,... | collective-permute-start | bytes 122888 | tf_op jit(solution)/shard_map/ppermute | solution.py:447
  71.5 5.7 %collective-permute-start.16 = (bf16[4,5120]{1,0:T(4,128)(2,1)S(1)}, bf16[4,5120]{1,0:T(4,128)(2,1)S(1)}, u32[]{:S(2)}, u32[]{:S(2)}) collective-permute-start(bf16[4,5120]{1,0:T(4,128)(2,1)S(1)} %get-tuple-element.81), channel_id=1, source_target_pairs={{0,8},{1,9},{2,10},{3,11},{4,12},{5,13},{6,14},{7,15},{8,0},{9,1},... | collective-permute-start | bytes 122888 | tf_op jit(solution)/shard_map/ppermute | solution.py:447
  74.0 5.8 %collective-permute-start.17 = (bf16[4,5120]{1,0:T(4,128)(2,1)S(1)}, bf16[4,5120]{1,0:T(4,128)(2,1)S(1)}, u32[]{:S(2)}, u32[]{:S(2)}) collective-permute-start(bf16[4,5120]{1,0:T(4,128)(2,1)S(1)} %get-tuple-element.82), channel_id=1, source_target_pairs={{0,12},{1,13},{2,14},{3,15},{4,8},{5,9},{6,10},{7,11},{8,4},{9,5},... | collective-permute-start | bytes 122888 | tf_op jit(solution)/shard_map/ppermute | solution.py:447
  (9 other events, 50.7 us)

commit v10 on v8

--- a/solution.py
+++ b/solution.py
@@ -354,43 +354,30 @@
         other_ref[:, at] = product[half:]
 
 
-def far_first_body(near, mine_ref, came_ref, *refs):
-    total = mine_ref[...] + came_ref[...]
-    rows = refs[0].shape[0] // near
-    for f, ref in enumerate(refs):
-        blocks = [(m * len(refs) + f) * rows for m in range(near)]
-        value = jnp.concatenate([total[at : at + rows] for at in blocks], axis=0)
-        ref[...] = value.astype(ref.dtype)
-
-
-def near_body(mine_ref, came_ref, *refs):
-    rows = refs[0].shape[0]
-    total = mine_ref[...] + came_ref[...]
-    refs[0][...] = total[:rows]
-    for m, ref in enumerate(refs[1:], 1):
-        ref[...] = total[m * rows : (m + 1) * rows].astype(BF16)
-
-
-def far_body(came, *refs):
-    total = refs[0][...]
-    for ref in refs[1 : 1 + came]:
+def near_body(mine_ref, came_ref, mine2_ref, came2_ref, keep_ref, *refs):
+    cut = mine_ref.shape[1]
+    kept, rows = keep_ref.shape[0], refs[0].shape[0]
+    for lanes, mine, came in (
+        (slice(0, cut), mine_ref, came_ref),
+        (slice(cut, None), mine2_ref, came2_ref),
+    ):
+        keep_ref[:, lanes] = mine[:kept] + came[:kept]
+        for f, ref in enumerate(refs):
+            at = slice(kept + f * rows, kept + (f + 1) * rows)
+            ref[:, lanes] = (mine[at] + came[at]).astype(BF16)
+
+
+def far_body(f, keep_ref, came_ref, out_ref):
+    rows = out_ref.shape[0]
+    total = keep_ref[f * rows : (f + 1) * rows] + came_ref[...].astype(F32)
+    out_ref[...] = total.astype(BF16)
+
+
+def last_body(first_ref, second_ref, keep_ref, *refs):
+    came, (one_ref, two_ref) = refs[:-2], refs[-2:]
+    total = keep_ref[: came[0].shape[0]]
+    for ref in came:
         total = total + ref[...].astype(F32)
-    refs = refs[1 + came :]
-    rows = refs[0].shape[0]
-    refs[0][...] = total[:rows]
-    for f, ref in enumerate(refs[1:], 1):
-        ref[...] = total[f * rows : (f + 1) * rows].astype(BF16)
-
-
-def last_body(longs, first_ref, second_ref, *refs):
-    one_ref, two_ref = refs[-2:]
-    totals = []
-    for part in (refs[:longs], refs[longs:-2]):
-        total = part[0][...]
-        for ref in part[1:]:
-            total = total + ref[...].astype(F32)
-        totals.append(total)
-    total = jnp.concatenate(totals, axis=1)
     own = one_ref.shape[0]
     one_ref[...] = (first_ref[...].astype(F32) + total[:own]).astype(BF16)
     two_ref[...] = (second_ref[...].astype(F32) + total[own:]).astype(BF16)
@@ -457,12 +444,10 @@
     )
     normed = normed[None]
     fars = [shift(normed, f, 0, 0) for f in range(1, far)]
-    nears = [shift(normed, 0, m, 0) for m in range(1, near)]
-    rest = jnp.concatenate(fars)
-    groups = [jnp.concatenate([normed, *fars, *nears[:1]])]
-    groups += [shift(rest, 0, m, 0) for m in range(1, near)]
-
-    rest, at = lax.optimization_barrier((rest, index[None]))
+    nears = [shift(normed, 0, 1, 0)] + [shift(part, 0, 1, 0) for part in fars]
+    groups = [jnp.concatenate([normed, *fars, nears[0]]), jnp.concatenate(nears[1:-1]), nears[-1]]
+
+    at = index[None]
     sent = -(-(rows * local + rows) // 8) * 8
     narrow = jax.ShapeDtypeStruct((all_rows, 1), jnp.int32)
     table = jax.ShapeDtypeStruct((all_rows, HEAD), F32)
@@ -493,9 +478,9 @@
         ],
         cost=4.0,
     )
-    slot, groups[1] = lax.optimization_barrier((slot, groups[1]))
-
-    groups += [shift(part, 0, 0, c) for c in range(1, cores) for part in groups[:near]]
+    slot, groups[-1] = lax.optimization_barrier((slot, groups[-1]))
+
+    groups += [shift(part, 0, 0, 1) for part in groups]
 
     query_down = jnp.swapaxes(query_down_weights, 1, 2).reshape(adapters * rank, width)
     value_down = jnp.swapaxes(value_down_weights, 1, 2).reshape(adapters * rank, width)
@@ -577,42 +562,33 @@
         cost=0.3,
     )
 
-    def kind(count, columns, dtype):
-        return jax.ShapeDtypeStruct((count * rows, columns), dtype)
-
+    message = jax.ShapeDtypeStruct((rows, width), BF16)
     keep, *others = whole_call(
         near_body,
-        (kind(far, cut, F32),) + (kind(far, cut, BF16),) * (near - 1),
-        (mine_long, shift(other_long, 0, 0, 1)),
-        cost=0.1,
-    )
-    others = [shift(other, 0, m, 0) for m, other in enumerate(others, 1)]
-    short, *sides = whole_call(
-        functools.partial(far_first_body, near),
-        (kind(near, width - cut, F32),) + (kind(near, width - cut, BF16),) * (far - 1),
-        (mine_short, shift(other_short, 0, 0, 1)),
-        cost=0.1,
-    )
-    sides = [shift(side, f, 0, 0) for f, side in enumerate(sides, 1)]
-    keep, *others = whole_call(
-        functools.partial(far_body, len(others)),
-        (kind(1, cut, F32),) + (kind(1, cut, BF16),) * (far - 1),
-        (keep, *others),
-        cost=0.1,
-    )
-    others = [shift(other, f, 0, 0) for f, other in enumerate(others, 1)]
-    short, *sides = whole_call(
-        functools.partial(far_body, len(sides)),
-        (kind(1, width - cut, F32),) + (kind(1, width - cut, BF16),) * (near - 1),
-        (short, *sides),
-        cost=0.1,
-    )
-    sides = [shift(side, 0, m, 0) for m, side in enumerate(sides, 1)]
+        (jax.ShapeDtypeStruct((far * rows, width), F32),) + (message,) * far,
+        (
+            mine_long,
+            shift(other_long, 0, 0, 1),
+            mine_short,
+            shift(other_short, 0, 0, 1),
+        ),
+        cost=0.2,
+    )
+    came = []
+    for f in range(1, far):
+        folded = whole_call(
+            functools.partial(far_body, f),
+            message,
+            (keep, shift(others[f], 0, 1, 0)),
+            cost=0.1,
+        )
+        came.append(shift(folded, f, 0, 0))
+    came.append(shift(others[0], 0, 1, 0))
     result = jax.ShapeDtypeStruct((own, width), BF16)
     out_one, out_two = whole_call(
-        functools.partial(last_body, 1 + len(others)),
+        last_body,
         (result, result),
-        (residual_first, residual_second, keep, *others, short, *sides),
+        (residual_first, residual_second, keep, *came),
         cost=0.1,
     )
     return (out_one, out_two, new_keys, new_values)

time: 76.2 us -> 79.5 us (1.043)
  waiting for transfers between devices: 18.3 us -> 22.4 us
    ppermute x23 -> x25, waiting for transfers between devices: 18.3 us -> 22.4 us  [shift(): return lax.ppermute(value, 'serve', partner(f, m, c))]
    ppermute x23 -> x25, starting transfers between devices: 24 us -> 23.3 us  [shift(): return lax.ppermute(value, 'serve', partner(f, m, c))]
  transfers between devices with their start and end apart: 23 -> 25, of which waited for: 10 -> 13; matrix products, arithmetic and copies ran while one was open for 0% -> 0% of each run, Pallas kernels for 7% -> 7%
where the time goes in v10:
time: 79.5 us; the launch traced here: 79.2 us
  starting transfers between devices  23.3 us (29%)
  waiting for transfers between devices  22.4 us (28%)
  blocking collectives  19.5 us (25%)
  Pallas kernels  12.1 us (15%)
  local copies, waits for them, and re-layouts  1.04 us (1%)
  between operations  1.01 us (1%)
    ppermute x25, starting transfers between devices, shift(): return lax.ppermute(value, 'serve', partner(f, m, c))  23.3 us
    ppermute x25, waiting for transfers between devices, shift(): return lax.ppermute(value, 'serve', partner(f, m, c))  22.4 us
    pallas_call x16, Pallas kernels, whole_call(): pl.pallas_call(body, out_shape=out_shape, in_specs=specs, out_specs=tuple...  12.1 us
    all_to_all x1, blocking collectives, shards(): lax.all_to_all(ready, 'serve', split_axis=0, concat_axis=0, tiled=True)  9.99 us
    all_to_all x1, blocking collectives, shards(): lax.all_to_all(context, 'serve', split_axis=0, concat_axis=0, tiled=True)  9.48 us
  transfers between devices with their start and end apart: 25, of which 13 were waited for; matrix products, arithmetic and copies ran while one was open for 0% of the time, Pallas kernels for 7%

profile of v10, /device:TPU:0, one launch (start us, length us, event | category | flops | bytes accessed | tf_op | source)
XLA Modules:
  0.0 79.2 jit_solution(17722289558280549044)
XLA Ops:
  1.8 3.0 %collective-permute-start.3 = (bf16[1,4,8192]{2,1,0:T(4,128)(2,1)S(1)}, bf16[1,4,8192]{2,1,0:T(4,128)(2,1)S(1)}, u32[]{:S(2)}, u32[]{:S(2)}) collective-permute-start(bf16[1,4,8192]{2,1,0:T(4,128)(2,1)S(1)} %bitcast.24), channel_id=1, source_target_pairs={{0,2},{1,3},{2,0},{3,1},{4,6},{5,7},{6,4},{7,5},{8,10},{9,11},{10,... | collective-permute-start | bytes 196616 | tf_op jit(solution)/shard_map/ppermute | solution.py:427
  4.9 3.6 %collective-permute-start.2 = (bf16[1,4,8192]{2,1,0:T(4,128)(2,1)S(1)}, bf16[1,4,8192]{2,1,0:T(4,128)(2,1)S(1)}, u32[]{:S(2)}, u32[]{:S(2)}) collective-permute-start(bf16[1,4,8192]{2,1,0:T(4,128)(2,1)S(1)} %bitcast.25), channel_id=1, source_target_pairs={{0,12},{1,13},{2,14},{3,15},{4,0},{5,1},{6,2},{7,3},{8,4},{9,5},{1... | collective-permute-start | bytes 196616 | tf_op jit(solution)/shard_map/ppermute | solution.py:427
  8.5 1.0 %collective-permute-start = (bf16[1,4,8192]{2,1,0:T(4,128)(2,1)S(1)}, bf16[1,4,8192]{2,1,0:T(4,128)(2,1)S(1)}, u32[]{:S(2)}, u32[]{:S(2)}) collective-permute-start(bf16[1,4,8192]{2,1,0:T(4,128)(2,1)S(1)} %bitcast.27), channel_id=1, source_target_pairs={{0,4},{1,5},{2,6},{3,7},{4,8},{5,9},{6,10},{7,11},{8,12},{9,13},{1... | collective-permute-start | bytes 196616 | tf_op jit(solution)/shard_map/ppermute | solution.py:427
  9.5 5.1 %collective-permute-done = bf16[1,4,8192]{2,1,0:T(4,128)(2,1)S(1)} collective-permute-done((bf16[1,4,8192]{2,1,0:T(4,128)(2,1)S(1)}, bf16[1,4,8192]{2,1,0:T(4,128)(2,1)S(1)}, u32[]{:S(2)}, u32[]{:S(2)}) %collective-permute-start) | collective-permute-done | bytes 65568 | tf_op jit(solution)/shard_map/ppermute | solution.py:427
  15.4 1.6 %collective-permute-start.6 = (bf16[1,4,8192]{2,1,0:T(4,128)(2,1)S(1)}, bf16[1,4,8192]{2,1,0:T(4,128)(2,1)S(1)}, u32[]{:S(2)}, u32[]{:S(2)}) collective-permute-start(bf16[1,4,8192]{2,1,0:T(4,128)(2,1)S(1)} %collective-permute-done.2), channel_id=1, source_target_pairs={{0,2},{1,3},{2,0},{3,1},{4,6},{5,7},{6,4},{7,5},{8,10},{9,11},{10,... | collective-permute-start | bytes 196616 | tf_op jit(solution)/shard_map/ppermute | solution.py:427
  17.5 1.8 %collective-permute-done.4 = bf16[1,4,8192]{2,1,0:T(4,128)(2,1)S(1)} collective-permute-done((bf16[1,4,8192]{2,1,0:T(4,128)(2,1)S(1)}, bf16[1,4,8192]{2,1,0:T(4,128)(2,1)S(1)}, u32[]{:S(2)}, u32[]{:S(2)}) %collective-permute-start.4) | collective-permute-done | bytes 65568 | tf_op jit(solution)/shard_map/ppermute | solution.py:427
  19.3 2.4 %collective-permute-done.5 = bf16[1,4,8192]{2,1,0:T(4,128)(2,1)S(1)} collective-permute-done((bf16[1,4,8192]{2,1,0:T(4,128)(2,1)S(1)}, bf16[1,4,8192]{2,1,0:T(4,128)(2,1)S(1)}, u32[]{:S(2)}, u32[]{:S(2)}) %collective-permute-start.5) | collective-permute-done | bytes 65568 | tf_op jit(solution)/shard_map/ppermute | solution.py:427
  21.9 1.8 %shard_map.185 = (s32[64,1]{1,0:T(8,128)S(1)}, s32[64,1]{1,0:T(8,128)S(1)}, f32[64,128]{1,0:T(8,128)S(1)}, f32[64,128]{1,0:T(8,128)S(1)}, f32[64,128]{1,0:T(8,12...) custom-call(s32[1]{0:T(128)} %bitcast.index_ref, ...), custom_call_target="tpu_custom_call" | custom-call | flops 4600000000 | tf_op jit(solution)/shard_map/pallas_call | solution.py:36
  24.3 0.9 %collective-permute-done.9.refs_5_ = bf16[1,4,8192]{2,1,0:T(4,128)(2,1)S(1)} collective-permute-done((bf16[1,4,8192]{2,1,0:T(4,128)(2,1)S(1)}, bf16[1,4,8192]{2,1,0:T(4,128)(2,1)S(1)}, u32[]{:S(2)}, u32[]{:S(2)}) %collective-permute-start.9) | collective-permute-done | bytes 65568 | tf_op jit(solution)/shard_map/ppermute | solution.py:427
  25.9 1.1 %collective-permute-start.12 = (bf16[16,128]{1,0:T(8,128)(2,1)S(1)}, bf16[16,128]{1,0:T(8,128)(2,1)S(1)}, u32[]{:S(2)}, u32[]{:S(2)}) collective-permute-start(bf16[16,128]{1,0:T(8,128)(2,1)S(1)} %get-tuple-element.48.refs_0_), channel_id=1, source_target_pairs={{0,3},{1,2},{2,1},{3,0},{4,7},{5,6},{6,5},{7,4},{8,11},{9,10},{10,... | collective-permute-start | bytes 12296 | tf_op jit(solution)/shard_map/ppermute | solution.py:427
  27.1 0.9 %collective-permute-start.11 = (bf16[16,128]{1,0:T(8,128)(2,1)S(1)}, bf16[16,128]{1,0:T(8,128)(2,1)S(1)}, u32[]{:S(2)}, u32[]{:S(2)}) collective-permute-start(bf16[16,128]{1,0:T(8,128)(2,1)S(1)} %get-tuple-element.48.refs_0_), channel_id=1, source_target_pairs={{0,2},{1,3},{2,0},{3,1},{4,6},{5,7},{6,4},{7,5},{8,10},{9,11},{10,... | collective-permute-start | bytes 12296 | tf_op jit(solution)/shard_map/ppermute | solution.py:427
  28.0 1.3 %shard_map.188 = (f32[64,512]{1,0:T(8,128)S(1)}, f32[64,128]{1,0:T(8,128)S(1)}) custom-call(bf16[64,8192]{1,0:T(8,128)(2,1)S(1)} %get-tuple-element.49.x_ref, bf16[8192,512]{1,0:T(8,128)(2,1)S(1)} %bitcast.15, bf16[64,8192]{1,0:T(8,128)(2,1)S(1)} %bitcast.18, bf16[64,8192]{1,0:T(8,128)(2,1)S(1)} %bitcast.20), custom_call_target="tpu_custom_call" | custom-call | flops 345000000 | tf_op jit(solution)/shard_map/pallas_call | solution.py:36
  29.4 1.3 %collective-permute-done.11.refs_2_ = bf16[16,128]{1,0:T(8,128)(2,1)S(1)} collective-permute-done((bf16[16,128]{1,0:T(8,128)(2,1)S(1)}, bf16[16,128]{1,0:T(8,128)(2,1)S(1)}, u32[]{:S(2)}, u32[]{:S(2)}) %collective-permute-start.11) | collective-permute-done | bytes 4128 | tf_op jit(solution)/shard_map/ppermute | solution.py:427
  30.7 1.1 %collective-permute-start.15 = (bf16[16,128]{1,0:T(8,128)(2,1)S(1)}, bf16[16,128]{1,0:T(8,128)(2,1)S(1)}, u32[]{:S(2)}, u32[]{:S(2)}) collective-permute-start(bf16[16,128]{1,0:T(8,128)(2,1)S(1)} %shard_map.187.refs_0_), channel_id=1, source_target_pairs={{0,12},{1,13},{2,14},{3,15},{4,0},{5,1},{6,2},{7,3},{8,4},{9,5},{1... | collective-permute-start | bytes 12296 | tf_op jit(solution)/shard_map/ppermute | solution.py:427
  32.6 1.9 %collective-permute-start.13 = (bf16[16,128]{1,0:T(8,128)(2,1)S(1)}, bf16[16,128]{1,0:T(8,128)(2,1)S(1)}, u32[]{:S(2)}, u32[]{:S(2)}) collective-permute-start(bf16[16,128]{1,0:T(8,128)(2,1)S(1)} %shard_map.187.refs_0_), channel_id=1, source_target_pairs={{0,4},{1,5},{2,6},{3,7},{4,8},{5,9},{6,10},{7,11},{8,12},{9,13},{1... | collective-permute-start | bytes 12296 | tf_op jit(solution)/shard_map/ppermute | solution.py:427
  34.6 1.3 %shard_map.189 = (f32[64,512]{1,0:T(8,128)S(1)}, f32[64,128]{1,0:T(8,128)S(1)}) custom-call(bf16[64,8192]{1,0:T(8,128)(2,1)S(1)} %get-tuple-element.49.x_ref, bf16[8192,512]{1,0:T(8,128)(2,1)S(1)} %bitcast.15, bf16[64,8192]{1,0:T(8,128)(2,1)S(1)} %bitcast.19, bf16[64,8192]{1,0:T(8,128)(2,1)S(1)} %bitcast.21), custom_call_target="tpu_custom_call" | custom-call | flops 345000000 | tf_op jit(solution)/shard_map/pallas_call | solution.py:36
  36.3 1.7 %collective-permute-done.13.refs_1_ = bf16[16,128]{1,0:T(8,128)(2,1)S(1)} collective-permute-done((bf16[16,128]{1,0:T(8,128)(2,1)S(1)}, bf16[16,128]{1,0:T(8,128)(2,1)S(1)}, u32[]{:S(2)}, u32[]{:S(2)}) %collective-permute-start.13) | collective-permute-done | bytes 4128 | tf_op jit(solution)/shard_map/ppermute | solution.py:427
  38.0 0.8 %shard_map.190 = bf16[16,24,128]{2,1,0:T(8,128)(2,1)S(1)} custom-call(bf16[16,128]{1,0:T(8,128)(2,1)S(1)} %shard_map.187.refs_0_, bf16[16,128]{1,0:T(8,128)(2,1)S(1)} %collective-permute-done.13.refs_1_, bf16[16,128]{1,0:T(8,128)(2,1)S(1)} %collective-permute-done.14.refs_2_, bf16[16,128]{1,0:T(8,128)(2,1)S(1)} %collective-permute-done.15.refs_3_, ...), custom_call_target="tpu_custom_call" | custom-call | flops 1035000000 | tf_op jit(solution)/shard_map/pallas_call | solution.py:36
  38.9 10.0 %all_to_all.10.x_ref = bf16[16,24,128]{2,1,0:T(8,128)(2,1)S(1)} all-to-all(bf16[16,24,128]{2,1,0:T(8,128)(2,1)S(1)} %shard_map.190), channel_id=1, replica_groups=mesh['replica'=2,'serve'=16] {'serve'}, dimensions={0} | all-to-all | bytes 196608 | tf_op jit(solution)/shard_map/all_to_all | solution.py:533
  48.9 2.0 %shard_map.191 = (bf16[2,2,1024]{2,1,0:T(2,128)(2,1)}, bf16[2,2,1024]{2,1,0:T(2,128)(2,1)}, bf16[16,16,128]{2,1,0:T(8,128)(2,1)S(1)}) custom-call(s32[1]{0:T(128)} %bitcast.index_ref, s32[32]{0:T(128)S(1)} %copy-done.13, bf16[16,24,128]{2,1,0:T(8,128)(2,1)S(1)} %all_to_all.10.x_ref, bf16[256,384]{1,0:T(8,128)(2,1)S(1)} %get-tuple-element.63.order_ref, ...), custom_call_target="tpu_custom_call" | custom-call | flops 1150000000 | tf_op jit(solution)/shard_map/pallas_call | solution.py:36
  50.9 9.5 %all_to_all.11.ctx_ref = bf16[16,16,128]{2,1,0:T(8,128)(2,1)S(1)} all-to-all(bf16[16,16,128]{2,1,0:T(8,128)(2,1)S(1)} %get-tuple-element.64), channel_id=1, replica_groups=mesh['replica'=2,'serve'=16] {'serve'}, dimensions={0} | all-to-all | bytes 131072 | tf_op jit(solution)/shard_map/all_to_all | solution.py:544
  60.3 1.7 %shard_map.192 = (bf16[64,512]{1,0:T(8,128)(2,1)S(1)}, f32[32,5120]{1,0:T(8,128)S(1)}, f32[32,5120]{1,0:T(8,128)S(1)}) custom-call(bf16[16,16,128]{2,1,0:T(8,128)(2,1)S(1)} %all_to_all.11.ctx_ref, bf16[256,256]{1,0:T(8,128)(2,1)S(1)} %get-tuple-element.65.take_ref, bf16[512,8192]{1,0:T(8,128)(2,1)S(1)} %bitcast.17), custom_call_target="tpu_custom_call" | custom-call | flops 460000000 | tf_op jit(solution)/shard_map/pallas_call | solution.py:36
  62.1 0.9 %shard_map.193 = (f32[32,3072]{1,0:T(8,128)S(1)}, f32[32,3072]{1,0:T(8,128)S(1)}) custom-call(bf16[64,512]{1,0:T(8,128)(2,1)S(1)} %get-tuple-element.68.a_ref, bf16[512,8192]{1,0:T(8,128)(2,1)S(1)} %bitcast.17), custom_call_target="tpu_custom_call" | custom-call | flops 345000000 | tf_op jit(solution)/shard_map/pallas_call | solution.py:36
  63.6 1.3 %collective-permute-done.17.came2_ref = f32[32,3072]{1,0:T(8,128)S(1)} collective-permute-done((f32[32,3072]{1,0:T(8,128)S(1)}, f32[32,3072]{1,0:T(8,128)S(1)}, u32[]{:S(2)}, u32[]{:S(2)}) %collective-permute-start.17) | collective-permute-done | bytes 393248 | tf_op jit(solution)/shard_map/ppermute | solution.py:427
  65.3 1.9 %collective-permute-start.20 = (bf16[4,8192]{1,0:T(4,128)(2,1)S(1)}, bf16[4,8192]{1,0:T(4,128)(2,1)S(1)}, u32[]{:S(2)}, u32[]{:S(2)}) collective-permute-start(bf16[4,8192]{1,0:T(4,128)(2,1)S(1)} %get-tuple-element.73), channel_id=1, source_target_pairs={{0,2},{1,3},{2,0},{3,1},{4,6},{5,7},{6,4},{7,5},{8,10},{9,11},{10,... | collective-permute-start | bytes 196616 | tf_op jit(solution)/shard_map/ppermute | solution.py:427
  67.3 1.9 %collective-permute-start.24 = (bf16[4,8192]{1,0:T(4,128)(2,1)S(1)}, bf16[4,8192]{1,0:T(4,128)(2,1)S(1)}, u32[]{:S(2)}, u32[]{:S(2)}) collective-permute-start(bf16[4,8192]{1,0:T(4,128)(2,1)S(1)} %get-tuple-element.75), channel_id=1, source_target_pairs={{0,2},{1,3},{2,0},{3,1},{4,6},{5,7},{6,4},{7,5},{8,10},{9,11},{10,... | collective-permute-start | bytes 196616 | tf_op jit(solution)/shard_map/ppermute | solution.py:427
  69.2 0.9 %collective-permute-done.18.came_ref = bf16[4,8192]{1,0:T(4,128)(2,1)S(1)} collective-permute-done((bf16[4,8192]{1,0:T(4,128)(2,1)S(1)}, bf16[4,8192]{1,0:T(4,128)(2,1)S(1)}, u32[]{:S(2)}, u32[]{:S(2)}) %collective-permute-start.18) | collective-permute-done | bytes 65568 | tf_op jit(solution)/shard_map/ppermute | solution.py:427
  70.3 1.2 %collective-permute-done.20.came_ref = bf16[4,8192]{1,0:T(4,128)(2,1)S(1)} collective-permute-done((bf16[4,8192]{1,0:T(4,128)(2,1)S(1)}, bf16[4,8192]{1,0:T(4,128)(2,1)S(1)}, u32[]{:S(2)}, u32[]{:S(2)}) %collective-permute-start.20) | collective-permute-done | bytes 65568 | tf_op jit(solution)/shard_map/ppermute | solution.py:427
  71.8 1.1 %collective-permute-done.22.came_ref = bf16[4,8192]{1,0:T(4,128)(2,1)S(1)} collective-permute-done((bf16[4,8192]{1,0:T(4,128)(2,1)S(1)}, bf16[4,8192]{1,0:T(4,128)(2,1)S(1)}, u32[]{:S(2)}, u32[]{:S(2)}) %collective-permute-start.22) | collective-permute-done | bytes 65568 | tf_op jit(solution)/shard_map/ppermute | solution.py:427
  72.9 1.3 %collective-permute-start.23 = (bf16[4,8192]{1,0:T(4,128)(2,1)S(1)}, bf16[4,8192]{1,0:T(4,128)(2,1)S(1)}, u32[]{:S(2)}, u32[]{:S(2)}) collective-permute-start(bf16[4,8192]{1,0:T(4,128)(2,1)S(1)} %shard_map.197), channel_id=1, source_target_pairs={{0,12},{1,13},{2,14},{3,15},{4,0},{5,1},{6,2},{7,3},{8,4},{9,5},{1... | collective-permute-start | bytes 196616 | tf_op jit(solution)/shard_map/ppermute | solution.py:427
  74.2 2.7 %collective-permute-done.19.refs_0_ = bf16[4,8192]{1,0:T(4,128)(2,1)S(1)} collective-permute-done((bf16[4,8192]{1,0:T(4,128)(2,1)S(1)}, bf16[4,8192]{1,0:T(4,128)(2,1)S(1)}, u32[]{:S(2)}, u32[]{:S(2)}) %collective-permute-start.19) | collective-permute-done | bytes 65568 | tf_op jit(solution)/shard_map/ppermute | solution.py:427
  76.9 1.6 %collective-permute-done.21.refs_1_ = bf16[4,8192]{1,0:T(4,128)(2,1)S(1)} collective-permute-done((bf16[4,8192]{1,0:T(4,128)(2,1)S(1)}, bf16[4,8192]{1,0:T(4,128)(2,1)S(1)}, u32[]{:S(2)}, u32[]{:S(2)}) %collective-permute-start.21) | collective-permute-done | bytes 65568 | tf_op jit(solution)/shard_map/ppermute | solution.py:427
  (81 shorter events, 7.5 us)
Async XLA Ops:
  0.7 21.2 %copy-start.13 = (s32[32]{0:T(128)S(1)}, s32[32]{0:T(128)}, u32[]{:S(2)}) copy-start(s32[32]{0:T(128)} %len_ref.1) | copy-start | bytes 388
  0.7 21.2 %copy-start.12 = (s32[32]{0:T(128)S(1)}, s32[32]{0:T(128)}, u32[]{:S(2)}) copy-start(s32[32]{0:T(128)} %slot_hbm.1) | copy-start | bytes 388
  0.7 21.2 %copy-start.11 = (s32[32]{0:T(128)S(1)}, s32[32]{0:T(128)}, u32[]{:S(2)}) copy-start(s32[32]{0:T(128)} %adapter_hbm.1) | copy-start | bytes 388
  1.8 13.4 %collective-permute-start.3 = (bf16[1,4,8192]{2,1,0:T(4,128)(2,1)S(1)}, bf16[1,4,8192]{2,1,0:T(4,128)(2,1)S(1)}, u32[]{:S(2)}, u32[]{:S(2)}) collective-permute-start(bf16[1,4,8192]{2,1,0:T(4,128)(2,1)S(1)} %bitcast.24), channel_id=1, source_target_pairs={{0,2},{1,3},{2,0},{3,1},{4,6},{5,7},{6,4},{7,5},{8,10},{9,11},{10,... | collective-permute-start | bytes 196616 | tf_op jit(solution)/shard_map/ppermute | solution.py:427
  4.9 10.4 %collective-permute-start.2 = (bf16[1,4,8192]{2,1,0:T(4,128)(2,1)S(1)}, bf16[1,4,8192]{2,1,0:T(4,128)(2,1)S(1)}, u32[]{:S(2)}, u32[]{:S(2)}) collective-permute-start(bf16[1,4,8192]{2,1,0:T(4,128)(2,1)S(1)} %bitcast.25), channel_id=1, source_target_pairs={{0,12},{1,13},{2,14},{3,15},{4,0},{5,1},{6,2},{7,3},{8,4},{9,5},{1... | collective-permute-start | bytes 196616 | tf_op jit(solution)/shard_map/ppermute | solution.py:427
  8.5 6.7 %collective-permute-start.1 = (bf16[1,4,8192]{2,1,0:T(4,128)(2,1)S(1)}, bf16[1,4,8192]{2,1,0:T(4,128)(2,1)S(1)}, u32[]{:S(2)}, u32[]{:S(2)}) collective-permute-start(bf16[1,4,8192]{2,1,0:T(4,128)(2,1)S(1)} %bitcast.26), channel_id=1, source_target_pairs={{0,8},{1,9},{2,10},{3,11},{4,12},{5,13},{6,14},{7,15},{8,0},{9,1},... | collective-permute-start | bytes 196616 | tf_op jit(solution)/shard_map/ppermute | solution.py:427
  8.5 6.2 %collective-permute-start = (bf16[1,4,8192]{2,1,0:T(4,128)(2,1)S(1)}, bf16[1,4,8192]{2,1,0:T(4,128)(2,1)S(1)}, u32[]{:S(2)}, u32[]{:S(2)}) collective-permute-start(bf16[1,4,8192]{2,1,0:T(4,128)(2,1)S(1)} %bitcast.27), channel_id=1, source_target_pairs={{0,4},{1,5},{2,6},{3,7},{4,8},{5,9},{6,10},{7,11},{8,12},{9,13},{1... | collective-permute-start | bytes 196616 | tf_op jit(solution)/shard_map/ppermute | solution.py:427
  14.6 4.6 %collective-permute-start.4 = (bf16[1,4,8192]{2,1,0:T(4,128)(2,1)S(1)}, bf16[1,4,8192]{2,1,0:T(4,128)(2,1)S(1)}, u32[]{:S(2)}, u32[]{:S(2)}) collective-permute-start(bf16[1,4,8192]{2,1,0:T(4,128)(2,1)S(1)} %collective-permute-done), channel_id=1, source_target_pairs={{0,2},{1,3},{2,0},{3,1},{4,6},{5,7},{6,4},{7,5},{8,10},{9,11},{10,... | collective-permute-start | bytes 196616 | tf_op jit(solution)/shard_map/ppermute | solution.py:427
  15.3 9.9 %collective-permute-start.7 = (bf16[5,4,8192]{2,1,0:T(4,128)(2,1)S(1)}, bf16[5,4,8192]{2,1,0:T(4,128)(2,1)S(1)}, u32[]{:S(2)}, u32[]{:S(2)}) collective-permute-start(bf16[5,4,8192]{2,1,0:T(4,128)(2,1)S(1)} %constant_dynamic-update-slice_fusion.refs_0_), channel_id=1, source_target_pairs={{0,1},{1,0},{2,3},{3,2},{4,5},{5,4},{6,7},{7,6},{8,9},{9,8},{10,11... | collective-permute-start | bytes 983048 | tf_op jit(solution)/shard_map/ppermute | solution.py:427
  15.4 8.3 %collective-permute-start.6 = (bf16[1,4,8192]{2,1,0:T(4,128)(2,1)S(1)}, bf16[1,4,8192]{2,1,0:T(4,128)(2,1)S(1)}, u32[]{:S(2)}, u32[]{:S(2)}) collective-permute-start(bf16[1,4,8192]{2,1,0:T(4,128)(2,1)S(1)} %collective-permute-done.2), channel_id=1, source_target_pairs={{0,2},{1,3},{2,0},{3,1},{4,6},{5,7},{6,4},{7,5},{8,10},{9,11},{10,... | collective-permute-start | bytes 196616 | tf_op jit(solution)/shard_map/ppermute | solution.py:427
  17.0 4.7 %collective-permute-start.5 = (bf16[1,4,8192]{2,1,0:T(4,128)(2,1)S(1)}, bf16[1,4,8192]{2,1,0:T(4,128)(2,1)S(1)}, u32[]{:S(2)}, u32[]{:S(2)}) collective-permute-start(bf16[1,4,8192]{2,1,0:T(4,128)(2,1)S(1)} %collective-permute-done.1), channel_id=1, source_target_pairs={{0,2},{1,3},{2,0},{3,1},{4,6},{5,7},{6,4},{7,5},{8,10},{9,11},{10,... | collective-permute-start | bytes 196616 | tf_op jit(solution)/shard_map/ppermute | solution.py:427
  21.7 3.4 %collective-permute-start.8 = (bf16[2,4,8192]{2,1,0:T(4,128)(2,1)S(1)}, bf16[2,4,8192]{2,1,0:T(4,128)(2,1)S(1)}, u32[]{:S(2)}, u32[]{:S(2)}) collective-permute-start(bf16[2,4,8192]{2,1,0:T(4,128)(2,1)S(1)} %constant_dynamic-update-slice_fusion.5.refs_1_), channel_id=1, source_target_pairs={{0,1},{1,0},{2,3},{3,2},{4,5},{5,4},{6,7},{7,6},{8,9},{9,8},{10,11... | collective-permute-start | bytes 393224 | tf_op jit(solution)/shard_map/ppermute | solution.py:427
  23.7 1.4 %collective-permute-start.9 = (bf16[1,4,8192]{2,1,0:T(4,128)(2,1)S(1)}, bf16[1,4,8192]{2,1,0:T(4,128)(2,1)S(1)}, u32[]{:S(2)}, u32[]{:S(2)}) collective-permute-start(bf16[1,4,8192]{2,1,0:T(4,128)(2,1)S(1)} %collective-permute-done.6.refs_2_), channel_id=1, source_target_pairs={{0,1},{1,0},{2,3},{3,2},{4,5},{5,4},{6,7},{7,6},{8,9},{9,8},{10,11... | collective-permute-start | bytes 196616 | tf_op jit(solution)/shard_map/ppermute | solution.py:427
  25.9 3.4 %collective-permute-start.12 = (bf16[16,128]{1,0:T(8,128)(2,1)S(1)}, bf16[16,128]{1,0:T(8,128)(2,1)S(1)}, u32[]{:S(2)}, u32[]{:S(2)}) collective-permute-start(bf16[16,128]{1,0:T(8,128)(2,1)S(1)} %get-tuple-element.48.refs_0_), channel_id=1, source_target_pairs={{0,3},{1,2},{2,1},{3,0},{4,7},{5,6},{6,5},{7,4},{8,11},{9,10},{10,... | collective-permute-start | bytes 12296 | tf_op jit(solution)/shard_map/ppermute | solution.py:427
  27.1 3.6 %collective-permute-start.11 = (bf16[16,128]{1,0:T(8,128)(2,1)S(1)}, bf16[16,128]{1,0:T(8,128)(2,1)S(1)}, u32[]{:S(2)}, u32[]{:S(2)}) collective-permute-start(bf16[16,128]{1,0:T(8,128)(2,1)S(1)} %get-tuple-element.48.refs_0_), channel_id=1, source_target_pairs={{0,2},{1,3},{2,0},{3,1},{4,6},{5,7},{6,4},{7,5},{8,10},{9,11},{10,... | collective-permute-start | bytes 12296 | tf_op jit(solution)/shard_map/ppermute | solution.py:427
  27.9 2.7 %collective-permute-start.10 = (bf16[16,128]{1,0:T(8,128)(2,1)S(1)}, bf16[16,128]{1,0:T(8,128)(2,1)S(1)}, u32[]{:S(2)}, u32[]{:S(2)}) collective-permute-start(bf16[16,128]{1,0:T(8,128)(2,1)S(1)} %get-tuple-element.48.refs_0_), channel_id=1, source_target_pairs={{0,1},{1,0},{2,3},{3,2},{4,5},{5,4},{6,7},{7,6},{8,9},{9,8},{10,11... | collective-permute-start | bytes 12296 | tf_op jit(solution)/shard_map/ppermute | solution.py:427
  29.3 19.5 %copy-start.6 = (bf16[2,384,1024]{2,1,0:T(8,128)(2,1)S(1)}, bf16[2,384,1024]{2,1,0:T(8,128)(2,1)}, u32[]{:S(2)}) copy-start(bf16[2,384,1024]{2,1,0:T(8,128)(2,1)} %k_ref.1) | copy-start | bytes 4718596
  29.4 19.5 %copy-start.7 = (bf16[2,384,1024]{2,1,0:T(8,128)(2,1)S(1)}, bf16[2,384,1024]{2,1,0:T(8,128)(2,1)}, u32[]{:S(2)}) copy-start(bf16[2,384,1024]{2,1,0:T(8,128)(2,1)} %v_ref.1) | copy-start | bytes 4718596
  30.7 29.7 %slice-start.2 = ((s8[8388608]{0:T(1024)(128)(4,1)}), s8[4194304]{0:T(1024)(128)(4,1)S(1)}, s32[]{:S(2)}) async-start(s8[8388608]{0:T(1024)(128)(4,1)} %bitcast.16), calls=%async_computation.4 | async-start | bytes 8388608
  30.7 29.7 %slice-start.3 = ((s8[8388608]{0:T(1024)(128)(4,1)}), s8[4194304]{0:T(1024)(128)(4,1)S(1)}, s32[]{:S(2)}) async-start(s8[8388608]{0:T(1024)(128)(4,1)} %bitcast.16), calls=%async_computation.5 | async-start | bytes 8388608
  30.7 5.2 %collective-permute-start.15 = (bf16[16,128]{1,0:T(8,128)(2,1)S(1)}, bf16[16,128]{1,0:T(8,128)(2,1)S(1)}, u32[]{:S(2)}, u32[]{:S(2)}) collective-permute-start(bf16[16,128]{1,0:T(8,128)(2,1)S(1)} %shard_map.187.refs_0_), channel_id=1, source_target_pairs={{0,12},{1,13},{2,14},{3,15},{4,0},{5,1},{6,2},{7,3},{8,4},{9,5},{1... | collective-permute-start | bytes 12296 | tf_op jit(solution)/shard_map/ppermute | solution.py:427
  31.8 4.5 %collective-permute-start.14 = (bf16[16,128]{1,0:T(8,128)(2,1)S(1)}, bf16[16,128]{1,0:T(8,128)(2,1)S(1)}, u32[]{:S(2)}, u32[]{:S(2)}) collective-permute-start(bf16[16,128]{1,0:T(8,128)(2,1)S(1)} %shard_map.187.refs_0_), channel_id=1, source_target_pairs={{0,8},{1,9},{2,10},{3,11},{4,12},{5,13},{6,14},{7,15},{8,0},{9,1},... | collective-permute-start | bytes 12296 | tf_op jit(solution)/shard_map/ppermute | solution.py:427
  32.6 5.4 %collective-permute-start.13 = (bf16[16,128]{1,0:T(8,128)(2,1)S(1)}, bf16[16,128]{1,0:T(8,128)(2,1)S(1)}, u32[]{:S(2)}, u32[]{:S(2)}) collective-permute-start(bf16[16,128]{1,0:T(8,128)(2,1)S(1)} %shard_map.187.refs_0_), channel_id=1, source_target_pairs={{0,4},{1,5},{2,6},{3,7},{4,8},{5,9},{6,10},{7,11},{8,12},{9,13},{1... | collective-permute-start | bytes 12296 | tf_op jit(solution)/shard_map/ppermute | solution.py:427
  62.0 2.9 %collective-permute-start.16 = (f32[32,5120]{1,0:T(8,128)S(1)}, f32[32,5120]{1,0:T(8,128)S(1)}, u32[]{:S(2)}, u32[]{:S(2)}) collective-permute-start(f32[32,5120]{1,0:T(8,128)S(1)} %get-tuple-element.67), channel_id=1, source_target_pairs={{0,1},{1,0},{2,3},{3,2},{4,5},{5,4},{6,7},{7,6},{8,9},{9,8},{10,11... | collective-permute-start | bytes 1966088 | tf_op jit(solution)/shard_map/ppermute | solution.py:427
  63.0 1.9 %collective-permute-start.17 = (f32[32,3072]{1,0:T(8,128)S(1)}, f32[32,3072]{1,0:T(8,128)S(1)}, u32[]{:S(2)}, u32[]{:S(2)}) collective-permute-start(f32[32,3072]{1,0:T(8,128)S(1)} %get-tuple-element.70), channel_id=1, source_target_pairs={{0,1},{1,0},{2,3},{3,2},{4,5},{5,4},{6,7},{7,6},{8,9},{9,8},{10,11... | collective-permute-start | bytes 1179656 | tf_op jit(solution)/shard_map/ppermute | solution.py:427
  65.1 5.0 %collective-permute-start.18 = (bf16[4,8192]{1,0:T(4,128)(2,1)S(1)}, bf16[4,8192]{1,0:T(4,128)(2,1)S(1)}, u32[]{:S(2)}, u32[]{:S(2)}) collective-permute-start(bf16[4,8192]{1,0:T(4,128)(2,1)S(1)} %get-tuple-element.72), channel_id=1, source_target_pairs={{0,2},{1,3},{2,0},{3,1},{4,6},{5,7},{6,4},{7,5},{8,10},{9,11},{10,... | collective-permute-start | bytes 196616 | tf_op jit(solution)/shard_map/ppermute | solution.py:427
  65.3 6.2 %collective-permute-start.20 = (bf16[4,8192]{1,0:T(4,128)(2,1)S(1)}, bf16[4,8192]{1,0:T(4,128)(2,1)S(1)}, u32[]{:S(2)}, u32[]{:S(2)}) collective-permute-start(bf16[4,8192]{1,0:T(4,128)(2,1)S(1)} %get-tuple-element.73), channel_id=1, source_target_pairs={{0,2},{1,3},{2,0},{3,1},{4,6},{5,7},{6,4},{7,5},{8,10},{9,11},{10,... | collective-permute-start | bytes 196616 | tf_op jit(solution)/shard_map/ppermute | solution.py:427
  67.2 5.7 %collective-permute-start.22 = (bf16[4,8192]{1,0:T(4,128)(2,1)S(1)}, bf16[4,8192]{1,0:T(4,128)(2,1)S(1)}, u32[]{:S(2)}, u32[]{:S(2)}) collective-permute-start(bf16[4,8192]{1,0:T(4,128)(2,1)S(1)} %get-tuple-element.74), channel_id=1, source_target_pairs={{0,2},{1,3},{2,0},{3,1},{4,6},{5,7},{6,4},{7,5},{8,10},{9,11},{10,... | collective-permute-start | bytes 196616 | tf_op jit(solution)/shard_map/ppermute | solution.py:427
  67.3 6.9 %collective-permute-start.24 = (bf16[4,8192]{1,0:T(4,128)(2,1)S(1)}, bf16[4,8192]{1,0:T(4,128)(2,1)S(1)}, u32[]{:S(2)}, u32[]{:S(2)}) collective-permute-start(bf16[4,8192]{1,0:T(4,128)(2,1)S(1)} %get-tuple-element.75), channel_id=1, source_target_pairs={{0,2},{1,3},{2,0},{3,1},{4,6},{5,7},{6,4},{7,5},{8,10},{9,11},{10,... | collective-permute-start | bytes 196616 | tf_op jit(solution)/shard_map/ppermute | solution.py:427
  70.1 6.8 %collective-permute-start.19 = (bf16[4,8192]{1,0:T(4,128)(2,1)S(1)}, bf16[4,8192]{1,0:T(4,128)(2,1)S(1)}, u32[]{:S(2)}, u32[]{:S(2)}) collective-permute-start(bf16[4,8192]{1,0:T(4,128)(2,1)S(1)} %shard_map.195), channel_id=1, source_target_pairs={{0,4},{1,5},{2,6},{3,7},{4,8},{5,9},{6,10},{7,11},{8,12},{9,13},{1... | collective-permute-start | bytes 196616 | tf_op jit(solution)/shard_map/ppermute | solution.py:427
  71.5 7.0 %collective-permute-start.21 = (bf16[4,8192]{1,0:T(4,128)(2,1)S(1)}, bf16[4,8192]{1,0:T(4,128)(2,1)S(1)}, u32[]{:S(2)}, u32[]{:S(2)}) collective-permute-start(bf16[4,8192]{1,0:T(4,128)(2,1)S(1)} %shard_map.196), channel_id=1, source_target_pairs={{0,8},{1,9},{2,10},{3,11},{4,12},{5,13},{6,14},{7,15},{8,0},{9,1},... | collective-permute-start | bytes 196616 | tf_op jit(solution)/shard_map/ppermute | solution.py:427
  72.9 5.6 %collective-permute-start.23 = (bf16[4,8192]{1,0:T(4,128)(2,1)S(1)}, bf16[4,8192]{1,0:T(4,128)(2,1)S(1)}, u32[]{:S(2)}, u32[]{:S(2)}) collective-permute-start(bf16[4,8192]{1,0:T(4,128)(2,1)S(1)} %shard_map.197), channel_id=1, source_target_pairs={{0,12},{1,13},{2,14},{3,15},{4,0},{5,1},{6,2},{7,3},{8,4},{9,5},{1... | collective-permute-start | bytes 196616 | tf_op jit(solution)/shard_map/ppermute | solution.py:427
  (11 other events, 57.2 us)

commit v11 on v8

--- a/solution.py
+++ b/solution.py
@@ -125,7 +125,10 @@
     for j in range(slot_ref.shape[0]):
         slot = jnp.where(adapter == j, slot_ref[j], slot)
     held_ref[...] = slot
-    local_ref[...] = slot - index * adapters
+    shared = cores * adapters
+    place = slot - index // cores * shared
+    turned_place = (place - core_at * adapters + shared) % shared
+    local_ref[...] = jnp.where((place >= 0) & (place < shared), turned_place, -1)
     position = (length + step).astype(F32)
     lane = iota((1, HEAD), 1)
     odd = jnp.where(lane % 2 == 0, -1.0, 1.0)
@@ -166,7 +169,8 @@
 
 
 def low_body(rank, groups, *refs):
-    parts, (qd_ref, vd_ref, local_ref, place_ref, x_ref, out_ref) = refs[:groups], refs[groups:]
+    parts, refs = refs[:groups], refs[groups:]
+    *map_refs, local_ref, place_ref, x_ref, out_ref = refs
     rows = parts[0].shape[1]
     sets = max(1, 16 // rows)
     blocks = [(part, i) for part in parts for i in range(part.shape[0])]
@@ -177,8 +181,8 @@
             block = [part[i, :, lanes].astype(F32) for part, i in group]
             block = jnp.concatenate(block, axis=0).astype(BF16)
             x_ref[first * rows : (first + sets) * rows, lanes] = block
-    adapters = qd_ref.shape[0] // rank
-    maps = jnp.concatenate((qd_ref[...], vd_ref[...]), axis=0)
+    maps = jnp.concatenate([ref[...] for ref in map_refs], axis=0)
+    adapters = maps.shape[0] // (2 * rank)
     low = dot_nt(x_ref[...], maps)
     lane = lax.broadcasted_iota(jnp.int32, low.shape, 1)
     low = jnp.where(lane // rank % adapters == local_ref[...], low, 0.0)
@@ -301,10 +305,15 @@
     for b in range(own):
         q = queries[b * KV_HEADS * mine : (b + 1) * KV_HEADS * mine]
         cached, newer = [], []
-        for g in range(KV_HEADS):
-            qg = q[g * mine : (g + 1) * mine]
-            cached.append(dot_nt(qg, k_ref[b, :, g * HEAD : (g + 1) * HEAD]))
-            newer.append(dot_nt(qg, keys[g]))
+        for g in range(0, KV_HEADS, 2):
+            one, two = q[g * mine : (g + 1) * mine], q[(g + 1) * mine : (g + 2) * mine]
+            none = jnp.zeros_like(one)
+            pair = jnp.concatenate(
+                (jnp.concatenate((one, none), axis=1), jnp.concatenate((none, two), axis=1)),
+                axis=0,
+            )
+            cached.append(dot_nt(pair, k_ref[b, :, g * HEAD : (g + 2) * HEAD]))
+            newer.append(dot_nt(pair, jnp.concatenate(keys[g : g + 2], axis=1)))
         cached = jnp.concatenate(cached, axis=0) * scale
         newer = jnp.concatenate(newer, axis=0) * scale
         place = lax.broadcasted_iota(jnp.int32, cached.shape, 1)
@@ -320,12 +329,13 @@
         total = jnp.sum(cached, axis=1, keepdims=True) + jnp.sum(newer, axis=1, keepdims=True)
         cached = (cached / total).astype(BF16)
         newer = (newer / total).astype(BF16)
-        for g in range(KV_HEADS):
-            at_rows = slice(g * mine, (g + 1) * mine)
-            part = dot(cached[at_rows], v_ref[b, :, g * HEAD : (g + 1) * HEAD])
-            s_ref[(b * KV_HEADS + g) * mine : (b * KV_HEADS + g + 1) * mine] = part + dot(
-                newer[at_rows], values[g]
-            )
+        for g in range(0, KV_HEADS, 2):
+            at_rows = slice(g * mine, (g + 2) * mine)
+            part = dot(cached[at_rows], v_ref[b, :, g * HEAD : (g + 2) * HEAD])
+            part = part + dot(newer[at_rows], jnp.concatenate(values[g : g + 2], axis=1))
+            at = (b * KV_HEADS + g) * mine
+            s_ref[at : at + mine] = part[:mine, :HEAD]
+            s_ref[at + mine : at + 2 * mine] = part[mine:, HEAD:]
     step = local * STEPS
     half = KV_HEADS * mine
     for i in range(n):
@@ -461,6 +471,9 @@
     rest = jnp.concatenate(fars)
     groups = [jnp.concatenate([normed, *fars, *nears[:1]])]
     groups += [shift(rest, 0, m, 0) for m in range(1, near)]
+    query_down = jnp.swapaxes(query_down_weights, 1, 2).reshape(adapters * rank, width)
+    value_down = jnp.swapaxes(value_down_weights, 1, 2).reshape(adapters * rank, width)
+    query_down, value_down, rest = lax.optimization_barrier((query_down, value_down, rest))
 
     rest, at = lax.optimization_barrier((rest, index[None]))
     sent = -(-(rows * local + rows) // 8) * 8
@@ -497,8 +510,6 @@
 
     groups += [shift(part, 0, 0, c) for c in range(1, cores) for part in groups[:near]]
 
-    query_down = jnp.swapaxes(query_down_weights, 1, 2).reshape(adapters * rank, width)
-    value_down = jnp.swapaxes(value_down_weights, 1, 2).reshape(adapters * rank, width)
     packed_rows = all_rows * 2 * rank // HEAD
     x, low = whole_call(
         functools.partial(low_body, rank, len(groups)),
@@ -506,7 +517,13 @@
             jax.ShapeDtypeStruct((all_rows, width), BF16),
             jax.ShapeDtypeStruct((packed_rows, HEAD), BF16),
         ),
-        (*groups, query_down, value_down, near_slot, place),
+        (
+            *groups,
+            *[query_down, *[shift(query_down, 0, 0, c) for c in range(1, cores)]],
+            *[value_down, *[shift(value_down, 0, 0, c) for c in range(1, cores)]],
+            near_slot,
+            place,
+        ),
         cost=0.3,
     )
     def base(start, stop):
@@ -520,7 +537,7 @@
             cost=0.3,
         )
 
-    lows = [shift(low, 0, m, c) for m in range(near) for c in range(cores) if m + c]
+    lows = [shift(low, 0, m, 0) for m in range(1, near)]
     base_q, base_kv = base(0, width // 2)
     low = whole_call(join_body, jax.ShapeDtypeStruct(low.shape, BF16), (low, *lows), cost=0.1)
     low, base_q = lax.optimization_barrier((low, base_q))
@@ -559,7 +576,7 @@
     context = lax.all_to_all(context, "serve", split_axis=0, concat_axis=0, tiled=True)
 
     half = all_rows // cores
-    cut = width * 5 // 8
+    cut = width // 2
 
     def kinds(count, columns):
         return (jax.ShapeDtypeStruct((count, columns), F32),) * 2

time: 76.2 us -> 79.2 us (1.039)
  waiting for transfers between devices: 18.3 us -> 22 us
  starting transfers between devices: 24 us -> 23 us
    ppermute x23, waiting for transfers between devices: 18.3 us -> 22 us  [shift(): return lax.ppermute(value, 'serve', partner(f, m, c))]
    ppermute x23, starting transfers between devices: 24 us -> 23 us  [shift(): return lax.ppermute(value, 'serve', partner(f, m, c))]
  transfers between devices with their start and end apart: 23 -> 23, of which waited for: 10 -> 13; matrix products, arithmetic and copies ran while one was open for 0% -> 0% of each run, Pallas kernels for 7% -> 7%
where the time goes in v11:
time: 79.2 us; the launch traced here: 78.9 us
  starting transfers between devices  23 us (29%)
  waiting for transfers between devices  22 us (28%)
  blocking collectives  19.5 us (25%)
  Pallas kernels  12.5 us (16%)
  local copies, waits for them, and re-layouts  1 us (1%)
  between operations  0.91 us (1%)
    ppermute x23, starting transfers between devices, shift(): return lax.ppermute(value, 'serve', partner(f, m, c))  23 us
    ppermute x23, waiting for transfers between devices, shift(): return lax.ppermute(value, 'serve', partner(f, m, c))  22 us
    pallas_call x16, Pallas kernels, whole_call(): pl.pallas_call(body, out_shape=out_shape, in_specs=specs, out_specs=tuple...  12.5 us
    all_to_all x1, blocking collectives, shards(): lax.all_to_all(ready, 'serve', split_axis=0, concat_axis=0, tiled=True)  9.99 us
    all_to_all x1, blocking collectives, shards(): lax.all_to_all(context, 'serve', split_axis=0, concat_axis=0, tiled=True)  9.47 us
  transfers between devices with their start and end apart: 23, of which 13 were waited for; matrix products, arithmetic and copies ran while one was open for 0% of the time, Pallas kernels for 7%

profile of v11, /device:TPU:0, one launch (start us, length us, event | category | flops | bytes accessed | tf_op | source)
XLA Modules:
  0.0 78.9 jit_solution(14377204886342354523)
XLA Ops:
  1.8 3.0 %collective-permute-start.3 = (bf16[1,4,8192]{2,1,0:T(4,128)(2,1)S(1)}, bf16[1,4,8192]{2,1,0:T(4,128)(2,1)S(1)}, u32[]{:S(2)}, u32[]{:S(2)}) collective-permute-start(bf16[1,4,8192]{2,1,0:T(4,128)(2,1)S(1)} %bitcast.26), channel_id=1, source_target_pairs={{0,2},{1,3},{2,0},{3,1},{4,6},{5,7},{6,4},{7,5},{8,10},{9,11},{10,... | collective-permute-start | bytes 196616 | tf_op jit(solution)/shard_map/ppermute | solution.py:450
  4.9 3.6 %collective-permute-start.2 = (bf16[1,4,8192]{2,1,0:T(4,128)(2,1)S(1)}, bf16[1,4,8192]{2,1,0:T(4,128)(2,1)S(1)}, u32[]{:S(2)}, u32[]{:S(2)}) collective-permute-start(bf16[1,4,8192]{2,1,0:T(4,128)(2,1)S(1)} %bitcast.27), channel_id=1, source_target_pairs={{0,12},{1,13},{2,14},{3,15},{4,0},{5,1},{6,2},{7,3},{8,4},{9,5},{1... | collective-permute-start | bytes 196616 | tf_op jit(solution)/shard_map/ppermute | solution.py:450
  8.5 1.0 %collective-permute-start = (bf16[1,4,8192]{2,1,0:T(4,128)(2,1)S(1)}, bf16[1,4,8192]{2,1,0:T(4,128)(2,1)S(1)}, u32[]{:S(2)}, u32[]{:S(2)}) collective-permute-start(bf16[1,4,8192]{2,1,0:T(4,128)(2,1)S(1)} %bitcast.29), channel_id=1, source_target_pairs={{0,4},{1,5},{2,6},{3,7},{4,8},{5,9},{6,10},{7,11},{8,12},{9,13},{1... | collective-permute-start | bytes 196616 | tf_op jit(solution)/shard_map/ppermute | solution.py:450
  9.5 5.1 %collective-permute-done = bf16[1,4,8192]{2,1,0:T(4,128)(2,1)S(1)} collective-permute-done((bf16[1,4,8192]{2,1,0:T(4,128)(2,1)S(1)}, bf16[1,4,8192]{2,1,0:T(4,128)(2,1)S(1)}, u32[]{:S(2)}, u32[]{:S(2)}) %collective-permute-start) | collective-permute-done | bytes 65568 | tf_op jit(solution)/shard_map/ppermute | solution.py:450
  16.1 1.8 %shard_map.185 = (s32[64,1]{1,0:T(8,128)S(1)}, s32[64,1]{1,0:T(8,128)S(1)}, f32[64,128]{1,0:T(8,128)S(1)}, f32[64,128]{1,0:T(8,128)S(1)}, f32[64,128]{1,0:T(8,12...) custom-call(s32[1]{0:T(128)} %bitcast.index_ref, ...), custom_call_target="tpu_custom_call" | custom-call | flops 4600000000 | tf_op jit(solution)/shard_map/pallas_call | solution.py:36
  18.0 2.7 %collective-permute-done.4.refs_1_ = bf16[3,4,8192]{2,1,0:T(4,128)(2,1)S(1)} collective-permute-done((bf16[3,4,8192]{2,1,0:T(4,128)(2,1)S(1)}, bf16[3,4,8192]{2,1,0:T(4,128)(2,1)S(1)}, u32[]{:S(2)}, u32[]{:S(2)}) %collective-permute-start.4) | collective-permute-done | bytes 196640 | tf_op jit(solution)/shard_map/ppermute | solution.py:450
  20.6 1.4 %collective-permute-done.6.refs_3_ = bf16[3,4,8192]{2,1,0:T(4,128)(2,1)S(1)} collective-permute-done((bf16[3,4,8192]{2,1,0:T(4,128)(2,1)S(1)}, bf16[3,4,8192]{2,1,0:T(4,128)(2,1)S(1)}, u32[]{:S(2)}, u32[]{:S(2)}) %collective-permute-start.6) | collective-permute-done | bytes 196640 | tf_op jit(solution)/shard_map/ppermute | solution.py:450
  22.1 1.1 %shard_map.186 = (bf16[64,8192]{1,0:T(8,128)(2,1)S(1)}, bf16[16,128]{1,0:T(8,128)(2,1)S(1)}) custom-call(bf16[5,4,8192]{2,1,0:T(4,128)(2,1)S(1)} %constant_dynamic-update-slice_fusion.refs_0_, bf16[3,4,8192]{2,1,0:T(4,128)(2,1)S(1)} %collective-permute-done.4.refs_1_, bf16[5,4,8192]{2,1,0:T(4,128)(2,1)S(1)} %collective-permute-done.5.refs_2_, ...), custom_call_target="tpu_custom_call" | custom-call | flops 345000000 | tf_op jit(solution)/shard_map/pallas_call | solution.py:36
  23.8 1.3 %shard_map.188 = (f32[64,512]{1,0:T(8,128)S(1)}, f32[64,128]{1,0:T(8,128)S(1)}) custom-call(bf16[64,8192]{1,0:T(8,128)(2,1)S(1)} %get-tuple-element.60.x_ref, bf16[8192,512]{1,0:T(8,128)(2,1)S(1)} %bitcast.15, bf16[64,8192]{1,0:T(8,128)(2,1)S(1)} %bitcast.18, bf16[64,8192]{1,0:T(8,128)(2,1)S(1)} %bitcast.20), custom_call_target="tpu_custom_call" | custom-call | flops 345000000 | tf_op jit(solution)/shard_map/pallas_call | solution.py:36
  25.2 1.7 %collective-permute-done.9.refs_1_ = bf16[16,128]{1,0:T(8,128)(2,1)S(1)} collective-permute-done((bf16[16,128]{1,0:T(8,128)(2,1)S(1)}, bf16[16,128]{1,0:T(8,128)(2,1)S(1)}, u32[]{:S(2)}, u32[]{:S(2)}) %collective-permute-start.9) | collective-permute-done | bytes 4128 | tf_op jit(solution)/shard_map/ppermute | solution.py:450
  26.9 1.8 %collective-permute-start.12 = (bf16[16,128]{1,0:T(8,128)(2,1)S(1)}, bf16[16,128]{1,0:T(8,128)(2,1)S(1)}, u32[]{:S(2)}, u32[]{:S(2)}) collective-permute-start(bf16[16,128]{1,0:T(8,128)(2,1)S(1)} %shard_map.187.refs_0_), channel_id=1, source_target_pairs={{0,12},{1,13},{2,14},{3,15},{4,0},{5,1},{6,2},{7,3},{8,4},{9,5},{1... | collective-permute-start | bytes 12296 | tf_op jit(solution)/shard_map/ppermute | solution.py:450
  29.3 1.9 %collective-permute-start.10 = (bf16[16,128]{1,0:T(8,128)(2,1)S(1)}, bf16[16,128]{1,0:T(8,128)(2,1)S(1)}, u32[]{:S(2)}, u32[]{:S(2)}) collective-permute-start(bf16[16,128]{1,0:T(8,128)(2,1)S(1)} %shard_map.187.refs_0_), channel_id=1, source_target_pairs={{0,4},{1,5},{2,6},{3,7},{4,8},{5,9},{6,10},{7,11},{8,12},{9,13},{1... | collective-permute-start | bytes 12296 | tf_op jit(solution)/shard_map/ppermute | solution.py:450
  31.3 1.3 %shard_map.189 = (f32[64,512]{1,0:T(8,128)S(1)}, f32[64,128]{1,0:T(8,128)S(1)}) custom-call(bf16[64,8192]{1,0:T(8,128)(2,1)S(1)} %get-tuple-element.60.x_ref, bf16[8192,512]{1,0:T(8,128)(2,1)S(1)} %bitcast.15, bf16[64,8192]{1,0:T(8,128)(2,1)S(1)} %bitcast.19, bf16[64,8192]{1,0:T(8,128)(2,1)S(1)} %bitcast.21), custom_call_target="tpu_custom_call" | custom-call | flops 345000000 | tf_op jit(solution)/shard_map/pallas_call | solution.py:36
  33.2 1.5 %collective-permute-done.10.refs_1_ = bf16[16,128]{1,0:T(8,128)(2,1)S(1)} collective-permute-done((bf16[16,128]{1,0:T(8,128)(2,1)S(1)}, bf16[16,128]{1,0:T(8,128)(2,1)S(1)}, u32[]{:S(2)}, u32[]{:S(2)}) %collective-permute-start.10) | collective-permute-done | bytes 4128 | tf_op jit(solution)/shard_map/ppermute | solution.py:450
  34.7 0.8 %shard_map.190 = bf16[16,24,128]{2,1,0:T(8,128)(2,1)S(1)} custom-call(bf16[16,128]{1,0:T(8,128)(2,1)S(1)} %shard_map.187.refs_0_, bf16[16,128]{1,0:T(8,128)(2,1)S(1)} %collective-permute-done.10.refs_1_, bf16[16,128]{1,0:T(8,128)(2,1)S(1)} %collective-permute-done.11.refs_2_, bf16[16,128]{1,0:T(8,128)(2,1)S(1)} %collective-permute-done.12.refs_3_, ...), custom_call_target="tpu_custom_call" | custom-call | flops 1035000000 | tf_op jit(solution)/shard_map/pallas_call | solution.py:36
  35.6 10.0 %all_to_all.10.x_ref = bf16[16,24,128]{2,1,0:T(8,128)(2,1)S(1)} all-to-all(bf16[16,24,128]{2,1,0:T(8,128)(2,1)S(1)} %shard_map.190), channel_id=1, replica_groups=mesh['replica'=2,'serve'=16] {'serve'}, dimensions={0} | all-to-all | bytes 196608 | tf_op jit(solution)/shard_map/all_to_all | solution.py:565
  45.6 2.1 %shard_map.191 = (bf16[2,2,1024]{2,1,0:T(2,128)(2,1)}, bf16[2,2,1024]{2,1,0:T(2,128)(2,1)}, bf16[16,16,128]{2,1,0:T(8,128)(2,1)S(1)}) custom-call(s32[1]{0:T(128)} %bitcast.index_ref, s32[32]{0:T(128)S(1)} %copy-done.13, bf16[16,24,128]{2,1,0:T(8,128)(2,1)S(1)} %all_to_all.10.x_ref, bf16[256,384]{1,0:T(8,128)(2,1)S(1)} %get-tuple-element.74.order_ref, ...), custom_call_target="tpu_custom_call" | custom-call | flops 1150000000 | tf_op jit(solution)/shard_map/pallas_call | solution.py:36
  47.7 9.5 %all_to_all.11.ctx_ref = bf16[16,16,128]{2,1,0:T(8,128)(2,1)S(1)} all-to-all(bf16[16,16,128]{2,1,0:T(8,128)(2,1)S(1)} %get-tuple-element.75), channel_id=1, replica_groups=mesh['replica'=2,'serve'=16] {'serve'}, dimensions={0} | all-to-all | bytes 131072 | tf_op jit(solution)/shard_map/all_to_all | solution.py:576
  57.2 1.4 %shard_map.192 = (bf16[64,512]{1,0:T(8,128)(2,1)S(1)}, f32[32,4096]{1,0:T(8,128)S(1)}, f32[32,4096]{1,0:T(8,128)S(1)}) custom-call(bf16[16,16,128]{2,1,0:T(8,128)(2,1)S(1)} %all_to_all.11.ctx_ref, bf16[256,256]{1,0:T(8,128)(2,1)S(1)} %get-tuple-element.76.take_ref, bf16[512,8192]{1,0:T(8,128)(2,1)S(1)} %bitcast.17), custom_call_target="tpu_custom_call" | custom-call | flops 460000000 | tf_op jit(solution)/shard_map/pallas_call | solution.py:36
  58.6 1.2 %shard_map.195 = (f32[32,4096]{1,0:T(8,128)S(1)}, f32[32,4096]{1,0:T(8,128)S(1)}) custom-call(bf16[64,512]{1,0:T(8,128)(2,1)S(1)} %get-tuple-element.85.a_ref, bf16[512,8192]{1,0:T(8,128)(2,1)S(1)} %bitcast.17), custom_call_target="tpu_custom_call" | custom-call | flops 345000000 | tf_op jit(solution)/shard_map/pallas_call | solution.py:36
  60.7 1.2 %collective-permute-done.18.came_ref = f32[32,4096]{1,0:T(8,128)S(1)} collective-permute-done((f32[32,4096]{1,0:T(8,128)S(1)}, f32[32,4096]{1,0:T(8,128)S(1)}, u32[]{:S(2)}, u32[]{:S(2)}) %collective-permute-start.18) | collective-permute-done | bytes 524320 | tf_op jit(solution)/shard_map/ppermute | solution.py:450
  62.2 0.9 %collective-permute-start.20 = (bf16[8,4096]{1,0:T(8,128)(2,1)S(1)}, bf16[8,4096]{1,0:T(8,128)(2,1)S(1)}, u32[]{:S(2)}, u32[]{:S(2)}) collective-permute-start(bf16[8,4096]{1,0:T(8,128)(2,1)S(1)} %get-tuple-element.90), channel_id=1, source_target_pairs={{0,8},{1,9},{2,10},{3,11},{4,12},{5,13},{6,14},{7,15},{8,0},{9,1},... | collective-permute-start | bytes 196616 | tf_op jit(solution)/shard_map/ppermute | solution.py:450
  63.1 2.8 %collective-permute-start.21 = (bf16[8,4096]{1,0:T(8,128)(2,1)S(1)}, bf16[8,4096]{1,0:T(8,128)(2,1)S(1)}, u32[]{:S(2)}, u32[]{:S(2)}) collective-permute-start(bf16[8,4096]{1,0:T(8,128)(2,1)S(1)} %get-tuple-element.91), channel_id=1, source_target_pairs={{0,12},{1,13},{2,14},{3,15},{4,0},{5,1},{6,2},{7,3},{8,4},{9,5},{1... | collective-permute-start | bytes 196616 | tf_op jit(solution)/shard_map/ppermute | solution.py:450
  65.9 3.0 %collective-permute-done.19.refs_1_ = bf16[8,4096]{1,0:T(8,128)(2,1)S(1)} collective-permute-done((bf16[8,4096]{1,0:T(8,128)(2,1)S(1)}, bf16[8,4096]{1,0:T(8,128)(2,1)S(1)}, u32[]{:S(2)}, u32[]{:S(2)}) %collective-permute-start.19) | collective-permute-done | bytes 65568 | tf_op jit(solution)/shard_map/ppermute | solution.py:450
  68.9 1.8 %collective-permute-done.20.refs_2_ = bf16[8,4096]{1,0:T(8,128)(2,1)S(1)} collective-permute-done((bf16[8,4096]{1,0:T(8,128)(2,1)S(1)}, bf16[8,4096]{1,0:T(8,128)(2,1)S(1)}, u32[]{:S(2)}, u32[]{:S(2)}) %collective-permute-start.20) | collective-permute-done | bytes 65568 | tf_op jit(solution)/shard_map/ppermute | solution.py:450
  70.7 0.6 collective-permute-start.22
  71.4 1.4 %collective-permute-start.15 = (bf16[4,4096]{1,0:T(4,128)(2,1)S(1)}, bf16[4,4096]{1,0:T(4,128)(2,1)S(1)}, u32[]{:S(2)}, u32[]{:S(2)}) collective-permute-start(bf16[4,4096]{1,0:T(4,128)(2,1)S(1)} %get-tuple-element.82), channel_id=1, source_target_pairs={{0,4},{1,5},{2,6},{3,7},{4,8},{5,9},{6,10},{7,11},{8,12},{9,13},{1... | collective-permute-start | bytes 98312 | tf_op jit(solution)/shard_map/ppermute | solution.py:450
  72.8 1.2 %collective-permute-start.16 = (bf16[4,4096]{1,0:T(4,128)(2,1)S(1)}, bf16[4,4096]{1,0:T(4,128)(2,1)S(1)}, u32[]{:S(2)}, u32[]{:S(2)}) collective-permute-start(bf16[4,4096]{1,0:T(4,128)(2,1)S(1)} %get-tuple-element.83), channel_id=1, source_target_pairs={{0,8},{1,9},{2,10},{3,11},{4,12},{5,13},{6,14},{7,15},{8,0},{9,1},... | collective-permute-start | bytes 98312 | tf_op jit(solution)/shard_map/ppermute | solution.py:450
  74.0 1.3 %collective-permute-start.17 = (bf16[4,4096]{1,0:T(4,128)(2,1)S(1)}, bf16[4,4096]{1,0:T(4,128)(2,1)S(1)}, u32[]{:S(2)}, u32[]{:S(2)}) collective-permute-start(bf16[4,4096]{1,0:T(4,128)(2,1)S(1)} %get-tuple-element.84), channel_id=1, source_target_pairs={{0,12},{1,13},{2,14},{3,15},{4,0},{5,1},{6,2},{7,3},{8,4},{9,5},{1... | collective-permute-start | bytes 98312 | tf_op jit(solution)/shard_map/ppermute | solution.py:450
  75.3 1.9 %collective-permute-done.15.refs_1_ = bf16[4,4096]{1,0:T(4,128)(2,1)S(1)} collective-permute-done((bf16[4,4096]{1,0:T(4,128)(2,1)S(1)}, bf16[4,4096]{1,0:T(4,128)(2,1)S(1)}, u32[]{:S(2)}, u32[]{:S(2)}) %collective-permute-start.15) | collective-permute-done | bytes 32800 | tf_op jit(solution)/shard_map/ppermute | solution.py:450
  77.2 0.8 %collective-permute-done.16.refs_2_ = bf16[4,4096]{1,0:T(4,128)(2,1)S(1)} collective-permute-done((bf16[4,4096]{1,0:T(4,128)(2,1)S(1)}, bf16[4,4096]{1,0:T(4,128)(2,1)S(1)}, u32[]{:S(2)}, u32[]{:S(2)}) %collective-permute-start.16) | collective-permute-done | bytes 32800 | tf_op jit(solution)/shard_map/ppermute | solution.py:450
  78.2 0.7 shard_map.198
  (75 shorter events, 5.9 us)
Async XLA Ops:
  0.7 15.4 %copy-start.3 = (bf16[2,8192,16]{1,2,0:T(8,128)(2,1)S(1)}, bf16[2,8192,16]{1,2,0:T(8,128)(2,1)}, u32[]{:S(2)}) copy-start(bf16[2,8192,16]{1,2,0:T(8,128)(2,1)} %param.24) | copy-start | bytes 1572868
  0.7 14.9 %copy-start.2 = (bf16[2,8192,16]{1,2,0:T(8,128)(2,1)S(1)}, bf16[2,8192,16]{1,2,0:T(8,128)(2,1)}, u32[]{:S(2)}) copy-start(bf16[2,8192,16]{1,2,0:T(8,128)(2,1)} %param.23) | copy-start | bytes 1572868
  0.7 15.5 %copy-start.13 = (s32[32]{0:T(128)S(1)}, s32[32]{0:T(128)}, u32[]{:S(2)}) copy-start(s32[32]{0:T(128)} %len_ref.1) | copy-start | bytes 388
  0.7 15.4 %copy-start.12 = (s32[32]{0:T(128)S(1)}, s32[32]{0:T(128)}, u32[]{:S(2)}) copy-start(s32[32]{0:T(128)} %slot_hbm.1) | copy-start | bytes 388
  0.7 15.4 %copy-start.11 = (s32[32]{0:T(128)S(1)}, s32[32]{0:T(128)}, u32[]{:S(2)}) copy-start(s32[32]{0:T(128)} %adapter_hbm.1) | copy-start | bytes 388
  1.8 13.6 %collective-permute-start.3 = (bf16[1,4,8192]{2,1,0:T(4,128)(2,1)S(1)}, bf16[1,4,8192]{2,1,0:T(4,128)(2,1)S(1)}, u32[]{:S(2)}, u32[]{:S(2)}) collective-permute-start(bf16[1,4,8192]{2,1,0:T(4,128)(2,1)S(1)} %bitcast.26), channel_id=1, source_target_pairs={{0,2},{1,3},{2,0},{3,1},{4,6},{5,7},{6,4},{7,5},{8,10},{9,11},{10,... | collective-permute-start | bytes 196616 | tf_op jit(solution)/shard_map/ppermute | solution.py:450
  4.9 9.9 %collective-permute-start.2 = (bf16[1,4,8192]{2,1,0:T(4,128)(2,1)S(1)}, bf16[1,4,8192]{2,1,0:T(4,128)(2,1)S(1)}, u32[]{:S(2)}, u32[]{:S(2)}) collective-permute-start(bf16[1,4,8192]{2,1,0:T(4,128)(2,1)S(1)} %bitcast.27), channel_id=1, source_target_pairs={{0,12},{1,13},{2,14},{3,15},{4,0},{5,1},{6,2},{7,3},{8,4},{9,5},{1... | collective-permute-start | bytes 196616 | tf_op jit(solution)/shard_map/ppermute | solution.py:450
  8.5 6.2 %collective-permute-start.1 = (bf16[1,4,8192]{2,1,0:T(4,128)(2,1)S(1)}, bf16[1,4,8192]{2,1,0:T(4,128)(2,1)S(1)}, u32[]{:S(2)}, u32[]{:S(2)}) collective-permute-start(bf16[1,4,8192]{2,1,0:T(4,128)(2,1)S(1)} %bitcast.28), channel_id=1, source_target_pairs={{0,8},{1,9},{2,10},{3,11},{4,12},{5,13},{6,14},{7,15},{8,0},{9,1},... | collective-permute-start | bytes 196616 | tf_op jit(solution)/shard_map/ppermute | solution.py:450
  8.5 6.2 %collective-permute-start = (bf16[1,4,8192]{2,1,0:T(4,128)(2,1)S(1)}, bf16[1,4,8192]{2,1,0:T(4,128)(2,1)S(1)}, u32[]{:S(2)}, u32[]{:S(2)}) collective-permute-start(bf16[1,4,8192]{2,1,0:T(4,128)(2,1)S(1)} %bitcast.29), channel_id=1, source_target_pairs={{0,4},{1,5},{2,6},{3,7},{4,8},{5,9},{6,10},{7,11},{8,12},{9,13},{1... | collective-permute-start | bytes 196616 | tf_op jit(solution)/shard_map/ppermute | solution.py:450
  14.8 5.8 %collective-permute-start.4 = (bf16[3,4,8192]{2,1,0:T(4,128)(2,1)S(1)}, bf16[3,4,8192]{2,1,0:T(4,128)(2,1)S(1)}, u32[]{:S(2)}, u32[]{:S(2)}) collective-permute-start(bf16[3,4,8192]{2,1,0:T(4,128)(2,1)S(1)} %get-tuple-element.98), channel_id=1, source_target_pairs={{0,2},{1,3},{2,0},{3,1},{4,6},{5,7},{6,4},{7,5},{8,10},{9,11},{10,... | collective-permute-start | bytes 589832 | tf_op jit(solution)/shard_map/ppermute | solution.py:450
  15.5 5.2 %collective-permute-start.5 = (bf16[5,4,8192]{2,1,0:T(4,128)(2,1)S(1)}, bf16[5,4,8192]{2,1,0:T(4,128)(2,1)S(1)}, u32[]{:S(2)}, u32[]{:S(2)}) collective-permute-start(bf16[5,4,8192]{2,1,0:T(4,128)(2,1)S(1)} %constant_dynamic-update-slice_fusion.refs_0_), channel_id=1, source_target_pairs={{0,1},{1,0},{2,3},{3,2},{4,5},{5,4},{6,7},{7,6},{8,9},{9,8},{10,11... | collective-permute-start | bytes 983048 | tf_op jit(solution)/shard_map/ppermute | solution.py:450
  15.6 6.5 %collective-permute-start.7 = (bf16[32,8192]{1,0:T(8,128)(2,1)S(1)}, bf16[32,8192]{1,0:T(8,128)(2,1)S(1)}, u32[]{:S(2)}, u32[]{:S(2)}) collective-permute-start(bf16[32,8192]{1,0:T(8,128)(2,1)S(1)} %bitcast.22), channel_id=1, source_target_pairs={{0,1},{1,0},{2,3},{3,2},{4,5},{5,4},{6,7},{7,6},{8,9},{9,8},{10,11... | collective-permute-start | bytes 1572872 | tf_op jit(solution)/shard_map/ppermute | solution.py:450
  16.0 6.0 %collective-permute-start.8 = (bf16[32,8192]{1,0:T(8,128)(2,1)S(1)}, bf16[32,8192]{1,0:T(8,128)(2,1)S(1)}, u32[]{:S(2)}, u32[]{:S(2)}) collective-permute-start(bf16[32,8192]{1,0:T(8,128)(2,1)S(1)} %bitcast.24), channel_id=1, source_target_pairs={{0,1},{1,0},{2,3},{3,2},{4,5},{5,4},{6,7},{7,6},{8,9},{9,8},{10,11... | collective-permute-start | bytes 1572872 | tf_op jit(solution)/shard_map/ppermute | solution.py:450
  20.6 1.4 %collective-permute-start.6 = (bf16[3,4,8192]{2,1,0:T(4,128)(2,1)S(1)}, bf16[3,4,8192]{2,1,0:T(4,128)(2,1)S(1)}, u32[]{:S(2)}, u32[]{:S(2)}) collective-permute-start(bf16[3,4,8192]{2,1,0:T(4,128)(2,1)S(1)} %collective-permute-done.4.refs_1_), channel_id=1, source_target_pairs={{0,1},{1,0},{2,3},{3,2},{4,5},{5,4},{6,7},{7,6},{8,9},{9,8},{10,11... | collective-permute-start | bytes 589832 | tf_op jit(solution)/shard_map/ppermute | solution.py:450
  23.2 3.6 %collective-permute-start.9 = (bf16[16,128]{1,0:T(8,128)(2,1)S(1)}, bf16[16,128]{1,0:T(8,128)(2,1)S(1)}, u32[]{:S(2)}, u32[]{:S(2)}) collective-permute-start(bf16[16,128]{1,0:T(8,128)(2,1)S(1)} %get-tuple-element.59.refs_0_), channel_id=1, source_target_pairs={{0,2},{1,3},{2,0},{3,1},{4,6},{5,7},{6,4},{7,5},{8,10},{9,11},{10,... | collective-permute-start | bytes 12296 | tf_op jit(solution)/shard_map/ppermute | solution.py:450
  25.1 20.4 %copy-start.4 = (bf16[2,384,1024]{2,1,0:T(8,128)(2,1)S(1)}, bf16[2,384,1024]{2,1,0:T(8,128)(2,1)}, u32[]{:S(2)}) copy-start(bf16[2,384,1024]{2,1,0:T(8,128)(2,1)} %k_ref.1) | copy-start | bytes 4718596
  25.2 20.4 %copy-start.5 = (bf16[2,384,1024]{2,1,0:T(8,128)(2,1)S(1)}, bf16[2,384,1024]{2,1,0:T(8,128)(2,1)}, u32[]{:S(2)}) copy-start(bf16[2,384,1024]{2,1,0:T(8,128)(2,1)} %v_ref.1) | copy-start | bytes 4718596
  26.9 30.3 %slice-start.2 = ((s8[8388608]{0:T(1024)(128)(4,1)}), s8[4194304]{0:T(1024)(128)(4,1)S(1)}, s32[]{:S(2)}) async-start(s8[8388608]{0:T(1024)(128)(4,1)} %bitcast.16), calls=%async_computation.4 | async-start | bytes 8388608
  26.9 30.3 %slice-start.3 = ((s8[8388608]{0:T(1024)(128)(4,1)}), s8[4194304]{0:T(1024)(128)(4,1)S(1)}, s32[]{:S(2)}) async-start(s8[8388608]{0:T(1024)(128)(4,1)} %bitcast.16), calls=%async_computation.5 | async-start | bytes 8388608
  26.9 5.8 %collective-permute-start.12 = (bf16[16,128]{1,0:T(8,128)(2,1)S(1)}, bf16[16,128]{1,0:T(8,128)(2,1)S(1)}, u32[]{:S(2)}, u32[]{:S(2)}) collective-permute-start(bf16[16,128]{1,0:T(8,128)(2,1)S(1)} %shard_map.187.refs_0_), channel_id=1, source_target_pairs={{0,12},{1,13},{2,14},{3,15},{4,0},{5,1},{6,2},{7,3},{8,4},{9,5},{1... | collective-permute-start | bytes 12296 | tf_op jit(solution)/shard_map/ppermute | solution.py:450
  28.7 4.5 %collective-permute-start.11 = (bf16[16,128]{1,0:T(8,128)(2,1)S(1)}, bf16[16,128]{1,0:T(8,128)(2,1)S(1)}, u32[]{:S(2)}, u32[]{:S(2)}) collective-permute-start(bf16[16,128]{1,0:T(8,128)(2,1)S(1)} %shard_map.187.refs_0_), channel_id=1, source_target_pairs={{0,8},{1,9},{2,10},{3,11},{4,12},{5,13},{6,14},{7,15},{8,0},{9,1},... | collective-permute-start | bytes 12296 | tf_op jit(solution)/shard_map/ppermute | solution.py:450
  29.3 5.4 %collective-permute-start.10 = (bf16[16,128]{1,0:T(8,128)(2,1)S(1)}, bf16[16,128]{1,0:T(8,128)(2,1)S(1)}, u32[]{:S(2)}, u32[]{:S(2)}) collective-permute-start(bf16[16,128]{1,0:T(8,128)(2,1)S(1)} %shard_map.187.refs_0_), channel_id=1, source_target_pairs={{0,4},{1,5},{2,6},{3,7},{4,8},{5,9},{6,10},{7,11},{8,12},{9,13},{1... | collective-permute-start | bytes 12296 | tf_op jit(solution)/shard_map/ppermute | solution.py:450
  58.5 2.0 %collective-permute-start.13 = (f32[32,4096]{1,0:T(8,128)S(1)}, f32[32,4096]{1,0:T(8,128)S(1)}, u32[]{:S(2)}, u32[]{:S(2)}) collective-permute-start(f32[32,4096]{1,0:T(8,128)S(1)} %get-tuple-element.78), channel_id=1, source_target_pairs={{0,1},{1,0},{2,3},{3,2},{4,5},{5,4},{6,7},{7,6},{8,9},{9,8},{10,11... | collective-permute-start | bytes 1572872 | tf_op jit(solution)/shard_map/ppermute | solution.py:450
  59.8 2.1 %collective-permute-start.18 = (f32[32,4096]{1,0:T(8,128)S(1)}, f32[32,4096]{1,0:T(8,128)S(1)}, u32[]{:S(2)}, u32[]{:S(2)}) collective-permute-start(f32[32,4096]{1,0:T(8,128)S(1)} %get-tuple-element.87), channel_id=1, source_target_pairs={{0,1},{1,0},{2,3},{3,2},{4,5},{5,4},{6,7},{7,6},{8,9},{9,8},{10,11... | collective-permute-start | bytes 1572872 | tf_op jit(solution)/shard_map/ppermute | solution.py:450
  60.6 10.8 %collective-permute-start.14 = (bf16[16,4096]{1,0:T(8,128)(2,1)S(1)}, bf16[16,4096]{1,0:T(8,128)(2,1)S(1)}, u32[]{:S(2)}, u32[]{:S(2)}) collective-permute-start(bf16[16,4096]{1,0:T(8,128)(2,1)S(1)} %get-tuple-element.80), channel_id=1, source_target_pairs={{0,2},{1,3},{2,0},{3,1},{4,6},{5,7},{6,4},{7,5},{8,10},{9,11},{10,... | collective-permute-start | bytes 393224 | tf_op jit(solution)/shard_map/ppermute | solution.py:450
  62.0 6.9 %collective-permute-start.19 = (bf16[8,4096]{1,0:T(8,128)(2,1)S(1)}, bf16[8,4096]{1,0:T(8,128)(2,1)S(1)}, u32[]{:S(2)}, u32[]{:S(2)}) collective-permute-start(bf16[8,4096]{1,0:T(8,128)(2,1)S(1)} %get-tuple-element.89), channel_id=1, source_target_pairs={{0,4},{1,5},{2,6},{3,7},{4,8},{5,9},{6,10},{7,11},{8,12},{9,13},{1... | collective-permute-start | bytes 196616 | tf_op jit(solution)/shard_map/ppermute | solution.py:450
  62.2 8.5 %collective-permute-start.20 = (bf16[8,4096]{1,0:T(8,128)(2,1)S(1)}, bf16[8,4096]{1,0:T(8,128)(2,1)S(1)}, u32[]{:S(2)}, u32[]{:S(2)}) collective-permute-start(bf16[8,4096]{1,0:T(8,128)(2,1)S(1)} %get-tuple-element.90), channel_id=1, source_target_pairs={{0,8},{1,9},{2,10},{3,11},{4,12},{5,13},{6,14},{7,15},{8,0},{9,1},... | collective-permute-start | bytes 196616 | tf_op jit(solution)/shard_map/ppermute | solution.py:450
  63.1 7.6 %collective-permute-start.21 = (bf16[8,4096]{1,0:T(8,128)(2,1)S(1)}, bf16[8,4096]{1,0:T(8,128)(2,1)S(1)}, u32[]{:S(2)}, u32[]{:S(2)}) collective-permute-start(bf16[8,4096]{1,0:T(8,128)(2,1)S(1)} %get-tuple-element.91), channel_id=1, source_target_pairs={{0,12},{1,13},{2,14},{3,15},{4,0},{5,1},{6,2},{7,3},{8,4},{9,5},{1... | collective-permute-start | bytes 196616 | tf_op jit(solution)/shard_map/ppermute | solution.py:450
  70.7 4.6 %collective-permute-start.22 = (bf16[4,4096]{1,0:T(4,128)(2,1)S(1)}, bf16[4,4096]{1,0:T(4,128)(2,1)S(1)}, u32[]{:S(2)}, u32[]{:S(2)}) collective-permute-start(bf16[4,4096]{1,0:T(4,128)(2,1)S(1)} %get-tuple-element.93), channel_id=1, source_target_pairs={{0,2},{1,3},{2,0},{3,1},{4,6},{5,7},{6,4},{7,5},{8,10},{9,11},{10,... | collective-permute-start | bytes 98312 | tf_op jit(solution)/shard_map/ppermute | solution.py:450
  71.4 5.8 %collective-permute-start.15 = (bf16[4,4096]{1,0:T(4,128)(2,1)S(1)}, bf16[4,4096]{1,0:T(4,128)(2,1)S(1)}, u32[]{:S(2)}, u32[]{:S(2)}) collective-permute-start(bf16[4,4096]{1,0:T(4,128)(2,1)S(1)} %get-tuple-element.82), channel_id=1, source_target_pairs={{0,4},{1,5},{2,6},{3,7},{4,8},{5,9},{6,10},{7,11},{8,12},{9,13},{1... | collective-permute-start | bytes 98312 | tf_op jit(solution)/shard_map/ppermute | solution.py:450
  72.8 5.2 %collective-permute-start.16 = (bf16[4,4096]{1,0:T(4,128)(2,1)S(1)}, bf16[4,4096]{1,0:T(4,128)(2,1)S(1)}, u32[]{:S(2)}, u32[]{:S(2)}) collective-permute-start(bf16[4,4096]{1,0:T(4,128)(2,1)S(1)} %get-tuple-element.83), channel_id=1, source_target_pairs={{0,8},{1,9},{2,10},{3,11},{4,12},{5,13},{6,14},{7,15},{8,0},{9,1},... | collective-permute-start | bytes 98312 | tf_op jit(solution)/shard_map/ppermute | solution.py:450
  74.0 4.2 %collective-permute-start.17 = (bf16[4,4096]{1,0:T(4,128)(2,1)S(1)}, bf16[4,4096]{1,0:T(4,128)(2,1)S(1)}, u32[]{:S(2)}, u32[]{:S(2)}) collective-permute-start(bf16[4,4096]{1,0:T(4,128)(2,1)S(1)} %get-tuple-element.84), channel_id=1, source_target_pairs={{0,12},{1,13},{2,14},{3,15},{4,0},{5,1},{6,2},{7,3},{8,4},{9,5},{1... | collective-permute-start | bytes 98312 | tf_op jit(solution)/shard_map/ppermute | solution.py:450
  (9 other events, 54.8 us)

commit v12 on v8

--- a/solution.py
+++ b/solution.py
@@ -125,7 +125,10 @@
     for j in range(slot_ref.shape[0]):
         slot = jnp.where(adapter == j, slot_ref[j], slot)
     held_ref[...] = slot
-    local_ref[...] = slot - index * adapters
+    shared = cores * adapters
+    place = slot - index // cores * shared
+    turned_place = (place - core_at * adapters + shared) % shared
+    local_ref[...] = jnp.where((place >= 0) & (place < shared), turned_place, -1)
     position = (length + step).astype(F32)
     lane = iota((1, HEAD), 1)
     odd = jnp.where(lane % 2 == 0, -1.0, 1.0)
@@ -166,7 +169,8 @@
 
 
 def low_body(rank, groups, *refs):
-    parts, (qd_ref, vd_ref, local_ref, place_ref, x_ref, out_ref) = refs[:groups], refs[groups:]
+    parts, refs = refs[:groups], refs[groups:]
+    *map_refs, local_ref, place_ref, x_ref, out_ref = refs
     rows = parts[0].shape[1]
     sets = max(1, 16 // rows)
     blocks = [(part, i) for part in parts for i in range(part.shape[0])]
@@ -177,8 +181,8 @@
             block = [part[i, :, lanes].astype(F32) for part, i in group]
             block = jnp.concatenate(block, axis=0).astype(BF16)
             x_ref[first * rows : (first + sets) * rows, lanes] = block
-    adapters = qd_ref.shape[0] // rank
-    maps = jnp.concatenate((qd_ref[...], vd_ref[...]), axis=0)
+    maps = jnp.concatenate([ref[...] for ref in map_refs], axis=0)
+    adapters = maps.shape[0] // (2 * rank)
     low = dot_nt(x_ref[...], maps)
     lane = lax.broadcasted_iota(jnp.int32, low.shape, 1)
     low = jnp.where(lane // rank % adapters == local_ref[...], low, 0.0)
@@ -318,8 +322,9 @@
         cached = jnp.exp(cached - top)
         newer = jnp.exp(newer - top)
         total = jnp.sum(cached, axis=1, keepdims=True) + jnp.sum(newer, axis=1, keepdims=True)
-        cached = (cached / total).astype(BF16)
-        newer = (newer / total).astype(BF16)
+        share = 1.0 / total
+        cached = (cached * share).astype(BF16)
+        newer = (newer * share).astype(BF16)
         for g in range(KV_HEADS):
             at_rows = slice(g * mine, (g + 1) * mine)
             part = dot(cached[at_rows], v_ref[b, :, g * HEAD : (g + 1) * HEAD])
@@ -461,6 +466,9 @@
     rest = jnp.concatenate(fars)
     groups = [jnp.concatenate([normed, *fars, *nears[:1]])]
     groups += [shift(rest, 0, m, 0) for m in range(1, near)]
+    query_down = jnp.swapaxes(query_down_weights, 1, 2).reshape(adapters * rank, width)
+    value_down = jnp.swapaxes(value_down_weights, 1, 2).reshape(adapters * rank, width)
+    query_down, value_down, rest = lax.optimization_barrier((query_down, value_down, rest))
 
     rest, at = lax.optimization_barrier((rest, index[None]))
     sent = -(-(rows * local + rows) // 8) * 8
@@ -497,8 +505,6 @@
 
     groups += [shift(part, 0, 0, c) for c in range(1, cores) for part in groups[:near]]
 
-    query_down = jnp.swapaxes(query_down_weights, 1, 2).reshape(adapters * rank, width)
-    value_down = jnp.swapaxes(value_down_weights, 1, 2).reshape(adapters * rank, width)
     packed_rows = all_rows * 2 * rank // HEAD
     x, low = whole_call(
         functools.partial(low_body, rank, len(groups)),
@@ -506,7 +512,13 @@
             jax.ShapeDtypeStruct((all_rows, width), BF16),
             jax.ShapeDtypeStruct((packed_rows, HEAD), BF16),
         ),
-        (*groups, query_down, value_down, near_slot, place),
+        (
+            *groups,
+            *[query_down, *[shift(query_down, 0, 0, c) for c in range(1, cores)]],
+            *[value_down, *[shift(value_down, 0, 0, c) for c in range(1, cores)]],
+            near_slot,
+            place,
+        ),
         cost=0.3,
     )
     def base(start, stop):
@@ -520,7 +532,7 @@
             cost=0.3,
         )
 
-    lows = [shift(low, 0, m, c) for m in range(near) for c in range(cores) if m + c]
+    lows = [shift(low, 0, m, 0) for m in range(1, near)]
     base_q, base_kv = base(0, width // 2)
     low = whole_call(join_body, jax.ShapeDtypeStruct(low.shape, BF16), (low, *lows), cost=0.1)
     low, base_q = lax.optimization_barrier((low, base_q))

time: 76.2 us -> 76.2 us (level)
    ppermute x23, starting transfers between devices: 24 us -> 23.3 us  [shift(): return lax.ppermute(value, 'serve', partner(f, m, c))]
where the time goes in v12:
time: 76.2 us; the launch traced here: 75.9 us
  starting transfers between devices  23.3 us (31%)
  blocking collectives  19.5 us (26%)
  waiting for transfers between devices  18.8 us (25%)
  Pallas kernels  12.4 us (16%)
  local copies, waits for them, and re-layouts  1 us (1%)
  between operations  0.92 us (1%)
    ppermute x23, starting transfers between devices, shift(): return lax.ppermute(value, 'serve', partner(f, m, c))  23.3 us
    ppermute x23, waiting for transfers between devices, shift(): return lax.ppermute(value, 'serve', partner(f, m, c))  18.8 us
    pallas_call x16, Pallas kernels, whole_call(): pl.pallas_call(body, out_shape=out_shape, in_specs=specs, out_specs=tuple...  12.4 us
    all_to_all x1, blocking collectives, shards(): lax.all_to_all(ready, 'serve', split_axis=0, concat_axis=0, tiled=True)  9.99 us
    all_to_all x1, blocking collectives, shards(): lax.all_to_all(context, 'serve', split_axis=0, concat_axis=0, tiled=True)  9.49 us
  transfers between devices with their start and end apart: 23, of which 10 were waited for; matrix products, arithmetic and copies ran while one was open for 0% of the time, Pallas kernels for 7%

profile of v12, /device:TPU:0, one launch (start us, length us, event | category | flops | bytes accessed | tf_op | source)
XLA Modules:
  0.0 75.9 jit_solution(12659501348748713557)
XLA Ops:
  0.7 0.6 copy-done.10
  1.8 3.0 %collective-permute-start.3 = (bf16[1,4,8192]{2,1,0:T(4,128)(2,1)S(1)}, bf16[1,4,8192]{2,1,0:T(4,128)(2,1)S(1)}, u32[]{:S(2)}, u32[]{:S(2)}) collective-permute-start(bf16[1,4,8192]{2,1,0:T(4,128)(2,1)S(1)} %bitcast.26), channel_id=1, source_target_pairs={{0,2},{1,3},{2,0},{3,1},{4,6},{5,7},{6,4},{7,5},{8,10},{9,11},{10,... | collective-permute-start | bytes 196616 | tf_op jit(solution)/shard_map/ppermute | solution.py:445
  4.9 3.6 %collective-permute-start.2 = (bf16[1,4,8192]{2,1,0:T(4,128)(2,1)S(1)}, bf16[1,4,8192]{2,1,0:T(4,128)(2,1)S(1)}, u32[]{:S(2)}, u32[]{:S(2)}) collective-permute-start(bf16[1,4,8192]{2,1,0:T(4,128)(2,1)S(1)} %bitcast.27), channel_id=1, source_target_pairs={{0,12},{1,13},{2,14},{3,15},{4,0},{5,1},{6,2},{7,3},{8,4},{9,5},{1... | collective-permute-start | bytes 196616 | tf_op jit(solution)/shard_map/ppermute | solution.py:445
  8.5 1.0 %collective-permute-start = (bf16[1,4,8192]{2,1,0:T(4,128)(2,1)S(1)}, bf16[1,4,8192]{2,1,0:T(4,128)(2,1)S(1)}, u32[]{:S(2)}, u32[]{:S(2)}) collective-permute-start(bf16[1,4,8192]{2,1,0:T(4,128)(2,1)S(1)} %bitcast.29), channel_id=1, source_target_pairs={{0,4},{1,5},{2,6},{3,7},{4,8},{5,9},{6,10},{7,11},{8,12},{9,13},{1... | collective-permute-start | bytes 196616 | tf_op jit(solution)/shard_map/ppermute | solution.py:445
  9.5 5.1 %collective-permute-done = bf16[1,4,8192]{2,1,0:T(4,128)(2,1)S(1)} collective-permute-done((bf16[1,4,8192]{2,1,0:T(4,128)(2,1)S(1)}, bf16[1,4,8192]{2,1,0:T(4,128)(2,1)S(1)}, u32[]{:S(2)}, u32[]{:S(2)}) %collective-permute-start) | collective-permute-done | bytes 65568 | tf_op jit(solution)/shard_map/ppermute | solution.py:445
  16.1 1.8 %shard_map.185 = (s32[64,1]{1,0:T(8,128)S(1)}, s32[64,1]{1,0:T(8,128)S(1)}, f32[64,128]{1,0:T(8,128)S(1)}, f32[64,128]{1,0:T(8,128)S(1)}, f32[64,128]{1,0:T(8,12...) custom-call(s32[1]{0:T(128)} %bitcast.index_ref, ...), custom_call_target="tpu_custom_call" | custom-call | flops 4600000000 | tf_op jit(solution)/shard_map/pallas_call | solution.py:36
  18.0 2.7 %collective-permute-done.4.refs_1_ = bf16[3,4,8192]{2,1,0:T(4,128)(2,1)S(1)} collective-permute-done((bf16[3,4,8192]{2,1,0:T(4,128)(2,1)S(1)}, bf16[3,4,8192]{2,1,0:T(4,128)(2,1)S(1)}, u32[]{:S(2)}, u32[]{:S(2)}) %collective-permute-start.4) | collective-permute-done | bytes 196640 | tf_op jit(solution)/shard_map/ppermute | solution.py:445
  20.6 1.4 %collective-permute-done.6.refs_3_ = bf16[3,4,8192]{2,1,0:T(4,128)(2,1)S(1)} collective-permute-done((bf16[3,4,8192]{2,1,0:T(4,128)(2,1)S(1)}, bf16[3,4,8192]{2,1,0:T(4,128)(2,1)S(1)}, u32[]{:S(2)}, u32[]{:S(2)}) %collective-permute-start.6) | collective-permute-done | bytes 196640 | tf_op jit(solution)/shard_map/ppermute | solution.py:445
  22.1 1.1 %shard_map.186 = (bf16[64,8192]{1,0:T(8,128)(2,1)S(1)}, bf16[16,128]{1,0:T(8,128)(2,1)S(1)}) custom-call(bf16[5,4,8192]{2,1,0:T(4,128)(2,1)S(1)} %constant_dynamic-update-slice_fusion.refs_0_, bf16[3,4,8192]{2,1,0:T(4,128)(2,1)S(1)} %collective-permute-done.4.refs_1_, bf16[5,4,8192]{2,1,0:T(4,128)(2,1)S(1)} %collective-permute-done.5.refs_2_, ...), custom_call_target="tpu_custom_call" | custom-call | flops 345000000 | tf_op jit(solution)/shard_map/pallas_call | solution.py:36
  23.8 1.3 %shard_map.188 = (f32[64,512]{1,0:T(8,128)S(1)}, f32[64,128]{1,0:T(8,128)S(1)}) custom-call(bf16[64,8192]{1,0:T(8,128)(2,1)S(1)} %get-tuple-element.60.x_ref, bf16[8192,512]{1,0:T(8,128)(2,1)S(1)} %bitcast.15, bf16[64,8192]{1,0:T(8,128)(2,1)S(1)} %bitcast.18, bf16[64,8192]{1,0:T(8,128)(2,1)S(1)} %bitcast.20), custom_call_target="tpu_custom_call" | custom-call | flops 345000000 | tf_op jit(solution)/shard_map/pallas_call | solution.py:36
  25.2 1.7 %collective-permute-done.9.refs_1_ = bf16[16,128]{1,0:T(8,128)(2,1)S(1)} collective-permute-done((bf16[16,128]{1,0:T(8,128)(2,1)S(1)}, bf16[16,128]{1,0:T(8,128)(2,1)S(1)}, u32[]{:S(2)}, u32[]{:S(2)}) %collective-permute-start.9) | collective-permute-done | bytes 4128 | tf_op jit(solution)/shard_map/ppermute | solution.py:445
  26.9 1.8 %collective-permute-start.12 = (bf16[16,128]{1,0:T(8,128)(2,1)S(1)}, bf16[16,128]{1,0:T(8,128)(2,1)S(1)}, u32[]{:S(2)}, u32[]{:S(2)}) collective-permute-start(bf16[16,128]{1,0:T(8,128)(2,1)S(1)} %shard_map.187.refs_0_), channel_id=1, source_target_pairs={{0,12},{1,13},{2,14},{3,15},{4,0},{5,1},{6,2},{7,3},{8,4},{9,5},{1... | collective-permute-start | bytes 12296 | tf_op jit(solution)/shard_map/ppermute | solution.py:445
  28.7 0.6 collective-permute-start.11
  29.3 1.9 %collective-permute-start.10 = (bf16[16,128]{1,0:T(8,128)(2,1)S(1)}, bf16[16,128]{1,0:T(8,128)(2,1)S(1)}, u32[]{:S(2)}, u32[]{:S(2)}) collective-permute-start(bf16[16,128]{1,0:T(8,128)(2,1)S(1)} %shard_map.187.refs_0_), channel_id=1, source_target_pairs={{0,4},{1,5},{2,6},{3,7},{4,8},{5,9},{6,10},{7,11},{8,12},{9,13},{1... | collective-permute-start | bytes 12296 | tf_op jit(solution)/shard_map/ppermute | solution.py:445
  31.3 1.3 %shard_map.189 = (f32[64,512]{1,0:T(8,128)S(1)}, f32[64,128]{1,0:T(8,128)S(1)}) custom-call(bf16[64,8192]{1,0:T(8,128)(2,1)S(1)} %get-tuple-element.60.x_ref, bf16[8192,512]{1,0:T(8,128)(2,1)S(1)} %bitcast.15, bf16[64,8192]{1,0:T(8,128)(2,1)S(1)} %bitcast.19, bf16[64,8192]{1,0:T(8,128)(2,1)S(1)} %bitcast.21), custom_call_target="tpu_custom_call" | custom-call | flops 345000000 | tf_op jit(solution)/shard_map/pallas_call | solution.py:36
  32.6 0.6 collective-permute-done.11.refs_2_
  33.2 1.5 %collective-permute-done.10.refs_1_ = bf16[16,128]{1,0:T(8,128)(2,1)S(1)} collective-permute-done((bf16[16,128]{1,0:T(8,128)(2,1)S(1)}, bf16[16,128]{1,0:T(8,128)(2,1)S(1)}, u32[]{:S(2)}, u32[]{:S(2)}) %collective-permute-start.10) | collective-permute-done | bytes 4128 | tf_op jit(solution)/shard_map/ppermute | solution.py:445
  34.7 0.8 %shard_map.190 = bf16[16,24,128]{2,1,0:T(8,128)(2,1)S(1)} custom-call(bf16[16,128]{1,0:T(8,128)(2,1)S(1)} %shard_map.187.refs_0_, bf16[16,128]{1,0:T(8,128)(2,1)S(1)} %collective-permute-done.10.refs_1_, bf16[16,128]{1,0:T(8,128)(2,1)S(1)} %collective-permute-done.11.refs_2_, bf16[16,128]{1,0:T(8,128)(2,1)S(1)} %collective-permute-done.12.refs_3_, ...), custom_call_target="tpu_custom_call" | custom-call | flops 1035000000 | tf_op jit(solution)/shard_map/pallas_call | solution.py:36
  35.6 10.0 %all_to_all.10.x_ref = bf16[16,24,128]{2,1,0:T(8,128)(2,1)S(1)} all-to-all(bf16[16,24,128]{2,1,0:T(8,128)(2,1)S(1)} %shard_map.190), channel_id=1, replica_groups=mesh['replica'=2,'serve'=16] {'serve'}, dimensions={0} | all-to-all | bytes 196608 | tf_op jit(solution)/shard_map/all_to_all | solution.py:560
  45.6 2.0 %shard_map.191 = (bf16[2,2,1024]{2,1,0:T(2,128)(2,1)}, bf16[2,2,1024]{2,1,0:T(2,128)(2,1)}, bf16[16,16,128]{2,1,0:T(8,128)(2,1)S(1)}) custom-call(s32[1]{0:T(128)} %bitcast.index_ref, s32[32]{0:T(128)S(1)} %copy-done.13, bf16[16,24,128]{2,1,0:T(8,128)(2,1)S(1)} %all_to_all.10.x_ref, bf16[256,384]{1,0:T(8,128)(2,1)S(1)} %get-tuple-element.74.order_ref, ...), custom_call_target="tpu_custom_call" | custom-call | flops 1150000000 | tf_op jit(solution)/shard_map/pallas_call | solution.py:36
  47.6 9.5 %all_to_all.11.ctx_ref = bf16[16,16,128]{2,1,0:T(8,128)(2,1)S(1)} all-to-all(bf16[16,16,128]{2,1,0:T(8,128)(2,1)S(1)} %get-tuple-element.75), channel_id=1, replica_groups=mesh['replica'=2,'serve'=16] {'serve'}, dimensions={0} | all-to-all | bytes 131072 | tf_op jit(solution)/shard_map/all_to_all | solution.py:571
  57.0 1.7 %shard_map.192 = (bf16[64,512]{1,0:T(8,128)(2,1)S(1)}, f32[32,5120]{1,0:T(8,128)S(1)}, f32[32,5120]{1,0:T(8,128)S(1)}) custom-call(bf16[16,16,128]{2,1,0:T(8,128)(2,1)S(1)} %all_to_all.11.ctx_ref, bf16[256,256]{1,0:T(8,128)(2,1)S(1)} %get-tuple-element.76.take_ref, bf16[512,8192]{1,0:T(8,128)(2,1)S(1)} %bitcast.17), custom_call_target="tpu_custom_call" | custom-call | flops 460000000 | tf_op jit(solution)/shard_map/pallas_call | solution.py:36
  58.8 0.9 %shard_map.195 = (f32[32,3072]{1,0:T(8,128)S(1)}, f32[32,3072]{1,0:T(8,128)S(1)}) custom-call(bf16[64,512]{1,0:T(8,128)(2,1)S(1)} %get-tuple-element.85.a_ref, bf16[512,8192]{1,0:T(8,128)(2,1)S(1)} %bitcast.17), custom_call_target="tpu_custom_call" | custom-call | flops 345000000 | tf_op jit(solution)/shard_map/pallas_call | solution.py:36
  60.3 0.6 collective-permute-done.13.came_ref
  61.9 1.0 %collective-permute-start.20 = (bf16[8,3072]{1,0:T(8,128)(2,1)S(1)}, bf16[8,3072]{1,0:T(8,128)(2,1)S(1)}, u32[]{:S(2)}, u32[]{:S(2)}) collective-permute-start(bf16[8,3072]{1,0:T(8,128)(2,1)S(1)} %get-tuple-element.90), channel_id=1, source_target_pairs={{0,8},{1,9},{2,10},{3,11},{4,12},{5,13},{6,14},{7,15},{8,0},{9,1},... | collective-permute-start | bytes 147464 | tf_op jit(solution)/shard_map/ppermute | solution.py:445
  62.9 2.7 %collective-permute-start.21 = (bf16[8,3072]{1,0:T(8,128)(2,1)S(1)}, bf16[8,3072]{1,0:T(8,128)(2,1)S(1)}, u32[]{:S(2)}, u32[]{:S(2)}) collective-permute-start(bf16[8,3072]{1,0:T(8,128)(2,1)S(1)} %get-tuple-element.91), channel_id=1, source_target_pairs={{0,12},{1,13},{2,14},{3,15},{4,0},{5,1},{6,2},{7,3},{8,4},{9,5},{1... | collective-permute-start | bytes 147464 | tf_op jit(solution)/shard_map/ppermute | solution.py:445
  65.6 1.7 %collective-permute-done.14.refs_1_ = bf16[16,5120]{1,0:T(8,128)(2,1)S(1)} collective-permute-done((bf16[16,5120]{1,0:T(8,128)(2,1)S(1)}, bf16[16,5120]{1,0:T(8,128)(2,1)S(1)}, u32[]{:S(2)}, u32[]{:S(2)}) %collective-permute-start.14) | collective-permute-done | bytes 163872 | tf_op jit(solution)/shard_map/ppermute | solution.py:445
  67.5 0.9 %collective-permute-start.16 = (bf16[4,5120]{1,0:T(4,128)(2,1)S(1)}, bf16[4,5120]{1,0:T(4,128)(2,1)S(1)}, u32[]{:S(2)}, u32[]{:S(2)}) collective-permute-start(bf16[4,5120]{1,0:T(4,128)(2,1)S(1)} %get-tuple-element.83), channel_id=1, source_target_pairs={{0,8},{1,9},{2,10},{3,11},{4,12},{5,13},{6,14},{7,15},{8,0},{9,1},... | collective-permute-start | bytes 122888 | tf_op jit(solution)/shard_map/ppermute | solution.py:445
  68.4 2.8 %collective-permute-start.17 = (bf16[4,5120]{1,0:T(4,128)(2,1)S(1)}, bf16[4,5120]{1,0:T(4,128)(2,1)S(1)}, u32[]{:S(2)}, u32[]{:S(2)}) collective-permute-start(bf16[4,5120]{1,0:T(4,128)(2,1)S(1)} %get-tuple-element.84), channel_id=1, source_target_pairs={{0,12},{1,13},{2,14},{3,15},{4,0},{5,1},{6,2},{7,3},{8,4},{9,5},{1... | collective-permute-start | bytes 122888 | tf_op jit(solution)/shard_map/ppermute | solution.py:445
  71.2 0.9 %collective-permute-start.22 = (bf16[4,3072]{1,0:T(4,128)(2,1)S(1)}, bf16[4,3072]{1,0:T(4,128)(2,1)S(1)}, u32[]{:S(2)}, u32[]{:S(2)}) collective-permute-start(bf16[4,3072]{1,0:T(4,128)(2,1)S(1)} %get-tuple-element.93), channel_id=1, source_target_pairs={{0,2},{1,3},{2,0},{3,1},{4,6},{5,7},{6,4},{7,5},{8,10},{9,11},{10,... | collective-permute-start | bytes 73736 | tf_op jit(solution)/shard_map/ppermute | solution.py:445
  72.1 3.0 %collective-permute-done.22.refs_5_ = bf16[4,3072]{1,0:T(4,128)(2,1)S(1)} collective-permute-done((bf16[4,3072]{1,0:T(4,128)(2,1)S(1)}, bf16[4,3072]{1,0:T(4,128)(2,1)S(1)}, u32[]{:S(2)}, u32[]{:S(2)}) %collective-permute-start.22) | collective-permute-done | bytes 24608 | tf_op jit(solution)/shard_map/ppermute | solution.py:445
  75.1 0.7 shard_map.198
  (75 shorter events, 4.4 us)
Async XLA Ops:
  0.7 15.4 %copy-start.3 = (bf16[2,8192,16]{1,2,0:T(8,128)(2,1)S(1)}, bf16[2,8192,16]{1,2,0:T(8,128)(2,1)}, u32[]{:S(2)}) copy-start(bf16[2,8192,16]{1,2,0:T(8,128)(2,1)} %param.24) | copy-start | bytes 1572868
  0.7 14.9 %copy-start.2 = (bf16[2,8192,16]{1,2,0:T(8,128)(2,1)S(1)}, bf16[2,8192,16]{1,2,0:T(8,128)(2,1)}, u32[]{:S(2)}) copy-start(bf16[2,8192,16]{1,2,0:T(8,128)(2,1)} %param.23) | copy-start | bytes 1572868
  0.7 15.5 %copy-start.13 = (s32[32]{0:T(128)S(1)}, s32[32]{0:T(128)}, u32[]{:S(2)}) copy-start(s32[32]{0:T(128)} %len_ref.1) | copy-start | bytes 388
  0.7 15.4 %copy-start.12 = (s32[32]{0:T(128)S(1)}, s32[32]{0:T(128)}, u32[]{:S(2)}) copy-start(s32[32]{0:T(128)} %slot_hbm.1) | copy-start | bytes 388
  0.7 15.4 %copy-start.11 = (s32[32]{0:T(128)S(1)}, s32[32]{0:T(128)}, u32[]{:S(2)}) copy-start(s32[32]{0:T(128)} %adapter_hbm.1) | copy-start | bytes 388
  1.8 13.6 %collective-permute-start.3 = (bf16[1,4,8192]{2,1,0:T(4,128)(2,1)S(1)}, bf16[1,4,8192]{2,1,0:T(4,128)(2,1)S(1)}, u32[]{:S(2)}, u32[]{:S(2)}) collective-permute-start(bf16[1,4,8192]{2,1,0:T(4,128)(2,1)S(1)} %bitcast.26), channel_id=1, source_target_pairs={{0,2},{1,3},{2,0},{3,1},{4,6},{5,7},{6,4},{7,5},{8,10},{9,11},{10,... | collective-permute-start | bytes 196616 | tf_op jit(solution)/shard_map/ppermute | solution.py:445
  4.9 9.9 %collective-permute-start.2 = (bf16[1,4,8192]{2,1,0:T(4,128)(2,1)S(1)}, bf16[1,4,8192]{2,1,0:T(4,128)(2,1)S(1)}, u32[]{:S(2)}, u32[]{:S(2)}) collective-permute-start(bf16[1,4,8192]{2,1,0:T(4,128)(2,1)S(1)} %bitcast.27), channel_id=1, source_target_pairs={{0,12},{1,13},{2,14},{3,15},{4,0},{5,1},{6,2},{7,3},{8,4},{9,5},{1... | collective-permute-start | bytes 196616 | tf_op jit(solution)/shard_map/ppermute | solution.py:445
  8.5 6.2 %collective-permute-start.1 = (bf16[1,4,8192]{2,1,0:T(4,128)(2,1)S(1)}, bf16[1,4,8192]{2,1,0:T(4,128)(2,1)S(1)}, u32[]{:S(2)}, u32[]{:S(2)}) collective-permute-start(bf16[1,4,8192]{2,1,0:T(4,128)(2,1)S(1)} %bitcast.28), channel_id=1, source_target_pairs={{0,8},{1,9},{2,10},{3,11},{4,12},{5,13},{6,14},{7,15},{8,0},{9,1},... | collective-permute-start | bytes 196616 | tf_op jit(solution)/shard_map/ppermute | solution.py:445
  8.5 6.2 %collective-permute-start = (bf16[1,4,8192]{2,1,0:T(4,128)(2,1)S(1)}, bf16[1,4,8192]{2,1,0:T(4,128)(2,1)S(1)}, u32[]{:S(2)}, u32[]{:S(2)}) collective-permute-start(bf16[1,4,8192]{2,1,0:T(4,128)(2,1)S(1)} %bitcast.29), channel_id=1, source_target_pairs={{0,4},{1,5},{2,6},{3,7},{4,8},{5,9},{6,10},{7,11},{8,12},{9,13},{1... | collective-permute-start | bytes 196616 | tf_op jit(solution)/shard_map/ppermute | solution.py:445
  14.8 5.8 %collective-permute-start.4 = (bf16[3,4,8192]{2,1,0:T(4,128)(2,1)S(1)}, bf16[3,4,8192]{2,1,0:T(4,128)(2,1)S(1)}, u32[]{:S(2)}, u32[]{:S(2)}) collective-permute-start(bf16[3,4,8192]{2,1,0:T(4,128)(2,1)S(1)} %get-tuple-element.98), channel_id=1, source_target_pairs={{0,2},{1,3},{2,0},{3,1},{4,6},{5,7},{6,4},{7,5},{8,10},{9,11},{10,... | collective-permute-start | bytes 589832 | tf_op jit(solution)/shard_map/ppermute | solution.py:445
  15.5 5.2 %collective-permute-start.5 = (bf16[5,4,8192]{2,1,0:T(4,128)(2,1)S(1)}, bf16[5,4,8192]{2,1,0:T(4,128)(2,1)S(1)}, u32[]{:S(2)}, u32[]{:S(2)}) collective-permute-start(bf16[5,4,8192]{2,1,0:T(4,128)(2,1)S(1)} %constant_dynamic-update-slice_fusion.refs_0_), channel_id=1, source_target_pairs={{0,1},{1,0},{2,3},{3,2},{4,5},{5,4},{6,7},{7,6},{8,9},{9,8},{10,11... | collective-permute-start | bytes 983048 | tf_op jit(solution)/shard_map/ppermute | solution.py:445
  15.6 6.5 %collective-permute-start.7 = (bf16[32,8192]{1,0:T(8,128)(2,1)S(1)}, bf16[32,8192]{1,0:T(8,128)(2,1)S(1)}, u32[]{:S(2)}, u32[]{:S(2)}) collective-permute-start(bf16[32,8192]{1,0:T(8,128)(2,1)S(1)} %bitcast.22), channel_id=1, source_target_pairs={{0,1},{1,0},{2,3},{3,2},{4,5},{5,4},{6,7},{7,6},{8,9},{9,8},{10,11... | collective-permute-start | bytes 1572872 | tf_op jit(solution)/shard_map/ppermute | solution.py:445
  16.0 6.0 %collective-permute-start.8 = (bf16[32,8192]{1,0:T(8,128)(2,1)S(1)}, bf16[32,8192]{1,0:T(8,128)(2,1)S(1)}, u32[]{:S(2)}, u32[]{:S(2)}) collective-permute-start(bf16[32,8192]{1,0:T(8,128)(2,1)S(1)} %bitcast.24), channel_id=1, source_target_pairs={{0,1},{1,0},{2,3},{3,2},{4,5},{5,4},{6,7},{7,6},{8,9},{9,8},{10,11... | collective-permute-start | bytes 1572872 | tf_op jit(solution)/shard_map/ppermute | solution.py:445
  20.6 1.4 %collective-permute-start.6 = (bf16[3,4,8192]{2,1,0:T(4,128)(2,1)S(1)}, bf16[3,4,8192]{2,1,0:T(4,128)(2,1)S(1)}, u32[]{:S(2)}, u32[]{:S(2)}) collective-permute-start(bf16[3,4,8192]{2,1,0:T(4,128)(2,1)S(1)} %collective-permute-done.4.refs_1_), channel_id=1, source_target_pairs={{0,1},{1,0},{2,3},{3,2},{4,5},{5,4},{6,7},{7,6},{8,9},{9,8},{10,11... | collective-permute-start | bytes 589832 | tf_op jit(solution)/shard_map/ppermute | solution.py:445
  23.2 3.6 %collective-permute-start.9 = (bf16[16,128]{1,0:T(8,128)(2,1)S(1)}, bf16[16,128]{1,0:T(8,128)(2,1)S(1)}, u32[]{:S(2)}, u32[]{:S(2)}) collective-permute-start(bf16[16,128]{1,0:T(8,128)(2,1)S(1)} %get-tuple-element.59.refs_0_), channel_id=1, source_target_pairs={{0,2},{1,3},{2,0},{3,1},{4,6},{5,7},{6,4},{7,5},{8,10},{9,11},{10,... | collective-permute-start | bytes 12296 | tf_op jit(solution)/shard_map/ppermute | solution.py:445
  25.1 20.4 %copy-start.4 = (bf16[2,384,1024]{2,1,0:T(8,128)(2,1)S(1)}, bf16[2,384,1024]{2,1,0:T(8,128)(2,1)}, u32[]{:S(2)}) copy-start(bf16[2,384,1024]{2,1,0:T(8,128)(2,1)} %k_ref.1) | copy-start | bytes 4718596
  25.2 20.4 %copy-start.5 = (bf16[2,384,1024]{2,1,0:T(8,128)(2,1)S(1)}, bf16[2,384,1024]{2,1,0:T(8,128)(2,1)}, u32[]{:S(2)}) copy-start(bf16[2,384,1024]{2,1,0:T(8,128)(2,1)} %v_ref.1) | copy-start | bytes 4718596
  26.9 30.2 %slice-start.2 = ((s8[8388608]{0:T(1024)(128)(4,1)}), s8[4194304]{0:T(1024)(128)(4,1)S(1)}, s32[]{:S(2)}) async-start(s8[8388608]{0:T(1024)(128)(4,1)} %bitcast.16), calls=%async_computation.4 | async-start | bytes 8388608
  26.9 30.2 %slice-start.3 = ((s8[8388608]{0:T(1024)(128)(4,1)}), s8[4194304]{0:T(1024)(128)(4,1)S(1)}, s32[]{:S(2)}) async-start(s8[8388608]{0:T(1024)(128)(4,1)} %bitcast.16), calls=%async_computation.5 | async-start | bytes 8388608
  26.9 5.8 %collective-permute-start.12 = (bf16[16,128]{1,0:T(8,128)(2,1)S(1)}, bf16[16,128]{1,0:T(8,128)(2,1)S(1)}, u32[]{:S(2)}, u32[]{:S(2)}) collective-permute-start(bf16[16,128]{1,0:T(8,128)(2,1)S(1)} %shard_map.187.refs_0_), channel_id=1, source_target_pairs={{0,12},{1,13},{2,14},{3,15},{4,0},{5,1},{6,2},{7,3},{8,4},{9,5},{1... | collective-permute-start | bytes 12296 | tf_op jit(solution)/shard_map/ppermute | solution.py:445
  28.7 4.5 %collective-permute-start.11 = (bf16[16,128]{1,0:T(8,128)(2,1)S(1)}, bf16[16,128]{1,0:T(8,128)(2,1)S(1)}, u32[]{:S(2)}, u32[]{:S(2)}) collective-permute-start(bf16[16,128]{1,0:T(8,128)(2,1)S(1)} %shard_map.187.refs_0_), channel_id=1, source_target_pairs={{0,8},{1,9},{2,10},{3,11},{4,12},{5,13},{6,14},{7,15},{8,0},{9,1},... | collective-permute-start | bytes 12296 | tf_op jit(solution)/shard_map/ppermute | solution.py:445
  29.3 5.4 %collective-permute-start.10 = (bf16[16,128]{1,0:T(8,128)(2,1)S(1)}, bf16[16,128]{1,0:T(8,128)(2,1)S(1)}, u32[]{:S(2)}, u32[]{:S(2)}) collective-permute-start(bf16[16,128]{1,0:T(8,128)(2,1)S(1)} %shard_map.187.refs_0_), channel_id=1, source_target_pairs={{0,4},{1,5},{2,6},{3,7},{4,8},{5,9},{6,10},{7,11},{8,12},{9,13},{1... | collective-permute-start | bytes 12296 | tf_op jit(solution)/shard_map/ppermute | solution.py:445
  58.7 2.2 %collective-permute-start.13 = (f32[32,5120]{1,0:T(8,128)S(1)}, f32[32,5120]{1,0:T(8,128)S(1)}, u32[]{:S(2)}, u32[]{:S(2)}) collective-permute-start(f32[32,5120]{1,0:T(8,128)S(1)} %get-tuple-element.78), channel_id=1, source_target_pairs={{0,1},{1,0},{2,3},{3,2},{4,5},{5,4},{6,7},{7,6},{8,9},{9,8},{10,11... | collective-permute-start | bytes 1966088 | tf_op jit(solution)/shard_map/ppermute | solution.py:445
  59.7 1.9 %collective-permute-start.18 = (f32[32,3072]{1,0:T(8,128)S(1)}, f32[32,3072]{1,0:T(8,128)S(1)}, u32[]{:S(2)}, u32[]{:S(2)}) collective-permute-start(f32[32,3072]{1,0:T(8,128)S(1)} %get-tuple-element.87), channel_id=1, source_target_pairs={{0,1},{1,0},{2,3},{3,2},{4,5},{5,4},{6,7},{7,6},{8,9},{9,8},{10,11... | collective-permute-start | bytes 1179656 | tf_op jit(solution)/shard_map/ppermute | solution.py:445
  61.0 6.3 %collective-permute-start.14 = (bf16[16,5120]{1,0:T(8,128)(2,1)S(1)}, bf16[16,5120]{1,0:T(8,128)(2,1)S(1)}, u32[]{:S(2)}, u32[]{:S(2)}) collective-permute-start(bf16[16,5120]{1,0:T(8,128)(2,1)S(1)} %get-tuple-element.80), channel_id=1, source_target_pairs={{0,2},{1,3},{2,0},{3,1},{4,6},{5,7},{6,4},{7,5},{8,10},{9,11},{10,... | collective-permute-start | bytes 491528 | tf_op jit(solution)/shard_map/ppermute | solution.py:445
  61.7 6.8 %collective-permute-start.19 = (bf16[8,3072]{1,0:T(8,128)(2,1)S(1)}, bf16[8,3072]{1,0:T(8,128)(2,1)S(1)}, u32[]{:S(2)}, u32[]{:S(2)}) collective-permute-start(bf16[8,3072]{1,0:T(8,128)(2,1)S(1)} %get-tuple-element.89), channel_id=1, source_target_pairs={{0,4},{1,5},{2,6},{3,7},{4,8},{5,9},{6,10},{7,11},{8,12},{9,13},{1... | collective-permute-start | bytes 147464 | tf_op jit(solution)/shard_map/ppermute | solution.py:445
  61.9 9.3 %collective-permute-start.20 = (bf16[8,3072]{1,0:T(8,128)(2,1)S(1)}, bf16[8,3072]{1,0:T(8,128)(2,1)S(1)}, u32[]{:S(2)}, u32[]{:S(2)}) collective-permute-start(bf16[8,3072]{1,0:T(8,128)(2,1)S(1)} %get-tuple-element.90), channel_id=1, source_target_pairs={{0,8},{1,9},{2,10},{3,11},{4,12},{5,13},{6,14},{7,15},{8,0},{9,1},... | collective-permute-start | bytes 147464 | tf_op jit(solution)/shard_map/ppermute | solution.py:445
  62.9 8.3 %collective-permute-start.21 = (bf16[8,3072]{1,0:T(8,128)(2,1)S(1)}, bf16[8,3072]{1,0:T(8,128)(2,1)S(1)}, u32[]{:S(2)}, u32[]{:S(2)}) collective-permute-start(bf16[8,3072]{1,0:T(8,128)(2,1)S(1)} %get-tuple-element.91), channel_id=1, source_target_pairs={{0,12},{1,13},{2,14},{3,15},{4,0},{5,1},{6,2},{7,3},{8,4},{9,5},{1... | collective-permute-start | bytes 147464 | tf_op jit(solution)/shard_map/ppermute | solution.py:445
  67.3 7.8 %collective-permute-start.15 = (bf16[4,5120]{1,0:T(4,128)(2,1)S(1)}, bf16[4,5120]{1,0:T(4,128)(2,1)S(1)}, u32[]{:S(2)}, u32[]{:S(2)}) collective-permute-start(bf16[4,5120]{1,0:T(4,128)(2,1)S(1)} %get-tuple-element.82), channel_id=1, source_target_pairs={{0,4},{1,5},{2,6},{3,7},{4,8},{5,9},{6,10},{7,11},{8,12},{9,13},{1... | collective-permute-start | bytes 122888 | tf_op jit(solution)/shard_map/ppermute | solution.py:445
  67.5 7.7 %collective-permute-start.16 = (bf16[4,5120]{1,0:T(4,128)(2,1)S(1)}, bf16[4,5120]{1,0:T(4,128)(2,1)S(1)}, u32[]{:S(2)}, u32[]{:S(2)}) collective-permute-start(bf16[4,5120]{1,0:T(4,128)(2,1)S(1)} %get-tuple-element.83), channel_id=1, source_target_pairs={{0,8},{1,9},{2,10},{3,11},{4,12},{5,13},{6,14},{7,15},{8,0},{9,1},... | collective-permute-start | bytes 122888 | tf_op jit(solution)/shard_map/ppermute | solution.py:445
  68.4 6.7 %collective-permute-start.17 = (bf16[4,5120]{1,0:T(4,128)(2,1)S(1)}, bf16[4,5120]{1,0:T(4,128)(2,1)S(1)}, u32[]{:S(2)}, u32[]{:S(2)}) collective-permute-start(bf16[4,5120]{1,0:T(4,128)(2,1)S(1)} %get-tuple-element.84), channel_id=1, source_target_pairs={{0,12},{1,13},{2,14},{3,15},{4,0},{5,1},{6,2},{7,3},{8,4},{9,5},{1... | collective-permute-start | bytes 122888 | tf_op jit(solution)/shard_map/ppermute | solution.py:445
  71.2 3.9 %collective-permute-start.22 = (bf16[4,3072]{1,0:T(4,128)(2,1)S(1)}, bf16[4,3072]{1,0:T(4,128)(2,1)S(1)}, u32[]{:S(2)}, u32[]{:S(2)}) collective-permute-start(bf16[4,3072]{1,0:T(4,128)(2,1)S(1)} %get-tuple-element.93), channel_id=1, source_target_pairs={{0,2},{1,3},{2,0},{3,1},{4,6},{5,7},{6,4},{7,5},{8,10},{9,11},{10,... | collective-permute-start | bytes 73736 | tf_op jit(solution)/shard_map/ppermute | solution.py:445
  (9 other events, 54.8 us)

commit v13 on v12

--- a/solution.py
+++ b/solution.py
@@ -198,20 +198,20 @@
     out_ref[...] = packed.astype(BF16)
 
 
-def join_body(*refs):
-    total = refs[0][...].astype(F32)
-    for ref in refs[1:-1]:
+def join_body(cores, index_ref, own_ref, *refs):
+    total = jnp.where(index_ref[0] % cores == 0, own_ref[...].astype(F32), 0.0)
+    for ref in refs[:-1]:
         total = total + ref[...].astype(F32)
     refs[-1][...] = total.astype(BF16)
 
 
-def base_body(depth, start, stop, x_ref, q_ref, k_ref, v_ref, oq_ref, okv_ref):
+def base_body(depth, x_ref, q_ref, k_ref, v_ref, oq_ref, okv_ref):
     oq_ref[...] = jnp.zeros_like(oq_ref)
     okv_ref[...] = jnp.zeros_like(okv_ref)
     columns = k_ref.shape[0]
     narrow = jnp.zeros((HEAD - 2 * columns, depth), BF16)
 
-    @pl.loop(start // depth, stop // depth)
+    @pl.loop(0, x_ref.shape[1] // depth)
     def _(i):
         at = pl.ds(pl.multiple_of(i * depth, depth), depth)
         x = x_ref[:, at]
@@ -235,7 +235,7 @@
 ):
     low_refs = refs[:lows]
     (
-        oq_ref, okv_ref, oq2_ref, okv2_ref, unplace_ref, slot_ref, uq_ref, uv_ref, cos_ref, sin_ref, kcos_ref, ksin_ref,
+        oq_ref, okv_ref, unplace_ref, slot_ref, uq_ref, uv_ref, cos_ref, sin_ref, kcos_ref, ksin_ref,
         send_ref, out_ref,
     ) = refs[lows:]
     packed = low_refs[0][...].astype(F32)
@@ -255,8 +255,8 @@
     spread_v = jnp.where(column % rank + rank == row, 1.0, 0.0).astype(BF16)
     wide_q = jnp.where(here, dot(low, spread_q), 0.0).astype(BF16)
     wide_v = jnp.where(here, dot(low, spread_v), 0.0).astype(BF16)
-    query = oq_ref[...] + oq2_ref[...] + dot(wide_q, uq_ref[...])
-    fresh = turned(okv_ref[...] + okv2_ref[...], kcos_ref[...], ksin_ref[...])
+    query = oq_ref[...] + dot(wide_q, uq_ref[...])
+    fresh = turned(okv_ref[...], kcos_ref[...], ksin_ref[...])
     columns = uv_ref.shape[1]
     value = dot(wide_v, uv_ref[...])
     pieces = [jnp.zeros((value.shape[0], columns), F32), value]
@@ -521,30 +521,43 @@
         ),
         cost=0.3,
     )
-    def base(start, stop):
-        return whole_call(
-            functools.partial(base_body, 2048, start, stop),
-            (
-                jax.ShapeDtypeStruct((all_rows, query_cols), F32),
-                jax.ShapeDtypeStruct((all_rows, HEAD), F32),
-            ),
-            (x, query_matrix, key_matrix.T, value_matrix.T),
-            cost=0.3,
-        )
-
-    lows = [shift(low, 0, m, 0) for m in range(1, near)]
-    base_q, base_kv = base(0, width // 2)
-    low = whole_call(join_body, jax.ShapeDtypeStruct(low.shape, BF16), (low, *lows), cost=0.1)
-    low, base_q = lax.optimization_barrier((low, base_q))
-    lows = [low] + [shift(low, f, 0, 0) for f in range(1, far)]
-    bases = (base_q, base_kv, *base(width // 2, width))
+    def spread(value, f):
+        pairs = []
+        for z in range(far):
+            for y in range(near):
+                for k in range(cores):
+                    if f or k % near:
+                        to = ((z + f) % far * near + (y + k) % near) * cores + k
+                        pairs.append(((z * near + y) * cores + k, to))
+        return lax.ppermute(value, "serve", pairs)
+
+    lows = [spread(low, f) for f in range(far)]
+    base_q, base_kv = whole_call(
+        functools.partial(base_body, 2048),
+        (
+            jax.ShapeDtypeStruct((all_rows, query_cols), F32),
+            jax.ShapeDtypeStruct((all_rows, HEAD), F32),
+        ),
+        (x, query_matrix, key_matrix.T, value_matrix.T),
+        cost=0.6,
+    )
+    lows[0], base_q = lax.optimization_barrier((lows[0], base_q))
+    low = whole_call(
+        functools.partial(join_body, cores),
+        jax.ShapeDtypeStruct(low.shape, BF16),
+        (index[None], low, *lows),
+        smem=1,
+        cost=0.1,
+    )
+    lows = [low] + [shift(low, 0, 0, c) for c in range(1, cores)]
 
     ready = whole_call(
         functools.partial(ready_body, rank, len(lows)),
         jax.ShapeDtypeStruct((n, sent, HEAD), BF16),
         (
             *lows,
-            *bases,
+            base_q,
+            base_kv,
             unplace,
             slot,
             query_up_weights.reshape(stored * rank, query_cols),

time: 76.2 us -> 76.8 us (level)
  waiting for transfers between devices: 18.8 us -> 15.8 us
  starting transfers between devices: 23.3 us -> 26.1 us
    ppermute x0 -> x4, starting transfers between devices: none -> 5.04 us  [spread(): return lax.ppermute(value, 'serve', pairs)]
    ppermute x23 -> x20, waiting for transfers between devices: 18.8 us -> 15.8 us  [shift(): return lax.ppermute(value, 'serve', partner(f, m, c))]
    ppermute x23 -> x20, starting transfers between devices: 23.3 us -> 21 us  [shift(): return lax.ppermute(value, 'serve', partner(f, m, c))]
    pallas_call x16 -> x15, Pallas kernels: 12.4 us -> 12.4 us  [whole_call(): pl.pallas_call(body, out_shape=out_shape, in_specs=specs, out_specs=tuple...]
  transfers between devices with their start and end apart: 23 -> 24, of which waited for: 10 -> 8; matrix products, arithmetic and copies ran while one was open for 0% -> 0% of each run, Pallas kernels for 7% -> 7%
where the time goes in v13:
time: 76.8 us; the launch traced here: 76.5 us
  starting transfers between devices  26.1 us (34%)
  blocking collectives  20.2 us (26%)
  waiting for transfers between devices  15.8 us (21%)
  Pallas kernels  12.4 us (16%)
  local copies, waits for them, and re-layouts  1 us (1%)
  between operations  0.95 us (1%)
    ppermute x20, starting transfers between devices, shift(): return lax.ppermute(value, 'serve', partner(f, m, c))  21 us
    ppermute x20, waiting for transfers between devices, shift(): return lax.ppermute(value, 'serve', partner(f, m, c))  15.8 us
    pallas_call x15, Pallas kernels, whole_call(): pl.pallas_call(body, out_shape=out_shape, in_specs=specs, out_specs=tuple...  12.4 us
    all_to_all x1, blocking collectives, shards(): lax.all_to_all(ready, 'serve', split_axis=0, concat_axis=0, tiled=True)  10.7 us
    all_to_all x1, blocking collectives, shards(): lax.all_to_all(context, 'serve', split_axis=0, concat_axis=0, tiled=True)  9.48 us
    ppermute x4, starting transfers between devices, spread(): return lax.ppermute(value, 'serve', pairs)  5.04 us
  transfers between devices with their start and end apart: 24, of which 8 were waited for; matrix products, arithmetic and copies ran while one was open for 0% of the time, Pallas kernels for 7%

profile of v13, /device:TPU:0, one launch (start us, length us, event | category | flops | bytes accessed | tf_op | source)
XLA Modules:
  0.0 76.5 jit_solution(9241718098520889026)
XLA Ops:
  0.7 0.6 copy-done.10
  1.8 3.0 %collective-permute-start.3 = (bf16[1,4,8192]{2,1,0:T(4,128)(2,1)S(1)}, bf16[1,4,8192]{2,1,0:T(4,128)(2,1)S(1)}, u32[]{:S(2)}, u32[]{:S(2)}) collective-permute-start(bf16[1,4,8192]{2,1,0:T(4,128)(2,1)S(1)} %bitcast.24), channel_id=1, source_target_pairs={{0,2},{1,3},{2,0},{3,1},{4,6},{5,7},{6,4},{7,5},{8,10},{9,11},{10,... | collective-permute-start | bytes 196616 | tf_op jit(solution)/shard_map/ppermute | solution.py:445
  4.9 3.6 %collective-permute-start.2 = (bf16[1,4,8192]{2,1,0:T(4,128)(2,1)S(1)}, bf16[1,4,8192]{2,1,0:T(4,128)(2,1)S(1)}, u32[]{:S(2)}, u32[]{:S(2)}) collective-permute-start(bf16[1,4,8192]{2,1,0:T(4,128)(2,1)S(1)} %bitcast.25), channel_id=1, source_target_pairs={{0,12},{1,13},{2,14},{3,15},{4,0},{5,1},{6,2},{7,3},{8,4},{9,5},{1... | collective-permute-start | bytes 196616 | tf_op jit(solution)/shard_map/ppermute | solution.py:445
  8.5 1.0 %collective-permute-start = (bf16[1,4,8192]{2,1,0:T(4,128)(2,1)S(1)}, bf16[1,4,8192]{2,1,0:T(4,128)(2,1)S(1)}, u32[]{:S(2)}, u32[]{:S(2)}) collective-permute-start(bf16[1,4,8192]{2,1,0:T(4,128)(2,1)S(1)} %bitcast.27), channel_id=1, source_target_pairs={{0,4},{1,5},{2,6},{3,7},{4,8},{5,9},{6,10},{7,11},{8,12},{9,13},{1... | collective-permute-start | bytes 196616 | tf_op jit(solution)/shard_map/ppermute | solution.py:445
  9.5 5.1 %collective-permute-done = bf16[1,4,8192]{2,1,0:T(4,128)(2,1)S(1)} collective-permute-done((bf16[1,4,8192]{2,1,0:T(4,128)(2,1)S(1)}, bf16[1,4,8192]{2,1,0:T(4,128)(2,1)S(1)}, u32[]{:S(2)}, u32[]{:S(2)}) %collective-permute-start) | collective-permute-done | bytes 65568 | tf_op jit(solution)/shard_map/ppermute | solution.py:445
  14.8 0.6 collective-permute-start.4
  16.1 1.8 %shard_map.185 = (s32[64,1]{1,0:T(8,128)S(1)}, s32[64,1]{1,0:T(8,128)S(1)}, f32[64,128]{1,0:T(8,128)S(1)}, f32[64,128]{1,0:T(8,128)S(1)}, f32[64,128]{1,0:T(8,12...) custom-call(s32[1]{0:T(128)} %bitcast.index_ref, ...), custom_call_target="tpu_custom_call" | custom-call | flops 4600000000 | tf_op jit(solution)/shard_map/pallas_call | solution.py:36
  18.0 2.6 %collective-permute-done.4.refs_1_ = bf16[3,4,8192]{2,1,0:T(4,128)(2,1)S(1)} collective-permute-done((bf16[3,4,8192]{2,1,0:T(4,128)(2,1)S(1)}, bf16[3,4,8192]{2,1,0:T(4,128)(2,1)S(1)}, u32[]{:S(2)}, u32[]{:S(2)}) %collective-permute-start.4) | collective-permute-done | bytes 196640 | tf_op jit(solution)/shard_map/ppermute | solution.py:445
  20.6 1.4 %collective-permute-done.6.refs_3_ = bf16[3,4,8192]{2,1,0:T(4,128)(2,1)S(1)} collective-permute-done((bf16[3,4,8192]{2,1,0:T(4,128)(2,1)S(1)}, bf16[3,4,8192]{2,1,0:T(4,128)(2,1)S(1)}, u32[]{:S(2)}, u32[]{:S(2)}) %collective-permute-start.6) | collective-permute-done | bytes 196640 | tf_op jit(solution)/shard_map/ppermute | solution.py:445
  22.1 1.1 %shard_map.186 = (bf16[64,8192]{1,0:T(8,128)(2,1)S(1)}, bf16[16,128]{1,0:T(8,128)(2,1)S(1)}) custom-call(bf16[5,4,8192]{2,1,0:T(4,128)(2,1)S(1)} %constant_dynamic-update-slice_fusion.refs_0_, bf16[3,4,8192]{2,1,0:T(4,128)(2,1)S(1)} %collective-permute-done.4.refs_1_, bf16[5,4,8192]{2,1,0:T(4,128)(2,1)S(1)} %collective-permute-done.5.refs_2_, ...), custom_call_target="tpu_custom_call" | custom-call | flops 345000000 | tf_op jit(solution)/shard_map/pallas_call | solution.py:36
  23.2 1.8 %collective-permute-start.12 = (bf16[16,128]{1,0:T(8,128)(2,1)S(1)}, bf16[16,128]{1,0:T(8,128)(2,1)S(1)}, u32[]{:S(2)}, u32[]{:S(2)}) collective-permute-start(bf16[16,128]{1,0:T(8,128)(2,1)S(1)} %get-tuple-element.57.own_ref), channel_id=1, source_target_pairs={{0,12},{1,15},{2,14},{3,13},{4,0},{5,3},{6,2},{7,1},{8,4},{9,7},{1... | collective-permute-start | bytes 12296 | tf_op jit(solution)/shard_map/ppermute | solution.py:532
  25.1 0.6 collective-permute-start.11
  25.7 1.9 %collective-permute-start.10 = (bf16[16,128]{1,0:T(8,128)(2,1)S(1)}, bf16[16,128]{1,0:T(8,128)(2,1)S(1)}, u32[]{:S(2)}, u32[]{:S(2)}) collective-permute-start(bf16[16,128]{1,0:T(8,128)(2,1)S(1)} %get-tuple-element.57.own_ref), channel_id=1, source_target_pairs={{0,4},{1,7},{2,6},{3,5},{4,8},{5,11},{6,10},{7,9},{8,12},{9,15},{1... | collective-permute-start | bytes 12296 | tf_op jit(solution)/shard_map/ppermute | solution.py:532
  27.6 0.6 collective-permute-start.9
  28.4 2.7 %shard_map.187 = (f32[64,512]{1,0:T(8,128)S(1)}, f32[64,128]{1,0:T(8,128)S(1)}) custom-call(bf16[64,8192]{1,0:T(8,128)(2,1)S(1)} %get-tuple-element.58.x_ref, bf16[8192,512]{1,0:T(8,128)(2,1)S(1)} %bitcast.17, bf16[64,8192]{1,0:T(8,128)(2,1)S(1)} %bitcast.18, bf16[64,8192]{1,0:T(8,128)(2,1)S(1)} %bitcast.19), custom_call_target="tpu_custom_call" | custom-call | flops 690000000 | tf_op jit(solution)/shard_map/pallas_call | solution.py:36
  31.1 2.7 %collective-permute-start.13 = (bf16[16,128]{1,0:T(8,128)(2,1)S(1)}, bf16[16,128]{1,0:T(8,128)(2,1)S(1)}, u32[]{:S(2)}, u32[]{:S(2)}) collective-permute-start(bf16[16,128]{1,0:T(8,128)(2,1)S(1)} %shard_map.188.refs_0_), channel_id=1, source_target_pairs={{0,1},{1,0},{2,3},{3,2},{4,5},{5,4},{6,7},{7,6},{8,9},{9,8},{10,11... | collective-permute-start | bytes 12296 | tf_op jit(solution)/shard_map/ppermute | solution.py:445
  33.8 0.8 %collective-permute-done.13.refs_1_ = bf16[16,128]{1,0:T(8,128)(2,1)S(1)} collective-permute-done((bf16[16,128]{1,0:T(8,128)(2,1)S(1)}, bf16[16,128]{1,0:T(8,128)(2,1)S(1)}, u32[]{:S(2)}, u32[]{:S(2)}) %collective-permute-start.13) | collective-permute-done | bytes 4128 | tf_op jit(solution)/shard_map/ppermute | solution.py:445
  34.6 0.8 %shard_map.189 = bf16[16,24,128]{2,1,0:T(8,128)(2,1)S(1)} custom-call(bf16[16,128]{1,0:T(8,128)(2,1)S(1)} %shard_map.188.refs_0_, bf16[16,128]{1,0:T(8,128)(2,1)S(1)} %collective-permute-done.13.refs_1_, f32[64,512]{1,0:T(8,128)S(1)} %get-tuple-element.61.refs_2_, f32[64,128]{1,0:T(8,128)S(1)} %get-tuple-element.62.refs_3_, ...), custom_call_target="tpu_custom_call" | custom-call | flops 1035000000 | tf_op jit(solution)/shard_map/pallas_call | solution.py:36
  35.5 10.7 %all_to_all.10.x_ref = bf16[16,24,128]{2,1,0:T(8,128)(2,1)S(1)} all-to-all(bf16[16,24,128]{2,1,0:T(8,128)(2,1)S(1)} %shard_map.189), channel_id=1, replica_groups=mesh['replica'=2,'serve'=16] {'serve'}, dimensions={0} | all-to-all | bytes 196608 | tf_op jit(solution)/shard_map/all_to_all | solution.py:573
  46.2 2.0 %shard_map.190 = (bf16[2,2,1024]{2,1,0:T(2,128)(2,1)}, bf16[2,2,1024]{2,1,0:T(2,128)(2,1)}, bf16[16,16,128]{2,1,0:T(8,128)(2,1)S(1)}) custom-call(s32[1]{0:T(128)} %bitcast.index_ref, s32[32]{0:T(128)S(1)} %copy-done.13, bf16[16,24,128]{2,1,0:T(8,128)(2,1)S(1)} %all_to_all.10.x_ref, bf16[256,384]{1,0:T(8,128)(2,1)S(1)} %get-tuple-element.70.order_ref, ...), custom_call_target="tpu_custom_call" | custom-call | flops 1150000000 | tf_op jit(solution)/shard_map/pallas_call | solution.py:36
  48.2 9.5 %all_to_all.11.ctx_ref = bf16[16,16,128]{2,1,0:T(8,128)(2,1)S(1)} all-to-all(bf16[16,16,128]{2,1,0:T(8,128)(2,1)S(1)} %get-tuple-element.71), channel_id=1, replica_groups=mesh['replica'=2,'serve'=16] {'serve'}, dimensions={0} | all-to-all | bytes 131072 | tf_op jit(solution)/shard_map/all_to_all | solution.py:584
  57.7 1.7 %shard_map.191 = (bf16[64,512]{1,0:T(8,128)(2,1)S(1)}, f32[32,5120]{1,0:T(8,128)S(1)}, f32[32,5120]{1,0:T(8,128)S(1)}) custom-call(bf16[16,16,128]{2,1,0:T(8,128)(2,1)S(1)} %all_to_all.11.ctx_ref, bf16[256,256]{1,0:T(8,128)(2,1)S(1)} %get-tuple-element.72.take_ref, bf16[512,8192]{1,0:T(8,128)(2,1)S(1)} %bitcast.15), custom_call_target="tpu_custom_call" | custom-call | flops 460000000 | tf_op jit(solution)/shard_map/pallas_call | solution.py:36
  59.4 0.9 %shard_map.194 = (f32[32,3072]{1,0:T(8,128)S(1)}, f32[32,3072]{1,0:T(8,128)S(1)}) custom-call(bf16[64,512]{1,0:T(8,128)(2,1)S(1)} %get-tuple-element.81.a_ref, bf16[512,8192]{1,0:T(8,128)(2,1)S(1)} %bitcast.15), custom_call_target="tpu_custom_call" | custom-call | flops 345000000 | tf_op jit(solution)/shard_map/pallas_call | solution.py:36
  60.9 0.6 collective-permute-done.14.came_ref
  62.5 1.0 %collective-permute-start.21 = (bf16[8,3072]{1,0:T(8,128)(2,1)S(1)}, bf16[8,3072]{1,0:T(8,128)(2,1)S(1)}, u32[]{:S(2)}, u32[]{:S(2)}) collective-permute-start(bf16[8,3072]{1,0:T(8,128)(2,1)S(1)} %get-tuple-element.86), channel_id=1, source_target_pairs={{0,8},{1,9},{2,10},{3,11},{4,12},{5,13},{6,14},{7,15},{8,0},{9,1},... | collective-permute-start | bytes 147464 | tf_op jit(solution)/shard_map/ppermute | solution.py:445
  63.5 2.7 %collective-permute-start.22 = (bf16[8,3072]{1,0:T(8,128)(2,1)S(1)}, bf16[8,3072]{1,0:T(8,128)(2,1)S(1)}, u32[]{:S(2)}, u32[]{:S(2)}) collective-permute-start(bf16[8,3072]{1,0:T(8,128)(2,1)S(1)} %get-tuple-element.87), channel_id=1, source_target_pairs={{0,12},{1,13},{2,14},{3,15},{4,0},{5,1},{6,2},{7,3},{8,4},{9,5},{1... | collective-permute-start | bytes 147464 | tf_op jit(solution)/shard_map/ppermute | solution.py:445
  66.2 1.7 %collective-permute-done.15.refs_1_ = bf16[16,5120]{1,0:T(8,128)(2,1)S(1)} collective-permute-done((bf16[16,5120]{1,0:T(8,128)(2,1)S(1)}, bf16[16,5120]{1,0:T(8,128)(2,1)S(1)}, u32[]{:S(2)}, u32[]{:S(2)}) %collective-permute-start.15) | collective-permute-done | bytes 163872 | tf_op jit(solution)/shard_map/ppermute | solution.py:445
  68.1 0.9 %collective-permute-start.17 = (bf16[4,5120]{1,0:T(4,128)(2,1)S(1)}, bf16[4,5120]{1,0:T(4,128)(2,1)S(1)}, u32[]{:S(2)}, u32[]{:S(2)}) collective-permute-start(bf16[4,5120]{1,0:T(4,128)(2,1)S(1)} %get-tuple-element.79), channel_id=1, source_target_pairs={{0,8},{1,9},{2,10},{3,11},{4,12},{5,13},{6,14},{7,15},{8,0},{9,1},... | collective-permute-start | bytes 122888 | tf_op jit(solution)/shard_map/ppermute | solution.py:445
  69.1 2.8 %collective-permute-start.18 = (bf16[4,5120]{1,0:T(4,128)(2,1)S(1)}, bf16[4,5120]{1,0:T(4,128)(2,1)S(1)}, u32[]{:S(2)}, u32[]{:S(2)}) collective-permute-start(bf16[4,5120]{1,0:T(4,128)(2,1)S(1)} %get-tuple-element.80), channel_id=1, source_target_pairs={{0,12},{1,13},{2,14},{3,15},{4,0},{5,1},{6,2},{7,3},{8,4},{9,5},{1... | collective-permute-start | bytes 122888 | tf_op jit(solution)/shard_map/ppermute | solution.py:445
  71.9 0.9 %collective-permute-start.23 = (bf16[4,3072]{1,0:T(4,128)(2,1)S(1)}, bf16[4,3072]{1,0:T(4,128)(2,1)S(1)}, u32[]{:S(2)}, u32[]{:S(2)}) collective-permute-start(bf16[4,3072]{1,0:T(4,128)(2,1)S(1)} %get-tuple-element.89), channel_id=1, source_target_pairs={{0,2},{1,3},{2,0},{3,1},{4,6},{5,7},{6,4},{7,5},{8,10},{9,11},{10,... | collective-permute-start | bytes 73736 | tf_op jit(solution)/shard_map/ppermute | solution.py:445
  72.8 3.0 %collective-permute-done.23.refs_5_ = bf16[4,3072]{1,0:T(4,128)(2,1)S(1)} collective-permute-done((bf16[4,3072]{1,0:T(4,128)(2,1)S(1)}, bf16[4,3072]{1,0:T(4,128)(2,1)S(1)}, u32[]{:S(2)}, u32[]{:S(2)}) %collective-permute-start.23) | collective-permute-done | bytes 24608 | tf_op jit(solution)/shard_map/ppermute | solution.py:445
  75.8 0.7 shard_map.197
  (76 shorter events, 3.4 us)
Async XLA Ops:
  0.7 15.5 %copy-start.13 = (s32[32]{0:T(128)S(1)}, s32[32]{0:T(128)}, u32[]{:S(2)}) copy-start(s32[32]{0:T(128)} %len_ref.1) | copy-start | bytes 388
  0.7 15.4 %copy-start.12 = (s32[32]{0:T(128)S(1)}, s32[32]{0:T(128)}, u32[]{:S(2)}) copy-start(s32[32]{0:T(128)} %slot_hbm.1) | copy-start | bytes 388
  1.8 13.6 %collective-permute-start.3 = (bf16[1,4,8192]{2,1,0:T(4,128)(2,1)S(1)}, bf16[1,4,8192]{2,1,0:T(4,128)(2,1)S(1)}, u32[]{:S(2)}, u32[]{:S(2)}) collective-permute-start(bf16[1,4,8192]{2,1,0:T(4,128)(2,1)S(1)} %bitcast.24), channel_id=1, source_target_pairs={{0,2},{1,3},{2,0},{3,1},{4,6},{5,7},{6,4},{7,5},{8,10},{9,11},{10,... | collective-permute-start | bytes 196616 | tf_op jit(solution)/shard_map/ppermute | solution.py:445
  4.9 9.9 %collective-permute-start.2 = (bf16[1,4,8192]{2,1,0:T(4,128)(2,1)S(1)}, bf16[1,4,8192]{2,1,0:T(4,128)(2,1)S(1)}, u32[]{:S(2)}, u32[]{:S(2)}) collective-permute-start(bf16[1,4,8192]{2,1,0:T(4,128)(2,1)S(1)} %bitcast.25), channel_id=1, source_target_pairs={{0,12},{1,13},{2,14},{3,15},{4,0},{5,1},{6,2},{7,3},{8,4},{9,5},{1... | collective-permute-start | bytes 196616 | tf_op jit(solution)/shard_map/ppermute | solution.py:445
  8.5 6.2 %collective-permute-start.1 = (bf16[1,4,8192]{2,1,0:T(4,128)(2,1)S(1)}, bf16[1,4,8192]{2,1,0:T(4,128)(2,1)S(1)}, u32[]{:S(2)}, u32[]{:S(2)}) collective-permute-start(bf16[1,4,8192]{2,1,0:T(4,128)(2,1)S(1)} %bitcast.26), channel_id=1, source_target_pairs={{0,8},{1,9},{2,10},{3,11},{4,12},{5,13},{6,14},{7,15},{8,0},{9,1},... | collective-permute-start | bytes 196616 | tf_op jit(solution)/shard_map/ppermute | solution.py:445
  8.5 6.2 %collective-permute-start = (bf16[1,4,8192]{2,1,0:T(4,128)(2,1)S(1)}, bf16[1,4,8192]{2,1,0:T(4,128)(2,1)S(1)}, u32[]{:S(2)}, u32[]{:S(2)}) collective-permute-start(bf16[1,4,8192]{2,1,0:T(4,128)(2,1)S(1)} %bitcast.27), channel_id=1, source_target_pairs={{0,4},{1,5},{2,6},{3,7},{4,8},{5,9},{6,10},{7,11},{8,12},{9,13},{1... | collective-permute-start | bytes 196616 | tf_op jit(solution)/shard_map/ppermute | solution.py:445
  14.8 5.8 %collective-permute-start.4 = (bf16[3,4,8192]{2,1,0:T(4,128)(2,1)S(1)}, bf16[3,4,8192]{2,1,0:T(4,128)(2,1)S(1)}, u32[]{:S(2)}, u32[]{:S(2)}) collective-permute-start(bf16[3,4,8192]{2,1,0:T(4,128)(2,1)S(1)} %get-tuple-element.94), channel_id=1, source_target_pairs={{0,2},{1,3},{2,0},{3,1},{4,6},{5,7},{6,4},{7,5},{8,10},{9,11},{10,... | collective-permute-start | bytes 589832 | tf_op jit(solution)/shard_map/ppermute | solution.py:445
  15.5 5.2 %collective-permute-start.5 = (bf16[5,4,8192]{2,1,0:T(4,128)(2,1)S(1)}, bf16[5,4,8192]{2,1,0:T(4,128)(2,1)S(1)}, u32[]{:S(2)}, u32[]{:S(2)}) collective-permute-start(bf16[5,4,8192]{2,1,0:T(4,128)(2,1)S(1)} %constant_dynamic-update-slice_fusion.refs_0_), channel_id=1, source_target_pairs={{0,1},{1,0},{2,3},{3,2},{4,5},{5,4},{6,7},{7,6},{8,9},{9,8},{10,11... | collective-permute-start | bytes 983048 | tf_op jit(solution)/shard_map/ppermute | solution.py:445
  15.6 6.5 %collective-permute-start.7 = (bf16[32,8192]{1,0:T(8,128)(2,1)S(1)}, bf16[32,8192]{1,0:T(8,128)(2,1)S(1)}, u32[]{:S(2)}, u32[]{:S(2)}) collective-permute-start(bf16[32,8192]{1,0:T(8,128)(2,1)S(1)} %bitcast.20), channel_id=1, source_target_pairs={{0,1},{1,0},{2,3},{3,2},{4,5},{5,4},{6,7},{7,6},{8,9},{9,8},{10,11... | collective-permute-start | bytes 1572872 | tf_op jit(solution)/shard_map/ppermute | solution.py:445
  16.0 6.0 %collective-permute-start.8 = (bf16[32,8192]{1,0:T(8,128)(2,1)S(1)}, bf16[32,8192]{1,0:T(8,128)(2,1)S(1)}, u32[]{:S(2)}, u32[]{:S(2)}) collective-permute-start(bf16[32,8192]{1,0:T(8,128)(2,1)S(1)} %bitcast.22), channel_id=1, source_target_pairs={{0,1},{1,0},{2,3},{3,2},{4,5},{5,4},{6,7},{7,6},{8,9},{9,8},{10,11... | collective-permute-start | bytes 1572872 | tf_op jit(solution)/shard_map/ppermute | solution.py:445
  18.0 16.6 %copy-start.6 = (bf16[32,16,512]{2,1,0:T(8,128)(2,1)S(1)}, bf16[32,16,512]{2,1,0:T(8,128)(2,1)}, u32[]{:S(2)}) copy-start(bf16[32,16,512]{2,1,0:T(8,128)(2,1)} %param.25) | copy-start | bytes 1572868
  18.0 16.6 %copy-start.7 = (bf16[32,16,64]{2,1,0:T(8,128)(2,1)S(1)}, bf16[32,16,64]{2,1,0:T(8,128)(2,1)}, u32[]{:S(2)}) copy-start(bf16[32,16,64]{2,1,0:T(8,128)(2,1)} %param.26) | copy-start | bytes 196612
  20.6 1.4 %collective-permute-start.6 = (bf16[3,4,8192]{2,1,0:T(4,128)(2,1)S(1)}, bf16[3,4,8192]{2,1,0:T(4,128)(2,1)S(1)}, u32[]{:S(2)}, u32[]{:S(2)}) collective-permute-start(bf16[3,4,8192]{2,1,0:T(4,128)(2,1)S(1)} %collective-permute-done.4.refs_1_), channel_id=1, source_target_pairs={{0,1},{1,0},{2,3},{3,2},{4,5},{5,4},{6,7},{7,6},{8,9},{9,8},{10,11... | collective-permute-start | bytes 589832 | tf_op jit(solution)/shard_map/ppermute | solution.py:445
  23.2 23.0 %copy-start.4 = (bf16[2,384,1024]{2,1,0:T(8,128)(2,1)S(1)}, bf16[2,384,1024]{2,1,0:T(8,128)(2,1)}, u32[]{:S(2)}) copy-start(bf16[2,384,1024]{2,1,0:T(8,128)(2,1)} %k_ref.1) | copy-start | bytes 4718596
  23.2 23.0 %copy-start.5 = (bf16[2,384,1024]{2,1,0:T(8,128)(2,1)S(1)}, bf16[2,384,1024]{2,1,0:T(8,128)(2,1)}, u32[]{:S(2)}) copy-start(bf16[2,384,1024]{2,1,0:T(8,128)(2,1)} %v_ref.1) | copy-start | bytes 4718596
  23.2 7.8 %collective-permute-start.12 = (bf16[16,128]{1,0:T(8,128)(2,1)S(1)}, bf16[16,128]{1,0:T(8,128)(2,1)S(1)}, u32[]{:S(2)}, u32[]{:S(2)}) collective-permute-start(bf16[16,128]{1,0:T(8,128)(2,1)S(1)} %get-tuple-element.57.own_ref), channel_id=1, source_target_pairs={{0,12},{1,15},{2,14},{3,13},{4,0},{5,3},{6,2},{7,1},{8,4},{9,7},{1... | collective-permute-start | bytes 12296 | tf_op jit(solution)/shard_map/ppermute | solution.py:532
  25.1 6.0 %collective-permute-start.11 = (bf16[16,128]{1,0:T(8,128)(2,1)S(1)}, bf16[16,128]{1,0:T(8,128)(2,1)S(1)}, u32[]{:S(2)}, u32[]{:S(2)}) collective-permute-start(bf16[16,128]{1,0:T(8,128)(2,1)S(1)} %get-tuple-element.57.own_ref), channel_id=1, source_target_pairs={{0,8},{1,11},{2,10},{3,9},{4,12},{5,15},{6,14},{7,13},{8,0},{9,3},... | collective-permute-start | bytes 12296 | tf_op jit(solution)/shard_map/ppermute | solution.py:532
  25.7 5.4 %collective-permute-start.10 = (bf16[16,128]{1,0:T(8,128)(2,1)S(1)}, bf16[16,128]{1,0:T(8,128)(2,1)S(1)}, u32[]{:S(2)}, u32[]{:S(2)}) collective-permute-start(bf16[16,128]{1,0:T(8,128)(2,1)S(1)} %get-tuple-element.57.own_ref), channel_id=1, source_target_pairs={{0,4},{1,7},{2,6},{3,5},{4,8},{5,11},{6,10},{7,9},{8,12},{9,15},{1... | collective-permute-start | bytes 12296 | tf_op jit(solution)/shard_map/ppermute | solution.py:532
  27.6 3.4 %collective-permute-start.9 = (bf16[16,128]{1,0:T(8,128)(2,1)S(1)}, bf16[16,128]{1,0:T(8,128)(2,1)S(1)}, u32[]{:S(2)}, u32[]{:S(2)}) collective-permute-start(bf16[16,128]{1,0:T(8,128)(2,1)S(1)} %get-tuple-element.57.own_ref), channel_id=1, source_target_pairs={{1,3},{3,1},{5,7},{7,5},{9,11},{11,9},{13,15},{15,13},{17,19},{19,... | collective-permute-start | bytes 12296 | tf_op jit(solution)/shard_map/ppermute | solution.py:532
  28.3 29.4 %slice-start = ((s8[8388608]{0:T(1024)(128)(4,1)}), s8[4194304]{0:T(1024)(128)(4,1)S(1)}, s32[]{:S(2)}) async-start(s8[8388608]{0:T(1024)(128)(4,1)} %bitcast.14), calls=%async_computation.2 | async-start | bytes 8388608
  28.3 29.3 %slice-start.1 = ((s8[8388608]{0:T(1024)(128)(4,1)}), s8[4194304]{0:T(1024)(128)(4,1)S(1)}, s32[]{:S(2)}) async-start(s8[8388608]{0:T(1024)(128)(4,1)} %bitcast.14), calls=%async_computation.3 | async-start | bytes 8388608
  31.1 3.5 %collective-permute-start.13 = (bf16[16,128]{1,0:T(8,128)(2,1)S(1)}, bf16[16,128]{1,0:T(8,128)(2,1)S(1)}, u32[]{:S(2)}, u32[]{:S(2)}) collective-permute-start(bf16[16,128]{1,0:T(8,128)(2,1)S(1)} %shard_map.188.refs_0_), channel_id=1, source_target_pairs={{0,1},{1,0},{2,3},{3,2},{4,5},{5,4},{6,7},{7,6},{8,9},{9,8},{10,11... | collective-permute-start | bytes 12296 | tf_op jit(solution)/shard_map/ppermute | solution.py:445
  59.4 2.2 %collective-permute-start.14 = (f32[32,5120]{1,0:T(8,128)S(1)}, f32[32,5120]{1,0:T(8,128)S(1)}, u32[]{:S(2)}, u32[]{:S(2)}) collective-permute-start(f32[32,5120]{1,0:T(8,128)S(1)} %get-tuple-element.74), channel_id=1, source_target_pairs={{0,1},{1,0},{2,3},{3,2},{4,5},{5,4},{6,7},{7,6},{8,9},{9,8},{10,11... | collective-permute-start | bytes 1966088 | tf_op jit(solution)/shard_map/ppermute | solution.py:445
  60.4 1.9 %collective-permute-start.19 = (f32[32,3072]{1,0:T(8,128)S(1)}, f32[32,3072]{1,0:T(8,128)S(1)}, u32[]{:S(2)}, u32[]{:S(2)}) collective-permute-start(f32[32,3072]{1,0:T(8,128)S(1)} %get-tuple-element.83), channel_id=1, source_target_pairs={{0,1},{1,0},{2,3},{3,2},{4,5},{5,4},{6,7},{7,6},{8,9},{9,8},{10,11... | collective-permute-start | bytes 1179656 | tf_op jit(solution)/shard_map/ppermute | solution.py:445
  61.6 6.3 %collective-permute-start.15 = (bf16[16,5120]{1,0:T(8,128)(2,1)S(1)}, bf16[16,5120]{1,0:T(8,128)(2,1)S(1)}, u32[]{:S(2)}, u32[]{:S(2)}) collective-permute-start(bf16[16,5120]{1,0:T(8,128)(2,1)S(1)} %get-tuple-element.76), channel_id=1, source_target_pairs={{0,2},{1,3},{2,0},{3,1},{4,6},{5,7},{6,4},{7,5},{8,10},{9,11},{10,... | collective-permute-start | bytes 491528 | tf_op jit(solution)/shard_map/ppermute | solution.py:445
  62.3 6.8 %collective-permute-start.20 = (bf16[8,3072]{1,0:T(8,128)(2,1)S(1)}, bf16[8,3072]{1,0:T(8,128)(2,1)S(1)}, u32[]{:S(2)}, u32[]{:S(2)}) collective-permute-start(bf16[8,3072]{1,0:T(8,128)(2,1)S(1)} %get-tuple-element.85), channel_id=1, source_target_pairs={{0,4},{1,5},{2,6},{3,7},{4,8},{5,9},{6,10},{7,11},{8,12},{9,13},{1... | collective-permute-start | bytes 147464 | tf_op jit(solution)/shard_map/ppermute | solution.py:445
  62.5 9.3 %collective-permute-start.21 = (bf16[8,3072]{1,0:T(8,128)(2,1)S(1)}, bf16[8,3072]{1,0:T(8,128)(2,1)S(1)}, u32[]{:S(2)}, u32[]{:S(2)}) collective-permute-start(bf16[8,3072]{1,0:T(8,128)(2,1)S(1)} %get-tuple-element.86), channel_id=1, source_target_pairs={{0,8},{1,9},{2,10},{3,11},{4,12},{5,13},{6,14},{7,15},{8,0},{9,1},... | collective-permute-start | bytes 147464 | tf_op jit(solution)/shard_map/ppermute | solution.py:445
  63.5 8.3 %collective-permute-start.22 = (bf16[8,3072]{1,0:T(8,128)(2,1)S(1)}, bf16[8,3072]{1,0:T(8,128)(2,1)S(1)}, u32[]{:S(2)}, u32[]{:S(2)}) collective-permute-start(bf16[8,3072]{1,0:T(8,128)(2,1)S(1)} %get-tuple-element.87), channel_id=1, source_target_pairs={{0,12},{1,13},{2,14},{3,15},{4,0},{5,1},{6,2},{7,3},{8,4},{9,5},{1... | collective-permute-start | bytes 147464 | tf_op jit(solution)/shard_map/ppermute | solution.py:445
  68.0 7.8 %collective-permute-start.16 = (bf16[4,5120]{1,0:T(4,128)(2,1)S(1)}, bf16[4,5120]{1,0:T(4,128)(2,1)S(1)}, u32[]{:S(2)}, u32[]{:S(2)}) collective-permute-start(bf16[4,5120]{1,0:T(4,128)(2,1)S(1)} %get-tuple-element.78), channel_id=1, source_target_pairs={{0,4},{1,5},{2,6},{3,7},{4,8},{5,9},{6,10},{7,11},{8,12},{9,13},{1... | collective-permute-start | bytes 122888 | tf_op jit(solution)/shard_map/ppermute | solution.py:445
  68.1 7.6 %collective-permute-start.17 = (bf16[4,5120]{1,0:T(4,128)(2,1)S(1)}, bf16[4,5120]{1,0:T(4,128)(2,1)S(1)}, u32[]{:S(2)}, u32[]{:S(2)}) collective-permute-start(bf16[4,5120]{1,0:T(4,128)(2,1)S(1)} %get-tuple-element.79), channel_id=1, source_target_pairs={{0,8},{1,9},{2,10},{3,11},{4,12},{5,13},{6,14},{7,15},{8,0},{9,1},... | collective-permute-start | bytes 122888 | tf_op jit(solution)/shard_map/ppermute | solution.py:445
  69.1 6.7 %collective-permute-start.18 = (bf16[4,5120]{1,0:T(4,128)(2,1)S(1)}, bf16[4,5120]{1,0:T(4,128)(2,1)S(1)}, u32[]{:S(2)}, u32[]{:S(2)}) collective-permute-start(bf16[4,5120]{1,0:T(4,128)(2,1)S(1)} %get-tuple-element.80), channel_id=1, source_target_pairs={{0,12},{1,13},{2,14},{3,15},{4,0},{5,1},{6,2},{7,3},{8,4},{9,5},{1... | collective-permute-start | bytes 122888 | tf_op jit(solution)/shard_map/ppermute | solution.py:445
  71.9 3.9 %collective-permute-start.23 = (bf16[4,3072]{1,0:T(4,128)(2,1)S(1)}, bf16[4,3072]{1,0:T(4,128)(2,1)S(1)}, u32[]{:S(2)}, u32[]{:S(2)}) collective-permute-start(bf16[4,3072]{1,0:T(4,128)(2,1)S(1)} %get-tuple-element.89), channel_id=1, source_target_pairs={{0,2},{1,3},{2,0},{3,1},{4,6},{5,7},{6,4},{7,5},{8,10},{9,11},{10,... | collective-permute-start | bytes 73736 | tf_op jit(solution)/shard_map/ppermute | solution.py:445
  (10 other events, 99.5 us)

commit v14 on v8

--- a/solution.py
+++ b/solution.py
@@ -301,31 +301,41 @@
     for b in range(own):
         q = queries[b * KV_HEADS * mine : (b + 1) * KV_HEADS * mine]
         cached, newer = [], []
-        for g in range(KV_HEADS):
-            qg = q[g * mine : (g + 1) * mine]
-            cached.append(dot_nt(qg, k_ref[b, :, g * HEAD : (g + 1) * HEAD]))
-            newer.append(dot_nt(qg, keys[g]))
-        cached = jnp.concatenate(cached, axis=0) * scale
-        newer = jnp.concatenate(newer, axis=0) * scale
-        place = lax.broadcasted_iota(jnp.int32, cached.shape, 1)
+        for g in range(0, KV_HEADS, 2):
+            one, two = q[g * mine : (g + 1) * mine], q[(g + 1) * mine : (g + 2) * mine]
+            none = jnp.zeros_like(one)
+            pair = jnp.concatenate(
+                (jnp.concatenate((one, none), axis=1), jnp.concatenate((none, two), axis=1)),
+                axis=0,
+            )
+            cached.append(dot_nt(k_ref[b, :, g * HEAD : (g + 2) * HEAD], pair))
+            newer.append(dot_nt(jnp.concatenate(keys[g : g + 2], axis=1), pair))
+        cached = jnp.concatenate(cached, axis=1) * scale
+        newer = jnp.concatenate(newer, axis=1) * scale
+        place = lax.broadcasted_iota(jnp.int32, cached.shape, 0)
         cached = jnp.where(place < len_ref[index_ref[0] * own + b], cached, -1e30)
-        step = lax.broadcasted_iota(jnp.int32, newer.shape, 0) % STEPS
-        at = lax.broadcasted_iota(jnp.int32, newer.shape, 1) - b * STEPS
+        step = lax.broadcasted_iota(jnp.int32, newer.shape, 1) % STEPS
+        at = lax.broadcasted_iota(jnp.int32, newer.shape, 0) - b * STEPS
         newer = jnp.where((at >= 0) & (at <= step), newer, -1e30)
         top = jnp.maximum(
-            jnp.max(cached, axis=1, keepdims=True), jnp.max(newer, axis=1, keepdims=True)
+            jnp.max(cached, axis=0, keepdims=True), jnp.max(newer, axis=0, keepdims=True)
         )
         cached = jnp.exp(cached - top)
         newer = jnp.exp(newer - top)
-        total = jnp.sum(cached, axis=1, keepdims=True) + jnp.sum(newer, axis=1, keepdims=True)
-        cached = (cached / total).astype(BF16)
-        newer = (newer / total).astype(BF16)
-        for g in range(KV_HEADS):
-            at_rows = slice(g * mine, (g + 1) * mine)
-            part = dot(cached[at_rows], v_ref[b, :, g * HEAD : (g + 1) * HEAD])
-            s_ref[(b * KV_HEADS + g) * mine : (b * KV_HEADS + g + 1) * mine] = part + dot(
-                newer[at_rows], values[g]
-            )
+        total = jnp.sum(cached, axis=0, keepdims=True) + jnp.sum(newer, axis=0, keepdims=True)
+        share = 1.0 / total
+        newer = jnp.concatenate(
+            (newer, jnp.zeros((HEAD - newer.shape[0], newer.shape[1]), F32)), axis=0
+        )
+        cached = (cached * share).T.astype(BF16)
+        newer = (newer * share).T.astype(BF16)[:, : 16]
+        for g in range(0, KV_HEADS, 2):
+            at_rows = slice(g * mine, (g + 2) * mine)
+            part = dot(cached[at_rows], v_ref[b, :, g * HEAD : (g + 2) * HEAD])
+            part = part + dot(newer[at_rows], jnp.concatenate(values[g : g + 2], axis=1))
+            at = (b * KV_HEADS + g) * mine
+            s_ref[at : at + mine] = part[:mine, :HEAD]
+            s_ref[at + mine : at + 2 * mine] = part[mine:, HEAD:]
     step = local * STEPS
     half = KV_HEADS * mine
     for i in range(n):

time: 76.2 us -> 76.4 us (level)
  no operation moved by 1% of the time
where the time goes in v14:
time: 76.4 us; the launch traced here: 76.1 us
  starting transfers between devices  24 us (31%)
  blocking collectives  19.6 us (26%)
  waiting for transfers between devices  18.3 us (24%)
  Pallas kernels  12.2 us (16%)
  local copies, waits for them, and re-layouts  1.02 us (1%)
  between operations  0.96 us (1%)
    ppermute x23, starting transfers between devices, shift(): return lax.ppermute(value, 'serve', partner(f, m, c))  24 us
    ppermute x23, waiting for transfers between devices, shift(): return lax.ppermute(value, 'serve', partner(f, m, c))  18.3 us
    pallas_call x16, Pallas kernels, whole_call(): pl.pallas_call(body, out_shape=out_shape, in_specs=specs, out_specs=tuple...  12.2 us
    all_to_all x1, blocking collectives, shards(): lax.all_to_all(ready, 'serve', split_axis=0, concat_axis=0, tiled=True)  10.1 us
    all_to_all x1, blocking collectives, shards(): lax.all_to_all(context, 'serve', split_axis=0, concat_axis=0, tiled=True)  9.48 us
  transfers between devices with their start and end apart: 23, of which 10 were waited for; matrix products, arithmetic and copies ran while one was open for 0% of the time, Pallas kernels for 7%

profile of v14, /device:TPU:0, one launch (start us, length us, event | category | flops | bytes accessed | tf_op | source)
XLA Modules:
  0.0 76.1 jit_solution(11167008305363532174)
XLA Ops:
  0.7 0.6 copy-done.10
  1.8 3.0 %collective-permute-start.3 = (bf16[1,4,8192]{2,1,0:T(4,128)(2,1)S(1)}, bf16[1,4,8192]{2,1,0:T(4,128)(2,1)S(1)}, u32[]{:S(2)}, u32[]{:S(2)}) collective-permute-start(bf16[1,4,8192]{2,1,0:T(4,128)(2,1)S(1)} %bitcast.24), channel_id=1, source_target_pairs={{0,2},{1,3},{2,0},{3,1},{4,6},{5,7},{6,4},{7,5},{8,10},{9,11},{10,... | collective-permute-start | bytes 196616 | tf_op jit(solution)/shard_map/ppermute | solution.py:450
  4.9 3.6 %collective-permute-start.2 = (bf16[1,4,8192]{2,1,0:T(4,128)(2,1)S(1)}, bf16[1,4,8192]{2,1,0:T(4,128)(2,1)S(1)}, u32[]{:S(2)}, u32[]{:S(2)}) collective-permute-start(bf16[1,4,8192]{2,1,0:T(4,128)(2,1)S(1)} %bitcast.25), channel_id=1, source_target_pairs={{0,12},{1,13},{2,14},{3,15},{4,0},{5,1},{6,2},{7,3},{8,4},{9,5},{1... | collective-permute-start | bytes 196616 | tf_op jit(solution)/shard_map/ppermute | solution.py:450
  8.5 1.0 %collective-permute-start = (bf16[1,4,8192]{2,1,0:T(4,128)(2,1)S(1)}, bf16[1,4,8192]{2,1,0:T(4,128)(2,1)S(1)}, u32[]{:S(2)}, u32[]{:S(2)}) collective-permute-start(bf16[1,4,8192]{2,1,0:T(4,128)(2,1)S(1)} %bitcast.27), channel_id=1, source_target_pairs={{0,4},{1,5},{2,6},{3,7},{4,8},{5,9},{6,10},{7,11},{8,12},{9,13},{1... | collective-permute-start | bytes 196616 | tf_op jit(solution)/shard_map/ppermute | solution.py:450
  9.5 5.1 %collective-permute-done = bf16[1,4,8192]{2,1,0:T(4,128)(2,1)S(1)} collective-permute-done((bf16[1,4,8192]{2,1,0:T(4,128)(2,1)S(1)}, bf16[1,4,8192]{2,1,0:T(4,128)(2,1)S(1)}, u32[]{:S(2)}, u32[]{:S(2)}) %collective-permute-start) | collective-permute-done | bytes 65568 | tf_op jit(solution)/shard_map/ppermute | solution.py:450
  15.6 1.8 %shard_map.185 = (s32[64,1]{1,0:T(8,128)S(1)}, s32[64,1]{1,0:T(8,128)S(1)}, f32[64,128]{1,0:T(8,128)S(1)}, f32[64,128]{1,0:T(8,128)S(1)}, f32[64,128]{1,0:T(8,12...) custom-call(s32[1]{0:T(128)} %bitcast.index_ref, ...), custom_call_target="tpu_custom_call" | custom-call | flops 4600000000 | tf_op jit(solution)/shard_map/pallas_call | solution.py:36
  17.4 3.2 %collective-permute-done.4.refs_1_ = bf16[3,4,8192]{2,1,0:T(4,128)(2,1)S(1)} collective-permute-done((bf16[3,4,8192]{2,1,0:T(4,128)(2,1)S(1)}, bf16[3,4,8192]{2,1,0:T(4,128)(2,1)S(1)}, u32[]{:S(2)}, u32[]{:S(2)}) %collective-permute-start.4) | collective-permute-done | bytes 196640 | tf_op jit(solution)/shard_map/ppermute | solution.py:450
  20.6 1.4 %collective-permute-done.6.refs_3_ = bf16[3,4,8192]{2,1,0:T(4,128)(2,1)S(1)} collective-permute-done((bf16[3,4,8192]{2,1,0:T(4,128)(2,1)S(1)}, bf16[3,4,8192]{2,1,0:T(4,128)(2,1)S(1)}, u32[]{:S(2)}, u32[]{:S(2)}) %collective-permute-start.6) | collective-permute-done | bytes 196640 | tf_op jit(solution)/shard_map/ppermute | solution.py:450
  22.1 0.7 shard_map.186
  23.1 1.5 %collective-permute-start.8 = (bf16[16,128]{1,0:T(8,128)(2,1)S(1)}, bf16[16,128]{1,0:T(8,128)(2,1)S(1)}, u32[]{:S(2)}, u32[]{:S(2)}) collective-permute-start(bf16[16,128]{1,0:T(8,128)(2,1)S(1)} %get-tuple-element.57.refs_0_), channel_id=1, source_target_pairs={{0,2},{1,3},{2,0},{3,1},{4,6},{5,7},{6,4},{7,5},{8,10},{9,11},{10,... | collective-permute-start | bytes 12296 | tf_op jit(solution)/shard_map/ppermute | solution.py:450
  24.7 1.3 %shard_map.188 = (f32[64,512]{1,0:T(8,128)S(1)}, f32[64,128]{1,0:T(8,128)S(1)}) custom-call(bf16[64,8192]{1,0:T(8,128)(2,1)S(1)} %get-tuple-element.58.x_ref, bf16[8192,512]{1,0:T(8,128)(2,1)S(1)} %bitcast.15, bf16[64,8192]{1,0:T(8,128)(2,1)S(1)} %bitcast.18, bf16[64,8192]{1,0:T(8,128)(2,1)S(1)} %bitcast.20), custom_call_target="tpu_custom_call" | custom-call | flops 345000000 | tf_op jit(solution)/shard_map/pallas_call | solution.py:36
  26.1 0.6 collective-permute-done.8.refs_2_
  26.7 1.8 %collective-permute-start.12 = (bf16[16,128]{1,0:T(8,128)(2,1)S(1)}, bf16[16,128]{1,0:T(8,128)(2,1)S(1)}, u32[]{:S(2)}, u32[]{:S(2)}) collective-permute-start(bf16[16,128]{1,0:T(8,128)(2,1)S(1)} %shard_map.187.refs_0_), channel_id=1, source_target_pairs={{0,12},{1,13},{2,14},{3,15},{4,0},{5,1},{6,2},{7,3},{8,4},{9,5},{1... | collective-permute-start | bytes 12296 | tf_op jit(solution)/shard_map/ppermute | solution.py:450
  28.6 0.6 collective-permute-start.11
  29.2 1.9 %collective-permute-start.10 = (bf16[16,128]{1,0:T(8,128)(2,1)S(1)}, bf16[16,128]{1,0:T(8,128)(2,1)S(1)}, u32[]{:S(2)}, u32[]{:S(2)}) collective-permute-start(bf16[16,128]{1,0:T(8,128)(2,1)S(1)} %shard_map.187.refs_0_), channel_id=1, source_target_pairs={{0,4},{1,5},{2,6},{3,7},{4,8},{5,9},{6,10},{7,11},{8,12},{9,13},{1... | collective-permute-start | bytes 12296 | tf_op jit(solution)/shard_map/ppermute | solution.py:450
  31.1 1.3 %shard_map.189 = (f32[64,512]{1,0:T(8,128)S(1)}, f32[64,128]{1,0:T(8,128)S(1)}) custom-call(bf16[64,8192]{1,0:T(8,128)(2,1)S(1)} %get-tuple-element.58.x_ref, bf16[8192,512]{1,0:T(8,128)(2,1)S(1)} %bitcast.15, bf16[64,8192]{1,0:T(8,128)(2,1)S(1)} %bitcast.19, bf16[64,8192]{1,0:T(8,128)(2,1)S(1)} %bitcast.21), custom_call_target="tpu_custom_call" | custom-call | flops 345000000 | tf_op jit(solution)/shard_map/pallas_call | solution.py:36
  33.1 1.5 %collective-permute-done.10.refs_1_ = bf16[16,128]{1,0:T(8,128)(2,1)S(1)} collective-permute-done((bf16[16,128]{1,0:T(8,128)(2,1)S(1)}, bf16[16,128]{1,0:T(8,128)(2,1)S(1)}, u32[]{:S(2)}, u32[]{:S(2)}) %collective-permute-start.10) | collective-permute-done | bytes 4128 | tf_op jit(solution)/shard_map/ppermute | solution.py:450
  34.6 0.8 %shard_map.190 = bf16[16,24,128]{2,1,0:T(8,128)(2,1)S(1)} custom-call(bf16[16,128]{1,0:T(8,128)(2,1)S(1)} %shard_map.187.refs_0_, bf16[16,128]{1,0:T(8,128)(2,1)S(1)} %collective-permute-done.10.refs_1_, bf16[16,128]{1,0:T(8,128)(2,1)S(1)} %collective-permute-done.11.refs_2_, bf16[16,128]{1,0:T(8,128)(2,1)S(1)} %collective-permute-done.12.refs_3_, ...), custom_call_target="tpu_custom_call" | custom-call | flops 1035000000 | tf_op jit(solution)/shard_map/pallas_call | solution.py:36
  35.4 10.1 %all_to_all.10.x_ref = bf16[16,24,128]{2,1,0:T(8,128)(2,1)S(1)} all-to-all(bf16[16,24,128]{2,1,0:T(8,128)(2,1)S(1)} %shard_map.190), channel_id=1, replica_groups=mesh['replica'=2,'serve'=16] {'serve'}, dimensions={0} | all-to-all | bytes 196608 | tf_op jit(solution)/shard_map/all_to_all | solution.py:558
  45.6 2.2 %shard_map.191 = (bf16[2,2,1024]{2,1,0:T(2,128)(2,1)}, bf16[2,2,1024]{2,1,0:T(2,128)(2,1)}, bf16[16,16,128]{2,1,0:T(8,128)(2,1)S(1)}) custom-call(s32[1]{0:T(128)} %bitcast.index_ref, s32[32]{0:T(128)S(1)} %copy-done.13, bf16[16,24,128]{2,1,0:T(8,128)(2,1)S(1)} %all_to_all.10.x_ref, bf16[256,384]{1,0:T(8,128)(2,1)S(1)} %get-tuple-element.72.order_ref, ...), custom_call_target="tpu_custom_call" | custom-call | flops 1150000000 | tf_op jit(solution)/shard_map/pallas_call | solution.py:36
  47.8 9.5 %all_to_all.11.ctx_ref = bf16[16,16,128]{2,1,0:T(8,128)(2,1)S(1)} all-to-all(bf16[16,16,128]{2,1,0:T(8,128)(2,1)S(1)} %get-tuple-element.73), channel_id=1, replica_groups=mesh['replica'=2,'serve'=16] {'serve'}, dimensions={0} | all-to-all | bytes 131072 | tf_op jit(solution)/shard_map/all_to_all | solution.py:569
  57.3 1.7 %shard_map.192 = (bf16[64,512]{1,0:T(8,128)(2,1)S(1)}, f32[32,5120]{1,0:T(8,128)S(1)}, f32[32,5120]{1,0:T(8,128)S(1)}) custom-call(bf16[16,16,128]{2,1,0:T(8,128)(2,1)S(1)} %all_to_all.11.ctx_ref, bf16[256,256]{1,0:T(8,128)(2,1)S(1)} %get-tuple-element.74.take_ref, bf16[512,8192]{1,0:T(8,128)(2,1)S(1)} %bitcast.17), custom_call_target="tpu_custom_call" | custom-call | flops 460000000 | tf_op jit(solution)/shard_map/pallas_call | solution.py:36
  59.0 0.9 %shard_map.195 = (f32[32,3072]{1,0:T(8,128)S(1)}, f32[32,3072]{1,0:T(8,128)S(1)}) custom-call(bf16[64,512]{1,0:T(8,128)(2,1)S(1)} %get-tuple-element.83.a_ref, bf16[512,8192]{1,0:T(8,128)(2,1)S(1)} %bitcast.17), custom_call_target="tpu_custom_call" | custom-call | flops 345000000 | tf_op jit(solution)/shard_map/pallas_call | solution.py:36
  60.5 0.6 collective-permute-done.13.came_ref
  62.1 1.0 %collective-permute-start.20 = (bf16[8,3072]{1,0:T(8,128)(2,1)S(1)}, bf16[8,3072]{1,0:T(8,128)(2,1)S(1)}, u32[]{:S(2)}, u32[]{:S(2)}) collective-permute-start(bf16[8,3072]{1,0:T(8,128)(2,1)S(1)} %get-tuple-element.88), channel_id=1, source_target_pairs={{0,8},{1,9},{2,10},{3,11},{4,12},{5,13},{6,14},{7,15},{8,0},{9,1},... | collective-permute-start | bytes 147464 | tf_op jit(solution)/shard_map/ppermute | solution.py:450
  63.1 2.7 %collective-permute-start.21 = (bf16[8,3072]{1,0:T(8,128)(2,1)S(1)}, bf16[8,3072]{1,0:T(8,128)(2,1)S(1)}, u32[]{:S(2)}, u32[]{:S(2)}) collective-permute-start(bf16[8,3072]{1,0:T(8,128)(2,1)S(1)} %get-tuple-element.89), channel_id=1, source_target_pairs={{0,12},{1,13},{2,14},{3,15},{4,0},{5,1},{6,2},{7,3},{8,4},{9,5},{1... | collective-permute-start | bytes 147464 | tf_op jit(solution)/shard_map/ppermute | solution.py:450
  65.8 1.7 %collective-permute-done.14.refs_1_ = bf16[16,5120]{1,0:T(8,128)(2,1)S(1)} collective-permute-done((bf16[16,5120]{1,0:T(8,128)(2,1)S(1)}, bf16[16,5120]{1,0:T(8,128)(2,1)S(1)}, u32[]{:S(2)}, u32[]{:S(2)}) %collective-permute-start.14) | collective-permute-done | bytes 163872 | tf_op jit(solution)/shard_map/ppermute | solution.py:450
  67.7 0.9 %collective-permute-start.16 = (bf16[4,5120]{1,0:T(4,128)(2,1)S(1)}, bf16[4,5120]{1,0:T(4,128)(2,1)S(1)}, u32[]{:S(2)}, u32[]{:S(2)}) collective-permute-start(bf16[4,5120]{1,0:T(4,128)(2,1)S(1)} %get-tuple-element.81), channel_id=1, source_target_pairs={{0,8},{1,9},{2,10},{3,11},{4,12},{5,13},{6,14},{7,15},{8,0},{9,1},... | collective-permute-start | bytes 122888 | tf_op jit(solution)/shard_map/ppermute | solution.py:450
  68.6 2.8 %collective-permute-start.17 = (bf16[4,5120]{1,0:T(4,128)(2,1)S(1)}, bf16[4,5120]{1,0:T(4,128)(2,1)S(1)}, u32[]{:S(2)}, u32[]{:S(2)}) collective-permute-start(bf16[4,5120]{1,0:T(4,128)(2,1)S(1)} %get-tuple-element.82), channel_id=1, source_target_pairs={{0,12},{1,13},{2,14},{3,15},{4,0},{5,1},{6,2},{7,3},{8,4},{9,5},{1... | collective-permute-start | bytes 122888 | tf_op jit(solution)/shard_map/ppermute | solution.py:450
  71.4 0.9 %collective-permute-start.22 = (bf16[4,3072]{1,0:T(4,128)(2,1)S(1)}, bf16[4,3072]{1,0:T(4,128)(2,1)S(1)}, u32[]{:S(2)}, u32[]{:S(2)}) collective-permute-start(bf16[4,3072]{1,0:T(4,128)(2,1)S(1)} %get-tuple-element.91), channel_id=1, source_target_pairs={{0,2},{1,3},{2,0},{3,1},{4,6},{5,7},{6,4},{7,5},{8,10},{9,11},{10,... | collective-permute-start | bytes 73736 | tf_op jit(solution)/shard_map/ppermute | solution.py:450
  72.4 3.0 %collective-permute-done.22.refs_5_ = bf16[4,3072]{1,0:T(4,128)(2,1)S(1)} collective-permute-done((bf16[4,3072]{1,0:T(4,128)(2,1)S(1)}, bf16[4,3072]{1,0:T(4,128)(2,1)S(1)}, u32[]{:S(2)}, u32[]{:S(2)}) %collective-permute-start.22) | collective-permute-done | bytes 24608 | tf_op jit(solution)/shard_map/ppermute | solution.py:450
  75.4 0.7 shard_map.198
  (75 shorter events, 4.3 us)
Async XLA Ops:
  0.7 14.9 %copy-start.13 = (s32[32]{0:T(128)S(1)}, s32[32]{0:T(128)}, u32[]{:S(2)}) copy-start(s32[32]{0:T(128)} %len_ref.1) | copy-start | bytes 388
  0.7 14.9 %copy-start.12 = (s32[32]{0:T(128)S(1)}, s32[32]{0:T(128)}, u32[]{:S(2)}) copy-start(s32[32]{0:T(128)} %slot_hbm.1) | copy-start | bytes 388
  0.7 14.9 %copy-start.11 = (s32[32]{0:T(128)S(1)}, s32[32]{0:T(128)}, u32[]{:S(2)}) copy-start(s32[32]{0:T(128)} %adapter_hbm.1) | copy-start | bytes 388
  1.8 13.6 %collective-permute-start.3 = (bf16[1,4,8192]{2,1,0:T(4,128)(2,1)S(1)}, bf16[1,4,8192]{2,1,0:T(4,128)(2,1)S(1)}, u32[]{:S(2)}, u32[]{:S(2)}) collective-permute-start(bf16[1,4,8192]{2,1,0:T(4,128)(2,1)S(1)} %bitcast.24), channel_id=1, source_target_pairs={{0,2},{1,3},{2,0},{3,1},{4,6},{5,7},{6,4},{7,5},{8,10},{9,11},{10,... | collective-permute-start | bytes 196616 | tf_op jit(solution)/shard_map/ppermute | solution.py:450
  4.9 9.9 %collective-permute-start.2 = (bf16[1,4,8192]{2,1,0:T(4,128)(2,1)S(1)}, bf16[1,4,8192]{2,1,0:T(4,128)(2,1)S(1)}, u32[]{:S(2)}, u32[]{:S(2)}) collective-permute-start(bf16[1,4,8192]{2,1,0:T(4,128)(2,1)S(1)} %bitcast.25), channel_id=1, source_target_pairs={{0,12},{1,13},{2,14},{3,15},{4,0},{5,1},{6,2},{7,3},{8,4},{9,5},{1... | collective-permute-start | bytes 196616 | tf_op jit(solution)/shard_map/ppermute | solution.py:450
  8.5 6.2 %collective-permute-start.1 = (bf16[1,4,8192]{2,1,0:T(4,128)(2,1)S(1)}, bf16[1,4,8192]{2,1,0:T(4,128)(2,1)S(1)}, u32[]{:S(2)}, u32[]{:S(2)}) collective-permute-start(bf16[1,4,8192]{2,1,0:T(4,128)(2,1)S(1)} %bitcast.26), channel_id=1, source_target_pairs={{0,8},{1,9},{2,10},{3,11},{4,12},{5,13},{6,14},{7,15},{8,0},{9,1},... | collective-permute-start | bytes 196616 | tf_op jit(solution)/shard_map/ppermute | solution.py:450
  8.5 6.2 %collective-permute-start = (bf16[1,4,8192]{2,1,0:T(4,128)(2,1)S(1)}, bf16[1,4,8192]{2,1,0:T(4,128)(2,1)S(1)}, u32[]{:S(2)}, u32[]{:S(2)}) collective-permute-start(bf16[1,4,8192]{2,1,0:T(4,128)(2,1)S(1)} %bitcast.27), channel_id=1, source_target_pairs={{0,4},{1,5},{2,6},{3,7},{4,8},{5,9},{6,10},{7,11},{8,12},{9,13},{1... | collective-permute-start | bytes 196616 | tf_op jit(solution)/shard_map/ppermute | solution.py:450
  14.8 5.8 %collective-permute-start.4 = (bf16[3,4,8192]{2,1,0:T(4,128)(2,1)S(1)}, bf16[3,4,8192]{2,1,0:T(4,128)(2,1)S(1)}, u32[]{:S(2)}, u32[]{:S(2)}) collective-permute-start(bf16[3,4,8192]{2,1,0:T(4,128)(2,1)S(1)} %get-tuple-element.96), channel_id=1, source_target_pairs={{0,2},{1,3},{2,0},{3,1},{4,6},{5,7},{6,4},{7,5},{8,10},{9,11},{10,... | collective-permute-start | bytes 589832 | tf_op jit(solution)/shard_map/ppermute | solution.py:450
  15.4 9.3 %slice-start = ((s8[8388608]{0:T(1024)(128)(4,1)}), s8[4194304]{0:T(1024)(128)(4,1)S(1)}, s32[]{:S(2)}) async-start(s8[8388608]{0:T(1024)(128)(4,1)} %bitcast.14), calls=%async_computation.2 | async-start | bytes 8388608
  15.4 9.2 %slice-start.1 = ((s8[8388608]{0:T(1024)(128)(4,1)}), s8[4194304]{0:T(1024)(128)(4,1)S(1)}, s32[]{:S(2)}) async-start(s8[8388608]{0:T(1024)(128)(4,1)} %bitcast.14), calls=%async_computation.3 | async-start | bytes 8388608
  15.5 5.1 %collective-permute-start.5 = (bf16[5,4,8192]{2,1,0:T(4,128)(2,1)S(1)}, bf16[5,4,8192]{2,1,0:T(4,128)(2,1)S(1)}, u32[]{:S(2)}, u32[]{:S(2)}) collective-permute-start(bf16[5,4,8192]{2,1,0:T(4,128)(2,1)S(1)} %constant_dynamic-update-slice_fusion.refs_0_), channel_id=1, source_target_pairs={{0,1},{1,0},{2,3},{3,2},{4,5},{5,4},{6,7},{7,6},{8,9},{9,8},{10,11... | collective-permute-start | bytes 983048 | tf_op jit(solution)/shard_map/ppermute | solution.py:450
  20.6 1.4 %collective-permute-start.6 = (bf16[3,4,8192]{2,1,0:T(4,128)(2,1)S(1)}, bf16[3,4,8192]{2,1,0:T(4,128)(2,1)S(1)}, u32[]{:S(2)}, u32[]{:S(2)}) collective-permute-start(bf16[3,4,8192]{2,1,0:T(4,128)(2,1)S(1)} %collective-permute-done.4.refs_1_), channel_id=1, source_target_pairs={{0,1},{1,0},{2,3},{3,2},{4,5},{5,4},{6,7},{7,6},{8,9},{9,8},{10,11... | collective-permute-start | bytes 589832 | tf_op jit(solution)/shard_map/ppermute | solution.py:450
  22.8 3.3 %collective-permute-start.9 = (bf16[16,128]{1,0:T(8,128)(2,1)S(1)}, bf16[16,128]{1,0:T(8,128)(2,1)S(1)}, u32[]{:S(2)}, u32[]{:S(2)}) collective-permute-start(bf16[16,128]{1,0:T(8,128)(2,1)S(1)} %get-tuple-element.57.refs_0_), channel_id=1, source_target_pairs={{0,3},{1,2},{2,1},{3,0},{4,7},{5,6},{6,5},{7,4},{8,11},{9,10},{10,... | collective-permute-start | bytes 12296 | tf_op jit(solution)/shard_map/ppermute | solution.py:450
  23.1 3.6 %collective-permute-start.8 = (bf16[16,128]{1,0:T(8,128)(2,1)S(1)}, bf16[16,128]{1,0:T(8,128)(2,1)S(1)}, u32[]{:S(2)}, u32[]{:S(2)}) collective-permute-start(bf16[16,128]{1,0:T(8,128)(2,1)S(1)} %get-tuple-element.57.refs_0_), channel_id=1, source_target_pairs={{0,2},{1,3},{2,0},{3,1},{4,6},{5,7},{6,4},{7,5},{8,10},{9,11},{10,... | collective-permute-start | bytes 12296 | tf_op jit(solution)/shard_map/ppermute | solution.py:450
  24.6 2.1 %collective-permute-start.7 = (bf16[16,128]{1,0:T(8,128)(2,1)S(1)}, bf16[16,128]{1,0:T(8,128)(2,1)S(1)}, u32[]{:S(2)}, u32[]{:S(2)}) collective-permute-start(bf16[16,128]{1,0:T(8,128)(2,1)S(1)} %get-tuple-element.57.refs_0_), channel_id=1, source_target_pairs={{0,1},{1,0},{2,3},{3,2},{4,5},{5,4},{6,7},{7,6},{8,9},{9,8},{10,11... | collective-permute-start | bytes 12296 | tf_op jit(solution)/shard_map/ppermute | solution.py:450
  26.1 19.5 %copy-start.4 = (bf16[2,384,1024]{2,1,0:T(8,128)(2,1)S(1)}, bf16[2,384,1024]{2,1,0:T(8,128)(2,1)}, u32[]{:S(2)}) copy-start(bf16[2,384,1024]{2,1,0:T(8,128)(2,1)} %k_ref.1) | copy-start | bytes 4718596
  26.1 19.5 %copy-start.5 = (bf16[2,384,1024]{2,1,0:T(8,128)(2,1)S(1)}, bf16[2,384,1024]{2,1,0:T(8,128)(2,1)}, u32[]{:S(2)}) copy-start(bf16[2,384,1024]{2,1,0:T(8,128)(2,1)} %v_ref.1) | copy-start | bytes 4718596
  26.7 30.5 %slice-start.2 = ((s8[8388608]{0:T(1024)(128)(4,1)}), s8[4194304]{0:T(1024)(128)(4,1)S(1)}, s32[]{:S(2)}) async-start(s8[8388608]{0:T(1024)(128)(4,1)} %bitcast.16), calls=%async_computation.4 | async-start | bytes 8388608
  26.7 30.5 %slice-start.3 = ((s8[8388608]{0:T(1024)(128)(4,1)}), s8[4194304]{0:T(1024)(128)(4,1)S(1)}, s32[]{:S(2)}) async-start(s8[8388608]{0:T(1024)(128)(4,1)} %bitcast.16), calls=%async_computation.5 | async-start | bytes 8388608
  26.7 5.7 %collective-permute-start.12 = (bf16[16,128]{1,0:T(8,128)(2,1)S(1)}, bf16[16,128]{1,0:T(8,128)(2,1)S(1)}, u32[]{:S(2)}, u32[]{:S(2)}) collective-permute-start(bf16[16,128]{1,0:T(8,128)(2,1)S(1)} %shard_map.187.refs_0_), channel_id=1, source_target_pairs={{0,12},{1,13},{2,14},{3,15},{4,0},{5,1},{6,2},{7,3},{8,4},{9,5},{1... | collective-permute-start | bytes 12296 | tf_op jit(solution)/shard_map/ppermute | solution.py:450
  28.6 4.5 %collective-permute-start.11 = (bf16[16,128]{1,0:T(8,128)(2,1)S(1)}, bf16[16,128]{1,0:T(8,128)(2,1)S(1)}, u32[]{:S(2)}, u32[]{:S(2)}) collective-permute-start(bf16[16,128]{1,0:T(8,128)(2,1)S(1)} %shard_map.187.refs_0_), channel_id=1, source_target_pairs={{0,8},{1,9},{2,10},{3,11},{4,12},{5,13},{6,14},{7,15},{8,0},{9,1},... | collective-permute-start | bytes 12296 | tf_op jit(solution)/shard_map/ppermute | solution.py:450
  29.2 5.4 %collective-permute-start.10 = (bf16[16,128]{1,0:T(8,128)(2,1)S(1)}, bf16[16,128]{1,0:T(8,128)(2,1)S(1)}, u32[]{:S(2)}, u32[]{:S(2)}) collective-permute-start(bf16[16,128]{1,0:T(8,128)(2,1)S(1)} %shard_map.187.refs_0_), channel_id=1, source_target_pairs={{0,4},{1,5},{2,6},{3,7},{4,8},{5,9},{6,10},{7,11},{8,12},{9,13},{1... | collective-permute-start | bytes 12296 | tf_op jit(solution)/shard_map/ppermute | solution.py:450
  58.9 2.2 %collective-permute-start.13 = (f32[32,5120]{1,0:T(8,128)S(1)}, f32[32,5120]{1,0:T(8,128)S(1)}, u32[]{:S(2)}, u32[]{:S(2)}) collective-permute-start(f32[32,5120]{1,0:T(8,128)S(1)} %get-tuple-element.76), channel_id=1, source_target_pairs={{0,1},{1,0},{2,3},{3,2},{4,5},{5,4},{6,7},{7,6},{8,9},{9,8},{10,11... | collective-permute-start | bytes 1966088 | tf_op jit(solution)/shard_map/ppermute | solution.py:450
  59.9 1.9 %collective-permute-start.18 = (f32[32,3072]{1,0:T(8,128)S(1)}, f32[32,3072]{1,0:T(8,128)S(1)}, u32[]{:S(2)}, u32[]{:S(2)}) collective-permute-start(f32[32,3072]{1,0:T(8,128)S(1)} %get-tuple-element.85), channel_id=1, source_target_pairs={{0,1},{1,0},{2,3},{3,2},{4,5},{5,4},{6,7},{7,6},{8,9},{9,8},{10,11... | collective-permute-start | bytes 1179656 | tf_op jit(solution)/shard_map/ppermute | solution.py:450
  61.2 6.3 %collective-permute-start.14 = (bf16[16,5120]{1,0:T(8,128)(2,1)S(1)}, bf16[16,5120]{1,0:T(8,128)(2,1)S(1)}, u32[]{:S(2)}, u32[]{:S(2)}) collective-permute-start(bf16[16,5120]{1,0:T(8,128)(2,1)S(1)} %get-tuple-element.78), channel_id=1, source_target_pairs={{0,2},{1,3},{2,0},{3,1},{4,6},{5,7},{6,4},{7,5},{8,10},{9,11},{10,... | collective-permute-start | bytes 491528 | tf_op jit(solution)/shard_map/ppermute | solution.py:450
  61.9 6.8 %collective-permute-start.19 = (bf16[8,3072]{1,0:T(8,128)(2,1)S(1)}, bf16[8,3072]{1,0:T(8,128)(2,1)S(1)}, u32[]{:S(2)}, u32[]{:S(2)}) collective-permute-start(bf16[8,3072]{1,0:T(8,128)(2,1)S(1)} %get-tuple-element.87), channel_id=1, source_target_pairs={{0,4},{1,5},{2,6},{3,7},{4,8},{5,9},{6,10},{7,11},{8,12},{9,13},{1... | collective-permute-start | bytes 147464 | tf_op jit(solution)/shard_map/ppermute | solution.py:450
  62.1 9.3 %collective-permute-start.20 = (bf16[8,3072]{1,0:T(8,128)(2,1)S(1)}, bf16[8,3072]{1,0:T(8,128)(2,1)S(1)}, u32[]{:S(2)}, u32[]{:S(2)}) collective-permute-start(bf16[8,3072]{1,0:T(8,128)(2,1)S(1)} %get-tuple-element.88), channel_id=1, source_target_pairs={{0,8},{1,9},{2,10},{3,11},{4,12},{5,13},{6,14},{7,15},{8,0},{9,1},... | collective-permute-start | bytes 147464 | tf_op jit(solution)/shard_map/ppermute | solution.py:450
  63.1 8.3 %collective-permute-start.21 = (bf16[8,3072]{1,0:T(8,128)(2,1)S(1)}, bf16[8,3072]{1,0:T(8,128)(2,1)S(1)}, u32[]{:S(2)}, u32[]{:S(2)}) collective-permute-start(bf16[8,3072]{1,0:T(8,128)(2,1)S(1)} %get-tuple-element.89), channel_id=1, source_target_pairs={{0,12},{1,13},{2,14},{3,15},{4,0},{5,1},{6,2},{7,3},{8,4},{9,5},{1... | collective-permute-start | bytes 147464 | tf_op jit(solution)/shard_map/ppermute | solution.py:450
  67.5 7.8 %collective-permute-start.15 = (bf16[4,5120]{1,0:T(4,128)(2,1)S(1)}, bf16[4,5120]{1,0:T(4,128)(2,1)S(1)}, u32[]{:S(2)}, u32[]{:S(2)}) collective-permute-start(bf16[4,5120]{1,0:T(4,128)(2,1)S(1)} %get-tuple-element.80), channel_id=1, source_target_pairs={{0,4},{1,5},{2,6},{3,7},{4,8},{5,9},{6,10},{7,11},{8,12},{9,13},{1... | collective-permute-start | bytes 122888 | tf_op jit(solution)/shard_map/ppermute | solution.py:450
  67.7 7.6 %collective-permute-start.16 = (bf16[4,5120]{1,0:T(4,128)(2,1)S(1)}, bf16[4,5120]{1,0:T(4,128)(2,1)S(1)}, u32[]{:S(2)}, u32[]{:S(2)}) collective-permute-start(bf16[4,5120]{1,0:T(4,128)(2,1)S(1)} %get-tuple-element.81), channel_id=1, source_target_pairs={{0,8},{1,9},{2,10},{3,11},{4,12},{5,13},{6,14},{7,15},{8,0},{9,1},... | collective-permute-start | bytes 122888 | tf_op jit(solution)/shard_map/ppermute | solution.py:450
  68.6 6.7 %collective-permute-start.17 = (bf16[4,5120]{1,0:T(4,128)(2,1)S(1)}, bf16[4,5120]{1,0:T(4,128)(2,1)S(1)}, u32[]{:S(2)}, u32[]{:S(2)}) collective-permute-start(bf16[4,5120]{1,0:T(4,128)(2,1)S(1)} %get-tuple-element.82), channel_id=1, source_target_pairs={{0,12},{1,13},{2,14},{3,15},{4,0},{5,1},{6,2},{7,3},{8,4},{9,5},{1... | collective-permute-start | bytes 122888 | tf_op jit(solution)/shard_map/ppermute | solution.py:450
  71.4 3.9 %collective-permute-start.22 = (bf16[4,3072]{1,0:T(4,128)(2,1)S(1)}, bf16[4,3072]{1,0:T(4,128)(2,1)S(1)}, u32[]{:S(2)}, u32[]{:S(2)}) collective-permute-start(bf16[4,3072]{1,0:T(4,128)(2,1)S(1)} %get-tuple-element.91), channel_id=1, source_target_pairs={{0,2},{1,3},{2,0},{3,1},{4,6},{5,7},{6,4},{7,5},{8,10},{9,11},{10,... | collective-permute-start | bytes 73736 | tf_op jit(solution)/shard_map/ppermute | solution.py:450
  (9 other events, 51.0 us)

commit v15 on v8

--- a/solution.py
+++ b/solution.py
@@ -344,7 +344,7 @@
 
 def out_body(start, a_ref, w_ref, mine_ref, other_ref):
     half = mine_ref.shape[0]
-    tile = 1024
+    tile = 512
 
     @pl.loop(0, mine_ref.shape[1] // tile)
     def _(i):
@@ -559,7 +559,7 @@
     context = lax.all_to_all(context, "serve", split_axis=0, concat_axis=0, tiled=True)
 
     half = all_rows // cores
-    cut = width * 5 // 8
+    cut = width * 18 // 32
 
     def kinds(count, columns):
         return (jax.ShapeDtypeStruct((count, columns), F32),) * 2

time: 76.2 us -> 76.7 us (level)
  Pallas kernels: 12 us -> 12.9 us
    pallas_call x16, Pallas kernels: 12 us -> 12.9 us  [whole_call(): pl.pallas_call(body, out_shape=out_shape, in_specs=specs, out_specs=tuple...]
  transfers between devices with their start and end apart: 23 -> 23, of which waited for: 10 -> 10; matrix products, arithmetic and copies ran while one was open for 0% -> 0% of each run, Pallas kernels for 7% -> 8%
where the time goes in v15:
time: 76.7 us; the launch traced here: 76.4 us
  starting transfers between devices  23.9 us (31%)
  blocking collectives  19.6 us (26%)
  waiting for transfers between devices  18 us (23%)
  Pallas kernels  12.9 us (17%)
  local copies, waits for them, and re-layouts  1.02 us (1%)
  between operations  0.96 us (1%)
    ppermute x23, starting transfers between devices, shift(): return lax.ppermute(value, 'serve', partner(f, m, c))  23.9 us
    ppermute x23, waiting for transfers between devices, shift(): return lax.ppermute(value, 'serve', partner(f, m, c))  18 us
    pallas_call x16, Pallas kernels, whole_call(): pl.pallas_call(body, out_shape=out_shape, in_specs=specs, out_specs=tuple...  12.9 us
    all_to_all x1, blocking collectives, shards(): lax.all_to_all(ready, 'serve', split_axis=0, concat_axis=0, tiled=True)  10.1 us
    all_to_all x1, blocking collectives, shards(): lax.all_to_all(context, 'serve', split_axis=0, concat_axis=0, tiled=True)  9.48 us
  transfers between devices with their start and end apart: 23, of which 10 were waited for; matrix products, arithmetic and copies ran while one was open for 0% of the time, Pallas kernels for 8%

profile of v15, /device:TPU:0, one launch (start us, length us, event | category | flops | bytes accessed | tf_op | source)
XLA Modules:
  0.0 76.4 jit_solution(12336502012707153383)
XLA Ops:
  0.7 0.6 copy-done.10
  1.8 3.0 %collective-permute-start.3 = (bf16[1,4,8192]{2,1,0:T(4,128)(2,1)S(1)}, bf16[1,4,8192]{2,1,0:T(4,128)(2,1)S(1)}, u32[]{:S(2)}, u32[]{:S(2)}) collective-permute-start(bf16[1,4,8192]{2,1,0:T(4,128)(2,1)S(1)} %bitcast.24), channel_id=1, source_target_pairs={{0,2},{1,3},{2,0},{3,1},{4,6},{5,7},{6,4},{7,5},{8,10},{9,11},{10,... | collective-permute-start | bytes 196616 | tf_op jit(solution)/shard_map/ppermute | solution.py:440
  4.9 3.6 %collective-permute-start.2 = (bf16[1,4,8192]{2,1,0:T(4,128)(2,1)S(1)}, bf16[1,4,8192]{2,1,0:T(4,128)(2,1)S(1)}, u32[]{:S(2)}, u32[]{:S(2)}) collective-permute-start(bf16[1,4,8192]{2,1,0:T(4,128)(2,1)S(1)} %bitcast.25), channel_id=1, source_target_pairs={{0,12},{1,13},{2,14},{3,15},{4,0},{5,1},{6,2},{7,3},{8,4},{9,5},{1... | collective-permute-start | bytes 196616 | tf_op jit(solution)/shard_map/ppermute | solution.py:440
  8.5 1.0 %collective-permute-start = (bf16[1,4,8192]{2,1,0:T(4,128)(2,1)S(1)}, bf16[1,4,8192]{2,1,0:T(4,128)(2,1)S(1)}, u32[]{:S(2)}, u32[]{:S(2)}) collective-permute-start(bf16[1,4,8192]{2,1,0:T(4,128)(2,1)S(1)} %bitcast.27), channel_id=1, source_target_pairs={{0,4},{1,5},{2,6},{3,7},{4,8},{5,9},{6,10},{7,11},{8,12},{9,13},{1... | collective-permute-start | bytes 196616 | tf_op jit(solution)/shard_map/ppermute | solution.py:440
  9.5 5.1 %collective-permute-done = bf16[1,4,8192]{2,1,0:T(4,128)(2,1)S(1)} collective-permute-done((bf16[1,4,8192]{2,1,0:T(4,128)(2,1)S(1)}, bf16[1,4,8192]{2,1,0:T(4,128)(2,1)S(1)}, u32[]{:S(2)}, u32[]{:S(2)}) %collective-permute-start) | collective-permute-done | bytes 65568 | tf_op jit(solution)/shard_map/ppermute | solution.py:440
  15.6 1.8 %shard_map.185 = (s32[64,1]{1,0:T(8,128)S(1)}, s32[64,1]{1,0:T(8,128)S(1)}, f32[64,128]{1,0:T(8,128)S(1)}, f32[64,128]{1,0:T(8,128)S(1)}, f32[64,128]{1,0:T(8,12...) custom-call(s32[1]{0:T(128)} %bitcast.index_ref, ...), custom_call_target="tpu_custom_call" | custom-call | flops 4600000000 | tf_op jit(solution)/shard_map/pallas_call | solution.py:36
  17.4 3.2 %collective-permute-done.4.refs_1_ = bf16[3,4,8192]{2,1,0:T(4,128)(2,1)S(1)} collective-permute-done((bf16[3,4,8192]{2,1,0:T(4,128)(2,1)S(1)}, bf16[3,4,8192]{2,1,0:T(4,128)(2,1)S(1)}, u32[]{:S(2)}, u32[]{:S(2)}) %collective-permute-start.4) | collective-permute-done | bytes 196640 | tf_op jit(solution)/shard_map/ppermute | solution.py:440
  20.6 1.4 %collective-permute-done.6.refs_3_ = bf16[3,4,8192]{2,1,0:T(4,128)(2,1)S(1)} collective-permute-done((bf16[3,4,8192]{2,1,0:T(4,128)(2,1)S(1)}, bf16[3,4,8192]{2,1,0:T(4,128)(2,1)S(1)}, u32[]{:S(2)}, u32[]{:S(2)}) %collective-permute-start.6) | collective-permute-done | bytes 196640 | tf_op jit(solution)/shard_map/ppermute | solution.py:440
  22.1 0.7 shard_map.186
  23.1 1.5 %collective-permute-start.8 = (bf16[16,128]{1,0:T(8,128)(2,1)S(1)}, bf16[16,128]{1,0:T(8,128)(2,1)S(1)}, u32[]{:S(2)}, u32[]{:S(2)}) collective-permute-start(bf16[16,128]{1,0:T(8,128)(2,1)S(1)} %get-tuple-element.57.refs_0_), channel_id=1, source_target_pairs={{0,2},{1,3},{2,0},{3,1},{4,6},{5,7},{6,4},{7,5},{8,10},{9,11},{10,... | collective-permute-start | bytes 12296 | tf_op jit(solution)/shard_map/ppermute | solution.py:440
  24.7 1.3 %shard_map.188 = (f32[64,512]{1,0:T(8,128)S(1)}, f32[64,128]{1,0:T(8,128)S(1)}) custom-call(bf16[64,8192]{1,0:T(8,128)(2,1)S(1)} %get-tuple-element.58.x_ref, bf16[8192,512]{1,0:T(8,128)(2,1)S(1)} %bitcast.15, bf16[64,8192]{1,0:T(8,128)(2,1)S(1)} %bitcast.18, bf16[64,8192]{1,0:T(8,128)(2,1)S(1)} %bitcast.20), custom_call_target="tpu_custom_call" | custom-call | flops 345000000 | tf_op jit(solution)/shard_map/pallas_call | solution.py:36
  26.1 0.6 collective-permute-done.8.refs_2_
  26.7 1.8 %collective-permute-start.12 = (bf16[16,128]{1,0:T(8,128)(2,1)S(1)}, bf16[16,128]{1,0:T(8,128)(2,1)S(1)}, u32[]{:S(2)}, u32[]{:S(2)}) collective-permute-start(bf16[16,128]{1,0:T(8,128)(2,1)S(1)} %shard_map.187.refs_0_), channel_id=1, source_target_pairs={{0,12},{1,13},{2,14},{3,15},{4,0},{5,1},{6,2},{7,3},{8,4},{9,5},{1... | collective-permute-start | bytes 12296 | tf_op jit(solution)/shard_map/ppermute | solution.py:440
  28.6 0.6 collective-permute-start.11
  29.2 1.9 %collective-permute-start.10 = (bf16[16,128]{1,0:T(8,128)(2,1)S(1)}, bf16[16,128]{1,0:T(8,128)(2,1)S(1)}, u32[]{:S(2)}, u32[]{:S(2)}) collective-permute-start(bf16[16,128]{1,0:T(8,128)(2,1)S(1)} %shard_map.187.refs_0_), channel_id=1, source_target_pairs={{0,4},{1,5},{2,6},{3,7},{4,8},{5,9},{6,10},{7,11},{8,12},{9,13},{1... | collective-permute-start | bytes 12296 | tf_op jit(solution)/shard_map/ppermute | solution.py:440
  31.1 1.3 %shard_map.189 = (f32[64,512]{1,0:T(8,128)S(1)}, f32[64,128]{1,0:T(8,128)S(1)}) custom-call(bf16[64,8192]{1,0:T(8,128)(2,1)S(1)} %get-tuple-element.58.x_ref, bf16[8192,512]{1,0:T(8,128)(2,1)S(1)} %bitcast.15, bf16[64,8192]{1,0:T(8,128)(2,1)S(1)} %bitcast.19, bf16[64,8192]{1,0:T(8,128)(2,1)S(1)} %bitcast.21), custom_call_target="tpu_custom_call" | custom-call | flops 345000000 | tf_op jit(solution)/shard_map/pallas_call | solution.py:36
  33.1 1.5 %collective-permute-done.10.refs_1_ = bf16[16,128]{1,0:T(8,128)(2,1)S(1)} collective-permute-done((bf16[16,128]{1,0:T(8,128)(2,1)S(1)}, bf16[16,128]{1,0:T(8,128)(2,1)S(1)}, u32[]{:S(2)}, u32[]{:S(2)}) %collective-permute-start.10) | collective-permute-done | bytes 4128 | tf_op jit(solution)/shard_map/ppermute | solution.py:440
  34.6 0.8 %shard_map.190 = bf16[16,24,128]{2,1,0:T(8,128)(2,1)S(1)} custom-call(bf16[16,128]{1,0:T(8,128)(2,1)S(1)} %shard_map.187.refs_0_, bf16[16,128]{1,0:T(8,128)(2,1)S(1)} %collective-permute-done.10.refs_1_, bf16[16,128]{1,0:T(8,128)(2,1)S(1)} %collective-permute-done.11.refs_2_, bf16[16,128]{1,0:T(8,128)(2,1)S(1)} %collective-permute-done.12.refs_3_, ...), custom_call_target="tpu_custom_call" | custom-call | flops 1035000000 | tf_op jit(solution)/shard_map/pallas_call | solution.py:36
  35.4 10.1 %all_to_all.10.x_ref = bf16[16,24,128]{2,1,0:T(8,128)(2,1)S(1)} all-to-all(bf16[16,24,128]{2,1,0:T(8,128)(2,1)S(1)} %shard_map.190), channel_id=1, replica_groups=mesh['replica'=2,'serve'=16] {'serve'}, dimensions={0} | all-to-all | bytes 196608 | tf_op jit(solution)/shard_map/all_to_all | solution.py:548
  45.6 2.0 %shard_map.191 = (bf16[2,2,1024]{2,1,0:T(2,128)(2,1)}, bf16[2,2,1024]{2,1,0:T(2,128)(2,1)}, bf16[16,16,128]{2,1,0:T(8,128)(2,1)S(1)}) custom-call(s32[1]{0:T(128)} %bitcast.index_ref, s32[32]{0:T(128)S(1)} %copy-done.13, bf16[16,24,128]{2,1,0:T(8,128)(2,1)S(1)} %all_to_all.10.x_ref, bf16[256,384]{1,0:T(8,128)(2,1)S(1)} %get-tuple-element.72.order_ref, ...), custom_call_target="tpu_custom_call" | custom-call | flops 1150000000 | tf_op jit(solution)/shard_map/pallas_call | solution.py:36
  47.5 9.5 %all_to_all.11.ctx_ref = bf16[16,16,128]{2,1,0:T(8,128)(2,1)S(1)} all-to-all(bf16[16,16,128]{2,1,0:T(8,128)(2,1)S(1)} %get-tuple-element.73), channel_id=1, replica_groups=mesh['replica'=2,'serve'=16] {'serve'}, dimensions={0} | all-to-all | bytes 131072 | tf_op jit(solution)/shard_map/all_to_all | solution.py:559
  57.0 2.1 %shard_map.192 = (bf16[64,512]{1,0:T(8,128)(2,1)S(1)}, f32[32,4608]{1,0:T(8,128)S(1)}, f32[32,4608]{1,0:T(8,128)S(1)}) custom-call(bf16[16,16,128]{2,1,0:T(8,128)(2,1)S(1)} %all_to_all.11.ctx_ref, bf16[256,256]{1,0:T(8,128)(2,1)S(1)} %get-tuple-element.74.take_ref, bf16[512,8192]{1,0:T(8,128)(2,1)S(1)} %bitcast.17), custom_call_target="tpu_custom_call" | custom-call | flops 460000000 | tf_op jit(solution)/shard_map/pallas_call | solution.py:36
  59.2 1.5 %shard_map.195 = (f32[32,3584]{1,0:T(8,128)S(1)}, f32[32,3584]{1,0:T(8,128)S(1)}) custom-call(bf16[64,512]{1,0:T(8,128)(2,1)S(1)} %get-tuple-element.83.a_ref, bf16[512,8192]{1,0:T(8,128)(2,1)S(1)} %bitcast.17), custom_call_target="tpu_custom_call" | custom-call | flops 345000000 | tf_op jit(solution)/shard_map/pallas_call | solution.py:36
  61.5 1.2 %collective-permute-done.18.came_ref = f32[32,3584]{1,0:T(8,128)S(1)} collective-permute-done((f32[32,3584]{1,0:T(8,128)S(1)}, f32[32,3584]{1,0:T(8,128)S(1)}, u32[]{:S(2)}, u32[]{:S(2)}) %collective-permute-start.18) | collective-permute-done | bytes 458784 | tf_op jit(solution)/shard_map/ppermute | solution.py:440
  62.9 0.9 %collective-permute-start.20 = (bf16[8,3584]{1,0:T(8,128)(2,1)S(1)}, bf16[8,3584]{1,0:T(8,128)(2,1)S(1)}, u32[]{:S(2)}, u32[]{:S(2)}) collective-permute-start(bf16[8,3584]{1,0:T(8,128)(2,1)S(1)} %get-tuple-element.88), channel_id=1, source_target_pairs={{0,8},{1,9},{2,10},{3,11},{4,12},{5,13},{6,14},{7,15},{8,0},{9,1},... | collective-permute-start | bytes 172040 | tf_op jit(solution)/shard_map/ppermute | solution.py:440
  63.9 2.8 %collective-permute-start.21 = (bf16[8,3584]{1,0:T(8,128)(2,1)S(1)}, bf16[8,3584]{1,0:T(8,128)(2,1)S(1)}, u32[]{:S(2)}, u32[]{:S(2)}) collective-permute-start(bf16[8,3584]{1,0:T(8,128)(2,1)S(1)} %get-tuple-element.89), channel_id=1, source_target_pairs={{0,12},{1,13},{2,14},{3,15},{4,0},{5,1},{6,2},{7,3},{8,4},{9,5},{1... | collective-permute-start | bytes 172040 | tf_op jit(solution)/shard_map/ppermute | solution.py:440
  67.4 1.4 %collective-permute-start.16 = (bf16[4,4608]{1,0:T(4,128)(2,1)S(1)}, bf16[4,4608]{1,0:T(4,128)(2,1)S(1)}, u32[]{:S(2)}, u32[]{:S(2)}) collective-permute-start(bf16[4,4608]{1,0:T(4,128)(2,1)S(1)} %get-tuple-element.81), channel_id=1, source_target_pairs={{0,8},{1,9},{2,10},{3,11},{4,12},{5,13},{6,14},{7,15},{8,0},{9,1},... | collective-permute-start | bytes 110600 | tf_op jit(solution)/shard_map/ppermute | solution.py:440
  68.8 0.6 collective-permute-done.19.refs_1_
  69.4 2.3 %collective-permute-start.17 = (bf16[4,4608]{1,0:T(4,128)(2,1)S(1)}, bf16[4,4608]{1,0:T(4,128)(2,1)S(1)}, u32[]{:S(2)}, u32[]{:S(2)}) collective-permute-start(bf16[4,4608]{1,0:T(4,128)(2,1)S(1)} %get-tuple-element.82), channel_id=1, source_target_pairs={{0,12},{1,13},{2,14},{3,15},{4,0},{5,1},{6,2},{7,3},{8,4},{9,5},{1... | collective-permute-start | bytes 110600 | tf_op jit(solution)/shard_map/ppermute | solution.py:440
  71.7 0.8 %collective-permute-start.22 = (bf16[4,3584]{1,0:T(4,128)(2,1)S(1)}, bf16[4,3584]{1,0:T(4,128)(2,1)S(1)}, u32[]{:S(2)}, u32[]{:S(2)}) collective-permute-start(bf16[4,3584]{1,0:T(4,128)(2,1)S(1)} %get-tuple-element.91), channel_id=1, source_target_pairs={{0,2},{1,3},{2,0},{3,1},{4,6},{5,7},{6,4},{7,5},{8,10},{9,11},{10,... | collective-permute-start | bytes 86024 | tf_op jit(solution)/shard_map/ppermute | solution.py:440
  72.5 3.2 %collective-permute-done.22.refs_5_ = bf16[4,3584]{1,0:T(4,128)(2,1)S(1)} collective-permute-done((bf16[4,3584]{1,0:T(4,128)(2,1)S(1)}, bf16[4,3584]{1,0:T(4,128)(2,1)S(1)}, u32[]{:S(2)}, u32[]{:S(2)}) %collective-permute-start.22) | collective-permute-done | bytes 28704 | tf_op jit(solution)/shard_map/ppermute | solution.py:440
  75.7 0.7 shard_map.198
  (75 shorter events, 4.4 us)
Async XLA Ops:
  0.7 14.9 %copy-start.13 = (s32[32]{0:T(128)S(1)}, s32[32]{0:T(128)}, u32[]{:S(2)}) copy-start(s32[32]{0:T(128)} %len_ref.1) | copy-start | bytes 388
  0.7 14.9 %copy-start.12 = (s32[32]{0:T(128)S(1)}, s32[32]{0:T(128)}, u32[]{:S(2)}) copy-start(s32[32]{0:T(128)} %slot_hbm.1) | copy-start | bytes 388
  0.7 14.9 %copy-start.11 = (s32[32]{0:T(128)S(1)}, s32[32]{0:T(128)}, u32[]{:S(2)}) copy-start(s32[32]{0:T(128)} %adapter_hbm.1) | copy-start | bytes 388
  1.8 13.6 %collective-permute-start.3 = (bf16[1,4,8192]{2,1,0:T(4,128)(2,1)S(1)}, bf16[1,4,8192]{2,1,0:T(4,128)(2,1)S(1)}, u32[]{:S(2)}, u32[]{:S(2)}) collective-permute-start(bf16[1,4,8192]{2,1,0:T(4,128)(2,1)S(1)} %bitcast.24), channel_id=1, source_target_pairs={{0,2},{1,3},{2,0},{3,1},{4,6},{5,7},{6,4},{7,5},{8,10},{9,11},{10,... | collective-permute-start | bytes 196616 | tf_op jit(solution)/shard_map/ppermute | solution.py:440
  4.9 9.9 %collective-permute-start.2 = (bf16[1,4,8192]{2,1,0:T(4,128)(2,1)S(1)}, bf16[1,4,8192]{2,1,0:T(4,128)(2,1)S(1)}, u32[]{:S(2)}, u32[]{:S(2)}) collective-permute-start(bf16[1,4,8192]{2,1,0:T(4,128)(2,1)S(1)} %bitcast.25), channel_id=1, source_target_pairs={{0,12},{1,13},{2,14},{3,15},{4,0},{5,1},{6,2},{7,3},{8,4},{9,5},{1... | collective-permute-start | bytes 196616 | tf_op jit(solution)/shard_map/ppermute | solution.py:440
  8.5 6.2 %collective-permute-start.1 = (bf16[1,4,8192]{2,1,0:T(4,128)(2,1)S(1)}, bf16[1,4,8192]{2,1,0:T(4,128)(2,1)S(1)}, u32[]{:S(2)}, u32[]{:S(2)}) collective-permute-start(bf16[1,4,8192]{2,1,0:T(4,128)(2,1)S(1)} %bitcast.26), channel_id=1, source_target_pairs={{0,8},{1,9},{2,10},{3,11},{4,12},{5,13},{6,14},{7,15},{8,0},{9,1},... | collective-permute-start | bytes 196616 | tf_op jit(solution)/shard_map/ppermute | solution.py:440
  8.5 6.2 %collective-permute-start = (bf16[1,4,8192]{2,1,0:T(4,128)(2,1)S(1)}, bf16[1,4,8192]{2,1,0:T(4,128)(2,1)S(1)}, u32[]{:S(2)}, u32[]{:S(2)}) collective-permute-start(bf16[1,4,8192]{2,1,0:T(4,128)(2,1)S(1)} %bitcast.27), channel_id=1, source_target_pairs={{0,4},{1,5},{2,6},{3,7},{4,8},{5,9},{6,10},{7,11},{8,12},{9,13},{1... | collective-permute-start | bytes 196616 | tf_op jit(solution)/shard_map/ppermute | solution.py:440
  14.8 5.8 %collective-permute-start.4 = (bf16[3,4,8192]{2,1,0:T(4,128)(2,1)S(1)}, bf16[3,4,8192]{2,1,0:T(4,128)(2,1)S(1)}, u32[]{:S(2)}, u32[]{:S(2)}) collective-permute-start(bf16[3,4,8192]{2,1,0:T(4,128)(2,1)S(1)} %get-tuple-element.96), channel_id=1, source_target_pairs={{0,2},{1,3},{2,0},{3,1},{4,6},{5,7},{6,4},{7,5},{8,10},{9,11},{10,... | collective-permute-start | bytes 589832 | tf_op jit(solution)/shard_map/ppermute | solution.py:440
  15.4 9.3 %slice-start = ((s8[8388608]{0:T(1024)(128)(4,1)}), s8[4194304]{0:T(1024)(128)(4,1)S(1)}, s32[]{:S(2)}) async-start(s8[8388608]{0:T(1024)(128)(4,1)} %bitcast.14), calls=%async_computation.2 | async-start | bytes 8388608
  15.4 9.2 %slice-start.1 = ((s8[8388608]{0:T(1024)(128)(4,1)}), s8[4194304]{0:T(1024)(128)(4,1)S(1)}, s32[]{:S(2)}) async-start(s8[8388608]{0:T(1024)(128)(4,1)} %bitcast.14), calls=%async_computation.3 | async-start | bytes 8388608
  15.5 5.1 %collective-permute-start.5 = (bf16[5,4,8192]{2,1,0:T(4,128)(2,1)S(1)}, bf16[5,4,8192]{2,1,0:T(4,128)(2,1)S(1)}, u32[]{:S(2)}, u32[]{:S(2)}) collective-permute-start(bf16[5,4,8192]{2,1,0:T(4,128)(2,1)S(1)} %constant_dynamic-update-slice_fusion.refs_0_), channel_id=1, source_target_pairs={{0,1},{1,0},{2,3},{3,2},{4,5},{5,4},{6,7},{7,6},{8,9},{9,8},{10,11... | collective-permute-start | bytes 983048 | tf_op jit(solution)/shard_map/ppermute | solution.py:440
  20.6 1.4 %collective-permute-start.6 = (bf16[3,4,8192]{2,1,0:T(4,128)(2,1)S(1)}, bf16[3,4,8192]{2,1,0:T(4,128)(2,1)S(1)}, u32[]{:S(2)}, u32[]{:S(2)}) collective-permute-start(bf16[3,4,8192]{2,1,0:T(4,128)(2,1)S(1)} %collective-permute-done.4.refs_1_), channel_id=1, source_target_pairs={{0,1},{1,0},{2,3},{3,2},{4,5},{5,4},{6,7},{7,6},{8,9},{9,8},{10,11... | collective-permute-start | bytes 589832 | tf_op jit(solution)/shard_map/ppermute | solution.py:440
  22.8 3.3 %collective-permute-start.9 = (bf16[16,128]{1,0:T(8,128)(2,1)S(1)}, bf16[16,128]{1,0:T(8,128)(2,1)S(1)}, u32[]{:S(2)}, u32[]{:S(2)}) collective-permute-start(bf16[16,128]{1,0:T(8,128)(2,1)S(1)} %get-tuple-element.57.refs_0_), channel_id=1, source_target_pairs={{0,3},{1,2},{2,1},{3,0},{4,7},{5,6},{6,5},{7,4},{8,11},{9,10},{10,... | collective-permute-start | bytes 12296 | tf_op jit(solution)/shard_map/ppermute | solution.py:440
  23.1 3.6 %collective-permute-start.8 = (bf16[16,128]{1,0:T(8,128)(2,1)S(1)}, bf16[16,128]{1,0:T(8,128)(2,1)S(1)}, u32[]{:S(2)}, u32[]{:S(2)}) collective-permute-start(bf16[16,128]{1,0:T(8,128)(2,1)S(1)} %get-tuple-element.57.refs_0_), channel_id=1, source_target_pairs={{0,2},{1,3},{2,0},{3,1},{4,6},{5,7},{6,4},{7,5},{8,10},{9,11},{10,... | collective-permute-start | bytes 12296 | tf_op jit(solution)/shard_map/ppermute | solution.py:440
  24.6 2.1 %collective-permute-start.7 = (bf16[16,128]{1,0:T(8,128)(2,1)S(1)}, bf16[16,128]{1,0:T(8,128)(2,1)S(1)}, u32[]{:S(2)}, u32[]{:S(2)}) collective-permute-start(bf16[16,128]{1,0:T(8,128)(2,1)S(1)} %get-tuple-element.57.refs_0_), channel_id=1, source_target_pairs={{0,1},{1,0},{2,3},{3,2},{4,5},{5,4},{6,7},{7,6},{8,9},{9,8},{10,11... | collective-permute-start | bytes 12296 | tf_op jit(solution)/shard_map/ppermute | solution.py:440
  26.1 19.5 %copy-start.4 = (bf16[2,384,1024]{2,1,0:T(8,128)(2,1)S(1)}, bf16[2,384,1024]{2,1,0:T(8,128)(2,1)}, u32[]{:S(2)}) copy-start(bf16[2,384,1024]{2,1,0:T(8,128)(2,1)} %k_ref.1) | copy-start | bytes 4718596
  26.1 19.5 %copy-start.5 = (bf16[2,384,1024]{2,1,0:T(8,128)(2,1)S(1)}, bf16[2,384,1024]{2,1,0:T(8,128)(2,1)}, u32[]{:S(2)}) copy-start(bf16[2,384,1024]{2,1,0:T(8,128)(2,1)} %v_ref.1) | copy-start | bytes 4718596
  26.7 30.3 %slice-start.2 = ((s8[8388608]{0:T(1024)(128)(4,1)}), s8[4194304]{0:T(1024)(128)(4,1)S(1)}, s32[]{:S(2)}) async-start(s8[8388608]{0:T(1024)(128)(4,1)} %bitcast.16), calls=%async_computation.4 | async-start | bytes 8388608
  26.7 30.3 %slice-start.3 = ((s8[8388608]{0:T(1024)(128)(4,1)}), s8[4194304]{0:T(1024)(128)(4,1)S(1)}, s32[]{:S(2)}) async-start(s8[8388608]{0:T(1024)(128)(4,1)} %bitcast.16), calls=%async_computation.5 | async-start | bytes 8388608
  26.7 5.7 %collective-permute-start.12 = (bf16[16,128]{1,0:T(8,128)(2,1)S(1)}, bf16[16,128]{1,0:T(8,128)(2,1)S(1)}, u32[]{:S(2)}, u32[]{:S(2)}) collective-permute-start(bf16[16,128]{1,0:T(8,128)(2,1)S(1)} %shard_map.187.refs_0_), channel_id=1, source_target_pairs={{0,12},{1,13},{2,14},{3,15},{4,0},{5,1},{6,2},{7,3},{8,4},{9,5},{1... | collective-permute-start | bytes 12296 | tf_op jit(solution)/shard_map/ppermute | solution.py:440
  28.6 4.5 %collective-permute-start.11 = (bf16[16,128]{1,0:T(8,128)(2,1)S(1)}, bf16[16,128]{1,0:T(8,128)(2,1)S(1)}, u32[]{:S(2)}, u32[]{:S(2)}) collective-permute-start(bf16[16,128]{1,0:T(8,128)(2,1)S(1)} %shard_map.187.refs_0_), channel_id=1, source_target_pairs={{0,8},{1,9},{2,10},{3,11},{4,12},{5,13},{6,14},{7,15},{8,0},{9,1},... | collective-permute-start | bytes 12296 | tf_op jit(solution)/shard_map/ppermute | solution.py:440
  29.2 5.4 %collective-permute-start.10 = (bf16[16,128]{1,0:T(8,128)(2,1)S(1)}, bf16[16,128]{1,0:T(8,128)(2,1)S(1)}, u32[]{:S(2)}, u32[]{:S(2)}) collective-permute-start(bf16[16,128]{1,0:T(8,128)(2,1)S(1)} %shard_map.187.refs_0_), channel_id=1, source_target_pairs={{0,4},{1,5},{2,6},{3,7},{4,8},{5,9},{6,10},{7,11},{8,12},{9,13},{1... | collective-permute-start | bytes 12296 | tf_op jit(solution)/shard_map/ppermute | solution.py:440
  59.1 2.1 %collective-permute-start.13 = (f32[32,4608]{1,0:T(8,128)S(1)}, f32[32,4608]{1,0:T(8,128)S(1)}, u32[]{:S(2)}, u32[]{:S(2)}) collective-permute-start(f32[32,4608]{1,0:T(8,128)S(1)} %get-tuple-element.76), channel_id=1, source_target_pairs={{0,1},{1,0},{2,3},{3,2},{4,5},{5,4},{6,7},{7,6},{8,9},{9,8},{10,11... | collective-permute-start | bytes 1769480 | tf_op jit(solution)/shard_map/ppermute | solution.py:440
  60.7 2.0 %collective-permute-start.18 = (f32[32,3584]{1,0:T(8,128)S(1)}, f32[32,3584]{1,0:T(8,128)S(1)}, u32[]{:S(2)}, u32[]{:S(2)}) collective-permute-start(f32[32,3584]{1,0:T(8,128)S(1)} %get-tuple-element.85), channel_id=1, source_target_pairs={{0,1},{1,0},{2,3},{3,2},{4,5},{5,4},{6,7},{7,6},{8,9},{9,8},{10,11... | collective-permute-start | bytes 1376264 | tf_op jit(solution)/shard_map/ppermute | solution.py:440
  61.3 5.9 %collective-permute-start.14 = (bf16[16,4608]{1,0:T(8,128)(2,1)S(1)}, bf16[16,4608]{1,0:T(8,128)(2,1)S(1)}, u32[]{:S(2)}, u32[]{:S(2)}) collective-permute-start(bf16[16,4608]{1,0:T(8,128)(2,1)S(1)} %get-tuple-element.78), channel_id=1, source_target_pairs={{0,2},{1,3},{2,0},{3,1},{4,6},{5,7},{6,4},{7,5},{8,10},{9,11},{10,... | collective-permute-start | bytes 442376 | tf_op jit(solution)/shard_map/ppermute | solution.py:440
  62.7 6.7 %collective-permute-start.19 = (bf16[8,3584]{1,0:T(8,128)(2,1)S(1)}, bf16[8,3584]{1,0:T(8,128)(2,1)S(1)}, u32[]{:S(2)}, u32[]{:S(2)}) collective-permute-start(bf16[8,3584]{1,0:T(8,128)(2,1)S(1)} %get-tuple-element.87), channel_id=1, source_target_pairs={{0,4},{1,5},{2,6},{3,7},{4,8},{5,9},{6,10},{7,11},{8,12},{9,13},{1... | collective-permute-start | bytes 172040 | tf_op jit(solution)/shard_map/ppermute | solution.py:440
  62.9 8.8 %collective-permute-start.20 = (bf16[8,3584]{1,0:T(8,128)(2,1)S(1)}, bf16[8,3584]{1,0:T(8,128)(2,1)S(1)}, u32[]{:S(2)}, u32[]{:S(2)}) collective-permute-start(bf16[8,3584]{1,0:T(8,128)(2,1)S(1)} %get-tuple-element.88), channel_id=1, source_target_pairs={{0,8},{1,9},{2,10},{3,11},{4,12},{5,13},{6,14},{7,15},{8,0},{9,1},... | collective-permute-start | bytes 172040 | tf_op jit(solution)/shard_map/ppermute | solution.py:440
  63.9 7.8 %collective-permute-start.21 = (bf16[8,3584]{1,0:T(8,128)(2,1)S(1)}, bf16[8,3584]{1,0:T(8,128)(2,1)S(1)}, u32[]{:S(2)}, u32[]{:S(2)}) collective-permute-start(bf16[8,3584]{1,0:T(8,128)(2,1)S(1)} %get-tuple-element.89), channel_id=1, source_target_pairs={{0,12},{1,13},{2,14},{3,15},{4,0},{5,1},{6,2},{7,3},{8,4},{9,5},{1... | collective-permute-start | bytes 172040 | tf_op jit(solution)/shard_map/ppermute | solution.py:440
  67.2 8.4 %collective-permute-start.15 = (bf16[4,4608]{1,0:T(4,128)(2,1)S(1)}, bf16[4,4608]{1,0:T(4,128)(2,1)S(1)}, u32[]{:S(2)}, u32[]{:S(2)}) collective-permute-start(bf16[4,4608]{1,0:T(4,128)(2,1)S(1)} %get-tuple-element.80), channel_id=1, source_target_pairs={{0,4},{1,5},{2,6},{3,7},{4,8},{5,9},{6,10},{7,11},{8,12},{9,13},{1... | collective-permute-start | bytes 110600 | tf_op jit(solution)/shard_map/ppermute | solution.py:440
  67.4 8.2 %collective-permute-start.16 = (bf16[4,4608]{1,0:T(4,128)(2,1)S(1)}, bf16[4,4608]{1,0:T(4,128)(2,1)S(1)}, u32[]{:S(2)}, u32[]{:S(2)}) collective-permute-start(bf16[4,4608]{1,0:T(4,128)(2,1)S(1)} %get-tuple-element.81), channel_id=1, source_target_pairs={{0,8},{1,9},{2,10},{3,11},{4,12},{5,13},{6,14},{7,15},{8,0},{9,1},... | collective-permute-start | bytes 110600 | tf_op jit(solution)/shard_map/ppermute | solution.py:440
  69.4 6.2 %collective-permute-start.17 = (bf16[4,4608]{1,0:T(4,128)(2,1)S(1)}, bf16[4,4608]{1,0:T(4,128)(2,1)S(1)}, u32[]{:S(2)}, u32[]{:S(2)}) collective-permute-start(bf16[4,4608]{1,0:T(4,128)(2,1)S(1)} %get-tuple-element.82), channel_id=1, source_target_pairs={{0,12},{1,13},{2,14},{3,15},{4,0},{5,1},{6,2},{7,3},{8,4},{9,5},{1... | collective-permute-start | bytes 110600 | tf_op jit(solution)/shard_map/ppermute | solution.py:440
  71.7 3.9 %collective-permute-start.22 = (bf16[4,3584]{1,0:T(4,128)(2,1)S(1)}, bf16[4,3584]{1,0:T(4,128)(2,1)S(1)}, u32[]{:S(2)}, u32[]{:S(2)}) collective-permute-start(bf16[4,3584]{1,0:T(4,128)(2,1)S(1)} %get-tuple-element.91), channel_id=1, source_target_pairs={{0,2},{1,3},{2,0},{3,1},{4,6},{5,7},{6,4},{7,5},{8,10},{9,11},{10,... | collective-permute-start | bytes 86024 | tf_op jit(solution)/shard_map/ppermute | solution.py:440
  (9 other events, 51.0 us)

commit v16 on v8

--- a/solution.py
+++ b/solution.py
@@ -202,20 +202,19 @@
 
 
 def base_body(depth, start, stop, x_ref, q_ref, k_ref, v_ref, oq_ref, okv_ref):
-    oq_ref[...] = jnp.zeros_like(oq_ref)
-    okv_ref[...] = jnp.zeros_like(okv_ref)
     columns = k_ref.shape[0]
     narrow = jnp.zeros((HEAD - 2 * columns, depth), BF16)
-
-    @pl.loop(start // depth, stop // depth)
-    def _(i):
-        at = pl.ds(pl.multiple_of(i * depth, depth), depth)
+    query, fresh = 0.0, 0.0
+    for first in range(start, stop, depth):
+        at = slice(first, first + depth)
         x = x_ref[:, at]
-        oq_ref[...] += dot(x, q_ref[at, :])
+        query = query + dot(x, q_ref[at, :])
         both = (k_ref[:, at], v_ref[:, at])
         if 2 * columns < HEAD:
             both += (narrow,)
-        okv_ref[...] += dot_nt(x, jnp.concatenate(both, axis=0))
+        fresh = fresh + dot_nt(x, jnp.concatenate(both, axis=0))
+    oq_ref[...] = query
+    okv_ref[...] = fresh
 
 
 def turned(values, cosine, sine):
@@ -346,12 +345,10 @@
     half = mine_ref.shape[0]
     tile = 1024
 
-    @pl.loop(0, mine_ref.shape[1] // tile)
-    def _(i):
-        at = pl.ds(pl.multiple_of(i * tile, tile), tile)
-        product = dot(a_ref[...], w_ref[:, pl.ds(pl.multiple_of(start + i * tile, tile), tile)])
-        mine_ref[:, at] = product[:half]
-        other_ref[:, at] = product[half:]
+    for at in range(0, mine_ref.shape[1], tile):
+        product = dot(a_ref[...], w_ref[:, start + at : start + at + tile])
+        mine_ref[:, at : at + tile] = product[:half]
+        other_ref[:, at : at + tile] = product[half:]
 
 
 def far_first_body(near, mine_ref, came_ref, *refs):

time: 76.2 us -> 75.6 us (level)
  Pallas kernels: 12 us -> 10.9 us
    pallas_call x16, Pallas kernels: 12 us -> 10.9 us  [whole_call(): pl.pallas_call(body, out_shape=out_shape, in_specs=specs, out_specs=tuple...]
where the time goes in v16:
time: 75.6 us; the launch traced here: 75.3 us
  starting transfers between devices  24 us (32%)
  blocking collectives  19.6 us (26%)
  waiting for transfers between devices  18.8 us (25%)
  Pallas kernels  10.9 us (14%)
  local copies, waits for them, and re-layouts  1.02 us (1%)
  between operations  0.95 us (1%)
    ppermute x23, starting transfers between devices, shift(): return lax.ppermute(value, 'serve', partner(f, m, c))  24 us
    ppermute x23, waiting for transfers between devices, shift(): return lax.ppermute(value, 'serve', partner(f, m, c))  18.8 us
    pallas_call x16, Pallas kernels, whole_call(): pl.pallas_call(body, out_shape=out_shape, in_specs=specs, out_specs=tuple...  10.9 us
    all_to_all x1, blocking collectives, shards(): lax.all_to_all(ready, 'serve', split_axis=0, concat_axis=0, tiled=True)  10.1 us
    all_to_all x1, blocking collectives, shards(): lax.all_to_all(context, 'serve', split_axis=0, concat_axis=0, tiled=True)  9.48 us
  transfers between devices with their start and end apart: 23, of which 10 were waited for; matrix products, arithmetic and copies ran while one was open for 0% of the time, Pallas kernels for 7%

profile of v16, /device:TPU:0, one launch (start us, length us, event | category | flops | bytes accessed | tf_op | source)
XLA Modules:
  0.0 75.3 jit_solution(11260597538901450144)
XLA Ops:
  0.7 0.6 copy-done.10
  1.8 3.0 %collective-permute-start.3 = (bf16[1,4,8192]{2,1,0:T(4,128)(2,1)S(1)}, bf16[1,4,8192]{2,1,0:T(4,128)(2,1)S(1)}, u32[]{:S(2)}, u32[]{:S(2)}) collective-permute-start(bf16[1,4,8192]{2,1,0:T(4,128)(2,1)S(1)} %bitcast.24), channel_id=1, source_target_pairs={{0,2},{1,3},{2,0},{3,1},{4,6},{5,7},{6,4},{7,5},{8,10},{9,11},{10,... | collective-permute-start | bytes 196616 | tf_op jit(solution)/shard_map/ppermute | solution.py:437
  4.9 3.6 %collective-permute-start.2 = (bf16[1,4,8192]{2,1,0:T(4,128)(2,1)S(1)}, bf16[1,4,8192]{2,1,0:T(4,128)(2,1)S(1)}, u32[]{:S(2)}, u32[]{:S(2)}) collective-permute-start(bf16[1,4,8192]{2,1,0:T(4,128)(2,1)S(1)} %bitcast.25), channel_id=1, source_target_pairs={{0,12},{1,13},{2,14},{3,15},{4,0},{5,1},{6,2},{7,3},{8,4},{9,5},{1... | collective-permute-start | bytes 196616 | tf_op jit(solution)/shard_map/ppermute | solution.py:437
  8.5 1.0 %collective-permute-start = (bf16[1,4,8192]{2,1,0:T(4,128)(2,1)S(1)}, bf16[1,4,8192]{2,1,0:T(4,128)(2,1)S(1)}, u32[]{:S(2)}, u32[]{:S(2)}) collective-permute-start(bf16[1,4,8192]{2,1,0:T(4,128)(2,1)S(1)} %bitcast.27), channel_id=1, source_target_pairs={{0,4},{1,5},{2,6},{3,7},{4,8},{5,9},{6,10},{7,11},{8,12},{9,13},{1... | collective-permute-start | bytes 196616 | tf_op jit(solution)/shard_map/ppermute | solution.py:437
  9.5 5.1 %collective-permute-done = bf16[1,4,8192]{2,1,0:T(4,128)(2,1)S(1)} collective-permute-done((bf16[1,4,8192]{2,1,0:T(4,128)(2,1)S(1)}, bf16[1,4,8192]{2,1,0:T(4,128)(2,1)S(1)}, u32[]{:S(2)}, u32[]{:S(2)}) %collective-permute-start) | collective-permute-done | bytes 65568 | tf_op jit(solution)/shard_map/ppermute | solution.py:437
  15.6 1.8 %shard_map.185 = (s32[64,1]{1,0:T(8,128)S(1)}, s32[64,1]{1,0:T(8,128)S(1)}, f32[64,128]{1,0:T(8,128)S(1)}, f32[64,128]{1,0:T(8,128)S(1)}, f32[64,128]{1,0:T(8,12...) custom-call(s32[1]{0:T(128)} %bitcast.index_ref, ...), custom_call_target="tpu_custom_call" | custom-call | flops 4600000000 | tf_op jit(solution)/shard_map/pallas_call | solution.py:36
  17.4 3.2 %collective-permute-done.4.refs_1_ = bf16[3,4,8192]{2,1,0:T(4,128)(2,1)S(1)} collective-permute-done((bf16[3,4,8192]{2,1,0:T(4,128)(2,1)S(1)}, bf16[3,4,8192]{2,1,0:T(4,128)(2,1)S(1)}, u32[]{:S(2)}, u32[]{:S(2)}) %collective-permute-start.4) | collective-permute-done | bytes 196640 | tf_op jit(solution)/shard_map/ppermute | solution.py:437
  20.6 1.4 %collective-permute-done.6.refs_3_ = bf16[3,4,8192]{2,1,0:T(4,128)(2,1)S(1)} collective-permute-done((bf16[3,4,8192]{2,1,0:T(4,128)(2,1)S(1)}, bf16[3,4,8192]{2,1,0:T(4,128)(2,1)S(1)}, u32[]{:S(2)}, u32[]{:S(2)}) %collective-permute-start.6) | collective-permute-done | bytes 196640 | tf_op jit(solution)/shard_map/ppermute | solution.py:437
  22.1 0.7 shard_map.186
  23.1 1.5 %collective-permute-start.8 = (bf16[16,128]{1,0:T(8,128)(2,1)S(1)}, bf16[16,128]{1,0:T(8,128)(2,1)S(1)}, u32[]{:S(2)}, u32[]{:S(2)}) collective-permute-start(bf16[16,128]{1,0:T(8,128)(2,1)S(1)} %get-tuple-element.57.refs_0_), channel_id=1, source_target_pairs={{0,2},{1,3},{2,0},{3,1},{4,6},{5,7},{6,4},{7,5},{8,10},{9,11},{10,... | collective-permute-start | bytes 12296 | tf_op jit(solution)/shard_map/ppermute | solution.py:437
  24.7 1.2 %shard_map.188 = (f32[64,512]{1,0:T(8,128)S(1)}, f32[64,128]{1,0:T(8,128)S(1)}) custom-call(bf16[64,8192]{1,0:T(8,128)(2,1)S(1)} %get-tuple-element.58.x_ref, bf16[8192,512]{1,0:T(8,128)(2,1)S(1)} %bitcast.15, bf16[64,8192]{1,0:T(8,128)(2,1)S(1)} %bitcast.18, bf16[64,8192]{1,0:T(8,128)(2,1)S(1)} %bitcast.20), custom_call_target="tpu_custom_call" | custom-call | flops 345000000 | tf_op jit(solution)/shard_map/pallas_call | solution.py:36
  26.0 0.7 collective-permute-done.8.refs_2_
  26.7 1.8 %collective-permute-start.12 = (bf16[16,128]{1,0:T(8,128)(2,1)S(1)}, bf16[16,128]{1,0:T(8,128)(2,1)S(1)}, u32[]{:S(2)}, u32[]{:S(2)}) collective-permute-start(bf16[16,128]{1,0:T(8,128)(2,1)S(1)} %shard_map.187.refs_0_), channel_id=1, source_target_pairs={{0,12},{1,13},{2,14},{3,15},{4,0},{5,1},{6,2},{7,3},{8,4},{9,5},{1... | collective-permute-start | bytes 12296 | tf_op jit(solution)/shard_map/ppermute | solution.py:437
  29.2 1.9 %collective-permute-start.10 = (bf16[16,128]{1,0:T(8,128)(2,1)S(1)}, bf16[16,128]{1,0:T(8,128)(2,1)S(1)}, u32[]{:S(2)}, u32[]{:S(2)}) collective-permute-start(bf16[16,128]{1,0:T(8,128)(2,1)S(1)} %shard_map.187.refs_0_), channel_id=1, source_target_pairs={{0,4},{1,5},{2,6},{3,7},{4,8},{5,9},{6,10},{7,11},{8,12},{9,13},{1... | collective-permute-start | bytes 12296 | tf_op jit(solution)/shard_map/ppermute | solution.py:437
  31.1 1.2 %shard_map.189 = (f32[64,512]{1,0:T(8,128)S(1)}, f32[64,128]{1,0:T(8,128)S(1)}) custom-call(bf16[64,8192]{1,0:T(8,128)(2,1)S(1)} %get-tuple-element.58.x_ref, bf16[8192,512]{1,0:T(8,128)(2,1)S(1)} %bitcast.15, bf16[64,8192]{1,0:T(8,128)(2,1)S(1)} %bitcast.19, bf16[64,8192]{1,0:T(8,128)(2,1)S(1)} %bitcast.21), custom_call_target="tpu_custom_call" | custom-call | flops 345000000 | tf_op jit(solution)/shard_map/pallas_call | solution.py:36
  32.3 0.7 collective-permute-done.11.refs_2_
  33.1 1.5 %collective-permute-done.10.refs_1_ = bf16[16,128]{1,0:T(8,128)(2,1)S(1)} collective-permute-done((bf16[16,128]{1,0:T(8,128)(2,1)S(1)}, bf16[16,128]{1,0:T(8,128)(2,1)S(1)}, u32[]{:S(2)}, u32[]{:S(2)}) %collective-permute-start.10) | collective-permute-done | bytes 4128 | tf_op jit(solution)/shard_map/ppermute | solution.py:437
  34.6 0.8 %shard_map.190 = bf16[16,24,128]{2,1,0:T(8,128)(2,1)S(1)} custom-call(bf16[16,128]{1,0:T(8,128)(2,1)S(1)} %shard_map.187.refs_0_, bf16[16,128]{1,0:T(8,128)(2,1)S(1)} %collective-permute-done.10.refs_1_, bf16[16,128]{1,0:T(8,128)(2,1)S(1)} %collective-permute-done.11.refs_2_, bf16[16,128]{1,0:T(8,128)(2,1)S(1)} %collective-permute-done.12.refs_3_, ...), custom_call_target="tpu_custom_call" | custom-call | flops 1035000000 | tf_op jit(solution)/shard_map/pallas_call | solution.py:36
  35.4 10.1 %all_to_all.10.x_ref = bf16[16,24,128]{2,1,0:T(8,128)(2,1)S(1)} all-to-all(bf16[16,24,128]{2,1,0:T(8,128)(2,1)S(1)} %shard_map.190), channel_id=1, replica_groups=mesh['replica'=2,'serve'=16] {'serve'}, dimensions={0} | all-to-all | bytes 196608 | tf_op jit(solution)/shard_map/all_to_all | solution.py:545
  45.6 2.0 %shard_map.191 = (bf16[2,2,1024]{2,1,0:T(2,128)(2,1)}, bf16[2,2,1024]{2,1,0:T(2,128)(2,1)}, bf16[16,16,128]{2,1,0:T(8,128)(2,1)S(1)}) custom-call(s32[1]{0:T(128)} %bitcast.index_ref, s32[32]{0:T(128)S(1)} %copy-done.13, bf16[16,24,128]{2,1,0:T(8,128)(2,1)S(1)} %all_to_all.10.x_ref, bf16[256,384]{1,0:T(8,128)(2,1)S(1)} %get-tuple-element.72.order_ref, ...), custom_call_target="tpu_custom_call" | custom-call | flops 1150000000 | tf_op jit(solution)/shard_map/pallas_call | solution.py:36
  47.5 9.5 %all_to_all.11.ctx_ref = bf16[16,16,128]{2,1,0:T(8,128)(2,1)S(1)} all-to-all(bf16[16,16,128]{2,1,0:T(8,128)(2,1)S(1)} %get-tuple-element.73), channel_id=1, replica_groups=mesh['replica'=2,'serve'=16] {'serve'}, dimensions={0} | all-to-all | bytes 131072 | tf_op jit(solution)/shard_map/all_to_all | solution.py:556
  57.0 1.2 %shard_map.192 = (bf16[64,512]{1,0:T(8,128)(2,1)S(1)}, f32[32,5120]{1,0:T(8,128)S(1)}, f32[32,5120]{1,0:T(8,128)S(1)}) custom-call(bf16[16,16,128]{2,1,0:T(8,128)(2,1)S(1)} %all_to_all.11.ctx_ref, bf16[256,256]{1,0:T(8,128)(2,1)S(1)} %get-tuple-element.74.take_ref, bf16[512,8192]{1,0:T(8,128)(2,1)S(1)} %bitcast.17), custom_call_target="tpu_custom_call" | custom-call | flops 460000000 | tf_op jit(solution)/shard_map/pallas_call | solution.py:36
  58.3 0.7 shard_map.195
  59.5 0.9 %collective-permute-done.13.came_ref = f32[32,5120]{1,0:T(8,128)S(1)} collective-permute-done((f32[32,5120]{1,0:T(8,128)S(1)}, f32[32,5120]{1,0:T(8,128)S(1)}, u32[]{:S(2)}, u32[]{:S(2)}) %collective-permute-start.13) | collective-permute-done | bytes 655392 | tf_op jit(solution)/shard_map/ppermute | solution.py:437
  61.4 1.0 %collective-permute-start.20 = (bf16[8,3072]{1,0:T(8,128)(2,1)S(1)}, bf16[8,3072]{1,0:T(8,128)(2,1)S(1)}, u32[]{:S(2)}, u32[]{:S(2)}) collective-permute-start(bf16[8,3072]{1,0:T(8,128)(2,1)S(1)} %get-tuple-element.88), channel_id=1, source_target_pairs={{0,8},{1,9},{2,10},{3,11},{4,12},{5,13},{6,14},{7,15},{8,0},{9,1},... | collective-permute-start | bytes 147464 | tf_op jit(solution)/shard_map/ppermute | solution.py:437
  62.3 2.5 %collective-permute-start.21 = (bf16[8,3072]{1,0:T(8,128)(2,1)S(1)}, bf16[8,3072]{1,0:T(8,128)(2,1)S(1)}, u32[]{:S(2)}, u32[]{:S(2)}) collective-permute-start(bf16[8,3072]{1,0:T(8,128)(2,1)S(1)} %get-tuple-element.89), channel_id=1, source_target_pairs={{0,12},{1,13},{2,14},{3,15},{4,0},{5,1},{6,2},{7,3},{8,4},{9,5},{1... | collective-permute-start | bytes 147464 | tf_op jit(solution)/shard_map/ppermute | solution.py:437
  64.9 1.9 %collective-permute-done.14.refs_1_ = bf16[16,5120]{1,0:T(8,128)(2,1)S(1)} collective-permute-done((bf16[16,5120]{1,0:T(8,128)(2,1)S(1)}, bf16[16,5120]{1,0:T(8,128)(2,1)S(1)}, u32[]{:S(2)}, u32[]{:S(2)}) %collective-permute-start.14) | collective-permute-done | bytes 163872 | tf_op jit(solution)/shard_map/ppermute | solution.py:437
  67.0 0.9 %collective-permute-start.16 = (bf16[4,5120]{1,0:T(4,128)(2,1)S(1)}, bf16[4,5120]{1,0:T(4,128)(2,1)S(1)}, u32[]{:S(2)}, u32[]{:S(2)}) collective-permute-start(bf16[4,5120]{1,0:T(4,128)(2,1)S(1)} %get-tuple-element.81), channel_id=1, source_target_pairs={{0,8},{1,9},{2,10},{3,11},{4,12},{5,13},{6,14},{7,15},{8,0},{9,1},... | collective-permute-start | bytes 122888 | tf_op jit(solution)/shard_map/ppermute | solution.py:437
  67.9 2.8 %collective-permute-start.17 = (bf16[4,5120]{1,0:T(4,128)(2,1)S(1)}, bf16[4,5120]{1,0:T(4,128)(2,1)S(1)}, u32[]{:S(2)}, u32[]{:S(2)}) collective-permute-start(bf16[4,5120]{1,0:T(4,128)(2,1)S(1)} %get-tuple-element.82), channel_id=1, source_target_pairs={{0,12},{1,13},{2,14},{3,15},{4,0},{5,1},{6,2},{7,3},{8,4},{9,5},{1... | collective-permute-start | bytes 122888 | tf_op jit(solution)/shard_map/ppermute | solution.py:437
  70.7 0.9 %collective-permute-start.22 = (bf16[4,3072]{1,0:T(4,128)(2,1)S(1)}, bf16[4,3072]{1,0:T(4,128)(2,1)S(1)}, u32[]{:S(2)}, u32[]{:S(2)}) collective-permute-start(bf16[4,3072]{1,0:T(4,128)(2,1)S(1)} %get-tuple-element.91), channel_id=1, source_target_pairs={{0,2},{1,3},{2,0},{3,1},{4,6},{5,7},{6,4},{7,5},{8,10},{9,11},{10,... | collective-permute-start | bytes 73736 | tf_op jit(solution)/shard_map/ppermute | solution.py:437
  71.6 3.0 %collective-permute-done.22.refs_5_ = bf16[4,3072]{1,0:T(4,128)(2,1)S(1)} collective-permute-done((bf16[4,3072]{1,0:T(4,128)(2,1)S(1)}, bf16[4,3072]{1,0:T(4,128)(2,1)S(1)}, u32[]{:S(2)}, u32[]{:S(2)}) %collective-permute-start.22) | collective-permute-done | bytes 24608 | tf_op jit(solution)/shard_map/ppermute | solution.py:437
  74.6 0.7 shard_map.198
  (75 shorter events, 4.3 us)
Async XLA Ops:
  0.7 14.9 %copy-start.13 = (s32[32]{0:T(128)S(1)}, s32[32]{0:T(128)}, u32[]{:S(2)}) copy-start(s32[32]{0:T(128)} %len_ref.1) | copy-start | bytes 388
  0.7 14.9 %copy-start.12 = (s32[32]{0:T(128)S(1)}, s32[32]{0:T(128)}, u32[]{:S(2)}) copy-start(s32[32]{0:T(128)} %slot_hbm.1) | copy-start | bytes 388
  0.7 14.9 %copy-start.11 = (s32[32]{0:T(128)S(1)}, s32[32]{0:T(128)}, u32[]{:S(2)}) copy-start(s32[32]{0:T(128)} %adapter_hbm.1) | copy-start | bytes 388
  1.8 13.6 %collective-permute-start.3 = (bf16[1,4,8192]{2,1,0:T(4,128)(2,1)S(1)}, bf16[1,4,8192]{2,1,0:T(4,128)(2,1)S(1)}, u32[]{:S(2)}, u32[]{:S(2)}) collective-permute-start(bf16[1,4,8192]{2,1,0:T(4,128)(2,1)S(1)} %bitcast.24), channel_id=1, source_target_pairs={{0,2},{1,3},{2,0},{3,1},{4,6},{5,7},{6,4},{7,5},{8,10},{9,11},{10,... | collective-permute-start | bytes 196616 | tf_op jit(solution)/shard_map/ppermute | solution.py:437
  4.9 9.9 %collective-permute-start.2 = (bf16[1,4,8192]{2,1,0:T(4,128)(2,1)S(1)}, bf16[1,4,8192]{2,1,0:T(4,128)(2,1)S(1)}, u32[]{:S(2)}, u32[]{:S(2)}) collective-permute-start(bf16[1,4,8192]{2,1,0:T(4,128)(2,1)S(1)} %bitcast.25), channel_id=1, source_target_pairs={{0,12},{1,13},{2,14},{3,15},{4,0},{5,1},{6,2},{7,3},{8,4},{9,5},{1... | collective-permute-start | bytes 196616 | tf_op jit(solution)/shard_map/ppermute | solution.py:437
  8.5 6.2 %collective-permute-start.1 = (bf16[1,4,8192]{2,1,0:T(4,128)(2,1)S(1)}, bf16[1,4,8192]{2,1,0:T(4,128)(2,1)S(1)}, u32[]{:S(2)}, u32[]{:S(2)}) collective-permute-start(bf16[1,4,8192]{2,1,0:T(4,128)(2,1)S(1)} %bitcast.26), channel_id=1, source_target_pairs={{0,8},{1,9},{2,10},{3,11},{4,12},{5,13},{6,14},{7,15},{8,0},{9,1},... | collective-permute-start | bytes 196616 | tf_op jit(solution)/shard_map/ppermute | solution.py:437
  8.5 6.2 %collective-permute-start = (bf16[1,4,8192]{2,1,0:T(4,128)(2,1)S(1)}, bf16[1,4,8192]{2,1,0:T(4,128)(2,1)S(1)}, u32[]{:S(2)}, u32[]{:S(2)}) collective-permute-start(bf16[1,4,8192]{2,1,0:T(4,128)(2,1)S(1)} %bitcast.27), channel_id=1, source_target_pairs={{0,4},{1,5},{2,6},{3,7},{4,8},{5,9},{6,10},{7,11},{8,12},{9,13},{1... | collective-permute-start | bytes 196616 | tf_op jit(solution)/shard_map/ppermute | solution.py:437
  14.8 5.8 %collective-permute-start.4 = (bf16[3,4,8192]{2,1,0:T(4,128)(2,1)S(1)}, bf16[3,4,8192]{2,1,0:T(4,128)(2,1)S(1)}, u32[]{:S(2)}, u32[]{:S(2)}) collective-permute-start(bf16[3,4,8192]{2,1,0:T(4,128)(2,1)S(1)} %get-tuple-element.96), channel_id=1, source_target_pairs={{0,2},{1,3},{2,0},{3,1},{4,6},{5,7},{6,4},{7,5},{8,10},{9,11},{10,... | collective-permute-start | bytes 589832 | tf_op jit(solution)/shard_map/ppermute | solution.py:437
  15.4 9.3 %slice-start = ((s8[8388608]{0:T(1024)(128)(4,1)}), s8[4194304]{0:T(1024)(128)(4,1)S(1)}, s32[]{:S(2)}) async-start(s8[8388608]{0:T(1024)(128)(4,1)} %bitcast.14), calls=%async_computation.2 | async-start | bytes 8388608
  15.4 9.2 %slice-start.1 = ((s8[8388608]{0:T(1024)(128)(4,1)}), s8[4194304]{0:T(1024)(128)(4,1)S(1)}, s32[]{:S(2)}) async-start(s8[8388608]{0:T(1024)(128)(4,1)} %bitcast.14), calls=%async_computation.3 | async-start | bytes 8388608
  15.5 5.1 %collective-permute-start.5 = (bf16[5,4,8192]{2,1,0:T(4,128)(2,1)S(1)}, bf16[5,4,8192]{2,1,0:T(4,128)(2,1)S(1)}, u32[]{:S(2)}, u32[]{:S(2)}) collective-permute-start(bf16[5,4,8192]{2,1,0:T(4,128)(2,1)S(1)} %constant_dynamic-update-slice_fusion.refs_0_), channel_id=1, source_target_pairs={{0,1},{1,0},{2,3},{3,2},{4,5},{5,4},{6,7},{7,6},{8,9},{9,8},{10,11... | collective-permute-start | bytes 983048 | tf_op jit(solution)/shard_map/ppermute | solution.py:437
  20.6 1.4 %collective-permute-start.6 = (bf16[3,4,8192]{2,1,0:T(4,128)(2,1)S(1)}, bf16[3,4,8192]{2,1,0:T(4,128)(2,1)S(1)}, u32[]{:S(2)}, u32[]{:S(2)}) collective-permute-start(bf16[3,4,8192]{2,1,0:T(4,128)(2,1)S(1)} %collective-permute-done.4.refs_1_), channel_id=1, source_target_pairs={{0,1},{1,0},{2,3},{3,2},{4,5},{5,4},{6,7},{7,6},{8,9},{9,8},{10,11... | collective-permute-start | bytes 589832 | tf_op jit(solution)/shard_map/ppermute | solution.py:437
  22.8 3.2 %collective-permute-start.9 = (bf16[16,128]{1,0:T(8,128)(2,1)S(1)}, bf16[16,128]{1,0:T(8,128)(2,1)S(1)}, u32[]{:S(2)}, u32[]{:S(2)}) collective-permute-start(bf16[16,128]{1,0:T(8,128)(2,1)S(1)} %get-tuple-element.57.refs_0_), channel_id=1, source_target_pairs={{0,3},{1,2},{2,1},{3,0},{4,7},{5,6},{6,5},{7,4},{8,11},{9,10},{10,... | collective-permute-start | bytes 12296 | tf_op jit(solution)/shard_map/ppermute | solution.py:437
  23.1 3.6 %collective-permute-start.8 = (bf16[16,128]{1,0:T(8,128)(2,1)S(1)}, bf16[16,128]{1,0:T(8,128)(2,1)S(1)}, u32[]{:S(2)}, u32[]{:S(2)}) collective-permute-start(bf16[16,128]{1,0:T(8,128)(2,1)S(1)} %get-tuple-element.57.refs_0_), channel_id=1, source_target_pairs={{0,2},{1,3},{2,0},{3,1},{4,6},{5,7},{6,4},{7,5},{8,10},{9,11},{10,... | collective-permute-start | bytes 12296 | tf_op jit(solution)/shard_map/ppermute | solution.py:437
  24.6 2.1 %collective-permute-start.7 = (bf16[16,128]{1,0:T(8,128)(2,1)S(1)}, bf16[16,128]{1,0:T(8,128)(2,1)S(1)}, u32[]{:S(2)}, u32[]{:S(2)}) collective-permute-start(bf16[16,128]{1,0:T(8,128)(2,1)S(1)} %get-tuple-element.57.refs_0_), channel_id=1, source_target_pairs={{0,1},{1,0},{2,3},{3,2},{4,5},{5,4},{6,7},{7,6},{8,9},{9,8},{10,11... | collective-permute-start | bytes 12296 | tf_op jit(solution)/shard_map/ppermute | solution.py:437
  25.9 19.6 %copy-start.4 = (bf16[2,384,1024]{2,1,0:T(8,128)(2,1)S(1)}, bf16[2,384,1024]{2,1,0:T(8,128)(2,1)}, u32[]{:S(2)}) copy-start(bf16[2,384,1024]{2,1,0:T(8,128)(2,1)} %k_ref.1) | copy-start | bytes 4718596
  25.9 19.6 %copy-start.5 = (bf16[2,384,1024]{2,1,0:T(8,128)(2,1)S(1)}, bf16[2,384,1024]{2,1,0:T(8,128)(2,1)}, u32[]{:S(2)}) copy-start(bf16[2,384,1024]{2,1,0:T(8,128)(2,1)} %v_ref.1) | copy-start | bytes 4718596
  26.7 30.3 %slice-start.2 = ((s8[8388608]{0:T(1024)(128)(4,1)}), s8[4194304]{0:T(1024)(128)(4,1)S(1)}, s32[]{:S(2)}) async-start(s8[8388608]{0:T(1024)(128)(4,1)} %bitcast.16), calls=%async_computation.4 | async-start | bytes 8388608
  26.7 30.3 %slice-start.3 = ((s8[8388608]{0:T(1024)(128)(4,1)}), s8[4194304]{0:T(1024)(128)(4,1)S(1)}, s32[]{:S(2)}) async-start(s8[8388608]{0:T(1024)(128)(4,1)} %bitcast.16), calls=%async_computation.5 | async-start | bytes 8388608
  26.7 5.6 %collective-permute-start.12 = (bf16[16,128]{1,0:T(8,128)(2,1)S(1)}, bf16[16,128]{1,0:T(8,128)(2,1)S(1)}, u32[]{:S(2)}, u32[]{:S(2)}) collective-permute-start(bf16[16,128]{1,0:T(8,128)(2,1)S(1)} %shard_map.187.refs_0_), channel_id=1, source_target_pairs={{0,12},{1,13},{2,14},{3,15},{4,0},{5,1},{6,2},{7,3},{8,4},{9,5},{1... | collective-permute-start | bytes 12296 | tf_op jit(solution)/shard_map/ppermute | solution.py:437
  28.6 4.5 %collective-permute-start.11 = (bf16[16,128]{1,0:T(8,128)(2,1)S(1)}, bf16[16,128]{1,0:T(8,128)(2,1)S(1)}, u32[]{:S(2)}, u32[]{:S(2)}) collective-permute-start(bf16[16,128]{1,0:T(8,128)(2,1)S(1)} %shard_map.187.refs_0_), channel_id=1, source_target_pairs={{0,8},{1,9},{2,10},{3,11},{4,12},{5,13},{6,14},{7,15},{8,0},{9,1},... | collective-permute-start | bytes 12296 | tf_op jit(solution)/shard_map/ppermute | solution.py:437
  29.2 5.4 %collective-permute-start.10 = (bf16[16,128]{1,0:T(8,128)(2,1)S(1)}, bf16[16,128]{1,0:T(8,128)(2,1)S(1)}, u32[]{:S(2)}, u32[]{:S(2)}) collective-permute-start(bf16[16,128]{1,0:T(8,128)(2,1)S(1)} %shard_map.187.refs_0_), channel_id=1, source_target_pairs={{0,4},{1,5},{2,6},{3,7},{4,8},{5,9},{6,10},{7,11},{8,12},{9,13},{1... | collective-permute-start | bytes 12296 | tf_op jit(solution)/shard_map/ppermute | solution.py:437
  58.2 2.2 %collective-permute-start.13 = (f32[32,5120]{1,0:T(8,128)S(1)}, f32[32,5120]{1,0:T(8,128)S(1)}, u32[]{:S(2)}, u32[]{:S(2)}) collective-permute-start(f32[32,5120]{1,0:T(8,128)S(1)} %get-tuple-element.76), channel_id=1, source_target_pairs={{0,1},{1,0},{2,3},{3,2},{4,5},{5,4},{6,7},{7,6},{8,9},{9,8},{10,11... | collective-permute-start | bytes 1966088 | tf_op jit(solution)/shard_map/ppermute | solution.py:437
  58.9 2.0 %collective-permute-start.18 = (f32[32,3072]{1,0:T(8,128)S(1)}, f32[32,3072]{1,0:T(8,128)S(1)}, u32[]{:S(2)}, u32[]{:S(2)}) collective-permute-start(f32[32,3072]{1,0:T(8,128)S(1)} %get-tuple-element.85), channel_id=1, source_target_pairs={{0,1},{1,0},{2,3},{3,2},{4,5},{5,4},{6,7},{7,6},{8,9},{9,8},{10,11... | collective-permute-start | bytes 1179656 | tf_op jit(solution)/shard_map/ppermute | solution.py:437
  60.4 6.3 %collective-permute-start.14 = (bf16[16,5120]{1,0:T(8,128)(2,1)S(1)}, bf16[16,5120]{1,0:T(8,128)(2,1)S(1)}, u32[]{:S(2)}, u32[]{:S(2)}) collective-permute-start(bf16[16,5120]{1,0:T(8,128)(2,1)S(1)} %get-tuple-element.78), channel_id=1, source_target_pairs={{0,2},{1,3},{2,0},{3,1},{4,6},{5,7},{6,4},{7,5},{8,10},{9,11},{10,... | collective-permute-start | bytes 491528 | tf_op jit(solution)/shard_map/ppermute | solution.py:437
  61.0 6.9 %collective-permute-start.19 = (bf16[8,3072]{1,0:T(8,128)(2,1)S(1)}, bf16[8,3072]{1,0:T(8,128)(2,1)S(1)}, u32[]{:S(2)}, u32[]{:S(2)}) collective-permute-start(bf16[8,3072]{1,0:T(8,128)(2,1)S(1)} %get-tuple-element.87), channel_id=1, source_target_pairs={{0,4},{1,5},{2,6},{3,7},{4,8},{5,9},{6,10},{7,11},{8,12},{9,13},{1... | collective-permute-start | bytes 147464 | tf_op jit(solution)/shard_map/ppermute | solution.py:437
  61.4 9.3 %collective-permute-start.20 = (bf16[8,3072]{1,0:T(8,128)(2,1)S(1)}, bf16[8,3072]{1,0:T(8,128)(2,1)S(1)}, u32[]{:S(2)}, u32[]{:S(2)}) collective-permute-start(bf16[8,3072]{1,0:T(8,128)(2,1)S(1)} %get-tuple-element.88), channel_id=1, source_target_pairs={{0,8},{1,9},{2,10},{3,11},{4,12},{5,13},{6,14},{7,15},{8,0},{9,1},... | collective-permute-start | bytes 147464 | tf_op jit(solution)/shard_map/ppermute | solution.py:437
  62.3 8.3 %collective-permute-start.21 = (bf16[8,3072]{1,0:T(8,128)(2,1)S(1)}, bf16[8,3072]{1,0:T(8,128)(2,1)S(1)}, u32[]{:S(2)}, u32[]{:S(2)}) collective-permute-start(bf16[8,3072]{1,0:T(8,128)(2,1)S(1)} %get-tuple-element.89), channel_id=1, source_target_pairs={{0,12},{1,13},{2,14},{3,15},{4,0},{5,1},{6,2},{7,3},{8,4},{9,5},{1... | collective-permute-start | bytes 147464 | tf_op jit(solution)/shard_map/ppermute | solution.py:437
  66.8 7.8 %collective-permute-start.15 = (bf16[4,5120]{1,0:T(4,128)(2,1)S(1)}, bf16[4,5120]{1,0:T(4,128)(2,1)S(1)}, u32[]{:S(2)}, u32[]{:S(2)}) collective-permute-start(bf16[4,5120]{1,0:T(4,128)(2,1)S(1)} %get-tuple-element.80), channel_id=1, source_target_pairs={{0,4},{1,5},{2,6},{3,7},{4,8},{5,9},{6,10},{7,11},{8,12},{9,13},{1... | collective-permute-start | bytes 122888 | tf_op jit(solution)/shard_map/ppermute | solution.py:437
  67.0 7.6 %collective-permute-start.16 = (bf16[4,5120]{1,0:T(4,128)(2,1)S(1)}, bf16[4,5120]{1,0:T(4,128)(2,1)S(1)}, u32[]{:S(2)}, u32[]{:S(2)}) collective-permute-start(bf16[4,5120]{1,0:T(4,128)(2,1)S(1)} %get-tuple-element.81), channel_id=1, source_target_pairs={{0,8},{1,9},{2,10},{3,11},{4,12},{5,13},{6,14},{7,15},{8,0},{9,1},... | collective-permute-start | bytes 122888 | tf_op jit(solution)/shard_map/ppermute | solution.py:437
  67.9 6.7 %collective-permute-start.17 = (bf16[4,5120]{1,0:T(4,128)(2,1)S(1)}, bf16[4,5120]{1,0:T(4,128)(2,1)S(1)}, u32[]{:S(2)}, u32[]{:S(2)}) collective-permute-start(bf16[4,5120]{1,0:T(4,128)(2,1)S(1)} %get-tuple-element.82), channel_id=1, source_target_pairs={{0,12},{1,13},{2,14},{3,15},{4,0},{5,1},{6,2},{7,3},{8,4},{9,5},{1... | collective-permute-start | bytes 122888 | tf_op jit(solution)/shard_map/ppermute | solution.py:437
  70.7 3.9 %collective-permute-start.22 = (bf16[4,3072]{1,0:T(4,128)(2,1)S(1)}, bf16[4,3072]{1,0:T(4,128)(2,1)S(1)}, u32[]{:S(2)}, u32[]{:S(2)}) collective-permute-start(bf16[4,3072]{1,0:T(4,128)(2,1)S(1)} %get-tuple-element.91), channel_id=1, source_target_pairs={{0,2},{1,3},{2,0},{3,1},{4,6},{5,7},{6,4},{7,5},{8,10},{9,11},{10,... | collective-permute-start | bytes 73736 | tf_op jit(solution)/shard_map/ppermute | solution.py:437
  (9 other events, 51.3 us)

commit v17 on v16

--- a/solution.py
+++ b/solution.py
@@ -454,12 +454,6 @@
     )
     normed = normed[None]
     fars = [shift(normed, f, 0, 0) for f in range(1, far)]
-    nears = [shift(normed, 0, m, 0) for m in range(1, near)]
-    rest = jnp.concatenate(fars)
-    groups = [jnp.concatenate([normed, *fars, *nears[:1]])]
-    groups += [shift(rest, 0, m, 0) for m in range(1, near)]
-
-    rest, at = lax.optimization_barrier((rest, index[None]))
     sent = -(-(rows * local + rows) // 8) * 8
     narrow = jax.ShapeDtypeStruct((all_rows, 1), jnp.int32)
     table = jax.ShapeDtypeStruct((all_rows, HEAD), F32)
@@ -479,7 +473,7 @@
             jax.ShapeDtypeStruct((own * HEADS * STEPS, n * sent), BF16),
             jax.ShapeDtypeStruct((all_rows * local, n * rows * local), BF16),
         ),
-        (at, lengths, request_adapter, adapter_slot, frequency),
+        (index[None], lengths, request_adapter, adapter_slot, frequency),
         smem=1,
         hbm=3,
         scratch=[
@@ -490,7 +484,11 @@
         ],
         cost=4.0,
     )
-    slot, groups[1] = lax.optimization_barrier((slot, groups[1]))
+    slot, ready_rows = lax.optimization_barrier((slot, normed))
+    nears = [shift(ready_rows, 0, m, 0) for m in range(1, near)]
+    rest = jnp.concatenate(fars)
+    groups = [jnp.concatenate([normed, *fars, *nears[:1]])]
+    groups += [shift(rest, 0, m, 0) for m in range(1, near)]
 
     groups += [shift(part, 0, 0, c) for c in range(1, cores) for part in groups[:near]]
 

time: 75.6 us -> 75.5 us (level)
  no operation moved by 1% of the time
where the time goes in v17:
time: 75.5 us; the launch traced here: 75.1 us
  starting transfers between devices  24.2 us (32%)
  blocking collectives  19.5 us (26%)
  waiting for transfers between devices  18.4 us (24%)
  Pallas kernels  10.9 us (14%)
  local copies, waits for them, and re-layouts  0.97 us (1%)
  between operations  0.93 us (1%)
    ppermute x23, starting transfers between devices, shift(): return lax.ppermute(value, 'serve', partner(f, m, c))  24.2 us
    ppermute x23, waiting for transfers between devices, shift(): return lax.ppermute(value, 'serve', partner(f, m, c))  18.4 us
    pallas_call x16, Pallas kernels, whole_call(): pl.pallas_call(body, out_shape=out_shape, in_specs=specs, out_specs=tuple...  10.9 us
    all_to_all x1, blocking collectives, shards(): lax.all_to_all(ready, 'serve', split_axis=0, concat_axis=0, tiled=True)  9.99 us
    all_to_all x1, blocking collectives, shards(): lax.all_to_all(context, 'serve', split_axis=0, concat_axis=0, tiled=True)  9.48 us
  transfers between devices with their start and end apart: 23, of which 10 were waited for; matrix products, arithmetic and copies ran while one was open for 0% of the time, Pallas kernels for 7%

profile of v17, /device:TPU:0, one launch (start us, length us, event | category | flops | bytes accessed | tf_op | source)
XLA Modules:
  0.0 75.1 jit_solution(15105278368949785962)
XLA Ops:
  1.8 5.1 %collective-permute-start.2 = (bf16[1,4,8192]{2,1,0:T(4,128)(2,1)S(1)}, bf16[1,4,8192]{2,1,0:T(4,128)(2,1)S(1)}, u32[]{:S(2)}, u32[]{:S(2)}) collective-permute-start(bf16[1,4,8192]{2,1,0:T(4,128)(2,1)S(1)} %bitcast.24), channel_id=1, source_target_pairs={{0,12},{1,13},{2,14},{3,15},{4,0},{5,1},{6,2},{7,3},{8,4},{9,5},{1... | collective-permute-start | bytes 196616 | tf_op jit(solution)/shard_map/ppermute | solution.py:437
  6.9 1.0 %collective-permute-start = (bf16[1,4,8192]{2,1,0:T(4,128)(2,1)S(1)}, bf16[1,4,8192]{2,1,0:T(4,128)(2,1)S(1)}, u32[]{:S(2)}, u32[]{:S(2)}) collective-permute-start(bf16[1,4,8192]{2,1,0:T(4,128)(2,1)S(1)} %bitcast.26), channel_id=1, source_target_pairs={{0,4},{1,5},{2,6},{3,7},{4,8},{5,9},{6,10},{7,11},{8,12},{9,13},{1... | collective-permute-start | bytes 196616 | tf_op jit(solution)/shard_map/ppermute | solution.py:437
  8.0 1.8 %shard_map.185 = (s32[64,1]{1,0:T(8,128)S(1)}, s32[64,1]{1,0:T(8,128)S(1)}, f32[64,128]{1,0:T(8,128)S(1)}, f32[64,128]{1,0:T(8,128)S(1)}, f32[64,128]{1,0:T(8,12...) custom-call(s32[1]{0:T(128)} %bitcast.index_ref, ...), custom_call_target="tpu_custom_call" | custom-call | flops 4600000000 | tf_op jit(solution)/shard_map/pallas_call | solution.py:36
  9.8 1.6 %collective-permute-start.3 = (bf16[1,4,8192]{2,1,0:T(4,128)(2,1)S(1)}, bf16[1,4,8192]{2,1,0:T(4,128)(2,1)S(1)}, u32[]{:S(2)}, u32[]{:S(2)}) collective-permute-start(bf16[1,4,8192]{2,1,0:T(4,128)(2,1)S(1)} %bitcast.27), channel_id=1, source_target_pairs={{0,2},{1,3},{2,0},{3,1},{4,6},{5,7},{6,4},{7,5},{8,10},{9,11},{10,... | collective-permute-start | bytes 196616 | tf_op jit(solution)/shard_map/ppermute | solution.py:437
  11.5 1.9 %collective-permute-done.1 = bf16[1,4,8192]{2,1,0:T(4,128)(2,1)S(1)} collective-permute-done((bf16[1,4,8192]{2,1,0:T(4,128)(2,1)S(1)}, bf16[1,4,8192]{2,1,0:T(4,128)(2,1)S(1)}, u32[]{:S(2)}, u32[]{:S(2)}) %collective-permute-start.1) | collective-permute-done | bytes 65568 | tf_op jit(solution)/shard_map/ppermute | solution.py:437
  13.6 1.6 %collective-permute-start.4 = (bf16[3,4,8192]{2,1,0:T(4,128)(2,1)S(1)}, bf16[3,4,8192]{2,1,0:T(4,128)(2,1)S(1)}, u32[]{:S(2)}, u32[]{:S(2)}) collective-permute-start(bf16[3,4,8192]{2,1,0:T(4,128)(2,1)S(1)} %pad_maximum_fusion), channel_id=1, source_target_pairs={{0,2},{1,3},{2,0},{3,1},{4,6},{5,7},{6,4},{7,5},{8,10},{9,11},{10,... | collective-permute-start | bytes 589832 | tf_op jit(solution)/shard_map/ppermute | solution.py:437
  15.4 4.9 %collective-permute-done.4.refs_1_ = bf16[3,4,8192]{2,1,0:T(4,128)(2,1)S(1)} collective-permute-done((bf16[3,4,8192]{2,1,0:T(4,128)(2,1)S(1)}, bf16[3,4,8192]{2,1,0:T(4,128)(2,1)S(1)}, u32[]{:S(2)}, u32[]{:S(2)}) %collective-permute-start.4) | collective-permute-done | bytes 196640 | tf_op jit(solution)/shard_map/ppermute | solution.py:437
  20.3 1.4 %collective-permute-done.6.refs_3_ = bf16[3,4,8192]{2,1,0:T(4,128)(2,1)S(1)} collective-permute-done((bf16[3,4,8192]{2,1,0:T(4,128)(2,1)S(1)}, bf16[3,4,8192]{2,1,0:T(4,128)(2,1)S(1)}, u32[]{:S(2)}, u32[]{:S(2)}) %collective-permute-start.6) | collective-permute-done | bytes 196640 | tf_op jit(solution)/shard_map/ppermute | solution.py:437
  21.7 0.7 shard_map.186
  22.4 1.3 %collective-permute-start.9 = (bf16[16,128]{1,0:T(8,128)(2,1)S(1)}, bf16[16,128]{1,0:T(8,128)(2,1)S(1)}, u32[]{:S(2)}, u32[]{:S(2)}) collective-permute-start(bf16[16,128]{1,0:T(8,128)(2,1)S(1)} %get-tuple-element.55.refs_0_), channel_id=1, source_target_pairs={{0,3},{1,2},{2,1},{3,0},{4,7},{5,6},{6,5},{7,4},{8,11},{9,10},{10,... | collective-permute-start | bytes 12296 | tf_op jit(solution)/shard_map/ppermute | solution.py:437
  24.3 1.2 %shard_map.188 = (f32[64,512]{1,0:T(8,128)S(1)}, f32[64,128]{1,0:T(8,128)S(1)}) custom-call(bf16[64,8192]{1,0:T(8,128)(2,1)S(1)} %get-tuple-element.56.x_ref, bf16[8192,512]{1,0:T(8,128)(2,1)S(1)} %bitcast.15, bf16[64,8192]{1,0:T(8,128)(2,1)S(1)} %bitcast.18, bf16[64,8192]{1,0:T(8,128)(2,1)S(1)} %bitcast.20), custom_call_target="tpu_custom_call" | custom-call | flops 345000000 | tf_op jit(solution)/shard_map/pallas_call | solution.py:36
  25.6 1.7 %collective-permute-done.8.refs_2_ = bf16[16,128]{1,0:T(8,128)(2,1)S(1)} collective-permute-done((bf16[16,128]{1,0:T(8,128)(2,1)S(1)}, bf16[16,128]{1,0:T(8,128)(2,1)S(1)}, u32[]{:S(2)}, u32[]{:S(2)}) %collective-permute-start.8) | collective-permute-done | bytes 4128 | tf_op jit(solution)/shard_map/ppermute | solution.py:437
  27.4 1.0 %collective-permute-start.12 = (bf16[16,128]{1,0:T(8,128)(2,1)S(1)}, bf16[16,128]{1,0:T(8,128)(2,1)S(1)}, u32[]{:S(2)}, u32[]{:S(2)}) collective-permute-start(bf16[16,128]{1,0:T(8,128)(2,1)S(1)} %shard_map.187.refs_0_), channel_id=1, source_target_pairs={{0,12},{1,13},{2,14},{3,15},{4,0},{5,1},{6,2},{7,3},{8,4},{9,5},{1... | collective-permute-start | bytes 12296 | tf_op jit(solution)/shard_map/ppermute | solution.py:437
  28.4 0.7 collective-permute-start.11
  29.1 1.8 %collective-permute-start.10 = (bf16[16,128]{1,0:T(8,128)(2,1)S(1)}, bf16[16,128]{1,0:T(8,128)(2,1)S(1)}, u32[]{:S(2)}, u32[]{:S(2)}) collective-permute-start(bf16[16,128]{1,0:T(8,128)(2,1)S(1)} %shard_map.187.refs_0_), channel_id=1, source_target_pairs={{0,4},{1,5},{2,6},{3,7},{4,8},{5,9},{6,10},{7,11},{8,12},{9,13},{1... | collective-permute-start | bytes 12296 | tf_op jit(solution)/shard_map/ppermute | solution.py:437
  30.9 1.2 %shard_map.189 = (f32[64,512]{1,0:T(8,128)S(1)}, f32[64,128]{1,0:T(8,128)S(1)}) custom-call(bf16[64,8192]{1,0:T(8,128)(2,1)S(1)} %get-tuple-element.56.x_ref, bf16[8192,512]{1,0:T(8,128)(2,1)S(1)} %bitcast.15, bf16[64,8192]{1,0:T(8,128)(2,1)S(1)} %bitcast.19, bf16[64,8192]{1,0:T(8,128)(2,1)S(1)} %bitcast.21), custom_call_target="tpu_custom_call" | custom-call | flops 345000000 | tf_op jit(solution)/shard_map/pallas_call | solution.py:36
  32.1 0.8 %collective-permute-done.11.refs_2_ = bf16[16,128]{1,0:T(8,128)(2,1)S(1)} collective-permute-done((bf16[16,128]{1,0:T(8,128)(2,1)S(1)}, bf16[16,128]{1,0:T(8,128)(2,1)S(1)}, u32[]{:S(2)}, u32[]{:S(2)}) %collective-permute-start.11) | collective-permute-done | bytes 4128 | tf_op jit(solution)/shard_map/ppermute | solution.py:437
  32.9 1.6 %collective-permute-done.10.refs_1_ = bf16[16,128]{1,0:T(8,128)(2,1)S(1)} collective-permute-done((bf16[16,128]{1,0:T(8,128)(2,1)S(1)}, bf16[16,128]{1,0:T(8,128)(2,1)S(1)}, u32[]{:S(2)}, u32[]{:S(2)}) %collective-permute-start.10) | collective-permute-done | bytes 4128 | tf_op jit(solution)/shard_map/ppermute | solution.py:437
  34.5 0.8 %shard_map.190 = bf16[16,24,128]{2,1,0:T(8,128)(2,1)S(1)} custom-call(bf16[16,128]{1,0:T(8,128)(2,1)S(1)} %shard_map.187.refs_0_, bf16[16,128]{1,0:T(8,128)(2,1)S(1)} %collective-permute-done.10.refs_1_, bf16[16,128]{1,0:T(8,128)(2,1)S(1)} %collective-permute-done.11.refs_2_, bf16[16,128]{1,0:T(8,128)(2,1)S(1)} %collective-permute-done.12.refs_3_, ...), custom_call_target="tpu_custom_call" | custom-call | flops 1035000000 | tf_op jit(solution)/shard_map/pallas_call | solution.py:36
  35.4 10.0 %all_to_all.10.x_ref = bf16[16,24,128]{2,1,0:T(8,128)(2,1)S(1)} all-to-all(bf16[16,24,128]{2,1,0:T(8,128)(2,1)S(1)} %shard_map.190), channel_id=1, replica_groups=mesh['replica'=2,'serve'=16] {'serve'}, dimensions={0} | all-to-all | bytes 196608 | tf_op jit(solution)/shard_map/all_to_all | solution.py:543
  45.4 2.0 %shard_map.191 = (bf16[2,2,1024]{2,1,0:T(2,128)(2,1)}, bf16[2,2,1024]{2,1,0:T(2,128)(2,1)}, bf16[16,16,128]{2,1,0:T(8,128)(2,1)S(1)}) custom-call(s32[1]{0:T(128)} %bitcast.index_ref, s32[32]{0:T(128)S(1)} %copy-done.13, bf16[16,24,128]{2,1,0:T(8,128)(2,1)S(1)} %all_to_all.10.x_ref, bf16[256,384]{1,0:T(8,128)(2,1)S(1)} %get-tuple-element.70.order_ref, ...), custom_call_target="tpu_custom_call" | custom-call | flops 1150000000 | tf_op jit(solution)/shard_map/pallas_call | solution.py:36
  47.3 9.5 %all_to_all.11.ctx_ref = bf16[16,16,128]{2,1,0:T(8,128)(2,1)S(1)} all-to-all(bf16[16,16,128]{2,1,0:T(8,128)(2,1)S(1)} %get-tuple-element.71), channel_id=1, replica_groups=mesh['replica'=2,'serve'=16] {'serve'}, dimensions={0} | all-to-all | bytes 131072 | tf_op jit(solution)/shard_map/all_to_all | solution.py:554
  56.8 1.2 %shard_map.192 = (bf16[64,512]{1,0:T(8,128)(2,1)S(1)}, f32[32,5120]{1,0:T(8,128)S(1)}, f32[32,5120]{1,0:T(8,128)S(1)}) custom-call(bf16[16,16,128]{2,1,0:T(8,128)(2,1)S(1)} %all_to_all.11.ctx_ref, bf16[256,256]{1,0:T(8,128)(2,1)S(1)} %get-tuple-element.72.take_ref, bf16[512,8192]{1,0:T(8,128)(2,1)S(1)} %bitcast.17), custom_call_target="tpu_custom_call" | custom-call | flops 460000000 | tf_op jit(solution)/shard_map/pallas_call | solution.py:36
  59.3 0.9 %collective-permute-done.13.came_ref = f32[32,5120]{1,0:T(8,128)S(1)} collective-permute-done((f32[32,5120]{1,0:T(8,128)S(1)}, f32[32,5120]{1,0:T(8,128)S(1)}, u32[]{:S(2)}, u32[]{:S(2)}) %collective-permute-start.13) | collective-permute-done | bytes 655392 | tf_op jit(solution)/shard_map/ppermute | solution.py:437
  61.2 1.0 %collective-permute-start.20 = (bf16[8,3072]{1,0:T(8,128)(2,1)S(1)}, bf16[8,3072]{1,0:T(8,128)(2,1)S(1)}, u32[]{:S(2)}, u32[]{:S(2)}) collective-permute-start(bf16[8,3072]{1,0:T(8,128)(2,1)S(1)} %get-tuple-element.86), channel_id=1, source_target_pairs={{0,8},{1,9},{2,10},{3,11},{4,12},{5,13},{6,14},{7,15},{8,0},{9,1},... | collective-permute-start | bytes 147464 | tf_op jit(solution)/shard_map/ppermute | solution.py:437
  62.1 2.5 %collective-permute-start.21 = (bf16[8,3072]{1,0:T(8,128)(2,1)S(1)}, bf16[8,3072]{1,0:T(8,128)(2,1)S(1)}, u32[]{:S(2)}, u32[]{:S(2)}) collective-permute-start(bf16[8,3072]{1,0:T(8,128)(2,1)S(1)} %get-tuple-element.87), channel_id=1, source_target_pairs={{0,12},{1,13},{2,14},{3,15},{4,0},{5,1},{6,2},{7,3},{8,4},{9,5},{1... | collective-permute-start | bytes 147464 | tf_op jit(solution)/shard_map/ppermute | solution.py:437
  64.7 1.9 %collective-permute-done.14.refs_1_ = bf16[16,5120]{1,0:T(8,128)(2,1)S(1)} collective-permute-done((bf16[16,5120]{1,0:T(8,128)(2,1)S(1)}, bf16[16,5120]{1,0:T(8,128)(2,1)S(1)}, u32[]{:S(2)}, u32[]{:S(2)}) %collective-permute-start.14) | collective-permute-done | bytes 163872 | tf_op jit(solution)/shard_map/ppermute | solution.py:437
  66.8 0.9 %collective-permute-start.16 = (bf16[4,5120]{1,0:T(4,128)(2,1)S(1)}, bf16[4,5120]{1,0:T(4,128)(2,1)S(1)}, u32[]{:S(2)}, u32[]{:S(2)}) collective-permute-start(bf16[4,5120]{1,0:T(4,128)(2,1)S(1)} %get-tuple-element.79), channel_id=1, source_target_pairs={{0,8},{1,9},{2,10},{3,11},{4,12},{5,13},{6,14},{7,15},{8,0},{9,1},... | collective-permute-start | bytes 122888 | tf_op jit(solution)/shard_map/ppermute | solution.py:437
  67.7 2.8 %collective-permute-start.17 = (bf16[4,5120]{1,0:T(4,128)(2,1)S(1)}, bf16[4,5120]{1,0:T(4,128)(2,1)S(1)}, u32[]{:S(2)}, u32[]{:S(2)}) collective-permute-start(bf16[4,5120]{1,0:T(4,128)(2,1)S(1)} %get-tuple-element.80), channel_id=1, source_target_pairs={{0,12},{1,13},{2,14},{3,15},{4,0},{5,1},{6,2},{7,3},{8,4},{9,5},{1... | collective-permute-start | bytes 122888 | tf_op jit(solution)/shard_map/ppermute | solution.py:437
  70.5 0.9 %collective-permute-start.22 = (bf16[4,3072]{1,0:T(4,128)(2,1)S(1)}, bf16[4,3072]{1,0:T(4,128)(2,1)S(1)}, u32[]{:S(2)}, u32[]{:S(2)}) collective-permute-start(bf16[4,3072]{1,0:T(4,128)(2,1)S(1)} %get-tuple-element.89), channel_id=1, source_target_pairs={{0,2},{1,3},{2,0},{3,1},{4,6},{5,7},{6,4},{7,5},{8,10},{9,11},{10,... | collective-permute-start | bytes 73736 | tf_op jit(solution)/shard_map/ppermute | solution.py:437
  71.4 3.0 %collective-permute-done.22.refs_5_ = bf16[4,3072]{1,0:T(4,128)(2,1)S(1)} collective-permute-done((bf16[4,3072]{1,0:T(4,128)(2,1)S(1)}, bf16[4,3072]{1,0:T(4,128)(2,1)S(1)}, u32[]{:S(2)}, u32[]{:S(2)}) %collective-permute-start.22) | collective-permute-done | bytes 24608 | tf_op jit(solution)/shard_map/ppermute | solution.py:437
  74.4 0.7 shard_map.198
  (76 shorter events, 4.8 us)
Async XLA Ops:
  1.8 9.6 %collective-permute-start.2 = (bf16[1,4,8192]{2,1,0:T(4,128)(2,1)S(1)}, bf16[1,4,8192]{2,1,0:T(4,128)(2,1)S(1)}, u32[]{:S(2)}, u32[]{:S(2)}) collective-permute-start(bf16[1,4,8192]{2,1,0:T(4,128)(2,1)S(1)} %bitcast.24), channel_id=1, source_target_pairs={{0,12},{1,13},{2,14},{3,15},{4,0},{5,1},{6,2},{7,3},{8,4},{9,5},{1... | collective-permute-start | bytes 196616 | tf_op jit(solution)/shard_map/ppermute | solution.py:437
  6.9 6.5 %collective-permute-start.1 = (bf16[1,4,8192]{2,1,0:T(4,128)(2,1)S(1)}, bf16[1,4,8192]{2,1,0:T(4,128)(2,1)S(1)}, u32[]{:S(2)}, u32[]{:S(2)}) collective-permute-start(bf16[1,4,8192]{2,1,0:T(4,128)(2,1)S(1)} %bitcast.25), channel_id=1, source_target_pairs={{0,8},{1,9},{2,10},{3,11},{4,12},{5,13},{6,14},{7,15},{8,0},{9,1},... | collective-permute-start | bytes 196616 | tf_op jit(solution)/shard_map/ppermute | solution.py:437
  6.9 6.5 %collective-permute-start = (bf16[1,4,8192]{2,1,0:T(4,128)(2,1)S(1)}, bf16[1,4,8192]{2,1,0:T(4,128)(2,1)S(1)}, u32[]{:S(2)}, u32[]{:S(2)}) collective-permute-start(bf16[1,4,8192]{2,1,0:T(4,128)(2,1)S(1)} %bitcast.26), channel_id=1, source_target_pairs={{0,4},{1,5},{2,6},{3,7},{4,8},{5,9},{6,10},{7,11},{8,12},{9,13},{1... | collective-permute-start | bytes 196616 | tf_op jit(solution)/shard_map/ppermute | solution.py:437
  7.9 16.4 %slice-start = ((s8[8388608]{0:T(1024)(128)(4,1)}), s8[4194304]{0:T(1024)(128)(4,1)S(1)}, s32[]{:S(2)}) async-start(s8[8388608]{0:T(1024)(128)(4,1)} %bitcast.14), calls=%async_computation.2 | async-start | bytes 8388608
  8.0 13.8 %copy-start.2 = (bf16[2,8192,16]{1,2,0:T(8,128)(2,1)S(1)}, bf16[2,8192,16]{1,2,0:T(8,128)(2,1)}, u32[]{:S(2)}) copy-start(bf16[2,8192,16]{1,2,0:T(8,128)(2,1)} %param.23) | copy-start | bytes 1572868
  8.0 16.3 %slice-start.1 = ((s8[8388608]{0:T(1024)(128)(4,1)}), s8[4194304]{0:T(1024)(128)(4,1)S(1)}, s32[]{:S(2)}) async-start(s8[8388608]{0:T(1024)(128)(4,1)} %bitcast.14), calls=%async_computation.3 | async-start | bytes 8388608
  8.0 16.3 %copy-start = (bf16[8192,64]{0,1:T(8,128)(2,1)S(1)}, bf16[8192,64]{0,1:T(8,128)(2,1)}, u32[]{:S(2)}) copy-start(bf16[8192,64]{0,1:T(8,128)(2,1)} %param.20) | copy-start | bytes 3145732
  8.0 16.3 %copy-start.1 = (bf16[8192,64]{0,1:T(8,128)(2,1)S(1)}, bf16[8192,64]{0,1:T(8,128)(2,1)}, u32[]{:S(2)}) copy-start(bf16[8192,64]{0,1:T(8,128)(2,1)} %param.21) | copy-start | bytes 3145732
  9.8 5.4 %collective-permute-start.3 = (bf16[1,4,8192]{2,1,0:T(4,128)(2,1)S(1)}, bf16[1,4,8192]{2,1,0:T(4,128)(2,1)S(1)}, u32[]{:S(2)}, u32[]{:S(2)}) collective-permute-start(bf16[1,4,8192]{2,1,0:T(4,128)(2,1)S(1)} %bitcast.27), channel_id=1, source_target_pairs={{0,2},{1,3},{2,0},{3,1},{4,6},{5,7},{6,4},{7,5},{8,10},{9,11},{10,... | collective-permute-start | bytes 196616 | tf_op jit(solution)/shard_map/ppermute | solution.py:437
  13.6 6.7 %collective-permute-start.4 = (bf16[3,4,8192]{2,1,0:T(4,128)(2,1)S(1)}, bf16[3,4,8192]{2,1,0:T(4,128)(2,1)S(1)}, u32[]{:S(2)}, u32[]{:S(2)}) collective-permute-start(bf16[3,4,8192]{2,1,0:T(4,128)(2,1)S(1)} %pad_maximum_fusion), channel_id=1, source_target_pairs={{0,2},{1,3},{2,0},{3,1},{4,6},{5,7},{6,4},{7,5},{8,10},{9,11},{10,... | collective-permute-start | bytes 589832 | tf_op jit(solution)/shard_map/ppermute | solution.py:437
  15.3 5.0 %collective-permute-start.5 = (bf16[5,4,8192]{2,1,0:T(4,128)(2,1)S(1)}, bf16[5,4,8192]{2,1,0:T(4,128)(2,1)S(1)}, u32[]{:S(2)}, u32[]{:S(2)}) collective-permute-start(bf16[5,4,8192]{2,1,0:T(4,128)(2,1)S(1)} %constant_dynamic-update-slice_fusion.refs_0_), channel_id=1, source_target_pairs={{0,1},{1,0},{2,3},{3,2},{4,5},{5,4},{6,7},{7,6},{8,9},{9,8},{10,11... | collective-permute-start | bytes 983048 | tf_op jit(solution)/shard_map/ppermute | solution.py:437
  20.3 1.4 %collective-permute-start.6 = (bf16[3,4,8192]{2,1,0:T(4,128)(2,1)S(1)}, bf16[3,4,8192]{2,1,0:T(4,128)(2,1)S(1)}, u32[]{:S(2)}, u32[]{:S(2)}) collective-permute-start(bf16[3,4,8192]{2,1,0:T(4,128)(2,1)S(1)} %collective-permute-done.4.refs_1_), channel_id=1, source_target_pairs={{0,1},{1,0},{2,3},{3,2},{4,5},{5,4},{6,7},{7,6},{8,9},{9,8},{10,11... | collective-permute-start | bytes 589832 | tf_op jit(solution)/shard_map/ppermute | solution.py:437
  22.4 3.2 %collective-permute-start.9 = (bf16[16,128]{1,0:T(8,128)(2,1)S(1)}, bf16[16,128]{1,0:T(8,128)(2,1)S(1)}, u32[]{:S(2)}, u32[]{:S(2)}) collective-permute-start(bf16[16,128]{1,0:T(8,128)(2,1)S(1)} %get-tuple-element.55.refs_0_), channel_id=1, source_target_pairs={{0,3},{1,2},{2,1},{3,0},{4,7},{5,6},{6,5},{7,4},{8,11},{9,10},{10,... | collective-permute-start | bytes 12296 | tf_op jit(solution)/shard_map/ppermute | solution.py:437
  23.7 3.6 %collective-permute-start.8 = (bf16[16,128]{1,0:T(8,128)(2,1)S(1)}, bf16[16,128]{1,0:T(8,128)(2,1)S(1)}, u32[]{:S(2)}, u32[]{:S(2)}) collective-permute-start(bf16[16,128]{1,0:T(8,128)(2,1)S(1)} %get-tuple-element.55.refs_0_), channel_id=1, source_target_pairs={{0,2},{1,3},{2,0},{3,1},{4,6},{5,7},{6,4},{7,5},{8,10},{9,11},{10,... | collective-permute-start | bytes 12296 | tf_op jit(solution)/shard_map/ppermute | solution.py:437
  24.2 3.1 %collective-permute-start.7 = (bf16[16,128]{1,0:T(8,128)(2,1)S(1)}, bf16[16,128]{1,0:T(8,128)(2,1)S(1)}, u32[]{:S(2)}, u32[]{:S(2)}) collective-permute-start(bf16[16,128]{1,0:T(8,128)(2,1)S(1)} %get-tuple-element.55.refs_0_), channel_id=1, source_target_pairs={{0,1},{1,0},{2,3},{3,2},{4,5},{5,4},{6,7},{7,6},{8,9},{9,8},{10,11... | collective-permute-start | bytes 12296 | tf_op jit(solution)/shard_map/ppermute | solution.py:437
  25.6 19.8 %copy-start.4 = (bf16[2,384,1024]{2,1,0:T(8,128)(2,1)S(1)}, bf16[2,384,1024]{2,1,0:T(8,128)(2,1)}, u32[]{:S(2)}) copy-start(bf16[2,384,1024]{2,1,0:T(8,128)(2,1)} %k_ref.1) | copy-start | bytes 4718596
  25.6 19.8 %copy-start.5 = (bf16[2,384,1024]{2,1,0:T(8,128)(2,1)S(1)}, bf16[2,384,1024]{2,1,0:T(8,128)(2,1)}, u32[]{:S(2)}) copy-start(bf16[2,384,1024]{2,1,0:T(8,128)(2,1)} %v_ref.1) | copy-start | bytes 4718596
  27.3 29.5 %slice-start.2 = ((s8[8388608]{0:T(1024)(128)(4,1)}), s8[4194304]{0:T(1024)(128)(4,1)S(1)}, s32[]{:S(2)}) async-start(s8[8388608]{0:T(1024)(128)(4,1)} %bitcast.16), calls=%async_computation.4 | async-start | bytes 8388608
  27.4 29.5 %slice-start.3 = ((s8[8388608]{0:T(1024)(128)(4,1)}), s8[4194304]{0:T(1024)(128)(4,1)S(1)}, s32[]{:S(2)}) async-start(s8[8388608]{0:T(1024)(128)(4,1)} %bitcast.16), calls=%async_computation.5 | async-start | bytes 8388608
  27.4 4.7 %collective-permute-start.12 = (bf16[16,128]{1,0:T(8,128)(2,1)S(1)}, bf16[16,128]{1,0:T(8,128)(2,1)S(1)}, u32[]{:S(2)}, u32[]{:S(2)}) collective-permute-start(bf16[16,128]{1,0:T(8,128)(2,1)S(1)} %shard_map.187.refs_0_), channel_id=1, source_target_pairs={{0,12},{1,13},{2,14},{3,15},{4,0},{5,1},{6,2},{7,3},{8,4},{9,5},{1... | collective-permute-start | bytes 12296 | tf_op jit(solution)/shard_map/ppermute | solution.py:437
  28.4 4.5 %collective-permute-start.11 = (bf16[16,128]{1,0:T(8,128)(2,1)S(1)}, bf16[16,128]{1,0:T(8,128)(2,1)S(1)}, u32[]{:S(2)}, u32[]{:S(2)}) collective-permute-start(bf16[16,128]{1,0:T(8,128)(2,1)S(1)} %shard_map.187.refs_0_), channel_id=1, source_target_pairs={{0,8},{1,9},{2,10},{3,11},{4,12},{5,13},{6,14},{7,15},{8,0},{9,1},... | collective-permute-start | bytes 12296 | tf_op jit(solution)/shard_map/ppermute | solution.py:437
  29.1 5.4 %collective-permute-start.10 = (bf16[16,128]{1,0:T(8,128)(2,1)S(1)}, bf16[16,128]{1,0:T(8,128)(2,1)S(1)}, u32[]{:S(2)}, u32[]{:S(2)}) collective-permute-start(bf16[16,128]{1,0:T(8,128)(2,1)S(1)} %shard_map.187.refs_0_), channel_id=1, source_target_pairs={{0,4},{1,5},{2,6},{3,7},{4,8},{5,9},{6,10},{7,11},{8,12},{9,13},{1... | collective-permute-start | bytes 12296 | tf_op jit(solution)/shard_map/ppermute | solution.py:437
  58.0 2.2 %collective-permute-start.13 = (f32[32,5120]{1,0:T(8,128)S(1)}, f32[32,5120]{1,0:T(8,128)S(1)}, u32[]{:S(2)}, u32[]{:S(2)}) collective-permute-start(f32[32,5120]{1,0:T(8,128)S(1)} %get-tuple-element.74), channel_id=1, source_target_pairs={{0,1},{1,0},{2,3},{3,2},{4,5},{5,4},{6,7},{7,6},{8,9},{9,8},{10,11... | collective-permute-start | bytes 1966088 | tf_op jit(solution)/shard_map/ppermute | solution.py:437
  58.7 2.0 %collective-permute-start.18 = (f32[32,3072]{1,0:T(8,128)S(1)}, f32[32,3072]{1,0:T(8,128)S(1)}, u32[]{:S(2)}, u32[]{:S(2)}) collective-permute-start(f32[32,3072]{1,0:T(8,128)S(1)} %get-tuple-element.83), channel_id=1, source_target_pairs={{0,1},{1,0},{2,3},{3,2},{4,5},{5,4},{6,7},{7,6},{8,9},{9,8},{10,11... | collective-permute-start | bytes 1179656 | tf_op jit(solution)/shard_map/ppermute | solution.py:437
  60.2 6.3 %collective-permute-start.14 = (bf16[16,5120]{1,0:T(8,128)(2,1)S(1)}, bf16[16,5120]{1,0:T(8,128)(2,1)S(1)}, u32[]{:S(2)}, u32[]{:S(2)}) collective-permute-start(bf16[16,5120]{1,0:T(8,128)(2,1)S(1)} %get-tuple-element.76), channel_id=1, source_target_pairs={{0,2},{1,3},{2,0},{3,1},{4,6},{5,7},{6,4},{7,5},{8,10},{9,11},{10,... | collective-permute-start | bytes 491528 | tf_op jit(solution)/shard_map/ppermute | solution.py:437
  60.8 6.9 %collective-permute-start.19 = (bf16[8,3072]{1,0:T(8,128)(2,1)S(1)}, bf16[8,3072]{1,0:T(8,128)(2,1)S(1)}, u32[]{:S(2)}, u32[]{:S(2)}) collective-permute-start(bf16[8,3072]{1,0:T(8,128)(2,1)S(1)} %get-tuple-element.85), channel_id=1, source_target_pairs={{0,4},{1,5},{2,6},{3,7},{4,8},{5,9},{6,10},{7,11},{8,12},{9,13},{1... | collective-permute-start | bytes 147464 | tf_op jit(solution)/shard_map/ppermute | solution.py:437
  61.2 9.3 %collective-permute-start.20 = (bf16[8,3072]{1,0:T(8,128)(2,1)S(1)}, bf16[8,3072]{1,0:T(8,128)(2,1)S(1)}, u32[]{:S(2)}, u32[]{:S(2)}) collective-permute-start(bf16[8,3072]{1,0:T(8,128)(2,1)S(1)} %get-tuple-element.86), channel_id=1, source_target_pairs={{0,8},{1,9},{2,10},{3,11},{4,12},{5,13},{6,14},{7,15},{8,0},{9,1},... | collective-permute-start | bytes 147464 | tf_op jit(solution)/shard_map/ppermute | solution.py:437
  62.1 8.3 %collective-permute-start.21 = (bf16[8,3072]{1,0:T(8,128)(2,1)S(1)}, bf16[8,3072]{1,0:T(8,128)(2,1)S(1)}, u32[]{:S(2)}, u32[]{:S(2)}) collective-permute-start(bf16[8,3072]{1,0:T(8,128)(2,1)S(1)} %get-tuple-element.87), channel_id=1, source_target_pairs={{0,12},{1,13},{2,14},{3,15},{4,0},{5,1},{6,2},{7,3},{8,4},{9,5},{1... | collective-permute-start | bytes 147464 | tf_op jit(solution)/shard_map/ppermute | solution.py:437
  66.6 7.8 %collective-permute-start.15 = (bf16[4,5120]{1,0:T(4,128)(2,1)S(1)}, bf16[4,5120]{1,0:T(4,128)(2,1)S(1)}, u32[]{:S(2)}, u32[]{:S(2)}) collective-permute-start(bf16[4,5120]{1,0:T(4,128)(2,1)S(1)} %get-tuple-element.78), channel_id=1, source_target_pairs={{0,4},{1,5},{2,6},{3,7},{4,8},{5,9},{6,10},{7,11},{8,12},{9,13},{1... | collective-permute-start | bytes 122888 | tf_op jit(solution)/shard_map/ppermute | solution.py:437
  66.8 7.6 %collective-permute-start.16 = (bf16[4,5120]{1,0:T(4,128)(2,1)S(1)}, bf16[4,5120]{1,0:T(4,128)(2,1)S(1)}, u32[]{:S(2)}, u32[]{:S(2)}) collective-permute-start(bf16[4,5120]{1,0:T(4,128)(2,1)S(1)} %get-tuple-element.79), channel_id=1, source_target_pairs={{0,8},{1,9},{2,10},{3,11},{4,12},{5,13},{6,14},{7,15},{8,0},{9,1},... | collective-permute-start | bytes 122888 | tf_op jit(solution)/shard_map/ppermute | solution.py:437
  67.7 6.7 %collective-permute-start.17 = (bf16[4,5120]{1,0:T(4,128)(2,1)S(1)}, bf16[4,5120]{1,0:T(4,128)(2,1)S(1)}, u32[]{:S(2)}, u32[]{:S(2)}) collective-permute-start(bf16[4,5120]{1,0:T(4,128)(2,1)S(1)} %get-tuple-element.80), channel_id=1, source_target_pairs={{0,12},{1,13},{2,14},{3,15},{4,0},{5,1},{6,2},{7,3},{8,4},{9,5},{1... | collective-permute-start | bytes 122888 | tf_op jit(solution)/shard_map/ppermute | solution.py:437
  70.5 3.9 %collective-permute-start.22 = (bf16[4,3072]{1,0:T(4,128)(2,1)S(1)}, bf16[4,3072]{1,0:T(4,128)(2,1)S(1)}, u32[]{:S(2)}, u32[]{:S(2)}) collective-permute-start(bf16[4,3072]{1,0:T(4,128)(2,1)S(1)} %get-tuple-element.89), channel_id=1, source_target_pairs={{0,2},{1,3},{2,0},{3,1},{4,6},{5,7},{6,4},{7,5},{8,10},{9,11},{10,... | collective-permute-start | bytes 73736 | tf_op jit(solution)/shard_map/ppermute | solution.py:437
  (9 other events, 55.7 us)

commit v18 on v17

--- a/solution.py
+++ b/solution.py
@@ -343,7 +343,7 @@
 
 def out_body(start, a_ref, w_ref, mine_ref, other_ref):
     half = mine_ref.shape[0]
-    tile = 1024
+    tile = 512
 
     for at in range(0, mine_ref.shape[1], tile):
         product = dot(a_ref[...], w_ref[:, start + at : start + at + tile])
@@ -554,7 +554,7 @@
     context = lax.all_to_all(context, "serve", split_axis=0, concat_axis=0, tiled=True)
 
     half = all_rows // cores
-    cut = width * 5 // 8
+    cut = width * 9 // 16
 
     def kinds(count, columns):
         return (jax.ShapeDtypeStruct((count, columns), F32),) * 2

time: 75.5 us -> 75 us (level)
  transfers between devices with their start and end apart: 23 -> 23, of which waited for: 10 -> 11; matrix products, arithmetic and copies ran while one was open for 0% -> 0% of each run, Pallas kernels for 7% -> 7%
where the time goes in v18:
time: 75 us; the launch traced here: 74.7 us
  starting transfers between devices  24.3 us (32%)
  blocking collectives  19.5 us (26%)
  waiting for transfers between devices  17.9 us (24%)
  Pallas kernels  11 us (15%)
  local copies, waits for them, and re-layouts  0.97 us (1%)
  between operations  0.93 us (1%)
    ppermute x23, starting transfers between devices, shift(): return lax.ppermute(value, 'serve', partner(f, m, c))  24.3 us
    ppermute x23, waiting for transfers between devices, shift(): return lax.ppermute(value, 'serve', partner(f, m, c))  17.9 us
    pallas_call x16, Pallas kernels, whole_call(): pl.pallas_call(body, out_shape=out_shape, in_specs=specs, out_specs=tuple...  11 us
    all_to_all x1, blocking collectives, shards(): lax.all_to_all(ready, 'serve', split_axis=0, concat_axis=0, tiled=True)  9.99 us
    all_to_all x1, blocking collectives, shards(): lax.all_to_all(context, 'serve', split_axis=0, concat_axis=0, tiled=True)  9.48 us
  transfers between devices with their start and end apart: 23, of which 11 were waited for; matrix products, arithmetic and copies ran while one was open for 0% of the time, Pallas kernels for 7%

profile of v18, /device:TPU:0, one launch (start us, length us, event | category | flops | bytes accessed | tf_op | source)
XLA Modules:
  0.0 74.7 jit_solution(6730761022325080009)
XLA Ops:
  1.8 5.1 %collective-permute-start.2 = (bf16[1,4,8192]{2,1,0:T(4,128)(2,1)S(1)}, bf16[1,4,8192]{2,1,0:T(4,128)(2,1)S(1)}, u32[]{:S(2)}, u32[]{:S(2)}) collective-permute-start(bf16[1,4,8192]{2,1,0:T(4,128)(2,1)S(1)} %bitcast.24), channel_id=1, source_target_pairs={{0,12},{1,13},{2,14},{3,15},{4,0},{5,1},{6,2},{7,3},{8,4},{9,5},{1... | collective-permute-start | bytes 196616 | tf_op jit(solution)/shard_map/ppermute | solution.py:437
  6.9 1.0 %collective-permute-start = (bf16[1,4,8192]{2,1,0:T(4,128)(2,1)S(1)}, bf16[1,4,8192]{2,1,0:T(4,128)(2,1)S(1)}, u32[]{:S(2)}, u32[]{:S(2)}) collective-permute-start(bf16[1,4,8192]{2,1,0:T(4,128)(2,1)S(1)} %bitcast.26), channel_id=1, source_target_pairs={{0,4},{1,5},{2,6},{3,7},{4,8},{5,9},{6,10},{7,11},{8,12},{9,13},{1... | collective-permute-start | bytes 196616 | tf_op jit(solution)/shard_map/ppermute | solution.py:437
  8.0 1.8 %shard_map.185 = (s32[64,1]{1,0:T(8,128)S(1)}, s32[64,1]{1,0:T(8,128)S(1)}, f32[64,128]{1,0:T(8,128)S(1)}, f32[64,128]{1,0:T(8,128)S(1)}, f32[64,128]{1,0:T(8,12...) custom-call(s32[1]{0:T(128)} %bitcast.index_ref, ...), custom_call_target="tpu_custom_call" | custom-call | flops 4600000000 | tf_op jit(solution)/shard_map/pallas_call | solution.py:36
  9.8 1.6 %collective-permute-start.3 = (bf16[1,4,8192]{2,1,0:T(4,128)(2,1)S(1)}, bf16[1,4,8192]{2,1,0:T(4,128)(2,1)S(1)}, u32[]{:S(2)}, u32[]{:S(2)}) collective-permute-start(bf16[1,4,8192]{2,1,0:T(4,128)(2,1)S(1)} %bitcast.27), channel_id=1, source_target_pairs={{0,2},{1,3},{2,0},{3,1},{4,6},{5,7},{6,4},{7,5},{8,10},{9,11},{10,... | collective-permute-start | bytes 196616 | tf_op jit(solution)/shard_map/ppermute | solution.py:437
  11.5 1.9 %collective-permute-done.1 = bf16[1,4,8192]{2,1,0:T(4,128)(2,1)S(1)} collective-permute-done((bf16[1,4,8192]{2,1,0:T(4,128)(2,1)S(1)}, bf16[1,4,8192]{2,1,0:T(4,128)(2,1)S(1)}, u32[]{:S(2)}, u32[]{:S(2)}) %collective-permute-start.1) | collective-permute-done | bytes 65568 | tf_op jit(solution)/shard_map/ppermute | solution.py:437
  13.6 1.6 %collective-permute-start.4 = (bf16[3,4,8192]{2,1,0:T(4,128)(2,1)S(1)}, bf16[3,4,8192]{2,1,0:T(4,128)(2,1)S(1)}, u32[]{:S(2)}, u32[]{:S(2)}) collective-permute-start(bf16[3,4,8192]{2,1,0:T(4,128)(2,1)S(1)} %pad_maximum_fusion), channel_id=1, source_target_pairs={{0,2},{1,3},{2,0},{3,1},{4,6},{5,7},{6,4},{7,5},{8,10},{9,11},{10,... | collective-permute-start | bytes 589832 | tf_op jit(solution)/shard_map/ppermute | solution.py:437
  15.4 4.9 %collective-permute-done.4.refs_1_ = bf16[3,4,8192]{2,1,0:T(4,128)(2,1)S(1)} collective-permute-done((bf16[3,4,8192]{2,1,0:T(4,128)(2,1)S(1)}, bf16[3,4,8192]{2,1,0:T(4,128)(2,1)S(1)}, u32[]{:S(2)}, u32[]{:S(2)}) %collective-permute-start.4) | collective-permute-done | bytes 196640 | tf_op jit(solution)/shard_map/ppermute | solution.py:437
  20.3 1.4 %collective-permute-done.6.refs_3_ = bf16[3,4,8192]{2,1,0:T(4,128)(2,1)S(1)} collective-permute-done((bf16[3,4,8192]{2,1,0:T(4,128)(2,1)S(1)}, bf16[3,4,8192]{2,1,0:T(4,128)(2,1)S(1)}, u32[]{:S(2)}, u32[]{:S(2)}) %collective-permute-start.6) | collective-permute-done | bytes 196640 | tf_op jit(solution)/shard_map/ppermute | solution.py:437
  21.7 0.7 shard_map.186
  22.4 1.3 %collective-permute-start.9 = (bf16[16,128]{1,0:T(8,128)(2,1)S(1)}, bf16[16,128]{1,0:T(8,128)(2,1)S(1)}, u32[]{:S(2)}, u32[]{:S(2)}) collective-permute-start(bf16[16,128]{1,0:T(8,128)(2,1)S(1)} %get-tuple-element.55.refs_0_), channel_id=1, source_target_pairs={{0,3},{1,2},{2,1},{3,0},{4,7},{5,6},{6,5},{7,4},{8,11},{9,10},{10,... | collective-permute-start | bytes 12296 | tf_op jit(solution)/shard_map/ppermute | solution.py:437
  24.3 1.2 %shard_map.188 = (f32[64,512]{1,0:T(8,128)S(1)}, f32[64,128]{1,0:T(8,128)S(1)}) custom-call(bf16[64,8192]{1,0:T(8,128)(2,1)S(1)} %get-tuple-element.56.x_ref, bf16[8192,512]{1,0:T(8,128)(2,1)S(1)} %bitcast.15, bf16[64,8192]{1,0:T(8,128)(2,1)S(1)} %bitcast.18, bf16[64,8192]{1,0:T(8,128)(2,1)S(1)} %bitcast.20), custom_call_target="tpu_custom_call" | custom-call | flops 345000000 | tf_op jit(solution)/shard_map/pallas_call | solution.py:36
  25.6 1.7 %collective-permute-done.8.refs_2_ = bf16[16,128]{1,0:T(8,128)(2,1)S(1)} collective-permute-done((bf16[16,128]{1,0:T(8,128)(2,1)S(1)}, bf16[16,128]{1,0:T(8,128)(2,1)S(1)}, u32[]{:S(2)}, u32[]{:S(2)}) %collective-permute-start.8) | collective-permute-done | bytes 4128 | tf_op jit(solution)/shard_map/ppermute | solution.py:437
  27.4 1.0 %collective-permute-start.12 = (bf16[16,128]{1,0:T(8,128)(2,1)S(1)}, bf16[16,128]{1,0:T(8,128)(2,1)S(1)}, u32[]{:S(2)}, u32[]{:S(2)}) collective-permute-start(bf16[16,128]{1,0:T(8,128)(2,1)S(1)} %shard_map.187.refs_0_), channel_id=1, source_target_pairs={{0,12},{1,13},{2,14},{3,15},{4,0},{5,1},{6,2},{7,3},{8,4},{9,5},{1... | collective-permute-start | bytes 12296 | tf_op jit(solution)/shard_map/ppermute | solution.py:437
  28.4 0.7 collective-permute-start.11
  29.1 1.8 %collective-permute-start.10 = (bf16[16,128]{1,0:T(8,128)(2,1)S(1)}, bf16[16,128]{1,0:T(8,128)(2,1)S(1)}, u32[]{:S(2)}, u32[]{:S(2)}) collective-permute-start(bf16[16,128]{1,0:T(8,128)(2,1)S(1)} %shard_map.187.refs_0_), channel_id=1, source_target_pairs={{0,4},{1,5},{2,6},{3,7},{4,8},{5,9},{6,10},{7,11},{8,12},{9,13},{1... | collective-permute-start | bytes 12296 | tf_op jit(solution)/shard_map/ppermute | solution.py:437
  30.9 1.2 %shard_map.189 = (f32[64,512]{1,0:T(8,128)S(1)}, f32[64,128]{1,0:T(8,128)S(1)}) custom-call(bf16[64,8192]{1,0:T(8,128)(2,1)S(1)} %get-tuple-element.56.x_ref, bf16[8192,512]{1,0:T(8,128)(2,1)S(1)} %bitcast.15, bf16[64,8192]{1,0:T(8,128)(2,1)S(1)} %bitcast.19, bf16[64,8192]{1,0:T(8,128)(2,1)S(1)} %bitcast.21), custom_call_target="tpu_custom_call" | custom-call | flops 345000000 | tf_op jit(solution)/shard_map/pallas_call | solution.py:36
  32.1 0.8 %collective-permute-done.11.refs_2_ = bf16[16,128]{1,0:T(8,128)(2,1)S(1)} collective-permute-done((bf16[16,128]{1,0:T(8,128)(2,1)S(1)}, bf16[16,128]{1,0:T(8,128)(2,1)S(1)}, u32[]{:S(2)}, u32[]{:S(2)}) %collective-permute-start.11) | collective-permute-done | bytes 4128 | tf_op jit(solution)/shard_map/ppermute | solution.py:437
  32.9 1.6 %collective-permute-done.10.refs_1_ = bf16[16,128]{1,0:T(8,128)(2,1)S(1)} collective-permute-done((bf16[16,128]{1,0:T(8,128)(2,1)S(1)}, bf16[16,128]{1,0:T(8,128)(2,1)S(1)}, u32[]{:S(2)}, u32[]{:S(2)}) %collective-permute-start.10) | collective-permute-done | bytes 4128 | tf_op jit(solution)/shard_map/ppermute | solution.py:437
  34.5 0.8 %shard_map.190 = bf16[16,24,128]{2,1,0:T(8,128)(2,1)S(1)} custom-call(bf16[16,128]{1,0:T(8,128)(2,1)S(1)} %shard_map.187.refs_0_, bf16[16,128]{1,0:T(8,128)(2,1)S(1)} %collective-permute-done.10.refs_1_, bf16[16,128]{1,0:T(8,128)(2,1)S(1)} %collective-permute-done.11.refs_2_, bf16[16,128]{1,0:T(8,128)(2,1)S(1)} %collective-permute-done.12.refs_3_, ...), custom_call_target="tpu_custom_call" | custom-call | flops 1035000000 | tf_op jit(solution)/shard_map/pallas_call | solution.py:36
  35.4 10.0 %all_to_all.10.x_ref = bf16[16,24,128]{2,1,0:T(8,128)(2,1)S(1)} all-to-all(bf16[16,24,128]{2,1,0:T(8,128)(2,1)S(1)} %shard_map.190), channel_id=1, replica_groups=mesh['replica'=2,'serve'=16] {'serve'}, dimensions={0} | all-to-all | bytes 196608 | tf_op jit(solution)/shard_map/all_to_all | solution.py:543
  45.4 2.0 %shard_map.191 = (bf16[2,2,1024]{2,1,0:T(2,128)(2,1)}, bf16[2,2,1024]{2,1,0:T(2,128)(2,1)}, bf16[16,16,128]{2,1,0:T(8,128)(2,1)S(1)}) custom-call(s32[1]{0:T(128)} %bitcast.index_ref, s32[32]{0:T(128)S(1)} %copy-done.13, bf16[16,24,128]{2,1,0:T(8,128)(2,1)S(1)} %all_to_all.10.x_ref, bf16[256,384]{1,0:T(8,128)(2,1)S(1)} %get-tuple-element.70.order_ref, ...), custom_call_target="tpu_custom_call" | custom-call | flops 1150000000 | tf_op jit(solution)/shard_map/pallas_call | solution.py:36
  47.3 9.5 %all_to_all.11.ctx_ref = bf16[16,16,128]{2,1,0:T(8,128)(2,1)S(1)} all-to-all(bf16[16,16,128]{2,1,0:T(8,128)(2,1)S(1)} %get-tuple-element.71), channel_id=1, replica_groups=mesh['replica'=2,'serve'=16] {'serve'}, dimensions={0} | all-to-all | bytes 131072 | tf_op jit(solution)/shard_map/all_to_all | solution.py:554
  56.8 1.1 %shard_map.192 = (bf16[64,512]{1,0:T(8,128)(2,1)S(1)}, f32[32,4608]{1,0:T(8,128)S(1)}, f32[32,4608]{1,0:T(8,128)S(1)}) custom-call(bf16[16,16,128]{2,1,0:T(8,128)(2,1)S(1)} %all_to_all.11.ctx_ref, bf16[256,256]{1,0:T(8,128)(2,1)S(1)} %get-tuple-element.72.take_ref, bf16[512,8192]{1,0:T(8,128)(2,1)S(1)} %bitcast.17), custom_call_target="tpu_custom_call" | custom-call | flops 460000000 | tf_op jit(solution)/shard_map/pallas_call | solution.py:36
  58.0 0.7 %shard_map.195 = (f32[32,3584]{1,0:T(8,128)S(1)}, f32[32,3584]{1,0:T(8,128)S(1)}) custom-call(bf16[64,512]{1,0:T(8,128)(2,1)S(1)} %get-tuple-element.81.a_ref, bf16[512,8192]{1,0:T(8,128)(2,1)S(1)} %bitcast.17), custom_call_target="tpu_custom_call" | custom-call | flops 345000000 | tf_op jit(solution)/shard_map/pallas_call | solution.py:36
  61.0 0.9 %collective-permute-start.20 = (bf16[8,3584]{1,0:T(8,128)(2,1)S(1)}, bf16[8,3584]{1,0:T(8,128)(2,1)S(1)}, u32[]{:S(2)}, u32[]{:S(2)}) collective-permute-start(bf16[8,3584]{1,0:T(8,128)(2,1)S(1)} %get-tuple-element.86), channel_id=1, source_target_pairs={{0,8},{1,9},{2,10},{3,11},{4,12},{5,13},{6,14},{7,15},{8,0},{9,1},... | collective-permute-start | bytes 172040 | tf_op jit(solution)/shard_map/ppermute | solution.py:437
  61.9 2.8 %collective-permute-start.21 = (bf16[8,3584]{1,0:T(8,128)(2,1)S(1)}, bf16[8,3584]{1,0:T(8,128)(2,1)S(1)}, u32[]{:S(2)}, u32[]{:S(2)}) collective-permute-start(bf16[8,3584]{1,0:T(8,128)(2,1)S(1)} %get-tuple-element.87), channel_id=1, source_target_pairs={{0,12},{1,13},{2,14},{3,15},{4,0},{5,1},{6,2},{7,3},{8,4},{9,5},{1... | collective-permute-start | bytes 172040 | tf_op jit(solution)/shard_map/ppermute | solution.py:437
  64.7 1.3 %collective-permute-done.14.refs_1_ = bf16[16,4608]{1,0:T(8,128)(2,1)S(1)} collective-permute-done((bf16[16,4608]{1,0:T(8,128)(2,1)S(1)}, bf16[16,4608]{1,0:T(8,128)(2,1)S(1)}, u32[]{:S(2)}, u32[]{:S(2)}) %collective-permute-start.14) | collective-permute-done | bytes 147488 | tf_op jit(solution)/shard_map/ppermute | solution.py:437
  66.2 0.9 %collective-permute-start.16 = (bf16[4,4608]{1,0:T(4,128)(2,1)S(1)}, bf16[4,4608]{1,0:T(4,128)(2,1)S(1)}, u32[]{:S(2)}, u32[]{:S(2)}) collective-permute-start(bf16[4,4608]{1,0:T(4,128)(2,1)S(1)} %get-tuple-element.79), channel_id=1, source_target_pairs={{0,8},{1,9},{2,10},{3,11},{4,12},{5,13},{6,14},{7,15},{8,0},{9,1},... | collective-permute-start | bytes 110600 | tf_op jit(solution)/shard_map/ppermute | solution.py:437
  67.5 2.4 %collective-permute-start.17 = (bf16[4,4608]{1,0:T(4,128)(2,1)S(1)}, bf16[4,4608]{1,0:T(4,128)(2,1)S(1)}, u32[]{:S(2)}, u32[]{:S(2)}) collective-permute-start(bf16[4,4608]{1,0:T(4,128)(2,1)S(1)} %get-tuple-element.80), channel_id=1, source_target_pairs={{0,12},{1,13},{2,14},{3,15},{4,0},{5,1},{6,2},{7,3},{8,4},{9,5},{1... | collective-permute-start | bytes 110600 | tf_op jit(solution)/shard_map/ppermute | solution.py:437
  70.0 1.3 %collective-permute-start.22 = (bf16[4,3584]{1,0:T(4,128)(2,1)S(1)}, bf16[4,3584]{1,0:T(4,128)(2,1)S(1)}, u32[]{:S(2)}, u32[]{:S(2)}) collective-permute-start(bf16[4,3584]{1,0:T(4,128)(2,1)S(1)} %get-tuple-element.89), channel_id=1, source_target_pairs={{0,2},{1,3},{2,0},{3,1},{4,6},{5,7},{6,4},{7,5},{8,10},{9,11},{10,... | collective-permute-start | bytes 86024 | tf_op jit(solution)/shard_map/ppermute | solution.py:437
  71.3 2.7 %collective-permute-done.22.refs_5_ = bf16[4,3584]{1,0:T(4,128)(2,1)S(1)} collective-permute-done((bf16[4,3584]{1,0:T(4,128)(2,1)S(1)}, bf16[4,3584]{1,0:T(4,128)(2,1)S(1)}, u32[]{:S(2)}, u32[]{:S(2)}) %collective-permute-start.22) | collective-permute-done | bytes 28704 | tf_op jit(solution)/shard_map/ppermute | solution.py:437
  73.9 0.7 shard_map.198
  (76 shorter events, 5.2 us)
Async XLA Ops:
  1.8 9.6 %collective-permute-start.2 = (bf16[1,4,8192]{2,1,0:T(4,128)(2,1)S(1)}, bf16[1,4,8192]{2,1,0:T(4,128)(2,1)S(1)}, u32[]{:S(2)}, u32[]{:S(2)}) collective-permute-start(bf16[1,4,8192]{2,1,0:T(4,128)(2,1)S(1)} %bitcast.24), channel_id=1, source_target_pairs={{0,12},{1,13},{2,14},{3,15},{4,0},{5,1},{6,2},{7,3},{8,4},{9,5},{1... | collective-permute-start | bytes 196616 | tf_op jit(solution)/shard_map/ppermute | solution.py:437
  6.9 6.5 %collective-permute-start.1 = (bf16[1,4,8192]{2,1,0:T(4,128)(2,1)S(1)}, bf16[1,4,8192]{2,1,0:T(4,128)(2,1)S(1)}, u32[]{:S(2)}, u32[]{:S(2)}) collective-permute-start(bf16[1,4,8192]{2,1,0:T(4,128)(2,1)S(1)} %bitcast.25), channel_id=1, source_target_pairs={{0,8},{1,9},{2,10},{3,11},{4,12},{5,13},{6,14},{7,15},{8,0},{9,1},... | collective-permute-start | bytes 196616 | tf_op jit(solution)/shard_map/ppermute | solution.py:437
  6.9 6.5 %collective-permute-start = (bf16[1,4,8192]{2,1,0:T(4,128)(2,1)S(1)}, bf16[1,4,8192]{2,1,0:T(4,128)(2,1)S(1)}, u32[]{:S(2)}, u32[]{:S(2)}) collective-permute-start(bf16[1,4,8192]{2,1,0:T(4,128)(2,1)S(1)} %bitcast.26), channel_id=1, source_target_pairs={{0,4},{1,5},{2,6},{3,7},{4,8},{5,9},{6,10},{7,11},{8,12},{9,13},{1... | collective-permute-start | bytes 196616 | tf_op jit(solution)/shard_map/ppermute | solution.py:437
  7.9 16.4 %slice-start = ((s8[8388608]{0:T(1024)(128)(4,1)}), s8[4194304]{0:T(1024)(128)(4,1)S(1)}, s32[]{:S(2)}) async-start(s8[8388608]{0:T(1024)(128)(4,1)} %bitcast.14), calls=%async_computation.2 | async-start | bytes 8388608
  8.0 13.8 %copy-start.2 = (bf16[2,8192,16]{1,2,0:T(8,128)(2,1)S(1)}, bf16[2,8192,16]{1,2,0:T(8,128)(2,1)}, u32[]{:S(2)}) copy-start(bf16[2,8192,16]{1,2,0:T(8,128)(2,1)} %param.23) | copy-start | bytes 1572868
  8.0 16.3 %slice-start.1 = ((s8[8388608]{0:T(1024)(128)(4,1)}), s8[4194304]{0:T(1024)(128)(4,1)S(1)}, s32[]{:S(2)}) async-start(s8[8388608]{0:T(1024)(128)(4,1)} %bitcast.14), calls=%async_computation.3 | async-start | bytes 8388608
  8.0 16.3 %copy-start = (bf16[8192,64]{0,1:T(8,128)(2,1)S(1)}, bf16[8192,64]{0,1:T(8,128)(2,1)}, u32[]{:S(2)}) copy-start(bf16[8192,64]{0,1:T(8,128)(2,1)} %param.20) | copy-start | bytes 3145732
  8.0 16.3 %copy-start.1 = (bf16[8192,64]{0,1:T(8,128)(2,1)S(1)}, bf16[8192,64]{0,1:T(8,128)(2,1)}, u32[]{:S(2)}) copy-start(bf16[8192,64]{0,1:T(8,128)(2,1)} %param.21) | copy-start | bytes 3145732
  9.8 5.4 %collective-permute-start.3 = (bf16[1,4,8192]{2,1,0:T(4,128)(2,1)S(1)}, bf16[1,4,8192]{2,1,0:T(4,128)(2,1)S(1)}, u32[]{:S(2)}, u32[]{:S(2)}) collective-permute-start(bf16[1,4,8192]{2,1,0:T(4,128)(2,1)S(1)} %bitcast.27), channel_id=1, source_target_pairs={{0,2},{1,3},{2,0},{3,1},{4,6},{5,7},{6,4},{7,5},{8,10},{9,11},{10,... | collective-permute-start | bytes 196616 | tf_op jit(solution)/shard_map/ppermute | solution.py:437
  13.6 6.7 %collective-permute-start.4 = (bf16[3,4,8192]{2,1,0:T(4,128)(2,1)S(1)}, bf16[3,4,8192]{2,1,0:T(4,128)(2,1)S(1)}, u32[]{:S(2)}, u32[]{:S(2)}) collective-permute-start(bf16[3,4,8192]{2,1,0:T(4,128)(2,1)S(1)} %pad_maximum_fusion), channel_id=1, source_target_pairs={{0,2},{1,3},{2,0},{3,1},{4,6},{5,7},{6,4},{7,5},{8,10},{9,11},{10,... | collective-permute-start | bytes 589832 | tf_op jit(solution)/shard_map/ppermute | solution.py:437
  15.3 5.0 %collective-permute-start.5 = (bf16[5,4,8192]{2,1,0:T(4,128)(2,1)S(1)}, bf16[5,4,8192]{2,1,0:T(4,128)(2,1)S(1)}, u32[]{:S(2)}, u32[]{:S(2)}) collective-permute-start(bf16[5,4,8192]{2,1,0:T(4,128)(2,1)S(1)} %constant_dynamic-update-slice_fusion.refs_0_), channel_id=1, source_target_pairs={{0,1},{1,0},{2,3},{3,2},{4,5},{5,4},{6,7},{7,6},{8,9},{9,8},{10,11... | collective-permute-start | bytes 983048 | tf_op jit(solution)/shard_map/ppermute | solution.py:437
  20.3 1.4 %collective-permute-start.6 = (bf16[3,4,8192]{2,1,0:T(4,128)(2,1)S(1)}, bf16[3,4,8192]{2,1,0:T(4,128)(2,1)S(1)}, u32[]{:S(2)}, u32[]{:S(2)}) collective-permute-start(bf16[3,4,8192]{2,1,0:T(4,128)(2,1)S(1)} %collective-permute-done.4.refs_1_), channel_id=1, source_target_pairs={{0,1},{1,0},{2,3},{3,2},{4,5},{5,4},{6,7},{7,6},{8,9},{9,8},{10,11... | collective-permute-start | bytes 589832 | tf_op jit(solution)/shard_map/ppermute | solution.py:437
  22.4 3.2 %collective-permute-start.9 = (bf16[16,128]{1,0:T(8,128)(2,1)S(1)}, bf16[16,128]{1,0:T(8,128)(2,1)S(1)}, u32[]{:S(2)}, u32[]{:S(2)}) collective-permute-start(bf16[16,128]{1,0:T(8,128)(2,1)S(1)} %get-tuple-element.55.refs_0_), channel_id=1, source_target_pairs={{0,3},{1,2},{2,1},{3,0},{4,7},{5,6},{6,5},{7,4},{8,11},{9,10},{10,... | collective-permute-start | bytes 12296 | tf_op jit(solution)/shard_map/ppermute | solution.py:437
  23.7 3.6 %collective-permute-start.8 = (bf16[16,128]{1,0:T(8,128)(2,1)S(1)}, bf16[16,128]{1,0:T(8,128)(2,1)S(1)}, u32[]{:S(2)}, u32[]{:S(2)}) collective-permute-start(bf16[16,128]{1,0:T(8,128)(2,1)S(1)} %get-tuple-element.55.refs_0_), channel_id=1, source_target_pairs={{0,2},{1,3},{2,0},{3,1},{4,6},{5,7},{6,4},{7,5},{8,10},{9,11},{10,... | collective-permute-start | bytes 12296 | tf_op jit(solution)/shard_map/ppermute | solution.py:437
  24.2 3.1 %collective-permute-start.7 = (bf16[16,128]{1,0:T(8,128)(2,1)S(1)}, bf16[16,128]{1,0:T(8,128)(2,1)S(1)}, u32[]{:S(2)}, u32[]{:S(2)}) collective-permute-start(bf16[16,128]{1,0:T(8,128)(2,1)S(1)} %get-tuple-element.55.refs_0_), channel_id=1, source_target_pairs={{0,1},{1,0},{2,3},{3,2},{4,5},{5,4},{6,7},{7,6},{8,9},{9,8},{10,11... | collective-permute-start | bytes 12296 | tf_op jit(solution)/shard_map/ppermute | solution.py:437
  25.6 19.8 %copy-start.4 = (bf16[2,384,1024]{2,1,0:T(8,128)(2,1)S(1)}, bf16[2,384,1024]{2,1,0:T(8,128)(2,1)}, u32[]{:S(2)}) copy-start(bf16[2,384,1024]{2,1,0:T(8,128)(2,1)} %k_ref.1) | copy-start | bytes 4718596
  25.6 19.8 %copy-start.5 = (bf16[2,384,1024]{2,1,0:T(8,128)(2,1)S(1)}, bf16[2,384,1024]{2,1,0:T(8,128)(2,1)}, u32[]{:S(2)}) copy-start(bf16[2,384,1024]{2,1,0:T(8,128)(2,1)} %v_ref.1) | copy-start | bytes 4718596
  27.3 29.5 %slice-start.2 = ((s8[8388608]{0:T(1024)(128)(4,1)}), s8[4194304]{0:T(1024)(128)(4,1)S(1)}, s32[]{:S(2)}) async-start(s8[8388608]{0:T(1024)(128)(4,1)} %bitcast.16), calls=%async_computation.4 | async-start | bytes 8388608
  27.4 29.5 %slice-start.3 = ((s8[8388608]{0:T(1024)(128)(4,1)}), s8[4194304]{0:T(1024)(128)(4,1)S(1)}, s32[]{:S(2)}) async-start(s8[8388608]{0:T(1024)(128)(4,1)} %bitcast.16), calls=%async_computation.5 | async-start | bytes 8388608
  27.4 4.7 %collective-permute-start.12 = (bf16[16,128]{1,0:T(8,128)(2,1)S(1)}, bf16[16,128]{1,0:T(8,128)(2,1)S(1)}, u32[]{:S(2)}, u32[]{:S(2)}) collective-permute-start(bf16[16,128]{1,0:T(8,128)(2,1)S(1)} %shard_map.187.refs_0_), channel_id=1, source_target_pairs={{0,12},{1,13},{2,14},{3,15},{4,0},{5,1},{6,2},{7,3},{8,4},{9,5},{1... | collective-permute-start | bytes 12296 | tf_op jit(solution)/shard_map/ppermute | solution.py:437
  28.4 4.5 %collective-permute-start.11 = (bf16[16,128]{1,0:T(8,128)(2,1)S(1)}, bf16[16,128]{1,0:T(8,128)(2,1)S(1)}, u32[]{:S(2)}, u32[]{:S(2)}) collective-permute-start(bf16[16,128]{1,0:T(8,128)(2,1)S(1)} %shard_map.187.refs_0_), channel_id=1, source_target_pairs={{0,8},{1,9},{2,10},{3,11},{4,12},{5,13},{6,14},{7,15},{8,0},{9,1},... | collective-permute-start | bytes 12296 | tf_op jit(solution)/shard_map/ppermute | solution.py:437
  29.1 5.4 %collective-permute-start.10 = (bf16[16,128]{1,0:T(8,128)(2,1)S(1)}, bf16[16,128]{1,0:T(8,128)(2,1)S(1)}, u32[]{:S(2)}, u32[]{:S(2)}) collective-permute-start(bf16[16,128]{1,0:T(8,128)(2,1)S(1)} %shard_map.187.refs_0_), channel_id=1, source_target_pairs={{0,4},{1,5},{2,6},{3,7},{4,8},{5,9},{6,10},{7,11},{8,12},{9,13},{1... | collective-permute-start | bytes 12296 | tf_op jit(solution)/shard_map/ppermute | solution.py:437
  57.9 2.1 %collective-permute-start.13 = (f32[32,4608]{1,0:T(8,128)S(1)}, f32[32,4608]{1,0:T(8,128)S(1)}, u32[]{:S(2)}, u32[]{:S(2)}) collective-permute-start(f32[32,4608]{1,0:T(8,128)S(1)} %get-tuple-element.74), channel_id=1, source_target_pairs={{0,1},{1,0},{2,3},{3,2},{4,5},{5,4},{6,7},{7,6},{8,9},{9,8},{10,11... | collective-permute-start | bytes 1769480 | tf_op jit(solution)/shard_map/ppermute | solution.py:437
  58.7 2.0 %collective-permute-start.18 = (f32[32,3584]{1,0:T(8,128)S(1)}, f32[32,3584]{1,0:T(8,128)S(1)}, u32[]{:S(2)}, u32[]{:S(2)}) collective-permute-start(f32[32,3584]{1,0:T(8,128)S(1)} %get-tuple-element.83), channel_id=1, source_target_pairs={{0,1},{1,0},{2,3},{3,2},{4,5},{5,4},{6,7},{7,6},{8,9},{9,8},{10,11... | collective-permute-start | bytes 1376264 | tf_op jit(solution)/shard_map/ppermute | solution.py:437
  60.0 6.0 %collective-permute-start.14 = (bf16[16,4608]{1,0:T(8,128)(2,1)S(1)}, bf16[16,4608]{1,0:T(8,128)(2,1)S(1)}, u32[]{:S(2)}, u32[]{:S(2)}) collective-permute-start(bf16[16,4608]{1,0:T(8,128)(2,1)S(1)} %get-tuple-element.76), channel_id=1, source_target_pairs={{0,2},{1,3},{2,0},{3,1},{4,6},{5,7},{6,4},{7,5},{8,10},{9,11},{10,... | collective-permute-start | bytes 442376 | tf_op jit(solution)/shard_map/ppermute | solution.py:437
  60.8 6.7 %collective-permute-start.19 = (bf16[8,3584]{1,0:T(8,128)(2,1)S(1)}, bf16[8,3584]{1,0:T(8,128)(2,1)S(1)}, u32[]{:S(2)}, u32[]{:S(2)}) collective-permute-start(bf16[8,3584]{1,0:T(8,128)(2,1)S(1)} %get-tuple-element.85), channel_id=1, source_target_pairs={{0,4},{1,5},{2,6},{3,7},{4,8},{5,9},{6,10},{7,11},{8,12},{9,13},{1... | collective-permute-start | bytes 172040 | tf_op jit(solution)/shard_map/ppermute | solution.py:437
  61.0 8.9 %collective-permute-start.20 = (bf16[8,3584]{1,0:T(8,128)(2,1)S(1)}, bf16[8,3584]{1,0:T(8,128)(2,1)S(1)}, u32[]{:S(2)}, u32[]{:S(2)}) collective-permute-start(bf16[8,3584]{1,0:T(8,128)(2,1)S(1)} %get-tuple-element.86), channel_id=1, source_target_pairs={{0,8},{1,9},{2,10},{3,11},{4,12},{5,13},{6,14},{7,15},{8,0},{9,1},... | collective-permute-start | bytes 172040 | tf_op jit(solution)/shard_map/ppermute | solution.py:437
  61.9 8.0 %collective-permute-start.21 = (bf16[8,3584]{1,0:T(8,128)(2,1)S(1)}, bf16[8,3584]{1,0:T(8,128)(2,1)S(1)}, u32[]{:S(2)}, u32[]{:S(2)}) collective-permute-start(bf16[8,3584]{1,0:T(8,128)(2,1)S(1)} %get-tuple-element.87), channel_id=1, source_target_pairs={{0,12},{1,13},{2,14},{3,15},{4,0},{5,1},{6,2},{7,3},{8,4},{9,5},{1... | collective-permute-start | bytes 172040 | tf_op jit(solution)/shard_map/ppermute | solution.py:437
  66.1 7.9 %collective-permute-start.15 = (bf16[4,4608]{1,0:T(4,128)(2,1)S(1)}, bf16[4,4608]{1,0:T(4,128)(2,1)S(1)}, u32[]{:S(2)}, u32[]{:S(2)}) collective-permute-start(bf16[4,4608]{1,0:T(4,128)(2,1)S(1)} %get-tuple-element.78), channel_id=1, source_target_pairs={{0,4},{1,5},{2,6},{3,7},{4,8},{5,9},{6,10},{7,11},{8,12},{9,13},{1... | collective-permute-start | bytes 110600 | tf_op jit(solution)/shard_map/ppermute | solution.py:437
  66.2 7.7 %collective-permute-start.16 = (bf16[4,4608]{1,0:T(4,128)(2,1)S(1)}, bf16[4,4608]{1,0:T(4,128)(2,1)S(1)}, u32[]{:S(2)}, u32[]{:S(2)}) collective-permute-start(bf16[4,4608]{1,0:T(4,128)(2,1)S(1)} %get-tuple-element.79), channel_id=1, source_target_pairs={{0,8},{1,9},{2,10},{3,11},{4,12},{5,13},{6,14},{7,15},{8,0},{9,1},... | collective-permute-start | bytes 110600 | tf_op jit(solution)/shard_map/ppermute | solution.py:437
  67.5 6.4 %collective-permute-start.17 = (bf16[4,4608]{1,0:T(4,128)(2,1)S(1)}, bf16[4,4608]{1,0:T(4,128)(2,1)S(1)}, u32[]{:S(2)}, u32[]{:S(2)}) collective-permute-start(bf16[4,4608]{1,0:T(4,128)(2,1)S(1)} %get-tuple-element.80), channel_id=1, source_target_pairs={{0,12},{1,13},{2,14},{3,15},{4,0},{5,1},{6,2},{7,3},{8,4},{9,5},{1... | collective-permute-start | bytes 110600 | tf_op jit(solution)/shard_map/ppermute | solution.py:437
  70.0 3.9 %collective-permute-start.22 = (bf16[4,3584]{1,0:T(4,128)(2,1)S(1)}, bf16[4,3584]{1,0:T(4,128)(2,1)S(1)}, u32[]{:S(2)}, u32[]{:S(2)}) collective-permute-start(bf16[4,3584]{1,0:T(4,128)(2,1)S(1)} %get-tuple-element.89), channel_id=1, source_target_pairs={{0,2},{1,3},{2,0},{3,1},{4,6},{5,7},{6,4},{7,5},{8,10},{9,11},{10,... | collective-permute-start | bytes 86024 | tf_op jit(solution)/shard_map/ppermute | solution.py:437
  (9 other events, 55.7 us)
